TPU v7x, 32 devices: a whole 2x2x4 slice. The times are simulated.
32 devices in a mesh: groups: 2 (over y), expert: 16 (over z, x, core).
Axes of the slice: x: 2, y: 2, z: 4, core: 2. Of those that a mesh axis runs over, the one named last changes fastest.
Arguments:
- hidden_of_route: bfloat16 [4096, 8, 1024], P(('groups', 'expert')), parts along dimension 0, may hold values from -6 to 6
- expert_of_route: int32 [4096, 8], P(('groups', 'expert')), parts along dimension 0, may hold values from 0 to 15, all different within a row; in each aligned block of 128 rows (0 to 127, 128 to 255, ...) at most 128 rows name the same one
- gate_of_route: bfloat16 [4096, 8], P(('groups', 'expert')), parts along dimension 0, may hold values from 0.019897461 to 0.25
- capacity: int32 [32], P('groups'), parts along dimension 0, may hold values from 512 to 2048
- output_gradient: bfloat16 [4096, 2048], P(('groups', 'expert')), parts along dimension 0, may hold values from -0.796875 to 0.796875
- curvature: float32 [4096], P(('groups', 'expert')), parts along dimension 0, may hold values from 0.01 to 0.1
- adapter_down: float32 [16, 1024, 16], P('expert'), may hold values from -0.1875 to 0.1875
- adapter_up: float32 [16, 16, 2048], P('expert'), may hold values from -1.5 to 1.5
- down_direction: float32 [32, 1024, 16], P(('groups', 'expert')), parts along dimension 0, may hold values from -0.1875 to 0.1875
- up_direction: float32 [32, 16, 2048], P(('groups', 'expert')), parts along dimension 0, may hold values from -1.5 to 1.5
Outputs:
- down_gradient: float32 [32, 1024, 16], P(('groups', 'expert')), parts along dimension 0
- up_gradient: float32 [32, 16, 2048], P(('groups', 'expert')), parts along dimension 0
- curvature_down: float32 [32, 1024, 16], P(('groups', 'expert')), parts along dimension 0
- curvature_up: float32 [32, 16, 2048], P(('groups', 'expert')), parts along dimension 0
There are 2 independent parts, one for each index of `groups`. A program takes and returns all parts, laid end to end along the dimension named above; an argument that names none is the same for every part. Nothing has to cross between parts.
Inputs may be any that keep to these rules, and one draw needn't show every extreme that they name: `expert_of_route`: each token names 8 different experts; the tokens of one block of 128 name one expert at most 128 times, a bound that some block reaches.
All inputs are finite; a program needn't handle non-finite values.
Results may differ from a plain program's by a relative error of at most 0.0017.
Values may be sent and summed in bfloat16 or wider, within the bound.
No kernel may reach another device: no remote copies, remote signals or barrier semaphores. Data moves between devices by JAX's collectives and lax.ppermute only.
A program may use at most 128 MiB of HBM per device.

v0:
```python
import jax
import jax.numpy as jnp
from jax import lax
from jax.sharding import PartitionSpec as P

adapter_scale = 2.0


def carried_in(value, axis, join, neutral):
    count, mine = (lax.axis_size(axis), lax.axis_index(axis))
    pieces = lax.all_gather(value, axis)
    so_far = jnp.full_like(value, 0) + jnp.asarray(neutral, value.dtype)

    def lap(position, so_far):
        longer = join(so_far, pieces[position])
        return jnp.where(position < mine, longer, so_far)

    return lax.fori_loop(0, count - 1, lap, so_far)


def add_counts(earlier, later):
    return earlier + later


def local(
    hidden_of_route,
    expert_of_route,
    gate_of_route,
    capacity,
    output_gradient,
    curvature,
    adapter_down,
    adapter_up,
    down_direction,
    up_direction,
):
    finest_precision = lax.Precision.HIGHEST
    group_size = lax.axis_size("expert")
    tok_rows, top_count = expert_of_route.shape
    hidden_width = hidden_of_route.shape[2]
    resident_experts = adapter_down.shape[0]
    adapter_rank = adapter_down.shape[2]
    model_width = output_gradient.shape[1]
    experts = resident_experts * group_size
    slot_most = 2 * tok_rows * top_count // experts
    routes = expert_of_route.reshape(-1)
    onehot = (routes[:, None] == jnp.arange(experts, dtype=jnp.int32)[None, :]).astype(jnp.int32)
    earlier = jnp.cumsum(onehot, axis=0) - onehot
    local_rank = jnp.sum(earlier * onehot, axis=1)
    counts = jnp.sum(onehot, axis=0)
    prior_count = carried_in(counts, "expert", add_counts, jnp.zeros_like(counts))
    global_rank = local_rank + jnp.sum(onehot * prior_count[None, :], axis=1)
    route_limit = jnp.sum(onehot * capacity[None, :], axis=1)
    retained_mask = (global_rank < route_limit).astype(jnp.float32)
    weight_of_route = (
        adapter_scale * gate_of_route.reshape(-1).astype(jnp.float32) * retained_mask
    ).astype(jnp.bfloat16)
    slot_index = routes * slot_most + local_rank
    layout = (group_size, resident_experts, slot_most)
    send_hidden = (
        jnp.zeros((experts * slot_most, hidden_width), jnp.bfloat16)
        .at[slot_index]
        .set(hidden_of_route.reshape(-1, hidden_width))
        .reshape(layout + (hidden_width,))
    )
    send_weight = (
        jnp.zeros((experts * slot_most,), jnp.bfloat16)
        .at[slot_index]
        .set(weight_of_route)
        .reshape(layout)
    )
    down_stacked = jnp.concatenate([adapter_down, down_direction], axis=2)
    up_stacked = jnp.concatenate([adapter_up, up_direction], axis=1)

    def spread(token_rows):
        per_route = jnp.repeat(token_rows, top_count, axis=0)
        placed = (
            jnp.zeros((experts * slot_most, model_width), jnp.bfloat16)
            .at[slot_index]
            .set(per_route)
        )
        return placed.reshape(layout + (model_width,))

    send_residual = spread(output_gradient)
    pieces = (
        lax.all_to_all(send_hidden, "expert", split_axis=0, concat_axis=0, tiled=True),
        lax.all_to_all(send_weight, "expert", split_axis=0, concat_axis=0, tiled=True),
    )
    hidden_rows = pieces[0].astype(jnp.float32)
    weight_rows = pieces[1].astype(jnp.float32)[..., None]
    reduced_hidden = jnp.einsum(
        "cjif,jfk->cjik", hidden_rows, down_stacked, precision=finest_precision
    )
    exchanged_rows = jnp.concatenate(
        [reduced_hidden[..., adapter_rank:], reduced_hidden[..., :adapter_rank]], axis=3
    )
    tangent_out = weight_rows * jnp.einsum(
        "cjik,jkd->cjid", exchanged_rows, up_stacked, precision=finest_precision
    )
    returned = lax.all_to_all(
        tangent_out.astype(jnp.bfloat16), "expert", split_axis=0, concat_axis=0, tiled=True
    )
    results = (returned, reduced_hidden) + tuple(pieces)
    returned = results[0]
    reduced_hidden = results[1]
    hidden_rows = results[2]
    weight_rows = results[3]
    route_tangent = returned.reshape(experts * slot_most, model_width)[slot_index]
    out_tangent = jnp.sum(
        route_tangent.reshape(tok_rows, top_count, model_width).astype(jnp.float32), axis=1
    )
    resid_tangent = (curvature[:, None] * out_tangent).astype(jnp.bfloat16)
    send_tangent = spread(resid_tangent)
    residual_rows, tangent_rows = (
        lax.all_to_all(send_residual, "expert", split_axis=0, concat_axis=0, tiled=True),
        lax.all_to_all(send_tangent, "expert", split_axis=0, concat_axis=0, tiled=True),
    )
    residual_full = residual_rows.astype(jnp.float32)
    complete_tangent = tangent_rows.astype(jnp.float32)
    weight_column = weight_rows.astype(jnp.float32)[..., None]
    residual_reduced = jnp.einsum(
        "wyov,yqv->wyoq", residual_full, up_stacked, precision=finest_precision
    )
    reduced_tangent = jnp.einsum(
        "wyov,yqv->wyoq", complete_tangent, adapter_up, precision=finest_precision
    )
    left_terms = jnp.concatenate(
        [
            weight_column * residual_reduced[..., :adapter_rank],
            weight_column * (reduced_tangent + residual_reduced[..., adapter_rank:]),
        ],
        axis=3,
    )
    down_terms = jnp.einsum(
        "cjif,cjik->jfk", hidden_rows.astype(jnp.float32), left_terms, precision=finest_precision
    )
    raised_update = weight_column * reduced_hidden[..., :adapter_rank]
    raised_tangent_update = weight_column * reduced_hidden[..., adapter_rank:]
    up_terms = jnp.einsum(
        "cjik,cjid->jkd",
        jnp.concatenate([raised_update, raised_tangent_update], axis=3),
        residual_full,
        precision=finest_precision,
    )
    curvature_piece = up_terms[:, adapter_rank:] + jnp.einsum(
        "cjik,cjid->jkd", raised_update, complete_tangent, precision=finest_precision
    )
    return (
        down_terms[..., :adapter_rank],
        up_terms[:, :adapter_rank],
        down_terms[..., adapter_rank:],
        curvature_piece,
    )


def solution(mesh):
    return jax.shard_map(
        local,
        mesh=mesh,
        in_specs=(
            P(("groups", "expert"), None, None),
            P(("groups", "expert"), None),
            P(("groups", "expert"), None),
            P("groups"),
            P(("groups", "expert"), None),
            P(("groups", "expert")),
            P("expert", None, None),
            P("expert", None, None),
            P(("groups", "expert"), None, None),
            P(("groups", "expert"), None, None),
        ),
        out_specs=(
            P(("groups", "expert"), None, None),
            P(("groups", "expert"), None, None),
            P(("groups", "expert"), None, None),
            P(("groups", "expert"), None, None),
        ),
        check_vma=False,
    )
```

profile of v0, /device:TPU:11, one launch (start us, length us, event | category | flops | bytes accessed | tf_op | source)
XLA Modules:
  0.0 793.8 jit_solution(12983391937682519867)
XLA Ops:
  5.9 7.9 all-reduce
  14.4 4.5 reduce-window.6
  20.2 7.6 scatter_custom_fusion.1
  28.4 8.4 %all-to-all-start.1 = ((bf16[16,1,128]{2,1,0:T(2,128)(2,1)}), bf16[16,1,128]{2,1,0:T(2,128)(2,1)S(1)}, u32[]{:S(2)}, u32[]{:S(2)}) async-start(bf16[16,1,128]{2,1,0:T(2,128)(2,1)} %copy.37), calls=%async_computation.1 | async-start | bytes 16384 | tf_op jit(solution)/shard_map/all_to_all | solution.py:87
  36.8 7.9 scatter_custom_fusion
  44.7 6.4 all-to-all-start
  51.1 11.2 %scatter_custom_fusion.2 = bf16[2048,2048]{1,0:T(8,128)(2,1)} fusion(s32[1024]{0:T(1024)S(1)} %bitcast.148, bf16[]{:T(256)} %constant.42.clone.1, bf16[128,2048]{1,0:T(8,128)(2,1)S(1)} %copy-done.4), kind=kCustom, calls=%fused_computation.21 | custom fusion | bytes 8912898 | tf_op jit(solution)/shard_map/scatter | solution.py:80
  62.3 81.1 %all-to-all-done = bf16[16,1,128,1024]{3,2,1,0:T(8,128)(2,1)} async-done(((bf16[16,1,128,1024]{3,2,1,0:T(8,128)(2,1)}), bf16[16,1,128,1024]{3,2,1,0:T(8,128)(2,1)}, u32[]{:S(2)}, u32[]{:S(2)}) %all-to-all-start) | async-done | bytes 4194336 | tf_op jit(solution)/shard_map/all_to_all | solution.py:86
  143.4 5.4 all-to-all-start.2
  148.8 5.4 fusion.34
  154.3 176.7 %all-to-all-done.2 = bf16[16,1,128,2048]{3,2,1,0:T(8,128)(2,1)} async-done(((bf16[16,1,128,2048]{3,2,1,0:T(8,128)(2,1)}), bf16[16,1,128,2048]{3,2,1,0:T(8,128)(2,1)}, u32[]{:S(2)}, u32[]{:S(2)}) %all-to-all-start.2) | async-done | bytes 8388640 | tf_op jit(solution)/shard_map/all_to_all | solution.py:115
  331.0 9.6 %fusion.37 = f32[16,1,128,32]{2,3,0,1:T(8,128)S(1)} fusion(bf16[16,1,128,2048]{3,2,1,0:T(8,128)(2,1)} %all-to-all-done.2, f32[1,16,2048]{2,1,0:T(8,128)S(1)} %copy-done.3, f32[1,16,2048]{2,1,0:T(8,128)S(1)} %copy-done.2), kind=kOutput, calls=%fused_computation.38 | convolution fusion | flops 1610678272 | bytes 8912896 | tf_op jit(solution)/shard_map/wyov,yqv->wyoq/dot_general | solution.py:121
  340.7 15.7 %fusion.1 = bf16[16,1,128,2048]{2,3,1,0:T(8,128)(2,1)} fusion(f32[16,128]{1,0:T(8,128)S(1)} %bitcast.141, f32[16,1,128,16]{2,3,0,1:T(8,128)S(1)} %get-tuple-element.112, f32[16,1,128,16]{2,3,0,1:T(8,128)S(1)} %get-tuple-element.113, f32[1,16,2048]{2,1,0:T(8,128)S(1)} %copy-done.3, f32[1,16,2048]{2,1,0:T(8,128)S(1)} %copy-done.2), kind=kOutput, calls=%fused_computation.9 | convolution fusion | flops 1619132416 | bytes 8921088 | tf_op jit(solution)/shard_map/cjik,jkd->cjid/dot_general | solution.py:97
  356.4 5.3 all-to-all-start.3
  361.7 182.2 %all-to-all-done.3 = bf16[16,1,128,2048]{2,3,1,0:T(8,128)(2,1)} async-done(((bf16[16,1,128,2048]{2,3,1,0:T(8,128)(2,1)}), bf16[16,1,128,2048]{2,3,1,0:T(8,128)(2,1)}, u32[]{:S(2)}, u32[]{:S(2)}) %all-to-all-start.3) | async-done | bytes 8388640 | tf_op jit(solution)/shard_map/all_to_all | solution.py:100
  543.9 12.3 %copy.39 = bf16[16,1,128,2048]{3,2,0,1:T(8,128)(2,1)} copy(bf16[16,1,128,2048]{2,3,1,0:T(8,128)(2,1)} %all-to-all-done.3) | data formatting | bytes 16777216 | tf_op jit(solution)/shard_map/all_to_all | solution.py:100
  556.2 13.3 %gather_fusion = bf16[1024,2048]{1,0:T(8,128)(2,1)} fusion(bf16[2048,2048]{1,0:T(8,128)(2,1)} %bitcast.136, s32[1024]{0:T(1024)S(1)} %broadcast_clamp_fusion), kind=kCustom, calls=%fused_computation | custom fusion | bytes 8392704 | tf_op jit(solution)/shard_map/gather | solution.py:108
  569.5 5.0 convert_reduce_fusion
  574.7 11.5 %scatter_custom_fusion.3 = bf16[2048,2048]{1,0:T(8,128)(2,1)} fusion(s32[1024]{0:T(1024)S(1)} %bitcast.150, bf16[]{:T(256)} %constant.42.clone.1, bf16[128,2048]{1,0:T(8,128)(2,1)S(1)} %multiply_convert_fusion), kind=kCustom, calls=%fused_computation.19 | custom fusion | bytes 8912898 | tf_op jit(solution)/shard_map/scatter | solution.py:80
  586.2 4.9 all-to-all-start.4
  591.1 6.5 fusion.20
  598.3 175.2 %all-to-all-done.4 = bf16[16,1,128,2048]{3,2,1,0:T(8,128)(2,1)} async-done(((bf16[16,1,128,2048]{3,2,1,0:T(8,128)(2,1)}), bf16[16,1,128,2048]{3,2,1,0:T(8,128)(2,1)}, u32[]{:S(2)}, u32[]{:S(2)}) %all-to-all-start.4) | async-done | bytes 8388640 | tf_op jit(solution)/shard_map/all_to_all | solution.py:116
  773.5 8.9 %fusion.49 = f32[16,1,128,16]{2,3,0,1:T(8,128)S(1)} fusion(bf16[16,1,128,2048]{3,2,1,0:T(8,128)(2,1)} %all-to-all-done.4, f32[16,1,128,32]{2,3,0,1:T(8,128)S(1)} %fusion.37, f32[1,16,2048]{2,1,0:T(8,128)S(1)} %copy-done.2, f32[16,128]{1,0:T(8,128)S(1)} %bitcast.142), kind=kOutput, calls=%fused_computation.42 | convolution fusion | flops 805371904 | bytes 8790016 | tf_op jit(solution)/shard_map/wyov,yqv->wyoq/dot_general | solution.py:124
  787.0 6.3 fusion.26
  (66 shorter events, 12.8 us)
Async XLA Ops:
  0.6 36.2 %copy-start = (bf16[128,8,1024]{2,1,0:T(8,128)(2,1)S(1)}, bf16[128,8,1024]{2,1,0:T(8,128)(2,1)}, u32[]{:S(2)}) copy-start(bf16[128,8,1024]{2,1,0:T(8,128)(2,1)} %param.12) | copy-start | bytes 6291460
  0.6 50.4 %copy-start.4 = (bf16[128,2048]{1,0:T(8,128)(2,1)S(1)}, bf16[128,2048]{1,0:T(8,128)(2,1)}, u32[]{:S(2)}) copy-start(bf16[128,2048]{1,0:T(8,128)(2,1)} %param.16) | copy-start | bytes 1572868
  28.4 16.3 %all-to-all-start.1 = ((bf16[16,1,128]{2,1,0:T(2,128)(2,1)}), bf16[16,1,128]{2,1,0:T(2,128)(2,1)S(1)}, u32[]{:S(2)}, u32[]{:S(2)}) async-start(bf16[16,1,128]{2,1,0:T(2,128)(2,1)} %copy.37), calls=%async_computation.1 | async-start | bytes 16384 | tf_op jit(solution)/shard_map/all_to_all | solution.py:87
  44.7 98.7 %all-to-all-start = ((bf16[16,1,128,1024]{3,2,1,0:T(8,128)(2,1)}), bf16[16,1,128,1024]{3,2,1,0:T(8,128)(2,1)}, u32[]{:S(2)}, u32[]{:S(2)}) async-start(bf16[16,1,128,1024]{3,2,1,0:T(8,128)(2,1)} %bitcast.139), calls=%async_computation | async-start | bytes 8388608 | tf_op jit(solution)/shard_map/all_to_all | solution.py:86
  143.4 5.4 copy-start.5
  143.4 5.4 copy-start.6
  143.4 187.6 %copy-start.2 = (f32[1,16,2048]{2,1,0:T(8,128)S(1)}, f32[1,16,2048]{2,1,0:T(8,128)}, u32[]{:S(2)}) copy-start(f32[1,16,2048]{2,1,0:T(8,128)} %param.19) | copy-start | bytes 393220
  143.4 187.6 %copy-start.3 = (f32[1,16,2048]{2,1,0:T(8,128)S(1)}, f32[1,16,2048]{2,1,0:T(8,128)}, u32[]{:S(2)}) copy-start(f32[1,16,2048]{2,1,0:T(8,128)} %param.21) | copy-start | bytes 393220
  143.4 187.6 %all-to-all-start.2 = ((bf16[16,1,128,2048]{3,2,1,0:T(8,128)(2,1)}), bf16[16,1,128,2048]{3,2,1,0:T(8,128)(2,1)}, u32[]{:S(2)}, u32[]{:S(2)}) async-start(bf16[16,1,128,2048]{3,2,1,0:T(8,128)(2,1)} %bitcast.137), calls=%async_computation.2 | async-start | bytes 16777216 | tf_op jit(solution)/shard_map/all_to_all | solution.py:115
  356.4 187.5 %all-to-all-start.3 = ((bf16[16,1,128,2048]{2,3,1,0:T(8,128)(2,1)}), bf16[16,1,128,2048]{2,3,1,0:T(8,128)(2,1)}, u32[]{:S(2)}, u32[]{:S(2)}) async-start(bf16[16,1,128,2048]{2,3,1,0:T(8,128)(2,1)} %fusion.1), calls=%async_computation.3 | async-start | bytes 16777216 | tf_op jit(solution)/shard_map/all_to_all | solution.py:100
  556.2 18.3 %copy-start.7 = (f32[128]{0:T(128)S(1)}, f32[128]{0:T(128)}, u32[]{:S(2)}) copy-start(f32[128]{0:T(128)} %param.17) | copy-start | bytes 1540
  586.2 187.2 %all-to-all-start.4 = ((bf16[16,1,128,2048]{3,2,1,0:T(8,128)(2,1)}), bf16[16,1,128,2048]{3,2,1,0:T(8,128)(2,1)}, u32[]{:S(2)}, u32[]{:S(2)}) async-start(bf16[16,1,128,2048]{3,2,1,0:T(8,128)(2,1)} %bitcast.138), calls=%async_computation.4 | async-start | bytes 16777216 | tf_op jit(solution)/shard_map/all_to_all | solution.py:116
  782.4 10.9 %copy-start.1 = (bf16[128,8,1024]{2,1,0:T(8,128)(2,1)S(1)}, bf16[128,8,1024]{2,1,0:T(8,128)(2,1)}, u32[]{:S(2)}) copy-start(bf16[128,8,1024]{2,1,0:T(8,128)(2,1)} %param.12) | copy-start | bytes 6291460
where the time goes:
time: 802 us; the launch traced here: 794 us
  waiting for transfers between devices  615 us (77%)
  local copies, waits for them, and re-layouts  69.1 us (9%)
  matrix products  56.4 us (7%)
  starting transfers between devices  30.4 us (4%)
  other arithmetic  12.5 us (2%)
    all_to_all x1, waiting for transfers between devices, local(): lax.all_to_all(tangent_out.astype(jnp.bfloat16), 'expert', split_axis=0,...  182 us
    all_to_all x1, waiting for transfers between devices, local(): lax.all_to_all(send_residual, 'expert', split_axis=0, concat_axis=0, tile...  177 us
    all_to_all x1, waiting for transfers between devices, local(): lax.all_to_all(send_tangent, 'expert', split_axis=0, concat_axis=0, tiled...  175 us
    all_to_all x1, waiting for transfers between devices, local(): lax.all_to_all(send_hidden, 'expert', split_axis=0, concat_axis=0, tiled=...  81.1 us
    scatter x2, local copies, waits for them, and re-layouts, spread(): placed = jnp.zeros((experts * slot_most, model_width), jnp.bfloat16).at[s...  22.7 us
  transfers between devices with their start and end apart: 5, of which 4 were waited for; matrix products, arithmetic and copies ran while one was open for 4% of the time, Pallas kernels for 0%

commit v1 on v0

--- a/solution.py
+++ b/solution.py
@@ -1,9 +1,170 @@
+import functools
+
 import jax
 import jax.numpy as jnp
 from jax import lax
+from jax.experimental import pallas as pl
+from jax.experimental.pallas import tpu as pltpu
 from jax.sharding import PartitionSpec as P
 
 adapter_scale = 2.0
+f32 = jnp.float32
+bf16 = jnp.bfloat16
+kernel_vmem = 56 * 2**20
+
+
+def halves(value):
+    high = value.astype(bf16)
+    return high, (value - high.astype(f32)).astype(bf16)
+
+
+def dot(a, b, a_dim, b_dim):
+    return lax.dot_general(a, b, (((a_dim,), (b_dim,)), ((), ())), preferred_element_type=f32)
+
+
+def dot_exact_left(a, b, a_dim, b_dim):
+    return dot(a, b[0], a_dim, b_dim) + dot(a, b[1], a_dim, b_dim)
+
+
+def dot_pairs(a, b, a_dim, b_dim):
+    return dot(a[0], b[0], a_dim, b_dim) + (dot(a[1], b[0], a_dim, b_dim) + dot(a[0], b[1], a_dim, b_dim))
+
+
+def token_kernel(
+    hidden_width,
+    hidden_ref,
+    expert_ref,
+    gate_ref,
+    prior_ref,
+    capacity_ref,
+    gradient_ref,
+    curvature_ref,
+    factor_ref,
+    out_ref,
+    left_ref,
+):
+    experts, _, rank, _ = factor_ref.shape
+    tokens, top = expert_ref.shape
+    wide = experts * rank
+    model_width = gradient_ref.shape[1]
+    column_expert = lax.broadcasted_iota(jnp.int32, (tokens, wide), 1) // rank
+
+    named = [expert_ref[:, k : k + 1] == column_expert for k in range(top)]
+    gate = jnp.zeros((tokens, wide), f32)
+    member = jnp.zeros((tokens, wide), f32)
+    for k in range(top):
+        gate = jnp.where(named[k], gate_ref[:, k : k + 1], gate)
+        member = jnp.where(named[k], 1.0, member)
+    below = (
+        lax.broadcasted_iota(jnp.int32, (tokens, tokens), 0)
+        > lax.broadcasted_iota(jnp.int32, (tokens, tokens), 1)
+    )
+    local_rank = dot(jnp.where(below, 1.0, 0.0).astype(bf16), member.astype(bf16), 1, 0)
+    retained = local_rank + prior_ref[...] < capacity_ref[...]
+    weight = jnp.where(retained, adapter_scale * gate, 0.0)
+
+    def factor(kind, start, width):
+        block = factor_ref[:, kind, :, start : start + width]
+        return halves(block.reshape(wide, width))
+
+    def reduced(kind):
+        full = dot_exact_left(hidden_ref[...], factor(kind, 0, hidden_width), 1, 1)
+        total = jnp.zeros((tokens, wide), f32)
+        for k in range(top):
+            total = jnp.where(named[k], full[k * tokens : (k + 1) * tokens], total)
+        return halves(weight * total)
+
+    weighted_du = reduced(0)
+    weighted_u = reduced(1)
+
+    adapter_up = factor(0, hidden_width, model_width)
+    up_direction = factor(1, hidden_width, model_width)
+    out_tangent = dot_pairs(weighted_du, adapter_up, 1, 0) + dot_pairs(weighted_u, up_direction, 1, 0)
+    resid = halves(curvature_ref[...] * out_tangent)
+
+    gradient = gradient_ref[...]
+    up_shape = (experts, rank, model_width)
+    up_gradient = dot(weighted_u[0], gradient, 0, 0) + dot(weighted_u[1], gradient, 0, 0)
+    out_ref[:, 1, :, hidden_width:] = up_gradient.reshape(up_shape)
+    up_curvature = (
+        dot(weighted_du[0], gradient, 0, 0)
+        + dot(weighted_du[1], gradient, 0, 0)
+        + dot_pairs(weighted_u, resid, 0, 0)
+    )
+    out_ref[:, 0, :, hidden_width:] = up_curvature.reshape(up_shape)
+
+    to_gradient = weight * dot_exact_left(gradient, adapter_up, 1, 1)
+    to_curvature = weight * (
+        dot_pairs(resid, adapter_up, 1, 1) + dot_exact_left(gradient, up_direction, 1, 1)
+    )
+    down_shape = (experts, rank, hidden_width)
+    for kind, terms in ((1, to_gradient), (0, to_curvature)):
+        for part, half in enumerate(halves(terms)):
+            for k in range(top):
+                left_ref[part, k * tokens : (k + 1) * tokens] = jnp.where(
+                    named[k], half, jnp.zeros_like(half)
+                )
+        down = dot(left_ref[0], hidden_ref[...], 0, 0) + dot(left_ref[1], hidden_ref[...], 0, 0)
+        out_ref[:, kind, :, :hidden_width] = down.reshape(down_shape)
+
+
+def gathered_plan(
+    hidden_of_route,
+    expert_of_route,
+    gate_of_route,
+    capacity,
+    output_gradient,
+    curvature,
+    adapter_down,
+    adapter_up,
+    down_direction,
+    up_direction,
+):
+    group_size = lax.axis_size("expert")
+    tokens, top = expert_of_route.shape
+    hidden_width = hidden_of_route.shape[2]
+    resident, _, rank = adapter_down.shape
+    model_width = output_gradient.shape[1]
+    experts = resident * group_size
+    wide = experts * rank
+
+    names = jnp.arange(experts, dtype=jnp.int32)
+    counts = jnp.sum((expert_of_route[:, :, None] == names).astype(jnp.int32), axis=(0, 1))
+    all_counts = lax.all_gather(counts, "expert")
+    earlier = jnp.arange(group_size)[:, None] < lax.axis_index("expert")
+    prior = jnp.sum(jnp.where(earlier, all_counts, 0), axis=0)
+
+    def by_column(per_expert):
+        return jnp.repeat(per_expert.astype(f32), rank)[None, :]
+
+    own = jnp.stack(
+        [
+            jnp.concatenate([down_direction.transpose(0, 2, 1), adapter_up], axis=2),
+            jnp.concatenate([adapter_down.transpose(0, 2, 1), up_direction], axis=2),
+        ],
+        axis=1,
+    )
+    factors = lax.all_gather(own, "expert", axis=0, tiled=True)
+    hidden_by_position = hidden_of_route.transpose(1, 0, 2).reshape(top * tokens, hidden_width)
+    partial_sums = pl.pallas_call(
+        functools.partial(token_kernel, hidden_width),
+        out_shape=jax.ShapeDtypeStruct((experts, 2, rank, hidden_width + model_width), f32),
+        scratch_shapes=[pltpu.VMEM((2, top * tokens, wide), bf16)],
+        compiler_params=pltpu.CompilerParams(vmem_limit_bytes=kernel_vmem),
+    )(
+        hidden_by_position,
+        expert_of_route,
+        gate_of_route.astype(f32),
+        by_column(prior),
+        by_column(capacity),
+        output_gradient,
+        curvature[:, None],
+        factors,
+    )
+    summed = lax.psum_scatter(partial_sums, "expert", scatter_dimension=0, tiled=True)
+    down = summed[..., :hidden_width].transpose(0, 1, 3, 2)
+    up = summed[..., hidden_width:]
+    return down[:, 1], up[:, 1], down[:, 0], up[:, 0]
 
 
 def carried_in(value, axis, join, neutral):
@@ -22,7 +183,7 @@
     return earlier + later
 
 
-def local(
+def routed_plan(
     hidden_of_route,
     expert_of_route,
     gate_of_route,
@@ -153,6 +314,13 @@
     )
 
 
+def local(*arguments):
+    adapter_down, adapter_up = arguments[6], arguments[7]
+    factor_bytes = 2 * 4 * (adapter_down.size + adapter_up.size) * lax.axis_size("expert")
+    plan = gathered_plan if 4 * factor_bytes <= kernel_vmem else routed_plan
+    return plan(*arguments)
+
+
 def solution(mesh):
     return jax.shard_map(
         local,

time: 802 us -> 186 us (0.23)
  the two profiles are of different devices: /device:TPU:11 before, /device:TPU:0 now
where the time goes in v1:
time: 186 us; the launch traced here: 185 us
  waiting for transfers between devices  122 us (66%)
  Pallas kernels  16.3 us (9%)
  between operations  14.7 us (8%)
  local copies, waits for them, and re-layouts  14.6 us (8%)
  blocking collectives  13.9 us (7%)
  other arithmetic  3.4 us (2%)
    reduce_scatter x1, waiting for transfers between devices, gathered_plan(): lax.psum_scatter(partial_sums, 'expert', scatter_dimension=0, tiled=True)  84 us
    all_gather x1, waiting for transfers between devices, gathered_plan(): factors = lax.all_gather(own, 'expert', axis=0, tiled=True)  38.4 us
    pallas_call x1, Pallas kernels, gathered_plan(): pl.pallas_call(functools.partial(token_kernel, hidden_width), out_shape=j...  16.3 us
    unnamed x1, blocking collectives  13.9 us
    transpose x1, local copies, waits for them, and re-layouts, gathered_plan(): hidden_of_route.transpose(1, 0, 2).reshape(top * tokens, hidden_width)  4.11 us
  transfers between devices with their start and end apart: 2, of which 2 were waited for; matrix products, arithmetic and copies ran while one was open for 7% of the time, Pallas kernels for 0%

profile of v1, /device:TPU:0, one launch (start us, length us, event | category | flops | bytes accessed | tf_op | source)
XLA Modules:
  0.0 185.4 jit_solution(11060998666221047731)
XLA Ops:
  7.2 1.0 maximum_bitcast_fusion
  8.2 0.8 pad_maximum_fusion
  9.1 0.0 reduce-scatter.2.cloned.1.call-start
  9.1 0.7 convert_element_type.15
  9.8 1.4 copy.29.expert_ref
  11.2 1.2 dynamic-slice
  13.1 0.8 convert_reduce_fusion
  13.9 0.2 dynamic-update-slice
  14.1 13.9 %all-reduce = s32[256]{0:T(256)S(1)} all-reduce(s32[256]{0:T(256)S(1)} %dynamic-update-slice), channel_id=2, replica_groups=mesh['groups'=2,'expert'=16] {'expert'}, use_global_device_ids=true, to_apply=%add | all-reduce | flops 256 | bytes 2048
  28.0 0.1 reshape.18
  28.1 0.1 select_reduce_fusion
  28.2 0.1 broadcast_in_dim.26
  28.3 0.7 broadcast_in_dim_reshape.6.prior_ref
  28.9 0.1 broadcast_in_dim.27
  29.0 0.7 broadcast_in_dim_reshape.7.capacity_ref
  29.6 1.4 copy.30.gate_ref
  31.1 1.4 copy.31.curvature_ref
  32.4 4.1 %copy.28 = bf16[8,128,1024]{2,1,0:T(8,128)(2,1)} copy(bf16[8,128,1024]{2,0,1:T(8,128)(2,1)} %bitcast.21) | data formatting | bytes 4194304 | tf_op jit(solution)/shard_map/transpose | solution.py:148
  36.6 38.4 %all-gather.3.cloned.1.call-done.factor_ref = f32[16,2,16,3072]{3,2,1,0:T(8,128)} async-done(((f32[1,2,16,3072]{3,2,1,0:T(8,128)}), f32[16,2,16,3072]{3,2,1,0:T(8,128)}) %all-gather.3.cloned.1.call-update) | async-done | bytes 6291472 | tf_op jit(solution)/shard_map/all_gather | solution.py:147
  75.0 16.3 %shard_map.129 = f32[16,2,16,3072]{3,2,1,0:T(8,128)} custom-call(bf16[1024,1024]{1,0:T(8,128)(2,1)} %bitcast.20, s32[128,8]{1,0:T(8,128)} %copy.29.expert_ref, f32[128,8]{1,0:T(8,128)} %copy.30.gate_ref, f32[1,256]{1,0:T(1,128)} %broadcast_in_dim_reshape.6.prior_ref, f32[1,256]{1,0:T(1,128)} %broadcast_in_dim_reshape.7.capacity_ref, ...), custom_call_target="tpu_custom_call" | custom-call | tf_op jit(solution)/shard_map/pallas_call | solution.py:149
  91.3 84.0 %reduce-scatter.2.cloned.1.call-done = f32[1,2,16,3072]{3,2,1,0:T(8,128)} async-done(((f32[16,2,16,3072]{3,2,1,0:T(8,128)}), f32[1,2,16,3072]{3,2,1,0:T(8,128)}) %reduce-scatter.2.cloned.1.call-update) | async-done | bytes 393232 | tf_op jit(solution)/shard_map/reduce_scatter | solution.py:164
  175.3 0.9 slice_bitcast_fusion.2
  176.2 0.7 slice_bitcast_fusion.3
  176.9 1.7 slice_bitcast_fusion
  (6 shorter events, 0.1 us)
Async XLA Ops:
  7.2 67.8 %all-gather.3.cloned.1.call-start = ((), (), s32[]{:S(2)}) async-start(), calls=%async_computation.1 | async-start | bytes 6684672 | tf_op jit(solution)/shard_map/all_gather | solution.py:147
  9.1 166.2 %reduce-scatter.2.cloned.1.call-start = ((), (), s32[]{:S(2)}) async-start(), calls=%async_computation.2 | async-start | bytes 6684672 | tf_op jit(solution)/shard_map/reduce_scatter | solution.py:164
Sparse Core Ops, SparseCore 0:
  10.3 64.6 all-gather.2
  91.4 83.8 reduce-scatter.1

commit v2 on v1

--- a/solution.py
+++ b/solution.py
@@ -10,6 +10,10 @@
 adapter_scale = 2.0
 f32 = jnp.float32
 bf16 = jnp.bfloat16
+f16 = jnp.float16
+lanes = 128
+down_scale = 2.0**18
+up_scale = 2.0**15
 kernel_vmem = 56 * 2**20
 
 
@@ -35,21 +39,21 @@
     hidden_ref,
     expert_ref,
     gate_ref,
+    column_ref,
     prior_ref,
     capacity_ref,
     gradient_ref,
     curvature_ref,
     factor_ref,
-    out_ref,
-    left_ref,
+    *rest,
 ):
-    experts, _, rank, _ = factor_ref.shape
+    slots, _, rank, _ = factor_ref.shape
+    out_refs, left_ref = rest[:slots], rest[slots]
     tokens, top = expert_ref.shape
-    wide = experts * rank
+    wide = slots * rank
     model_width = gradient_ref.shape[1]
-    column_expert = lax.broadcasted_iota(jnp.int32, (tokens, wide), 1) // rank
-
-    named = [expert_ref[:, k : k + 1] == column_expert for k in range(top)]
+
+    named = [expert_ref[:, k : k + 1] == column_ref[...] for k in range(top)]
     gate = jnp.zeros((tokens, wide), f32)
     member = jnp.zeros((tokens, wide), f32)
     for k in range(top):
@@ -82,30 +86,86 @@
     out_tangent = dot_pairs(weighted_du, adapter_up, 1, 0) + dot_pairs(weighted_u, up_direction, 1, 0)
     resid = halves(curvature_ref[...] * out_tangent)
 
+    def put(kind, start, value):
+        for slot in range(slots):
+            out_refs[slot][kind, :, start : start + value.shape[1]] = value[slot * rank : (slot + 1) * rank]
+
     gradient = gradient_ref[...]
-    up_shape = (experts, rank, model_width)
-    up_gradient = dot(weighted_u[0], gradient, 0, 0) + dot(weighted_u[1], gradient, 0, 0)
-    out_ref[:, 1, :, hidden_width:] = up_gradient.reshape(up_shape)
-    up_curvature = (
+    put(1, hidden_width, dot(weighted_u[0], gradient, 0, 0) + dot(weighted_u[1], gradient, 0, 0))
+    put(
+        0,
+        hidden_width,
         dot(weighted_du[0], gradient, 0, 0)
         + dot(weighted_du[1], gradient, 0, 0)
-        + dot_pairs(weighted_u, resid, 0, 0)
-    )
-    out_ref[:, 0, :, hidden_width:] = up_curvature.reshape(up_shape)
+        + dot_pairs(weighted_u, resid, 0, 0),
+    )
 
     to_gradient = weight * dot_exact_left(gradient, adapter_up, 1, 1)
     to_curvature = weight * (
         dot_pairs(resid, adapter_up, 1, 1) + dot_exact_left(gradient, up_direction, 1, 1)
     )
-    down_shape = (experts, rank, hidden_width)
     for kind, terms in ((1, to_gradient), (0, to_curvature)):
         for part, half in enumerate(halves(terms)):
             for k in range(top):
                 left_ref[part, k * tokens : (k + 1) * tokens] = jnp.where(
                     named[k], half, jnp.zeros_like(half)
                 )
-        down = dot(left_ref[0], hidden_ref[...], 0, 0) + dot(left_ref[1], hidden_ref[...], 0, 0)
-        out_ref[:, kind, :, :hidden_width] = down.reshape(down_shape)
+        put(kind, 0, dot(left_ref[0], hidden_ref[...], 0, 0) + dot(left_ref[1], hidden_ref[...], 0, 0))
+
+
+class Ring:
+    def __init__(self, size):
+        self.length = size // 2
+        rows = self.length // 2
+        self.order = [4 * z for z in range(rows)] + [4 * z + 2 for z in reversed(range(rows))]
+
+    def pairs(self, step):
+        return [
+            (chip + core, self.order[(place + step) % self.length] + core)
+            for place, chip in enumerate(self.order)
+            for core in range(2)
+        ]
+
+    def shift(self, value, step):
+        return lax.ppermute(value, "expert", self.pairs(step))
+
+    def swap(self, value):
+        return lax.ppermute(value, "expert", [(i, i ^ 1) for i in range(2 * self.length)])
+
+    def members(self):
+        me = lax.axis_index("expert")
+        rows = self.length // 2
+        place = jnp.where(me // 2 % 2 == 0, me // 4, self.length - 1 - me // 4)
+        slot = jnp.arange(2 * self.length, dtype=jnp.int32)
+        there = (place + slot // 2) % self.length
+        chip = jnp.where(there < rows, 4 * there, 4 * (self.length - 1 - there) + 2)
+        return chip + (me + slot) % 2
+
+    def gather(self, own):
+        half = self.length // 2
+        found = {0: own}
+        ahead, behind = own, own
+        for step in range(1, half):
+            behind = self.shift(behind, 1)
+            ahead = self.shift(ahead, -1)
+            found[self.length - step], found[step] = behind, ahead
+        found[half] = jnp.concatenate([self.shift(behind[:1], 1), self.shift(ahead[1:], -1)])
+        return [[found[offset], self.swap(found[offset])] for offset in range(self.length)]
+
+    def scatter(self, chunks, encode, decode):
+        half = self.length // 2
+        mine = {}
+        for offset in [half] + [o for step in range(half - 1, 0, -1) for o in (step, -step)] + [0]:
+            own, other = chunks[offset % self.length]
+            mine[offset] = own + self.swap(other)
+        forward = decode(self.shift(encode(mine[half][:1]), 1))
+        backward = decode(self.shift(encode(mine[half][1:]), -1))
+        onward = jnp.concatenate([forward, jnp.zeros_like(forward)])
+        back = jnp.concatenate([jnp.zeros_like(backward), backward])
+        for step in range(half - 1, 0, -1):
+            onward = decode(self.shift(encode(mine[step] + onward), 1))
+            back = decode(self.shift(encode(mine[-step] + back), -1))
+        return mine[0] + onward + back
 
 
 def gathered_plan(
@@ -120,51 +180,78 @@
     down_direction,
     up_direction,
 ):
-    group_size = lax.axis_size("expert")
+    ring = Ring(lax.axis_size("expert"))
     tokens, top = expert_of_route.shape
     hidden_width = hidden_of_route.shape[2]
-    resident, _, rank = adapter_down.shape
+    _, _, rank = adapter_down.shape
     model_width = output_gradient.shape[1]
-    experts = resident * group_size
-    wide = experts * rank
+    experts = capacity.shape[0]
+    width = hidden_width + model_width
 
     names = jnp.arange(experts, dtype=jnp.int32)
     counts = jnp.sum((expert_of_route[:, :, None] == names).astype(jnp.int32), axis=(0, 1))
-    all_counts = lax.all_gather(counts, "expert")
-    earlier = jnp.arange(group_size)[:, None] < lax.axis_index("expert")
-    prior = jnp.sum(jnp.where(earlier, all_counts, 0), axis=0)
-
-    def by_column(per_expert):
-        return jnp.repeat(per_expert.astype(f32), rank)[None, :]
-
-    own = jnp.stack(
+
+    own = jnp.concatenate(
         [
-            jnp.concatenate([down_direction.transpose(0, 2, 1), adapter_up], axis=2),
-            jnp.concatenate([adapter_down.transpose(0, 2, 1), up_direction], axis=2),
+            down_scale * jnp.concatenate([down_direction, adapter_down]).transpose(0, 2, 1),
+            up_scale * jnp.concatenate([adapter_up, up_direction]),
+            jnp.broadcast_to(jnp.pad(counts.astype(f32), (0, lanes - experts)), (2, rank, lanes)),
         ],
-        axis=1,
-    )
-    factors = lax.all_gather(own, "expert", axis=0, tiled=True)
+        axis=2,
+    ).astype(f16)
+    gathered = jnp.stack([piece for pair in ring.gather(own) for piece in pair])
+    factors = jnp.concatenate(
+        [
+            gathered[..., :hidden_width].astype(f32) * (1 / down_scale),
+            gathered[..., hidden_width:width].astype(f32) * (1 / up_scale),
+        ],
+        axis=3,
+    )
+    members = ring.members()
+    all_counts = gathered[:, 0, 0, width : width + experts].astype(f32)
+    earlier = members[:, None] < lax.axis_index("expert")
+    prior = jnp.sum(jnp.where(earlier, all_counts, 0.0), axis=0)
+
+    def by_column(per_slot):
+        return jnp.repeat(per_slot, rank)[None, :]
+
+    def of_slot(per_expert):
+        return jnp.sum(jnp.where(members[:, None] == names, per_expert, 0), axis=1)
+
     hidden_by_position = hidden_of_route.transpose(1, 0, 2).reshape(top * tokens, hidden_width)
+    chunk = jax.ShapeDtypeStruct((2, rank, width), f32)
     partial_sums = pl.pallas_call(
         functools.partial(token_kernel, hidden_width),
-        out_shape=jax.ShapeDtypeStruct((experts, 2, rank, hidden_width + model_width), f32),
-        scratch_shapes=[pltpu.VMEM((2, top * tokens, wide), bf16)],
+        out_shape=[chunk] * experts,
+        scratch_shapes=[pltpu.VMEM((2, top * tokens, experts * rank), bf16)],
         compiler_params=pltpu.CompilerParams(vmem_limit_bytes=kernel_vmem),
     )(
         hidden_by_position,
         expert_of_route,
         gate_of_route.astype(f32),
-        by_column(prior),
-        by_column(capacity),
+        by_column(members),
+        by_column(of_slot(prior)),
+        by_column(of_slot(capacity).astype(f32)),
         output_gradient,
         curvature[:, None],
         factors,
     )
-    summed = lax.psum_scatter(partial_sums, "expert", scatter_dimension=0, tiled=True)
-    down = summed[..., :hidden_width].transpose(0, 1, 3, 2)
+
+    def encode(value):
+        largest = jnp.max(jnp.abs(value), axis=2, keepdims=True)
+        exponent = jnp.ceil(jnp.log2(jnp.maximum(largest, 1e-30)))
+        scaled = value * jnp.exp2(15.0 - exponent)
+        extra = jnp.broadcast_to(exponent, value.shape[:2] + (lanes,))
+        return jnp.concatenate([scaled, extra], axis=2).astype(f16)
+
+    def decode(coded):
+        return coded[..., :width].astype(f32) * jnp.exp2(coded[..., width : width + 1].astype(f32) - 15.0)
+
+    pairs = [partial_sums[2 * offset : 2 * offset + 2] for offset in range(ring.length)]
+    summed = ring.scatter(pairs, encode, decode)
+    down = summed[..., :hidden_width].transpose(0, 2, 1)
     up = summed[..., hidden_width:]
-    return down[:, 1], up[:, 1], down[:, 0], up[:, 0]
+    return down[1:], up[1:], down[:1], up[:1]
 
 
 def carried_in(value, axis, join, neutral):

time: 186 us -> 122 us (0.66)
  waiting for transfers between devices: 122 us -> 44.7 us
  starting transfers between devices: 0.08 us -> 19.3 us
  other arithmetic: 3.4 us -> 22.4 us
  blocking collectives: 13.9 us -> 0 us
  between operations: 14.7 us -> 1.09 us
  local copies, waits for them, and re-layouts: 14.6 us -> 17.7 us
    reduce_scatter x1 -> x0, waiting for transfers between devices: 84 us -> none  [gathered_plan(): lax.psum_scatter(partial_sums, 'expert', scatter_dimension=0, tiled=True)]
    ppermute x0 -> x32, waiting for transfers between devices: none -> 44.7 us  [the longest x16 41.2 us: shift(): return lax.ppermute(value, 'expert', self.pairs(step))]
    all_gather x1 -> x0, waiting for transfers between devices: 38.4 us -> none  [gathered_plan(): factors = lax.all_gather(own, 'expert', axis=0, tiled=True)]
    ppermute x0 -> x32, starting transfers between devices: none -> 19.3 us  [the longest x16 17.4 us: shift(): return lax.ppermute(value, 'expert', self.pairs(step))]
    unnamed x1 -> x0, blocking collectives: 13.9 us -> none
    concatenate x0 -> x11, other arithmetic: none -> 7.54 us  [the longest x1 5.41 us: gathered_plan(): jnp.concatenate([gathered[..., :hidden_width].astype(f32) * (1 / down_sca...]
    mul x0 -> x4, other arithmetic: none -> 5.74 us  [the longest x1 4.07 us: gathered_plan(): gathered[..., hidden_width:width].astype(f32) * (1 / up_scale)]
    unnamed x4 -> x36, local copies, waits for them, and re-layouts: 2.9 us -> 6.56 us
  transfers between devices with their start and end apart: 2 -> 32, of which waited for: 2 -> 14; matrix products, arithmetic and copies ran while one was open for 7% -> 18% of each run, Pallas kernels for 0% -> 0%
where the time goes in v2:
time: 122 us
  waiting for transfers between devices  44.7 us (37%)
  other arithmetic  22.4 us (18%)
  starting transfers between devices  19.3 us (16%)
  local copies, waits for them, and re-layouts  17.7 us (15%)
  Pallas kernels  16.3 us (13%)
    ppermute x16, waiting for transfers between devices, shift(): return lax.ppermute(value, 'expert', self.pairs(step))  41.2 us
    ppermute x16, starting transfers between devices, shift(): return lax.ppermute(value, 'expert', self.pairs(step))  17.4 us
    pallas_call x1, Pallas kernels, gathered_plan(): pl.pallas_call(functools.partial(token_kernel, hidden_width), out_shape=[...  16.3 us
    unnamed x36, local copies, waits for them, and re-layouts  6.56 us
    concatenate x1, other arithmetic, gathered_plan(): jnp.concatenate([gathered[..., :hidden_width].astype(f32) * (1 / down_sca...  5.41 us
    transpose x1, local copies, waits for them, and re-layouts, gathered_plan(): hidden_of_route.transpose(1, 0, 2).reshape(top * tokens, hidden_width)  4.09 us
    mul x1, other arithmetic, gathered_plan(): gathered[..., hidden_width:width].astype(f32) * (1 / up_scale)  4.07 us
    ppermute x16, waiting for transfers between devices, swap(): lax.ppermute(value, 'expert', [(i, i ^ 1) for i in range(2 * self.length)])  3.52 us
  transfers between devices with their start and end apart: 32, of which 14 were waited for; matrix products, arithmetic and copies ran while one was open for 18% of the time, Pallas kernels for 0%

profile of v2, /device:TPU:0, one launch (start us, length us, event | category | flops | bytes accessed | tf_op | source)
XLA Modules:
  0.0 121.5 jit_solution(2397781451553057611)
XLA Ops:
  4.1 3.0 %collective-permute-start.7 = (f16[2,16,3200]{2,1,0:T(8,128)(2,1)}, f16[2,16,3200]{2,1,0:T(8,128)(2,1)}, u32[]{:S(2)}, u32[]{:S(2)}) collective-permute-start(f16[2,16,3200]{2,1,0:T(8,128)(2,1)} %maximum_maximum_fusion), channel_id=1, source_target_pairs={{0,4},{1,5},{4,8},{5,9},{8,12},{9,13},{12,14},{13,15},{14,10},{15,... | collective-permute-start | bytes 614408 | tf_op jit(solution)/shard_map/ppermute | solution.py:130
  14.8 4.1 %copy.28 = bf16[8,128,1024]{2,1,0:T(8,128)(2,1)} copy(bf16[8,128,1024]{2,0,1:T(8,128)(2,1)} %bitcast.44) | data formatting | bytes 4194304 | tf_op jit(solution)/shard_map/transpose | solution.py:221
  19.5 2.0 %collective-permute-start.8 = (f16[2,16,3200]{2,1,0:T(8,128)(2,1)}, f16[2,16,3200]{2,1,0:T(8,128)(2,1)S(1)}, u32[]{:S(2)}, u32[]{:S(2)}) collective-permute-start(f16[2,16,3200]{2,1,0:T(8,128)(2,1)} %collective-permute-done.7), channel_id=1, source_target_pairs={{0,4},{1,5},{4,8},{5,9},{8,12},{9,13},{12,14},{13,15},{14,10},{15,... | collective-permute-start | bytes 614408 | tf_op jit(solution)/shard_map/ppermute | solution.py:130
  23.5 3.5 %collective-permute-done.8 = f16[2,16,3200]{2,1,0:T(8,128)(2,1)S(1)} collective-permute-done((f16[2,16,3200]{2,1,0:T(8,128)(2,1)}, f16[2,16,3200]{2,1,0:T(8,128)(2,1)S(1)}, u32[]{:S(2)}, u32[]{:S(2)}) %collective-permute-start.8) | collective-permute-done | bytes 204832 | tf_op jit(solution)/shard_map/ppermute | solution.py:130
  27.0 1.8 %collective-permute-start.9 = (f16[2,16,3200]{2,1,0:T(8,128)(2,1)S(1)}, f16[2,16,3200]{2,1,0:T(8,128)(2,1)S(1)}, u32[]{:S(2)}, u32[]{:S(2)}) collective-permute-start(f16[2,16,3200]{2,1,0:T(8,128)(2,1)S(1)} %collective-permute-done.8), channel_id=1, source_target_pairs={{0,4},{1,5},{4,8},{5,9},{8,12},{9,13},{12,14},{13,15},{14,10},{15,... | collective-permute-start | bytes 614408 | tf_op jit(solution)/shard_map/ppermute | solution.py:130
  29.2 5.3 %collective-permute-done.9 = f16[2,16,3200]{2,1,0:T(8,128)(2,1)S(1)} collective-permute-done((f16[2,16,3200]{2,1,0:T(8,128)(2,1)S(1)}, f16[2,16,3200]{2,1,0:T(8,128)(2,1)S(1)}, u32[]{:S(2)}, u32[]{:S(2)}) %collective-permute-start.9) | collective-permute-done | bytes 204832 | tf_op jit(solution)/shard_map/ppermute | solution.py:130
  34.5 1.9 %collective-permute-start.10 = (f16[1,16,3200]{2,1,0:T(8,128)(2,1)S(1)}, f16[1,16,3200]{2,1,0:T(8,128)(2,1)S(1)}, u32[]{:S(2)}, u32[]{:S(2)}) collective-permute-start(f16[1,16,3200]{2,1,0:T(8,128)(2,1)S(1)} %slice.115), channel_id=1, source_target_pairs={{0,4},{1,5},{4,8},{5,9},{8,12},{9,13},{12,14},{13,15},{14,10},{15,... | collective-permute-start | bytes 307208 | tf_op jit(solution)/shard_map/ppermute | solution.py:130
  36.9 2.3 %collective-permute-done.10 = f16[1,16,3200]{2,1,0:T(8,128)(2,1)S(1)} collective-permute-done((f16[1,16,3200]{2,1,0:T(8,128)(2,1)S(1)}, f16[1,16,3200]{2,1,0:T(8,128)(2,1)S(1)}, u32[]{:S(2)}, u32[]{:S(2)}) %collective-permute-start.10) | collective-permute-done | bytes 102432 | tf_op jit(solution)/shard_map/ppermute | solution.py:130
  39.2 2.1 %collective-permute-done.11 = f16[1,16,3200]{2,1,0:T(8,128)(2,1)S(1)} collective-permute-done((f16[1,16,3200]{2,1,0:T(8,128)(2,1)S(1)}, f16[1,16,3200]{2,1,0:T(8,128)(2,1)S(1)}, u32[]{:S(2)}, u32[]{:S(2)}) %collective-permute-start.11) | collective-permute-done | bytes 102432 | tf_op jit(solution)/shard_map/ppermute | solution.py:130
  44.1 1.7 %copy-done = f16[16,2,16,3200]{3,2,1,0:T(8,128)(2,1)} copy-done((f16[16,2,16,3200]{3,2,1,0:T(8,128)(2,1)}, f16[16,2,16,3200]{3,2,1,0:T(8,128)(2,1)S(1)}, u32[]{:S(2)}) %copy-start) | copy-done | bytes 3276824
  47.3 4.1 %convert_multiply_fusion = f32[16,2,16,2048]{3,2,1,0:T(8,128)} fusion(f16[16,2,16,3200]{3,2,1,0:T(8,128)(2,1)} %copy-done), kind=kLoop, calls=%fused_computation.1 | loop fusion | flops 2097152 | bytes 6291456 | tf_op jit(solution)/shard_map/mul | solution.py:206
  52.3 5.4 %pad_maximum_fusion.factor_ref = f32[16,2,16,3072]{3,2,1,0:T(8,128)} fusion(f32[16,2,16,2048]{3,2,1,0:T(8,128)} %convert_multiply_fusion, f32[16,2,16,1024]{3,2,1,0:T(8,128)S(1)} %convert_multiply_fusion.1), kind=kLoop, calls=%fused_computation | loop fusion | flops 1572864 | bytes 12582912 | tf_op jit(solution)/shard_map/concatenate | solution.py:203
  57.7 16.3 %shard_map.129 = (f32[2,16,3072]{2,1,0:T(8,128)}, f32[2,16,3072]{2,1,0:T(8,128)}, f32[2,16,3072]{2,1,0:T(8,128)}, f32[2,16,3072]{2,1,0:T(8,128)}, f32[2,16,3072]...) custom-call(bf16[1024,1024]{1,0:T(8,128)(2,1)} %bitcast.43, ...), custom_call_target="tpu_custom_call" | custom-call | tf_op jit(solution)/shard_map/pallas_call | solution.py:223
  77.5 1.6 %collective-permute-start.21 = (f16[1,16,3200]{2,1,0:T(8,128)(2,1)S(1)}, f16[1,16,3200]{2,1,0:T(8,128)(2,1)S(1)}, u32[]{:S(2)}, u32[]{:S(2)}) collective-permute-start(f16[1,16,3200]{2,1,0:T(8,128)(2,1)S(1)} %pad_maximum_fusion.7), channel_id=1, source_target_pairs={{0,4},{1,5},{4,8},{5,9},{8,12},{9,13},{12,14},{13,15},{14,10},{15,... | collective-permute-start | bytes 307208 | tf_op jit(solution)/shard_map/ppermute | solution.py:130
  79.2 3.2 %collective-permute-done.21 = f16[1,16,3200]{2,1,0:T(8,128)(2,1)S(1)} collective-permute-done((f16[1,16,3200]{2,1,0:T(8,128)(2,1)S(1)}, f16[1,16,3200]{2,1,0:T(8,128)(2,1)S(1)}, u32[]{:S(2)}, u32[]{:S(2)}) %collective-permute-start.21) | collective-permute-done | bytes 102432 | tf_op jit(solution)/shard_map/ppermute | solution.py:130
  84.2 3.8 %collective-permute-done.28 = f16[1,16,3200]{2,1,0:T(8,128)(2,1)S(1)} collective-permute-done((f16[1,16,3200]{2,1,0:T(8,128)(2,1)S(1)}, f16[1,16,3200]{2,1,0:T(8,128)(2,1)S(1)}, u32[]{:S(2)}, u32[]{:S(2)}) %collective-permute-start.28) | collective-permute-done | bytes 102432 | tf_op jit(solution)/shard_map/ppermute | solution.py:130
  89.8 1.6 %collective-permute-start.22 = (f16[2,16,3200]{2,1,0:T(8,128)(2,1)S(1)}, f16[2,16,3200]{2,1,0:T(8,128)(2,1)S(1)}, u32[]{:S(2)}, u32[]{:S(2)}) collective-permute-start(f16[2,16,3200]{2,1,0:T(8,128)(2,1)S(1)} %pad_maximum_fusion.1), channel_id=1, source_target_pairs={{0,4},{1,5},{4,8},{5,9},{8,12},{9,13},{12,14},{13,15},{14,10},{15,... | collective-permute-start | bytes 614408 | tf_op jit(solution)/shard_map/ppermute | solution.py:130
  91.7 5.1 %collective-permute-done.22 = f16[2,16,3200]{2,1,0:T(8,128)(2,1)S(1)} collective-permute-done((f16[2,16,3200]{2,1,0:T(8,128)(2,1)S(1)}, f16[2,16,3200]{2,1,0:T(8,128)(2,1)S(1)}, u32[]{:S(2)}, u32[]{:S(2)}) %collective-permute-start.22) | collective-permute-done | bytes 204832 | tf_op jit(solution)/shard_map/ppermute | solution.py:130
  97.8 6.7 %collective-permute-done.29 = f16[2,16,3200]{2,1,0:T(8,128)(2,1)S(1)} collective-permute-done((f16[2,16,3200]{2,1,0:T(8,128)(2,1)S(1)}, f16[2,16,3200]{2,1,0:T(8,128)(2,1)S(1)}, u32[]{:S(2)}, u32[]{:S(2)}) %collective-permute-start.29) | collective-permute-done | bytes 204832 | tf_op jit(solution)/shard_map/ppermute | solution.py:130
  104.5 1.6 %collective-permute-start.23 = (f16[2,16,3200]{2,1,0:T(8,128)(2,1)S(1)}, f16[2,16,3200]{2,1,0:T(8,128)(2,1)S(1)}, u32[]{:S(2)}, u32[]{:S(2)}) collective-permute-start(f16[2,16,3200]{2,1,0:T(8,128)(2,1)S(1)} %pad_maximum_fusion.2), channel_id=1, source_target_pairs={{0,4},{1,5},{4,8},{5,9},{8,12},{9,13},{12,14},{13,15},{14,10},{15,... | collective-permute-start | bytes 614408 | tf_op jit(solution)/shard_map/ppermute | solution.py:130
  107.2 4.0 %collective-permute-done.23 = f16[2,16,3200]{2,1,0:T(8,128)(2,1)S(1)} collective-permute-done((f16[2,16,3200]{2,1,0:T(8,128)(2,1)S(1)}, f16[2,16,3200]{2,1,0:T(8,128)(2,1)S(1)}, u32[]{:S(2)}, u32[]{:S(2)}) %collective-permute-start.23) | collective-permute-done | bytes 204832 | tf_op jit(solution)/shard_map/ppermute | solution.py:130
  111.8 1.6 %collective-permute-start.24 = (f16[2,16,3200]{2,1,0:T(8,128)(2,1)S(1)}, f16[2,16,3200]{2,1,0:T(8,128)(2,1)S(1)}, u32[]{:S(2)}, u32[]{:S(2)}) collective-permute-start(f16[2,16,3200]{2,1,0:T(8,128)(2,1)S(1)} %pad_maximum_fusion.3), channel_id=1, source_target_pairs={{0,4},{1,5},{4,8},{5,9},{8,12},{9,13},{12,14},{13,15},{14,10},{15,... | collective-permute-start | bytes 614408 | tf_op jit(solution)/shard_map/ppermute | solution.py:130
  114.5 3.1 %collective-permute-done.24 = f16[2,16,3200]{2,1,0:T(8,128)(2,1)S(1)} collective-permute-done((f16[2,16,3200]{2,1,0:T(8,128)(2,1)S(1)}, f16[2,16,3200]{2,1,0:T(8,128)(2,1)S(1)}, u32[]{:S(2)}, u32[]{:S(2)}) %collective-permute-start.24) | collective-permute-done | bytes 204832 | tf_op jit(solution)/shard_map/ppermute | solution.py:130
  117.8 2.1 %collective-permute-done.31 = f16[2,16,3200]{2,1,0:T(8,128)(2,1)S(1)} collective-permute-done((f16[2,16,3200]{2,1,0:T(8,128)(2,1)S(1)}, f16[2,16,3200]{2,1,0:T(8,128)(2,1)S(1)}, u32[]{:S(2)}, u32[]{:S(2)}) %collective-permute-start.31) | collective-permute-done | bytes 204832 | tf_op jit(solution)/shard_map/ppermute | solution.py:130
  (161 shorter events, 32.6 us)
Async XLA Ops:
  4.1 14.8 %collective-permute-start.7 = (f16[2,16,3200]{2,1,0:T(8,128)(2,1)}, f16[2,16,3200]{2,1,0:T(8,128)(2,1)}, u32[]{:S(2)}, u32[]{:S(2)}) collective-permute-start(f16[2,16,3200]{2,1,0:T(8,128)(2,1)} %maximum_maximum_fusion), channel_id=1, source_target_pairs={{0,4},{1,5},{4,8},{5,9},{8,12},{9,13},{12,14},{13,15},{14,10},{15,... | collective-permute-start | bytes 614408 | tf_op jit(solution)/shard_map/ppermute | solution.py:130
  7.1 14.4 %collective-permute-start.1 = (f16[2,16,3200]{2,1,0:T(8,128)(2,1)}, f16[2,16,3200]{2,1,0:T(8,128)(2,1)}, u32[]{:S(2)}, u32[]{:S(2)}) collective-permute-start(f16[2,16,3200]{2,1,0:T(8,128)(2,1)} %maximum_maximum_fusion), channel_id=1, source_target_pairs={{0,2},{1,3},{4,0},{5,1},{8,4},{9,5},{12,8},{13,9},{14,12},{15,13},... | collective-permute-start | bytes 614408 | tf_op jit(solution)/shard_map/ppermute | solution.py:130
  7.1 14.4 %collective-permute-start = (f16[2,16,3200]{2,1,0:T(8,128)(2,1)}, f16[2,16,3200]{2,1,0:T(8,128)(2,1)}, u32[]{:S(2)}, u32[]{:S(2)}) collective-permute-start(f16[2,16,3200]{2,1,0:T(8,128)(2,1)} %maximum_maximum_fusion), channel_id=1, source_target_pairs={{0,1},{1,0},{2,3},{3,2},{4,5},{5,4},{6,7},{7,6},{8,9},{9,8},{10,11... | collective-permute-start | bytes 614408 | tf_op jit(solution)/shard_map/ppermute | solution.py:133
  18.9 25.1 %collective-permute-start.15 = (f16[2,16,3200]{2,1,0:T(8,128)(2,1)}, f16[2,16,3200]{2,1,0:T(8,128)(2,1)S(1)}, u32[]{:S(2)}, u32[]{:S(2)}) collective-permute-start(f16[2,16,3200]{2,1,0:T(8,128)(2,1)} %collective-permute-done.7), channel_id=1, source_target_pairs={{0,1},{1,0},{2,3},{3,2},{4,5},{5,4},{6,7},{7,6},{8,9},{9,8},{10,11... | collective-permute-start | bytes 614408 | tf_op jit(solution)/shard_map/ppermute | solution.py:133
  19.5 7.5 %collective-permute-start.8 = (f16[2,16,3200]{2,1,0:T(8,128)(2,1)}, f16[2,16,3200]{2,1,0:T(8,128)(2,1)S(1)}, u32[]{:S(2)}, u32[]{:S(2)}) collective-permute-start(f16[2,16,3200]{2,1,0:T(8,128)(2,1)} %collective-permute-done.7), channel_id=1, source_target_pairs={{0,4},{1,5},{4,8},{5,9},{8,12},{9,13},{12,14},{13,15},{14,10},{15,... | collective-permute-start | bytes 614408 | tf_op jit(solution)/shard_map/ppermute | solution.py:130
  21.5 7.3 %collective-permute-start.3 = (f16[2,16,3200]{2,1,0:T(8,128)(2,1)}, f16[2,16,3200]{2,1,0:T(8,128)(2,1)S(1)}, u32[]{:S(2)}, u32[]{:S(2)}) collective-permute-start(f16[2,16,3200]{2,1,0:T(8,128)(2,1)} %collective-permute-done.1), channel_id=1, source_target_pairs={{0,2},{1,3},{4,0},{5,1},{8,4},{9,5},{12,8},{13,9},{14,12},{15,13},... | collective-permute-start | bytes 614408 | tf_op jit(solution)/shard_map/ppermute | solution.py:130
  21.5 7.5 %collective-permute-start.2 = (f16[2,16,3200]{2,1,0:T(8,128)(2,1)}, f16[2,16,3200]{2,1,0:T(8,128)(2,1)S(1)}, u32[]{:S(2)}, u32[]{:S(2)}) collective-permute-start(f16[2,16,3200]{2,1,0:T(8,128)(2,1)} %collective-permute-done.1), channel_id=1, source_target_pairs={{0,1},{1,0},{2,3},{3,2},{4,5},{5,4},{6,7},{7,6},{8,9},{9,8},{10,11... | collective-permute-start | bytes 614408 | tf_op jit(solution)/shard_map/ppermute | solution.py:133
  27.0 16.1 %collective-permute-start.14 = (f16[2,16,3200]{2,1,0:T(8,128)(2,1)S(1)}, f16[2,16,3200]{2,1,0:T(8,128)(2,1)S(1)}, u32[]{:S(2)}, u32[]{:S(2)}) collective-permute-start(f16[2,16,3200]{2,1,0:T(8,128)(2,1)S(1)} %collective-permute-done.8), channel_id=1, source_target_pairs={{0,1},{1,0},{2,3},{3,2},{4,5},{5,4},{6,7},{7,6},{8,9},{9,8},{10,11... | collective-permute-start | bytes 614408 | tf_op jit(solution)/shard_map/ppermute | solution.py:133
  27.0 7.5 %collective-permute-start.9 = (f16[2,16,3200]{2,1,0:T(8,128)(2,1)S(1)}, f16[2,16,3200]{2,1,0:T(8,128)(2,1)S(1)}, u32[]{:S(2)}, u32[]{:S(2)}) collective-permute-start(f16[2,16,3200]{2,1,0:T(8,128)(2,1)S(1)} %collective-permute-done.8), channel_id=1, source_target_pairs={{0,4},{1,5},{4,8},{5,9},{8,12},{9,13},{12,14},{13,15},{14,10},{15,... | collective-permute-start | bytes 614408 | tf_op jit(solution)/shard_map/ppermute | solution.py:130
  28.8 7.6 %collective-permute-start.5 = (f16[2,16,3200]{2,1,0:T(8,128)(2,1)S(1)}, f16[2,16,3200]{2,1,0:T(8,128)(2,1)S(1)}, u32[]{:S(2)}, u32[]{:S(2)}) collective-permute-start(f16[2,16,3200]{2,1,0:T(8,128)(2,1)S(1)} %collective-permute-done.3), channel_id=1, source_target_pairs={{0,2},{1,3},{4,0},{5,1},{8,4},{9,5},{12,8},{13,9},{14,12},{15,13},... | collective-permute-start | bytes 614408 | tf_op jit(solution)/shard_map/ppermute | solution.py:130
  29.0 7.8 %collective-permute-start.4 = (f16[2,16,3200]{2,1,0:T(8,128)(2,1)S(1)}, f16[2,16,3200]{2,1,0:T(8,128)(2,1)S(1)}, u32[]{:S(2)}, u32[]{:S(2)}) collective-permute-start(f16[2,16,3200]{2,1,0:T(8,128)(2,1)S(1)} %collective-permute-done.3), channel_id=1, source_target_pairs={{0,1},{1,0},{2,3},{3,2},{4,5},{5,4},{6,7},{7,6},{8,9},{9,8},{10,11... | collective-permute-start | bytes 614408 | tf_op jit(solution)/shard_map/ppermute | solution.py:133
  36.8 6.1 %collective-permute-start.13 = (f16[2,16,3200]{2,1,0:T(8,128)(2,1)S(1)}, f16[2,16,3200]{2,1,0:T(8,128)(2,1)S(1)}, u32[]{:S(2)}, u32[]{:S(2)}) collective-permute-start(f16[2,16,3200]{2,1,0:T(8,128)(2,1)S(1)} %collective-permute-done.9), channel_id=1, source_target_pairs={{0,1},{1,0},{2,3},{3,2},{4,5},{5,4},{6,7},{7,6},{8,9},{9,8},{10,11... | collective-permute-start | bytes 614408 | tf_op jit(solution)/shard_map/ppermute | solution.py:133
  74.2 45.7 %collective-permute-start.16 = (f32[2,16,3072]{2,1,0:T(8,128)}, f32[2,16,3072]{2,1,0:T(8,128)S(1)}, u32[]{:S(2)}, u32[]{:S(2)}) collective-permute-start(f32[2,16,3072]{2,1,0:T(8,128)} %get-tuple-element.21), channel_id=1, source_target_pairs={{0,1},{1,0},{2,3},{3,2},{4,5},{5,4},{6,7},{7,6},{8,9},{9,8},{10,11... | collective-permute-start | bytes 1179656 | tf_op jit(solution)/shard_map/ppermute | solution.py:133
  74.6 36.7 %collective-permute-start.17 = (f32[2,16,3072]{2,1,0:T(8,128)}, f32[2,16,3072]{2,1,0:T(8,128)S(1)}, u32[]{:S(2)}, u32[]{:S(2)}) collective-permute-start(f32[2,16,3072]{2,1,0:T(8,128)} %get-tuple-element.23), channel_id=1, source_target_pairs={{0,1},{1,0},{2,3},{3,2},{4,5},{5,4},{6,7},{7,6},{8,9},{9,8},{10,11... | collective-permute-start | bytes 1179656 | tf_op jit(solution)/shard_map/ppermute | solution.py:133
  74.7 22.2 %collective-permute-start.18 = (f32[2,16,3072]{2,1,0:T(8,128)}, f32[2,16,3072]{2,1,0:T(8,128)S(1)}, u32[]{:S(2)}, u32[]{:S(2)}) collective-permute-start(f32[2,16,3072]{2,1,0:T(8,128)} %get-tuple-element.25), channel_id=1, source_target_pairs={{0,1},{1,0},{2,3},{3,2},{4,5},{5,4},{6,7},{7,6},{8,9},{9,8},{10,11... | collective-permute-start | bytes 1179656 | tf_op jit(solution)/shard_map/ppermute | solution.py:133
  75.1 7.6 %collective-permute-start.19 = (f32[2,16,3072]{2,1,0:T(8,128)}, f32[2,16,3072]{2,1,0:T(8,128)S(1)}, u32[]{:S(2)}, u32[]{:S(2)}) collective-permute-start(f32[2,16,3072]{2,1,0:T(8,128)} %get-tuple-element.27), channel_id=1, source_target_pairs={{0,1},{1,0},{2,3},{3,2},{4,5},{5,4},{6,7},{7,6},{8,9},{9,8},{10,11... | collective-permute-start | bytes 1179656 | tf_op jit(solution)/shard_map/ppermute | solution.py:133
  82.5 31.1 %collective-permute-start.25 = (f32[2,16,3072]{2,1,0:T(8,128)}, f32[2,16,3072]{2,1,0:T(8,128)S(1)}, u32[]{:S(2)}, u32[]{:S(2)}) collective-permute-start(f32[2,16,3072]{2,1,0:T(8,128)} %get-tuple-element.31), channel_id=1, source_target_pairs={{0,1},{1,0},{2,3},{3,2},{4,5},{5,4},{6,7},{7,6},{8,9},{9,8},{10,11... | collective-permute-start | bytes 1179656 | tf_op jit(solution)/shard_map/ppermute | solution.py:133
  89.8 7.1 %collective-permute-start.22 = (f16[2,16,3200]{2,1,0:T(8,128)(2,1)S(1)}, f16[2,16,3200]{2,1,0:T(8,128)(2,1)S(1)}, u32[]{:S(2)}, u32[]{:S(2)}) collective-permute-start(f16[2,16,3200]{2,1,0:T(8,128)(2,1)S(1)} %pad_maximum_fusion.1), channel_id=1, source_target_pairs={{0,4},{1,5},{4,8},{5,9},{8,12},{9,13},{12,14},{13,15},{14,10},{15,... | collective-permute-start | bytes 614408 | tf_op jit(solution)/shard_map/ppermute | solution.py:130
  96.9 9.3 %collective-permute-start.26 = (f32[2,16,3072]{2,1,0:T(8,128)S(1)}, f32[2,16,3072]{2,1,0:T(8,128)S(1)}, u32[]{:S(2)}, u32[]{:S(2)}) collective-permute-start(f32[2,16,3072]{2,1,0:T(8,128)S(1)} %copy-done.8), channel_id=1, source_target_pairs={{0,1},{1,0},{2,3},{3,2},{4,5},{5,4},{6,7},{7,6},{8,9},{9,8},{10,11... | collective-permute-start | bytes 1179656 | tf_op jit(solution)/shard_map/ppermute | solution.py:133
  97.0 7.5 %collective-permute-start.29 = (f16[2,16,3200]{2,1,0:T(8,128)(2,1)S(1)}, f16[2,16,3200]{2,1,0:T(8,128)(2,1)S(1)}, u32[]{:S(2)}, u32[]{:S(2)}) collective-permute-start(f16[2,16,3200]{2,1,0:T(8,128)(2,1)S(1)} %pad_maximum_fusion.4), channel_id=1, source_target_pairs={{0,2},{1,3},{4,0},{5,1},{8,4},{9,5},{12,8},{13,9},{14,12},{15,13},... | collective-permute-start | bytes 614408 | tf_op jit(solution)/shard_map/ppermute | solution.py:130
  104.5 6.7 %collective-permute-start.23 = (f16[2,16,3200]{2,1,0:T(8,128)(2,1)S(1)}, f16[2,16,3200]{2,1,0:T(8,128)(2,1)S(1)}, u32[]{:S(2)}, u32[]{:S(2)}) collective-permute-start(f16[2,16,3200]{2,1,0:T(8,128)(2,1)S(1)} %pad_maximum_fusion.2), channel_id=1, source_target_pairs={{0,4},{1,5},{4,8},{5,9},{8,12},{9,13},{12,14},{13,15},{14,10},{15,... | collective-permute-start | bytes 614408 | tf_op jit(solution)/shard_map/ppermute | solution.py:130
  106.7 6.7 %collective-permute-start.30 = (f16[2,16,3200]{2,1,0:T(8,128)(2,1)S(1)}, f16[2,16,3200]{2,1,0:T(8,128)(2,1)S(1)}, u32[]{:S(2)}, u32[]{:S(2)}) collective-permute-start(f16[2,16,3200]{2,1,0:T(8,128)(2,1)S(1)} %pad_maximum_fusion.5), channel_id=1, source_target_pairs={{0,2},{1,3},{4,0},{5,1},{8,4},{9,5},{12,8},{13,9},{14,12},{15,13},... | collective-permute-start | bytes 614408 | tf_op jit(solution)/shard_map/ppermute | solution.py:130
  111.8 5.9 %collective-permute-start.24 = (f16[2,16,3200]{2,1,0:T(8,128)(2,1)S(1)}, f16[2,16,3200]{2,1,0:T(8,128)(2,1)S(1)}, u32[]{:S(2)}, u32[]{:S(2)}) collective-permute-start(f16[2,16,3200]{2,1,0:T(8,128)(2,1)S(1)} %pad_maximum_fusion.3), channel_id=1, source_target_pairs={{0,4},{1,5},{4,8},{5,9},{8,12},{9,13},{12,14},{13,15},{14,10},{15,... | collective-permute-start | bytes 614408 | tf_op jit(solution)/shard_map/ppermute | solution.py:130
  114.0 5.8 %collective-permute-start.31 = (f16[2,16,3200]{2,1,0:T(8,128)(2,1)S(1)}, f16[2,16,3200]{2,1,0:T(8,128)(2,1)S(1)}, u32[]{:S(2)}, u32[]{:S(2)}) collective-permute-start(f16[2,16,3200]{2,1,0:T(8,128)(2,1)S(1)} %pad_maximum_fusion.6), channel_id=1, source_target_pairs={{0,2},{1,3},{4,0},{5,1},{8,4},{9,5},{12,8},{13,9},{14,12},{15,13},... | collective-permute-start | bytes 614408 | tf_op jit(solution)/shard_map/ppermute | solution.py:130
  (18 other events, 181.6 us)

commit v3 on v0

--- a/solution.py
+++ b/solution.py
@@ -1,9 +1,375 @@
+import functools
+
 import jax
 import jax.numpy as jnp
 from jax import lax
+from jax.experimental import pallas as pl
+from jax.experimental.pallas import tpu as pltpu
 from jax.sharding import PartitionSpec as P
 
 adapter_scale = 2.0
+f32 = jnp.float32
+bf16 = jnp.bfloat16
+f16 = jnp.float16
+lanes = 128
+down_scale = 2.0**18
+up_scale = 2.0**15
+kernel_vmem = 32 * 2**20
+
+
+def halves(value):
+    high = value.astype(bf16)
+    return high, (value - high.astype(f32)).astype(bf16)
+
+
+def dot(a, b, a_dim, b_dim):
+    return lax.dot_general(a, b, (((a_dim,), (b_dim,)), ((), ())), preferred_element_type=f32)
+
+
+def dot_pairs(a, b, a_dim, b_dim):
+    return dot(a[0], b[0], a_dim, b_dim) + (dot(a[1], b[0], a_dim, b_dim) + dot(a[0], b[1], a_dim, b_dim))
+
+
+def token_columns(small_ref, top):
+    small = small_ref[...].T
+    experts = [small[:, k : k + 1] for k in range(top)]
+    gates = [small[:, top + k : top + k + 1] for k in range(top)]
+    return experts, gates, small[:, 2 * top : 2 * top + 1]
+
+
+def stacked(refs, kind):
+    return jnp.concatenate([ref[kind] for ref in refs], axis=0)
+
+
+def reduce_kernel(top, slots, small_ref, column_ref, own_ref, other_ref, *rest):
+    factor_refs, reduced_ref = rest[:slots], rest[slots]
+    experts, _, _ = token_columns(small_ref, top)
+    high, low = halves(jnp.concatenate([stacked(factor_refs, 0), stacked(factor_refs, 1)], axis=0))
+    wide = high.shape[0] // 2
+    tokens = own_ref.shape[0] // top
+    for block, hidden_ref in enumerate((own_ref, other_ref)):
+        rows = slice(block * tokens, (block + 1) * tokens)
+        full = dot(hidden_ref[...], high, 1, 1) + dot(hidden_ref[...], low, 1, 1)
+        total = jnp.zeros((tokens, 2 * wide), f32)
+        for k in range(top):
+            named = experts[k][rows] == column_ref[...]
+            total = jnp.where(jnp.concatenate([named, named], axis=1), full[k * tokens : (k + 1) * tokens], total)
+        reduced_ref[0, rows] = total[:, :wide]
+        reduced_ref[1, rows] = total[:, wide:]
+
+
+def tangent_kernel(top, slots, small_ref, column_ref, limit_ref, reduced_ref, *rest):
+    factor_refs = rest[:slots]
+    weight_ref, weighted_ref, tangent_ref, high_ref, low_ref = rest[slots:]
+    experts, gates, _ = token_columns(small_ref, top)
+    tokens, wide = weight_ref.shape
+    block = tokens // 2
+    gate = jnp.zeros((tokens, wide), f32)
+    member = jnp.zeros((tokens, wide), f32)
+    for k in range(top):
+        named = experts[k] == column_ref[...]
+        gate = jnp.where(named, gates[k], gate)
+        member = jnp.where(named, 1.0, member)
+    below = (
+        lax.broadcasted_iota(jnp.int32, (block, block), 0)
+        > lax.broadcasted_iota(jnp.int32, (block, block), 1)
+    )
+    below = jnp.where(below, 1.0, 0.0).astype(bf16)
+    weights = []
+    for part in range(2):
+        rows = slice(part * block, (part + 1) * block)
+        local_rank = dot(below, member[rows].astype(bf16), 1, 0)
+        weights.append(jnp.where(local_rank < limit_ref[part : part + 1], adapter_scale * gate[rows], 0.0))
+    weight = jnp.concatenate(weights, axis=0)
+    weight_ref[...] = weight
+    weighted = jnp.concatenate([weight * reduced_ref[0], weight * reduced_ref[1]], axis=1)
+    weighted_ref[...] = weighted
+    factor = halves(jnp.concatenate([stacked(factor_refs, 0), stacked(factor_refs, 1)], axis=0))
+    high_ref[...], low_ref[...] = factor
+    tangent_ref[...] = dot_pairs(halves(weighted), factor, 1, 0)
+
+
+def put_left(left_ref, experts, column_ref, terms, top):
+    both = jnp.concatenate(halves(terms), axis=1)
+    tokens = terms.shape[0] // 2
+    for block in range(2):
+        rows = slice(block * tokens, (block + 1) * tokens)
+        for k in range(top):
+            named = experts[k][rows] == column_ref[...]
+            named = jnp.concatenate([named, named], axis=1)
+            left_ref[block, k * tokens : (k + 1) * tokens] = jnp.where(named, both[rows], jnp.zeros_like(both[rows]))
+
+
+def add_halves(both, axis):
+    middle = both.shape[axis] // 2
+    if axis == 0:
+        return both[:middle] + both[middle:]
+    return both[:, :middle] + both[:, middle:]
+
+
+def put_chunks(out_refs, start, value):
+    rank, width = out_refs[0].shape[0], value.shape[1]
+    for slot, out_ref in enumerate(out_refs):
+        out_ref[:, start : start + width] = value[slot * rank : (slot + 1) * rank]
+
+
+def gradient_kernel(
+    top,
+    small_ref,
+    column_ref,
+    own_ref,
+    other_ref,
+    own_gradient_ref,
+    other_gradient_ref,
+    weight_ref,
+    weighted_ref,
+    high_ref,
+    low_ref,
+    *rest,
+):
+    out_refs, (up_ref, to_ref, left_ref) = rest[:-3], rest[-3:]
+    experts, _, _ = token_columns(small_ref, top)
+    wide = weight_ref.shape[1]
+    hidden_width = own_ref.shape[1]
+    gradient = jnp.concatenate([own_gradient_ref[...], other_gradient_ref[...]], axis=0)
+    to_both = dot(gradient, high_ref[...], 1, 1) + dot(gradient, low_ref[...], 1, 1)
+    to_ref[...] = to_both[:, wide:]
+    put_left(left_ref, experts, column_ref, weight_ref[...] * to_both[:, :wide], top)
+    down = dot(left_ref[0], own_ref[...], 0, 0) + dot(left_ref[1], other_ref[...], 0, 0)
+    put_chunks(out_refs, 0, add_halves(down, 0))
+    up = add_halves(dot(jnp.concatenate(halves(weighted_ref[...]), axis=1), gradient, 0, 0), 0)
+    up_ref[...] = up[:wide]
+    put_chunks(out_refs, hidden_width, up[wide:])
+
+
+def curvature_kernel(
+    top,
+    small_ref,
+    column_ref,
+    own_ref,
+    other_ref,
+    weight_ref,
+    weighted_ref,
+    high_ref,
+    low_ref,
+    up_ref,
+    to_ref,
+    tangent_ref,
+    arrived_ref,
+    *rest,
+):
+    out_refs, left_ref = rest[:-1], rest[-1]
+    experts, _, curvature = token_columns(small_ref, top)
+    tokens, wide = weight_ref.shape
+    block = tokens // 2
+    hidden_width = own_ref.shape[1]
+    arrived = jnp.concatenate([arrived_ref[block:], arrived_ref[:block]], axis=0)
+    resid = halves(curvature * (tangent_ref[...] + arrived))
+    adapter_up = high_ref[:wide], low_ref[:wide]
+    put_left(
+        left_ref, experts, column_ref, weight_ref[...] * (dot_pairs(resid, adapter_up, 1, 1) + to_ref[...]), top
+    )
+    down = dot(left_ref[0], own_ref[...], 0, 0) + dot(left_ref[1], other_ref[...], 0, 0)
+    put_chunks(out_refs, 0, add_halves(down, 0))
+    weighted_u = halves(weighted_ref[:, wide:])
+    up = add_halves(dot(jnp.concatenate(weighted_u, axis=1), resid[0], 0, 0), 0) + dot(weighted_u[0], resid[1], 0, 0)
+    put_chunks(out_refs, hidden_width, up_ref[...] + up)
+
+
+class Ring:
+    def __init__(self, size):
+        self.length = size // 2
+        rows = self.length // 2
+        self.order = [4 * z for z in range(rows)] + [4 * z + 2 for z in reversed(range(rows))]
+
+    def shift(self, value, step):
+        pairs = [
+            (chip + core, self.order[(place + step) % self.length] + core)
+            for place, chip in enumerate(self.order)
+            for core in range(2)
+        ]
+        return lax.ppermute(value, "expert", pairs)
+
+    def swap(self, value):
+        return lax.ppermute(value, "expert", [(i, i ^ 1) for i in range(2 * self.length)])
+
+    def members(self):
+        me = lax.axis_index("expert")
+        rows = self.length // 2
+        place = jnp.where(me // 2 % 2 == 0, me // 4, self.length - 1 - me // 4)
+        there = (place + jnp.arange(self.length, dtype=jnp.int32)) % self.length
+        return jnp.where(there < rows, 4 * there, 4 * (self.length - 1 - there) + 2) + me % 2
+
+    def gather(self, own):
+        half = self.length // 2
+        found = {0: own}
+        ahead, behind = own, own
+        for step in range(1, half):
+            behind = self.shift(behind, 1)
+            ahead = self.shift(ahead, -1)
+            found[self.length - step], found[step] = behind, ahead
+        found[half] = jnp.concatenate([self.shift(behind[:1], 1), self.shift(ahead[1:], -1)])
+        return [found[offset] for offset in range(self.length)]
+
+    def scatter(self, chunks, longer):
+        half = self.length // 2
+        total = chunks[0]
+        for way in (longer, -longer):
+            start = half if way == longer else half - 1
+            moving = chunks[way * start % self.length]
+            for step in range(start, 0, -1):
+                arrived = decode(self.shift(encode(moving), way))
+                moving = arrived if step == 1 else chunks[way * (step - 1) % self.length] + arrived
+            total = total + moving
+        return total
+
+
+def encode(value):
+    largest = jnp.max(jnp.abs(value), axis=1, keepdims=True)
+    exponent = jnp.ceil(jnp.log2(jnp.maximum(largest, 1e-30)))
+    scaled = value * jnp.exp2(15.0 - exponent)
+    extra = jnp.broadcast_to(exponent, (value.shape[0], lanes))
+    return jnp.concatenate([scaled, extra], axis=1).astype(f16)
+
+
+def decode(coded):
+    width = coded.shape[1] - lanes
+    return coded[:, :width].astype(f32) * jnp.exp2(coded[:, width : width + 1].astype(f32) - 15.0)
+
+
+def gathered_plan(
+    hidden_of_route,
+    expert_of_route,
+    gate_of_route,
+    capacity,
+    output_gradient,
+    curvature,
+    adapter_down,
+    adapter_up,
+    down_direction,
+    up_direction,
+):
+    ring = Ring(lax.axis_size("expert"))
+    slots = ring.length
+    me = lax.axis_index("expert")
+    tokens, top = expert_of_route.shape
+    hidden_width = hidden_of_route.shape[2]
+    rank = adapter_down.shape[2]
+    model_width = output_gradient.shape[1]
+    experts = capacity.shape[0]
+    wide = slots * rank
+    names = jnp.arange(experts, dtype=jnp.int32)
+
+    counts = jnp.sum((expert_of_route[:, :, None] == names).astype(f32), axis=(0, 1))
+    own_down = jnp.concatenate(
+        [
+            down_scale * jnp.concatenate([down_direction, adapter_down]).transpose(0, 2, 1),
+            jnp.broadcast_to(jnp.pad(counts, (0, lanes - experts)), (2, rank, lanes)),
+        ],
+        axis=2,
+    ).astype(f16)
+    own_up = (up_scale * jnp.concatenate([adapter_up, up_direction])).astype(f16)
+    down_pieces = ring.gather(own_down)
+    up_pieces = ring.gather(own_up)
+
+    small = jnp.concatenate(
+        [
+            expert_of_route.T.astype(f32),
+            gate_of_route.T.astype(f32),
+            curvature[None, :],
+            jnp.zeros((-(2 * top + 1) % 8, tokens), f32),
+        ]
+    )
+    small = jnp.concatenate([small, ring.swap(small)], axis=1)
+    hidden = hidden_of_route.transpose(1, 0, 2).reshape(top * tokens, hidden_width)
+    hidden_other = ring.swap(hidden)
+    gradient_other = ring.swap(output_gradient)
+
+    members = ring.members()
+    all_counts = jnp.stack([piece[0, 0, hidden_width : hidden_width + experts] for piece in down_pieces]).astype(f32)
+    blocks = jnp.stack([me, me ^ 1])
+    prior = jnp.sum(jnp.where(members[None, :, None] < blocks[:, None, None], all_counts, 0.0), axis=1)
+    prior = prior + ring.swap(prior)[::-1]
+    of_slot = members[:, None] == names
+    limit = jnp.sum(jnp.where(of_slot, capacity.astype(f32) - prior[:, None, :], 0.0), axis=2)
+    limit = jnp.repeat(limit, rank, axis=1)
+    column = jnp.repeat(members.astype(f32), rank)[None, :]
+
+    def call(kernel, outs, *operands, scratch=()):
+        return pl.pallas_call(
+            kernel,
+            out_shape=[jax.ShapeDtypeStruct(shape, dtype) for shape, dtype in outs],
+            scratch_shapes=scratch,
+            compiler_params=pltpu.CompilerParams(vmem_limit_bytes=kernel_vmem),
+        )(*operands)
+
+    (reduced,) = call(
+        functools.partial(reduce_kernel, top, slots),
+        [((2, 2 * tokens, wide), f32)],
+        small,
+        column,
+        hidden,
+        hidden_other,
+        *[piece[..., :hidden_width].astype(f32) * (1 / down_scale) for piece in down_pieces],
+    )
+    weight, weighted, tangent, high, low = call(
+        functools.partial(tangent_kernel, top, slots),
+        [
+            ((2 * tokens, wide), f32),
+            ((2 * tokens, 2 * wide), f32),
+            ((2 * tokens, model_width), f32),
+            ((2 * wide, model_width), bf16),
+            ((2 * wide, model_width), bf16),
+        ],
+        small,
+        column,
+        limit,
+        reduced,
+        *[piece.astype(f32) * (1 / up_scale) for piece in up_pieces],
+    )
+    arrived = ring.swap(tangent)
+    left = [pltpu.VMEM((2, top * tokens, 2 * wide), bf16)]
+    chunk = ((rank, hidden_width + model_width), f32)
+    *gradients, up, to = call(
+        functools.partial(gradient_kernel, top),
+        [chunk] * slots + [((wide, model_width), f32), ((2 * tokens, wide), f32)],
+        small,
+        column,
+        hidden,
+        hidden_other,
+        output_gradient,
+        gradient_other,
+        weight,
+        weighted,
+        high,
+        low,
+        scratch=left,
+    )
+    curvatures = call(
+        functools.partial(curvature_kernel, top),
+        [chunk] * slots,
+        small,
+        column,
+        hidden,
+        hidden_other,
+        weight,
+        weighted,
+        high,
+        low,
+        up,
+        to,
+        tangent,
+        arrived,
+        scratch=left,
+    )
+    gradient_sum = ring.scatter(gradients, 1)
+    curvature_sum = ring.scatter(curvatures, -1)
+    return (
+        gradient_sum[:, :hidden_width].T[None],
+        gradient_sum[None, :, hidden_width:],
+        curvature_sum[:, :hidden_width].T[None],
+        curvature_sum[None, :, hidden_width:],
+    )
 
 
 def carried_in(value, axis, join, neutral):
@@ -22,7 +388,7 @@
     return earlier + later
 
 
-def local(
+def routed_plan(
     hidden_of_route,
     expert_of_route,
     gate_of_route,
@@ -153,6 +519,13 @@
     )
 
 
+def local(*arguments):
+    adapter_down, adapter_up = arguments[6], arguments[7]
+    factor_bytes = 2 * 4 * (adapter_down.size + adapter_up.size) * lax.axis_size("expert")
+    plan = gathered_plan if 4 * factor_bytes <= kernel_vmem else routed_plan
+    return plan(*arguments)
+
+
 def solution(mesh):
     return jax.shard_map(
         local,

time: 802 us -> 124 us (0.15)
  the two profiles are of different devices: /device:TPU:11 before, /device:TPU:0 now
where the time goes in v3:
time: 124 us; the launch traced here: 123 us
  waiting for transfers between devices  35.1 us (28%)
  starting transfers between devices  33.3 us (27%)
  other arithmetic  24 us (19%)
  Pallas kernels  16.1 us (13%)
  local copies, waits for them, and re-layouts  13.1 us (11%)
  between operations  1.25 us (1%)
    ppermute x30, waiting for transfers between devices, shift(): return lax.ppermute(value, 'expert', pairs)  34.7 us
    ppermute x30, starting transfers between devices, shift(): return lax.ppermute(value, 'expert', pairs)  32.7 us
    pallas_call x4, Pallas kernels, call(): pl.pallas_call(kernel, out_shape=[jax.ShapeDtypeStruct(shape, dtype) for...  16.1 us
    mul x8, other arithmetic, gathered_plan(): piece[..., :hidden_width].astype(f32) * (1 / down_scale)  7.03 us
    another operation x9, local copies, waits for them, and re-layouts, gathered_plan(): jnp.stack([piece[0, 0, hidden_width:hidden_width + experts] for piece in...  5.69 us
    mul x8, other arithmetic, gathered_plan(): piece.astype(f32) * (1 / up_scale)  4.8 us
    transpose x1, local copies, waits for them, and re-layouts, gathered_plan(): hidden_of_route.transpose(1, 0, 2).reshape(top * tokens, hidden_width)  2.8 us
    reduce_max x14, other arithmetic, encode(): largest = jnp.max(jnp.abs(value), axis=1, keepdims=True)  2.51 us
  transfers between devices with their start and end apart: 35, of which 16 were waited for; matrix products, arithmetic and copies ran while one was open for 25% of the time, Pallas kernels for 5%

profile of v3, /device:TPU:0, one launch (start us, length us, event | category | flops | bytes accessed | tf_op | source)
XLA Modules:
  0.0 123.0 jit_solution(17398812727624588057)
XLA Ops:
  3.0 3.0 %collective-permute-start.3 = (f16[2,16,1152]{2,1,0:T(8,128)(2,1)S(1)}, f16[2,16,1152]{2,1,0:T(8,128)(2,1)}, u32[]{:S(2)}, u32[]{:S(2)}) collective-permute-start(f16[2,16,1152]{2,1,0:T(8,128)(2,1)S(1)} %pad_maximum_fusion.14), channel_id=1, source_target_pairs={{0,2},{1,3},{4,0},{5,1},{8,4},{9,5},{12,8},{13,9},{14,12},{15,13},... | collective-permute-start | bytes 221192 | tf_op jit(solution)/shard_map/ppermute | solution.py:191
  7.2 1.9 %collective-permute-start.12 = (f16[2,16,2048]{2,1,0:T(8,128)(2,1)S(1)}, f16[2,16,2048]{2,1,0:T(8,128)(2,1)}, u32[]{:S(2)}, u32[]{:S(2)}) collective-permute-start(f16[2,16,2048]{2,1,0:T(8,128)(2,1)S(1)} %get-tuple-element.51), channel_id=1, source_target_pairs={{0,2},{1,3},{4,0},{5,1},{8,4},{9,5},{12,8},{13,9},{14,12},{15,13},... | collective-permute-start | bytes 393224 | tf_op jit(solution)/shard_map/ppermute | solution.py:191
  12.8 2.8 %copy.18 = bf16[8,128,1024]{2,1,0:T(8,128)(2,1)S(1)} copy(bf16[8,128,1024]{2,0,1:T(8,128)(2,1)} %bitcast.44) | data formatting | bytes 4194304 | tf_op jit(solution)/shard_map/transpose | solution.py:284
  19.5 1.9 %collective-permute-start.4 = (f16[2,16,1152]{2,1,0:T(8,128)(2,1)}, f16[2,16,1152]{2,1,0:T(8,128)(2,1)S(1)}, u32[]{:S(2)}, u32[]{:S(2)}) collective-permute-start(f16[2,16,1152]{2,1,0:T(8,128)(2,1)} %collective-permute-done.3), channel_id=1, source_target_pairs={{0,2},{1,3},{4,0},{5,1},{8,4},{9,5},{12,8},{13,9},{14,12},{15,13},... | collective-permute-start | bytes 221192 | tf_op jit(solution)/shard_map/ppermute | solution.py:191
  24.4 1.8 %collective-permute-start.13 = (f16[2,16,2048]{2,1,0:T(8,128)(2,1)}, f16[2,16,2048]{2,1,0:T(8,128)(2,1)}, u32[]{:S(2)}, u32[]{:S(2)}) collective-permute-start(f16[2,16,2048]{2,1,0:T(8,128)(2,1)} %collective-permute-done.12), channel_id=1, source_target_pairs={{0,2},{1,3},{4,0},{5,1},{8,4},{9,5},{12,8},{13,9},{14,12},{15,13},... | collective-permute-start | bytes 393224 | tf_op jit(solution)/shard_map/ppermute | solution.py:191
  31.6 2.7 %collective-permute-done.8 = f16[2,16,1152]{2,1,0:T(8,128)(2,1)S(1)} collective-permute-done((f16[2,16,1152]{2,1,0:T(8,128)(2,1)S(1)}, f16[2,16,1152]{2,1,0:T(8,128)(2,1)S(1)}, u32[]{:S(2)}, u32[]{:S(2)}) %collective-permute-start.8) | collective-permute-done | bytes 73760 | tf_op jit(solution)/shard_map/ppermute | solution.py:191
  37.5 2.4 %collective-permute-done.9 = f16[1,16,1152]{2,1,0:T(8,128)(2,1)S(1)} collective-permute-done((f16[1,16,1152]{2,1,0:T(8,128)(2,1)S(1)}, f16[1,16,1152]{2,1,0:T(8,128)(2,1)S(1)}, u32[]{:S(2)}, u32[]{:S(2)}) %collective-permute-start.9) | collective-permute-done | bytes 36896 | tf_op jit(solution)/shard_map/ppermute | solution.py:191
  49.8 1.9 %collective-permute-done.14 = f16[2,16,2048]{2,1,0:T(8,128)(2,1)S(1)} collective-permute-done((f16[2,16,2048]{2,1,0:T(8,128)(2,1)}, f16[2,16,2048]{2,1,0:T(8,128)(2,1)S(1)}, u32[]{:S(2)}, u32[]{:S(2)}) %collective-permute-start.14) | collective-permute-done | bytes 131104 | tf_op jit(solution)/shard_map/ppermute | solution.py:191
  54.0 2.1 %collective-permute-done.19 = f16[1,16,2048]{2,1,0:T(8,128)(2,1)S(1)} collective-permute-done((f16[1,16,2048]{2,1,0:T(8,128)(2,1)S(1)}, f16[1,16,2048]{2,1,0:T(8,128)(2,1)S(1)}, u32[]{:S(2)}, u32[]{:S(2)}) %collective-permute-start.19) | collective-permute-done | bytes 65568 | tf_op jit(solution)/shard_map/ppermute | solution.py:191
  56.1 1.7 %collective-permute-done.18 = f16[1,16,2048]{2,1,0:T(8,128)(2,1)S(1)} collective-permute-done((f16[1,16,2048]{2,1,0:T(8,128)(2,1)S(1)}, f16[1,16,2048]{2,1,0:T(8,128)(2,1)S(1)}, u32[]{:S(2)}, u32[]{:S(2)}) %collective-permute-start.18) | collective-permute-done | bytes 65568 | tf_op jit(solution)/shard_map/ppermute | solution.py:191
  57.9 4.0 %shard_map.129.reduced_ref = f32[2,256,128]{2,1,0:T(8,128)S(1)} custom-call(f32[24,256]{1,0:T(8,128)S(1)} %pad_maximum_fusion.16.small_ref, f32[1,128]{1,0:T(1,128)S(1)} %broadcast_in_dim_reshape.3.column_ref, bf16[1024,1024]{1,0:T(8,128)(2,1)S(1)} %bitcast.41, bf16[1024,1024]{1,0:T(8,128)(2,1)} %collective-permute-done.1.other_ref, ...), custom_call_target="tpu_custom_call" | custom-call | tf_op jit(solution)/shard_map/pallas_call | solution.py:299
  61.9 1.9 %shard_map.130 = (f32[256,128]{1,0:T(8,128)S(1)}, f32[256,256]{1,0:T(8,128)S(1)}, f32[256,2048]{1,0:T(8,128)S(1)}, bf16[256,2048]{1,0:T(8,128)(2,1)S(1)}, bf16[256,2048]{1,0:T(8,128)(2,1)S(1)}) custom-call(f32[24,256]{1,0:T(8,128)S(1)} %pad_maximum_fusion.16.small_ref, f32[1,128]{1,0:T(1,128)S(1)} %broadcast_in_dim_reshape.3.column_ref, ...), custom_call_target="tpu_custom_call" | custom-call | tf_op jit(solution)/shard_map/pallas_call | solution.py:299
  63.8 5.5 %shard_map.131 = (f32[16,3072]{1,0:T(8,128)S(1)}, f32[16,3072]{1,0:T(8,128)S(1)}, f32[16,3072]{1,0:T(8,128)S(1)}, f32[16,3072]{1,0:T(8,128)S(1)}, f32[16,3072]{1...) custom-call(f32[24,256]{1,0:T(8,128)S(1)} %pad_maximum_fusion.16.sma, ...), custom_call_target="tpu_custom_call" | custom-call | tf_op jit(solution)/shard_map/pallas_call | solution.py:299
  72.2 2.2 %collective-permute-done.24 = f16[16,3200]{1,0:T(8,128)(2,1)S(1)} collective-permute-done((f16[16,3200]{1,0:T(8,128)(2,1)S(1)}, f16[16,3200]{1,0:T(8,128)(2,1)S(1)}, u32[]{:S(2)}, u32[]{:S(2)}) %collective-permute-start.24) | collective-permute-done | bytes 102432 | tf_op jit(solution)/shard_map/ppermute | solution.py:191
  77.7 2.0 %collective-permute-done.25 = f16[16,3200]{1,0:T(8,128)(2,1)S(1)} collective-permute-done((f16[16,3200]{1,0:T(8,128)(2,1)S(1)}, f16[16,3200]{1,0:T(8,128)(2,1)S(1)}, u32[]{:S(2)}, u32[]{:S(2)}) %collective-permute-start.25) | collective-permute-done | bytes 102432 | tf_op jit(solution)/shard_map/ppermute | solution.py:191
  80.1 1.9 %collective-permute-done.21 = f16[16,3200]{1,0:T(8,128)(2,1)S(1)} collective-permute-done((f16[16,3200]{1,0:T(8,128)(2,1)S(1)}, f16[16,3200]{1,0:T(8,128)(2,1)S(1)}, u32[]{:S(2)}, u32[]{:S(2)}) %collective-permute-start.21) | collective-permute-done | bytes 102432 | tf_op jit(solution)/shard_map/ppermute | solution.py:191
  83.2 1.8 %collective-permute-start.26 = (f16[16,3200]{1,0:T(8,128)(2,1)S(1)}, f16[16,3200]{1,0:T(8,128)(2,1)S(1)}, u32[]{:S(2)}, u32[]{:S(2)}) collective-permute-start(f16[16,3200]{1,0:T(8,128)(2,1)S(1)} %pad_maximum_fusion.6), channel_id=1, source_target_pairs={{0,2},{1,3},{4,0},{5,1},{8,4},{9,5},{12,8},{13,9},{14,12},{15,13},... | collective-permute-start | bytes 307208 | tf_op jit(solution)/shard_map/ppermute | solution.py:191
  85.0 3.0 %collective-permute-done.22 = f16[16,3200]{1,0:T(8,128)(2,1)S(1)} collective-permute-done((f16[16,3200]{1,0:T(8,128)(2,1)S(1)}, f16[16,3200]{1,0:T(8,128)(2,1)S(1)}, u32[]{:S(2)}, u32[]{:S(2)}) %collective-permute-start.22) | collective-permute-done | bytes 102432 | tf_op jit(solution)/shard_map/ppermute | solution.py:191
  89.2 4.1 %collective-permute-done.23 = f16[16,3200]{1,0:T(8,128)(2,1)S(1)} collective-permute-done((f16[16,3200]{1,0:T(8,128)(2,1)S(1)}, f16[16,3200]{1,0:T(8,128)(2,1)S(1)}, u32[]{:S(2)}, u32[]{:S(2)}) %collective-permute-start.23) | collective-permute-done | bytes 102432 | tf_op jit(solution)/shard_map/ppermute | solution.py:191
  94.8 4.6 %shard_map.132 = (f32[16,3072]{1,0:T(8,128)S(1)}, f32[16,3072]{1,0:T(8,128)S(1)}, f32[16,3072]{1,0:T(8,128)S(1)}, f32[16,3072]{1,0:T(8,128)S(1)}, f32[16,3072]{1...) custom-call(f32[24,256]{1,0:T(8,128)S(1)} %pad_maximum_fusion.16.small_ref, ...), custom_call_target="tpu_custom_call" | custom-call | tf_op jit(solution)/shard_map/pallas_call | solution.py:299
  102.3 2.2 %collective-permute-done.32 = f16[16,3200]{1,0:T(8,128)(2,1)S(1)} collective-permute-done((f16[16,3200]{1,0:T(8,128)(2,1)S(1)}, f16[16,3200]{1,0:T(8,128)(2,1)S(1)}, u32[]{:S(2)}, u32[]{:S(2)}) %collective-permute-start.32) | collective-permute-done | bytes 102432 | tf_op jit(solution)/shard_map/ppermute | solution.py:191
  107.8 2.7 %collective-permute-done.33 = f16[16,3200]{1,0:T(8,128)(2,1)S(1)} collective-permute-done((f16[16,3200]{1,0:T(8,128)(2,1)S(1)}, f16[16,3200]{1,0:T(8,128)(2,1)S(1)}, u32[]{:S(2)}, u32[]{:S(2)}) %collective-permute-start.33) | collective-permute-done | bytes 102432 | tf_op jit(solution)/shard_map/ppermute | solution.py:191
  113.8 2.4 %collective-permute-done.30 = f16[16,3200]{1,0:T(8,128)(2,1)S(1)} collective-permute-done((f16[16,3200]{1,0:T(8,128)(2,1)S(1)}, f16[16,3200]{1,0:T(8,128)(2,1)S(1)}, u32[]{:S(2)}, u32[]{:S(2)}) %collective-permute-start.30) | collective-permute-done | bytes 102432 | tf_op jit(solution)/shard_map/ppermute | solution.py:191
  118.5 3.0 %collective-permute-done.31 = f16[16,3200]{1,0:T(8,128)(2,1)S(1)} collective-permute-done((f16[16,3200]{1,0:T(8,128)(2,1)S(1)}, f16[16,3200]{1,0:T(8,128)(2,1)S(1)}, u32[]{:S(2)}, u32[]{:S(2)}) %collective-permute-start.31) | collective-permute-done | bytes 102432 | tf_op jit(solution)/shard_map/ppermute | solution.py:191
  (216 shorter events, 58.2 us)
Async XLA Ops:
  3.0 13.6 %collective-permute-start.3 = (f16[2,16,1152]{2,1,0:T(8,128)(2,1)S(1)}, f16[2,16,1152]{2,1,0:T(8,128)(2,1)}, u32[]{:S(2)}, u32[]{:S(2)}) collective-permute-start(f16[2,16,1152]{2,1,0:T(8,128)(2,1)S(1)} %pad_maximum_fusion.14), channel_id=1, source_target_pairs={{0,2},{1,3},{4,0},{5,1},{8,4},{9,5},{12,8},{13,9},{14,12},{15,13},... | collective-permute-start | bytes 221192 | tf_op jit(solution)/shard_map/ppermute | solution.py:191
  6.0 13.5 %collective-permute-start.6 = (f16[2,16,1152]{2,1,0:T(8,128)(2,1)S(1)}, f16[2,16,1152]{2,1,0:T(8,128)(2,1)S(1)}, u32[]{:S(2)}, u32[]{:S(2)}) collective-permute-start(f16[2,16,1152]{2,1,0:T(8,128)(2,1)S(1)} %pad_maximum_fusion.14), channel_id=1, source_target_pairs={{0,4},{1,5},{4,8},{5,9},{8,12},{9,13},{12,14},{13,15},{14,10},{15,... | collective-permute-start | bytes 221192 | tf_op jit(solution)/shard_map/ppermute | solution.py:191
  7.2 15.4 %collective-permute-start.12 = (f16[2,16,2048]{2,1,0:T(8,128)(2,1)S(1)}, f16[2,16,2048]{2,1,0:T(8,128)(2,1)}, u32[]{:S(2)}, u32[]{:S(2)}) collective-permute-start(f16[2,16,2048]{2,1,0:T(8,128)(2,1)S(1)} %get-tuple-element.51), channel_id=1, source_target_pairs={{0,2},{1,3},{4,0},{5,1},{8,4},{9,5},{12,8},{13,9},{14,12},{15,13},... | collective-permute-start | bytes 393224 | tf_op jit(solution)/shard_map/ppermute | solution.py:191
  9.1 14.6 %collective-permute-start.15 = (f16[2,16,2048]{2,1,0:T(8,128)(2,1)S(1)}, f16[2,16,2048]{2,1,0:T(8,128)(2,1)S(1)}, u32[]{:S(2)}, u32[]{:S(2)}) collective-permute-start(f16[2,16,2048]{2,1,0:T(8,128)(2,1)S(1)} %get-tuple-element.51), channel_id=1, source_target_pairs={{0,4},{1,5},{4,8},{5,9},{8,12},{9,13},{12,14},{13,15},{14,10},{15,... | collective-permute-start | bytes 393224 | tf_op jit(solution)/shard_map/ppermute | solution.py:191
  11.3 4.9 %collective-permute-start = (f32[24,128]{1,0:T(8,128)S(1)}, f32[24,128]{1,0:T(8,128)S(1)}, u32[]{:S(2)}, u32[]{:S(2)}) collective-permute-start(f32[24,128]{1,0:T(8,128)S(1)} %pad_maximum_fusion.17), channel_id=1, source_target_pairs={{0,1},{1,0},{2,3},{3,2},{4,5},{5,4},{6,7},{7,6},{8,9},{9,8},{10,11... | collective-permute-start | bytes 36872 | tf_op jit(solution)/shard_map/ppermute | solution.py:194
  16.2 41.6 %collective-permute-start.1 = (bf16[1024,1024]{1,0:T(8,128)(2,1)S(1)}, bf16[1024,1024]{1,0:T(8,128)(2,1)}, u32[]{:S(2)}, u32[]{:S(2)}) collective-permute-start(bf16[1024,1024]{1,0:T(8,128)(2,1)S(1)} %bitcast.40), channel_id=1, source_target_pairs={{0,1},{1,0},{2,3},{3,2},{4,5},{5,4},{6,7},{7,6},{8,9},{9,8},{10,11... | collective-permute-start | bytes 6291464 | tf_op jit(solution)/shard_map/ppermute | solution.py:194
  16.7 47.2 %collective-permute-start.2 = (bf16[128,2048]{1,0:T(8,128)(2,1)S(1)}, bf16[128,2048]{1,0:T(8,128)(2,1)}, u32[]{:S(2)}, u32[]{:S(2)}) collective-permute-start(bf16[128,2048]{1,0:T(8,128)(2,1)S(1)} %copy-done), channel_id=1, source_target_pairs={{0,1},{1,0},{2,3},{3,2},{4,5},{5,4},{6,7},{7,6},{8,9},{9,8},{10,11... | collective-permute-start | bytes 1572872 | tf_op jit(solution)/shard_map/ppermute | solution.py:194
  19.5 7.6 %collective-permute-start.4 = (f16[2,16,1152]{2,1,0:T(8,128)(2,1)}, f16[2,16,1152]{2,1,0:T(8,128)(2,1)S(1)}, u32[]{:S(2)}, u32[]{:S(2)}) collective-permute-start(f16[2,16,1152]{2,1,0:T(8,128)(2,1)} %collective-permute-done.3), channel_id=1, source_target_pairs={{0,2},{1,3},{4,0},{5,1},{8,4},{9,5},{12,8},{13,9},{14,12},{15,13},... | collective-permute-start | bytes 221192 | tf_op jit(solution)/shard_map/ppermute | solution.py:191
  22.6 7.4 %collective-permute-start.7 = (f16[2,16,1152]{2,1,0:T(8,128)(2,1)S(1)}, f16[2,16,1152]{2,1,0:T(8,128)(2,1)S(1)}, u32[]{:S(2)}, u32[]{:S(2)}) collective-permute-start(f16[2,16,1152]{2,1,0:T(8,128)(2,1)S(1)} %collective-permute-done.6), channel_id=1, source_target_pairs={{0,4},{1,5},{4,8},{5,9},{8,12},{9,13},{12,14},{13,15},{14,10},{15,... | collective-permute-start | bytes 221192 | tf_op jit(solution)/shard_map/ppermute | solution.py:191
  24.4 21.5 %collective-permute-start.13 = (f16[2,16,2048]{2,1,0:T(8,128)(2,1)}, f16[2,16,2048]{2,1,0:T(8,128)(2,1)}, u32[]{:S(2)}, u32[]{:S(2)}) collective-permute-start(f16[2,16,2048]{2,1,0:T(8,128)(2,1)} %collective-permute-done.12), channel_id=1, source_target_pairs={{0,2},{1,3},{4,0},{5,1},{8,4},{9,5},{12,8},{13,9},{14,12},{15,13},... | collective-permute-start | bytes 393224 | tf_op jit(solution)/shard_map/ppermute | solution.py:191
  27.7 7.1 %collective-permute-start.5 = (f16[2,16,1152]{2,1,0:T(8,128)(2,1)S(1)}, f16[2,16,1152]{2,1,0:T(8,128)(2,1)S(1)}, u32[]{:S(2)}, u32[]{:S(2)}) collective-permute-start(f16[2,16,1152]{2,1,0:T(8,128)(2,1)S(1)} %collective-permute-done.4), channel_id=1, source_target_pairs={{0,2},{1,3},{4,0},{5,1},{8,4},{9,5},{12,8},{13,9},{14,12},{15,13},... | collective-permute-start | bytes 221192 | tf_op jit(solution)/shard_map/ppermute | solution.py:191
  34.3 13.2 %collective-permute-start.16 = (f16[2,16,2048]{2,1,0:T(8,128)(2,1)}, f16[2,16,2048]{2,1,0:T(8,128)(2,1)}, u32[]{:S(2)}, u32[]{:S(2)}) collective-permute-start(f16[2,16,2048]{2,1,0:T(8,128)(2,1)} %copy-done.9), channel_id=1, source_target_pairs={{0,4},{1,5},{4,8},{5,9},{8,12},{9,13},{12,14},{13,15},{14,10},{15,... | collective-permute-start | bytes 393224 | tf_op jit(solution)/shard_map/ppermute | solution.py:191
  34.8 5.1 %collective-permute-start.9 = (f16[1,16,1152]{2,1,0:T(8,128)(2,1)S(1)}, f16[1,16,1152]{2,1,0:T(8,128)(2,1)S(1)}, u32[]{:S(2)}, u32[]{:S(2)}) collective-permute-start(f16[1,16,1152]{2,1,0:T(8,128)(2,1)S(1)} %slice.210), channel_id=1, source_target_pairs={{0,4},{1,5},{4,8},{5,9},{8,12},{9,13},{12,14},{13,15},{14,10},{15,... | collective-permute-start | bytes 110600 | tf_op jit(solution)/shard_map/ppermute | solution.py:191
  45.9 5.9 %collective-permute-start.14 = (f16[2,16,2048]{2,1,0:T(8,128)(2,1)}, f16[2,16,2048]{2,1,0:T(8,128)(2,1)S(1)}, u32[]{:S(2)}, u32[]{:S(2)}) collective-permute-start(f16[2,16,2048]{2,1,0:T(8,128)(2,1)} %collective-permute-done.13), channel_id=1, source_target_pairs={{0,2},{1,3},{4,0},{5,1},{8,4},{9,5},{12,8},{13,9},{14,12},{15,13},... | collective-permute-start | bytes 393224 | tf_op jit(solution)/shard_map/ppermute | solution.py:191
  47.5 5.9 %collective-permute-start.17 = (f16[2,16,2048]{2,1,0:T(8,128)(2,1)}, f16[2,16,2048]{2,1,0:T(8,128)(2,1)S(1)}, u32[]{:S(2)}, u32[]{:S(2)}) collective-permute-start(f16[2,16,2048]{2,1,0:T(8,128)(2,1)} %collective-permute-done.16), channel_id=1, source_target_pairs={{0,4},{1,5},{4,8},{5,9},{8,12},{9,13},{12,14},{13,15},{14,10},{15,... | collective-permute-start | bytes 393224 | tf_op jit(solution)/shard_map/ppermute | solution.py:191
  69.7 4.7 %collective-permute-start.24 = (f16[16,3200]{1,0:T(8,128)(2,1)S(1)}, f16[16,3200]{1,0:T(8,128)(2,1)S(1)}, u32[]{:S(2)}, u32[]{:S(2)}) collective-permute-start(f16[16,3200]{1,0:T(8,128)(2,1)S(1)} %pad_maximum_fusion.4), channel_id=1, source_target_pairs={{0,2},{1,3},{4,0},{5,1},{8,4},{9,5},{12,8},{13,9},{14,12},{15,13},... | collective-permute-start | bytes 307208 | tf_op jit(solution)/shard_map/ppermute | solution.py:191
  71.7 4.9 %collective-permute-start.20 = (f16[16,3200]{1,0:T(8,128)(2,1)S(1)}, f16[16,3200]{1,0:T(8,128)(2,1)S(1)}, u32[]{:S(2)}, u32[]{:S(2)}) collective-permute-start(f16[16,3200]{1,0:T(8,128)(2,1)S(1)} %pad_maximum_fusion), channel_id=1, source_target_pairs={{0,4},{1,5},{4,8},{5,9},{8,12},{9,13},{12,14},{13,15},{14,10},{15,... | collective-permute-start | bytes 307208 | tf_op jit(solution)/shard_map/ppermute | solution.py:191
  72.2 22.6 %collective-permute-start.27 = (f32[256,2048]{1,0:T(8,128)S(1)}, f32[256,2048]{1,0:T(8,128)S(1)}, u32[]{:S(2)}, u32[]{:S(2)}) collective-permute-start(f32[256,2048]{1,0:T(8,128)S(1)} %get-tuple-element.41.tangent_ref), channel_id=1, source_target_pairs={{0,1},{1,0},{2,3},{3,2},{4,5},{5,4},{6,7},{7,6},{8,9},{9,8},{10,11... | collective-permute-start | bytes 6291464 | tf_op jit(solution)/shard_map/ppermute | solution.py:194
  77.2 4.7 %collective-permute-start.21 = (f16[16,3200]{1,0:T(8,128)(2,1)S(1)}, f16[16,3200]{1,0:T(8,128)(2,1)S(1)}, u32[]{:S(2)}, u32[]{:S(2)}) collective-permute-start(f16[16,3200]{1,0:T(8,128)(2,1)S(1)} %pad_maximum_fusion.1), channel_id=1, source_target_pairs={{0,4},{1,5},{4,8},{5,9},{8,12},{9,13},{12,14},{13,15},{14,10},{15,... | collective-permute-start | bytes 307208 | tf_op jit(solution)/shard_map/ppermute | solution.py:191
  82.5 5.5 %collective-permute-start.22 = (f16[16,3200]{1,0:T(8,128)(2,1)S(1)}, f16[16,3200]{1,0:T(8,128)(2,1)S(1)}, u32[]{:S(2)}, u32[]{:S(2)}) collective-permute-start(f16[16,3200]{1,0:T(8,128)(2,1)S(1)} %pad_maximum_fusion.2), channel_id=1, source_target_pairs={{0,4},{1,5},{4,8},{5,9},{8,12},{9,13},{12,14},{13,15},{14,10},{15,... | collective-permute-start | bytes 307208 | tf_op jit(solution)/shard_map/ppermute | solution.py:191
  83.2 5.9 %collective-permute-start.26 = (f16[16,3200]{1,0:T(8,128)(2,1)S(1)}, f16[16,3200]{1,0:T(8,128)(2,1)S(1)}, u32[]{:S(2)}, u32[]{:S(2)}) collective-permute-start(f16[16,3200]{1,0:T(8,128)(2,1)S(1)} %pad_maximum_fusion.6), channel_id=1, source_target_pairs={{0,2},{1,3},{4,0},{5,1},{8,4},{9,5},{12,8},{13,9},{14,12},{15,13},... | collective-permute-start | bytes 307208 | tf_op jit(solution)/shard_map/ppermute | solution.py:191
  100.6 4.9 %collective-permute-start.28 = (f16[16,3200]{1,0:T(8,128)(2,1)S(1)}, f16[16,3200]{1,0:T(8,128)(2,1)S(1)}, u32[]{:S(2)}, u32[]{:S(2)}) collective-permute-start(f16[16,3200]{1,0:T(8,128)(2,1)S(1)} %pad_maximum_fusion.7), channel_id=1, source_target_pairs={{0,2},{1,3},{4,0},{5,1},{8,4},{9,5},{12,8},{13,9},{14,12},{15,13},... | collective-permute-start | bytes 307208 | tf_op jit(solution)/shard_map/ppermute | solution.py:191
  105.1 5.4 %collective-permute-start.33 = (f16[16,3200]{1,0:T(8,128)(2,1)S(1)}, f16[16,3200]{1,0:T(8,128)(2,1)S(1)}, u32[]{:S(2)}, u32[]{:S(2)}) collective-permute-start(f16[16,3200]{1,0:T(8,128)(2,1)S(1)} %pad_maximum_fusion.12), channel_id=1, source_target_pairs={{0,4},{1,5},{4,8},{5,9},{8,12},{9,13},{12,14},{13,15},{14,10},{15,... | collective-permute-start | bytes 307208 | tf_op jit(solution)/shard_map/ppermute | solution.py:191
  113.3 5.1 %collective-permute-start.34 = (f16[16,3200]{1,0:T(8,128)(2,1)S(1)}, f16[16,3200]{1,0:T(8,128)(2,1)S(1)}, u32[]{:S(2)}, u32[]{:S(2)}) collective-permute-start(f16[16,3200]{1,0:T(8,128)(2,1)S(1)} %pad_maximum_fusion.13), channel_id=1, source_target_pairs={{0,4},{1,5},{4,8},{5,9},{8,12},{9,13},{12,14},{13,15},{14,10},{15,... | collective-permute-start | bytes 307208 | tf_op jit(solution)/shard_map/ppermute | solution.py:191
  (23 other events, 153.3 us)

commit v4 on v3

--- a/solution.py
+++ b/solution.py
@@ -37,14 +37,14 @@
     return experts, gates, small[:, 2 * top : 2 * top + 1]
 
 
-def stacked(refs, kind):
-    return jnp.concatenate([ref[kind] for ref in refs], axis=0)
-
-
-def reduce_kernel(top, slots, small_ref, column_ref, own_ref, other_ref, *rest):
-    factor_refs, reduced_ref = rest[:slots], rest[slots]
+def stacked(refs, width):
+    rows = [ref[:, kind, :, :width].reshape(-1, width) for kind in range(2) for ref in refs]
+    return halves(jnp.concatenate(rows, axis=0))
+
+
+def reduce_kernel(top, small_ref, column_ref, own_ref, other_ref, factor_ref, reduced_ref):
     experts, _, _ = token_columns(small_ref, top)
-    high, low = halves(jnp.concatenate([stacked(factor_refs, 0), stacked(factor_refs, 1)], axis=0))
+    high, low = stacked([factor_ref], own_ref.shape[1])
     wide = high.shape[0] // 2
     tokens = own_ref.shape[0] // top
     for block, hidden_ref in enumerate((own_ref, other_ref)):
@@ -58,12 +58,41 @@
         reduced_ref[1, rows] = total[:, wide:]
 
 
-def tangent_kernel(top, slots, small_ref, column_ref, limit_ref, reduced_ref, *rest):
-    factor_refs = rest[:slots]
-    weight_ref, weighted_ref, tangent_ref, high_ref, low_ref = rest[slots:]
+def rank_limits(rank, column_ref, capacity_ref, factor_refs):
+    wide = column_ref.shape[1]
+    member = [column_ref[:, start : start + 1] for start in range(0, wide, rank)]
+    me = member[0]
+    across = 1.0 - 2.0 * (me - 2.0 * jnp.floor(me * 0.5))
+    left = []
+    for block in (me, me + across):
+        total = capacity_ref[...]
+        slot = 0
+        for ref in factor_refs:
+            for piece in range(ref.shape[0]):
+                own = ref[piece, 0, 0:1, ref.shape[3] - lanes :]
+                other = ref[piece, 0, 1:2, ref.shape[3] - lanes :]
+                total = total - jnp.where(member[slot] < block, own, 0.0)
+                total = total - jnp.where(member[slot] + across < block, other, 0.0)
+                slot += 1
+        left.append(total)
+    lane = lax.broadcasted_iota(jnp.int32, (1, lanes), 1).astype(f32)
+    slot_of = lax.broadcasted_iota(jnp.int32, (1, wide), 1) // rank
+    limits = []
+    for total in left:
+        limit = jnp.zeros((1, wide), f32)
+        for slot, expert in enumerate(member):
+            value = jnp.sum(jnp.where(lane == expert, total, 0.0), axis=1, keepdims=True)
+            limit = jnp.where(slot_of == slot, value, limit)
+        limits.append(limit)
+    return limits
+
+
+def tangent_kernel(top, small_ref, column_ref, capacity_ref, reduced_ref, near_ref, far_ref, *outs):
+    weight_ref, weighted_ref, tangent_ref, high_ref, low_ref = outs
     experts, gates, _ = token_columns(small_ref, top)
     tokens, wide = weight_ref.shape
     block = tokens // 2
+    limits = rank_limits(near_ref.shape[2], column_ref, capacity_ref, (near_ref, far_ref))
     gate = jnp.zeros((tokens, wide), f32)
     member = jnp.zeros((tokens, wide), f32)
     for k in range(top):
@@ -79,12 +108,12 @@
     for part in range(2):
         rows = slice(part * block, (part + 1) * block)
         local_rank = dot(below, member[rows].astype(bf16), 1, 0)
-        weights.append(jnp.where(local_rank < limit_ref[part : part + 1], adapter_scale * gate[rows], 0.0))
+        weights.append(jnp.where(local_rank < limits[part], adapter_scale * gate[rows], 0.0))
     weight = jnp.concatenate(weights, axis=0)
     weight_ref[...] = weight
     weighted = jnp.concatenate([weight * reduced_ref[0], weight * reduced_ref[1]], axis=1)
     weighted_ref[...] = weighted
-    factor = halves(jnp.concatenate([stacked(factor_refs, 0), stacked(factor_refs, 1)], axis=0))
+    factor = stacked([near_ref, far_ref], high_ref.shape[1])
     high_ref[...], low_ref[...] = factor
     tangent_ref[...] = dot_pairs(halves(weighted), factor, 1, 0)
 
@@ -108,9 +137,10 @@
 
 
 def put_chunks(out_refs, start, value):
-    rank, width = out_refs[0].shape[0], value.shape[1]
-    for slot, out_ref in enumerate(out_refs):
-        out_ref[:, start : start + width] = value[slot * rank : (slot + 1) * rank]
+    for place, out_ref in enumerate(out_refs):
+        count, rank, _ = out_ref.shape
+        rows = value[place * count * rank : (place + 1) * count * rank]
+        out_ref[:, :, start : start + value.shape[1]] = rows.reshape(count, rank, value.shape[1])
 
 
 def gradient_kernel(
@@ -176,65 +206,22 @@
     put_chunks(out_refs, hidden_width, up_ref[...] + up)
 
 
-class Ring:
-    def __init__(self, size):
-        self.length = size // 2
-        rows = self.length // 2
-        self.order = [4 * z for z in range(rows)] + [4 * z + 2 for z in reversed(range(rows))]
-
-    def shift(self, value, step):
-        pairs = [
-            (chip + core, self.order[(place + step) % self.length] + core)
-            for place, chip in enumerate(self.order)
-            for core in range(2)
-        ]
-        return lax.ppermute(value, "expert", pairs)
-
-    def swap(self, value):
-        return lax.ppermute(value, "expert", [(i, i ^ 1) for i in range(2 * self.length)])
-
-    def members(self):
-        me = lax.axis_index("expert")
-        rows = self.length // 2
-        place = jnp.where(me // 2 % 2 == 0, me // 4, self.length - 1 - me // 4)
-        there = (place + jnp.arange(self.length, dtype=jnp.int32)) % self.length
-        return jnp.where(there < rows, 4 * there, 4 * (self.length - 1 - there) + 2) + me % 2
-
-    def gather(self, own):
-        half = self.length // 2
-        found = {0: own}
-        ahead, behind = own, own
-        for step in range(1, half):
-            behind = self.shift(behind, 1)
-            ahead = self.shift(ahead, -1)
-            found[self.length - step], found[step] = behind, ahead
-        found[half] = jnp.concatenate([self.shift(behind[:1], 1), self.shift(ahead[1:], -1)])
-        return [found[offset] for offset in range(self.length)]
-
-    def scatter(self, chunks, longer):
-        half = self.length // 2
-        total = chunks[0]
-        for way in (longer, -longer):
-            start = half if way == longer else half - 1
-            moving = chunks[way * start % self.length]
-            for step in range(start, 0, -1):
-                arrived = decode(self.shift(encode(moving), way))
-                moving = arrived if step == 1 else chunks[way * (step - 1) % self.length] + arrived
-            total = total + moving
-        return total
+def exchange(value, mask):
+    size = lax.axis_size("expert")
+    return lax.ppermute(value, "expert", [(device, device ^ mask) for device in range(size)])
 
 
 def encode(value):
-    largest = jnp.max(jnp.abs(value), axis=1, keepdims=True)
+    largest = jnp.max(jnp.abs(value), axis=-1, keepdims=True)
     exponent = jnp.ceil(jnp.log2(jnp.maximum(largest, 1e-30)))
     scaled = value * jnp.exp2(15.0 - exponent)
-    extra = jnp.broadcast_to(exponent, (value.shape[0], lanes))
-    return jnp.concatenate([scaled, extra], axis=1).astype(f16)
+    extra = jnp.broadcast_to(exponent, value.shape[:-1] + (lanes,))
+    return jnp.concatenate([scaled, extra], axis=-1).astype(f16)
 
 
 def decode(coded):
-    width = coded.shape[1] - lanes
-    return coded[:, :width].astype(f32) * jnp.exp2(coded[:, width : width + 1].astype(f32) - 15.0)
+    width = coded.shape[-1] - lanes
+    return coded[..., :width].astype(f32) * jnp.exp2(coded[..., width : width + 1].astype(f32) - 15.0)
 
 
 def gathered_plan(
@@ -249,28 +236,23 @@
     down_direction,
     up_direction,
 ):
-    ring = Ring(lax.axis_size("expert"))
-    slots = ring.length
+    rows = lax.axis_size("expert") // 4
+    masks = [4 * z for z in range(rows)] + [4 * z + 2 for z in range(rows)]
     me = lax.axis_index("expert")
     tokens, top = expert_of_route.shape
     hidden_width = hidden_of_route.shape[2]
     rank = adapter_down.shape[2]
     model_width = output_gradient.shape[1]
     experts = capacity.shape[0]
-    wide = slots * rank
-    names = jnp.arange(experts, dtype=jnp.int32)
-
-    counts = jnp.sum((expert_of_route[:, :, None] == names).astype(f32), axis=(0, 1))
-    own_down = jnp.concatenate(
-        [
-            down_scale * jnp.concatenate([down_direction, adapter_down]).transpose(0, 2, 1),
-            jnp.broadcast_to(jnp.pad(counts, (0, lanes - experts)), (2, rank, lanes)),
-        ],
-        axis=2,
-    ).astype(f16)
-    own_up = (up_scale * jnp.concatenate([adapter_up, up_direction])).astype(f16)
-    down_pieces = ring.gather(own_down)
-    up_pieces = ring.gather(own_up)
+    wide = 2 * rows * rank
+    names = jnp.arange(experts, dtype=f32)
+
+    def gather(own):
+        near = [own] + [exchange(own, 4 * z) for z in range(1, rows)]
+        return near, [exchange(piece, 2) for piece in near]
+
+    own_down = (down_scale * jnp.concatenate([down_direction, adapter_down]).transpose(0, 2, 1)).astype(f16)
+    down_near, down_far = gather(own_down)
 
     small = jnp.concatenate(
         [
@@ -280,40 +262,44 @@
             jnp.zeros((-(2 * top + 1) % 8, tokens), f32),
         ]
     )
-    small = jnp.concatenate([small, ring.swap(small)], axis=1)
+    small_other = exchange(small, 1)
+    counts = jnp.stack(
+        [jnp.sum((part[:top, :, None] == names).astype(f32), axis=(0, 1)) for part in (small, small_other)]
+    )
+    counts = jnp.pad(counts, ((0, rank - 2), (0, lanes - experts)))
+    own_up = jnp.concatenate(
+        [
+            up_scale * jnp.concatenate([adapter_up, up_direction]),
+            jnp.broadcast_to(counts, (2, rank, lanes)),
+        ],
+        axis=2,
+    ).astype(f16)
+    up_near, up_far = gather(own_up)
+
+    hidden_of_route, _ = lax.optimization_barrier((hidden_of_route, own_up))
+    small = jnp.concatenate([small, small_other], axis=1)
     hidden = hidden_of_route.transpose(1, 0, 2).reshape(top * tokens, hidden_width)
-    hidden_other = ring.swap(hidden)
-    gradient_other = ring.swap(output_gradient)
-
-    members = ring.members()
-    all_counts = jnp.stack([piece[0, 0, hidden_width : hidden_width + experts] for piece in down_pieces]).astype(f32)
-    blocks = jnp.stack([me, me ^ 1])
-    prior = jnp.sum(jnp.where(members[None, :, None] < blocks[:, None, None], all_counts, 0.0), axis=1)
-    prior = prior + ring.swap(prior)[::-1]
-    of_slot = members[:, None] == names
-    limit = jnp.sum(jnp.where(of_slot, capacity.astype(f32) - prior[:, None, :], 0.0), axis=2)
-    limit = jnp.repeat(limit, rank, axis=1)
-    column = jnp.repeat(members.astype(f32), rank)[None, :]
+    hidden_other = exchange(hidden, 1)
+    gradient_other = exchange(output_gradient, 1)
+    column = jnp.repeat((me ^ jnp.array(masks, jnp.int32)).astype(f32), rank)[None, :]
+    capacity_row = jnp.pad(capacity.astype(f32), (0, lanes - experts))[None, :]
 
     def call(kernel, outs, *operands, scratch=()):
         return pl.pallas_call(
-            kernel,
+            functools.partial(kernel, top),
             out_shape=[jax.ShapeDtypeStruct(shape, dtype) for shape, dtype in outs],
             scratch_shapes=scratch,
             compiler_params=pltpu.CompilerParams(vmem_limit_bytes=kernel_vmem),
         )(*operands)
 
+    down_factors = jnp.stack(down_near + down_far).astype(f32) * (1 / down_scale)
+    down_factors, *_ = lax.optimization_barrier((down_factors, *up_near))
     (reduced,) = call(
-        functools.partial(reduce_kernel, top, slots),
-        [((2, 2 * tokens, wide), f32)],
-        small,
-        column,
-        hidden,
-        hidden_other,
-        *[piece[..., :hidden_width].astype(f32) * (1 / down_scale) for piece in down_pieces],
-    )
+        reduce_kernel, [((2, 2 * tokens, wide), f32)], small, column, hidden, hidden_other, down_factors
+    )
+    unscale = jnp.concatenate([jnp.full((model_width,), 1 / up_scale, f32), jnp.ones((lanes,), f32)])
     weight, weighted, tangent, high, low = call(
-        functools.partial(tangent_kernel, top, slots),
+        tangent_kernel,
         [
             ((2 * tokens, wide), f32),
             ((2 * tokens, 2 * wide), f32),
@@ -323,16 +309,17 @@
         ],
         small,
         column,
-        limit,
+        capacity_row,
         reduced,
-        *[piece.astype(f32) * (1 / up_scale) for piece in up_pieces],
-    )
-    arrived = ring.swap(tangent)
+        jnp.stack(up_near).astype(f32) * unscale,
+        jnp.stack(up_far).astype(f32) * unscale,
+    )
+    arrived = exchange(tangent, 1)
     left = [pltpu.VMEM((2, top * tokens, 2 * wide), bf16)]
-    chunk = ((rank, hidden_width + model_width), f32)
+    chunks = [((rows // 2, rank, hidden_width + model_width), f32)] * 4
     *gradients, up, to = call(
-        functools.partial(gradient_kernel, top),
-        [chunk] * slots + [((wide, model_width), f32), ((2 * tokens, wide), f32)],
+        gradient_kernel,
+        chunks + [((wide, model_width), f32), ((2 * tokens, wide), f32)],
         small,
         column,
         hidden,
@@ -346,8 +333,8 @@
         scratch=left,
     )
     curvatures = call(
-        functools.partial(curvature_kernel, top),
-        [chunk] * slots,
+        curvature_kernel,
+        chunks,
         small,
         column,
         hidden,
@@ -362,8 +349,24 @@
         arrived,
         scratch=left,
     )
-    gradient_sum = ring.scatter(gradients, 1)
-    curvature_sum = ring.scatter(curvatures, -1)
+
+    def along_x(parts):
+        later = exchange(encode(parts[3]), 2)
+        sooner = exchange(encode(parts[2]), 2)
+        return sooner, later
+
+    def along_z(parts, moved):
+        later = encode(parts[1] + decode(moved[1]))
+        arrived = [exchange(later[z - rows // 2], 4 * z) for z in range(rows // 2, rows)]
+        sooner = parts[0] + decode(moved[0])
+        arrived += [exchange(encode(sooner[z]), 4 * z) for z in range(1, rows // 2)]
+        return sooner[0] + sum(decode(piece) for piece in arrived)
+
+    gradients_moved = along_x(gradients)
+    gradients_moved, curvatures = lax.optimization_barrier((gradients_moved, curvatures))
+    curvatures_moved = along_x(curvatures)
+    gradient_sum = along_z(gradients, gradients_moved)
+    curvature_sum = along_z(curvatures, curvatures_moved)
     return (
         gradient_sum[:, :hidden_width].T[None],
         gradient_sum[None, :, hidden_width:],

time: 124 us -> 101 us (0.81)
  other arithmetic: 24 us -> 10.7 us
  local copies, waits for them, and re-layouts: 13.1 us -> 6.26 us
  waiting for transfers between devices: 35.1 us -> 40.2 us
  Pallas kernels: 16.1 us -> 12.4 us
  starting transfers between devices: 33.3 us -> 29.6 us
    mul x16 -> x2, other arithmetic: 11.8 us -> 0.45 us  [the longest x1 0.33 us: gathered_plan(): jnp.stack(up_far).astype(f32) * unscale]
    another operation x10 -> x2, local copies, waits for them, and re-layouts: 5.78 us -> 0.1 us  [the longest x1 0.08 us: gathered_plan(): jnp.repeat((me ^ jnp.array(masks, jnp.int32)).astype(f32), rank)[None, :]]
    ppermute x35 -> x28, waiting for transfers between devices: 35.1 us -> 40.2 us  [exchange(): lax.ppermute(value, 'expert', [(device, device ^ mask) for device in rang...]
    pallas_call x4, Pallas kernels: 16.1 us -> 12.4 us  [call(): pl.pallas_call(functools.partial(kernel, top), out_shape=[jax.ShapeDtypeS...]
    ppermute x35 -> x28, starting transfers between devices: 33.3 us -> 29.6 us  [exchange(): lax.ppermute(value, 'expert', [(device, device ^ mask) for device in rang...]
    reduce_max x14 -> x8, other arithmetic: 2.51 us -> 1.04 us  [encode(): largest = jnp.max(jnp.abs(value), axis=-1, keepdims=True)]
    reduce_sum x2, other arithmetic: 1.55 us -> 0.25 us  [gathered_plan(): jnp.sum((part[:top, :, None] == names).astype(f32), axis=(0, 1))]
  transfers between devices with their start and end apart: 35 -> 28, of which waited for: 16 -> 15; matrix products, arithmetic and copies ran while one was open for 25% -> 14% of each run, Pallas kernels for 5% -> 9%
where the time goes in v4:
time: 101 us; the launch traced here: 100 us
  waiting for transfers between devices  40.2 us (40%)
  starting transfers between devices  29.6 us (29%)
  Pallas kernels  12.4 us (12%)
  other arithmetic  10.7 us (11%)
  local copies, waits for them, and re-layouts  6.26 us (6%)
  between operations  1.08 us (1%)
    ppermute x28, waiting for transfers between devices, exchange(): lax.ppermute(value, 'expert', [(device, device ^ mask) for device in rang...  40.2 us
    ppermute x28, starting transfers between devices, exchange(): lax.ppermute(value, 'expert', [(device, device ^ mask) for device in rang...  29.6 us
    pallas_call x4, Pallas kernels, call(): pl.pallas_call(functools.partial(kernel, top), out_shape=[jax.ShapeDtypeS...  12.4 us
    transpose x1, local copies, waits for them, and re-layouts, gathered_plan(): hidden_of_route.transpose(1, 0, 2).reshape(top * tokens, hidden_width)  2.76 us
  transfers between devices with their start and end apart: 28, of which 15 were waited for; matrix products, arithmetic and copies ran while one was open for 14% of the time, Pallas kernels for 9%

profile of v4, /device:TPU:0, one launch (start us, length us, event | category | flops | bytes accessed | tf_op | source)
XLA Modules:
  0.0 100.2 jit_solution(9222898446047974650)
XLA Ops:
  1.6 3.1 %collective-permute-start.3 = (f16[2,16,1024]{2,1,0:T(8,128)(2,1)S(1)}, f16[2,16,1024]{2,1,0:T(8,128)(2,1)S(1)}, u32[]{:S(2)}, u32[]{:S(2)}) collective-permute-start(f16[2,16,1024]{2,1,0:T(8,128)(2,1)S(1)} %fusion.11), channel_id=1, source_target_pairs={{0,4},{1,5},{2,6},{3,7},{4,0},{5,1},{6,2},{7,3},{8,12},{9,13},{10,... | collective-permute-start | bytes 196616 | tf_op jit(solution)/shard_map/ppermute | solution.py:211
  4.6 2.6 %collective-permute-start.4 = (f16[2,16,1024]{2,1,0:T(8,128)(2,1)S(1)}, f16[2,16,1024]{2,1,0:T(8,128)(2,1)S(1)}, u32[]{:S(2)}, u32[]{:S(2)}) collective-permute-start(f16[2,16,1024]{2,1,0:T(8,128)(2,1)S(1)} %fusion.11), channel_id=1, source_target_pairs={{0,8},{1,9},{2,10},{3,11},{4,12},{5,13},{6,14},{7,15},{8,0},{9,1},... | collective-permute-start | bytes 196616 | tf_op jit(solution)/shard_map/ppermute | solution.py:211
  7.2 1.7 %collective-permute-start.6 = (f16[2,16,1024]{2,1,0:T(8,128)(2,1)S(1)}, f16[2,16,1024]{2,1,0:T(8,128)(2,1)S(1)}, u32[]{:S(2)}, u32[]{:S(2)}) collective-permute-start(f16[2,16,1024]{2,1,0:T(8,128)(2,1)S(1)} %fusion.11), channel_id=1, source_target_pairs={{0,2},{1,3},{2,0},{3,1},{4,6},{5,7},{6,4},{7,5},{8,10},{9,11},{10,... | collective-permute-start | bytes 196616 | tf_op jit(solution)/shard_map/ppermute | solution.py:211
  15.2 2.8 %copy.17 = bf16[8,128,1024]{2,1,0:T(8,128)(2,1)S(1)} copy(bf16[8,128,1024]{2,0,1:T(8,128)(2,1)} %bitcast.83) | data formatting | bytes 4194304 | tf_op jit(solution)/shard_map/transpose | solution.py:281
  18.0 3.6 %collective-permute-start.11 = (f16[2,16,2176]{2,1,0:T(8,128)(2,1)S(1)}, f16[2,16,2176]{2,1,0:T(8,128)(2,1)S(1)}, u32[]{:S(2)}, u32[]{:S(2)}) collective-permute-start(f16[2,16,2176]{2,1,0:T(8,128)(2,1)S(1)} %pad_maximum_fusion.4), channel_id=1, source_target_pairs={{0,8},{1,9},{2,10},{3,11},{4,12},{5,13},{6,14},{7,15},{8,0},{9,1},... | collective-permute-start | bytes 417800 | tf_op jit(solution)/shard_map/ppermute | solution.py:211
  22.4 4.1 %collective-permute-done.7 = f16[2,16,1024]{2,1,0:T(8,128)(2,1)S(1)} collective-permute-done((f16[2,16,1024]{2,1,0:T(8,128)(2,1)S(1)}, f16[2,16,1024]{2,1,0:T(8,128)(2,1)S(1)}, u32[]{:S(2)}, u32[]{:S(2)}) %collective-permute-start.7) | collective-permute-done | bytes 65568 | tf_op jit(solution)/shard_map/ppermute | solution.py:211
  26.9 3.9 %collective-permute-done.8 = f16[2,16,1024]{2,1,0:T(8,128)(2,1)S(1)} collective-permute-done((f16[2,16,1024]{2,1,0:T(8,128)(2,1)S(1)}, f16[2,16,1024]{2,1,0:T(8,128)(2,1)S(1)}, u32[]{:S(2)}, u32[]{:S(2)}) %collective-permute-start.8) | collective-permute-done | bytes 65568 | tf_op jit(solution)/shard_map/ppermute | solution.py:211
  31.2 3.9 %collective-permute-done.9 = f16[2,16,1024]{2,1,0:T(8,128)(2,1)S(1)} collective-permute-done((f16[2,16,1024]{2,1,0:T(8,128)(2,1)S(1)}, f16[2,16,1024]{2,1,0:T(8,128)(2,1)S(1)}, u32[]{:S(2)}, u32[]{:S(2)}) %collective-permute-start.9) | collective-permute-done | bytes 65568 | tf_op jit(solution)/shard_map/ppermute | solution.py:211
  35.5 1.8 %collective-permute-start.16 = (f16[2,16,2176]{2,1,0:T(8,128)(2,1)S(1)}, f16[2,16,2176]{2,1,0:T(8,128)(2,1)S(1)}, u32[]{:S(2)}, u32[]{:S(2)}) collective-permute-start(f16[2,16,2176]{2,1,0:T(8,128)(2,1)S(1)} %collective-permute-done.12), channel_id=1, source_target_pairs={{0,2},{1,3},{2,0},{3,1},{4,6},{5,7},{6,4},{7,5},{8,10},{9,11},{10,... | collective-permute-start | bytes 417800 | tf_op jit(solution)/shard_map/ppermute | solution.py:211
  37.5 1.7 %collective-permute-start.14 = (f16[2,16,2176]{2,1,0:T(8,128)(2,1)S(1)}, f16[2,16,2176]{2,1,0:T(8,128)(2,1)S(1)}, u32[]{:S(2)}, u32[]{:S(2)}) collective-permute-start(f16[2,16,2176]{2,1,0:T(8,128)(2,1)S(1)} %collective-permute-done.10), channel_id=1, source_target_pairs={{0,2},{1,3},{2,0},{3,1},{4,6},{5,7},{6,4},{7,5},{8,10},{9,11},{10,... | collective-permute-start | bytes 417800 | tf_op jit(solution)/shard_map/ppermute | solution.py:211
  39.4 2.3 %collective-permute-done.13 = f16[2,16,2176]{2,1,0:T(8,128)(2,1)S(1)} collective-permute-done((f16[2,16,2176]{2,1,0:T(8,128)(2,1)S(1)}, f16[2,16,2176]{2,1,0:T(8,128)(2,1)S(1)}, u32[]{:S(2)}, u32[]{:S(2)}) %collective-permute-start.13) | collective-permute-done | bytes 139296 | tf_op jit(solution)/shard_map/ppermute | solution.py:211
  41.7 2.6 %collective-permute-done.16 = f16[2,16,2176]{2,1,0:T(8,128)(2,1)S(1)} collective-permute-done((f16[2,16,2176]{2,1,0:T(8,128)(2,1)S(1)}, f16[2,16,2176]{2,1,0:T(8,128)(2,1)S(1)}, u32[]{:S(2)}, u32[]{:S(2)}) %collective-permute-start.16) | collective-permute-done | bytes 139296 | tf_op jit(solution)/shard_map/ppermute | solution.py:211
  47.7 2.4 %shard_map.138.reduced_ref = f32[2,256,128]{2,1,0:T(8,128)S(1)} custom-call(f32[24,256]{1,0:T(8,128)S(1)} %pad_maximum_fusion.9.small_ref, f32[1,128]{1,0:T(1,128)S(1)} %broadcast_in_dim_reshape.3.column_ref, bf16[1024,1024]{1,0:T(8,128)(2,1)S(1)} %bitcast.80, bf16[1024,1024]{1,0:T(8,128)(2,1)S(1)} %collective-permute-done.1.other_ref, ...), custom_call_target="tpu_custom_call" | custom-call | tf_op jit(solution)/shard_map/pallas_call | solution.py:288
  50.1 2.9 %shard_map.139 = (f32[256,128]{1,0:T(8,128)S(1)}, f32[256,256]{1,0:T(8,128)S(1)}, f32[256,2048]{1,0:T(8,128)S(1)}, bf16[256,2048]{1,0:T(8,128)(2,1)S(1)}, bf16[256,2048]{1,0:T(8,128)(2,1)S(1)}) custom-call(f32[24,256]{1,0:T(8,128)S(1)} %pad_maximum_fusion.9.small_ref, f32[1,128]{1,0:T(1,128)S(1)} %broadcast_in_dim_reshape.3.column_ref, ...), custom_call_target="tpu_custom_call" | custom-call | tf_op jit(solution)/shard_map/pallas_call | solution.py:288
  53.0 3.8 %shard_map.140 = (f32[2,16,3072]{2,1,0:T(8,128)S(1)}, f32[2,16,3072]{2,1,0:T(8,128)S(1)}, f32[2,16,3072]{2,1,0:T(8,128)S(1)}, f32[2,16,3072]{2,1,0:T(8,128)S(1)}...) custom-call(f32[24,256]{1,0:T(8,128)S(1)} %pad_maximum_fusion.9.small_ref, ...), custom_call_target="tpu_custom_call" | custom-call | tf_op jit(solution)/shard_map/pallas_call | solution.py:288
  58.0 1.7 %collective-permute-start.18 = (f16[2,16,3200]{2,1,0:T(8,128)(2,1)S(1)}, f16[2,16,3200]{2,1,0:T(8,128)(2,1)S(1)}, u32[]{:S(2)}, u32[]{:S(2)}) collective-permute-start(f16[2,16,3200]{2,1,0:T(8,128)(2,1)S(1)} %pad_maximum_fusion.1), channel_id=1, source_target_pairs={{0,2},{1,3},{2,0},{3,1},{4,6},{5,7},{6,4},{7,5},{8,10},{9,11},{10,... | collective-permute-start | bytes 614408 | tf_op jit(solution)/shard_map/ppermute | solution.py:211
  61.2 3.3 %shard_map.141 = (f32[2,16,3072]{2,1,0:T(8,128)S(1)}, f32[2,16,3072]{2,1,0:T(8,128)S(1)}, f32[2,16,3072]{2,1,0:T(8,128)S(1)}, f32[2,16,3072]{2,1,0:T(8,128)S(1)}) custom-call(f32[24,256]{1,0:T(8,128)S(1)} %pad_maximum_fusion.9.small_ref, f32[1,128]{1,0:T(1,128)S(1)} %broadcast_in_dim_reshape.3.column_ref, bf16[1024,1024]{1,0:T(8,128)(2,1)S(1)} %bitcast.82, ...), custom_call_target="tpu_custom_call" | custom-call | tf_op jit(solution)/shard_map/pallas_call | solution.py:288
  65.2 4.0 %collective-permute-done.18 = f16[2,16,3200]{2,1,0:T(8,128)(2,1)S(1)} collective-permute-done((f16[2,16,3200]{2,1,0:T(8,128)(2,1)S(1)}, f16[2,16,3200]{2,1,0:T(8,128)(2,1)S(1)}, u32[]{:S(2)}, u32[]{:S(2)}) %collective-permute-start.18) | collective-permute-done | bytes 204832 | tf_op jit(solution)/shard_map/ppermute | solution.py:211
  71.2 2.9 %collective-permute-start.21 = (f16[16,3200]{1,0:T(8,128)(2,1)S(1)}, f16[16,3200]{1,0:T(8,128)(2,1)S(1)}, u32[]{:S(2)}, u32[]{:S(2)}) collective-permute-start(f16[16,3200]{1,0:T(8,128)(2,1)S(1)} %get-tuple-element.53), channel_id=1, source_target_pairs={{0,12},{1,13},{2,14},{3,15},{4,8},{5,9},{6,10},{7,11},{8,4},{9,5},... | collective-permute-start | bytes 307208 | tf_op jit(solution)/shard_map/ppermute | solution.py:211
  77.7 1.7 %collective-permute-done.21 = f16[16,3200]{1,0:T(8,128)(2,1)S(1)} collective-permute-done((f16[16,3200]{1,0:T(8,128)(2,1)S(1)}, f16[16,3200]{1,0:T(8,128)(2,1)S(1)}, u32[]{:S(2)}, u32[]{:S(2)}) %collective-permute-start.21) | collective-permute-done | bytes 102432 | tf_op jit(solution)/shard_map/ppermute | solution.py:211
  79.5 4.2 %collective-permute-done.20 = f16[16,3200]{1,0:T(8,128)(2,1)S(1)} collective-permute-done((f16[16,3200]{1,0:T(8,128)(2,1)S(1)}, f16[16,3200]{1,0:T(8,128)(2,1)S(1)}, u32[]{:S(2)}, u32[]{:S(2)}) %collective-permute-start.20) | collective-permute-done | bytes 102432 | tf_op jit(solution)/shard_map/ppermute | solution.py:211
  86.5 2.7 %collective-permute-start.26 = (f16[16,3200]{1,0:T(8,128)(2,1)S(1)}, f16[16,3200]{1,0:T(8,128)(2,1)S(1)}, u32[]{:S(2)}, u32[]{:S(2)}) collective-permute-start(f16[16,3200]{1,0:T(8,128)(2,1)S(1)} %get-tuple-element.51), channel_id=1, source_target_pairs={{0,12},{1,13},{2,14},{3,15},{4,8},{5,9},{6,10},{7,11},{8,4},{9,5},... | collective-permute-start | bytes 307208 | tf_op jit(solution)/shard_map/ppermute | solution.py:211
  90.9 3.4 %collective-permute-done.26 = f16[16,3200]{1,0:T(8,128)(2,1)S(1)} collective-permute-done((f16[16,3200]{1,0:T(8,128)(2,1)S(1)}, f16[16,3200]{1,0:T(8,128)(2,1)S(1)}, u32[]{:S(2)}, u32[]{:S(2)}) %collective-permute-start.26) | collective-permute-done | bytes 102432 | tf_op jit(solution)/shard_map/ppermute | solution.py:211
  94.5 4.2 %collective-permute-done.25 = f16[16,3200]{1,0:T(8,128)(2,1)S(1)} collective-permute-done((f16[16,3200]{1,0:T(8,128)(2,1)S(1)}, f16[16,3200]{1,0:T(8,128)(2,1)S(1)}, u32[]{:S(2)}, u32[]{:S(2)}) %collective-permute-start.25) | collective-permute-done | bytes 102432 | tf_op jit(solution)/shard_map/ppermute | solution.py:211
  (135 shorter events, 27.9 us)
Async XLA Ops:
  1.6 16.4 %collective-permute-start.3 = (f16[2,16,1024]{2,1,0:T(8,128)(2,1)S(1)}, f16[2,16,1024]{2,1,0:T(8,128)(2,1)S(1)}, u32[]{:S(2)}, u32[]{:S(2)}) collective-permute-start(f16[2,16,1024]{2,1,0:T(8,128)(2,1)S(1)} %fusion.11), channel_id=1, source_target_pairs={{0,4},{1,5},{2,6},{3,7},{4,0},{5,1},{6,2},{7,3},{8,12},{9,13},{10,... | collective-permute-start | bytes 196616 | tf_op jit(solution)/shard_map/ppermute | solution.py:211
  4.6 16.9 %collective-permute-start.4 = (f16[2,16,1024]{2,1,0:T(8,128)(2,1)S(1)}, f16[2,16,1024]{2,1,0:T(8,128)(2,1)S(1)}, u32[]{:S(2)}, u32[]{:S(2)}) collective-permute-start(f16[2,16,1024]{2,1,0:T(8,128)(2,1)S(1)} %fusion.11), channel_id=1, source_target_pairs={{0,8},{1,9},{2,10},{3,11},{4,12},{5,13},{6,14},{7,15},{8,0},{9,1},... | collective-permute-start | bytes 196616 | tf_op jit(solution)/shard_map/ppermute | solution.py:211
  7.2 14.6 %collective-permute-start.5 = (f16[2,16,1024]{2,1,0:T(8,128)(2,1)S(1)}, f16[2,16,1024]{2,1,0:T(8,128)(2,1)S(1)}, u32[]{:S(2)}, u32[]{:S(2)}) collective-permute-start(f16[2,16,1024]{2,1,0:T(8,128)(2,1)S(1)} %fusion.11), channel_id=1, source_target_pairs={{0,12},{1,13},{2,14},{3,15},{4,8},{5,9},{6,10},{7,11},{8,4},{9,5},... | collective-permute-start | bytes 196616 | tf_op jit(solution)/shard_map/ppermute | solution.py:211
  7.2 14.8 %collective-permute-start.6 = (f16[2,16,1024]{2,1,0:T(8,128)(2,1)S(1)}, f16[2,16,1024]{2,1,0:T(8,128)(2,1)S(1)}, u32[]{:S(2)}, u32[]{:S(2)}) collective-permute-start(f16[2,16,1024]{2,1,0:T(8,128)(2,1)S(1)} %fusion.11), channel_id=1, source_target_pairs={{0,2},{1,3},{2,0},{3,1},{4,6},{5,7},{6,4},{7,5},{8,10},{9,11},{10,... | collective-permute-start | bytes 196616 | tf_op jit(solution)/shard_map/ppermute | solution.py:211
  14.4 23.1 %collective-permute-start.10 = (f16[2,16,2176]{2,1,0:T(8,128)(2,1)S(1)}, f16[2,16,2176]{2,1,0:T(8,128)(2,1)S(1)}, u32[]{:S(2)}, u32[]{:S(2)}) collective-permute-start(f16[2,16,2176]{2,1,0:T(8,128)(2,1)S(1)} %pad_maximum_fusion.4), channel_id=1, source_target_pairs={{0,4},{1,5},{2,6},{3,7},{4,0},{5,1},{6,2},{7,3},{8,12},{9,13},{10,... | collective-permute-start | bytes 417800 | tf_op jit(solution)/shard_map/ppermute | solution.py:211
  18.0 19.2 %collective-permute-start.11 = (f16[2,16,2176]{2,1,0:T(8,128)(2,1)S(1)}, f16[2,16,2176]{2,1,0:T(8,128)(2,1)S(1)}, u32[]{:S(2)}, u32[]{:S(2)}) collective-permute-start(f16[2,16,2176]{2,1,0:T(8,128)(2,1)S(1)} %pad_maximum_fusion.4), channel_id=1, source_target_pairs={{0,8},{1,9},{2,10},{3,11},{4,12},{5,13},{6,14},{7,15},{8,0},{9,1},... | collective-permute-start | bytes 417800 | tf_op jit(solution)/shard_map/ppermute | solution.py:211
  21.5 13.9 %collective-permute-start.12 = (f16[2,16,2176]{2,1,0:T(8,128)(2,1)S(1)}, f16[2,16,2176]{2,1,0:T(8,128)(2,1)S(1)}, u32[]{:S(2)}, u32[]{:S(2)}) collective-permute-start(f16[2,16,2176]{2,1,0:T(8,128)(2,1)S(1)} %pad_maximum_fusion.4), channel_id=1, source_target_pairs={{0,12},{1,13},{2,14},{3,15},{4,8},{5,9},{6,10},{7,11},{8,4},{9,5},... | collective-permute-start | bytes 417800 | tf_op jit(solution)/shard_map/ppermute | solution.py:211
  21.9 25.8 %collective-permute-start.1 = (bf16[1024,1024]{1,0:T(8,128)(2,1)S(1)}, bf16[1024,1024]{1,0:T(8,128)(2,1)S(1)}, u32[]{:S(2)}, u32[]{:S(2)}) collective-permute-start(bf16[1024,1024]{1,0:T(8,128)(2,1)S(1)} %bitcast.79), channel_id=1, source_target_pairs={{0,1},{1,0},{2,3},{3,2},{4,5},{5,4},{6,7},{7,6},{8,9},{9,8},{10,11... | collective-permute-start | bytes 6291464 | tf_op jit(solution)/shard_map/ppermute | solution.py:211
  22.0 4.6 %collective-permute-start.7 = (f16[2,16,1024]{2,1,0:T(8,128)(2,1)S(1)}, f16[2,16,1024]{2,1,0:T(8,128)(2,1)S(1)}, u32[]{:S(2)}, u32[]{:S(2)}) collective-permute-start(f16[2,16,1024]{2,1,0:T(8,128)(2,1)S(1)} %collective-permute-done.3), channel_id=1, source_target_pairs={{0,2},{1,3},{2,0},{3,1},{4,6},{5,7},{6,4},{7,5},{8,10},{9,11},{10,... | collective-permute-start | bytes 196616 | tf_op jit(solution)/shard_map/ppermute | solution.py:211
  35.1 6.6 %collective-permute-start.13 = (f16[2,16,2176]{2,1,0:T(8,128)(2,1)S(1)}, f16[2,16,2176]{2,1,0:T(8,128)(2,1)S(1)}, u32[]{:S(2)}, u32[]{:S(2)}) collective-permute-start(f16[2,16,2176]{2,1,0:T(8,128)(2,1)S(1)} %pad_maximum_fusion.4), channel_id=1, source_target_pairs={{0,2},{1,3},{2,0},{3,1},{4,6},{5,7},{6,4},{7,5},{8,10},{9,11},{10,... | collective-permute-start | bytes 417800 | tf_op jit(solution)/shard_map/ppermute | solution.py:211
  35.5 8.9 %collective-permute-start.16 = (f16[2,16,2176]{2,1,0:T(8,128)(2,1)S(1)}, f16[2,16,2176]{2,1,0:T(8,128)(2,1)S(1)}, u32[]{:S(2)}, u32[]{:S(2)}) collective-permute-start(f16[2,16,2176]{2,1,0:T(8,128)(2,1)S(1)} %collective-permute-done.12), channel_id=1, source_target_pairs={{0,2},{1,3},{2,0},{3,1},{4,6},{5,7},{6,4},{7,5},{8,10},{9,11},{10,... | collective-permute-start | bytes 417800 | tf_op jit(solution)/shard_map/ppermute | solution.py:211
  37.2 8.6 %collective-permute-start.15 = (f16[2,16,2176]{2,1,0:T(8,128)(2,1)S(1)}, f16[2,16,2176]{2,1,0:T(8,128)(2,1)S(1)}, u32[]{:S(2)}, u32[]{:S(2)}) collective-permute-start(f16[2,16,2176]{2,1,0:T(8,128)(2,1)S(1)} %collective-permute-done.11), channel_id=1, source_target_pairs={{0,2},{1,3},{2,0},{3,1},{4,6},{5,7},{6,4},{7,5},{8,10},{9,11},{10,... | collective-permute-start | bytes 417800 | tf_op jit(solution)/shard_map/ppermute | solution.py:211
  37.5 9.8 %collective-permute-start.14 = (f16[2,16,2176]{2,1,0:T(8,128)(2,1)S(1)}, f16[2,16,2176]{2,1,0:T(8,128)(2,1)S(1)}, u32[]{:S(2)}, u32[]{:S(2)}) collective-permute-start(f16[2,16,2176]{2,1,0:T(8,128)(2,1)S(1)} %collective-permute-done.10), channel_id=1, source_target_pairs={{0,2},{1,3},{2,0},{3,1},{4,6},{5,7},{6,4},{7,5},{8,10},{9,11},{10,... | collective-permute-start | bytes 417800 | tf_op jit(solution)/shard_map/ppermute | solution.py:211
  41.7 11.3 %collective-permute-start.2 = (bf16[128,2048]{1,0:T(8,128)(2,1)S(1)}, bf16[128,2048]{1,0:T(8,128)(2,1)S(1)}, u32[]{:S(2)}, u32[]{:S(2)}) collective-permute-start(bf16[128,2048]{1,0:T(8,128)(2,1)S(1)} %copy-done), channel_id=1, source_target_pairs={{0,1},{1,0},{2,3},{3,2},{4,5},{5,4},{6,7},{7,6},{8,9},{9,8},{10,11... | collective-permute-start | bytes 1572872 | tf_op jit(solution)/shard_map/ppermute | solution.py:211
  57.2 7.9 %collective-permute-start.17 = (f16[2,16,3200]{2,1,0:T(8,128)(2,1)S(1)}, f16[2,16,3200]{2,1,0:T(8,128)(2,1)S(1)}, u32[]{:S(2)}, u32[]{:S(2)}) collective-permute-start(f16[2,16,3200]{2,1,0:T(8,128)(2,1)S(1)} %pad_maximum_fusion), channel_id=1, source_target_pairs={{0,2},{1,3},{2,0},{3,1},{4,6},{5,7},{6,4},{7,5},{8,10},{9,11},{10,... | collective-permute-start | bytes 614408 | tf_op jit(solution)/shard_map/ppermute | solution.py:211
  58.0 11.1 %collective-permute-start.18 = (f16[2,16,3200]{2,1,0:T(8,128)(2,1)S(1)}, f16[2,16,3200]{2,1,0:T(8,128)(2,1)S(1)}, u32[]{:S(2)}, u32[]{:S(2)}) collective-permute-start(f16[2,16,3200]{2,1,0:T(8,128)(2,1)S(1)} %pad_maximum_fusion.1), channel_id=1, source_target_pairs={{0,2},{1,3},{2,0},{3,1},{4,6},{5,7},{6,4},{7,5},{8,10},{9,11},{10,... | collective-permute-start | bytes 614408 | tf_op jit(solution)/shard_map/ppermute | solution.py:211
  69.7 7.9 %collective-permute-start.22 = (f16[16,3200]{1,0:T(8,128)(2,1)S(1)}, f16[16,3200]{1,0:T(8,128)(2,1)S(1)}, u32[]{:S(2)}, u32[]{:S(2)}) collective-permute-start(f16[16,3200]{1,0:T(8,128)(2,1)S(1)} %pad_maximum_fusion.7), channel_id=1, source_target_pairs={{0,4},{1,5},{2,6},{3,7},{4,0},{5,1},{6,2},{7,3},{8,12},{9,13},{10,... | collective-permute-start | bytes 307208 | tf_op jit(solution)/shard_map/ppermute | solution.py:211
  71.2 8.2 %collective-permute-start.21 = (f16[16,3200]{1,0:T(8,128)(2,1)S(1)}, f16[16,3200]{1,0:T(8,128)(2,1)S(1)}, u32[]{:S(2)}, u32[]{:S(2)}) collective-permute-start(f16[16,3200]{1,0:T(8,128)(2,1)S(1)} %get-tuple-element.53), channel_id=1, source_target_pairs={{0,12},{1,13},{2,14},{3,15},{4,8},{5,9},{6,10},{7,11},{8,4},{9,5},... | collective-permute-start | bytes 307208 | tf_op jit(solution)/shard_map/ppermute | solution.py:211
  74.1 9.6 %collective-permute-start.20 = (f16[16,3200]{1,0:T(8,128)(2,1)S(1)}, f16[16,3200]{1,0:T(8,128)(2,1)S(1)}, u32[]{:S(2)}, u32[]{:S(2)}) collective-permute-start(f16[16,3200]{1,0:T(8,128)(2,1)S(1)} %get-tuple-element.52), channel_id=1, source_target_pairs={{0,8},{1,9},{2,10},{3,11},{4,12},{5,13},{6,14},{7,15},{8,0},{9,1},... | collective-permute-start | bytes 307208 | tf_op jit(solution)/shard_map/ppermute | solution.py:211
  75.1 10.2 %collective-permute-start.23 = (f16[2,16,3200]{2,1,0:T(8,128)(2,1)S(1)}, f16[2,16,3200]{2,1,0:T(8,128)(2,1)S(1)}, u32[]{:S(2)}, u32[]{:S(2)}) collective-permute-start(f16[2,16,3200]{2,1,0:T(8,128)(2,1)S(1)} %pad_maximum_fusion.2), channel_id=1, source_target_pairs={{0,2},{1,3},{2,0},{3,1},{4,6},{5,7},{6,4},{7,5},{8,10},{9,11},{10,... | collective-permute-start | bytes 614408 | tf_op jit(solution)/shard_map/ppermute | solution.py:211
  76.1 9.9 %collective-permute-start.24 = (f16[2,16,3200]{2,1,0:T(8,128)(2,1)S(1)}, f16[2,16,3200]{2,1,0:T(8,128)(2,1)S(1)}, u32[]{:S(2)}, u32[]{:S(2)}) collective-permute-start(f16[2,16,3200]{2,1,0:T(8,128)(2,1)S(1)} %pad_maximum_fusion.3), channel_id=1, source_target_pairs={{0,2},{1,3},{2,0},{3,1},{4,6},{5,7},{6,4},{7,5},{8,10},{9,11},{10,... | collective-permute-start | bytes 614408 | tf_op jit(solution)/shard_map/ppermute | solution.py:211
  85.8 5.0 %collective-permute-start.27 = (f16[16,3200]{1,0:T(8,128)(2,1)S(1)}, f16[16,3200]{1,0:T(8,128)(2,1)S(1)}, u32[]{:S(2)}, u32[]{:S(2)}) collective-permute-start(f16[16,3200]{1,0:T(8,128)(2,1)S(1)} %pad_maximum_fusion.8), channel_id=1, source_target_pairs={{0,4},{1,5},{2,6},{3,7},{4,0},{5,1},{6,2},{7,3},{8,12},{9,13},{10,... | collective-permute-start | bytes 307208 | tf_op jit(solution)/shard_map/ppermute | solution.py:211
  86.5 7.8 %collective-permute-start.26 = (f16[16,3200]{1,0:T(8,128)(2,1)S(1)}, f16[16,3200]{1,0:T(8,128)(2,1)S(1)}, u32[]{:S(2)}, u32[]{:S(2)}) collective-permute-start(f16[16,3200]{1,0:T(8,128)(2,1)S(1)} %get-tuple-element.51), channel_id=1, source_target_pairs={{0,12},{1,13},{2,14},{3,15},{4,8},{5,9},{6,10},{7,11},{8,4},{9,5},... | collective-permute-start | bytes 307208 | tf_op jit(solution)/shard_map/ppermute | solution.py:211
  89.2 9.4 %collective-permute-start.25 = (f16[16,3200]{1,0:T(8,128)(2,1)S(1)}, f16[16,3200]{1,0:T(8,128)(2,1)S(1)}, u32[]{:S(2)}, u32[]{:S(2)}) collective-permute-start(f16[16,3200]{1,0:T(8,128)(2,1)S(1)} %get-tuple-element.50), channel_id=1, source_target_pairs={{0,8},{1,9},{2,10},{3,11},{4,12},{5,13},{6,14},{7,15},{8,0},{9,1},... | collective-permute-start | bytes 307208 | tf_op jit(solution)/shard_map/ppermute | solution.py:211
  (9 other events, 90.8 us)

commit v5 on v4

--- a/solution.py
+++ b/solution.py
@@ -37,14 +37,14 @@
     return experts, gates, small[:, 2 * top : 2 * top + 1]
 
 
-def stacked(refs, width):
-    rows = [ref[:, kind, :, :width].reshape(-1, width) for kind in range(2) for ref in refs]
+def stacked(chip_ref, masks, factor_ref, width):
+    rows = [factor_ref[chip_ref[0] ^ mask, kind, :, :width] for kind in range(2) for mask in masks]
     return halves(jnp.concatenate(rows, axis=0))
 
 
-def reduce_kernel(top, small_ref, column_ref, own_ref, other_ref, factor_ref, reduced_ref):
+def reduce_kernel(top, masks, chip_ref, small_ref, column_ref, own_ref, other_ref, factor_ref, reduced_ref):
     experts, _, _ = token_columns(small_ref, top)
-    high, low = stacked([factor_ref], own_ref.shape[1])
+    high, low = stacked(chip_ref, masks, factor_ref, own_ref.shape[1])
     wide = high.shape[0] // 2
     tokens = own_ref.shape[0] // top
     for block, hidden_ref in enumerate((own_ref, other_ref)):
@@ -58,22 +58,21 @@
         reduced_ref[1, rows] = total[:, wide:]
 
 
-def rank_limits(rank, column_ref, capacity_ref, factor_refs):
+def rank_limits(rank, column_ref, capacity_ref, factor_ref):
     wide = column_ref.shape[1]
     member = [column_ref[:, start : start + 1] for start in range(0, wide, rank)]
     me = member[0]
-    across = 1.0 - 2.0 * (me - 2.0 * jnp.floor(me * 0.5))
+    core = me - 2.0 * jnp.floor(me * 0.5)
+    across = 1.0 - 2.0 * core
     left = []
     for block in (me, me + across):
         total = capacity_ref[...]
-        slot = 0
-        for ref in factor_refs:
-            for piece in range(ref.shape[0]):
-                own = ref[piece, 0, 0:1, ref.shape[3] - lanes :]
-                other = ref[piece, 0, 1:2, ref.shape[3] - lanes :]
-                total = total - jnp.where(member[slot] < block, own, 0.0)
-                total = total - jnp.where(member[slot] + across < block, other, 0.0)
-                slot += 1
+        for chip in range(factor_ref.shape[0]):
+            own = factor_ref[chip, 0, 0:1, factor_ref.shape[3] - lanes :]
+            other = factor_ref[chip, 0, 1:2, factor_ref.shape[3] - lanes :]
+            device = 2.0 * chip + core
+            total = total - jnp.where(device < block, own, 0.0)
+            total = total - jnp.where(device + across < block, other, 0.0)
         left.append(total)
     lane = lax.broadcasted_iota(jnp.int32, (1, lanes), 1).astype(f32)
     slot_of = lax.broadcasted_iota(jnp.int32, (1, wide), 1) // rank
@@ -87,12 +86,12 @@
     return limits
 
 
-def tangent_kernel(top, small_ref, column_ref, capacity_ref, reduced_ref, near_ref, far_ref, *outs):
+def tangent_kernel(top, masks, chip_ref, small_ref, column_ref, capacity_ref, reduced_ref, factor_ref, *outs):
     weight_ref, weighted_ref, tangent_ref, high_ref, low_ref = outs
     experts, gates, _ = token_columns(small_ref, top)
     tokens, wide = weight_ref.shape
     block = tokens // 2
-    limits = rank_limits(near_ref.shape[2], column_ref, capacity_ref, (near_ref, far_ref))
+    limits = rank_limits(factor_ref.shape[2], column_ref, capacity_ref, factor_ref)
     gate = jnp.zeros((tokens, wide), f32)
     member = jnp.zeros((tokens, wide), f32)
     for k in range(top):
@@ -113,7 +112,7 @@
     weight_ref[...] = weight
     weighted = jnp.concatenate([weight * reduced_ref[0], weight * reduced_ref[1]], axis=1)
     weighted_ref[...] = weighted
-    factor = stacked([near_ref, far_ref], high_ref.shape[1])
+    factor = stacked(chip_ref, masks, factor_ref, high_ref.shape[1])
     high_ref[...], low_ref[...] = factor
     tangent_ref[...] = dot_pairs(halves(weighted), factor, 1, 0)
 
@@ -236,8 +235,10 @@
     down_direction,
     up_direction,
 ):
-    rows = lax.axis_size("expert") // 4
-    masks = [4 * z for z in range(rows)] + [4 * z + 2 for z in range(rows)]
+    size = lax.axis_size("expert")
+    rows = size // 4
+    masks = [2 * z for z in range(rows)] + [2 * z + 1 for z in range(rows)]
+    cores = [list(range(core, size, 2)) for core in range(2)]
     me = lax.axis_index("expert")
     tokens, top = expert_of_route.shape
     hidden_width = hidden_of_route.shape[2]
@@ -248,11 +249,10 @@
     names = jnp.arange(experts, dtype=f32)
 
     def gather(own):
-        near = [own] + [exchange(own, 4 * z) for z in range(1, rows)]
-        return near, [exchange(piece, 2) for piece in near]
+        return lax.all_gather(own, "expert", axis_index_groups=cores)
 
     own_down = (down_scale * jnp.concatenate([down_direction, adapter_down]).transpose(0, 2, 1)).astype(f16)
-    down_near, down_far = gather(own_down)
+    down_factors = gather(own_down).astype(f32) * (1 / down_scale)
 
     small = jnp.concatenate(
         [
@@ -274,32 +274,42 @@
         ],
         axis=2,
     ).astype(f16)
-    up_near, up_far = gather(own_up)
+    unscale = jnp.concatenate([jnp.full((model_width,), 1 / up_scale, f32), jnp.ones((lanes,), f32)])
+    up_factors = gather(own_up).astype(f32) * unscale
 
     hidden_of_route, _ = lax.optimization_barrier((hidden_of_route, own_up))
     small = jnp.concatenate([small, small_other], axis=1)
     hidden = hidden_of_route.transpose(1, 0, 2).reshape(top * tokens, hidden_width)
     hidden_other = exchange(hidden, 1)
     gradient_other = exchange(output_gradient, 1)
-    column = jnp.repeat((me ^ jnp.array(masks, jnp.int32)).astype(f32), rank)[None, :]
+    chip = (me // 2)[None]
+    column = jnp.repeat((me ^ (2 * jnp.array(masks, jnp.int32))).astype(f32), rank)[None, :]
     capacity_row = jnp.pad(capacity.astype(f32), (0, lanes - experts))[None, :]
 
     def call(kernel, outs, *operands, scratch=()):
+        places = [
+            pl.BlockSpec(memory_space=pltpu.SMEM if operand is chip else pltpu.VMEM) for operand in operands
+        ]
         return pl.pallas_call(
-            functools.partial(kernel, top),
+            kernel,
             out_shape=[jax.ShapeDtypeStruct(shape, dtype) for shape, dtype in outs],
+            in_specs=places,
             scratch_shapes=scratch,
             compiler_params=pltpu.CompilerParams(vmem_limit_bytes=kernel_vmem),
         )(*operands)
 
-    down_factors = jnp.stack(down_near + down_far).astype(f32) * (1 / down_scale)
-    down_factors, *_ = lax.optimization_barrier((down_factors, *up_near))
     (reduced,) = call(
-        reduce_kernel, [((2, 2 * tokens, wide), f32)], small, column, hidden, hidden_other, down_factors
-    )
-    unscale = jnp.concatenate([jnp.full((model_width,), 1 / up_scale, f32), jnp.ones((lanes,), f32)])
+        functools.partial(reduce_kernel, top, masks),
+        [((2, 2 * tokens, wide), f32)],
+        chip,
+        small,
+        column,
+        hidden,
+        hidden_other,
+        down_factors,
+    )
     weight, weighted, tangent, high, low = call(
-        tangent_kernel,
+        functools.partial(tangent_kernel, top, masks),
         [
             ((2 * tokens, wide), f32),
             ((2 * tokens, 2 * wide), f32),
@@ -307,18 +317,18 @@
             ((2 * wide, model_width), bf16),
             ((2 * wide, model_width), bf16),
         ],
+        chip,
         small,
         column,
         capacity_row,
         reduced,
-        jnp.stack(up_near).astype(f32) * unscale,
-        jnp.stack(up_far).astype(f32) * unscale,
+        up_factors,
     )
     arrived = exchange(tangent, 1)
     left = [pltpu.VMEM((2, top * tokens, 2 * wide), bf16)]
     chunks = [((rows // 2, rank, hidden_width + model_width), f32)] * 4
     *gradients, up, to = call(
-        gradient_kernel,
+        functools.partial(gradient_kernel, top),
         chunks + [((wide, model_width), f32), ((2 * tokens, wide), f32)],
         small,
         column,
@@ -332,8 +342,11 @@
         low,
         scratch=left,
     )
+    coded = encode(gradients[3]), encode(gradients[2])
+    gradients_far, gradients_near = [exchange(part, 2) for part in coded]
+    arrived, _ = lax.optimization_barrier((arrived, coded))
     curvatures = call(
-        curvature_kernel,
+        functools.partial(curvature_kernel, top),
         chunks,
         small,
         column,
@@ -350,23 +363,21 @@
         scratch=left,
     )
 
-    def along_x(parts):
-        later = exchange(encode(parts[3]), 2)
-        sooner = exchange(encode(parts[2]), 2)
-        return sooner, later
-
-    def along_z(parts, moved):
-        later = encode(parts[1] + decode(moved[1]))
-        arrived = [exchange(later[z - rows // 2], 4 * z) for z in range(rows // 2, rows)]
-        sooner = parts[0] + decode(moved[0])
-        arrived += [exchange(encode(sooner[z]), 4 * z) for z in range(1, rows // 2)]
-        return sooner[0] + sum(decode(piece) for piece in arrived)
-
-    gradients_moved = along_x(gradients)
-    gradients_moved, curvatures = lax.optimization_barrier((gradients_moved, curvatures))
-    curvatures_moved = along_x(curvatures)
-    gradient_sum = along_z(gradients, gradients_moved)
-    curvature_sum = along_z(curvatures, curvatures_moved)
+    coded = encode(curvatures[3]), encode(curvatures[2])
+    curvatures_far, curvatures_near = [exchange(part, 2) for part in coded]
+
+    def along_z(parts):
+        return [exchange(parts[z - rows // 2], 4 * z) for z in range(rows // 2, rows)]
+
+    gradients_far, _ = lax.optimization_barrier((gradients_far, coded))
+    gradients_far = along_z(encode(gradients[1] + decode(gradients_far)))
+    curvatures_far = along_z(encode(curvatures[1] + decode(curvatures_far)))
+    near = jnp.stack([gradients[0] + decode(gradients_near), curvatures[0] + decode(curvatures_near)])
+    total = near[:, 0]
+    for z in range(1, rows // 2):
+        total = total + decode(exchange(encode(near[:, z]), 4 * z))
+    gradient_sum = total[0] + sum(decode(part) for part in gradients_far)
+    curvature_sum = total[1] + sum(decode(part) for part in curvatures_far)
     return (
         gradient_sum[:, :hidden_width].T[None],
         gradient_sum[None, :, hidden_width:],

time: 101 us -> 133 us (1.32)
  blocking collectives: 0 us -> 66.8 us
  waiting for transfers between devices: 40.2 us -> 20.8 us
  starting transfers between devices: 29.6 us -> 12.5 us
  Pallas kernels: 12.4 us -> 16.6 us
  other arithmetic: 10.7 us -> 8.4 us
    all_gather x0 -> x2, blocking collectives: none -> 66.8 us  [gather(): return lax.all_gather(own, 'expert', axis_index_groups=cores)]
    ppermute x28 -> x13, waiting for transfers between devices: 40.2 us -> 20.8 us  [exchange(): lax.ppermute(value, 'expert', [(device, device ^ mask) for device in rang...]
    ppermute x28 -> x13, starting transfers between devices: 29.6 us -> 12.5 us  [exchange(): lax.ppermute(value, 'expert', [(device, device ^ mask) for device in rang...]
    pallas_call x4, Pallas kernels: 12.4 us -> 16.6 us  [call(): pl.pallas_call(kernel, out_shape=[jax.ShapeDtypeStruct(shape, dtype) for...]
  transfers between devices with their start and end apart: 28 -> 13, of which waited for: 15 -> 7; matrix products, arithmetic and copies ran while one was open for 14% -> 6% of each run, Pallas kernels for 9% -> 8%
where the time goes in v5:
time: 133 us
  blocking collectives  66.8 us (50%)
  waiting for transfers between devices  20.8 us (16%)
  Pallas kernels  16.6 us (12%)
  starting transfers between devices  12.5 us (9%)
  other arithmetic  8.4 us (6%)
  local copies, waits for them, and re-layouts  6.78 us (5%)
    all_gather x2, blocking collectives, gather(): return lax.all_gather(own, 'expert', axis_index_groups=cores)  66.8 us
    ppermute x13, waiting for transfers between devices, exchange(): lax.ppermute(value, 'expert', [(device, device ^ mask) for device in rang...  20.8 us
    pallas_call x4, Pallas kernels, call(): pl.pallas_call(kernel, out_shape=[jax.ShapeDtypeStruct(shape, dtype) for...  16.6 us
    ppermute x13, starting transfers between devices, exchange(): lax.ppermute(value, 'expert', [(device, device ^ mask) for device in rang...  12.5 us
    transpose x1, local copies, waits for them, and re-layouts, gathered_plan(): hidden_of_route.transpose(1, 0, 2).reshape(top * tokens, hidden_width)  2.78 us
  transfers between devices with their start and end apart: 13, of which 7 were waited for; matrix products, arithmetic and copies ran while one was open for 6% of the time, Pallas kernels for 8%

profile of v5, /device:TPU:0, one launch (start us, length us, event | category | flops | bytes accessed | tf_op | source)
XLA Modules:
  0.0 132.8 jit_solution(12905240786927360562)
XLA Ops:
  1.3 0.7 convert_bitcast_fusion.1
  2.0 1.3 pad_maximum_fusion.10
  3.7 2.8 %copy.18 = bf16[8,128,1024]{2,1,0:T(8,128)(2,1)S(1)} copy(bf16[8,128,1024]{2,0,1:T(8,128)(2,1)} %bitcast.64) | data formatting | bytes 4194304 | tf_op jit(solution)/shard_map/transpose | solution.py:282
  7.2 33.0 %all-gather = f16[16,16,1024]{2,1,0:T(8,128)(2,1)S(1)} all-gather(f16[2,16,1024]{2,1,0:T(8,128)(2,1)S(1)} %fusion.15), channel_id=2, replica_groups={{0,2,4,6,8,10,12,14},{1,3,5,7,9,11,13,15},{16,18,20,22,24,26,28,30},{17..., dimensions={0}, use_global_device_ids=true | all-gather | bytes 589824 | tf_op jit(solution)/shard_map/all_gather | solution.py:252
  41.5 0.7 pad_maximum_fusion.9.small_ref
  42.3 33.8 %all-gather.2 = f16[8,2,16,2176]{3,2,1,0:T(8,128)(2,1)S(1)} all-gather(f16[1,2,16,2176]{3,2,1,0:T(8,128)(2,1)S(1)} %pad_maximum_fusion.6), channel_id=1, replica_groups={{0,2,4,6,8,10,12,14},{1,3,5,7,9,11,13,15},{16,18,20,22,24,26,28,30},{17..., dimensions={0}, use_global_device_ids=true | all-gather | bytes 1253376 | tf_op jit(solution)/shard_map/all_gather | solution.py:252
  76.1 0.9 convert_multiply_fusion.factor_ref
  77.0 4.0 %shard_map.138.reduced_ref = f32[2,256,128]{2,1,0:T(8,128)S(1)} custom-call(s32[1]{0:T(128)} %bitcast.5.chip_ref, f32[24,256]{1,0:T(8,128)S(1)} %pad_maximum_fusion.9.small_ref, f32[1,128]{1,0:T(1,128)S(1)} %broadcast_in_dim_reshape.3.column_ref, bf16[1024,1024]{1,0:T(8,128)(2,1)S(1)} %bitcast.60, bf16[1024,1024]{1,0:T(8,128)(2,1)} %collective-permute-done.1.other_ref, ...), custom_call_target="tpu_custom_call" | custom-call | tf_op jit(solution)/shard_map/pallas_call | solution.py:293
  81.0 2.3 %shard_map.139 = (f32[256,128]{1,0:T(8,128)S(1)}, f32[256,256]{1,0:T(8,128)S(1)}, f32[256,2048]{1,0:T(8,128)S(1)}, bf16[256,2048]{1,0:T(8,128)(2,1)S(1)}, bf16[256,2048]{1,0:T(8,128)(2,1)S(1)}) custom-call(s32[1]{0:T(128)} %bitcast.5.chip_ref, f32[24,256]{1,0:T(8,128)S(1)} %pad_maximum_fusion.9.small_ref, f32[1,128]{1,0:T(1,128)S(1)} %broadcast_in_dim_reshape.3.column_ref, ...), custom_call_target="tpu_custom_call" | custom-call | tf_op jit(solution)/shard_map/pallas_call | solution.py:293
  83.4 5.6 %shard_map.140 = (f32[2,16,3072]{2,1,0:T(8,128)S(1)}, f32[2,16,3072]{2,1,0:T(8,128)S(1)}, f32[2,16,3072]{2,1,0:T(8,128)S(1)}, f32[2,16,3072]{2,1,0:T(8,128)S(1)}...) custom-call(f32[24,256]{1,0:T(8,128)S(1)} %pad_maximum_fusion.9.small_ref, ...), custom_call_target="tpu_custom_call" | custom-call | tf_op jit(solution)/shard_map/pallas_call | solution.py:293
  89.7 1.4 %collective-permute-start.3 = (f16[2,16,3200]{2,1,0:T(8,128)(2,1)S(1)}, f16[2,16,3200]{2,1,0:T(8,128)(2,1)S(1)}, u32[]{:S(2)}, u32[]{:S(2)}) collective-permute-start(f16[2,16,3200]{2,1,0:T(8,128)(2,1)S(1)} %get-tuple-element.58), channel_id=1, source_target_pairs={{0,2},{1,3},{2,0},{3,1},{4,6},{5,7},{6,4},{7,5},{8,10},{9,11},{10,... | collective-permute-start | bytes 614408 | tf_op jit(solution)/shard_map/ppermute | solution.py:210
  91.1 0.7 collective-permute-start.7
  91.8 5.8 %collective-permute-done.3 = f16[2,16,3200]{2,1,0:T(8,128)(2,1)S(1)} collective-permute-done((f16[2,16,3200]{2,1,0:T(8,128)(2,1)S(1)}, f16[2,16,3200]{2,1,0:T(8,128)(2,1)S(1)}, u32[]{:S(2)}, u32[]{:S(2)}) %collective-permute-start.3) | collective-permute-done | bytes 204832 | tf_op jit(solution)/shard_map/ppermute | solution.py:210
  97.8 4.7 %shard_map.141 = (f32[2,16,3072]{2,1,0:T(8,128)S(1)}, f32[2,16,3072]{2,1,0:T(8,128)S(1)}, f32[2,16,3072]{2,1,0:T(8,128)S(1)}, f32[2,16,3072]{2,1,0:T(8,128)S(1)}) custom-call(f32[24,256]{1,0:T(8,128)S(1)} %pad_maximum_fusion.9.small_ref, f32[1,128]{1,0:T(1,128)S(1)} %broadcast_in_dim_reshape.3.column_ref, bf16[1024,1024]{1,0:T(8,128)(2,1)S(1)} %bitcast.62, ...), custom_call_target="tpu_custom_call" | custom-call | tf_op jit(solution)/shard_map/pallas_call | solution.py:293
  103.8 2.7 %collective-permute-start.9 = (f16[16,3200]{1,0:T(8,128)(2,1)S(1)}, f16[16,3200]{1,0:T(8,128)(2,1)S(1)}, u32[]{:S(2)}, u32[]{:S(2)}) collective-permute-start(f16[16,3200]{1,0:T(8,128)(2,1)S(1)} %get-tuple-element.43), channel_id=1, source_target_pairs={{0,12},{1,13},{2,14},{3,15},{4,8},{5,9},{6,10},{7,11},{8,4},{9,5},... | collective-permute-start | bytes 307208 | tf_op jit(solution)/shard_map/ppermute | solution.py:210
  106.6 2.0 %collective-permute-start.5 = (f16[2,16,3200]{2,1,0:T(8,128)(2,1)S(1)}, f16[2,16,3200]{2,1,0:T(8,128)(2,1)S(1)}, u32[]{:S(2)}, u32[]{:S(2)}) collective-permute-start(f16[2,16,3200]{2,1,0:T(8,128)(2,1)S(1)} %pad_maximum_fusion.3), channel_id=1, source_target_pairs={{0,2},{1,3},{2,0},{3,1},{4,6},{5,7},{6,4},{7,5},{8,10},{9,11},{10,... | collective-permute-start | bytes 614408 | tf_op jit(solution)/shard_map/ppermute | solution.py:210
  108.7 2.8 %collective-permute-done.9 = f16[16,3200]{1,0:T(8,128)(2,1)S(1)} collective-permute-done((f16[16,3200]{1,0:T(8,128)(2,1)S(1)}, f16[16,3200]{1,0:T(8,128)(2,1)S(1)}, u32[]{:S(2)}, u32[]{:S(2)}) %collective-permute-start.9) | collective-permute-done | bytes 102432 | tf_op jit(solution)/shard_map/ppermute | solution.py:210
  111.6 3.1 %collective-permute-done.8 = f16[16,3200]{1,0:T(8,128)(2,1)S(1)} collective-permute-done((f16[16,3200]{1,0:T(8,128)(2,1)S(1)}, f16[16,3200]{1,0:T(8,128)(2,1)S(1)}, u32[]{:S(2)}, u32[]{:S(2)}) %collective-permute-start.8) | collective-permute-done | bytes 102432 | tf_op jit(solution)/shard_map/ppermute | solution.py:210
  115.3 2.2 %collective-permute-done.10 = f16[2,16,3200]{2,1,0:T(8,128)(2,1)S(1)} collective-permute-done((f16[2,16,3200]{2,1,0:T(8,128)(2,1)S(1)}, f16[2,16,3200]{2,1,0:T(8,128)(2,1)S(1)}, u32[]{:S(2)}, u32[]{:S(2)}) %collective-permute-start.10) | collective-permute-done | bytes 204832 | tf_op jit(solution)/shard_map/ppermute | solution.py:210
  118.1 0.9 collective-permute-start.12
  119.2 3.6 %collective-permute-start.11 = (f16[16,3200]{1,0:T(8,128)(2,1)S(1)}, f16[16,3200]{1,0:T(8,128)(2,1)S(1)}, u32[]{:S(2)}, u32[]{:S(2)}) collective-permute-start(f16[16,3200]{1,0:T(8,128)(2,1)S(1)} %get-tuple-element.40), channel_id=1, source_target_pairs={{0,8},{1,9},{2,10},{3,11},{4,12},{5,13},{6,14},{7,15},{8,0},{9,1},... | collective-permute-start | bytes 307208 | tf_op jit(solution)/shard_map/ppermute | solution.py:210
  122.7 3.1 %collective-permute-done.12 = f16[16,3200]{1,0:T(8,128)(2,1)S(1)} collective-permute-done((f16[16,3200]{1,0:T(8,128)(2,1)S(1)}, f16[16,3200]{1,0:T(8,128)(2,1)S(1)}, u32[]{:S(2)}, u32[]{:S(2)}) %collective-permute-start.12) | collective-permute-done | bytes 102432 | tf_op jit(solution)/shard_map/ppermute | solution.py:210
  126.0 1.5 %collective-permute-done.11 = f16[16,3200]{1,0:T(8,128)(2,1)S(1)} collective-permute-done((f16[16,3200]{1,0:T(8,128)(2,1)S(1)}, f16[16,3200]{1,0:T(8,128)(2,1)S(1)}, u32[]{:S(2)}, u32[]{:S(2)}) %collective-permute-start.11) | collective-permute-done | bytes 102432 | tf_op jit(solution)/shard_map/ppermute | solution.py:210
  127.6 2.2 %collective-permute-done.6 = f16[2,16,3200]{2,1,0:T(8,128)(2,1)S(1)} collective-permute-done((f16[2,16,3200]{2,1,0:T(8,128)(2,1)S(1)}, f16[2,16,3200]{2,1,0:T(8,128)(2,1)S(1)}, u32[]{:S(2)}, u32[]{:S(2)}) %collective-permute-start.6) | collective-permute-done | bytes 204832 | tf_op jit(solution)/shard_map/ppermute | solution.py:210
  (94 shorter events, 10.1 us)
Async XLA Ops:
  2.0 1.7 %copy-start.4 = (f32[7,128]{1,0:T(8,128)}, f32[7,128]{1,0:T(8,128)S(1)}, u32[]{:S(2)}) copy-start(f32[7,128]{1,0:T(8,128)S(1)} %broadcast_in_dim.35) | copy-start | bytes 10756
  3.3 37.4 %collective-permute-start = (f32[24,128]{1,0:T(8,128)}, f32[24,128]{1,0:T(8,128)}, u32[]{:S(2)}, u32[]{:S(2)}) collective-permute-start(f32[24,128]{1,0:T(8,128)} %pad_maximum_fusion.10), channel_id=1, source_target_pairs={{0,1},{1,0},{2,3},{3,2},{4,5},{5,4},{6,7},{7,6},{8,9},{9,8},{10,11... | collective-permute-start | bytes 36872 | tf_op jit(solution)/shard_map/ppermute | solution.py:210
  3.7 3.4 %copy-start.2 = (f32[1,1024,16]{1,2,0:T(8,128)S(1)}, f32[1,1024,16]{1,2,0:T(8,128)}, u32[]{:S(2)}) copy-start(f32[1,1024,16]{1,2,0:T(8,128)} %param.17) | copy-start | bytes 196612
  3.7 3.4 %copy-start.3 = (f32[1,1024,16]{1,2,0:T(8,128)S(1)}, f32[1,1024,16]{1,2,0:T(8,128)}, u32[]{:S(2)}) copy-start(f32[1,1024,16]{1,2,0:T(8,128)} %param.19) | copy-start | bytes 196612
  6.5 33.8 %copy-start.6 = (s32[8]{0:T(128)S(1)}, s32[8]{0:T(128)}, u32[]{:S(2)}) copy-start(s32[8]{0:T(128)} %constant.67) | copy-start | bytes 100
  6.5 33.8 %copy-start = (f32[1,16,2048]{2,1,0:T(8,128)S(1)}, f32[1,16,2048]{2,1,0:T(8,128)}, u32[]{:S(2)}) copy-start(f32[1,16,2048]{2,1,0:T(8,128)} %param.20) | copy-start | bytes 393220
  6.5 33.8 %copy-start.1 = (f32[1,16,2048]{2,1,0:T(8,128)S(1)}, f32[1,16,2048]{2,1,0:T(8,128)}, u32[]{:S(2)}) copy-start(f32[1,16,2048]{2,1,0:T(8,128)} %param.18) | copy-start | bytes 393220
  6.6 33.9 %copy-start.5 = (s32[16]{0:T(128)S(1)}, s32[16]{0:T(128)}, u32[]{:S(2)}) copy-start(s32[16]{0:T(128)} %param.14) | copy-start | bytes 196
  6.6 70.4 %collective-permute-start.1 = (bf16[1024,1024]{1,0:T(8,128)(2,1)S(1)}, bf16[1024,1024]{1,0:T(8,128)(2,1)}, u32[]{:S(2)}, u32[]{:S(2)}) collective-permute-start(bf16[1024,1024]{1,0:T(8,128)(2,1)S(1)} %bitcast.59), channel_id=1, source_target_pairs={{0,1},{1,0},{2,3},{3,2},{4,5},{5,4},{6,7},{7,6},{8,9},{9,8},{10,11... | collective-permute-start | bytes 6291464 | tf_op jit(solution)/shard_map/ppermute | solution.py:210
  6.7 76.7 %collective-permute-start.2 = (bf16[128,2048]{1,0:T(8,128)(2,1)}, bf16[128,2048]{1,0:T(8,128)(2,1)}, u32[]{:S(2)}, u32[]{:S(2)}) collective-permute-start(bf16[128,2048]{1,0:T(8,128)(2,1)} %own_gradient_ref.1), channel_id=1, source_target_pairs={{0,1},{1,0},{2,3},{3,2},{4,5},{5,4},{6,7},{7,6},{8,9},{9,8},{10,11... | collective-permute-start | bytes 1572872 | tf_op jit(solution)/shard_map/ppermute | solution.py:210
  89.2 8.6 %collective-permute-start.4 = (f32[256,2048]{1,0:T(8,128)S(1)}, f32[256,2048]{1,0:T(8,128)S(1)}, u32[]{:S(2)}, u32[]{:S(2)}) collective-permute-start(f32[256,2048]{1,0:T(8,128)S(1)} %get-tuple-element.29.tangent_ref), channel_id=1, source_target_pairs={{0,1},{1,0},{2,3},{3,2},{4,5},{5,4},{6,7},{7,6},{8,9},{9,8},{10,11... | collective-permute-start | bytes 6291464 | tf_op jit(solution)/shard_map/ppermute | solution.py:210
  89.7 7.9 %collective-permute-start.3 = (f16[2,16,3200]{2,1,0:T(8,128)(2,1)S(1)}, f16[2,16,3200]{2,1,0:T(8,128)(2,1)S(1)}, u32[]{:S(2)}, u32[]{:S(2)}) collective-permute-start(f16[2,16,3200]{2,1,0:T(8,128)(2,1)S(1)} %get-tuple-element.58), channel_id=1, source_target_pairs={{0,2},{1,3},{2,0},{3,1},{4,6},{5,7},{6,4},{7,5},{8,10},{9,11},{10,... | collective-permute-start | bytes 614408 | tf_op jit(solution)/shard_map/ppermute | solution.py:210
  91.1 12.1 %collective-permute-start.7 = (f16[2,16,3200]{2,1,0:T(8,128)(2,1)S(1)}, f16[2,16,3200]{2,1,0:T(8,128)(2,1)S(1)}, u32[]{:S(2)}, u32[]{:S(2)}) collective-permute-start(f16[2,16,3200]{2,1,0:T(8,128)(2,1)S(1)} %get-tuple-element.59), channel_id=1, source_target_pairs={{0,2},{1,3},{2,0},{3,1},{4,6},{5,7},{6,4},{7,5},{8,10},{9,11},{10,... | collective-permute-start | bytes 614408 | tf_op jit(solution)/shard_map/ppermute | solution.py:210
  103.8 7.7 %collective-permute-start.9 = (f16[16,3200]{1,0:T(8,128)(2,1)S(1)}, f16[16,3200]{1,0:T(8,128)(2,1)S(1)}, u32[]{:S(2)}, u32[]{:S(2)}) collective-permute-start(f16[16,3200]{1,0:T(8,128)(2,1)S(1)} %get-tuple-element.43), channel_id=1, source_target_pairs={{0,12},{1,13},{2,14},{3,15},{4,8},{5,9},{6,10},{7,11},{8,4},{9,5},... | collective-permute-start | bytes 307208 | tf_op jit(solution)/shard_map/ppermute | solution.py:210
  106.6 8.2 %collective-permute-start.5 = (f16[2,16,3200]{2,1,0:T(8,128)(2,1)S(1)}, f16[2,16,3200]{2,1,0:T(8,128)(2,1)S(1)}, u32[]{:S(2)}, u32[]{:S(2)}) collective-permute-start(f16[2,16,3200]{2,1,0:T(8,128)(2,1)S(1)} %pad_maximum_fusion.3), channel_id=1, source_target_pairs={{0,2},{1,3},{2,0},{3,1},{4,6},{5,7},{6,4},{7,5},{8,10},{9,11},{10,... | collective-permute-start | bytes 614408 | tf_op jit(solution)/shard_map/ppermute | solution.py:210
  108.6 8.9 %collective-permute-start.10 = (f16[2,16,3200]{2,1,0:T(8,128)(2,1)S(1)}, f16[2,16,3200]{2,1,0:T(8,128)(2,1)S(1)}, u32[]{:S(2)}, u32[]{:S(2)}) collective-permute-start(f16[2,16,3200]{2,1,0:T(8,128)(2,1)S(1)} %pad_maximum_fusion.5), channel_id=1, source_target_pairs={{0,2},{1,3},{2,0},{3,1},{4,6},{5,7},{6,4},{7,5},{8,10},{9,11},{10,... | collective-permute-start | bytes 614408 | tf_op jit(solution)/shard_map/ppermute | solution.py:210
  108.7 6.0 %collective-permute-start.8 = (f16[16,3200]{1,0:T(8,128)(2,1)S(1)}, f16[16,3200]{1,0:T(8,128)(2,1)S(1)}, u32[]{:S(2)}, u32[]{:S(2)}) collective-permute-start(f16[16,3200]{1,0:T(8,128)(2,1)S(1)} %get-tuple-element.42), channel_id=1, source_target_pairs={{0,8},{1,9},{2,10},{3,11},{4,12},{5,13},{6,14},{7,15},{8,0},{9,1},... | collective-permute-start | bytes 307208 | tf_op jit(solution)/shard_map/ppermute | solution.py:210
  118.1 7.8 %collective-permute-start.12 = (f16[16,3200]{1,0:T(8,128)(2,1)S(1)}, f16[16,3200]{1,0:T(8,128)(2,1)S(1)}, u32[]{:S(2)}, u32[]{:S(2)}) collective-permute-start(f16[16,3200]{1,0:T(8,128)(2,1)S(1)} %get-tuple-element.41), channel_id=1, source_target_pairs={{0,12},{1,13},{2,14},{3,15},{4,8},{5,9},{6,10},{7,11},{8,4},{9,5},... | collective-permute-start | bytes 307208 | tf_op jit(solution)/shard_map/ppermute | solution.py:210
  119.1 10.8 %collective-permute-start.6 = (f16[2,16,3200]{2,1,0:T(8,128)(2,1)S(1)}, f16[2,16,3200]{2,1,0:T(8,128)(2,1)S(1)}, u32[]{:S(2)}, u32[]{:S(2)}) collective-permute-start(f16[2,16,3200]{2,1,0:T(8,128)(2,1)S(1)} %pad_maximum_fusion.4), channel_id=1, source_target_pairs={{0,4},{1,5},{2,6},{3,7},{4,0},{5,1},{6,2},{7,3},{8,12},{9,13},{10,... | collective-permute-start | bytes 614408 | tf_op jit(solution)/shard_map/ppermute | solution.py:210
  119.2 8.4 %collective-permute-start.11 = (f16[16,3200]{1,0:T(8,128)(2,1)S(1)}, f16[16,3200]{1,0:T(8,128)(2,1)S(1)}, u32[]{:S(2)}, u32[]{:S(2)}) collective-permute-start(f16[16,3200]{1,0:T(8,128)(2,1)S(1)} %get-tuple-element.40), channel_id=1, source_target_pairs={{0,8},{1,9},{2,10},{3,11},{4,12},{5,13},{6,14},{7,15},{8,0},{9,1},... | collective-permute-start | bytes 307208 | tf_op jit(solution)/shard_map/ppermute | solution.py:210

commit v6 on v5

--- a/solution.py
+++ b/solution.py
@@ -12,8 +12,6 @@
 bf16 = jnp.bfloat16
 f16 = jnp.float16
 lanes = 128
-down_scale = 2.0**18
-up_scale = 2.0**15
 kernel_vmem = 32 * 2**20
 
 
@@ -206,8 +204,8 @@
 
 
 def exchange(value, mask):
-    size = lax.axis_size("expert")
-    return lax.ppermute(value, "expert", [(device, device ^ mask) for device in range(size)])
+    size = lax.axis_size("chip") * 2
+    return lax.ppermute(value, ("chip", "core"), [(device, device ^ mask) for device in range(size)])
 
 
 def encode(value):
@@ -235,11 +233,10 @@
     down_direction,
     up_direction,
 ):
-    size = lax.axis_size("expert")
+    size = lax.axis_size("chip") * 2
     rows = size // 4
     masks = [2 * z for z in range(rows)] + [2 * z + 1 for z in range(rows)]
-    cores = [list(range(core, size, 2)) for core in range(2)]
-    me = lax.axis_index("expert")
+    me = 2 * lax.axis_index("chip") + lax.axis_index("core")
     tokens, top = expert_of_route.shape
     hidden_width = hidden_of_route.shape[2]
     rank = adapter_down.shape[2]
@@ -249,10 +246,9 @@
     names = jnp.arange(experts, dtype=f32)
 
     def gather(own):
-        return lax.all_gather(own, "expert", axis_index_groups=cores)
-
-    own_down = (down_scale * jnp.concatenate([down_direction, adapter_down]).transpose(0, 2, 1)).astype(f16)
-    down_factors = gather(own_down).astype(f32) * (1 / down_scale)
+        return lax.all_gather(own, "chip")
+
+    down_factors = gather(jnp.concatenate([down_direction, adapter_down]).transpose(0, 2, 1))
 
     small = jnp.concatenate(
         [
@@ -268,14 +264,9 @@
     )
     counts = jnp.pad(counts, ((0, rank - 2), (0, lanes - experts)))
     own_up = jnp.concatenate(
-        [
-            up_scale * jnp.concatenate([adapter_up, up_direction]),
-            jnp.broadcast_to(counts, (2, rank, lanes)),
-        ],
-        axis=2,
-    ).astype(f16)
-    unscale = jnp.concatenate([jnp.full((model_width,), 1 / up_scale, f32), jnp.ones((lanes,), f32)])
-    up_factors = gather(own_up).astype(f32) * unscale
+        [jnp.concatenate([adapter_up, up_direction]), jnp.broadcast_to(counts, (2, rank, lanes))], axis=2
+    )
+    up_factors = gather(own_up)
 
     hidden_of_route, _ = lax.optimization_barrier((hidden_of_route, own_up))
     small = jnp.concatenate([small, small_other], axis=1)
@@ -286,7 +277,7 @@
     column = jnp.repeat((me ^ (2 * jnp.array(masks, jnp.int32))).astype(f32), rank)[None, :]
     capacity_row = jnp.pad(capacity.astype(f32), (0, lanes - experts))[None, :]
 
-    def call(kernel, outs, *operands, scratch=()):
+    def call(kernel, multiplies, outs, *operands, scratch=()):
         places = [
             pl.BlockSpec(memory_space=pltpu.SMEM if operand is chip else pltpu.VMEM) for operand in operands
         ]
@@ -296,10 +287,13 @@
             in_specs=places,
             scratch_shapes=scratch,
             compiler_params=pltpu.CompilerParams(vmem_limit_bytes=kernel_vmem),
+            cost_estimate=pl.CostEstimate(flops=2 * multiplies, bytes_accessed=2**23, transcendentals=0),
         )(*operands)
 
+    both = 2 * tokens
     (reduced,) = call(
         functools.partial(reduce_kernel, top, masks),
+        4 * top * both * hidden_width * wide,
         [((2, 2 * tokens, wide), f32)],
         chip,
         small,
@@ -310,6 +304,7 @@
     )
     weight, weighted, tangent, high, low = call(
         functools.partial(tangent_kernel, top, masks),
+        6 * both * model_width * wide,
         [
             ((2 * tokens, wide), f32),
             ((2 * tokens, 2 * wide), f32),
@@ -329,6 +324,7 @@
     chunks = [((rows // 2, rank, hidden_width + model_width), f32)] * 4
     *gradients, up, to = call(
         functools.partial(gradient_kernel, top),
+        2 * top * both * hidden_width * wide + 8 * both * model_width * wide,
         chunks + [((wide, model_width), f32), ((2 * tokens, wide), f32)],
         small,
         column,
@@ -347,6 +343,7 @@
     arrived, _ = lax.optimization_barrier((arrived, coded))
     curvatures = call(
         functools.partial(curvature_kernel, top),
+        2 * top * both * hidden_width * wide + 6 * both * model_width * wide,
         chunks,
         small,
         column,
@@ -533,34 +530,22 @@
     )
 
 
-def local(*arguments):
-    adapter_down, adapter_up = arguments[6], arguments[7]
-    factor_bytes = 2 * 4 * (adapter_down.size + adapter_up.size) * lax.axis_size("expert")
-    plan = gathered_plan if 4 * factor_bytes <= kernel_vmem else routed_plan
-    return plan(*arguments)
-
-
 def solution(mesh):
-    return jax.shard_map(
-        local,
-        mesh=mesh,
-        in_specs=(
-            P(("groups", "expert"), None, None),
-            P(("groups", "expert"), None),
-            P(("groups", "expert"), None),
-            P("groups"),
-            P(("groups", "expert"), None),
-            P(("groups", "expert")),
-            P("expert", None, None),
-            P("expert", None, None),
-            P(("groups", "expert"), None, None),
-            P(("groups", "expert"), None, None),
-        ),
-        out_specs=(
-            P(("groups", "expert"), None, None),
-            P(("groups", "expert"), None, None),
-            P(("groups", "expert"), None, None),
-            P(("groups", "expert"), None, None),
-        ),
-        check_vma=False,
-    )
+    def whole(*arguments):
+        factor_bytes = 2 * 4 * (arguments[6].size + arguments[7].size)
+        devices, plan, part = mesh, routed_plan, "expert"
+        if 4 * factor_bytes <= kernel_vmem:
+            devices = jax.sharding.Mesh(
+                mesh.devices.reshape(mesh.shape["groups"], mesh.shape["expert"] // 2, 2), ("groups", "chip", "core")
+            )
+            plan, part = gathered_plan, ("chip", "core")
+        every = P(("groups",) + part if isinstance(part, tuple) else ("groups", part))
+        return jax.shard_map(
+            plan,
+            mesh=devices,
+            in_specs=(every, every, every, P("groups"), every, every, P(part), P(part), every, every),
+            out_specs=(every,) * 4,
+            check_vma=False,
+        )(*arguments)
+
+    return whole

time: 133 us -> 165 us (1.24)
  waiting for transfers between devices: 20.8 us -> 103 us
  blocking collectives: 66.8 us -> 0 us
  between operations: 0.95 us -> 14.3 us
  local copies, waits for them, and re-layouts: 6.78 us -> 8.96 us
    all_gather x0 -> x2, waiting for transfers between devices: none -> 82.3 us  [gather(): return lax.all_gather(own, 'chip')]
    all_gather x2 -> x0, blocking collectives: 66.8 us -> none  [gather(): return lax.all_gather(own, 'expert', axis_index_groups=cores)]
    unnamed x14 -> x12, local copies, waits for them, and re-layouts: 0.04 us -> 2.88 us
    concatenate x2 -> x1, other arithmetic: 0.07 us -> 1.72 us  [gathered_plan(): jnp.concatenate([jnp.concatenate([adapter_up, up_direction]), jnp.broadca...]
  transfers between devices with their start and end apart: 13 -> 15, of which waited for: 7 -> 10; matrix products, arithmetic and copies ran while one was open for 6% -> 6% of each run, Pallas kernels for 8% -> 7%
where the time goes in v6:
time: 165 us
  waiting for transfers between devices  103 us (62%)
  Pallas kernels  16.3 us (10%)
  between operations  14.3 us (9%)
  starting transfers between devices  12.9 us (8%)
  other arithmetic  9.23 us (6%)
  local copies, waits for them, and re-layouts  8.96 us (5%)
    all_gather x2, waiting for transfers between devices, gather(): return lax.all_gather(own, 'chip')  82.3 us
    ppermute x13, waiting for transfers between devices, exchange(): lax.ppermute(value, ('chip', 'core'), [(device, device ^ mask) for device...  20.7 us
    pallas_call x4, Pallas kernels, call(): pl.pallas_call(kernel, out_shape=[jax.ShapeDtypeStruct(shape, dtype) for...  16.3 us
    ppermute x13, starting transfers between devices, exchange(): lax.ppermute(value, ('chip', 'core'), [(device, device ^ mask) for device...  12.8 us
  transfers between devices with their start and end apart: 15, of which 10 were waited for; matrix products, arithmetic and copies ran while one was open for 6% of the time, Pallas kernels for 7%

profile of v6, /device:TPU:0, one launch (start us, length us, event | category | flops | bytes accessed | tf_op | source)
XLA Modules:
  0.0 164.7 jit_solution(6096163076533176263)
XLA Ops:
  7.2 1.5 maximum_bitcast_fusion
  11.4 0.7 collective-permute-done
  12.3 1.7 %pad_maximum_fusion.1 = f32[2,16,2176]{2,1,0:T(8,128)} fusion(f32[2,16,128]{2,1,0:T(8,128)S(1)} %broadcast_in_dim.37, f32[1,16,2048]{2,1,0:T(8,128)} %param.20, f32[1,16,2048]{2,1,0:T(8,128)} %param.18), kind=kLoop, calls=%fused_computation.25 | loop fusion | flops 139264 | bytes 557056 | tf_op jit(solution)/shard_map/concatenate | solution.py:266
  14.1 2.8 %copy.18 = bf16[8,128,1024]{2,1,0:T(8,128)(2,1)S(1)} copy(bf16[8,128,1024]{2,0,1:T(8,128)(2,1)} %bitcast.64) | data formatting | bytes 4194304 | tf_op jit(solution)/shard_map/transpose | solution.py:273
  17.7 35.9 %all-gather.5.cloned.1.call-done = f32[16,16,1024]{2,1,0:T(8,128)} async-done(((f32[2,16,1024]{2,1,0:T(8,128)}), f32[16,16,1024]{2,1,0:T(8,128)}) %all-gather.5.cloned.1.call-update) | async-done | bytes 1048592 | tf_op jit(solution)/shard_map/all_gather | solution.py:249
  53.6 1.2 copy-done.1
  54.8 4.0 %shard_map.138.reduced_ref = f32[2,256,128]{2,1,0:T(8,128)S(1)} custom-call(s32[1]{0:T(128)} %bitcast.7.chip_ref, f32[24,256]{1,0:T(8,128)S(1)} %pad_maximum_fusion.9.small_ref, f32[1,128]{1,0:T(1,128)S(1)} %broadcast_in_dim_reshape.3.column_ref, bf16[1024,1024]{1,0:T(8,128)(2,1)S(1)} %bitcast.59, bf16[1024,1024]{1,0:T(8,128)(2,1)} %collective-permute-done.1.other_ref, ...), custom_call_target="tpu_custom_call" | custom-call | flops 2147483648 | bytes 8388608 | tf_op jit(solution)/shard_map/pallas_call | solution.py:284
  58.8 46.4 %all-gather.7.cloned.1.call-done = f32[16,16,2176]{2,1,0:T(8,128)} async-done(((f32[2,16,2176]{2,1,0:T(8,128)}), f32[16,16,2176]{2,1,0:T(8,128)}) %all-gather.7.cloned.1.call-update) | async-done | bytes 2228240 | tf_op jit(solution)/shard_map/all_gather | solution.py:249
  105.2 1.6 copy-done
  106.8 2.3 %shard_map.139 = (f32[256,128]{1,0:T(8,128)S(1)}, f32[256,256]{1,0:T(8,128)S(1)}, f32[256,2048]{1,0:T(8,128)S(1)}, bf16[256,2048]{1,0:T(8,128)(2,1)S(1)}, bf16[256,2048]{1,0:T(8,128)(2,1)S(1)}) custom-call(s32[1]{0:T(128)} %bitcast.7.chip_ref, f32[24,256]{1,0:T(8,128)S(1)} %pad_maximum_fusion.9.small_ref, f32[1,128]{1,0:T(1,128)S(1)} %broadcast_in_dim_reshape.3.column_ref, ...), custom_call_target="tpu_custom_call" | custom-call | flops 805306368 | bytes 8388608 | tf_op jit(solution)/shard_map/pallas_call | solution.py:284
  109.2 5.3 %shard_map.140 = (f32[2,16,3072]{2,1,0:T(8,128)S(1)}, f32[2,16,3072]{2,1,0:T(8,128)S(1)}, f32[2,16,3072]{2,1,0:T(8,128)S(1)}, f32[2,16,3072]{2,1,0:T(8,128)S(1)}...) custom-call(f32[24,256]{1,0:T(8,128)S(1)} %pad_maximum_fusion.9.small_ref, ...), custom_call_target="tpu_custom_call" | custom-call | flops 2147483648 | bytes 8388608 | tf_op jit(solution)/shard_map/pallas_call | solution.py:284
  115.9 1.5 collective-permute-start.7
  117.4 5.8 %collective-permute-done.3 = f16[2,16,3200]{2,1,0:T(8,128)(2,1)S(1)} collective-permute-done((f16[2,16,3200]{2,1,0:T(8,128)(2,1)S(1)}, f16[2,16,3200]{2,1,0:T(8,128)(2,1)S(1)}, u32[]{:S(2)}, u32[]{:S(2)}) %collective-permute-start.3) | collective-permute-done | bytes 204832 | tf_op jit(solution)/shard_map/ppermute | solution.py:208
  123.3 4.6 %shard_map.141 = (f32[2,16,3072]{2,1,0:T(8,128)S(1)}, f32[2,16,3072]{2,1,0:T(8,128)S(1)}, f32[2,16,3072]{2,1,0:T(8,128)S(1)}, f32[2,16,3072]{2,1,0:T(8,128)S(1)}) custom-call(f32[24,256]{1,0:T(8,128)S(1)} %pad_maximum_fusion.9.small_ref, f32[1,128]{1,0:T(1,128)S(1)} %broadcast_in_dim_reshape.3.column_ref, bf16[1024,1024]{1,0:T(8,128)(2,1)S(1)} %bitcast.61, ...), custom_call_target="tpu_custom_call" | custom-call | flops 1879048192 | bytes 8388608 | tf_op jit(solution)/shard_map/pallas_call | solution.py:284
  129.3 1.9 %collective-permute-start.9 = (f16[16,3200]{1,0:T(8,128)(2,1)S(1)}, f16[16,3200]{1,0:T(8,128)(2,1)S(1)}, u32[]{:S(2)}, u32[]{:S(2)}) collective-permute-start(f16[16,3200]{1,0:T(8,128)(2,1)S(1)} %get-tuple-element.45), channel_id=1, source_target_pairs={{0,12},{1,13},{2,14},{3,15},{4,8},{5,9},{6,10},{7,11},{8,4},{9,5},... | collective-permute-start | bytes 307208 | tf_op jit(solution)/shard_map/ppermute | solution.py:208
  131.9 1.5 collective-permute-start.10
  133.4 1.1 collective-permute-start.8
  134.5 1.9 %collective-permute-done.9 = f16[16,3200]{1,0:T(8,128)(2,1)S(1)} collective-permute-done((f16[16,3200]{1,0:T(8,128)(2,1)S(1)}, f16[16,3200]{1,0:T(8,128)(2,1)S(1)}, u32[]{:S(2)}, u32[]{:S(2)}) %collective-permute-start.9) | collective-permute-done | bytes 102432 | tf_op jit(solution)/shard_map/ppermute | solution.py:208
  136.5 4.4 %collective-permute-done.8 = f16[16,3200]{1,0:T(8,128)(2,1)S(1)} collective-permute-done((f16[16,3200]{1,0:T(8,128)(2,1)S(1)}, f16[16,3200]{1,0:T(8,128)(2,1)S(1)}, u32[]{:S(2)}, u32[]{:S(2)}) %collective-permute-start.8) | collective-permute-done | bytes 102432 | tf_op jit(solution)/shard_map/ppermute | solution.py:208
  142.4 2.1 %collective-permute-start.12 = (f16[16,3200]{1,0:T(8,128)(2,1)S(1)}, f16[16,3200]{1,0:T(8,128)(2,1)S(1)}, u32[]{:S(2)}, u32[]{:S(2)}) collective-permute-start(f16[16,3200]{1,0:T(8,128)(2,1)S(1)} %get-tuple-element.43), channel_id=1, source_target_pairs={{0,12},{1,13},{2,14},{3,15},{4,8},{5,9},{6,10},{7,11},{8,4},{9,5},... | collective-permute-start | bytes 307208 | tf_op jit(solution)/shard_map/ppermute | solution.py:208
  144.6 2.4 %collective-permute-start.11 = (f16[16,3200]{1,0:T(8,128)(2,1)S(1)}, f16[16,3200]{1,0:T(8,128)(2,1)S(1)}, u32[]{:S(2)}, u32[]{:S(2)}) collective-permute-start(f16[16,3200]{1,0:T(8,128)(2,1)S(1)} %get-tuple-element.42), channel_id=1, source_target_pairs={{0,8},{1,9},{2,10},{3,11},{4,12},{5,13},{6,14},{7,15},{8,0},{9,1},... | collective-permute-start | bytes 307208 | tf_op jit(solution)/shard_map/ppermute | solution.py:208
  147.0 3.0 %collective-permute-done.12 = f16[16,3200]{1,0:T(8,128)(2,1)S(1)} collective-permute-done((f16[16,3200]{1,0:T(8,128)(2,1)S(1)}, f16[16,3200]{1,0:T(8,128)(2,1)S(1)}, u32[]{:S(2)}, u32[]{:S(2)}) %collective-permute-start.12) | collective-permute-done | bytes 102432 | tf_op jit(solution)/shard_map/ppermute | solution.py:208
  150.2 2.3 %collective-permute-done.11 = f16[16,3200]{1,0:T(8,128)(2,1)S(1)} collective-permute-done((f16[16,3200]{1,0:T(8,128)(2,1)S(1)}, f16[16,3200]{1,0:T(8,128)(2,1)S(1)}, u32[]{:S(2)}, u32[]{:S(2)}) %collective-permute-start.11) | collective-permute-done | bytes 102432 | tf_op jit(solution)/shard_map/ppermute | solution.py:208
  152.6 2.3 %collective-permute-done.6 = f16[2,16,3200]{2,1,0:T(8,128)(2,1)S(1)} collective-permute-done((f16[2,16,3200]{2,1,0:T(8,128)(2,1)S(1)}, f16[2,16,3200]{2,1,0:T(8,128)(2,1)S(1)}, u32[]{:S(2)}, u32[]{:S(2)}) %collective-permute-start.6) | collective-permute-done | bytes 204832 | tf_op jit(solution)/shard_map/ppermute | solution.py:208
  (93 shorter events, 12.0 us)
Async XLA Ops:
  7.2 46.4 %all-gather.5.cloned.1.call-start = ((), (), s32[]{:S(2)}) async-start(), calls=%async_computation | async-start | bytes 1179648 | tf_op jit(solution)/shard_map/all_gather | solution.py:249
  8.8 96.4 %all-gather.7.cloned.1.call-start = ((), (), s32[]{:S(2)}) async-start(), calls=%async_computation.1 | async-start | bytes 2506752 | tf_op jit(solution)/shard_map/all_gather | solution.py:249
  10.9 1.3 collective-permute-start
  14.0 3.3 %copy-start.2 = (bf16[128,2048]{1,0:T(8,128)(2,1)S(1)}, bf16[128,2048]{1,0:T(8,128)(2,1)}, u32[]{:S(2)}) copy-start(bf16[128,2048]{1,0:T(8,128)(2,1)} %own_gradient_ref.1) | copy-start | bytes 1572868
  14.1 3.4 %copy-start.5 = (s32[8]{0:T(128)S(1)}, s32[8]{0:T(128)}, u32[]{:S(2)}) copy-start(s32[8]{0:T(128)} %constant.62) | copy-start | bytes 100
  14.1 3.6 %copy-start.4 = (s32[16]{0:T(128)S(1)}, s32[16]{0:T(128)}, u32[]{:S(2)}) copy-start(s32[16]{0:T(128)} %param.14) | copy-start | bytes 196
  14.1 3.6 %copy-start.3 = (f32[128]{0:T(128)S(1)}, f32[128]{0:T(128)}, u32[]{:S(2)}) copy-start(f32[128]{0:T(128)} %param.16) | copy-start | bytes 1540
  16.9 36.7 %collective-permute-start.1 = (bf16[1024,1024]{1,0:T(8,128)(2,1)S(1)}, bf16[1024,1024]{1,0:T(8,128)(2,1)}, u32[]{:S(2)}, u32[]{:S(2)}) collective-permute-start(bf16[1024,1024]{1,0:T(8,128)(2,1)S(1)} %bitcast.58), channel_id=1, source_target_pairs={{0,1},{1,0},{2,3},{3,2},{4,5},{5,4},{6,7},{7,6},{8,9},{9,8},{10,11... | collective-permute-start | bytes 6291464 | tf_op jit(solution)/shard_map/ppermute | solution.py:208
  17.3 91.8 %collective-permute-start.2 = (bf16[128,2048]{1,0:T(8,128)(2,1)S(1)}, bf16[128,2048]{1,0:T(8,128)(2,1)S(1)}, u32[]{:S(2)}, u32[]{:S(2)}) collective-permute-start(bf16[128,2048]{1,0:T(8,128)(2,1)S(1)} %copy-done.2), channel_id=1, source_target_pairs={{0,1},{1,0},{2,3},{3,2},{4,5},{5,4},{6,7},{7,6},{8,9},{9,8},{10,11... | collective-permute-start | bytes 1572872 | tf_op jit(solution)/shard_map/ppermute | solution.py:208
  53.6 1.2 copy-start.1
  105.2 1.6 copy-start
  114.7 8.6 %collective-permute-start.4 = (f32[256,2048]{1,0:T(8,128)S(1)}, f32[256,2048]{1,0:T(8,128)S(1)}, u32[]{:S(2)}, u32[]{:S(2)}) collective-permute-start(f32[256,2048]{1,0:T(8,128)S(1)} %get-tuple-element.31.tangent_ref), channel_id=1, source_target_pairs={{0,1},{1,0},{2,3},{3,2},{4,5},{5,4},{6,7},{7,6},{8,9},{9,8},{10,11... | collective-permute-start | bytes 6291464 | tf_op jit(solution)/shard_map/ppermute | solution.py:208
  115.3 7.9 %collective-permute-start.3 = (f16[2,16,3200]{2,1,0:T(8,128)(2,1)S(1)}, f16[2,16,3200]{2,1,0:T(8,128)(2,1)S(1)}, u32[]{:S(2)}, u32[]{:S(2)}) collective-permute-start(f16[2,16,3200]{2,1,0:T(8,128)(2,1)S(1)} %get-tuple-element.60), channel_id=1, source_target_pairs={{0,2},{1,3},{2,0},{3,1},{4,6},{5,7},{6,4},{7,5},{8,10},{9,11},{10,... | collective-permute-start | bytes 614408 | tf_op jit(solution)/shard_map/ppermute | solution.py:208
  115.9 12.8 %collective-permute-start.7 = (f16[2,16,3200]{2,1,0:T(8,128)(2,1)S(1)}, f16[2,16,3200]{2,1,0:T(8,128)(2,1)S(1)}, u32[]{:S(2)}, u32[]{:S(2)}) collective-permute-start(f16[2,16,3200]{2,1,0:T(8,128)(2,1)S(1)} %get-tuple-element.61), channel_id=1, source_target_pairs={{0,2},{1,3},{2,0},{3,1},{4,6},{5,7},{6,4},{7,5},{8,10},{9,11},{10,... | collective-permute-start | bytes 614408 | tf_op jit(solution)/shard_map/ppermute | solution.py:208
  129.3 7.1 %collective-permute-start.9 = (f16[16,3200]{1,0:T(8,128)(2,1)S(1)}, f16[16,3200]{1,0:T(8,128)(2,1)S(1)}, u32[]{:S(2)}, u32[]{:S(2)}) collective-permute-start(f16[16,3200]{1,0:T(8,128)(2,1)S(1)} %get-tuple-element.45), channel_id=1, source_target_pairs={{0,12},{1,13},{2,14},{3,15},{4,8},{5,9},{6,10},{7,11},{8,4},{9,5},... | collective-permute-start | bytes 307208 | tf_op jit(solution)/shard_map/ppermute | solution.py:208
  131.3 9.8 %collective-permute-start.5 = (f16[2,16,3200]{2,1,0:T(8,128)(2,1)S(1)}, f16[2,16,3200]{2,1,0:T(8,128)(2,1)S(1)}, u32[]{:S(2)}, u32[]{:S(2)}) collective-permute-start(f16[2,16,3200]{2,1,0:T(8,128)(2,1)S(1)} %pad_maximum_fusion.4), channel_id=1, source_target_pairs={{0,2},{1,3},{2,0},{3,1},{4,6},{5,7},{6,4},{7,5},{8,10},{9,11},{10,... | collective-permute-start | bytes 614408 | tf_op jit(solution)/shard_map/ppermute | solution.py:208
  131.9 9.8 %collective-permute-start.10 = (f16[2,16,3200]{2,1,0:T(8,128)(2,1)S(1)}, f16[2,16,3200]{2,1,0:T(8,128)(2,1)S(1)}, u32[]{:S(2)}, u32[]{:S(2)}) collective-permute-start(f16[2,16,3200]{2,1,0:T(8,128)(2,1)S(1)} %pad_maximum_fusion.6), channel_id=1, source_target_pairs={{0,2},{1,3},{2,0},{3,1},{4,6},{5,7},{6,4},{7,5},{8,10},{9,11},{10,... | collective-permute-start | bytes 614408 | tf_op jit(solution)/shard_map/ppermute | solution.py:208
  133.4 7.6 %collective-permute-start.8 = (f16[16,3200]{1,0:T(8,128)(2,1)S(1)}, f16[16,3200]{1,0:T(8,128)(2,1)S(1)}, u32[]{:S(2)}, u32[]{:S(2)}) collective-permute-start(f16[16,3200]{1,0:T(8,128)(2,1)S(1)} %get-tuple-element.44), channel_id=1, source_target_pairs={{0,8},{1,9},{2,10},{3,11},{4,12},{5,13},{6,14},{7,15},{8,0},{9,1},... | collective-permute-start | bytes 307208 | tf_op jit(solution)/shard_map/ppermute | solution.py:208
  142.4 7.7 %collective-permute-start.12 = (f16[16,3200]{1,0:T(8,128)(2,1)S(1)}, f16[16,3200]{1,0:T(8,128)(2,1)S(1)}, u32[]{:S(2)}, u32[]{:S(2)}) collective-permute-start(f16[16,3200]{1,0:T(8,128)(2,1)S(1)} %get-tuple-element.43), channel_id=1, source_target_pairs={{0,12},{1,13},{2,14},{3,15},{4,8},{5,9},{6,10},{7,11},{8,4},{9,5},... | collective-permute-start | bytes 307208 | tf_op jit(solution)/shard_map/ppermute | solution.py:208
  144.6 10.3 %collective-permute-start.6 = (f16[2,16,3200]{2,1,0:T(8,128)(2,1)S(1)}, f16[2,16,3200]{2,1,0:T(8,128)(2,1)S(1)}, u32[]{:S(2)}, u32[]{:S(2)}) collective-permute-start(f16[2,16,3200]{2,1,0:T(8,128)(2,1)S(1)} %pad_maximum_fusion.5), channel_id=1, source_target_pairs={{0,4},{1,5},{2,6},{3,7},{4,0},{5,1},{6,2},{7,3},{8,12},{9,13},{10,... | collective-permute-start | bytes 614408 | tf_op jit(solution)/shard_map/ppermute | solution.py:208
  144.6 7.8 %collective-permute-start.11 = (f16[16,3200]{1,0:T(8,128)(2,1)S(1)}, f16[16,3200]{1,0:T(8,128)(2,1)S(1)}, u32[]{:S(2)}, u32[]{:S(2)}) collective-permute-start(f16[16,3200]{1,0:T(8,128)(2,1)S(1)} %get-tuple-element.42), channel_id=1, source_target_pairs={{0,8},{1,9},{2,10},{3,11},{4,12},{5,13},{6,14},{7,15},{8,0},{9,1},... | collective-permute-start | bytes 307208 | tf_op jit(solution)/shard_map/ppermute | solution.py:208
Sparse Core Ops, SparseCore 0:
  10.7 42.8 all-gather.4
  55.8 49.4 all-gather.6

commit v7 on v3

v7 whole, which is shorter than its diff:
```python
import functools

import jax
import jax.numpy as jnp
from jax import lax
from jax.experimental import pallas as pl
from jax.experimental.pallas import tpu as pltpu
from jax.sharding import PartitionSpec as P

adapter_scale = 2.0
f32 = jnp.float32
bf16 = jnp.bfloat16
i16 = jnp.int16
lanes = 128
counts_lane = 64
kernel_vmem = 32 * 2**20


def halves(value):
    high = value.astype(bf16)
    return high, (value - high.astype(f32)).astype(bf16)


def dot(a, b, a_dim, b_dim):
    return lax.dot_general(a, b, (((a_dim,), (b_dim,)), ((), ())), preferred_element_type=f32)


def dot_pairs(a, b, a_dim, b_dim):
    return dot(a[0], b[0], a_dim, b_dim) + (dot(a[1], b[0], a_dim, b_dim) + dot(a[0], b[1], a_dim, b_dim))


def encode(down, up, counts=0.0):
    def scaled(value):
        largest = jnp.max(jnp.abs(value), axis=-1, keepdims=True)
        exponent = jnp.ceil(jnp.log2(jnp.maximum(largest, 1e-30)))
        coded = jnp.round(value * jnp.exp2(15.0 - exponent))
        return jnp.clip(coded, -32767.0, 32767.0), exponent

    down, down_exponent = scaled(down)
    up, up_exponent = scaled(up)
    lane = lax.broadcasted_iota(jnp.int32, down.shape[:-1] + (lanes,), down.ndim - 1)
    tail = jnp.where(lane < counts_lane // 2, down_exponent, up_exponent)
    tail = jnp.where(lane < counts_lane, tail, counts)
    return jnp.concatenate([down, up, tail], axis=-1).astype(jnp.int32).astype(i16)


def decode(coded, hidden_width):
    width = coded.shape[-1] - lanes
    value = coded.astype(jnp.int32).astype(f32)
    down_scale = jnp.exp2(value[..., width : width + 1] - 15.0)
    up_scale = jnp.exp2(value[..., width + counts_lane // 2 : width + counts_lane // 2 + 1] - 15.0)
    return value[..., :hidden_width] * down_scale, value[..., hidden_width:width] * up_scale


def prepare_kernel(expert_ref, gate_ref, curvature_ref, *rest):
    (down_direction_ref, adapter_down_ref, adapter_up_ref, up_direction_ref, piece_ref, small_ref) = rest
    top = expert_ref.shape[0]
    small_ref[...] = jnp.zeros_like(small_ref)
    small_ref[:top] = expert_ref[...].astype(f32)
    small_ref[top : 2 * top] = gate_ref[...].astype(f32)
    small_ref[2 * top : 2 * top + 1] = curvature_ref[...]
    lane = lax.broadcasted_iota(jnp.int32, (1, lanes), 1)
    counts = jnp.zeros((1, lanes), f32)
    for expert in range(lanes - counts_lane):
        named = jnp.where(expert_ref[...] == expert, 1.0, 0.0)
        total = jnp.sum(jnp.sum(named, axis=0, keepdims=True), axis=1, keepdims=True)
        counts = jnp.where(lane == counts_lane + expert, total, counts)
    piece_ref[0] = encode(down_direction_ref[...], adapter_up_ref[...], counts)
    piece_ref[1] = encode(adapter_down_ref[...], up_direction_ref[...], counts)


def token_columns(own_ref, other_ref, top):
    small = jnp.concatenate([own_ref[...], other_ref[...]], axis=1).T
    experts = [small[:, k : k + 1] for k in range(top)]
    gates = [small[:, top + k : top + k + 1] for k in range(top)]
    return experts, gates, small[:, 2 * top : 2 * top + 1]


def members(place_ref, wide, masks):
    slot_of = lax.broadcasted_iota(jnp.int32, (1, wide), 1) // (wide // len(masks))
    found = jnp.zeros((1, wide), jnp.int32)
    for slot, mask in enumerate(masks):
        found = jnp.where(slot_of == slot, place_ref[0] ^ mask, found)
    return found.astype(f32)


def prior_kernel(masks, place_ref, *rest):
    piece_refs, prior_ref = rest[:-1], rest[-1]
    me = place_ref[0]
    slots = len(masks)
    prior_ref[...] = jnp.zeros_like(prior_ref)
    for block, number in enumerate((me, me ^ 1)):
        total = jnp.zeros((1, lanes), f32)
        for offset in range(slots):
            device = place_ref[1 + slots + offset]
            tail = piece_refs[offset][0, :, piece_refs[offset].shape[2] - lanes :]
            counts = tail.astype(jnp.int32).astype(f32)[0:1]
            total = total + jnp.where(device < number, counts, 0.0)
        prior_ref[block : block + 1] = total


def piece_part(refs, offset, kind):
    last = len(refs) - 2
    half = last // 2 + 1
    if offset == half:
        return refs[last + kind][0]
    return refs[offset if offset < half else offset - 1][kind]


def reduce_kernel(top, masks, place_ref, small_ref, small_other_ref, own_ref, other_ref, *rest):
    slots = len(masks)
    piece_refs, (_, reduced_ref, high_ref, low_ref) = rest[: slots + 1], rest[slots + 1 :]
    hidden_width = own_ref.shape[1]
    for offset in range(slots):
        slot = place_ref[1 + offset]
        for kind in range(2):
            down, _ = decode(piece_part(piece_refs, offset, kind), hidden_width)
            high_ref[kind, slot], low_ref[kind, slot] = halves(down)
    experts, _, _ = token_columns(small_ref, small_other_ref, top)
    wide = reduced_ref.shape[2]
    column = members(place_ref, wide, masks)
    high = high_ref[...].reshape(2 * wide, hidden_width)
    low = low_ref[...].reshape(2 * wide, hidden_width)
    tokens = own_ref.shape[0] // top
    for block, hidden_ref in enumerate((own_ref, other_ref)):
        rows = slice(block * tokens, (block + 1) * tokens)
        full = dot(hidden_ref[...], high, 1, 1) + dot(hidden_ref[...], low, 1, 1)
        total = jnp.zeros((tokens, 2 * wide), f32)
        for k in range(top):
            named = experts[k][rows] == column
            total = jnp.where(jnp.concatenate([named, named], axis=1), full[k * tokens : (k + 1) * tokens], total)
        reduced_ref[0, rows] = total[:, :wide]
        reduced_ref[1, rows] = total[:, wide:]


def rank_limits(place_ref, masks, wide, capacity_ref, prior_ref, arrived_ref):
    lane = lax.broadcasted_iota(jnp.int32, (1, lanes), 1)
    slot_of = lax.broadcasted_iota(jnp.int32, (1, wide), 1) // (wide // len(masks))
    limits = []
    for block in range(2):
        total = capacity_ref[...] - prior_ref[block : block + 1] - arrived_ref[1 - block : 2 - block]
        limit = jnp.zeros((1, wide), f32)
        for slot, mask in enumerate(masks):
            picked = jnp.where(lane == counts_lane + (place_ref[0] ^ mask), total, 0.0)
            limit = jnp.where(slot_of == slot, jnp.sum(picked, axis=1, keepdims=True), limit)
        limits.append(limit)
    return limits


def tangent_kernel(
    top, masks, place_ref, small_ref, small_other_ref, capacity_ref, prior_ref, arrived_ref, reduced_ref, *rest
):
    slots = len(masks)
    piece_refs = rest[: slots + 1]
    weight_ref, weighted_ref, tangent_ref, coded_ref, high_ref, low_ref = rest[slots + 1 :]
    experts, gates, _ = token_columns(small_ref, small_other_ref, top)
    tokens, wide = weight_ref.shape
    model_width = tangent_ref.shape[1]
    hidden_width = piece_refs[0].shape[2] - model_width - lanes
    block = tokens // 2
    column = members(place_ref, wide, masks)
    limits = rank_limits(place_ref, masks, wide, capacity_ref, prior_ref, arrived_ref)
    gate = jnp.zeros((tokens, wide), f32)
    member = jnp.zeros((tokens, wide), f32)
    for k in range(top):
        named = experts[k] == column
        gate = jnp.where(named, gates[k], gate)
        member = jnp.where(named, 1.0, member)
    below = (
        lax.broadcasted_iota(jnp.int32, (block, block), 0)
        > lax.broadcasted_iota(jnp.int32, (block, block), 1)
    )
    below = jnp.where(below, 1.0, 0.0).astype(bf16)
    weights = []
    for part in range(2):
        rows = slice(part * block, (part + 1) * block)
        local_rank = dot(below, member[rows].astype(bf16), 1, 0)
        weights.append(jnp.where(local_rank < limits[part], adapter_scale * gate[rows], 0.0))
    weight = jnp.concatenate(weights, axis=0)
    weight_ref[...] = weight
    weighted = jnp.concatenate([weight * reduced_ref[0], weight * reduced_ref[1]], axis=1)
    weighted_ref[...] = weighted
    for offset in range(slots):
        slot = place_ref[1 + offset]
        for kind in range(2):
            _, up = decode(piece_part(piece_refs, offset, kind), hidden_width)
            high_ref[kind, slot], low_ref[kind, slot] = halves(up)
    factor = high_ref[...].reshape(2 * wide, model_width), low_ref[...].reshape(2 * wide, model_width)
    tangent = dot_pairs(halves(weighted), factor, 1, 0)
    tangent_ref[...] = tangent
    coded_ref[...] = tangent.astype(bf16)


def put_left(left_ref, experts, column, terms, top):
    both = jnp.concatenate(halves(terms), axis=1)
    tokens = terms.shape[0] // 2
    for block in range(2):
        rows = slice(block * tokens, (block + 1) * tokens)
        for k in range(top):
            named = experts[k][rows] == column
            named = jnp.concatenate([named, named], axis=1)
            left_ref[block, k * tokens : (k + 1) * tokens] = jnp.where(named, both[rows], jnp.zeros_like(both[rows]))


def add_halves(both):
    middle = both.shape[0] // 2
    return both[:middle] + both[middle:]


def put_chunks(own_ref, near_ref, far_ref, down, up):
    count, rank, _ = own_ref.shape
    hidden_width = down.shape[1]
    own_ref[:, :, :hidden_width] = down[: count * rank].reshape(count, rank, -1)
    own_ref[:, :, hidden_width:] = up[: count * rank].reshape(count, rank, -1)
    start = count * rank
    for out_ref in (near_ref, far_ref):
        stop = start + out_ref.shape[0] * rank
        out_ref[...] = encode(down[start:stop], up[start:stop]).reshape(out_ref.shape)
        start = stop


def gradient_kernel(
    top,
    masks,
    place_ref,
    small_ref,
    small_other_ref,
    own_ref,
    other_ref,
    own_gradient_ref,
    other_gradient_ref,
    weight_ref,
    weighted_ref,
    high_ref,
    low_ref,
    chunk_ref,
    near_ref,
    far_ref,
    up_ref,
    to_ref,
    left_ref,
):
    experts, _, _ = token_columns(small_ref, small_other_ref, top)
    wide = weight_ref.shape[1]
    model_width = up_ref.shape[1]
    column = members(place_ref, wide, masks)
    gradient = jnp.concatenate([own_gradient_ref[...], other_gradient_ref[...]], axis=0)
    high = high_ref[...].reshape(2 * wide, model_width)
    low = low_ref[...].reshape(2 * wide, model_width)
    to_both = dot(gradient, high, 1, 1) + dot(gradient, low, 1, 1)
    to_ref[...] = to_both[:, wide:]
    put_left(left_ref, experts, column, weight_ref[...] * to_both[:, :wide], top)
    down = dot(left_ref[0], own_ref[...], 0, 0) + dot(left_ref[1], other_ref[...], 0, 0)
    up = add_halves(dot(jnp.concatenate(halves(weighted_ref[...]), axis=1), gradient, 0, 0))
    up_ref[...] = up[:wide]
    put_chunks(chunk_ref, near_ref, far_ref, add_halves(down), up[wide:])


def curvature_kernel(
    top,
    masks,
    place_ref,
    small_ref,
    small_other_ref,
    own_ref,
    other_ref,
    weight_ref,
    weighted_ref,
    high_ref,
    low_ref,
    up_ref,
    to_ref,
    tangent_ref,
    arrived_ref,
    chunk_ref,
    near_ref,
    far_ref,
    left_ref,
):
    experts, _, curvature = token_columns(small_ref, small_other_ref, top)
    tokens, wide = weight_ref.shape
    block = tokens // 2
    model_width = up_ref.shape[1]
    column = members(place_ref, wide, masks)
    arrived = jnp.concatenate([arrived_ref[block:], arrived_ref[:block]], axis=0).astype(f32)
    resid = halves(curvature * (tangent_ref[...] + arrived))
    adapter_up = high_ref[0].reshape(wide, model_width), low_ref[0].reshape(wide, model_width)
    put_left(
        left_ref, experts, column, weight_ref[...] * (dot_pairs(resid, adapter_up, 1, 1) + to_ref[...]), top
    )
    down = dot(left_ref[0], own_ref[...], 0, 0) + dot(left_ref[1], other_ref[...], 0, 0)
    weighted_u = halves(weighted_ref[:, wide:])
    up = add_halves(dot(jnp.concatenate(weighted_u, axis=1), resid[0], 0, 0)) + dot(weighted_u[0], resid[1], 0, 0)
    put_chunks(chunk_ref, near_ref, far_ref, add_halves(down), up_ref[...] + up)


def far_kernel(hidden_width, arrived_ref, chunk_ref, _, *out_refs):
    count = len(out_refs)
    for place, out_ref in enumerate(out_refs):
        down, up = decode(arrived_ref[place], hidden_width)
        own = chunk_ref[chunk_ref.shape[0] - count + place]
        out_ref[...] = encode(own[:, :hidden_width] + down, own[:, hidden_width:] + up)


def near_kernel(hidden_width, gradient_ref, curvature_ref, gradient_chunk_ref, curvature_chunk_ref, out_ref, total_ref):
    pairs = ((gradient_ref, gradient_chunk_ref), (curvature_ref, curvature_chunk_ref))
    for kind, (arrived_ref, chunk_ref) in enumerate(pairs):
        for place in range(arrived_ref.shape[0]):
            down, up = decode(arrived_ref[place], hidden_width)
            own = chunk_ref[place]
            down, up = own[:, :hidden_width] + down, own[:, hidden_width:] + up
            if place == 0:
                total_ref[kind] = jnp.concatenate([down, up], axis=1)
            else:
                out_ref[place - 1, kind] = encode(down, up)


def total_kernel(hidden_width, far, total_ref, *rest):
    near_refs, far_refs, out_refs = rest[: -2 * far - 4], rest[-2 * far - 4 : -4], rest[-4:]
    for kind in range(2):
        down = total_ref[kind, :, :hidden_width]
        up = total_ref[kind, :, hidden_width:]
        arrived = [ref[kind] for ref in near_refs] + [ref[...] for ref in far_refs[kind * far : (kind + 1) * far]]
        for coded in arrived:
            more = decode(coded, hidden_width)
            down, up = down + more[0], up + more[1]
        out_refs[2 * kind][...] = down
        out_refs[2 * kind + 1][...] = up


class Ring:
    def __init__(self, size):
        self.length = size // 2
        rows = self.length // 2
        self.order = [4 * z for z in range(rows)] + [4 * z + 2 for z in reversed(range(rows))]

    def shift(self, value, step):
        pairs = [
            (chip + core, self.order[(place + step) % self.length] + core)
            for place, chip in enumerate(self.order)
            for core in range(2)
        ]
        return lax.ppermute(value, "expert", pairs)

    def members(self, me):
        rows = self.length // 2
        place = jnp.where(me // 2 % 2 == 0, me // 4, self.length - 1 - me // 4)
        there = (place + jnp.arange(self.length, dtype=jnp.int32)) % self.length
        return jnp.where(there < rows, 4 * there, 4 * (self.length - 1 - there) + 2) + me % 2

    def gather(self, own):
        half = self.length // 2
        found = {0: own}
        ahead, behind = own, own
        for step in range(1, half):
            behind = self.shift(behind, 1)
            ahead = self.shift(ahead, -1)
            found[self.length - step], found[step] = behind, ahead
        last = [self.shift(behind[:1], 1), self.shift(ahead[1:], -1)]
        return [found[offset] for offset in sorted(found)] + last


def exchange(value, mask):
    size = lax.axis_size("expert")
    return lax.ppermute(value, "expert", [(device, device ^ mask) for device in range(size)])


def gathered_plan(
    hidden_of_route,
    expert_of_route,
    gate_of_route,
    capacity,
    output_gradient,
    curvature,
    adapter_down,
    adapter_up,
    down_direction,
    up_direction,
):
    ring = Ring(lax.axis_size("expert"))
    slots = ring.length
    rows = slots // 2
    far = rows // 2
    masks = [4 * z for z in range(rows)] + [4 * z + 2 for z in range(rows)]
    me = lax.axis_index("expert")
    tokens, top = expert_of_route.shape
    both = 2 * tokens
    hidden_width = hidden_of_route.shape[2]
    rank = adapter_down.shape[2]
    model_width = output_gradient.shape[1]
    experts = capacity.shape[0]
    wide = slots * rank
    coded_width = hidden_width + model_width + lanes

    ring_members = ring.members(me)
    differs = ring_members ^ me
    slot_of_offset = differs // 4 + rows * (differs // 2 % 2)
    place = jnp.concatenate([me[None], slot_of_offset, ring_members]).astype(jnp.int32)

    def call(kernel, multiplies, outs, *operands, scratch=(), after=()):
        places = [
            pl.BlockSpec(memory_space=pltpu.SMEM if operand is place else pltpu.VMEM) for operand in operands
        ] + [pl.BlockSpec(memory_space=pl.ANY) for _ in after]
        return pl.pallas_call(
            kernel,
            out_shape=[jax.ShapeDtypeStruct(shape, dtype) for shape, dtype in outs],
            in_specs=places,
            scratch_shapes=scratch,
            compiler_params=pltpu.CompilerParams(vmem_limit_bytes=kernel_vmem),
            cost_estimate=pl.CostEstimate(flops=2 * multiplies, bytes_accessed=2**20, transcendentals=0),
        )(*operands, *after)

    down_multiplies = 2 * top * both * hidden_width * wide
    up_multiplies = both * model_width * wide

    piece, small = call(
        prepare_kernel,
        10**8,
        [((2, rank, coded_width), i16), (((2 * top + 8) // 8 * 8, tokens), f32)],
        expert_of_route.T,
        gate_of_route.T,
        curvature[None],
        down_direction[0].T,
        adapter_down[0].T,
        adapter_up[0],
        up_direction[0],
    )
    pieces = ring.gather(piece)
    small_other = exchange(small, 1)
    hidden = hidden_of_route.transpose(1, 0, 2).reshape(top * tokens, hidden_width)
    hidden_other = exchange(hidden, 1)
    gradient_other = exchange(output_gradient, 1)
    capacity_row = jnp.pad(capacity.astype(f32), (counts_lane, lanes - counts_lane - experts))[None, :]

    by_offset = pieces[:rows] + [pieces[-2]] + pieces[rows:-2]
    (prior,) = call(functools.partial(prior_kernel, masks), 10**8, [((8, lanes), f32)], place, *by_offset)
    prior_arrived = exchange(prior, 1)
    factor_halves = [pltpu.VMEM((2, slots, rank, hidden_width), bf16)] * 2
    (reduced,) = call(
        functools.partial(reduce_kernel, top, masks),
        2 * down_multiplies,
        [((2, both, wide), f32)],
        place,
        small,
        small_other,
        hidden,
        hidden_other,
        *pieces,
        scratch=factor_halves,
        after=[prior],
    )
    weight, weighted, tangent, coded, high, low = call(
        functools.partial(tangent_kernel, top, masks),
        6 * up_multiplies,
        [
            ((both, wide), f32),
            ((both, 2 * wide), f32),
            ((both, model_width), f32),
            ((both, model_width), bf16),
            ((2, slots, rank, model_width), bf16),
            ((2, slots, rank, model_width), bf16),
        ],
        place,
        small,
        small_other,
        capacity_row,
        prior,
        prior_arrived,
        reduced,
        *pieces,
    )
    arrived = exchange(coded, 1)
    left = [pltpu.VMEM((2, top * tokens, 2 * wide), bf16)]
    chunks = [
        ((rows, rank, hidden_width + model_width), f32),
        ((rows - far, rank, coded_width), i16),
        ((far, rank, coded_width), i16),
    ]
    gradient_own, gradient_near, gradient_far, up, to = call(
        functools.partial(gradient_kernel, top, masks),
        down_multiplies + 8 * up_multiplies,
        chunks + [((wide, model_width), f32), ((both, wide), f32)],
        place,
        small,
        small_other,
        hidden,
        hidden_other,
        output_gradient,
        gradient_other,
        weight,
        weighted,
        high,
        low,
        scratch=left,
    )
    gradient_far = exchange(gradient_far, 2)
    gradient_near = exchange(gradient_near, 2)
    curvature_own, curvature_near, curvature_far = call(
        functools.partial(curvature_kernel, top, masks),
        down_multiplies + 6 * up_multiplies,
        chunks,
        place,
        small,
        small_other,
        hidden,
        hidden_other,
        weight,
        weighted,
        high,
        low,
        up,
        to,
        tangent,
        arrived,
        scratch=left,
    )

    def along_z(arrived, own, after):
        sums = call(
            functools.partial(far_kernel, hidden_width),
            10**8,
            [((rank, coded_width), i16)] * far,
            arrived,
            own,
            after=[after],
        )
        return [exchange(part, 4 * z) for z, part in zip(range(rows - far, rows), sums)]

    gradient_parts = along_z(gradient_far, gradient_own, curvature_far)
    curvature_far = exchange(curvature_far, 2)
    curvature_near = exchange(curvature_near, 2)
    curvature_parts = along_z(curvature_far, curvature_own, gradient_near)
    near, total = call(
        functools.partial(near_kernel, hidden_width),
        10**8,
        [((rows - far - 1, 2, rank, coded_width), i16), ((2, rank, hidden_width + model_width), f32)],
        gradient_near,
        curvature_near,
        gradient_own,
        curvature_own,
    )
    near_parts = [exchange(near[z - 1], 4 * z) for z in range(1, rows - far)]
    down_gradient, up_gradient, curvature_down, curvature_up = call(
        functools.partial(total_kernel, hidden_width, far),
        10**8,
        [((rank, hidden_width), f32), ((rank, model_width), f32)] * 2,
        total,
        *near_parts,
        *gradient_parts,
        *curvature_parts,
    )
    return down_gradient.T[None], up_gradient[None], curvature_down.T[None], curvature_up[None]


def carried_in(value, axis, join, neutral):
    count, mine = (lax.axis_size(axis), lax.axis_index(axis))
    pieces = lax.all_gather(value, axis)
    so_far = jnp.full_like(value, 0) + jnp.asarray(neutral, value.dtype)

    def lap(position, so_far):
        longer = join(so_far, pieces[position])
        return jnp.where(position < mine, longer, so_far)

    return lax.fori_loop(0, count - 1, lap, so_far)


def add_counts(earlier, later):
    return earlier + later


def routed_plan(
    hidden_of_route,
    expert_of_route,
    gate_of_route,
    capacity,
    output_gradient,
    curvature,
    adapter_down,
    adapter_up,
    down_direction,
    up_direction,
):
    finest_precision = lax.Precision.HIGHEST
    group_size = lax.axis_size("expert")
    tok_rows, top_count = expert_of_route.shape
    hidden_width = hidden_of_route.shape[2]
    resident_experts = adapter_down.shape[0]
    adapter_rank = adapter_down.shape[2]
    model_width = output_gradient.shape[1]
    experts = resident_experts * group_size
    slot_most = 2 * tok_rows * top_count // experts
    routes = expert_of_route.reshape(-1)
    onehot = (routes[:, None] == jnp.arange(experts, dtype=jnp.int32)[None, :]).astype(jnp.int32)
    earlier = jnp.cumsum(onehot, axis=0) - onehot
    local_rank = jnp.sum(earlier * onehot, axis=1)
    counts = jnp.sum(onehot, axis=0)
    prior_count = carried_in(counts, "expert", add_counts, jnp.zeros_like(counts))
    global_rank = local_rank + jnp.sum(onehot * prior_count[None, :], axis=1)
    route_limit = jnp.sum(onehot * capacity[None, :], axis=1)
    retained_mask = (global_rank < route_limit).astype(jnp.float32)
    weight_of_route = (
        adapter_scale * gate_of_route.reshape(-1).astype(jnp.float32) * retained_mask
    ).astype(jnp.bfloat16)
    slot_index = routes * slot_most + local_rank
    layout = (group_size, resident_experts, slot_most)
    send_hidden = (
        jnp.zeros((experts * slot_most, hidden_width), jnp.bfloat16)
        .at[slot_index]
        .set(hidden_of_route.reshape(-1, hidden_width))
        .reshape(layout + (hidden_width,))
    )
    send_weight = (
        jnp.zeros((experts * slot_most,), jnp.bfloat16)
        .at[slot_index]
        .set(weight_of_route)
        .reshape(layout)
    )
    down_stacked = jnp.concatenate([adapter_down, down_direction], axis=2)
    up_stacked = jnp.concatenate([adapter_up, up_direction], axis=1)

    def spread(token_rows):
        per_route = jnp.repeat(token_rows, top_count, axis=0)
        placed = (
            jnp.zeros((experts * slot_most, model_width), jnp.bfloat16)
            .at[slot_index]
            .set(per_route)
        )
        return placed.reshape(layout + (model_width,))

    send_residual = spread(output_gradient)
    pieces = (
        lax.all_to_all(send_hidden, "expert", split_axis=0, concat_axis=0, tiled=True),
        lax.all_to_all(send_weight, "expert", split_axis=0, concat_axis=0, tiled=True),
    )
    hidden_rows = pieces[0].astype(jnp.float32)
    weight_rows = pieces[1].astype(jnp.float32)[..., None]
    reduced_hidden = jnp.einsum(
        "cjif,jfk->cjik", hidden_rows, down_stacked, precision=finest_precision
    )
    exchanged_rows = jnp.concatenate(
        [reduced_hidden[..., adapter_rank:], reduced_hidden[..., :adapter_rank]], axis=3
    )
    tangent_out = weight_rows * jnp.einsum(
        "cjik,jkd->cjid", exchanged_rows, up_stacked, precision=finest_precision
    )
    returned = lax.all_to_all(
        tangent_out.astype(jnp.bfloat16), "expert", split_axis=0, concat_axis=0, tiled=True
    )
    results = (returned, reduced_hidden) + tuple(pieces)
    returned = results[0]
    reduced_hidden = results[1]
    hidden_rows = results[2]
    weight_rows = results[3]
    route_tangent = returned.reshape(experts * slot_most, model_width)[slot_index]
    out_tangent = jnp.sum(
        route_tangent.reshape(tok_rows, top_count, model_width).astype(jnp.float32), axis=1
    )
    resid_tangent = (curvature[:, None] * out_tangent).astype(jnp.bfloat16)
    send_tangent = spread(resid_tangent)
    residual_rows, tangent_rows = (
        lax.all_to_all(send_residual, "expert", split_axis=0, concat_axis=0, tiled=True),
        lax.all_to_all(send_tangent, "expert", split_axis=0, concat_axis=0, tiled=True),
    )
    residual_full = residual_rows.astype(jnp.float32)
    complete_tangent = tangent_rows.astype(jnp.float32)
    weight_column = weight_rows.astype(jnp.float32)[..., None]
    residual_reduced = jnp.einsum(
        "wyov,yqv->wyoq", residual_full, up_stacked, precision=finest_precision
    )
    reduced_tangent = jnp.einsum(
        "wyov,yqv->wyoq", complete_tangent, adapter_up, precision=finest_precision
    )
    left_terms = jnp.concatenate(
        [
            weight_column * residual_reduced[..., :adapter_rank],
            weight_column * (reduced_tangent + residual_reduced[..., adapter_rank:]),
        ],
        axis=3,
    )
    down_terms = jnp.einsum(
        "cjif,cjik->jfk", hidden_rows.astype(jnp.float32), left_terms, precision=finest_precision
    )
    raised_update = weight_column * reduced_hidden[..., :adapter_rank]
    raised_tangent_update = weight_column * reduced_hidden[..., adapter_rank:]
    up_terms = jnp.einsum(
        "cjik,cjid->jkd",
        jnp.concatenate([raised_update, raised_tangent_update], axis=3),
        residual_full,
        precision=finest_precision,
    )
    curvature_piece = up_terms[:, adapter_rank:] + jnp.einsum(
        "cjik,cjid->jkd", raised_update, complete_tangent, precision=finest_precision
    )
    return (
        down_terms[..., :adapter_rank],
        up_terms[:, :adapter_rank],
        down_terms[..., adapter_rank:],
        curvature_piece,
    )


def local(*arguments):
    factor_bytes = 2 * 4 * (arguments[6].size + arguments[7].size) * lax.axis_size("expert")
    plan = gathered_plan if 4 * factor_bytes <= kernel_vmem else routed_plan
    return plan(*arguments)


def solution(mesh):
    return jax.shard_map(
        local,
        mesh=mesh,
        in_specs=(
            P(("groups", "expert"), None, None),
            P(("groups", "expert"), None),
            P(("groups", "expert"), None),
            P("groups"),
            P(("groups", "expert"), None),
            P(("groups", "expert")),
            P("expert", None, None),
            P("expert", None, None),
            P(("groups", "expert"), None, None),
            P(("groups", "expert"), None, None),
        ),
        out_specs=(
            P(("groups", "expert"), None, None),
            P(("groups", "expert"), None, None),
            P(("groups", "expert"), None, None),
            P(("groups", "expert"), None, None),
        ),
        check_vma=False,
    )
```

time: 124 us -> 86.1 us (0.69)
  other arithmetic: 24 us -> 0.11 us
  starting transfers between devices: 33.3 us -> 22.9 us
  local copies, waits for them, and re-layouts: 13.1 us -> 3 us
  Pallas kernels: 16.1 us -> 20 us
  waiting for transfers between devices: 35.1 us -> 39 us
    ppermute x30 -> x8, starting transfers between devices: 32.7 us -> 9.03 us  [shift(): return lax.ppermute(value, 'expert', pairs)]
    ppermute x5 -> x14, waiting for transfers between devices: 0.48 us -> 21.4 us  [exchange(): lax.ppermute(value, 'expert', [(device, device ^ mask) for device in rang...]
    ppermute x30 -> x8, waiting for transfers between devices: 34.7 us -> 17.6 us  [shift(): return lax.ppermute(value, 'expert', pairs)]
    ppermute x5 -> x14, starting transfers between devices: 0.58 us -> 13.8 us  [exchange(): lax.ppermute(value, 'expert', [(device, device ^ mask) for device in rang...]
    mul x16 -> x0, other arithmetic: 11.8 us -> none  [the longest x8 7.03 us: gathered_plan(): piece[..., :hidden_width].astype(f32) * (1 / down_scale)]
    another operation x10 -> x0, local copies, waits for them, and re-layouts: 5.78 us -> none  [the longest x9 5.69 us: gathered_plan(): jnp.stack([piece[0, 0, hidden_width:hidden_width + experts] for piece in...]
    pallas_call x4 -> x10, Pallas kernels: 16.1 us -> 20 us  [call(): pl.pallas_call(kernel, out_shape=[jax.ShapeDtypeStruct(shape, dtype) for...]
    broadcast_in_dim x20 -> x1, local copies, waits for them, and re-layouts: 3.71 us -> 0.07 us  [gathered_plan(): jnp.pad(capacity.astype(f32), (counts_lane, lanes - counts_lane - experts))]
  transfers between devices with their start and end apart: 35 -> 22, of which waited for: 16 -> 10; matrix products, arithmetic and copies ran while one was open for 25% -> 0% of each run, Pallas kernels for 5% -> 19%
where the time goes in v7:
time: 86.1 us; the launch traced here: 85.9 us
  waiting for transfers between devices  39 us (45%)
  starting transfers between devices  22.9 us (27%)
  Pallas kernels  20 us (23%)
  local copies, waits for them, and re-layouts  3 us (3%)
  between operations  0.89 us (1%)
    ppermute x14, waiting for transfers between devices, exchange(): lax.ppermute(value, 'expert', [(device, device ^ mask) for device in rang...  21.4 us
    pallas_call x10, Pallas kernels, call(): pl.pallas_call(kernel, out_shape=[jax.ShapeDtypeStruct(shape, dtype) for...  20 us
    ppermute x8, waiting for transfers between devices, shift(): return lax.ppermute(value, 'expert', pairs)  17.6 us
    ppermute x14, starting transfers between devices, exchange(): lax.ppermute(value, 'expert', [(device, device ^ mask) for device in rang...  13.8 us
    ppermute x8, starting transfers between devices, shift(): return lax.ppermute(value, 'expert', pairs)  9.03 us
    transpose x1, local copies, waits for them, and re-layouts, gathered_plan(): hidden_of_route.transpose(1, 0, 2).reshape(top * tokens, hidden_width)  2.87 us
  transfers between devices with their start and end apart: 22, of which 10 were waited for; matrix products, arithmetic and copies ran while one was open for 0% of the time, Pallas kernels for 19%

profile of v7, /device:TPU:0, one launch (start us, length us, event | category | flops | bytes accessed | tf_op | source)
XLA Modules:
  0.0 85.9 jit_solution(12971026863930812177)
XLA Ops:
  0.7 2.9 %copy.14 = bf16[8,128,1024]{2,1,0:T(8,128)(2,1)S(1)} copy(bf16[8,128,1024]{2,0,1:T(8,128)(2,1)} %bitcast.37) | data formatting | bytes 4194304 | tf_op jit(solution)/shard_map/transpose | solution.py:430
  4.4 2.7 %collective-permute-start.6 = (s16[2,16,3200]{2,1,0:T(8,128)(2,1)S(1)}, s16[2,16,3200]{2,1,0:T(8,128)(2,1)S(1)}, u32[]{:S(2)}, u32[]{:S(2)}) collective-permute-start(s16[2,16,3200]{2,1,0:T(8,128)(2,1)S(1)} %get-tuple-element.31.rest_0_), channel_id=1, source_target_pairs={{0,4},{1,5},{4,8},{5,9},{8,12},{9,13},{12,14},{13,15},{14,10},{15,... | collective-permute-start | bytes 614408 | tf_op jit(solution)/shard_map/ppermute | solution.py:343
  7.0 5.6 %collective-permute-done.6.rest_7_.rest_6_ = s16[2,16,3200]{2,1,0:T(8,128)(2,1)S(1)} collective-permute-done((s16[2,16,3200]{2,1,0:T(8,128)(2,1)S(1)}, s16[2,16,3200]{2,1,0:T(8,128)(2,1)S(1)}, u32[]{:S(2)}, u32[]{:S(2)}) %collective-permute-start.6) | collective-permute-done | bytes 204832 | tf_op jit(solution)/shard_map/ppermute | solution.py:343
  12.6 1.8 %collective-permute-start.7 = (s16[2,16,3200]{2,1,0:T(8,128)(2,1)S(1)}, s16[2,16,3200]{2,1,0:T(8,128)(2,1)S(1)}, u32[]{:S(2)}, u32[]{:S(2)}) collective-permute-start(s16[2,16,3200]{2,1,0:T(8,128)(2,1)S(1)} %collective-permute-done.6.rest_7_.rest_6_), channel_id=1, source_target_pairs={{0,4},{1,5},{4,8},{5,9},{8,12},{9,13},{12,14},{13,15},{14,10},{15,... | collective-permute-start | bytes 614408 | tf_op jit(solution)/shard_map/ppermute | solution.py:343
  14.7 4.8 %collective-permute-done.7.rest_6_.rest_5_ = s16[2,16,3200]{2,1,0:T(8,128)(2,1)S(1)} collective-permute-done((s16[2,16,3200]{2,1,0:T(8,128)(2,1)S(1)}, s16[2,16,3200]{2,1,0:T(8,128)(2,1)S(1)}, u32[]{:S(2)}, u32[]{:S(2)}) %collective-permute-start.7) | collective-permute-done | bytes 204832 | tf_op jit(solution)/shard_map/ppermute | solution.py:343
  19.5 1.6 %collective-permute-start.8 = (s16[2,16,3200]{2,1,0:T(8,128)(2,1)S(1)}, s16[2,16,3200]{2,1,0:T(8,128)(2,1)S(1)}, u32[]{:S(2)}, u32[]{:S(2)}) collective-permute-start(s16[2,16,3200]{2,1,0:T(8,128)(2,1)S(1)} %collective-permute-done.7.rest_6_.rest_5_), channel_id=1, source_target_pairs={{0,4},{1,5},{4,8},{5,9},{8,12},{9,13},{12,14},{13,15},{14,10},{15,... | collective-permute-start | bytes 614408 | tf_op jit(solution)/shard_map/ppermute | solution.py:343
  21.7 3.9 %collective-permute-done.8.rest_5_.rest_4_ = s16[2,16,3200]{2,1,0:T(8,128)(2,1)S(1)} collective-permute-done((s16[2,16,3200]{2,1,0:T(8,128)(2,1)S(1)}, s16[2,16,3200]{2,1,0:T(8,128)(2,1)S(1)}, u32[]{:S(2)}, u32[]{:S(2)}) %collective-permute-start.8) | collective-permute-done | bytes 204832 | tf_op jit(solution)/shard_map/ppermute | solution.py:343
  25.5 1.4 %collective-permute-start.9 = (s16[1,16,3200]{2,1,0:T(8,128)(2,1)S(1)}, s16[1,16,3200]{2,1,0:T(8,128)(2,1)S(1)}, u32[]{:S(2)}, u32[]{:S(2)}) collective-permute-start(s16[1,16,3200]{2,1,0:T(8,128)(2,1)S(1)} %slice.8), channel_id=1, source_target_pairs={{0,4},{1,5},{4,8},{5,9},{8,12},{9,13},{12,14},{13,15},{14,10},{15,... | collective-permute-start | bytes 307208 | tf_op jit(solution)/shard_map/ppermute | solution.py:343
  27.9 2.3 %collective-permute-done.9.rest_4_.rest_7_ = s16[1,16,3200]{2,1,0:T(8,128)(2,1)S(1)} collective-permute-done((s16[1,16,3200]{2,1,0:T(8,128)(2,1)S(1)}, s16[1,16,3200]{2,1,0:T(8,128)(2,1)S(1)}, u32[]{:S(2)}, u32[]{:S(2)}) %collective-permute-start.9) | collective-permute-done | bytes 102432 | tf_op jit(solution)/shard_map/ppermute | solution.py:343
  31.9 4.3 %shard_map.131.reduced_ref = f32[2,256,128]{2,1,0:T(8,128)S(1)} custom-call(s32[17]{0:T(128)S(1)} %pad_add_fusion.place_ref, f32[24,128]{1,0:T(8,128)S(1)} %get-tuple-element.30.small_ref, f32[24,128]{1,0:T(8,128)S(1)} %collective-permute-done.small_other_ref, bf16[1024,1024]{1,0:T(8,128)(2,1)S(1)} %bitcast.26, ...), custom_call_target="tpu_custom_call" | custom-call | flops 2147483648 | bytes 1048576 | tf_op jit(solution)/shard_map/pallas_call | solution.py:404
  36.2 2.9 %shard_map.132 = (f32[256,128]{1,0:T(8,128)S(1)}, f32[256,256]{1,0:T(8,128)S(1)}, f32[256,2048]{1,0:T(8,128)S(1)}, bf16[256,2048]{1,0:T(8,128)(2,1)S(1)}, bf16[2...) custom-call(s32[17]{0:T(128)S(1)} %pad_add_fusion.place_ref, ...), custom_call_target="tpu_custom_call" | custom-call | flops 805306368 | bytes 1048576 | tf_op jit(solution)/shard_map/pallas_call | solution.py:404
  39.7 2.9 %collective-permute-done.2.other_gradient_ref = bf16[128,2048]{1,0:T(8,128)(2,1)S(1)} collective-permute-done((bf16[128,2048]{1,0:T(8,128)(2,1)S(1)}, bf16[128,2048]{1,0:T(8,128)(2,1)S(1)}, u32[]{:S(2)}, u32[]{:S(2)}) %collective-permute-start.2) | collective-permute-done | bytes 524320 | tf_op jit(solution)/shard_map/ppermute | solution.py:365
  42.6 5.5 %shard_map.133 = (f32[4,16,3072]{2,1,0:T(8,128)S(1)}, s16[2,16,3200]{2,1,0:T(8,128)(2,1)S(1)}, s16[2,16,3200]{2,1,0:T(8,128)(2,1)S(1)}, f32[128,2048]{1,0:T(8,128)S(1)}, f32[256,128]{1,0:T(8,128)S(1)}) custom-call(s32[17]{0:T(128)S(1)} %pad_add_fusion.place_ref, f32[24,128]{1,0:T(8,128)S(1)} %get-tuple-element.30.small_ref, ...), custom_call_target="tpu_custom_call" | custom-call | flops 2147483648 | bytes 1048576 | tf_op jit(solution)/shard_map/pallas_call | solution.py:404
  48.8 4.9 %shard_map.134 = (f32[4,16,3072]{2,1,0:T(8,128)S(1)}, s16[2,16,3200]{2,1,0:T(8,128)(2,1)S(1)}, s16[2,16,3200]{2,1,0:T(8,128)(2,1)S(1)}) custom-call(s32[17]{0:T(128)S(1)} %pad_add_fusion.place_ref, f32[24,128]{1,0:T(8,128)S(1)} %get-tuple-element.30.small_ref, f32[24,128]{1,0:T(8,128)S(1)} %collective-permute-done.small_other_ref, ...), custom_call_target="tpu_custom_call" | custom-call | flops 1879048192 | bytes 1048576 | tf_op jit(solution)/shard_map/pallas_call | solution.py:404
  53.7 1.5 %collective-permute-start.14 = (s16[2,16,3200]{2,1,0:T(8,128)(2,1)S(1)}, s16[2,16,3200]{2,1,0:T(8,128)(2,1)S(1)}, u32[]{:S(2)}, u32[]{:S(2)}) collective-permute-start(s16[2,16,3200]{2,1,0:T(8,128)(2,1)S(1)} %get-tuple-element.41), channel_id=1, source_target_pairs={{0,2},{1,3},{2,0},{3,1},{4,6},{5,7},{6,4},{7,5},{8,10},{9,11},{10,... | collective-permute-start | bytes 614408 | tf_op jit(solution)/shard_map/ppermute | solution.py:365
  55.8 1.4 %collective-permute-start.19 = (s16[2,16,3200]{2,1,0:T(8,128)(2,1)S(1)}, s16[2,16,3200]{2,1,0:T(8,128)(2,1)S(1)}, u32[]{:S(2)}, u32[]{:S(2)}) collective-permute-start(s16[2,16,3200]{2,1,0:T(8,128)(2,1)S(1)} %get-tuple-element.47._), channel_id=1, source_target_pairs={{0,2},{1,3},{2,0},{3,1},{4,6},{5,7},{6,4},{7,5},{8,10},{9,11},{10,... | collective-permute-start | bytes 614408 | tf_op jit(solution)/shard_map/ppermute | solution.py:365
  57.2 4.5 %collective-permute-done.14.curvature_ref = s16[2,16,3200]{2,1,0:T(8,128)(2,1)S(1)} collective-permute-done((s16[2,16,3200]{2,1,0:T(8,128)(2,1)S(1)}, s16[2,16,3200]{2,1,0:T(8,128)(2,1)S(1)}, u32[]{:S(2)}, u32[]{:S(2)}) %collective-permute-start.14) | collective-permute-done | bytes 204832 | tf_op jit(solution)/shard_map/ppermute | solution.py:365
  62.0 1.4 %collective-permute-start.15 = (s16[2,16,3200]{2,1,0:T(8,128)(2,1)S(1)}, s16[2,16,3200]{2,1,0:T(8,128)(2,1)S(1)}, u32[]{:S(2)}, u32[]{:S(2)}) collective-permute-start(s16[2,16,3200]{2,1,0:T(8,128)(2,1)S(1)} %bitcast.29), channel_id=1, source_target_pairs={{0,4},{1,5},{2,6},{3,7},{4,0},{5,1},{6,2},{7,3},{8,12},{9,13},{10,... | collective-permute-start | bytes 614408 | tf_op jit(solution)/shard_map/ppermute | solution.py:365
  63.4 2.7 %collective-permute-done.16.arrived_ref = s16[2,16,3200]{2,1,0:T(8,128)(2,1)S(1)} collective-permute-done((s16[2,16,3200]{2,1,0:T(8,128)(2,1)S(1)}, s16[2,16,3200]{2,1,0:T(8,128)(2,1)S(1)}, u32[]{:S(2)}, u32[]{:S(2)}) %collective-permute-start.16) | collective-permute-done | bytes 204832 | tf_op jit(solution)/shard_map/ppermute | solution.py:365
  66.3 2.5 %collective-permute-start.17 = (s16[16,3200]{1,0:T(8,128)(2,1)S(1)}, s16[16,3200]{1,0:T(8,128)(2,1)S(1)}, u32[]{:S(2)}, u32[]{:S(2)}) collective-permute-start(s16[16,3200]{1,0:T(8,128)(2,1)S(1)} %get-tuple-element.48), channel_id=1, source_target_pairs={{0,8},{1,9},{2,10},{3,11},{4,12},{5,13},{6,14},{7,15},{8,0},{9,1},... | collective-permute-start | bytes 307208 | tf_op jit(solution)/shard_map/ppermute | solution.py:365
  68.8 1.3 %collective-permute-start.18 = (s16[16,3200]{1,0:T(8,128)(2,1)S(1)}, s16[16,3200]{1,0:T(8,128)(2,1)S(1)}, u32[]{:S(2)}, u32[]{:S(2)}) collective-permute-start(s16[16,3200]{1,0:T(8,128)(2,1)S(1)} %get-tuple-element.49), channel_id=1, source_target_pairs={{0,12},{1,13},{2,14},{3,15},{4,8},{5,9},{6,10},{7,11},{8,4},{9,5},... | collective-permute-start | bytes 307208 | tf_op jit(solution)/shard_map/ppermute | solution.py:365
  70.4 1.9 %collective-permute-start.20 = (s16[16,3200]{1,0:T(8,128)(2,1)S(1)}, s16[16,3200]{1,0:T(8,128)(2,1)S(1)}, u32[]{:S(2)}, u32[]{:S(2)}) collective-permute-start(s16[16,3200]{1,0:T(8,128)(2,1)S(1)} %get-tuple-element.50), channel_id=1, source_target_pairs={{0,8},{1,9},{2,10},{3,11},{4,12},{5,13},{6,14},{7,15},{8,0},{9,1},... | collective-permute-start | bytes 307208 | tf_op jit(solution)/shard_map/ppermute | solution.py:365
  73.7 7.1 %collective-permute-done.17.rest_1_ = s16[16,3200]{1,0:T(8,128)(2,1)S(1)} collective-permute-done((s16[16,3200]{1,0:T(8,128)(2,1)S(1)}, s16[16,3200]{1,0:T(8,128)(2,1)S(1)}, u32[]{:S(2)}, u32[]{:S(2)}) %collective-permute-start.17) | collective-permute-done | bytes 102432 | tf_op jit(solution)/shard_map/ppermute | solution.py:365
  80.8 4.2 %collective-permute-done.20.rest_3_ = s16[16,3200]{1,0:T(8,128)(2,1)S(1)} collective-permute-done((s16[16,3200]{1,0:T(8,128)(2,1)S(1)}, s16[16,3200]{1,0:T(8,128)(2,1)S(1)}, u32[]{:S(2)}, u32[]{:S(2)}) %collective-permute-start.20) | collective-permute-done | bytes 102432 | tf_op jit(solution)/shard_map/ppermute | solution.py:365
  (55 shorter events, 9.0 us)
Async XLA Ops:
  0.6 3.5 %copy-start.1 = (f32[1,16,2048]{2,1,0:T(8,128)S(1)}, f32[1,16,2048]{2,1,0:T(8,128)}, u32[]{:S(2)}) copy-start(f32[1,16,2048]{2,1,0:T(8,128)} %param.17) | copy-start | bytes 393220
  0.7 14.0 %copy-start.8 = (s32[16]{0:T(128)S(1)}, s32[16]{0:T(128)}, u32[]{:S(2)}) copy-start(s32[16]{0:T(128)} %param.13) | copy-start | bytes 196
  3.6 28.3 %collective-permute-start.1 = (bf16[1024,1024]{1,0:T(8,128)(2,1)S(1)}, bf16[1024,1024]{1,0:T(8,128)(2,1)}, u32[]{:S(2)}, u32[]{:S(2)}) collective-permute-start(bf16[1024,1024]{1,0:T(8,128)(2,1)S(1)} %bitcast.25), channel_id=1, source_target_pairs={{0,1},{1,0},{2,3},{3,2},{4,5},{5,4},{6,7},{7,6},{8,9},{9,8},{10,11... | collective-permute-start | bytes 6291464 | tf_op jit(solution)/shard_map/ppermute | solution.py:365
  4.4 8.3 %collective-permute-start.6 = (s16[2,16,3200]{2,1,0:T(8,128)(2,1)S(1)}, s16[2,16,3200]{2,1,0:T(8,128)(2,1)S(1)}, u32[]{:S(2)}, u32[]{:S(2)}) collective-permute-start(s16[2,16,3200]{2,1,0:T(8,128)(2,1)S(1)} %get-tuple-element.31.rest_0_), channel_id=1, source_target_pairs={{0,4},{1,5},{4,8},{5,9},{8,12},{9,13},{12,14},{13,15},{14,10},{15,... | collective-permute-start | bytes 614408 | tf_op jit(solution)/shard_map/ppermute | solution.py:343
  7.0 7.5 %collective-permute-start.3 = (s16[2,16,3200]{2,1,0:T(8,128)(2,1)S(1)}, s16[2,16,3200]{2,1,0:T(8,128)(2,1)S(1)}, u32[]{:S(2)}, u32[]{:S(2)}) collective-permute-start(s16[2,16,3200]{2,1,0:T(8,128)(2,1)S(1)} %get-tuple-element.31.rest_0_), channel_id=1, source_target_pairs={{0,2},{1,3},{4,0},{5,1},{8,4},{9,5},{12,8},{13,9},{14,12},{15,13},... | collective-permute-start | bytes 614408 | tf_op jit(solution)/shard_map/ppermute | solution.py:343
  12.6 6.9 %collective-permute-start.7 = (s16[2,16,3200]{2,1,0:T(8,128)(2,1)S(1)}, s16[2,16,3200]{2,1,0:T(8,128)(2,1)S(1)}, u32[]{:S(2)}, u32[]{:S(2)}) collective-permute-start(s16[2,16,3200]{2,1,0:T(8,128)(2,1)S(1)} %collective-permute-done.6.rest_7_.rest_6_), channel_id=1, source_target_pairs={{0,4},{1,5},{4,8},{5,9},{8,12},{9,13},{12,14},{13,15},{14,10},{15,... | collective-permute-start | bytes 614408 | tf_op jit(solution)/shard_map/ppermute | solution.py:343
  14.5 6.7 %collective-permute-start.4 = (s16[2,16,3200]{2,1,0:T(8,128)(2,1)S(1)}, s16[2,16,3200]{2,1,0:T(8,128)(2,1)S(1)}, u32[]{:S(2)}, u32[]{:S(2)}) collective-permute-start(s16[2,16,3200]{2,1,0:T(8,128)(2,1)S(1)} %collective-permute-done.3.rest_1_), channel_id=1, source_target_pairs={{0,2},{1,3},{4,0},{5,1},{8,4},{9,5},{12,8},{13,9},{14,12},{15,13},... | collective-permute-start | bytes 614408 | tf_op jit(solution)/shard_map/ppermute | solution.py:343
  14.7 16.2 %collective-permute-start = (f32[24,128]{1,0:T(8,128)S(1)}, f32[24,128]{1,0:T(8,128)S(1)}, u32[]{:S(2)}, u32[]{:S(2)}) collective-permute-start(f32[24,128]{1,0:T(8,128)S(1)} %get-tuple-element.30.small_ref), channel_id=1, source_target_pairs={{0,1},{1,0},{2,3},{3,2},{4,5},{5,4},{6,7},{7,6},{8,9},{9,8},{10,11... | collective-permute-start | bytes 36872 | tf_op jit(solution)/shard_map/ppermute | solution.py:365
  19.5 6.0 %collective-permute-start.8 = (s16[2,16,3200]{2,1,0:T(8,128)(2,1)S(1)}, s16[2,16,3200]{2,1,0:T(8,128)(2,1)S(1)}, u32[]{:S(2)}, u32[]{:S(2)}) collective-permute-start(s16[2,16,3200]{2,1,0:T(8,128)(2,1)S(1)} %collective-permute-done.7.rest_6_.rest_5_), channel_id=1, source_target_pairs={{0,4},{1,5},{4,8},{5,9},{8,12},{9,13},{12,14},{13,15},{14,10},{15,... | collective-permute-start | bytes 614408 | tf_op jit(solution)/shard_map/ppermute | solution.py:343
  21.1 5.8 %collective-permute-start.5 = (s16[2,16,3200]{2,1,0:T(8,128)(2,1)S(1)}, s16[2,16,3200]{2,1,0:T(8,128)(2,1)S(1)}, u32[]{:S(2)}, u32[]{:S(2)}) collective-permute-start(s16[2,16,3200]{2,1,0:T(8,128)(2,1)S(1)} %collective-permute-done.4.rest_2_), channel_id=1, source_target_pairs={{0,2},{1,3},{4,0},{5,1},{8,4},{9,5},{12,8},{13,9},{14,12},{15,13},... | collective-permute-start | bytes 614408 | tf_op jit(solution)/shard_map/ppermute | solution.py:343
  25.5 4.7 %collective-permute-start.9 = (s16[1,16,3200]{2,1,0:T(8,128)(2,1)S(1)}, s16[1,16,3200]{2,1,0:T(8,128)(2,1)S(1)}, u32[]{:S(2)}, u32[]{:S(2)}) collective-permute-start(s16[1,16,3200]{2,1,0:T(8,128)(2,1)S(1)} %slice.8), channel_id=1, source_target_pairs={{0,4},{1,5},{4,8},{5,9},{8,12},{9,13},{12,14},{13,15},{14,10},{15,... | collective-permute-start | bytes 307208 | tf_op jit(solution)/shard_map/ppermute | solution.py:343
  27.0 4.9 %collective-permute-start.11 = (s16[1,16,3200]{2,1,0:T(8,128)(2,1)S(1)}, s16[1,16,3200]{2,1,0:T(8,128)(2,1)S(1)}, u32[]{:S(2)}, u32[]{:S(2)}) collective-permute-start(s16[1,16,3200]{2,1,0:T(8,128)(2,1)S(1)} %slice.9), channel_id=1, source_target_pairs={{0,2},{1,3},{4,0},{5,1},{8,4},{9,5},{12,8},{13,9},{14,12},{15,13},... | collective-permute-start | bytes 307208 | tf_op jit(solution)/shard_map/ppermute | solution.py:343
  30.8 5.3 %collective-permute-start.10 = (f32[8,128]{1,0:T(8,128)S(1)}, f32[8,128]{1,0:T(8,128)S(1)}, u32[]{:S(2)}, u32[]{:S(2)}) collective-permute-start(f32[8,128]{1,0:T(8,128)S(1)} %shard_map.130.rest_9_.prior_ref), channel_id=1, source_target_pairs={{0,1},{1,0},{2,3},{3,2},{4,5},{5,4},{6,7},{7,6},{8,9},{9,8},{10,11... | collective-permute-start | bytes 12296 | tf_op jit(solution)/shard_map/ppermute | solution.py:365
  39.1 9.7 %collective-permute-start.13 = (bf16[256,2048]{1,0:T(8,128)(2,1)S(1)}, bf16[256,2048]{1,0:T(8,128)(2,1)S(1)}, u32[]{:S(2)}, u32[]{:S(2)}) collective-permute-start(bf16[256,2048]{1,0:T(8,128)(2,1)S(1)} %get-tuple-element.40), channel_id=1, source_target_pairs={{0,1},{1,0},{2,3},{3,2},{4,5},{5,4},{6,7},{7,6},{8,9},{9,8},{10,11... | collective-permute-start | bytes 3145736 | tf_op jit(solution)/shard_map/ppermute | solution.py:365
  39.2 3.4 %collective-permute-start.2 = (bf16[128,2048]{1,0:T(8,128)(2,1)S(1)}, bf16[128,2048]{1,0:T(8,128)(2,1)S(1)}, u32[]{:S(2)}, u32[]{:S(2)}) collective-permute-start(bf16[128,2048]{1,0:T(8,128)(2,1)S(1)} %copy-done), channel_id=1, source_target_pairs={{0,1},{1,0},{2,3},{3,2},{4,5},{5,4},{6,7},{7,6},{8,9},{9,8},{10,11... | collective-permute-start | bytes 1572872 | tf_op jit(solution)/shard_map/ppermute | solution.py:365
  48.1 9.1 %collective-permute-start.12 = (s16[2,16,3200]{2,1,0:T(8,128)(2,1)S(1)}, s16[2,16,3200]{2,1,0:T(8,128)(2,1)S(1)}, u32[]{:S(2)}, u32[]{:S(2)}) collective-permute-start(s16[2,16,3200]{2,1,0:T(8,128)(2,1)S(1)} %get-tuple-element.36), channel_id=1, source_target_pairs={{0,2},{1,3},{2,0},{3,1},{4,6},{5,7},{6,4},{7,5},{8,10},{9,11},{10,... | collective-permute-start | bytes 614408 | tf_op jit(solution)/shard_map/ppermute | solution.py:365
  53.7 8.0 %collective-permute-start.14 = (s16[2,16,3200]{2,1,0:T(8,128)(2,1)S(1)}, s16[2,16,3200]{2,1,0:T(8,128)(2,1)S(1)}, u32[]{:S(2)}, u32[]{:S(2)}) collective-permute-start(s16[2,16,3200]{2,1,0:T(8,128)(2,1)S(1)} %get-tuple-element.41), channel_id=1, source_target_pairs={{0,2},{1,3},{2,0},{3,1},{4,6},{5,7},{6,4},{7,5},{8,10},{9,11},{10,... | collective-permute-start | bytes 614408 | tf_op jit(solution)/shard_map/ppermute | solution.py:365
  55.1 11.0 %collective-permute-start.16 = (s16[2,16,3200]{2,1,0:T(8,128)(2,1)S(1)}, s16[2,16,3200]{2,1,0:T(8,128)(2,1)S(1)}, u32[]{:S(2)}, u32[]{:S(2)}) collective-permute-start(s16[2,16,3200]{2,1,0:T(8,128)(2,1)S(1)} %get-tuple-element.46), channel_id=1, source_target_pairs={{0,2},{1,3},{2,0},{3,1},{4,6},{5,7},{6,4},{7,5},{8,10},{9,11},{10,... | collective-permute-start | bytes 614408 | tf_op jit(solution)/shard_map/ppermute | solution.py:365
  55.8 14.4 %collective-permute-start.19 = (s16[2,16,3200]{2,1,0:T(8,128)(2,1)S(1)}, s16[2,16,3200]{2,1,0:T(8,128)(2,1)S(1)}, u32[]{:S(2)}, u32[]{:S(2)}) collective-permute-start(s16[2,16,3200]{2,1,0:T(8,128)(2,1)S(1)} %get-tuple-element.47._), channel_id=1, source_target_pairs={{0,2},{1,3},{2,0},{3,1},{4,6},{5,7},{6,4},{7,5},{8,10},{9,11},{10,... | collective-permute-start | bytes 614408 | tf_op jit(solution)/shard_map/ppermute | solution.py:365
  62.0 23.0 %collective-permute-start.15 = (s16[2,16,3200]{2,1,0:T(8,128)(2,1)S(1)}, s16[2,16,3200]{2,1,0:T(8,128)(2,1)S(1)}, u32[]{:S(2)}, u32[]{:S(2)}) collective-permute-start(s16[2,16,3200]{2,1,0:T(8,128)(2,1)S(1)} %bitcast.29), channel_id=1, source_target_pairs={{0,4},{1,5},{2,6},{3,7},{4,0},{5,1},{6,2},{7,3},{8,12},{9,13},{10,... | collective-permute-start | bytes 614408 | tf_op jit(solution)/shard_map/ppermute | solution.py:365
  66.3 14.4 %collective-permute-start.17 = (s16[16,3200]{1,0:T(8,128)(2,1)S(1)}, s16[16,3200]{1,0:T(8,128)(2,1)S(1)}, u32[]{:S(2)}, u32[]{:S(2)}) collective-permute-start(s16[16,3200]{1,0:T(8,128)(2,1)S(1)} %get-tuple-element.48), channel_id=1, source_target_pairs={{0,8},{1,9},{2,10},{3,11},{4,12},{5,13},{6,14},{7,15},{8,0},{9,1},... | collective-permute-start | bytes 307208 | tf_op jit(solution)/shard_map/ppermute | solution.py:365
  68.8 11.9 %collective-permute-start.18 = (s16[16,3200]{1,0:T(8,128)(2,1)S(1)}, s16[16,3200]{1,0:T(8,128)(2,1)S(1)}, u32[]{:S(2)}, u32[]{:S(2)}) collective-permute-start(s16[16,3200]{1,0:T(8,128)(2,1)S(1)} %get-tuple-element.49), channel_id=1, source_target_pairs={{0,12},{1,13},{2,14},{3,15},{4,8},{5,9},{6,10},{7,11},{8,4},{9,5},... | collective-permute-start | bytes 307208 | tf_op jit(solution)/shard_map/ppermute | solution.py:365
  70.4 14.6 %collective-permute-start.20 = (s16[16,3200]{1,0:T(8,128)(2,1)S(1)}, s16[16,3200]{1,0:T(8,128)(2,1)S(1)}, u32[]{:S(2)}, u32[]{:S(2)}) collective-permute-start(s16[16,3200]{1,0:T(8,128)(2,1)S(1)} %get-tuple-element.50), channel_id=1, source_target_pairs={{0,8},{1,9},{2,10},{3,11},{4,12},{5,13},{6,14},{7,15},{8,0},{9,1},... | collective-permute-start | bytes 307208 | tf_op jit(solution)/shard_map/ppermute | solution.py:365
  72.3 12.7 %collective-permute-start.21 = (s16[16,3200]{1,0:T(8,128)(2,1)S(1)}, s16[16,3200]{1,0:T(8,128)(2,1)S(1)}, u32[]{:S(2)}, u32[]{:S(2)}) collective-permute-start(s16[16,3200]{1,0:T(8,128)(2,1)S(1)} %get-tuple-element.51), channel_id=1, source_target_pairs={{0,12},{1,13},{2,14},{3,15},{4,8},{5,9},{6,10},{7,11},{8,4},{9,5},... | collective-permute-start | bytes 307208 | tf_op jit(solution)/shard_map/ppermute | solution.py:365
  (7 other events, 23.7 us)

commit v8 on v7

--- a/solution.py
+++ b/solution.py
@@ -53,7 +53,7 @@
 
 
 def prepare_kernel(expert_ref, gate_ref, curvature_ref, *rest):
-    (down_direction_ref, adapter_down_ref, adapter_up_ref, up_direction_ref, piece_ref, small_ref) = rest
+    (down_direction_ref, adapter_down_ref, adapter_up_ref, up_direction_ref, *piece_refs, small_ref) = rest
     top = expert_ref.shape[0]
     small_ref[...] = jnp.zeros_like(small_ref)
     small_ref[:top] = expert_ref[...].astype(f32)
@@ -65,8 +65,8 @@
         named = jnp.where(expert_ref[...] == expert, 1.0, 0.0)
         total = jnp.sum(jnp.sum(named, axis=0, keepdims=True), axis=1, keepdims=True)
         counts = jnp.where(lane == counts_lane + expert, total, counts)
-    piece_ref[0] = encode(down_direction_ref[...], adapter_up_ref[...], counts)
-    piece_ref[1] = encode(adapter_down_ref[...], up_direction_ref[...], counts)
+    piece_refs[0][...] = encode(down_direction_ref[...], adapter_up_ref[...], counts)
+    piece_refs[1][...] = encode(adapter_down_ref[...], up_direction_ref[...], counts)
 
 
 def token_columns(own_ref, other_ref, top):
@@ -93,44 +93,67 @@
         total = jnp.zeros((1, lanes), f32)
         for offset in range(slots):
             device = place_ref[1 + slots + offset]
-            tail = piece_refs[offset][0, :, piece_refs[offset].shape[2] - lanes :]
+            tail = piece_refs[offset][:, piece_refs[offset].shape[1] - lanes :]
             counts = tail.astype(jnp.int32).astype(f32)[0:1]
             total = total + jnp.where(device < number, counts, 0.0)
         prior_ref[block : block + 1] = total
 
 
-def piece_part(refs, offset, kind):
-    last = len(refs) - 2
-    half = last // 2 + 1
-    if offset == half:
-        return refs[last + kind][0]
-    return refs[offset if offset < half else offset - 1][kind]
-
-
-def reduce_kernel(top, masks, place_ref, small_ref, small_other_ref, own_ref, other_ref, *rest):
+def rows_kernel(
+    top,
+    masks,
+    place_ref,
+    small_ref,
+    small_other_ref,
+    hidden_other_ref,
+    gradient_ref,
+    gradient_other_ref,
+    piece_ref,
+    same_ref,
+    mask_ref,
+    hidden_ref,
+    both_ref,
+    onward_ref,
+):
+    onward_ref[...] = piece_ref[...]
+    rows, tokens = same_ref.shape
+    wide = mask_ref.shape[2]
+    row = lax.broadcasted_iota(jnp.int32, (rows, tokens), 0)
+    same = jnp.where(row // top == lax.broadcasted_iota(jnp.int32, (rows, tokens), 1), 1.0, 0.0).astype(bf16)
+    same_ref[...] = same
+    column = members(place_ref, wide, masks)
+    for core, ref in enumerate((small_ref, small_other_ref)):
+        small = ref[...].T
+        experts = dot(same, small.astype(bf16), 1, 0)
+        position = lax.broadcasted_iota(jnp.int32, experts.shape, 0) % top
+        own = lax.broadcasted_iota(jnp.int32, experts.shape, 1) == position
+        expert = jnp.sum(jnp.where(own, experts, 0.0), axis=1, keepdims=True)
+        mask_ref[core] = jnp.where(expert == column, 1.0, 0.0).astype(bf16)
+    hidden_ref[...] = hidden_other_ref[...]
+    both_ref[:tokens] = gradient_ref[...]
+    both_ref[tokens:] = gradient_other_ref[...]
+
+
+def reduce_kernel(masks, place_ref, same_ref, mask_ref, own_ref, other_ref, *rest):
     slots = len(masks)
-    piece_refs, (_, reduced_ref, high_ref, low_ref) = rest[: slots + 1], rest[slots + 1 :]
+    piece_refs, (_, reduced_ref, high_ref, low_ref) = rest[: 2 * slots], rest[2 * slots :]
     hidden_width = own_ref.shape[1]
     for offset in range(slots):
         slot = place_ref[1 + offset]
         for kind in range(2):
-            down, _ = decode(piece_part(piece_refs, offset, kind), hidden_width)
+            down, _ = decode(piece_refs[kind * slots + offset][...], hidden_width)
             high_ref[kind, slot], low_ref[kind, slot] = halves(down)
-    experts, _, _ = token_columns(small_ref, small_other_ref, top)
     wide = reduced_ref.shape[2]
-    column = members(place_ref, wide, masks)
     high = high_ref[...].reshape(2 * wide, hidden_width)
     low = low_ref[...].reshape(2 * wide, hidden_width)
-    tokens = own_ref.shape[0] // top
-    for block, hidden_ref in enumerate((own_ref, other_ref)):
-        rows = slice(block * tokens, (block + 1) * tokens)
+    tokens = same_ref.shape[1]
+    for core, hidden_ref in enumerate((own_ref, other_ref)):
         full = dot(hidden_ref[...], high, 1, 1) + dot(hidden_ref[...], low, 1, 1)
-        total = jnp.zeros((tokens, 2 * wide), f32)
-        for k in range(top):
-            named = experts[k][rows] == column
-            total = jnp.where(jnp.concatenate([named, named], axis=1), full[k * tokens : (k + 1) * tokens], total)
-        reduced_ref[0, rows] = total[:, :wide]
-        reduced_ref[1, rows] = total[:, wide:]
+        mask = mask_ref[core].astype(f32)
+        named = halves(full * jnp.concatenate([mask, mask], axis=1))
+        total = dot(same_ref[...], named[0], 0, 0) + dot(same_ref[...], named[1], 0, 0)
+        reduced_ref[0, core * tokens : (core + 1) * tokens] = total[:, :wide]
+        reduced_ref[1, core * tokens : (core + 1) * tokens] = total[:, wide:]
 
 
 def rank_limits(place_ref, masks, wide, capacity_ref, prior_ref, arrived_ref):
@@ -151,12 +174,12 @@
     top, masks, place_ref, small_ref, small_other_ref, capacity_ref, prior_ref, arrived_ref, reduced_ref, *rest
 ):
     slots = len(masks)
-    piece_refs = rest[: slots + 1]
-    weight_ref, weighted_ref, tangent_ref, coded_ref, high_ref, low_ref = rest[slots + 1 :]
+    piece_refs = rest[: 2 * slots]
+    weight_ref, weighted_ref, tangent_ref, coded_ref, high_ref, low_ref = rest[2 * slots :]
     experts, gates, _ = token_columns(small_ref, small_other_ref, top)
     tokens, wide = weight_ref.shape
     model_width = tangent_ref.shape[1]
-    hidden_width = piece_refs[0].shape[2] - model_width - lanes
+    hidden_width = piece_refs[0].shape[1] - model_width - lanes
     block = tokens // 2
     column = members(place_ref, wide, masks)
     limits = rank_limits(place_ref, masks, wide, capacity_ref, prior_ref, arrived_ref)
@@ -183,7 +206,7 @@
     for offset in range(slots):
         slot = place_ref[1 + offset]
         for kind in range(2):
-            _, up = decode(piece_part(piece_refs, offset, kind), hidden_width)
+            _, up = decode(piece_refs[kind * slots + offset][...], hidden_width)
             high_ref[kind, slot], low_ref[kind, slot] = halves(up)
     factor = high_ref[...].reshape(2 * wide, model_width), low_ref[...].reshape(2 * wide, model_width)
     tangent = dot_pairs(halves(weighted), factor, 1, 0)
@@ -191,15 +214,13 @@
     coded_ref[...] = tangent.astype(bf16)
 
 
-def put_left(left_ref, experts, column, terms, top):
+def put_left(left_ref, same_ref, mask_ref, terms):
     both = jnp.concatenate(halves(terms), axis=1)
     tokens = terms.shape[0] // 2
-    for block in range(2):
-        rows = slice(block * tokens, (block + 1) * tokens)
-        for k in range(top):
-            named = experts[k][rows] == column
-            named = jnp.concatenate([named, named], axis=1)
-            left_ref[block, k * tokens : (k + 1) * tokens] = jnp.where(named, both[rows], jnp.zeros_like(both[rows]))
+    for core in range(2):
+        repeated = dot(same_ref[...], both[core * tokens : (core + 1) * tokens], 1, 0).astype(bf16)
+        mask = mask_ref[core]
+        left_ref[core] = repeated * jnp.concatenate([mask, mask], axis=1)
 
 
 def add_halves(both):
@@ -220,15 +241,11 @@
 
 
 def gradient_kernel(
-    top,
-    masks,
-    place_ref,
-    small_ref,
-    small_other_ref,
+    same_ref,
+    mask_ref,
     own_ref,
     other_ref,
-    own_gradient_ref,
-    other_gradient_ref,
+    gradient_ref,
     weight_ref,
     weighted_ref,
     high_ref,
@@ -240,16 +257,14 @@
     to_ref,
     left_ref,
 ):
-    experts, _, _ = token_columns(small_ref, small_other_ref, top)
     wide = weight_ref.shape[1]
     model_width = up_ref.shape[1]
-    column = members(place_ref, wide, masks)
-    gradient = jnp.concatenate([own_gradient_ref[...], other_gradient_ref[...]], axis=0)
+    gradient = gradient_ref[...]
     high = high_ref[...].reshape(2 * wide, model_width)
     low = low_ref[...].reshape(2 * wide, model_width)
     to_both = dot(gradient, high, 1, 1) + dot(gradient, low, 1, 1)
     to_ref[...] = to_both[:, wide:]
-    put_left(left_ref, experts, column, weight_ref[...] * to_both[:, :wide], top)
+    put_left(left_ref, same_ref, mask_ref, weight_ref[...] * to_both[:, :wide])
     down = dot(left_ref[0], own_ref[...], 0, 0) + dot(left_ref[1], other_ref[...], 0, 0)
     up = add_halves(dot(jnp.concatenate(halves(weighted_ref[...]), axis=1), gradient, 0, 0))
     up_ref[...] = up[:wide]
@@ -258,10 +273,10 @@
 
 def curvature_kernel(
     top,
-    masks,
-    place_ref,
     small_ref,
     small_other_ref,
+    same_ref,
+    mask_ref,
     own_ref,
     other_ref,
     weight_ref,
@@ -277,17 +292,14 @@
     far_ref,
     left_ref,
 ):
-    experts, _, curvature = token_columns(small_ref, small_other_ref, top)
+    _, _, curvature = token_columns(small_ref, small_other_ref, top)
     tokens, wide = weight_ref.shape
     block = tokens // 2
     model_width = up_ref.shape[1]
-    column = members(place_ref, wide, masks)
     arrived = jnp.concatenate([arrived_ref[block:], arrived_ref[:block]], axis=0).astype(f32)
     resid = halves(curvature * (tangent_ref[...] + arrived))
     adapter_up = high_ref[0].reshape(wide, model_width), low_ref[0].reshape(wide, model_width)
-    put_left(
-        left_ref, experts, column, weight_ref[...] * (dot_pairs(resid, adapter_up, 1, 1) + to_ref[...]), top
-    )
+    put_left(left_ref, same_ref, mask_ref, weight_ref[...] * (dot_pairs(resid, adapter_up, 1, 1) + to_ref[...]))
     down = dot(left_ref[0], own_ref[...], 0, 0) + dot(left_ref[1], other_ref[...], 0, 0)
     weighted_u = halves(weighted_ref[:, wide:])
     up = add_halves(dot(jnp.concatenate(weighted_u, axis=1), resid[0], 0, 0)) + dot(weighted_u[0], resid[1], 0, 0)
@@ -302,7 +314,9 @@
         out_ref[...] = encode(own[:, :hidden_width] + down, own[:, hidden_width:] + up)
 
 
-def near_kernel(hidden_width, gradient_ref, curvature_ref, gradient_chunk_ref, curvature_chunk_ref, out_ref, total_ref):
+def near_kernel(
+    hidden_width, gradient_ref, curvature_ref, gradient_chunk_ref, curvature_chunk_ref, _, out_ref, total_ref
+):
     pairs = ((gradient_ref, gradient_chunk_ref), (curvature_ref, curvature_chunk_ref))
     for kind, (arrived_ref, chunk_ref) in enumerate(pairs):
         for place in range(arrived_ref.shape[0]):
@@ -315,14 +329,20 @@
                 out_ref[place - 1, kind] = encode(down, up)
 
 
-def total_kernel(hidden_width, far, total_ref, *rest):
-    near_refs, far_refs, out_refs = rest[: -2 * far - 4], rest[-2 * far - 4 : -4], rest[-4:]
-    for kind in range(2):
-        down = total_ref[kind, :, :hidden_width]
-        up = total_ref[kind, :, hidden_width:]
-        arrived = [ref[kind] for ref in near_refs] + [ref[...] for ref in far_refs[kind * far : (kind + 1) * far]]
-        for coded in arrived:
-            more = decode(coded, hidden_width)
+def add_kernel(hidden_width, *refs):
+    coded_refs, total_ref = refs[:-2], refs[-1]
+    parts = [decode(ref[...], hidden_width) for ref in coded_refs]
+    total_ref[:, :hidden_width] = sum(part[0] for part in parts)
+    total_ref[:, hidden_width:] = sum(part[1] for part in parts)
+
+
+def total_kernel(hidden_width, own_ref, gradient_ref, curvature_ref, *rest):
+    near_refs, out_refs = rest[:-4], rest[-4:]
+    for kind, far_ref in enumerate((gradient_ref, curvature_ref)):
+        total = own_ref[kind] + far_ref[...]
+        down, up = total[:, :hidden_width], total[:, hidden_width:]
+        for ref in near_refs:
+            more = decode(ref[kind], hidden_width)
             down, up = down + more[0], up + more[1]
         out_refs[2 * kind][...] = down
         out_refs[2 * kind + 1][...] = up
@@ -348,16 +368,17 @@
         there = (place + jnp.arange(self.length, dtype=jnp.int32)) % self.length
         return jnp.where(there < rows, 4 * there, 4 * (self.length - 1 - there) + 2) + me % 2
 
-    def gather(self, own):
+    def gather(self, own, way, passing=lambda piece: piece):
         half = self.length // 2
         found = {0: own}
-        ahead, behind = own, own
-        for step in range(1, half):
-            behind = self.shift(behind, 1)
-            ahead = self.shift(ahead, -1)
-            found[self.length - step], found[step] = behind, ahead
-        last = [self.shift(behind[:1], 1), self.shift(ahead[1:], -1)]
-        return [found[offset] for offset in sorted(found)] + last
+        for direction in (way, -way):
+            moving = own
+            for step in range(1, half + (direction == way)):
+                moving = self.shift(moving, direction)
+                if step == 1 and direction != way:
+                    moving = passing(moving)
+                found[-direction * step % self.length] = moving
+        return [found[offset] for offset in range(self.length)]
 
 
 def exchange(value, mask):
@@ -413,10 +434,10 @@
     down_multiplies = 2 * top * both * hidden_width * wide
     up_multiplies = both * model_width * wide
 
-    piece, small = call(
+    *own_pieces, small = call(
         prepare_kernel,
         10**8,
-        [((2, rank, coded_width), i16), (((2 * top + 8) // 8 * 8, tokens), f32)],
+        [((rank, coded_width), i16)] * 2 + [(((2 * top + 8) // 8 * 8, tokens), f32)],
         expert_of_route.T,
         gate_of_route.T,
         curvature[None],
@@ -425,24 +446,46 @@
         adapter_up[0],
         up_direction[0],
     )
-    pieces = ring.gather(piece)
     small_other = exchange(small, 1)
-    hidden = hidden_of_route.transpose(1, 0, 2).reshape(top * tokens, hidden_width)
-    hidden_other = exchange(hidden, 1)
-    gradient_other = exchange(output_gradient, 1)
+    hidden = hidden_of_route.reshape(tokens * top, hidden_width)
+    beside = []
+
+    def passing(piece):
+        *made, onward = call(
+            functools.partial(rows_kernel, top, masks),
+            10**9,
+            [
+                ((tokens * top, tokens), bf16),
+                ((2, tokens * top, wide), bf16),
+                ((tokens * top, hidden_width), bf16),
+                ((both, model_width), bf16),
+                ((rank, coded_width), i16),
+            ],
+            place,
+            small,
+            small_other,
+            exchange(hidden, 1),
+            output_gradient,
+            exchange(output_gradient, 1),
+            piece,
+        )
+        beside.extend(made)
+        return onward
+
+    pieces = ring.gather(own_pieces[0], 1, passing) + ring.gather(own_pieces[1], -1)
+    same, mask, hidden_other, gradient = beside
     capacity_row = jnp.pad(capacity.astype(f32), (counts_lane, lanes - counts_lane - experts))[None, :]
 
-    by_offset = pieces[:rows] + [pieces[-2]] + pieces[rows:-2]
-    (prior,) = call(functools.partial(prior_kernel, masks), 10**8, [((8, lanes), f32)], place, *by_offset)
+    (prior,) = call(functools.partial(prior_kernel, masks), 10**8, [((8, lanes), f32)], place, *pieces[:slots])
     prior_arrived = exchange(prior, 1)
     factor_halves = [pltpu.VMEM((2, slots, rank, hidden_width), bf16)] * 2
     (reduced,) = call(
-        functools.partial(reduce_kernel, top, masks),
+        functools.partial(reduce_kernel, masks),
         2 * down_multiplies,
         [((2, both, wide), f32)],
         place,
-        small,
-        small_other,
+        same,
+        mask,
         hidden,
         hidden_other,
         *pieces,
@@ -477,16 +520,14 @@
         ((far, rank, coded_width), i16),
     ]
     gradient_own, gradient_near, gradient_far, up, to = call(
-        functools.partial(gradient_kernel, top, masks),
+        gradient_kernel,
         down_multiplies + 8 * up_multiplies,
         chunks + [((wide, model_width), f32), ((both, wide), f32)],
-        place,
-        small,
-        small_other,
+        same,
+        mask,
         hidden,
         hidden_other,
-        output_gradient,
-        gradient_other,
+        gradient,
         weight,
         weighted,
         high,
@@ -496,12 +537,13 @@
     gradient_far = exchange(gradient_far, 2)
     gradient_near = exchange(gradient_near, 2)
     curvature_own, curvature_near, curvature_far = call(
-        functools.partial(curvature_kernel, top, masks),
+        functools.partial(curvature_kernel, top),
         down_multiplies + 6 * up_multiplies,
         chunks,
-        place,
         small,
         small_other,
+        same,
+        mask,
         hidden,
         hidden_other,
         weight,
@@ -515,39 +557,53 @@
         scratch=left,
     )
 
+    hop = 2 * 10**9
+
     def along_z(arrived, own, after):
         sums = call(
             functools.partial(far_kernel, hidden_width),
-            10**8,
+            hop,
             [((rank, coded_width), i16)] * far,
             arrived,
             own,
             after=[after],
         )
-        return [exchange(part, 4 * z) for z, part in zip(range(rows - far, rows), sums)]
-
-    gradient_parts = along_z(gradient_far, gradient_own, curvature_far)
+        return sums, [exchange(part, 4 * z) for z, part in zip(range(rows - far, rows), sums)]
+
+    def added(parts, after):
+        return call(
+            functools.partial(add_kernel, hidden_width),
+            hop,
+            [((rank, hidden_width + model_width), f32)],
+            *parts,
+            after=[after],
+        )[0]
+
+    sums, gradient_parts = along_z(gradient_far, gradient_own, curvature_far)
     curvature_far = exchange(curvature_far, 2)
     curvature_near = exchange(curvature_near, 2)
-    curvature_parts = along_z(curvature_far, curvature_own, gradient_near)
+    sums, curvature_parts = along_z(curvature_far, curvature_own, sums[0])
     near, total = call(
         functools.partial(near_kernel, hidden_width),
-        10**8,
+        hop,
         [((rows - far - 1, 2, rank, coded_width), i16), ((2, rank, hidden_width + model_width), f32)],
         gradient_near,
         curvature_near,
         gradient_own,
         curvature_own,
+        after=[sums[0]],
     )
     near_parts = [exchange(near[z - 1], 4 * z) for z in range(1, rows - far)]
+    gradient_total = added(gradient_parts, near)
+    curvature_total = added(curvature_parts, gradient_total)
     down_gradient, up_gradient, curvature_down, curvature_up = call(
-        functools.partial(total_kernel, hidden_width, far),
-        10**8,
+        functools.partial(total_kernel, hidden_width),
+        hop,
         [((rank, hidden_width), f32), ((rank, model_width), f32)] * 2,
         total,
+        gradient_total,
+        curvature_total,
         *near_parts,
-        *gradient_parts,
-        *curvature_parts,
     )
     return down_gradient.T[None], up_gradient[None], curvature_down.T[None], curvature_up[None]
 

time: 86.1 us -> 84.8 us (0.985)
  waiting for transfers between devices: 39 us -> 26.2 us
  starting transfers between devices: 22.9 us -> 30.5 us
  local copies, waits for them, and re-layouts: 3 us -> 6.63 us
    ppermute x8 -> x14, waiting for transfers between devices: 17.6 us -> 9.27 us  [shift(): return lax.ppermute(value, 'expert', pairs)]
    ppermute x8 -> x14, starting transfers between devices: 9.03 us -> 16.8 us  [shift(): return lax.ppermute(value, 'expert', pairs)]
    unnamed x18 -> x20, local copies, waits for them, and re-layouts: 0.04 us -> 6.56 us
    ppermute x14, waiting for transfers between devices: 21.4 us -> 17 us  [exchange(): lax.ppermute(value, 'expert', [(device, device ^ mask) for device in rang...]
    transpose x1 -> x0, local copies, waits for them, and re-layouts: 2.87 us -> none  [gathered_plan(): hidden_of_route.transpose(1, 0, 2).reshape(top * tokens, hidden_width)]
    pallas_call x10 -> x13, Pallas kernels: 20 us -> 20.1 us  [call(): pl.pallas_call(kernel, out_shape=[jax.ShapeDtypeStruct(shape, dtype) for...]
  transfers between devices with their start and end apart: 22 -> 28, of which waited for: 10 -> 10; matrix products, arithmetic and copies ran while one was open for 0% -> 0% of each run, Pallas kernels for 19% -> 19%
where the time goes in v8:
time: 84.8 us; the launch traced here: 84.4 us
  starting transfers between devices  30.5 us (36%)
  waiting for transfers between devices  26.2 us (31%)
  Pallas kernels  20.1 us (24%)
  local copies, waits for them, and re-layouts  6.63 us (8%)
    pallas_call x13, Pallas kernels, call(): pl.pallas_call(kernel, out_shape=[jax.ShapeDtypeStruct(shape, dtype) for...  20.1 us
    ppermute x14, waiting for transfers between devices, exchange(): lax.ppermute(value, 'expert', [(device, device ^ mask) for device in rang...  17 us
    ppermute x14, starting transfers between devices, shift(): return lax.ppermute(value, 'expert', pairs)  16.8 us
    ppermute x14, starting transfers between devices, exchange(): lax.ppermute(value, 'expert', [(device, device ^ mask) for device in rang...  13.8 us
    ppermute x14, waiting for transfers between devices, shift(): return lax.ppermute(value, 'expert', pairs)  9.27 us
    unnamed x20, local copies, waits for them, and re-layouts  6.56 us
  transfers between devices with their start and end apart: 28, of which 10 were waited for; matrix products, arithmetic and copies ran while one was open for 0% of the time, Pallas kernels for 19%

profile of v8, /device:TPU:0, one launch (start us, length us, event | category | flops | bytes accessed | tf_op | source)
XLA Modules:
  0.0 84.4 jit_solution(9666145509239625009)
XLA Ops:
  7.4 2.7 %collective-permute-start.15 = (s16[16,3200]{1,0:T(8,128)(2,1)S(1)}, s16[16,3200]{1,0:T(8,128)(2,1)S(1)}, u32[]{:S(2)}, u32[]{:S(2)}) collective-permute-start(s16[16,3200]{1,0:T(8,128)(2,1)S(1)} %get-tuple-element.43.rest_8_), channel_id=1, source_target_pairs={{0,4},{1,5},{4,8},{5,9},{8,12},{9,13},{12,14},{13,15},{14,10},{15,... | collective-permute-start | bytes 307208 | tf_op jit(solution)/shard_map/ppermute | solution.py:363
  10.1 2.0 %collective-permute-start.6 = (s16[16,3200]{1,0:T(8,128)(2,1)S(1)}, s16[16,3200]{1,0:T(8,128)(2,1)S(1)}, u32[]{:S(2)}, u32[]{:S(2)}) collective-permute-start(s16[16,3200]{1,0:T(8,128)(2,1)S(1)} %get-tuple-element.37.rest_0_), channel_id=1, source_target_pairs={{0,4},{1,5},{4,8},{5,9},{8,12},{9,13},{12,14},{13,15},{14,10},{15,... | collective-permute-start | bytes 307208 | tf_op jit(solution)/shard_map/ppermute | solution.py:363
  12.2 1.6 %collective-permute-done.15.rest_15_ = s16[16,3200]{1,0:T(8,128)(2,1)S(1)} collective-permute-done((s16[16,3200]{1,0:T(8,128)(2,1)S(1)}, s16[16,3200]{1,0:T(8,128)(2,1)S(1)}, u32[]{:S(2)}, u32[]{:S(2)}) %collective-permute-start.15) | collective-permute-done | bytes 102432 | tf_op jit(solution)/shard_map/ppermute | solution.py:363
  13.7 1.9 %collective-permute-start.3 = (s16[16,3200]{1,0:T(8,128)(2,1)S(1)}, s16[16,3200]{1,0:T(8,128)(2,1)S(1)}, u32[]{:S(2)}, u32[]{:S(2)}) collective-permute-start(s16[16,3200]{1,0:T(8,128)(2,1)S(1)} %get-tuple-element.37.rest_0_), channel_id=1, source_target_pairs={{0,2},{1,3},{4,0},{5,1},{8,4},{9,5},{12,8},{13,9},{14,12},{15,13},... | collective-permute-start | bytes 307208 | tf_op jit(solution)/shard_map/ppermute | solution.py:363
  15.7 1.6 %collective-permute-start.12 = (s16[16,3200]{1,0:T(8,128)(2,1)S(1)}, s16[16,3200]{1,0:T(8,128)(2,1)S(1)}, u32[]{:S(2)}, u32[]{:S(2)}) collective-permute-start(s16[16,3200]{1,0:T(8,128)(2,1)S(1)} %collective-permute-done.11.rest_9_), channel_id=1, source_target_pairs={{0,2},{1,3},{4,0},{5,1},{8,4},{9,5},{12,8},{13,9},{14,12},{15,13},... | collective-permute-start | bytes 307208 | tf_op jit(solution)/shard_map/ppermute | solution.py:363
  17.8 1.6 %collective-permute-done.3.piece_ref = s16[16,3200]{1,0:T(8,128)(2,1)S(1)} collective-permute-done((s16[16,3200]{1,0:T(8,128)(2,1)S(1)}, s16[16,3200]{1,0:T(8,128)(2,1)S(1)}, u32[]{:S(2)}, u32[]{:S(2)}) %collective-permute-start.3) | collective-permute-done | bytes 102432 | tf_op jit(solution)/shard_map/ppermute | solution.py:363
  19.4 1.5 %collective-permute-start.16 = (s16[16,3200]{1,0:T(8,128)(2,1)S(1)}, s16[16,3200]{1,0:T(8,128)(2,1)S(1)}, u32[]{:S(2)}, u32[]{:S(2)}) collective-permute-start(s16[16,3200]{1,0:T(8,128)(2,1)S(1)} %collective-permute-done.15.rest_15_), channel_id=1, source_target_pairs={{0,4},{1,5},{4,8},{5,9},{8,12},{9,13},{12,14},{13,15},{14,10},{15,... | collective-permute-start | bytes 307208 | tf_op jit(solution)/shard_map/ppermute | solution.py:363
  26.5 1.3 %collective-permute-start.17 = (s16[16,3200]{1,0:T(8,128)(2,1)S(1)}, s16[16,3200]{1,0:T(8,128)(2,1)S(1)}, u32[]{:S(2)}, u32[]{:S(2)}) collective-permute-start(s16[16,3200]{1,0:T(8,128)(2,1)S(1)} %collective-permute-done.16.rest_14_), channel_id=1, source_target_pairs={{0,4},{1,5},{4,8},{5,9},{8,12},{9,13},{12,14},{13,15},{14,10},{15,... | collective-permute-start | bytes 307208 | tf_op jit(solution)/shard_map/ppermute | solution.py:363
  28.6 1.3 %collective-permute-start.9 = (s16[16,3200]{1,0:T(8,128)(2,1)S(1)}, s16[16,3200]{1,0:T(8,128)(2,1)S(1)}, u32[]{:S(2)}, u32[]{:S(2)}) collective-permute-start(s16[16,3200]{1,0:T(8,128)(2,1)S(1)} %collective-permute-done.8.rest_5_), channel_id=1, source_target_pairs={{0,4},{1,5},{4,8},{5,9},{8,12},{9,13},{12,14},{13,15},{14,10},{15,... | collective-permute-start | bytes 307208 | tf_op jit(solution)/shard_map/ppermute | solution.py:363
  29.9 1.5 %collective-permute-done.4.rest_2_ = s16[16,3200]{1,0:T(8,128)(2,1)S(1)} collective-permute-done((s16[16,3200]{1,0:T(8,128)(2,1)S(1)}, s16[16,3200]{1,0:T(8,128)(2,1)S(1)}, u32[]{:S(2)}, u32[]{:S(2)}) %collective-permute-start.4) | collective-permute-done | bytes 102432 | tf_op jit(solution)/shard_map/ppermute | solution.py:363
  31.4 1.8 %collective-permute-done.9.rest_4_ = s16[16,3200]{1,0:T(8,128)(2,1)S(1)} collective-permute-done((s16[16,3200]{1,0:T(8,128)(2,1)S(1)}, s16[16,3200]{1,0:T(8,128)(2,1)S(1)}, u32[]{:S(2)}, u32[]{:S(2)}) %collective-permute-start.9) | collective-permute-done | bytes 102432 | tf_op jit(solution)/shard_map/ppermute | solution.py:363
  33.3 2.8 %collective-permute-done.5.rest_3_ = s16[16,3200]{1,0:T(8,128)(2,1)S(1)} collective-permute-done((s16[16,3200]{1,0:T(8,128)(2,1)S(1)}, s16[16,3200]{1,0:T(8,128)(2,1)S(1)}, u32[]{:S(2)}, u32[]{:S(2)}) %collective-permute-start.5) | collective-permute-done | bytes 102432 | tf_op jit(solution)/shard_map/ppermute | solution.py:363
  36.7 6.0 %shard_map.132.reduced_ref = f32[2,256,128]{2,1,0:T(8,128)S(1)} custom-call(s32[17]{0:T(128)S(1)} %pad_add_fusion.place_ref, bf16[1024,128]{1,0:T(8,128)(2,1)S(1)} %get-tuple-element.38.same_ref, bf16[2,1024,128]{2,1,0:T(8,128)(2,1)S(1)} %get-tuple-element.39.mask_ref, bf16[1024,1024]{1,0:T(8,128)(2,1)S(1)} %bitcast.25, ...), custom_call_target="tpu_custom_call" | custom-call | flops 2147483648 | bytes 1048576 | tf_op jit(solution)/shard_map/pallas_call | solution.py:425
  42.7 2.9 %shard_map.133 = (f32[256,128]{1,0:T(8,128)S(1)}, f32[256,256]{1,0:T(8,128)S(1)}, f32[256,2048]{1,0:T(8,128)S(1)}, bf16[256,2048]{1,0:T(8,128)(2,1)S(1)}, bf16[2...) custom-call(s32[17]{0:T(128)S(1)} %pad_add_fusion.place_ref, ...), custom_call_target="tpu_custom_call" | custom-call | flops 805306368 | bytes 1048576 | tf_op jit(solution)/shard_map/pallas_call | solution.py:425
  46.2 4.0 %shard_map.134 = (f32[4,16,3072]{2,1,0:T(8,128)S(1)}, s16[2,16,3200]{2,1,0:T(8,128)(2,1)S(1)}, s16[2,16,3200]{2,1,0:T(8,128)(2,1)S(1)}, f32[128,2048]{1,0:T(8,128)S(1)}, f32[256,128]{1,0:T(8,128)S(1)}) custom-call(bf16[1024,128]{1,0:T(8,128)(2,1)S(1)} %get-tuple-element.38.same_ref, bf16[2,1024,128]{2,1,0:T(8,128)(2,1)S(1)} %get-tuple-element.39.mask_ref, ...), custom_call_target="tpu_custom_call" | custom-call | flops 2147483648 | bytes 1048576 | tf_op jit(solution)/shard_map/pallas_call | solution.py:425
  50.3 2.0 %collective-permute-start.18 = (s16[2,16,3200]{2,1,0:T(8,128)(2,1)S(1)}, s16[2,16,3200]{2,1,0:T(8,128)(2,1)S(1)}, u32[]{:S(2)}, u32[]{:S(2)}) collective-permute-start(s16[2,16,3200]{2,1,0:T(8,128)(2,1)S(1)} %get-tuple-element.48), channel_id=1, source_target_pairs={{0,2},{1,3},{2,0},{3,1},{4,6},{5,7},{6,4},{7,5},{8,10},{9,11},{10,... | collective-permute-start | bytes 614408 | tf_op jit(solution)/shard_map/ppermute | solution.py:386
  52.3 3.4 %shard_map.135 = (f32[4,16,3072]{2,1,0:T(8,128)S(1)}, s16[2,16,3200]{2,1,0:T(8,128)(2,1)S(1)}, s16[2,16,3200]{2,1,0:T(8,128)(2,1)S(1)}) custom-call(f32[24,128]{1,0:T(8,128)S(1)} %get-tuple-element.36.small_ref, f32[24,128]{1,0:T(8,128)S(1)} %collective-permute-done.small_other_ref, bf16[1024,128]{1,0:T(8,128)(2,1)S(1)} %get-tuple-element.38.same_ref, ...), custom_call_target="tpu_custom_call" | custom-call | flops 1879048192 | bytes 1048576 | tf_op jit(solution)/shard_map/pallas_call | solution.py:425
  55.8 1.9 %collective-permute-start.21 = (s16[2,16,3200]{2,1,0:T(8,128)(2,1)S(1)}, s16[2,16,3200]{2,1,0:T(8,128)(2,1)S(1)}, u32[]{:S(2)}, u32[]{:S(2)}) collective-permute-start(s16[2,16,3200]{2,1,0:T(8,128)(2,1)S(1)} %get-tuple-element.56._), channel_id=1, source_target_pairs={{0,2},{1,3},{2,0},{3,1},{4,6},{5,7},{6,4},{7,5},{8,10},{9,11},{10,... | collective-permute-start | bytes 614408 | tf_op jit(solution)/shard_map/ppermute | solution.py:386
  58.4 3.4 %collective-permute-start.24 = (s16[16,3200]{1,0:T(8,128)(2,1)S(1)}, s16[16,3200]{1,0:T(8,128)(2,1)S(1)}, u32[]{:S(2)}, u32[]{:S(2)}) collective-permute-start(s16[16,3200]{1,0:T(8,128)(2,1)S(1)} %get-tuple-element.61), channel_id=1, source_target_pairs={{0,12},{1,13},{2,14},{3,15},{4,8},{5,9},{6,10},{7,11},{8,4},{9,5},... | collective-permute-start | bytes 307208 | tf_op jit(solution)/shard_map/ppermute | solution.py:386
  61.8 8.6 %collective-permute-done.21.arrived_ref = s16[2,16,3200]{2,1,0:T(8,128)(2,1)S(1)} collective-permute-done((s16[2,16,3200]{2,1,0:T(8,128)(2,1)S(1)}, s16[2,16,3200]{2,1,0:T(8,128)(2,1)S(1)}, u32[]{:S(2)}, u32[]{:S(2)}) %collective-permute-start.21) | collective-permute-done | bytes 204832 | tf_op jit(solution)/shard_map/ppermute | solution.py:386
  70.7 3.4 %collective-permute-start.26 = (s16[16,3200]{1,0:T(8,128)(2,1)S(1)}, s16[16,3200]{1,0:T(8,128)(2,1)S(1)}, u32[]{:S(2)}, u32[]{:S(2)}) collective-permute-start(s16[16,3200]{1,0:T(8,128)(2,1)S(1)} %get-tuple-element.63), channel_id=1, source_target_pairs={{0,12},{1,13},{2,14},{3,15},{4,8},{5,9},{6,10},{7,11},{8,4},{9,5},... | collective-permute-start | bytes 307208 | tf_op jit(solution)/shard_map/ppermute | solution.py:386
  75.6 2.3 %collective-permute-done.26.refs_1_ = s16[16,3200]{1,0:T(8,128)(2,1)S(1)} collective-permute-done((s16[16,3200]{1,0:T(8,128)(2,1)S(1)}, s16[16,3200]{1,0:T(8,128)(2,1)S(1)}, u32[]{:S(2)}, u32[]{:S(2)}) %collective-permute-start.26) | collective-permute-done | bytes 102432 | tf_op jit(solution)/shard_map/ppermute | solution.py:386
  77.9 4.2 %collective-permute-done.25.refs_0_ = s16[16,3200]{1,0:T(8,128)(2,1)S(1)} collective-permute-done((s16[16,3200]{1,0:T(8,128)(2,1)S(1)}, s16[16,3200]{1,0:T(8,128)(2,1)S(1)}, u32[]{:S(2)}, u32[]{:S(2)}) %collective-permute-start.25) | collective-permute-done | bytes 102432 | tf_op jit(solution)/shard_map/ppermute | solution.py:386
  82.2 1.4 %collective-permute-done.27.rest_0_ = s16[2,16,3200]{2,1,0:T(8,128)(2,1)S(1)} collective-permute-done((s16[2,16,3200]{2,1,0:T(8,128)(2,1)S(1)}, s16[2,16,3200]{2,1,0:T(8,128)(2,1)S(1)}, u32[]{:S(2)}, u32[]{:S(2)}) %collective-permute-start.27) | collective-permute-done | bytes 204832 | tf_op jit(solution)/shard_map/ppermute | solution.py:386
  (69 shorter events, 18.6 us)
Async XLA Ops:
  0.6 22.7 %collective-permute-start.1 = (bf16[1024,1024]{1,0:T(8,128)(2,1)}, bf16[1024,1024]{1,0:T(8,128)(2,1)S(1)}, u32[]{:S(2)}, u32[]{:S(2)}) collective-permute-start(bf16[1024,1024]{1,0:T(8,128)(2,1)} %bitcast.24), channel_id=1, source_target_pairs={{0,1},{1,0},{2,3},{3,2},{4,5},{5,4},{6,7},{7,6},{8,9},{9,8},{10,11... | collective-permute-start | bytes 6291464 | tf_op jit(solution)/shard_map/ppermute | solution.py:386
  1.2 22.2 %collective-permute-start.2 = (bf16[128,2048]{1,0:T(8,128)(2,1)}, bf16[128,2048]{1,0:T(8,128)(2,1)S(1)}, u32[]{:S(2)}, u32[]{:S(2)}) collective-permute-start(bf16[128,2048]{1,0:T(8,128)(2,1)} %gradient_ref.1), channel_id=1, source_target_pairs={{0,1},{1,0},{2,3},{3,2},{4,5},{5,4},{6,7},{7,6},{8,9},{9,8},{10,11... | collective-permute-start | bytes 1572872 | tf_op jit(solution)/shard_map/ppermute | solution.py:386
  7.4 6.3 %collective-permute-start.15 = (s16[16,3200]{1,0:T(8,128)(2,1)S(1)}, s16[16,3200]{1,0:T(8,128)(2,1)S(1)}, u32[]{:S(2)}, u32[]{:S(2)}) collective-permute-start(s16[16,3200]{1,0:T(8,128)(2,1)S(1)} %get-tuple-element.43.rest_8_), channel_id=1, source_target_pairs={{0,4},{1,5},{4,8},{5,9},{8,12},{9,13},{12,14},{13,15},{14,10},{15,... | collective-permute-start | bytes 307208 | tf_op jit(solution)/shard_map/ppermute | solution.py:363
  10.1 5.6 %collective-permute-start.11 = (s16[16,3200]{1,0:T(8,128)(2,1)S(1)}, s16[16,3200]{1,0:T(8,128)(2,1)S(1)}, u32[]{:S(2)}, u32[]{:S(2)}) collective-permute-start(s16[16,3200]{1,0:T(8,128)(2,1)S(1)} %get-tuple-element.43.rest_8_), channel_id=1, source_target_pairs={{0,2},{1,3},{4,0},{5,1},{8,4},{9,5},{12,8},{13,9},{14,12},{15,13},... | collective-permute-start | bytes 307208 | tf_op jit(solution)/shard_map/ppermute | solution.py:363
  10.1 7.2 %collective-permute-start.6 = (s16[16,3200]{1,0:T(8,128)(2,1)S(1)}, s16[16,3200]{1,0:T(8,128)(2,1)S(1)}, u32[]{:S(2)}, u32[]{:S(2)}) collective-permute-start(s16[16,3200]{1,0:T(8,128)(2,1)S(1)} %get-tuple-element.37.rest_0_), channel_id=1, source_target_pairs={{0,4},{1,5},{4,8},{5,9},{8,12},{9,13},{12,14},{13,15},{14,10},{15,... | collective-permute-start | bytes 307208 | tf_op jit(solution)/shard_map/ppermute | solution.py:363
  13.7 5.7 %collective-permute-start.3 = (s16[16,3200]{1,0:T(8,128)(2,1)S(1)}, s16[16,3200]{1,0:T(8,128)(2,1)S(1)}, u32[]{:S(2)}, u32[]{:S(2)}) collective-permute-start(s16[16,3200]{1,0:T(8,128)(2,1)S(1)} %get-tuple-element.37.rest_0_), channel_id=1, source_target_pairs={{0,2},{1,3},{4,0},{5,1},{8,4},{9,5},{12,8},{13,9},{14,12},{15,13},... | collective-permute-start | bytes 307208 | tf_op jit(solution)/shard_map/ppermute | solution.py:363
  15.7 5.2 %collective-permute-start.12 = (s16[16,3200]{1,0:T(8,128)(2,1)S(1)}, s16[16,3200]{1,0:T(8,128)(2,1)S(1)}, u32[]{:S(2)}, u32[]{:S(2)}) collective-permute-start(s16[16,3200]{1,0:T(8,128)(2,1)S(1)} %collective-permute-done.11.rest_9_), channel_id=1, source_target_pairs={{0,2},{1,3},{4,0},{5,1},{8,4},{9,5},{12,8},{13,9},{14,12},{15,13},... | collective-permute-start | bytes 307208 | tf_op jit(solution)/shard_map/ppermute | solution.py:363
  19.4 7.1 %collective-permute-start.16 = (s16[16,3200]{1,0:T(8,128)(2,1)S(1)}, s16[16,3200]{1,0:T(8,128)(2,1)S(1)}, u32[]{:S(2)}, u32[]{:S(2)}) collective-permute-start(s16[16,3200]{1,0:T(8,128)(2,1)S(1)} %collective-permute-done.15.rest_15_), channel_id=1, source_target_pairs={{0,4},{1,5},{4,8},{5,9},{8,12},{9,13},{12,14},{13,15},{14,10},{15,... | collective-permute-start | bytes 307208 | tf_op jit(solution)/shard_map/ppermute | solution.py:363
  20.9 7.0 %collective-permute-start.13 = (s16[16,3200]{1,0:T(8,128)(2,1)S(1)}, s16[16,3200]{1,0:T(8,128)(2,1)S(1)}, u32[]{:S(2)}, u32[]{:S(2)}) collective-permute-start(s16[16,3200]{1,0:T(8,128)(2,1)S(1)} %collective-permute-done.12.rest_10_), channel_id=1, source_target_pairs={{0,2},{1,3},{4,0},{5,1},{8,4},{9,5},{12,8},{13,9},{14,12},{15,13},... | collective-permute-start | bytes 307208 | tf_op jit(solution)/shard_map/ppermute | solution.py:363
  22.1 6.5 %collective-permute-start.8 = (s16[16,3200]{1,0:T(8,128)(2,1)S(1)}, s16[16,3200]{1,0:T(8,128)(2,1)S(1)}, u32[]{:S(2)}, u32[]{:S(2)}) collective-permute-start(s16[16,3200]{1,0:T(8,128)(2,1)S(1)} %collective-permute-done.7.rest_6_), channel_id=1, source_target_pairs={{0,4},{1,5},{4,8},{5,9},{8,12},{9,13},{12,14},{13,15},{14,10},{15,... | collective-permute-start | bytes 307208 | tf_op jit(solution)/shard_map/ppermute | solution.py:363
  25.7 5.7 %collective-permute-start.4 = (s16[16,3200]{1,0:T(8,128)(2,1)S(1)}, s16[16,3200]{1,0:T(8,128)(2,1)S(1)}, u32[]{:S(2)}, u32[]{:S(2)}) collective-permute-start(s16[16,3200]{1,0:T(8,128)(2,1)S(1)} %get-tuple-element.42.rest_1_), channel_id=1, source_target_pairs={{0,2},{1,3},{4,0},{5,1},{8,4},{9,5},{12,8},{13,9},{14,12},{15,13},... | collective-permute-start | bytes 307208 | tf_op jit(solution)/shard_map/ppermute | solution.py:363
  26.5 10.2 %collective-permute-start.17 = (s16[16,3200]{1,0:T(8,128)(2,1)S(1)}, s16[16,3200]{1,0:T(8,128)(2,1)S(1)}, u32[]{:S(2)}, u32[]{:S(2)}) collective-permute-start(s16[16,3200]{1,0:T(8,128)(2,1)S(1)} %collective-permute-done.16.rest_14_), channel_id=1, source_target_pairs={{0,4},{1,5},{4,8},{5,9},{8,12},{9,13},{12,14},{13,15},{14,10},{15,... | collective-permute-start | bytes 307208 | tf_op jit(solution)/shard_map/ppermute | solution.py:363
  27.8 8.8 %collective-permute-start.14 = (s16[16,3200]{1,0:T(8,128)(2,1)S(1)}, s16[16,3200]{1,0:T(8,128)(2,1)S(1)}, u32[]{:S(2)}, u32[]{:S(2)}) collective-permute-start(s16[16,3200]{1,0:T(8,128)(2,1)S(1)} %collective-permute-done.13.rest_11_), channel_id=1, source_target_pairs={{0,2},{1,3},{4,0},{5,1},{8,4},{9,5},{12,8},{13,9},{14,12},{15,13},... | collective-permute-start | bytes 307208 | tf_op jit(solution)/shard_map/ppermute | solution.py:363
  36.6 6.1 %collective-permute-start.10 = (f32[8,128]{1,0:T(8,128)S(1)}, f32[8,128]{1,0:T(8,128)S(1)}, u32[]{:S(2)}, u32[]{:S(2)}) collective-permute-start(f32[8,128]{1,0:T(8,128)S(1)} %shard_map.131.rest_16_.prior_ref), channel_id=1, source_target_pairs={{0,1},{1,0},{2,3},{3,2},{4,5},{5,4},{6,7},{7,6},{8,9},{9,8},{10,11... | collective-permute-start | bytes 12296 | tf_op jit(solution)/shard_map/ppermute | solution.py:386
  45.6 6.7 %collective-permute-start.19 = (bf16[256,2048]{1,0:T(8,128)(2,1)S(1)}, bf16[256,2048]{1,0:T(8,128)(2,1)S(1)}, u32[]{:S(2)}, u32[]{:S(2)}) collective-permute-start(bf16[256,2048]{1,0:T(8,128)(2,1)S(1)} %get-tuple-element.52), channel_id=1, source_target_pairs={{0,1},{1,0},{2,3},{3,2},{4,5},{5,4},{6,7},{7,6},{8,9},{9,8},{10,11... | collective-permute-start | bytes 3145736 | tf_op jit(solution)/shard_map/ppermute | solution.py:386
  50.2 8.0 %collective-permute-start.22 = (s16[2,16,3200]{2,1,0:T(8,128)(2,1)S(1)}, s16[2,16,3200]{2,1,0:T(8,128)(2,1)S(1)}, u32[]{:S(2)}, u32[]{:S(2)}) collective-permute-start(s16[2,16,3200]{2,1,0:T(8,128)(2,1)S(1)} %get-tuple-element.57), channel_id=1, source_target_pairs={{0,2},{1,3},{2,0},{3,1},{4,6},{5,7},{6,4},{7,5},{8,10},{9,11},{10,... | collective-permute-start | bytes 614408 | tf_op jit(solution)/shard_map/ppermute | solution.py:386
  50.3 23.8 %collective-permute-start.18 = (s16[2,16,3200]{2,1,0:T(8,128)(2,1)S(1)}, s16[2,16,3200]{2,1,0:T(8,128)(2,1)S(1)}, u32[]{:S(2)}, u32[]{:S(2)}) collective-permute-start(s16[2,16,3200]{2,1,0:T(8,128)(2,1)S(1)} %get-tuple-element.48), channel_id=1, source_target_pairs={{0,2},{1,3},{2,0},{3,1},{4,6},{5,7},{6,4},{7,5},{8,10},{9,11},{10,... | collective-permute-start | bytes 614408 | tf_op jit(solution)/shard_map/ppermute | solution.py:386
  55.7 18.4 %collective-permute-start.20 = (s16[2,16,3200]{2,1,0:T(8,128)(2,1)S(1)}, s16[2,16,3200]{2,1,0:T(8,128)(2,1)S(1)}, u32[]{:S(2)}, u32[]{:S(2)}) collective-permute-start(s16[2,16,3200]{2,1,0:T(8,128)(2,1)S(1)} %get-tuple-element.53), channel_id=1, source_target_pairs={{0,2},{1,3},{2,0},{3,1},{4,6},{5,7},{6,4},{7,5},{8,10},{9,11},{10,... | collective-permute-start | bytes 614408 | tf_op jit(solution)/shard_map/ppermute | solution.py:386
  55.8 14.6 %collective-permute-start.21 = (s16[2,16,3200]{2,1,0:T(8,128)(2,1)S(1)}, s16[2,16,3200]{2,1,0:T(8,128)(2,1)S(1)}, u32[]{:S(2)}, u32[]{:S(2)}) collective-permute-start(s16[2,16,3200]{2,1,0:T(8,128)(2,1)S(1)} %get-tuple-element.56._), channel_id=1, source_target_pairs={{0,2},{1,3},{2,0},{3,1},{4,6},{5,7},{6,4},{7,5},{8,10},{9,11},{10,... | collective-permute-start | bytes 614408 | tf_op jit(solution)/shard_map/ppermute | solution.py:386
  58.4 17.0 %collective-permute-start.24 = (s16[16,3200]{1,0:T(8,128)(2,1)S(1)}, s16[16,3200]{1,0:T(8,128)(2,1)S(1)}, u32[]{:S(2)}, u32[]{:S(2)}) collective-permute-start(s16[16,3200]{1,0:T(8,128)(2,1)S(1)} %get-tuple-element.61), channel_id=1, source_target_pairs={{0,12},{1,13},{2,14},{3,15},{4,8},{5,9},{6,10},{7,11},{8,4},{9,5},... | collective-permute-start | bytes 307208 | tf_op jit(solution)/shard_map/ppermute | solution.py:386
  61.8 13.7 %collective-permute-start.23 = (s16[16,3200]{1,0:T(8,128)(2,1)S(1)}, s16[16,3200]{1,0:T(8,128)(2,1)S(1)}, u32[]{:S(2)}, u32[]{:S(2)}) collective-permute-start(s16[16,3200]{1,0:T(8,128)(2,1)S(1)} %get-tuple-element.58._), channel_id=1, source_target_pairs={{0,8},{1,9},{2,10},{3,11},{4,12},{5,13},{6,14},{7,15},{8,0},{9,1},... | collective-permute-start | bytes 307208 | tf_op jit(solution)/shard_map/ppermute | solution.py:386
  70.7 7.2 %collective-permute-start.26 = (s16[16,3200]{1,0:T(8,128)(2,1)S(1)}, s16[16,3200]{1,0:T(8,128)(2,1)S(1)}, u32[]{:S(2)}, u32[]{:S(2)}) collective-permute-start(s16[16,3200]{1,0:T(8,128)(2,1)S(1)} %get-tuple-element.63), channel_id=1, source_target_pairs={{0,12},{1,13},{2,14},{3,15},{4,8},{5,9},{6,10},{7,11},{8,4},{9,5},... | collective-permute-start | bytes 307208 | tf_op jit(solution)/shard_map/ppermute | solution.py:386
  74.1 8.1 %collective-permute-start.25 = (s16[16,3200]{1,0:T(8,128)(2,1)S(1)}, s16[16,3200]{1,0:T(8,128)(2,1)S(1)}, u32[]{:S(2)}, u32[]{:S(2)}) collective-permute-start(s16[16,3200]{1,0:T(8,128)(2,1)S(1)} %get-tuple-element.59._), channel_id=1, source_target_pairs={{0,8},{1,9},{2,10},{3,11},{4,12},{5,13},{6,14},{7,15},{8,0},{9,1},... | collective-permute-start | bytes 307208 | tf_op jit(solution)/shard_map/ppermute | solution.py:386
  74.3 9.2 %collective-permute-start.27 = (s16[2,16,3200]{2,1,0:T(8,128)(2,1)S(1)}, s16[2,16,3200]{2,1,0:T(8,128)(2,1)S(1)}, u32[]{:S(2)}, u32[]{:S(2)}) collective-permute-start(s16[2,16,3200]{2,1,0:T(8,128)(2,1)S(1)} %bitcast.28), channel_id=1, source_target_pairs={{0,4},{1,5},{2,6},{3,7},{4,0},{5,1},{6,2},{7,3},{8,12},{9,13},{10,... | collective-permute-start | bytes 614408 | tf_op jit(solution)/shard_map/ppermute | solution.py:386
  (14 other events, 51.5 us)

commit v9 on v8

--- a/solution.py
+++ b/solution.py
@@ -14,6 +14,7 @@
 lanes = 128
 counts_lane = 64
 kernel_vmem = 32 * 2**20
+whole_vmem = 60 * 2**20
 
 
 def halves(value):
@@ -52,21 +53,27 @@
     return value[..., :hidden_width] * down_scale, value[..., hidden_width:width] * up_scale
 
 
-def prepare_kernel(expert_ref, gate_ref, curvature_ref, *rest):
-    (down_direction_ref, adapter_down_ref, adapter_up_ref, up_direction_ref, *piece_refs, small_ref) = rest
-    top = expert_ref.shape[0]
+def prepare_kernel(*refs):
+    (piece_ref, small_ref), sem, refs = refs[7:9], refs[-1], refs[:7] + refs[9:-1]
+    copies = [pltpu.make_async_copy(refs[i], refs[7 + i], sem.at[i]) for i in range(7)]
+    for copy in copies:
+        copy.start()
+    for copy in copies:
+        copy.wait()
+    expert, gate, curvature, down_direction, adapter_down, adapter_up, up_direction = [ref[...] for ref in refs[7:]]
+    top = expert.shape[0]
     small_ref[...] = jnp.zeros_like(small_ref)
-    small_ref[:top] = expert_ref[...].astype(f32)
-    small_ref[top : 2 * top] = gate_ref[...].astype(f32)
-    small_ref[2 * top : 2 * top + 1] = curvature_ref[...]
+    small_ref[:top] = expert.astype(f32)
+    small_ref[top : 2 * top] = gate.astype(f32)
+    small_ref[2 * top : 2 * top + 1] = curvature
     lane = lax.broadcasted_iota(jnp.int32, (1, lanes), 1)
     counts = jnp.zeros((1, lanes), f32)
-    for expert in range(lanes - counts_lane):
-        named = jnp.where(expert_ref[...] == expert, 1.0, 0.0)
+    for number in range(lanes - counts_lane):
+        named = jnp.where(expert == number, 1.0, 0.0)
         total = jnp.sum(jnp.sum(named, axis=0, keepdims=True), axis=1, keepdims=True)
-        counts = jnp.where(lane == counts_lane + expert, total, counts)
-    piece_refs[0][...] = encode(down_direction_ref[...], adapter_up_ref[...], counts)
-    piece_refs[1][...] = encode(adapter_down_ref[...], up_direction_ref[...], counts)
+        counts = jnp.where(lane == counts_lane + number, total, counts)
+    piece_ref[0] = encode(down_direction, adapter_up, counts)
+    piece_ref[1] = encode(adapter_down, up_direction, counts)
 
 
 def token_columns(own_ref, other_ref, top):
@@ -93,35 +100,42 @@
         total = jnp.zeros((1, lanes), f32)
         for offset in range(slots):
             device = place_ref[1 + slots + offset]
-            tail = piece_refs[offset][:, piece_refs[offset].shape[1] - lanes :]
+            tail = piece_refs[offset][0, :, piece_refs[offset].shape[2] - lanes :]
             counts = tail.astype(jnp.int32).astype(f32)[0:1]
             total = total + jnp.where(device < number, counts, 0.0)
         prior_ref[block : block + 1] = total
 
 
-def rows_kernel(
-    top,
-    masks,
-    place_ref,
-    small_ref,
-    small_other_ref,
-    hidden_other_ref,
-    gradient_ref,
-    gradient_other_ref,
-    piece_ref,
-    same_ref,
-    mask_ref,
-    hidden_ref,
-    both_ref,
-    onward_ref,
-):
+def piece_part(refs, offset, kind):
+    last = len(refs) - 2
+    half = last // 2 + 1
+    if offset == half:
+        return refs[last + kind][0]
+    return refs[offset if offset < half else offset - 1][kind]
+
+
+def rows_kernel(top, masks, place_ref, small_ref, small_other_ref, hidden_other_ref, gradient_other_ref, piece_ref, *outs):
+    same_ref, same_turned_ref, mask_ref, rank_ref, gate_ref, hidden_ref, gradient_ref, onward_ref = outs
     onward_ref[...] = piece_ref[...]
+    hidden_ref[...] = hidden_other_ref[...]
+    gradient_ref[...] = gradient_other_ref[...]
     rows, tokens = same_ref.shape
     wide = mask_ref.shape[2]
-    row = lax.broadcasted_iota(jnp.int32, (rows, tokens), 0)
-    same = jnp.where(row // top == lax.broadcasted_iota(jnp.int32, (rows, tokens), 1), 1.0, 0.0).astype(bf16)
+
+    def ones(row_dim):
+        row = lax.broadcasted_iota(jnp.int32, (rows, tokens) if row_dim == 0 else (tokens, rows), row_dim)
+        token = lax.broadcasted_iota(jnp.int32, row.shape, 1 - row_dim)
+        return jnp.where(row // top == token, 1.0, 0.0).astype(bf16)
+
+    same = ones(0)
     same_ref[...] = same
+    same_turned_ref[...] = ones(1)
     column = members(place_ref, wide, masks)
+    below = (
+        lax.broadcasted_iota(jnp.int32, (tokens, tokens), 0)
+        > lax.broadcasted_iota(jnp.int32, (tokens, tokens), 1)
+    )
+    below = jnp.where(below, 1.0, 0.0).astype(bf16)
     for core, ref in enumerate((small_ref, small_other_ref)):
         small = ref[...].T
         experts = dot(same, small.astype(bf16), 1, 0)
@@ -129,29 +143,34 @@
         own = lax.broadcasted_iota(jnp.int32, experts.shape, 1) == position
         expert = jnp.sum(jnp.where(own, experts, 0.0), axis=1, keepdims=True)
         mask_ref[core] = jnp.where(expert == column, 1.0, 0.0).astype(bf16)
-    hidden_ref[...] = hidden_other_ref[...]
-    both_ref[:tokens] = gradient_ref[...]
-    both_ref[tokens:] = gradient_other_ref[...]
-
-
-def reduce_kernel(masks, place_ref, same_ref, mask_ref, own_ref, other_ref, *rest):
+        gate = jnp.zeros((tokens, wide), f32)
+        member = jnp.zeros((tokens, wide), f32)
+        for k in range(top):
+            named = small[:, k : k + 1] == column
+            gate = jnp.where(named, small[:, top + k : top + k + 1], gate)
+            member = jnp.where(named, 1.0, member)
+        gate_ref[core] = gate
+        rank_ref[core] = dot(below, member.astype(bf16), 1, 0)
+
+
+def reduce_kernel(masks, place_ref, same_turned_ref, mask_ref, own_ref, other_ref, *rest):
     slots = len(masks)
-    piece_refs, (_, reduced_ref, high_ref, low_ref) = rest[: 2 * slots], rest[2 * slots :]
+    piece_refs, (_, reduced_ref, high_ref, low_ref) = rest[: slots + 1], rest[slots + 1 :]
     hidden_width = own_ref.shape[1]
     for offset in range(slots):
         slot = place_ref[1 + offset]
         for kind in range(2):
-            down, _ = decode(piece_refs[kind * slots + offset][...], hidden_width)
+            down, _ = decode(piece_part(piece_refs, offset, kind), hidden_width)
             high_ref[kind, slot], low_ref[kind, slot] = halves(down)
     wide = reduced_ref.shape[2]
     high = high_ref[...].reshape(2 * wide, hidden_width)
     low = low_ref[...].reshape(2 * wide, hidden_width)
-    tokens = same_ref.shape[1]
+    tokens = same_turned_ref.shape[0]
     for core, hidden_ref in enumerate((own_ref, other_ref)):
         full = dot(hidden_ref[...], high, 1, 1) + dot(hidden_ref[...], low, 1, 1)
         mask = mask_ref[core].astype(f32)
         named = halves(full * jnp.concatenate([mask, mask], axis=1))
-        total = dot(same_ref[...], named[0], 0, 0) + dot(same_ref[...], named[1], 0, 0)
+        total = dot(same_turned_ref[...], named[0], 1, 0) + dot(same_turned_ref[...], named[1], 1, 0)
         reduced_ref[0, core * tokens : (core + 1) * tokens] = total[:, :wide]
         reduced_ref[1, core * tokens : (core + 1) * tokens] = total[:, wide:]
 
@@ -170,35 +189,17 @@
     return limits
 
 
-def tangent_kernel(
-    top, masks, place_ref, small_ref, small_other_ref, capacity_ref, prior_ref, arrived_ref, reduced_ref, *rest
-):
+def tangent_kernel(masks, place_ref, rank_ref, gate_ref, capacity_ref, prior_ref, arrived_ref, reduced_ref, *rest):
     slots = len(masks)
-    piece_refs = rest[: 2 * slots]
-    weight_ref, weighted_ref, tangent_ref, coded_ref, high_ref, low_ref = rest[2 * slots :]
-    experts, gates, _ = token_columns(small_ref, small_other_ref, top)
-    tokens, wide = weight_ref.shape
+    piece_refs = rest[: slots + 1]
+    weight_ref, weighted_ref, tangent_ref, coded_ref, high_ref, low_ref = rest[slots + 1 :]
+    _, wide = weight_ref.shape
     model_width = tangent_ref.shape[1]
-    hidden_width = piece_refs[0].shape[1] - model_width - lanes
-    block = tokens // 2
-    column = members(place_ref, wide, masks)
+    hidden_width = piece_refs[0].shape[2] - model_width - lanes
     limits = rank_limits(place_ref, masks, wide, capacity_ref, prior_ref, arrived_ref)
-    gate = jnp.zeros((tokens, wide), f32)
-    member = jnp.zeros((tokens, wide), f32)
-    for k in range(top):
-        named = experts[k] == column
-        gate = jnp.where(named, gates[k], gate)
-        member = jnp.where(named, 1.0, member)
-    below = (
-        lax.broadcasted_iota(jnp.int32, (block, block), 0)
-        > lax.broadcasted_iota(jnp.int32, (block, block), 1)
-    )
-    below = jnp.where(below, 1.0, 0.0).astype(bf16)
-    weights = []
-    for part in range(2):
-        rows = slice(part * block, (part + 1) * block)
-        local_rank = dot(below, member[rows].astype(bf16), 1, 0)
-        weights.append(jnp.where(local_rank < limits[part], adapter_scale * gate[rows], 0.0))
+    weights = [
+        jnp.where(rank_ref[core] < limits[core], adapter_scale * gate_ref[core], 0.0) for core in range(2)
+    ]
     weight = jnp.concatenate(weights, axis=0)
     weight_ref[...] = weight
     weighted = jnp.concatenate([weight * reduced_ref[0], weight * reduced_ref[1]], axis=1)
@@ -206,7 +207,7 @@
     for offset in range(slots):
         slot = place_ref[1 + offset]
         for kind in range(2):
-            _, up = decode(piece_refs[kind * slots + offset][...], hidden_width)
+            _, up = decode(piece_part(piece_refs, offset, kind), hidden_width)
             high_ref[kind, slot], low_ref[kind, slot] = halves(up)
     factor = high_ref[...].reshape(2 * wide, model_width), low_ref[...].reshape(2 * wide, model_width)
     tangent = dot_pairs(halves(weighted), factor, 1, 0)
@@ -245,7 +246,8 @@
     mask_ref,
     own_ref,
     other_ref,
-    gradient_ref,
+    own_gradient_ref,
+    other_gradient_ref,
     weight_ref,
     weighted_ref,
     high_ref,
@@ -259,7 +261,7 @@
 ):
     wide = weight_ref.shape[1]
     model_width = up_ref.shape[1]
-    gradient = gradient_ref[...]
+    gradient = jnp.concatenate([own_gradient_ref[...], other_gradient_ref[...]], axis=0)
     high = high_ref[...].reshape(2 * wide, model_width)
     low = low_ref[...].reshape(2 * wide, model_width)
     to_both = dot(gradient, high, 1, 1) + dot(gradient, low, 1, 1)
@@ -306,7 +308,8 @@
     put_chunks(chunk_ref, near_ref, far_ref, add_halves(down), up_ref[...] + up)
 
 
-def far_kernel(hidden_width, arrived_ref, chunk_ref, _, *out_refs):
+def far_kernel(hidden_width, arrived_ref, chunk_ref, near_ref, _, onward_ref, *out_refs):
+    onward_ref[...] = near_ref[...]
     count = len(out_refs)
     for place, out_ref in enumerate(out_refs):
         down, up = decode(arrived_ref[place], hidden_width)
@@ -368,17 +371,18 @@
         there = (place + jnp.arange(self.length, dtype=jnp.int32)) % self.length
         return jnp.where(there < rows, 4 * there, 4 * (self.length - 1 - there) + 2) + me % 2
 
-    def gather(self, own, way, passing=lambda piece: piece):
+    def gather(self, own, passing):
         half = self.length // 2
         found = {0: own}
-        for direction in (way, -way):
-            moving = own
-            for step in range(1, half + (direction == way)):
-                moving = self.shift(moving, direction)
-                if step == 1 and direction != way:
-                    moving = passing(moving)
-                found[-direction * step % self.length] = moving
-        return [found[offset] for offset in range(self.length)]
+        ahead, behind = own, own
+        for step in range(1, half):
+            behind = self.shift(behind, 1)
+            ahead = self.shift(ahead, -1)
+            if step == 1:
+                ahead = passing(ahead)
+            found[self.length - step], found[step] = behind, ahead
+        last = [self.shift(behind[:1], 1), self.shift(ahead[1:], -1)]
+        return [found[offset] for offset in sorted(found)] + last
 
 
 def exchange(value, mask):
@@ -418,26 +422,24 @@
     slot_of_offset = differs // 4 + rows * (differs // 2 % 2)
     place = jnp.concatenate([me[None], slot_of_offset, ring_members]).astype(jnp.int32)
 
-    def call(kernel, multiplies, outs, *operands, scratch=(), after=()):
+    def call(kernel, multiplies, outs, *operands, scratch=(), after=(), grant=kernel_vmem):
+        space = pltpu.HBM if kernel is prepare_kernel else pltpu.VMEM
         places = [
-            pl.BlockSpec(memory_space=pltpu.SMEM if operand is place else pltpu.VMEM) for operand in operands
+            pl.BlockSpec(memory_space=pltpu.SMEM if operand is place else space) for operand in operands
         ] + [pl.BlockSpec(memory_space=pl.ANY) for _ in after]
         return pl.pallas_call(
             kernel,
             out_shape=[jax.ShapeDtypeStruct(shape, dtype) for shape, dtype in outs],
             in_specs=places,
             scratch_shapes=scratch,
-            compiler_params=pltpu.CompilerParams(vmem_limit_bytes=kernel_vmem),
+            compiler_params=pltpu.CompilerParams(vmem_limit_bytes=grant),
             cost_estimate=pl.CostEstimate(flops=2 * multiplies, bytes_accessed=2**20, transcendentals=0),
         )(*operands, *after)
 
     down_multiplies = 2 * top * both * hidden_width * wide
     up_multiplies = both * model_width * wide
 
-    *own_pieces, small = call(
-        prepare_kernel,
-        10**8,
-        [((rank, coded_width), i16)] * 2 + [(((2 * top + 8) // 8 * 8, tokens), f32)],
+    first = (
         expert_of_route.T,
         gate_of_route.T,
         curvature[None],
@@ -446,6 +448,15 @@
         adapter_up[0],
         up_direction[0],
     )
+    piece, small = call(
+        prepare_kernel,
+        10**8,
+        [((2, rank, coded_width), i16), (((2 * top + 8) // 8 * 8, tokens), f32)],
+        *first,
+        scratch=[pltpu.VMEM(operand.shape, operand.dtype) for operand in first]
+        + [pltpu.SemaphoreType.DMA((len(first),))],
+        grant=whole_vmem,
+    )
     small_other = exchange(small, 1)
     hidden = hidden_of_route.reshape(tokens * top, hidden_width)
     beside = []
@@ -456,27 +467,30 @@
             10**9,
             [
                 ((tokens * top, tokens), bf16),
+                ((tokens, tokens * top), bf16),
                 ((2, tokens * top, wide), bf16),
+                ((2, tokens, wide), f32),
+                ((2, tokens, wide), f32),
                 ((tokens * top, hidden_width), bf16),
-                ((both, model_width), bf16),
-                ((rank, coded_width), i16),
+                ((tokens, model_width), bf16),
+                (piece.shape, i16),
             ],
             place,
             small,
             small_other,
             exchange(hidden, 1),
-            output_gradient,
             exchange(output_gradient, 1),
             piece,
         )
         beside.extend(made)
         return onward
 
-    pieces = ring.gather(own_pieces[0], 1, passing) + ring.gather(own_pieces[1], -1)
-    same, mask, hidden_other, gradient = beside
+    pieces = ring.gather(piece, passing)
+    same, same_turned, mask, local_rank, gate, hidden_other, gradient_other = beside
     capacity_row = jnp.pad(capacity.astype(f32), (counts_lane, lanes - counts_lane - experts))[None, :]
 
-    (prior,) = call(functools.partial(prior_kernel, masks), 10**8, [((8, lanes), f32)], place, *pieces[:slots])
+    by_offset = pieces[:rows] + [pieces[-2]] + pieces[rows:-2]
+    (prior,) = call(functools.partial(prior_kernel, masks), 10**8, [((8, lanes), f32)], place, *by_offset)
     prior_arrived = exchange(prior, 1)
     factor_halves = [pltpu.VMEM((2, slots, rank, hidden_width), bf16)] * 2
     (reduced,) = call(
@@ -484,7 +498,7 @@
         2 * down_multiplies,
         [((2, both, wide), f32)],
         place,
-        same,
+        same_turned,
         mask,
         hidden,
         hidden_other,
@@ -493,7 +507,7 @@
         after=[prior],
     )
     weight, weighted, tangent, coded, high, low = call(
-        functools.partial(tangent_kernel, top, masks),
+        functools.partial(tangent_kernel, masks),
         6 * up_multiplies,
         [
             ((both, wide), f32),
@@ -504,8 +518,8 @@
             ((2, slots, rank, model_width), bf16),
         ],
         place,
-        small,
-        small_other,
+        local_rank,
+        gate,
         capacity_row,
         prior,
         prior_arrived,
@@ -527,7 +541,8 @@
         mask,
         hidden,
         hidden_other,
-        gradient,
+        output_gradient,
+        gradient_other,
         weight,
         weighted,
         high,
@@ -535,7 +550,6 @@
         scratch=left,
     )
     gradient_far = exchange(gradient_far, 2)
-    gradient_near = exchange(gradient_near, 2)
     curvature_own, curvature_near, curvature_far = call(
         functools.partial(curvature_kernel, top),
         down_multiplies + 6 * up_multiplies,
@@ -559,16 +573,17 @@
 
     hop = 2 * 10**9
 
-    def along_z(arrived, own, after):
-        sums = call(
+    def along_z(arrived, own, near, after):
+        onward, *sums = call(
             functools.partial(far_kernel, hidden_width),
             hop,
-            [((rank, coded_width), i16)] * far,
+            [(near.shape, i16)] + [((rank, coded_width), i16)] * far,
             arrived,
             own,
+            near,
             after=[after],
         )
-        return sums, [exchange(part, 4 * z) for z, part in zip(range(rows - far, rows), sums)]
+        return exchange(onward, 2), sums, [exchange(part, 4 * z) for z, part in zip(range(rows - far, rows), sums)]
 
     def added(parts, after):
         return call(
@@ -579,10 +594,10 @@
             after=[after],
         )[0]
 
-    sums, gradient_parts = along_z(gradient_far, gradient_own, curvature_far)
+    gradient_near, sums, gradient_parts = along_z(gradient_far, gradient_own, gradient_near, curvature_far)
     curvature_far = exchange(curvature_far, 2)
-    curvature_near = exchange(curvature_near, 2)
-    sums, curvature_parts = along_z(curvature_far, curvature_own, sums[0])
+    curvature_near, sums, curvature_parts = along_z(curvature_far, curvature_own, curvature_near, sums[0])
+    gradient_total = added(gradient_parts, sums[0])
     near, total = call(
         functools.partial(near_kernel, hidden_width),
         hop,
@@ -591,11 +606,10 @@
         curvature_near,
         gradient_own,
         curvature_own,
-        after=[sums[0]],
+        after=[gradient_total],
     )
     near_parts = [exchange(near[z - 1], 4 * z) for z in range(1, rows - far)]
-    gradient_total = added(gradient_parts, near)
-    curvature_total = added(curvature_parts, gradient_total)
+    curvature_total = added(curvature_parts, near)
     down_gradient, up_gradient, curvature_down, curvature_up = call(
         functools.partial(total_kernel, hidden_width),
         hop,

time: 84.8 us -> 79.8 us (0.941)
  starting transfers between devices: 30.5 us -> 24.5 us
  local copies, waits for them, and re-layouts: 6.63 us -> 0.82 us
  waiting for transfers between devices: 26.2 us -> 31.2 us
  Pallas kernels: 20.1 us -> 22 us
    ppermute x14 -> x8, waiting for transfers between devices: 9.27 us -> 16.5 us  [shift(): return lax.ppermute(value, 'expert', pairs)]
    ppermute x14 -> x8, starting transfers between devices: 16.8 us -> 9.94 us  [shift(): return lax.ppermute(value, 'expert', pairs)]
    unnamed x20 -> x12, local copies, waits for them, and re-layouts: 6.56 us -> 0.73 us
    ppermute x14, waiting for transfers between devices: 17 us -> 14.7 us  [exchange(): lax.ppermute(value, 'expert', [(device, device ^ mask) for device in rang...]
    pallas_call x13, Pallas kernels: 20.1 us -> 22 us  [call(): pl.pallas_call(kernel, out_shape=[jax.ShapeDtypeStruct(shape, dtype) for...]
  transfers between devices with their start and end apart: 28 -> 22, of which waited for: 10 -> 11; matrix products, arithmetic and copies ran while one was open for 0% -> 0% of each run, Pallas kernels for 19% -> 24%
where the time goes in v9:
time: 79.8 us; the launch traced here: 79.5 us
  waiting for transfers between devices  31.2 us (39%)
  starting transfers between devices  24.5 us (31%)
  Pallas kernels  22 us (28%)
  between operations  0.84 us (1%)
  local copies, waits for them, and re-layouts  0.82 us (1%)
    pallas_call x13, Pallas kernels, call(): pl.pallas_call(kernel, out_shape=[jax.ShapeDtypeStruct(shape, dtype) for...  22 us
    ppermute x8, waiting for transfers between devices, shift(): return lax.ppermute(value, 'expert', pairs)  16.5 us
    ppermute x14, waiting for transfers between devices, exchange(): lax.ppermute(value, 'expert', [(device, device ^ mask) for device in rang...  14.7 us
    ppermute x14, starting transfers between devices, exchange(): lax.ppermute(value, 'expert', [(device, device ^ mask) for device in rang...  14.5 us
    ppermute x8, starting transfers between devices, shift(): return lax.ppermute(value, 'expert', pairs)  9.94 us
  transfers between devices with their start and end apart: 22, of which 11 were waited for; matrix products, arithmetic and copies ran while one was open for 0% of the time, Pallas kernels for 24%

profile of v9, /device:TPU:0, one launch (start us, length us, event | category | flops | bytes accessed | tf_op | source)
XLA Modules:
  0.0 79.5 jit_solution(7351741116926032139)
XLA Ops:
  1.2 2.0 %shard_map.129 = (s16[2,16,3200]{2,1,0:T(8,128)(2,1)}, f32[24,128]{1,0:T(8,128)}) custom-call(s32[8,128]{1,0:T(8,128)} %bitcast.33, bf16[8,128]{1,0:T(8,128)(2,1)} %bitcast.34, f32[1,128]{1,0:T(1,128)} %bitcast.35, f32[16,1024]{1,0:T(8,128)} %bitcast.31, f32[16,1024]{1,0:T(8,128)} %bitcast.32, f32[16,2048]{1,0:T(8,128)} %bitcast.29, f32[16,2048]{1,0:T(8,128)} %bitcast.30), custom_call_target="tpu_custom_call" | custom-call | flops 200000000 | bytes 1048576 | tf_op jit(solution)/shard_map/pallas_call | solution.py:430
  3.2 3.0 %collective-permute-start.3 = (s16[2,16,3200]{2,1,0:T(8,128)(2,1)}, s16[2,16,3200]{2,1,0:T(8,128)(2,1)S(1)}, u32[]{:S(2)}, u32[]{:S(2)}) collective-permute-start(s16[2,16,3200]{2,1,0:T(8,128)(2,1)} %get-tuple-element.41.rest_0_), channel_id=1, source_target_pairs={{0,2},{1,3},{4,0},{5,1},{8,4},{9,5},{12,8},{13,9},{14,12},{15,13},... | collective-permute-start | bytes 614408 | tf_op jit(solution)/shard_map/ppermute | solution.py:366
  6.5 6.7 %collective-permute-done.6.rest_7_.rest_6_ = s16[2,16,3200]{2,1,0:T(8,128)(2,1)S(1)} collective-permute-done((s16[2,16,3200]{2,1,0:T(8,128)(2,1)}, s16[2,16,3200]{2,1,0:T(8,128)(2,1)S(1)}, u32[]{:S(2)}, u32[]{:S(2)}) %collective-permute-start.6) | collective-permute-done | bytes 204832 | tf_op jit(solution)/shard_map/ppermute | solution.py:366
  14.4 2.1 %shard_map.130 = (bf16[1024,128]{1,0:T(8,128)(2,1)S(1)}, bf16[128,1024]{1,0:T(8,128)(2,1)S(1)}, bf16[2,1024,128]{2,1,0:T(8,128)(2,1)S(1)}, f32[2,128,128]{2,1,0:...) custom-call(s32[17]{0:T(128)S(1)} %pad_add_fusion.place_ref, ...), custom_call_target="tpu_custom_call" | custom-call | flops 2000000000 | bytes 1048576 | tf_op jit(solution)/shard_map/pallas_call | solution.py:430
  16.5 1.6 %collective-permute-start.4 = (s16[2,16,3200]{2,1,0:T(8,128)(2,1)S(1)}, s16[2,16,3200]{2,1,0:T(8,128)(2,1)S(1)}, u32[]{:S(2)}, u32[]{:S(2)}) collective-permute-start(s16[2,16,3200]{2,1,0:T(8,128)(2,1)S(1)} %get-tuple-element.48.rest_1_), channel_id=1, source_target_pairs={{0,2},{1,3},{4,0},{5,1},{8,4},{9,5},{12,8},{13,9},{14,12},{15,13},... | collective-permute-start | bytes 614408 | tf_op jit(solution)/shard_map/ppermute | solution.py:366
  19.9 2.6 %collective-permute-done.4.rest_2_ = s16[2,16,3200]{2,1,0:T(8,128)(2,1)S(1)} collective-permute-done((s16[2,16,3200]{2,1,0:T(8,128)(2,1)S(1)}, s16[2,16,3200]{2,1,0:T(8,128)(2,1)S(1)}, u32[]{:S(2)}, u32[]{:S(2)}) %collective-permute-start.4) | collective-permute-done | bytes 204832 | tf_op jit(solution)/shard_map/ppermute | solution.py:366
  22.5 1.4 %collective-permute-start.5 = (s16[2,16,3200]{2,1,0:T(8,128)(2,1)S(1)}, s16[2,16,3200]{2,1,0:T(8,128)(2,1)S(1)}, u32[]{:S(2)}, u32[]{:S(2)}) collective-permute-start(s16[2,16,3200]{2,1,0:T(8,128)(2,1)S(1)} %collective-permute-done.4.rest_2_), channel_id=1, source_target_pairs={{0,2},{1,3},{4,0},{5,1},{8,4},{9,5},{12,8},{13,9},{14,12},{15,13},... | collective-permute-start | bytes 614408 | tf_op jit(solution)/shard_map/ppermute | solution.py:366
  25.7 2.7 %collective-permute-done.5.rest_3_ = s16[2,16,3200]{2,1,0:T(8,128)(2,1)S(1)} collective-permute-done((s16[2,16,3200]{2,1,0:T(8,128)(2,1)S(1)}, s16[2,16,3200]{2,1,0:T(8,128)(2,1)S(1)}, u32[]{:S(2)}, u32[]{:S(2)}) %collective-permute-start.5) | collective-permute-done | bytes 204832 | tf_op jit(solution)/shard_map/ppermute | solution.py:366
  28.4 1.9 %collective-permute-start.11 = (s16[1,16,3200]{2,1,0:T(8,128)(2,1)S(1)}, s16[1,16,3200]{2,1,0:T(8,128)(2,1)S(1)}, u32[]{:S(2)}, u32[]{:S(2)}) collective-permute-start(s16[1,16,3200]{2,1,0:T(8,128)(2,1)S(1)} %slice.9), channel_id=1, source_target_pairs={{0,2},{1,3},{4,0},{5,1},{8,4},{9,5},{12,8},{13,9},{14,12},{15,13},... | collective-permute-start | bytes 307208 | tf_op jit(solution)/shard_map/ppermute | solution.py:366
  31.1 2.3 %collective-permute-done.11.rest_8_ = s16[1,16,3200]{2,1,0:T(8,128)(2,1)S(1)} collective-permute-done((s16[1,16,3200]{2,1,0:T(8,128)(2,1)S(1)}, s16[1,16,3200]{2,1,0:T(8,128)(2,1)S(1)}, u32[]{:S(2)}, u32[]{:S(2)}) %collective-permute-start.11) | collective-permute-done | bytes 102432 | tf_op jit(solution)/shard_map/ppermute | solution.py:366
  33.4 6.0 %shard_map.132.reduced_ref = f32[2,256,128]{2,1,0:T(8,128)S(1)} custom-call(s32[17]{0:T(128)S(1)} %pad_add_fusion.place_ref, bf16[128,1024]{1,0:T(8,128)(2,1)S(1)} %get-tuple-element.49.same_turned_ref, bf16[2,1024,128]{2,1,0:T(8,128)(2,1)S(1)} %get-tuple-element.43.mask_ref, bf16[1024,1024]{1,0:T(8,128)(2,1)S(1)} %bitcast.25, ...), custom_call_target="tpu_custom_call" | custom-call | flops 2147483648 | bytes 1048576 | tf_op jit(solution)/shard_map/pallas_call | solution.py:430
  39.4 2.2 %shard_map.133 = (f32[256,128]{1,0:T(8,128)S(1)}, f32[256,256]{1,0:T(8,128)S(1)}, f32[256,2048]{1,0:T(8,128)S(1)}, bf16[256,2048]{1,0:T(8,128)(2,1)S(1)}, bf16[2...) custom-call(s32[17]{0:T(128)S(1)} %pad_add_fusion.place_ref, ...), custom_call_target="tpu_custom_call" | custom-call | flops 805306368 | bytes 1048576 | tf_op jit(solution)/shard_map/pallas_call | solution.py:430
  41.7 4.0 %shard_map.134 = (f32[4,16,3072]{2,1,0:T(8,128)S(1)}, s16[2,16,3200]{2,1,0:T(8,128)(2,1)S(1)}, s16[2,16,3200]{2,1,0:T(8,128)(2,1)S(1)}, f32[128,2048]{1,0:T(8,128)S(1)}, f32[256,128]{1,0:T(8,128)S(1)}) custom-call(bf16[1024,128]{1,0:T(8,128)(2,1)S(1)} %get-tuple-element.42.same_ref, bf16[2,1024,128]{2,1,0:T(8,128)(2,1)S(1)} %get-tuple-element.43.mask_ref, ...), custom_call_target="tpu_custom_call" | custom-call | flops 2147483648 | bytes 1048576 | tf_op jit(solution)/shard_map/pallas_call | solution.py:430
  45.7 1.7 %collective-permute-start.12 = (s16[2,16,3200]{2,1,0:T(8,128)(2,1)S(1)}, s16[2,16,3200]{2,1,0:T(8,128)(2,1)S(1)}, u32[]{:S(2)}, u32[]{:S(2)}) collective-permute-start(s16[2,16,3200]{2,1,0:T(8,128)(2,1)S(1)} %get-tuple-element.54), channel_id=1, source_target_pairs={{0,2},{1,3},{2,0},{3,1},{4,6},{5,7},{6,4},{7,5},{8,10},{9,11},{10,... | collective-permute-start | bytes 614408 | tf_op jit(solution)/shard_map/ppermute | solution.py:390
  47.4 3.4 %shard_map.135 = (f32[4,16,3072]{2,1,0:T(8,128)S(1)}, s16[2,16,3200]{2,1,0:T(8,128)(2,1)S(1)}, s16[2,16,3200]{2,1,0:T(8,128)(2,1)S(1)}) custom-call(f32[24,128]{1,0:T(8,128)S(1)} %copy-done.4, f32[24,128]{1,0:T(8,128)S(1)} %collective-permute-done.small_other_ref, bf16[1024,128]{1,0:T(8,128)(2,1)S(1)} %get-tuple-element.42.same_ref, ...), custom_call_target="tpu_custom_call" | custom-call | flops 1879048192 | bytes 1048576 | tf_op jit(solution)/shard_map/pallas_call | solution.py:430
  51.3 2.0 %collective-permute-done.12.arrived_ref = s16[2,16,3200]{2,1,0:T(8,128)(2,1)S(1)} collective-permute-done((s16[2,16,3200]{2,1,0:T(8,128)(2,1)S(1)}, s16[2,16,3200]{2,1,0:T(8,128)(2,1)S(1)}, u32[]{:S(2)}, u32[]{:S(2)}) %collective-permute-start.12) | collective-permute-done | bytes 204832 | tf_op jit(solution)/shard_map/ppermute | solution.py:390
  53.5 2.1 %collective-permute-start.14 = (s16[2,16,3200]{2,1,0:T(8,128)(2,1)S(1)}, s16[2,16,3200]{2,1,0:T(8,128)(2,1)S(1)}, u32[]{:S(2)}, u32[]{:S(2)}) collective-permute-start(s16[2,16,3200]{2,1,0:T(8,128)(2,1)S(1)} %get-tuple-element.62), channel_id=1, source_target_pairs={{0,2},{1,3},{2,0},{3,1},{4,6},{5,7},{6,4},{7,5},{8,10},{9,11},{10,... | collective-permute-start | bytes 614408 | tf_op jit(solution)/shard_map/ppermute | solution.py:390
  55.6 2.5 %collective-permute-start.17 = (s16[16,3200]{1,0:T(8,128)(2,1)S(1)}, s16[16,3200]{1,0:T(8,128)(2,1)S(1)}, u32[]{:S(2)}, u32[]{:S(2)}) collective-permute-start(s16[16,3200]{1,0:T(8,128)(2,1)S(1)} %get-tuple-element.65._), channel_id=1, source_target_pairs={{0,8},{1,9},{2,10},{3,11},{4,12},{5,13},{6,14},{7,15},{8,0},{9,1},... | collective-permute-start | bytes 307208 | tf_op jit(solution)/shard_map/ppermute | solution.py:390
  58.1 1.4 %collective-permute-start.18 = (s16[16,3200]{1,0:T(8,128)(2,1)S(1)}, s16[16,3200]{1,0:T(8,128)(2,1)S(1)}, u32[]{:S(2)}, u32[]{:S(2)}) collective-permute-start(s16[16,3200]{1,0:T(8,128)(2,1)S(1)} %get-tuple-element.67), channel_id=1, source_target_pairs={{0,12},{1,13},{2,14},{3,15},{4,8},{5,9},{6,10},{7,11},{8,4},{9,5},... | collective-permute-start | bytes 307208 | tf_op jit(solution)/shard_map/ppermute | solution.py:390
  60.3 2.2 %collective-permute-start.19 = (s16[16,3200]{1,0:T(8,128)(2,1)S(1)}, s16[16,3200]{1,0:T(8,128)(2,1)S(1)}, u32[]{:S(2)}, u32[]{:S(2)}) collective-permute-start(s16[16,3200]{1,0:T(8,128)(2,1)S(1)} %get-tuple-element.68.refs_2_), channel_id=1, source_target_pairs={{0,8},{1,9},{2,10},{3,11},{4,12},{5,13},{6,14},{7,15},{8,0},{9,1},... | collective-permute-start | bytes 307208 | tf_op jit(solution)/shard_map/ppermute | solution.py:390
  62.5 5.3 %collective-permute-done.17.refs_0_ = s16[16,3200]{1,0:T(8,128)(2,1)S(1)} collective-permute-done((s16[16,3200]{1,0:T(8,128)(2,1)S(1)}, s16[16,3200]{1,0:T(8,128)(2,1)S(1)}, u32[]{:S(2)}, u32[]{:S(2)}) %collective-permute-start.17) | collective-permute-done | bytes 102432 | tf_op jit(solution)/shard_map/ppermute | solution.py:390
  67.8 2.8 %collective-permute-start.20 = (s16[16,3200]{1,0:T(8,128)(2,1)S(1)}, s16[16,3200]{1,0:T(8,128)(2,1)S(1)}, u32[]{:S(2)}, u32[]{:S(2)}) collective-permute-start(s16[16,3200]{1,0:T(8,128)(2,1)S(1)} %get-tuple-element.70), channel_id=1, source_target_pairs={{0,12},{1,13},{2,14},{3,15},{4,8},{5,9},{6,10},{7,11},{8,4},{9,5},... | collective-permute-start | bytes 307208 | tf_op jit(solution)/shard_map/ppermute | solution.py:390
  71.0 3.2 %collective-permute-done.19.refs_0_ = s16[16,3200]{1,0:T(8,128)(2,1)S(1)} collective-permute-done((s16[16,3200]{1,0:T(8,128)(2,1)S(1)}, s16[16,3200]{1,0:T(8,128)(2,1)S(1)}, u32[]{:S(2)}, u32[]{:S(2)}) %collective-permute-start.19) | collective-permute-done | bytes 102432 | tf_op jit(solution)/shard_map/ppermute | solution.py:390
  74.7 4.0 %collective-permute-done.21.rest_0_ = s16[2,16,3200]{2,1,0:T(8,128)(2,1)S(1)} collective-permute-done((s16[2,16,3200]{2,1,0:T(8,128)(2,1)S(1)}, s16[2,16,3200]{2,1,0:T(8,128)(2,1)S(1)}, u32[]{:S(2)}, u32[]{:S(2)}) %collective-permute-start.21) | collective-permute-done | bytes 204832 | tf_op jit(solution)/shard_map/ppermute | solution.py:390
  (51 shorter events, 9.5 us)
Async XLA Ops:
  0.6 13.0 %collective-permute-start.1 = (bf16[1024,1024]{1,0:T(8,128)(2,1)}, bf16[1024,1024]{1,0:T(8,128)(2,1)S(1)}, u32[]{:S(2)}, u32[]{:S(2)}) collective-permute-start(bf16[1024,1024]{1,0:T(8,128)(2,1)} %bitcast.24), channel_id=1, source_target_pairs={{0,1},{1,0},{2,3},{3,2},{4,5},{5,4},{6,7},{7,6},{8,9},{9,8},{10,11... | collective-permute-start | bytes 6291464 | tf_op jit(solution)/shard_map/ppermute | solution.py:390
  1.2 12.5 %collective-permute-start.2 = (bf16[128,2048]{1,0:T(8,128)(2,1)}, bf16[128,2048]{1,0:T(8,128)(2,1)S(1)}, u32[]{:S(2)}, u32[]{:S(2)}) collective-permute-start(bf16[128,2048]{1,0:T(8,128)(2,1)} %own_gradient_ref.1), channel_id=1, source_target_pairs={{0,1},{1,0},{2,3},{3,2},{4,5},{5,4},{6,7},{7,6},{8,9},{9,8},{10,11... | collective-permute-start | bytes 1572872 | tf_op jit(solution)/shard_map/ppermute | solution.py:390
  3.2 10.4 %collective-permute-start.3 = (s16[2,16,3200]{2,1,0:T(8,128)(2,1)}, s16[2,16,3200]{2,1,0:T(8,128)(2,1)S(1)}, u32[]{:S(2)}, u32[]{:S(2)}) collective-permute-start(s16[2,16,3200]{2,1,0:T(8,128)(2,1)} %get-tuple-element.41.rest_0_), channel_id=1, source_target_pairs={{0,2},{1,3},{4,0},{5,1},{8,4},{9,5},{12,8},{13,9},{14,12},{15,13},... | collective-permute-start | bytes 614408 | tf_op jit(solution)/shard_map/ppermute | solution.py:366
  6.2 7.0 %collective-permute-start.6 = (s16[2,16,3200]{2,1,0:T(8,128)(2,1)}, s16[2,16,3200]{2,1,0:T(8,128)(2,1)S(1)}, u32[]{:S(2)}, u32[]{:S(2)}) collective-permute-start(s16[2,16,3200]{2,1,0:T(8,128)(2,1)} %get-tuple-element.41.rest_0_), channel_id=1, source_target_pairs={{0,4},{1,5},{4,8},{5,9},{8,12},{9,13},{12,14},{13,15},{14,10},{15,... | collective-permute-start | bytes 614408 | tf_op jit(solution)/shard_map/ppermute | solution.py:366
  6.4 7.3 %collective-permute-start = (f32[24,128]{1,0:T(8,128)}, f32[24,128]{1,0:T(8,128)S(1)}, u32[]{:S(2)}, u32[]{:S(2)}) collective-permute-start(f32[24,128]{1,0:T(8,128)} %get-tuple-element.40.small_ref), channel_id=1, source_target_pairs={{0,1},{1,0},{2,3},{3,2},{4,5},{5,4},{6,7},{7,6},{8,9},{9,8},{10,11... | collective-permute-start | bytes 36872 | tf_op jit(solution)/shard_map/ppermute | solution.py:390
  6.5 23.9 %copy-start.2 = (s16[2,16,3200]{2,1,0:T(8,128)(2,1)S(1)}, s16[2,16,3200]{2,1,0:T(8,128)(2,1)}, u32[]{:S(2)}) copy-start(s16[2,16,3200]{2,1,0:T(8,128)(2,1)} %get-tuple-element.41.rest_0_) | copy-start | bytes 614404
  6.5 26.9 %copy-start = (bf16[128,8,1024]{2,1,0:T(8,128)(2,1)S(1)}, bf16[128,8,1024]{2,1,0:T(8,128)(2,1)}, u32[]{:S(2)}) copy-start(bf16[128,8,1024]{2,1,0:T(8,128)(2,1)} %param.10) | copy-start | bytes 6291460
  13.2 5.9 %collective-permute-start.7 = (s16[2,16,3200]{2,1,0:T(8,128)(2,1)S(1)}, s16[2,16,3200]{2,1,0:T(8,128)(2,1)S(1)}, u32[]{:S(2)}, u32[]{:S(2)}) collective-permute-start(s16[2,16,3200]{2,1,0:T(8,128)(2,1)S(1)} %collective-permute-done.6.rest_7_.rest_6_), channel_id=1, source_target_pairs={{0,4},{1,5},{4,8},{5,9},{8,12},{9,13},{12,14},{13,15},{14,10},{15,... | collective-permute-start | bytes 614408 | tf_op jit(solution)/shard_map/ppermute | solution.py:366
  16.5 6.0 %collective-permute-start.4 = (s16[2,16,3200]{2,1,0:T(8,128)(2,1)S(1)}, s16[2,16,3200]{2,1,0:T(8,128)(2,1)S(1)}, u32[]{:S(2)}, u32[]{:S(2)}) collective-permute-start(s16[2,16,3200]{2,1,0:T(8,128)(2,1)S(1)} %get-tuple-element.48.rest_1_), channel_id=1, source_target_pairs={{0,2},{1,3},{4,0},{5,1},{8,4},{9,5},{12,8},{13,9},{14,12},{15,13},... | collective-permute-start | bytes 614408 | tf_op jit(solution)/shard_map/ppermute | solution.py:366
  19.1 5.9 %collective-permute-start.8 = (s16[2,16,3200]{2,1,0:T(8,128)(2,1)S(1)}, s16[2,16,3200]{2,1,0:T(8,128)(2,1)S(1)}, u32[]{:S(2)}, u32[]{:S(2)}) collective-permute-start(s16[2,16,3200]{2,1,0:T(8,128)(2,1)S(1)} %collective-permute-done.7.rest_6_.rest_5_), channel_id=1, source_target_pairs={{0,4},{1,5},{4,8},{5,9},{8,12},{9,13},{12,14},{13,15},{14,10},{15,... | collective-permute-start | bytes 614408 | tf_op jit(solution)/shard_map/ppermute | solution.py:366
  22.5 6.0 %collective-permute-start.5 = (s16[2,16,3200]{2,1,0:T(8,128)(2,1)S(1)}, s16[2,16,3200]{2,1,0:T(8,128)(2,1)S(1)}, u32[]{:S(2)}, u32[]{:S(2)}) collective-permute-start(s16[2,16,3200]{2,1,0:T(8,128)(2,1)S(1)} %collective-permute-done.4.rest_2_), channel_id=1, source_target_pairs={{0,2},{1,3},{4,0},{5,1},{8,4},{9,5},{12,8},{13,9},{14,12},{15,13},... | collective-permute-start | bytes 614408 | tf_op jit(solution)/shard_map/ppermute | solution.py:366
  25.0 5.4 %collective-permute-start.9 = (s16[1,16,3200]{2,1,0:T(8,128)(2,1)S(1)}, s16[1,16,3200]{2,1,0:T(8,128)(2,1)S(1)}, u32[]{:S(2)}, u32[]{:S(2)}) collective-permute-start(s16[1,16,3200]{2,1,0:T(8,128)(2,1)S(1)} %slice.8), channel_id=1, source_target_pairs={{0,4},{1,5},{4,8},{5,9},{8,12},{9,13},{12,14},{13,15},{14,10},{15,... | collective-permute-start | bytes 307208 | tf_op jit(solution)/shard_map/ppermute | solution.py:366
  28.4 4.9 %collective-permute-start.11 = (s16[1,16,3200]{2,1,0:T(8,128)(2,1)S(1)}, s16[1,16,3200]{2,1,0:T(8,128)(2,1)S(1)}, u32[]{:S(2)}, u32[]{:S(2)}) collective-permute-start(s16[1,16,3200]{2,1,0:T(8,128)(2,1)S(1)} %slice.9), channel_id=1, source_target_pairs={{0,2},{1,3},{4,0},{5,1},{8,4},{9,5},{12,8},{13,9},{14,12},{15,13},... | collective-permute-start | bytes 307208 | tf_op jit(solution)/shard_map/ppermute | solution.py:366
  31.0 8.4 %collective-permute-start.10 = (f32[8,128]{1,0:T(8,128)S(1)}, f32[8,128]{1,0:T(8,128)S(1)}, u32[]{:S(2)}, u32[]{:S(2)}) collective-permute-start(f32[8,128]{1,0:T(8,128)S(1)} %shard_map.131.rest_9_.prior_ref), channel_id=1, source_target_pairs={{0,1},{1,0},{2,3},{3,2},{4,5},{5,4},{6,7},{7,6},{8,9},{9,8},{10,11... | collective-permute-start | bytes 12296 | tf_op jit(solution)/shard_map/ppermute | solution.py:390
  41.6 5.8 %collective-permute-start.13 = (bf16[256,2048]{1,0:T(8,128)(2,1)S(1)}, bf16[256,2048]{1,0:T(8,128)(2,1)S(1)}, u32[]{:S(2)}, u32[]{:S(2)}) collective-permute-start(bf16[256,2048]{1,0:T(8,128)(2,1)S(1)} %get-tuple-element.60), channel_id=1, source_target_pairs={{0,1},{1,0},{2,3},{3,2},{4,5},{5,4},{6,7},{7,6},{8,9},{9,8},{10,11... | collective-permute-start | bytes 3145736 | tf_op jit(solution)/shard_map/ppermute | solution.py:390
  45.7 7.5 %collective-permute-start.12 = (s16[2,16,3200]{2,1,0:T(8,128)(2,1)S(1)}, s16[2,16,3200]{2,1,0:T(8,128)(2,1)S(1)}, u32[]{:S(2)}, u32[]{:S(2)}) collective-permute-start(s16[2,16,3200]{2,1,0:T(8,128)(2,1)S(1)} %get-tuple-element.54), channel_id=1, source_target_pairs={{0,2},{1,3},{2,0},{3,1},{4,6},{5,7},{6,4},{7,5},{8,10},{9,11},{10,... | collective-permute-start | bytes 614408 | tf_op jit(solution)/shard_map/ppermute | solution.py:390
  50.8 8.7 %collective-permute-start.15 = (s16[2,16,3200]{2,1,0:T(8,128)(2,1)S(1)}, s16[2,16,3200]{2,1,0:T(8,128)(2,1)S(1)}, u32[]{:S(2)}, u32[]{:S(2)}) collective-permute-start(s16[2,16,3200]{2,1,0:T(8,128)(2,1)S(1)} %get-tuple-element.61._), channel_id=1, source_target_pairs={{0,2},{1,3},{2,0},{3,1},{4,6},{5,7},{6,4},{7,5},{8,10},{9,11},{10,... | collective-permute-start | bytes 614408 | tf_op jit(solution)/shard_map/ppermute | solution.py:390
  53.5 17.2 %collective-permute-start.14 = (s16[2,16,3200]{2,1,0:T(8,128)(2,1)S(1)}, s16[2,16,3200]{2,1,0:T(8,128)(2,1)S(1)}, u32[]{:S(2)}, u32[]{:S(2)}) collective-permute-start(s16[2,16,3200]{2,1,0:T(8,128)(2,1)S(1)} %get-tuple-element.62), channel_id=1, source_target_pairs={{0,2},{1,3},{2,0},{3,1},{4,6},{5,7},{6,4},{7,5},{8,10},{9,11},{10,... | collective-permute-start | bytes 614408 | tf_op jit(solution)/shard_map/ppermute | solution.py:390
  55.6 12.2 %collective-permute-start.17 = (s16[16,3200]{1,0:T(8,128)(2,1)S(1)}, s16[16,3200]{1,0:T(8,128)(2,1)S(1)}, u32[]{:S(2)}, u32[]{:S(2)}) collective-permute-start(s16[16,3200]{1,0:T(8,128)(2,1)S(1)} %get-tuple-element.65._), channel_id=1, source_target_pairs={{0,8},{1,9},{2,10},{3,11},{4,12},{5,13},{6,14},{7,15},{8,0},{9,1},... | collective-permute-start | bytes 307208 | tf_op jit(solution)/shard_map/ppermute | solution.py:390
  58.1 12.5 %collective-permute-start.18 = (s16[16,3200]{1,0:T(8,128)(2,1)S(1)}, s16[16,3200]{1,0:T(8,128)(2,1)S(1)}, u32[]{:S(2)}, u32[]{:S(2)}) collective-permute-start(s16[16,3200]{1,0:T(8,128)(2,1)S(1)} %get-tuple-element.67), channel_id=1, source_target_pairs={{0,12},{1,13},{2,14},{3,15},{4,8},{5,9},{6,10},{7,11},{8,4},{9,5},... | collective-permute-start | bytes 307208 | tf_op jit(solution)/shard_map/ppermute | solution.py:390
  59.8 10.9 %collective-permute-start.16 = (s16[2,16,3200]{2,1,0:T(8,128)(2,1)S(1)}, s16[2,16,3200]{2,1,0:T(8,128)(2,1)S(1)}, u32[]{:S(2)}, u32[]{:S(2)}) collective-permute-start(s16[2,16,3200]{2,1,0:T(8,128)(2,1)S(1)} %get-tuple-element.66), channel_id=1, source_target_pairs={{0,2},{1,3},{2,0},{3,1},{4,6},{5,7},{6,4},{7,5},{8,10},{9,11},{10,... | collective-permute-start | bytes 614408 | tf_op jit(solution)/shard_map/ppermute | solution.py:390
  60.3 14.0 %collective-permute-start.19 = (s16[16,3200]{1,0:T(8,128)(2,1)S(1)}, s16[16,3200]{1,0:T(8,128)(2,1)S(1)}, u32[]{:S(2)}, u32[]{:S(2)}) collective-permute-start(s16[16,3200]{1,0:T(8,128)(2,1)S(1)} %get-tuple-element.68.refs_2_), channel_id=1, source_target_pairs={{0,8},{1,9},{2,10},{3,11},{4,12},{5,13},{6,14},{7,15},{8,0},{9,1},... | collective-permute-start | bytes 307208 | tf_op jit(solution)/shard_map/ppermute | solution.py:390
  67.8 6.7 %collective-permute-start.20 = (s16[16,3200]{1,0:T(8,128)(2,1)S(1)}, s16[16,3200]{1,0:T(8,128)(2,1)S(1)}, u32[]{:S(2)}, u32[]{:S(2)}) collective-permute-start(s16[16,3200]{1,0:T(8,128)(2,1)S(1)} %get-tuple-element.70), channel_id=1, source_target_pairs={{0,12},{1,13},{2,14},{3,15},{4,8},{5,9},{6,10},{7,11},{8,4},{9,5},... | collective-permute-start | bytes 307208 | tf_op jit(solution)/shard_map/ppermute | solution.py:390
  71.0 7.7 %collective-permute-start.21 = (s16[2,16,3200]{2,1,0:T(8,128)(2,1)S(1)}, s16[2,16,3200]{2,1,0:T(8,128)(2,1)S(1)}, u32[]{:S(2)}, u32[]{:S(2)}) collective-permute-start(s16[2,16,3200]{2,1,0:T(8,128)(2,1)S(1)} %bitcast.28), channel_id=1, source_target_pairs={{0,4},{1,5},{2,6},{3,7},{4,0},{5,1},{6,2},{7,3},{8,12},{9,13},{10,... | collective-permute-start | bytes 614408 | tf_op jit(solution)/shard_map/ppermute | solution.py:390
  (4 other events, 26.2 us)

commit v10 on v9

--- a/solution.py
+++ b/solution.py
@@ -115,21 +115,19 @@
 
 
 def rows_kernel(top, masks, place_ref, small_ref, small_other_ref, hidden_other_ref, gradient_other_ref, piece_ref, *outs):
-    same_ref, same_turned_ref, mask_ref, rank_ref, gate_ref, hidden_ref, gradient_ref, onward_ref = outs
-    onward_ref[...] = piece_ref[...]
-    hidden_ref[...] = hidden_other_ref[...]
-    gradient_ref[...] = gradient_other_ref[...]
+    same_ref, mask_ref, rank_ref, gate_ref, hidden_ref, gradient_ref, onward_ref, sem = outs
+    copies = [
+        pltpu.make_async_copy(hidden_other_ref, hidden_ref, sem.at[0]),
+        pltpu.make_async_copy(gradient_other_ref, gradient_ref, sem.at[1]),
+        pltpu.make_async_copy(piece_ref, onward_ref, sem.at[2]),
+    ]
+    for copy in copies:
+        copy.start()
     rows, tokens = same_ref.shape
     wide = mask_ref.shape[2]
-
-    def ones(row_dim):
-        row = lax.broadcasted_iota(jnp.int32, (rows, tokens) if row_dim == 0 else (tokens, rows), row_dim)
-        token = lax.broadcasted_iota(jnp.int32, row.shape, 1 - row_dim)
-        return jnp.where(row // top == token, 1.0, 0.0).astype(bf16)
-
-    same = ones(0)
+    row = lax.broadcasted_iota(jnp.int32, (rows, tokens), 0)
+    same = jnp.where(row // top == lax.broadcasted_iota(jnp.int32, (rows, tokens), 1), 1.0, 0.0).astype(bf16)
     same_ref[...] = same
-    same_turned_ref[...] = ones(1)
     column = members(place_ref, wide, masks)
     below = (
         lax.broadcasted_iota(jnp.int32, (tokens, tokens), 0)
@@ -151,28 +149,35 @@
             member = jnp.where(named, 1.0, member)
         gate_ref[core] = gate
         rank_ref[core] = dot(below, member.astype(bf16), 1, 0)
-
-
-def reduce_kernel(masks, place_ref, same_turned_ref, mask_ref, own_ref, other_ref, *rest):
+    for copy in copies:
+        copy.wait()
+
+
+def reduce_kernel(top, masks, place_ref, small_ref, small_other_ref, own_ref, other_ref, *rest):
     slots = len(masks)
-    piece_refs, (_, reduced_ref, high_ref, low_ref) = rest[: slots + 1], rest[slots + 1 :]
+    piece_refs, (_, reduced_ref, high_ref, low_ref, full_ref) = rest[: slots + 1], rest[slots + 1 :]
     hidden_width = own_ref.shape[1]
     for offset in range(slots):
         slot = place_ref[1 + offset]
         for kind in range(2):
             down, _ = decode(piece_part(piece_refs, offset, kind), hidden_width)
             high_ref[kind, slot], low_ref[kind, slot] = halves(down)
+    experts, _, _ = token_columns(small_ref, small_other_ref, top)
     wide = reduced_ref.shape[2]
+    column = members(place_ref, wide, masks)
     high = high_ref[...].reshape(2 * wide, hidden_width)
     low = low_ref[...].reshape(2 * wide, hidden_width)
-    tokens = same_turned_ref.shape[0]
+    tokens = own_ref.shape[0] // top
     for core, hidden_ref in enumerate((own_ref, other_ref)):
         full = dot(hidden_ref[...], high, 1, 1) + dot(hidden_ref[...], low, 1, 1)
-        mask = mask_ref[core].astype(f32)
-        named = halves(full * jnp.concatenate([mask, mask], axis=1))
-        total = dot(same_turned_ref[...], named[0], 1, 0) + dot(same_turned_ref[...], named[1], 1, 0)
-        reduced_ref[0, core * tokens : (core + 1) * tokens] = total[:, :wide]
-        reduced_ref[1, core * tokens : (core + 1) * tokens] = total[:, wide:]
+        full_ref[0], full_ref[1] = full[:, :wide], full[:, wide:]
+        tokens_of = slice(core * tokens, (core + 1) * tokens)
+        for kind in range(2):
+            total = jnp.zeros((tokens, wide), f32)
+            for k in range(top):
+                here = full_ref[kind, pl.ds(k, tokens, stride=top), :]
+                total = jnp.where(experts[k][tokens_of] == column, here, total)
+            reduced_ref[kind, tokens_of] = total
 
 
 def rank_limits(place_ref, masks, wide, capacity_ref, prior_ref, arrived_ref):
@@ -229,16 +234,21 @@
     return both[:middle] + both[middle:]
 
 
-def put_chunks(own_ref, near_ref, far_ref, down, up):
-    count, rank, _ = own_ref.shape
-    hidden_width = down.shape[1]
-    own_ref[:, :, :hidden_width] = down[: count * rank].reshape(count, rank, -1)
-    own_ref[:, :, hidden_width:] = up[: count * rank].reshape(count, rank, -1)
-    start = count * rank
-    for out_ref in (near_ref, far_ref):
-        stop = start + out_ref.shape[0] * rank
-        out_ref[...] = encode(down[start:stop], up[start:stop]).reshape(out_ref.shape)
-        start = stop
+def put_chunks(keep_ref, chunk_ref, far_ref, near_ref, kind, down, up):
+    far, rank, _ = chunk_ref.shape
+    rows = down.shape[0] // rank // 2
+
+    def slot(number):
+        start = number * rank
+        return down[start : start + rank], up[start : start + rank]
+
+    for x in range(2):
+        keep_ref[x] = jnp.concatenate(slot(x * rows), axis=1)
+        for z in range(1, rows - far):
+            near_ref[z - 1, kind, x] = encode(*slot(x * rows + z))
+    for place in range(far):
+        chunk_ref[place] = jnp.concatenate(slot(rows - far + place), axis=1)
+        far_ref[place] = encode(*slot(2 * rows - far + place))
 
 
 def gradient_kernel(
@@ -252,9 +262,10 @@
     weighted_ref,
     high_ref,
     low_ref,
+    keep_ref,
     chunk_ref,
+    far_ref,
     near_ref,
-    far_ref,
     up_ref,
     to_ref,
     left_ref,
@@ -270,7 +281,7 @@
     down = dot(left_ref[0], own_ref[...], 0, 0) + dot(left_ref[1], other_ref[...], 0, 0)
     up = add_halves(dot(jnp.concatenate(halves(weighted_ref[...]), axis=1), gradient, 0, 0))
     up_ref[...] = up[:wide]
-    put_chunks(chunk_ref, near_ref, far_ref, add_halves(down), up[wide:])
+    put_chunks(keep_ref, chunk_ref, far_ref, near_ref, 0, add_halves(down), up[wide:])
 
 
 def curvature_kernel(
@@ -289,11 +300,14 @@
     to_ref,
     tangent_ref,
     arrived_ref,
+    gradient_near_ref,
+    keep_ref,
     chunk_ref,
+    far_ref,
     near_ref,
-    far_ref,
     left_ref,
 ):
+    near_ref[:, 0:1] = gradient_near_ref[...]
     _, _, curvature = token_columns(small_ref, small_other_ref, top)
     tokens, wide = weight_ref.shape
     block = tokens // 2
@@ -305,31 +319,28 @@
     down = dot(left_ref[0], own_ref[...], 0, 0) + dot(left_ref[1], other_ref[...], 0, 0)
     weighted_u = halves(weighted_ref[:, wide:])
     up = add_halves(dot(jnp.concatenate(weighted_u, axis=1), resid[0], 0, 0)) + dot(weighted_u[0], resid[1], 0, 0)
-    put_chunks(chunk_ref, near_ref, far_ref, add_halves(down), up_ref[...] + up)
-
-
-def far_kernel(hidden_width, arrived_ref, chunk_ref, near_ref, _, onward_ref, *out_refs):
-    onward_ref[...] = near_ref[...]
-    count = len(out_refs)
+    put_chunks(keep_ref, chunk_ref, far_ref, near_ref, 1, add_halves(down), up_ref[...] + up)
+
+
+def far_kernel(hidden_width, arrived_ref, chunk_ref, _, *out_refs):
     for place, out_ref in enumerate(out_refs):
         down, up = decode(arrived_ref[place], hidden_width)
-        own = chunk_ref[chunk_ref.shape[0] - count + place]
+        own = chunk_ref[place]
         out_ref[...] = encode(own[:, :hidden_width] + down, own[:, hidden_width:] + up)
 
 
-def near_kernel(
-    hidden_width, gradient_ref, curvature_ref, gradient_chunk_ref, curvature_chunk_ref, _, out_ref, total_ref
-):
-    pairs = ((gradient_ref, gradient_chunk_ref), (curvature_ref, curvature_chunk_ref))
-    for kind, (arrived_ref, chunk_ref) in enumerate(pairs):
-        for place in range(arrived_ref.shape[0]):
-            down, up = decode(arrived_ref[place], hidden_width)
-            own = chunk_ref[place]
-            down, up = own[:, :hidden_width] + down, own[:, hidden_width:] + up
-            if place == 0:
+def near_kernel(hidden_width, gradient_ref, curvature_ref, *rest):
+    arrived_refs, (_, across_ref, total_ref) = rest[:-3], rest[-3:]
+    for kind, keep_ref in enumerate((gradient_ref, curvature_ref)):
+        for x in range(2):
+            down, up = keep_ref[x, :, :hidden_width], keep_ref[x, :, hidden_width:]
+            for ref in arrived_refs:
+                more = decode(ref[kind, x], hidden_width)
+                down, up = down + more[0], up + more[1]
+            if x == 0:
                 total_ref[kind] = jnp.concatenate([down, up], axis=1)
             else:
-                out_ref[place - 1, kind] = encode(down, up)
+                across_ref[kind] = encode(down, up)
 
 
 def add_kernel(hidden_width, *refs):
@@ -339,16 +350,12 @@
     total_ref[:, hidden_width:] = sum(part[1] for part in parts)
 
 
-def total_kernel(hidden_width, own_ref, gradient_ref, curvature_ref, *rest):
-    near_refs, out_refs = rest[:-4], rest[-4:]
+def total_kernel(hidden_width, own_ref, gradient_ref, curvature_ref, across_ref, *out_refs):
     for kind, far_ref in enumerate((gradient_ref, curvature_ref)):
         total = own_ref[kind] + far_ref[...]
-        down, up = total[:, :hidden_width], total[:, hidden_width:]
-        for ref in near_refs:
-            more = decode(ref[kind], hidden_width)
-            down, up = down + more[0], up + more[1]
-        out_refs[2 * kind][...] = down
-        out_refs[2 * kind + 1][...] = up
+        down, up = decode(across_ref[kind], hidden_width)
+        out_refs[2 * kind][...] = total[:, :hidden_width] + down
+        out_refs[2 * kind + 1][...] = total[:, hidden_width:] + up
 
 
 class Ring:
@@ -467,7 +474,6 @@
             10**9,
             [
                 ((tokens * top, tokens), bf16),
-                ((tokens, tokens * top), bf16),
                 ((2, tokens * top, wide), bf16),
                 ((2, tokens, wide), f32),
                 ((2, tokens, wide), f32),
@@ -481,12 +487,13 @@
             exchange(hidden, 1),
             exchange(output_gradient, 1),
             piece,
+            scratch=[pltpu.SemaphoreType.DMA((3,))],
         )
         beside.extend(made)
         return onward
 
     pieces = ring.gather(piece, passing)
-    same, same_turned, mask, local_rank, gate, hidden_other, gradient_other = beside
+    same, mask, local_rank, gate, hidden_other, gradient_other = beside
     capacity_row = jnp.pad(capacity.astype(f32), (counts_lane, lanes - counts_lane - experts))[None, :]
 
     by_offset = pieces[:rows] + [pieces[-2]] + pieces[rows:-2]
@@ -494,16 +501,16 @@
     prior_arrived = exchange(prior, 1)
     factor_halves = [pltpu.VMEM((2, slots, rank, hidden_width), bf16)] * 2
     (reduced,) = call(
-        functools.partial(reduce_kernel, masks),
+        functools.partial(reduce_kernel, top, masks),
         2 * down_multiplies,
         [((2, both, wide), f32)],
         place,
-        same_turned,
-        mask,
+        small,
+        small_other,
         hidden,
         hidden_other,
         *pieces,
-        scratch=factor_halves,
+        scratch=factor_halves + [pltpu.VMEM((2, tokens * top, wide), f32)],
         after=[prior],
     )
     weight, weighted, tangent, coded, high, low = call(
@@ -528,15 +535,18 @@
     )
     arrived = exchange(coded, 1)
     left = [pltpu.VMEM((2, top * tokens, 2 * wide), bf16)]
-    chunks = [
-        ((rows, rank, hidden_width + model_width), f32),
-        ((rows - far, rank, coded_width), i16),
-        ((far, rank, coded_width), i16),
-    ]
-    gradient_own, gradient_near, gradient_far, up, to = call(
+    def chunks(kinds):
+        return [
+            ((2, rank, hidden_width + model_width), f32),
+            ((far, rank, hidden_width + model_width), f32),
+            ((far, rank, coded_width), i16),
+            ((rows - far - 1, kinds, 2, rank, coded_width), i16),
+        ]
+
+    gradient_keep, gradient_chunk, gradient_far, near, up, to = call(
         gradient_kernel,
         down_multiplies + 8 * up_multiplies,
-        chunks + [((wide, model_width), f32), ((both, wide), f32)],
+        chunks(1) + [((wide, model_width), f32), ((both, wide), f32)],
         same,
         mask,
         hidden,
@@ -550,10 +560,10 @@
         scratch=left,
     )
     gradient_far = exchange(gradient_far, 2)
-    curvature_own, curvature_near, curvature_far = call(
+    curvature_keep, curvature_chunk, curvature_far, near = call(
         functools.partial(curvature_kernel, top),
         down_multiplies + 6 * up_multiplies,
-        chunks,
+        chunks(2),
         small,
         small_other,
         same,
@@ -568,22 +578,22 @@
         to,
         tangent,
         arrived,
+        near,
         scratch=left,
     )
 
     hop = 2 * 10**9
 
-    def along_z(arrived, own, near, after):
-        onward, *sums = call(
+    def along_z(arrived, own, after):
+        sums = call(
             functools.partial(far_kernel, hidden_width),
             hop,
-            [(near.shape, i16)] + [((rank, coded_width), i16)] * far,
+            [((rank, coded_width), i16)] * far,
             arrived,
             own,
-            near,
             after=[after],
         )
-        return exchange(onward, 2), sums, [exchange(part, 4 * z) for z, part in zip(range(rows - far, rows), sums)]
+        return sums[0], [exchange(part, 4 * z) for z, part in zip(range(rows - far, rows), sums)]
 
     def added(parts, after):
         return call(
@@ -594,22 +604,21 @@
             after=[after],
         )[0]
 
-    gradient_near, sums, gradient_parts = along_z(gradient_far, gradient_own, gradient_near, curvature_far)
     curvature_far = exchange(curvature_far, 2)
-    curvature_near, sums, curvature_parts = along_z(curvature_far, curvature_own, curvature_near, sums[0])
-    gradient_total = added(gradient_parts, sums[0])
-    near, total = call(
+    near_parts = [exchange(near[z - 1], 4 * z) for z in range(1, rows - far)]
+    done, gradient_parts = along_z(gradient_far, gradient_chunk, near)
+    done, curvature_parts = along_z(curvature_far, curvature_chunk, done)
+    across, total = call(
         functools.partial(near_kernel, hidden_width),
         hop,
-        [((rows - far - 1, 2, rank, coded_width), i16), ((2, rank, hidden_width + model_width), f32)],
-        gradient_near,
-        curvature_near,
-        gradient_own,
-        curvature_own,
-        after=[gradient_total],
-    )
-    near_parts = [exchange(near[z - 1], 4 * z) for z in range(1, rows - far)]
-    curvature_total = added(curvature_parts, near)
+        [((2, rank, coded_width), i16), ((2, rank, hidden_width + model_width), f32)],
+        gradient_keep,
+        curvature_keep,
+        *near_parts,
+        after=[done],
+    )
+    gradient_total = added(gradient_parts, across)
+    curvature_total = added(curvature_parts, gradient_total)
     down_gradient, up_gradient, curvature_down, curvature_up = call(
         functools.partial(total_kernel, hidden_width),
         hop,
@@ -617,7 +626,7 @@
         total,
         gradient_total,
         curvature_total,
-        *near_parts,
+        exchange(across, 2),
     )
     return down_gradient.T[None], up_gradient[None], curvature_down.T[None], curvature_up[None]
 

time: 79.8 us -> 74.5 us (0.934)
  starting transfers between devices: 24.5 us -> 21.3 us
  Pallas kernels: 22 us -> 19.8 us
    ppermute x14 -> x13, starting transfers between devices: 14.5 us -> 12 us  [exchange(): lax.ppermute(value, 'expert', [(device, device ^ mask) for device in rang...]
    pallas_call x13, Pallas kernels: 22 us -> 19.8 us  [call(): pl.pallas_call(kernel, out_shape=[jax.ShapeDtypeStruct(shape, dtype) for...]
    ppermute x14 -> x13, waiting for transfers between devices: 14.7 us -> 14.3 us  [exchange(): lax.ppermute(value, 'expert', [(device, device ^ mask) for device in rang...]
  transfers between devices with their start and end apart: 22 -> 21, of which waited for: 11 -> 12; matrix products, arithmetic and copies ran while one was open for 0% -> 0% of each run, Pallas kernels for 24% -> 23%
where the time goes in v10:
time: 74.5 us; the launch traced here: 74.2 us
  waiting for transfers between devices  31.4 us (42%)
  starting transfers between devices  21.3 us (29%)
  Pallas kernels  19.8 us (27%)
  between operations  0.82 us (1%)
  local copies, waits for them, and re-layouts  0.81 us (1%)
    pallas_call x13, Pallas kernels, call(): pl.pallas_call(kernel, out_shape=[jax.ShapeDtypeStruct(shape, dtype) for...  19.8 us
    ppermute x8, waiting for transfers between devices, shift(): return lax.ppermute(value, 'expert', pairs)  17 us
    ppermute x13, waiting for transfers between devices, exchange(): lax.ppermute(value, 'expert', [(device, device ^ mask) for device in rang...  14.3 us
    ppermute x13, starting transfers between devices, exchange(): lax.ppermute(value, 'expert', [(device, device ^ mask) for device in rang...  12 us
    ppermute x8, starting transfers between devices, shift(): return lax.ppermute(value, 'expert', pairs)  9.26 us
  transfers between devices with their start and end apart: 21, of which 12 were waited for; matrix products, arithmetic and copies ran while one was open for 0% of the time, Pallas kernels for 23%

profile of v10, /device:TPU:0, one launch (start us, length us, event | category | flops | bytes accessed | tf_op | source)
XLA Modules:
  0.0 74.2 jit_solution(6552127719526861539)
XLA Ops:
  1.2 2.0 %shard_map.129 = (s16[2,16,3200]{2,1,0:T(8,128)(2,1)}, f32[24,128]{1,0:T(8,128)}) custom-call(s32[8,128]{1,0:T(8,128)} %bitcast.33, bf16[8,128]{1,0:T(8,128)(2,1)} %bitcast.34, f32[1,128]{1,0:T(1,128)} %bitcast.35, f32[16,1024]{1,0:T(8,128)} %bitcast.31, f32[16,1024]{1,0:T(8,128)} %bitcast.32, f32[16,2048]{1,0:T(8,128)} %bitcast.29, f32[16,2048]{1,0:T(8,128)} %bitcast.30), custom_call_target="tpu_custom_call" | custom-call | flops 200000000 | bytes 1048576 | tf_op jit(solution)/shard_map/pallas_call | solution.py:437
  3.2 3.1 %collective-permute-start.6 = (s16[2,16,3200]{2,1,0:T(8,128)(2,1)}, s16[2,16,3200]{2,1,0:T(8,128)(2,1)S(1)}, u32[]{:S(2)}, u32[]{:S(2)}) collective-permute-start(s16[2,16,3200]{2,1,0:T(8,128)(2,1)} %get-tuple-element.40.rest_0_), channel_id=1, source_target_pairs={{0,4},{1,5},{4,8},{5,9},{8,12},{9,13},{12,14},{13,15},{14,10},{15,... | collective-permute-start | bytes 614408 | tf_op jit(solution)/shard_map/ppermute | solution.py:373
  6.4 5.3 %collective-permute-done.6.rest_7_.rest_6_ = s16[2,16,3200]{2,1,0:T(8,128)(2,1)S(1)} collective-permute-done((s16[2,16,3200]{2,1,0:T(8,128)(2,1)}, s16[2,16,3200]{2,1,0:T(8,128)(2,1)S(1)}, u32[]{:S(2)}, u32[]{:S(2)}) %collective-permute-start.6) | collective-permute-done | bytes 204832 | tf_op jit(solution)/shard_map/ppermute | solution.py:373
  11.7 1.8 %collective-permute-start.7 = (s16[2,16,3200]{2,1,0:T(8,128)(2,1)S(1)}, s16[2,16,3200]{2,1,0:T(8,128)(2,1)S(1)}, u32[]{:S(2)}, u32[]{:S(2)}) collective-permute-start(s16[2,16,3200]{2,1,0:T(8,128)(2,1)S(1)} %collective-permute-done.6.rest_7_.rest_6_), channel_id=1, source_target_pairs={{0,4},{1,5},{4,8},{5,9},{8,12},{9,13},{12,14},{13,15},{14,10},{15,... | collective-permute-start | bytes 614408 | tf_op jit(solution)/shard_map/ppermute | solution.py:373
  14.3 2.4 %shard_map.130 = (bf16[1024,128]{1,0:T(8,128)(2,1)S(1)}, bf16[2,1024,128]{2,1,0:T(8,128)(2,1)S(1)}, f32[2,128,128]{2,1,0:T(8,128)S(1)}, f32[2,128,128]{2,1,0:T(8...) custom-call(s32[17]{0:T(128)S(1)} %pad_add_fusion.place_ref, ...), custom_call_target="tpu_custom_call" | custom-call | flops 2000000000 | bytes 1048576 | tf_op jit(solution)/shard_map/pallas_call | solution.py:437
  17.0 1.3 %collective-permute-done.7.rest_6_.rest_5_ = s16[2,16,3200]{2,1,0:T(8,128)(2,1)S(1)} collective-permute-done((s16[2,16,3200]{2,1,0:T(8,128)(2,1)S(1)}, s16[2,16,3200]{2,1,0:T(8,128)(2,1)S(1)}, u32[]{:S(2)}, u32[]{:S(2)}) %collective-permute-start.7) | collective-permute-done | bytes 204832 | tf_op jit(solution)/shard_map/ppermute | solution.py:373
  18.3 1.5 %collective-permute-start.8 = (s16[2,16,3200]{2,1,0:T(8,128)(2,1)S(1)}, s16[2,16,3200]{2,1,0:T(8,128)(2,1)S(1)}, u32[]{:S(2)}, u32[]{:S(2)}) collective-permute-start(s16[2,16,3200]{2,1,0:T(8,128)(2,1)S(1)} %collective-permute-done.7.rest_6_.rest_5_), channel_id=1, source_target_pairs={{0,4},{1,5},{4,8},{5,9},{8,12},{9,13},{12,14},{13,15},{14,10},{15,... | collective-permute-start | bytes 614408 | tf_op jit(solution)/shard_map/ppermute | solution.py:373
  19.8 2.9 %collective-permute-done.4.rest_2_ = s16[2,16,3200]{2,1,0:T(8,128)(2,1)S(1)} collective-permute-done((s16[2,16,3200]{2,1,0:T(8,128)(2,1)S(1)}, s16[2,16,3200]{2,1,0:T(8,128)(2,1)S(1)}, u32[]{:S(2)}, u32[]{:S(2)}) %collective-permute-start.4) | collective-permute-done | bytes 204832 | tf_op jit(solution)/shard_map/ppermute | solution.py:373
  24.1 1.6 %collective-permute-start.9 = (s16[1,16,3200]{2,1,0:T(8,128)(2,1)S(1)}, s16[1,16,3200]{2,1,0:T(8,128)(2,1)S(1)}, u32[]{:S(2)}, u32[]{:S(2)}) collective-permute-start(s16[1,16,3200]{2,1,0:T(8,128)(2,1)S(1)} %slice.8), channel_id=1, source_target_pairs={{0,4},{1,5},{4,8},{5,9},{8,12},{9,13},{12,14},{13,15},{14,10},{15,... | collective-permute-start | bytes 307208 | tf_op jit(solution)/shard_map/ppermute | solution.py:373
  25.6 3.1 %collective-permute-done.5.rest_3_ = s16[2,16,3200]{2,1,0:T(8,128)(2,1)S(1)} collective-permute-done((s16[2,16,3200]{2,1,0:T(8,128)(2,1)S(1)}, s16[2,16,3200]{2,1,0:T(8,128)(2,1)S(1)}, u32[]{:S(2)}, u32[]{:S(2)}) %collective-permute-start.5) | collective-permute-done | bytes 204832 | tf_op jit(solution)/shard_map/ppermute | solution.py:373
  30.0 3.6 %collective-permute-done.11.rest_8_ = s16[1,16,3200]{2,1,0:T(8,128)(2,1)S(1)} collective-permute-done((s16[1,16,3200]{2,1,0:T(8,128)(2,1)S(1)}, s16[1,16,3200]{2,1,0:T(8,128)(2,1)S(1)}, u32[]{:S(2)}, u32[]{:S(2)}) %collective-permute-start.11) | collective-permute-done | bytes 102432 | tf_op jit(solution)/shard_map/ppermute | solution.py:373
  33.6 3.4 %shard_map.132.reduced_ref = f32[2,256,128]{2,1,0:T(8,128)S(1)} custom-call(s32[17]{0:T(128)S(1)} %pad_add_fusion.place_ref, f32[24,128]{1,0:T(8,128)S(1)} %copy-done.4, f32[24,128]{1,0:T(8,128)S(1)} %collective-permute-done.small_other_ref, bf16[1024,1024]{1,0:T(8,128)(2,1)S(1)} %bitcast.25, bf16[1024,1024]{1,0:T(8,128)(2,1)S(1)} %get-tuple-element.43.other_ref, ...), custom_call_target="tpu_custom_call" | custom-call | flops 2147483648 | bytes 1048576 | tf_op jit(solution)/shard_map/pallas_call | solution.py:437
  37.1 2.2 %shard_map.133 = (f32[256,128]{1,0:T(8,128)S(1)}, f32[256,256]{1,0:T(8,128)S(1)}, f32[256,2048]{1,0:T(8,128)S(1)}, bf16[256,2048]{1,0:T(8,128)(2,1)S(1)}, bf16[2...) custom-call(s32[17]{0:T(128)S(1)} %pad_add_fusion.place_ref, ...), custom_call_target="tpu_custom_call" | custom-call | flops 805306368 | bytes 1048576 | tf_op jit(solution)/shard_map/pallas_call | solution.py:437
  39.4 4.0 %shard_map.134 = (f32[2,16,3072]{2,1,0:T(8,128)S(1)}, f32[2,16,3072]{2,1,0:T(8,128)S(1)}, s16[2,16,3200]{2,1,0:T(8,128)(2,1)S(1)}, s16[1,1,2,16,3200]{4,3,2,1,0:...) custom-call(bf16[1024,128]{1,0:T(8,128)(2,1)S(1)} %get-tuple-element.41.same_ref, ...), custom_call_target="tpu_custom_call" | custom-call | flops 2147483648 | bytes 1048576 | tf_op jit(solution)/shard_map/pallas_call | solution.py:437
  43.8 3.4 %shard_map.135 = (f32[2,16,3072]{2,1,0:T(8,128)S(1)}, f32[2,16,3072]{2,1,0:T(8,128)S(1)}, s16[2,16,3200]{2,1,0:T(8,128)(2,1)S(1)}, s16[1,2,2,16,3200]{4,3,2,1,0:T(8,128)(2,1)S(1)}) custom-call(f32[24,128]{1,0:T(8,128)S(1)} %copy-done.4, f32[24,128]{1,0:T(8,128)S(1)} %collective-permute-done.small_other_ref, ...), custom_call_target="tpu_custom_call" | custom-call | flops 1879048192 | bytes 1048576 | tf_op jit(solution)/shard_map/pallas_call | solution.py:437
  47.2 1.8 %collective-permute-start.14 = (s16[2,16,3200]{2,1,0:T(8,128)(2,1)S(1)}, s16[2,16,3200]{2,1,0:T(8,128)(2,1)S(1)}, u32[]{:S(2)}, u32[]{:S(2)}) collective-permute-start(s16[2,16,3200]{2,1,0:T(8,128)(2,1)S(1)} %get-tuple-element.60), channel_id=1, source_target_pairs={{0,2},{1,3},{2,0},{3,1},{4,6},{5,7},{6,4},{7,5},{8,10},{9,11},{10,... | collective-permute-start | bytes 614408 | tf_op jit(solution)/shard_map/ppermute | solution.py:397
  48.9 1.6 %collective-permute-start.13 = (s16[2,2,16,3200]{3,2,1,0:T(8,128)(2,1)S(1)}, s16[2,2,16,3200]{3,2,1,0:T(8,128)(2,1)S(1)}, u32[]{:S(2)}, u32[]{:S(2)}) collective-permute-start(s16[2,2,16,3200]{3,2,1,0:T(8,128)(2,1)S(1)} %bitcast.28), channel_id=1, source_target_pairs={{0,4},{1,5},{2,6},{3,7},{4,0},{5,1},{6,2},{7,3},{8,12},{9,13},{10,... | collective-permute-start | bytes 1228808 | tf_op jit(solution)/shard_map/ppermute | solution.py:397
  50.5 0.8 %collective-permute-done.15.arrived_ref = s16[2,16,3200]{2,1,0:T(8,128)(2,1)S(1)} collective-permute-done((s16[2,16,3200]{2,1,0:T(8,128)(2,1)S(1)}, s16[2,16,3200]{2,1,0:T(8,128)(2,1)S(1)}, u32[]{:S(2)}, u32[]{:S(2)}) %collective-permute-start.15) | collective-permute-done | bytes 204832 | tf_op jit(solution)/shard_map/ppermute | solution.py:397
  51.6 3.6 %collective-permute-start.17 = (s16[16,3200]{1,0:T(8,128)(2,1)S(1)}, s16[16,3200]{1,0:T(8,128)(2,1)S(1)}, u32[]{:S(2)}, u32[]{:S(2)}) collective-permute-start(s16[16,3200]{1,0:T(8,128)(2,1)S(1)} %get-tuple-element.67), channel_id=1, source_target_pairs={{0,12},{1,13},{2,14},{3,15},{4,8},{5,9},{6,10},{7,11},{8,4},{9,5},... | collective-permute-start | bytes 307208 | tf_op jit(solution)/shard_map/ppermute | solution.py:397
  55.6 3.6 %collective-permute-start.19 = (s16[16,3200]{1,0:T(8,128)(2,1)S(1)}, s16[16,3200]{1,0:T(8,128)(2,1)S(1)}, u32[]{:S(2)}, u32[]{:S(2)}) collective-permute-start(s16[16,3200]{1,0:T(8,128)(2,1)S(1)} %get-tuple-element.69), channel_id=1, source_target_pairs={{0,12},{1,13},{2,14},{3,15},{4,8},{5,9},{6,10},{7,11},{8,4},{9,5},... | collective-permute-start | bytes 307208 | tf_op jit(solution)/shard_map/ppermute | solution.py:397
  59.2 5.1 %collective-permute-done.13.rest_0_ = s16[2,2,16,3200]{3,2,1,0:T(8,128)(2,1)S(1)} collective-permute-done((s16[2,2,16,3200]{3,2,1,0:T(8,128)(2,1)S(1)}, s16[2,2,16,3200]{3,2,1,0:T(8,128)(2,1)S(1)}, u32[]{:S(2)}, u32[]{:S(2)}) %collective-permute-start.13) | collective-permute-done | bytes 409632 | tf_op jit(solution)/shard_map/ppermute | solution.py:397
  65.7 4.3 %collective-permute-done.19.refs_1_ = s16[16,3200]{1,0:T(8,128)(2,1)S(1)} collective-permute-done((s16[16,3200]{1,0:T(8,128)(2,1)S(1)}, s16[16,3200]{1,0:T(8,128)(2,1)S(1)}, u32[]{:S(2)}, u32[]{:S(2)}) %collective-permute-start.19) | collective-permute-done | bytes 102432 | tf_op jit(solution)/shard_map/ppermute | solution.py:397
  70.0 3.2 %collective-permute-done.18.refs_0_ = s16[16,3200]{1,0:T(8,128)(2,1)S(1)} collective-permute-done((s16[16,3200]{1,0:T(8,128)(2,1)S(1)}, s16[16,3200]{1,0:T(8,128)(2,1)S(1)}, u32[]{:S(2)}, u32[]{:S(2)}) %collective-permute-start.18) | collective-permute-done | bytes 102432 | tf_op jit(solution)/shard_map/ppermute | solution.py:397
  73.4 0.8 %shard_map.141 = (f32[16,1024]{1,0:T(8,128)}, f32[16,2048]{1,0:T(8,128)}, f32[16,1024]{1,0:T(8,128)}, f32[16,2048]{1,0:T(8,128)}) custom-call(f32[2,16,3072]{2,1,0:T(8,128)S(1)} %get-tuple-element.66.own_ref, f32[16,3072]{1,0:T(8,128)S(1)} %shard_map.139.refs_2_.gradient_ref, f32[16,3072]{1,0:T(8,128)S(1)} %shard_map.140.curvature_ref, ...), custom_call_target="tpu_custom_call" | custom-call | flops 4000000000 | bytes 1048576 | tf_op jit(solution)/shard_map/pallas_call | solution.py:437
  (49 shorter events, 6.9 us)
Async XLA Ops:
  0.6 13.0 %collective-permute-start.1 = (bf16[1024,1024]{1,0:T(8,128)(2,1)}, bf16[1024,1024]{1,0:T(8,128)(2,1)S(1)}, u32[]{:S(2)}, u32[]{:S(2)}) collective-permute-start(bf16[1024,1024]{1,0:T(8,128)(2,1)} %bitcast.24), channel_id=1, source_target_pairs={{0,1},{1,0},{2,3},{3,2},{4,5},{5,4},{6,7},{7,6},{8,9},{9,8},{10,11... | collective-permute-start | bytes 6291464 | tf_op jit(solution)/shard_map/ppermute | solution.py:397
  1.2 12.4 %collective-permute-start.2 = (bf16[128,2048]{1,0:T(8,128)(2,1)}, bf16[128,2048]{1,0:T(8,128)(2,1)S(1)}, u32[]{:S(2)}, u32[]{:S(2)}) collective-permute-start(bf16[128,2048]{1,0:T(8,128)(2,1)} %own_gradient_ref.1), channel_id=1, source_target_pairs={{0,1},{1,0},{2,3},{3,2},{4,5},{5,4},{6,7},{7,6},{8,9},{9,8},{10,11... | collective-permute-start | bytes 1572872 | tf_op jit(solution)/shard_map/ppermute | solution.py:397
  3.2 8.5 %collective-permute-start.6 = (s16[2,16,3200]{2,1,0:T(8,128)(2,1)}, s16[2,16,3200]{2,1,0:T(8,128)(2,1)S(1)}, u32[]{:S(2)}, u32[]{:S(2)}) collective-permute-start(s16[2,16,3200]{2,1,0:T(8,128)(2,1)} %get-tuple-element.40.rest_0_), channel_id=1, source_target_pairs={{0,4},{1,5},{4,8},{5,9},{8,12},{9,13},{12,14},{13,15},{14,10},{15,... | collective-permute-start | bytes 614408 | tf_op jit(solution)/shard_map/ppermute | solution.py:373
  6.3 7.3 %collective-permute-start.3 = (s16[2,16,3200]{2,1,0:T(8,128)(2,1)}, s16[2,16,3200]{2,1,0:T(8,128)(2,1)S(1)}, u32[]{:S(2)}, u32[]{:S(2)}) collective-permute-start(s16[2,16,3200]{2,1,0:T(8,128)(2,1)} %get-tuple-element.40.rest_0_), channel_id=1, source_target_pairs={{0,2},{1,3},{4,0},{5,1},{8,4},{9,5},{12,8},{13,9},{14,12},{15,13},... | collective-permute-start | bytes 614408 | tf_op jit(solution)/shard_map/ppermute | solution.py:373
  6.3 7.3 %collective-permute-start = (f32[24,128]{1,0:T(8,128)}, f32[24,128]{1,0:T(8,128)S(1)}, u32[]{:S(2)}, u32[]{:S(2)}) collective-permute-start(f32[24,128]{1,0:T(8,128)} %get-tuple-element.39.small_ref), channel_id=1, source_target_pairs={{0,1},{1,0},{2,3},{3,2},{4,5},{5,4},{6,7},{7,6},{8,9},{9,8},{10,11... | collective-permute-start | bytes 36872 | tf_op jit(solution)/shard_map/ppermute | solution.py:397
  6.4 22.9 %copy-start.2 = (s16[2,16,3200]{2,1,0:T(8,128)(2,1)S(1)}, s16[2,16,3200]{2,1,0:T(8,128)(2,1)}, u32[]{:S(2)}) copy-start(s16[2,16,3200]{2,1,0:T(8,128)(2,1)} %get-tuple-element.40.rest_0_) | copy-start | bytes 614404
  6.4 27.2 %copy-start = (bf16[128,8,1024]{2,1,0:T(8,128)(2,1)S(1)}, bf16[128,8,1024]{2,1,0:T(8,128)(2,1)}, u32[]{:S(2)}) copy-start(bf16[128,8,1024]{2,1,0:T(8,128)(2,1)} %param.10) | copy-start | bytes 6291460
  11.7 6.5 %collective-permute-start.7 = (s16[2,16,3200]{2,1,0:T(8,128)(2,1)S(1)}, s16[2,16,3200]{2,1,0:T(8,128)(2,1)S(1)}, u32[]{:S(2)}, u32[]{:S(2)}) collective-permute-start(s16[2,16,3200]{2,1,0:T(8,128)(2,1)S(1)} %collective-permute-done.6.rest_7_.rest_6_), channel_id=1, source_target_pairs={{0,4},{1,5},{4,8},{5,9},{8,12},{9,13},{12,14},{13,15},{14,10},{15,... | collective-permute-start | bytes 614408 | tf_op jit(solution)/shard_map/ppermute | solution.py:373
  14.3 19.3 %copy-start.4 = (f32[24,128]{1,0:T(8,128)S(1)}, f32[24,128]{1,0:T(8,128)}, u32[]{:S(2)}) copy-start(f32[24,128]{1,0:T(8,128)} %get-tuple-element.39.small_ref) | copy-start | bytes 36868
  16.7 6.0 %collective-permute-start.4 = (s16[2,16,3200]{2,1,0:T(8,128)(2,1)S(1)}, s16[2,16,3200]{2,1,0:T(8,128)(2,1)S(1)}, u32[]{:S(2)}, u32[]{:S(2)}) collective-permute-start(s16[2,16,3200]{2,1,0:T(8,128)(2,1)S(1)} %get-tuple-element.47.rest_1_), channel_id=1, source_target_pairs={{0,2},{1,3},{4,0},{5,1},{8,4},{9,5},{12,8},{13,9},{14,12},{15,13},... | collective-permute-start | bytes 614408 | tf_op jit(solution)/shard_map/ppermute | solution.py:373
  18.3 5.8 %collective-permute-start.8 = (s16[2,16,3200]{2,1,0:T(8,128)(2,1)S(1)}, s16[2,16,3200]{2,1,0:T(8,128)(2,1)S(1)}, u32[]{:S(2)}, u32[]{:S(2)}) collective-permute-start(s16[2,16,3200]{2,1,0:T(8,128)(2,1)S(1)} %collective-permute-done.7.rest_6_.rest_5_), channel_id=1, source_target_pairs={{0,4},{1,5},{4,8},{5,9},{8,12},{9,13},{12,14},{13,15},{14,10},{15,... | collective-permute-start | bytes 614408 | tf_op jit(solution)/shard_map/ppermute | solution.py:373
  22.7 6.0 %collective-permute-start.5 = (s16[2,16,3200]{2,1,0:T(8,128)(2,1)S(1)}, s16[2,16,3200]{2,1,0:T(8,128)(2,1)S(1)}, u32[]{:S(2)}, u32[]{:S(2)}) collective-permute-start(s16[2,16,3200]{2,1,0:T(8,128)(2,1)S(1)} %collective-permute-done.4.rest_2_), channel_id=1, source_target_pairs={{0,2},{1,3},{4,0},{5,1},{8,4},{9,5},{12,8},{13,9},{14,12},{15,13},... | collective-permute-start | bytes 614408 | tf_op jit(solution)/shard_map/ppermute | solution.py:373
  24.1 5.3 %collective-permute-start.9 = (s16[1,16,3200]{2,1,0:T(8,128)(2,1)S(1)}, s16[1,16,3200]{2,1,0:T(8,128)(2,1)S(1)}, u32[]{:S(2)}, u32[]{:S(2)}) collective-permute-start(s16[1,16,3200]{2,1,0:T(8,128)(2,1)S(1)} %slice.8), channel_id=1, source_target_pairs={{0,4},{1,5},{4,8},{5,9},{8,12},{9,13},{12,14},{13,15},{14,10},{15,... | collective-permute-start | bytes 307208 | tf_op jit(solution)/shard_map/ppermute | solution.py:373
  28.7 4.9 %collective-permute-start.11 = (s16[1,16,3200]{2,1,0:T(8,128)(2,1)S(1)}, s16[1,16,3200]{2,1,0:T(8,128)(2,1)S(1)}, u32[]{:S(2)}, u32[]{:S(2)}) collective-permute-start(s16[1,16,3200]{2,1,0:T(8,128)(2,1)S(1)} %slice.9), channel_id=1, source_target_pairs={{0,2},{1,3},{4,0},{5,1},{8,4},{9,5},{12,8},{13,9},{14,12},{15,13},... | collective-permute-start | bytes 307208 | tf_op jit(solution)/shard_map/ppermute | solution.py:373
  29.9 7.2 %collective-permute-start.10 = (f32[8,128]{1,0:T(8,128)S(1)}, f32[8,128]{1,0:T(8,128)S(1)}, u32[]{:S(2)}, u32[]{:S(2)}) collective-permute-start(f32[8,128]{1,0:T(8,128)S(1)} %shard_map.131.rest_9_.prior_ref), channel_id=1, source_target_pairs={{0,1},{1,0},{2,3},{3,2},{4,5},{5,4},{6,7},{7,6},{8,9},{9,8},{10,11... | collective-permute-start | bytes 12296 | tf_op jit(solution)/shard_map/ppermute | solution.py:397
  39.3 4.5 %collective-permute-start.12 = (bf16[256,2048]{1,0:T(8,128)(2,1)S(1)}, bf16[256,2048]{1,0:T(8,128)(2,1)S(1)}, u32[]{:S(2)}, u32[]{:S(2)}) collective-permute-start(bf16[256,2048]{1,0:T(8,128)(2,1)S(1)} %get-tuple-element.56), channel_id=1, source_target_pairs={{0,1},{1,0},{2,3},{3,2},{4,5},{5,4},{6,7},{7,6},{8,9},{9,8},{10,11... | collective-permute-start | bytes 3145736 | tf_op jit(solution)/shard_map/ppermute | solution.py:397
  43.4 7.9 %collective-permute-start.15 = (s16[2,16,3200]{2,1,0:T(8,128)(2,1)S(1)}, s16[2,16,3200]{2,1,0:T(8,128)(2,1)S(1)}, u32[]{:S(2)}, u32[]{:S(2)}) collective-permute-start(s16[2,16,3200]{2,1,0:T(8,128)(2,1)S(1)} %get-tuple-element.62), channel_id=1, source_target_pairs={{0,2},{1,3},{2,0},{3,1},{4,6},{5,7},{6,4},{7,5},{8,10},{9,11},{10,... | collective-permute-start | bytes 614408 | tf_op jit(solution)/shard_map/ppermute | solution.py:397
  47.2 8.2 %collective-permute-start.14 = (s16[2,16,3200]{2,1,0:T(8,128)(2,1)S(1)}, s16[2,16,3200]{2,1,0:T(8,128)(2,1)S(1)}, u32[]{:S(2)}, u32[]{:S(2)}) collective-permute-start(s16[2,16,3200]{2,1,0:T(8,128)(2,1)S(1)} %get-tuple-element.60), channel_id=1, source_target_pairs={{0,2},{1,3},{2,0},{3,1},{4,6},{5,7},{6,4},{7,5},{8,10},{9,11},{10,... | collective-permute-start | bytes 614408 | tf_op jit(solution)/shard_map/ppermute | solution.py:397
  48.9 15.3 %collective-permute-start.13 = (s16[2,2,16,3200]{3,2,1,0:T(8,128)(2,1)S(1)}, s16[2,2,16,3200]{3,2,1,0:T(8,128)(2,1)S(1)}, u32[]{:S(2)}, u32[]{:S(2)}) collective-permute-start(s16[2,2,16,3200]{3,2,1,0:T(8,128)(2,1)S(1)} %bitcast.28), channel_id=1, source_target_pairs={{0,4},{1,5},{2,6},{3,7},{4,0},{5,1},{6,2},{7,3},{8,12},{9,13},{10,... | collective-permute-start | bytes 1228808 | tf_op jit(solution)/shard_map/ppermute | solution.py:397
  51.6 14.0 %collective-permute-start.17 = (s16[16,3200]{1,0:T(8,128)(2,1)S(1)}, s16[16,3200]{1,0:T(8,128)(2,1)S(1)}, u32[]{:S(2)}, u32[]{:S(2)}) collective-permute-start(s16[16,3200]{1,0:T(8,128)(2,1)S(1)} %get-tuple-element.67), channel_id=1, source_target_pairs={{0,12},{1,13},{2,14},{3,15},{4,8},{5,9},{6,10},{7,11},{8,4},{9,5},... | collective-permute-start | bytes 307208 | tf_op jit(solution)/shard_map/ppermute | solution.py:397
  55.2 10.5 %collective-permute-start.16 = (s16[16,3200]{1,0:T(8,128)(2,1)S(1)}, s16[16,3200]{1,0:T(8,128)(2,1)S(1)}, u32[]{:S(2)}, u32[]{:S(2)}) collective-permute-start(s16[16,3200]{1,0:T(8,128)(2,1)S(1)} %get-tuple-element.64._), channel_id=1, source_target_pairs={{0,8},{1,9},{2,10},{3,11},{4,12},{5,13},{6,14},{7,15},{8,0},{9,1},... | collective-permute-start | bytes 307208 | tf_op jit(solution)/shard_map/ppermute | solution.py:397
  55.6 14.4 %collective-permute-start.19 = (s16[16,3200]{1,0:T(8,128)(2,1)S(1)}, s16[16,3200]{1,0:T(8,128)(2,1)S(1)}, u32[]{:S(2)}, u32[]{:S(2)}) collective-permute-start(s16[16,3200]{1,0:T(8,128)(2,1)S(1)} %get-tuple-element.69), channel_id=1, source_target_pairs={{0,12},{1,13},{2,14},{3,15},{4,8},{5,9},{6,10},{7,11},{8,4},{9,5},... | collective-permute-start | bytes 307208 | tf_op jit(solution)/shard_map/ppermute | solution.py:397
  59.2 14.1 %collective-permute-start.18 = (s16[16,3200]{1,0:T(8,128)(2,1)S(1)}, s16[16,3200]{1,0:T(8,128)(2,1)S(1)}, u32[]{:S(2)}, u32[]{:S(2)}) collective-permute-start(s16[16,3200]{1,0:T(8,128)(2,1)S(1)} %get-tuple-element.65.rest_1_), channel_id=1, source_target_pairs={{0,8},{1,9},{2,10},{3,11},{4,12},{5,13},{6,14},{7,15},{8,0},{9,1},... | collective-permute-start | bytes 307208 | tf_op jit(solution)/shard_map/ppermute | solution.py:397
  64.5 8.8 %collective-permute-start.20 = (s16[2,16,3200]{2,1,0:T(8,128)(2,1)S(1)}, s16[2,16,3200]{2,1,0:T(8,128)(2,1)S(1)}, u32[]{:S(2)}, u32[]{:S(2)}) collective-permute-start(s16[2,16,3200]{2,1,0:T(8,128)(2,1)S(1)} %get-tuple-element.68.refs_2_), channel_id=1, source_target_pairs={{0,2},{1,3},{2,0},{3,1},{4,6},{5,7},{6,4},{7,5},{8,10},{9,11},{10,... | collective-permute-start | bytes 614408 | tf_op jit(solution)/shard_map/ppermute | solution.py:397
  (3 other events, 20.0 us)

commit v11 on v10

--- a/solution.py
+++ b/solution.py
@@ -76,11 +76,10 @@
     piece_ref[1] = encode(adapter_down, up_direction, counts)
 
 
-def token_columns(own_ref, other_ref, top):
-    small = jnp.concatenate([own_ref[...], other_ref[...]], axis=1).T
-    experts = [small[:, k : k + 1] for k in range(top)]
-    gates = [small[:, top + k : top + k + 1] for k in range(top)]
-    return experts, gates, small[:, 2 * top : 2 * top + 1]
+def token_columns(small_ref, top):
+    experts = [small_ref[:, k : k + 1] for k in range(top)]
+    gates = [small_ref[:, top + k : top + k + 1] for k in range(top)]
+    return experts, gates, small_ref[:, 2 * top : 2 * top + 1]
 
 
 def members(place_ref, wide, masks):
@@ -114,46 +113,31 @@
     return refs[offset if offset < half else offset - 1][kind]
 
 
-def rows_kernel(top, masks, place_ref, small_ref, small_other_ref, hidden_other_ref, gradient_other_ref, piece_ref, *outs):
-    same_ref, mask_ref, rank_ref, gate_ref, hidden_ref, gradient_ref, onward_ref, sem = outs
-    copies = [
-        pltpu.make_async_copy(hidden_other_ref, hidden_ref, sem.at[0]),
-        pltpu.make_async_copy(gradient_other_ref, gradient_ref, sem.at[1]),
-        pltpu.make_async_copy(piece_ref, onward_ref, sem.at[2]),
-    ]
-    for copy in copies:
-        copy.start()
-    rows, tokens = same_ref.shape
-    wide = mask_ref.shape[2]
-    row = lax.broadcasted_iota(jnp.int32, (rows, tokens), 0)
-    same = jnp.where(row // top == lax.broadcasted_iota(jnp.int32, (rows, tokens), 1), 1.0, 0.0).astype(bf16)
-    same_ref[...] = same
+def tokens_kernel(top, masks, place_ref, own_ref, other_ref, piece_ref, *rest):
+    small_ref, rank_ref, gate_ref, onward_ref = rest[-4:]
+    onward_ref[...] = piece_ref[...]
+    small_ref[...] = jnp.concatenate([own_ref[...], other_ref[...]], axis=1).T
+    experts, gates, _ = token_columns(small_ref, top)
+    _, tokens, wide = rank_ref.shape
     column = members(place_ref, wide, masks)
     below = (
         lax.broadcasted_iota(jnp.int32, (tokens, tokens), 0)
         > lax.broadcasted_iota(jnp.int32, (tokens, tokens), 1)
     )
     below = jnp.where(below, 1.0, 0.0).astype(bf16)
-    for core, ref in enumerate((small_ref, small_other_ref)):
-        small = ref[...].T
-        experts = dot(same, small.astype(bf16), 1, 0)
-        position = lax.broadcasted_iota(jnp.int32, experts.shape, 0) % top
-        own = lax.broadcasted_iota(jnp.int32, experts.shape, 1) == position
-        expert = jnp.sum(jnp.where(own, experts, 0.0), axis=1, keepdims=True)
-        mask_ref[core] = jnp.where(expert == column, 1.0, 0.0).astype(bf16)
+    for core in range(2):
+        tokens_of = slice(core * tokens, (core + 1) * tokens)
         gate = jnp.zeros((tokens, wide), f32)
         member = jnp.zeros((tokens, wide), f32)
         for k in range(top):
-            named = small[:, k : k + 1] == column
-            gate = jnp.where(named, small[:, top + k : top + k + 1], gate)
+            named = experts[k][tokens_of] == column
+            gate = jnp.where(named, gates[k][tokens_of], gate)
             member = jnp.where(named, 1.0, member)
         gate_ref[core] = gate
         rank_ref[core] = dot(below, member.astype(bf16), 1, 0)
-    for copy in copies:
-        copy.wait()
-
-
-def reduce_kernel(top, masks, place_ref, small_ref, small_other_ref, own_ref, other_ref, *rest):
+
+
+def reduce_kernel(top, masks, place_ref, small_ref, own_ref, other_ref, *rest):
     slots = len(masks)
     piece_refs, (_, reduced_ref, high_ref, low_ref, full_ref) = rest[: slots + 1], rest[slots + 1 :]
     hidden_width = own_ref.shape[1]
@@ -162,7 +146,7 @@
         for kind in range(2):
             down, _ = decode(piece_part(piece_refs, offset, kind), hidden_width)
             high_ref[kind, slot], low_ref[kind, slot] = halves(down)
-    experts, _, _ = token_columns(small_ref, small_other_ref, top)
+    experts, _, _ = token_columns(small_ref, top)
     wide = reduced_ref.shape[2]
     column = members(place_ref, wide, masks)
     high = high_ref[...].reshape(2 * wide, hidden_width)
@@ -220,13 +204,16 @@
     coded_ref[...] = tangent.astype(bf16)
 
 
-def put_left(left_ref, same_ref, mask_ref, terms):
-    both = jnp.concatenate(halves(terms), axis=1)
-    tokens = terms.shape[0] // 2
+def put_left(left_ref, wide_ref, top, masks, place_ref, small_ref, terms):
+    experts, _, _ = token_columns(small_ref, top)
+    tokens, wide = terms.shape[0] // 2, terms.shape[1]
+    column = members(place_ref, wide, masks)
     for core in range(2):
-        repeated = dot(same_ref[...], both[core * tokens : (core + 1) * tokens], 1, 0).astype(bf16)
-        mask = mask_ref[core]
-        left_ref[core] = repeated * jnp.concatenate([mask, mask], axis=1)
+        tokens_of = slice(core * tokens, (core + 1) * tokens)
+        for k in range(top):
+            named = experts[k][tokens_of] == column
+            wide_ref[core, pl.ds(k, tokens, stride=top), :] = jnp.where(named, terms[tokens_of], 0.0)
+        left_ref[core] = jnp.concatenate(halves(wide_ref[core]), axis=1)
 
 
 def add_halves(both):
@@ -235,7 +222,7 @@
 
 
 def put_chunks(keep_ref, chunk_ref, far_ref, near_ref, kind, down, up):
-    far, rank, _ = chunk_ref.shape
+    rank = keep_ref.shape[1]
     rows = down.shape[0] // rank // 2
 
     def slot(number):
@@ -244,16 +231,16 @@
 
     for x in range(2):
         keep_ref[x] = jnp.concatenate(slot(x * rows), axis=1)
-        for z in range(1, rows - far):
-            near_ref[z - 1, kind, x] = encode(*slot(x * rows + z))
-    for place in range(far):
-        chunk_ref[place] = jnp.concatenate(slot(rows - far + place), axis=1)
-        far_ref[place] = encode(*slot(2 * rows - far + place))
+        chunk_ref[x] = jnp.concatenate(slot(x * rows + 2), axis=1)
+        far_ref[x] = encode(*slot(x * rows + 3))
+        near_ref[kind, x] = encode(*slot(x * rows + 1))
 
 
 def gradient_kernel(
-    same_ref,
-    mask_ref,
+    top,
+    masks,
+    place_ref,
+    small_ref,
     own_ref,
     other_ref,
     own_gradient_ref,
@@ -269,6 +256,7 @@
     up_ref,
     to_ref,
     left_ref,
+    wide_ref,
 ):
     wide = weight_ref.shape[1]
     model_width = up_ref.shape[1]
@@ -277,7 +265,7 @@
     low = low_ref[...].reshape(2 * wide, model_width)
     to_both = dot(gradient, high, 1, 1) + dot(gradient, low, 1, 1)
     to_ref[...] = to_both[:, wide:]
-    put_left(left_ref, same_ref, mask_ref, weight_ref[...] * to_both[:, :wide])
+    put_left(left_ref, wide_ref, top, masks, place_ref, small_ref, weight_ref[...] * to_both[:, :wide])
     down = dot(left_ref[0], own_ref[...], 0, 0) + dot(left_ref[1], other_ref[...], 0, 0)
     up = add_halves(dot(jnp.concatenate(halves(weighted_ref[...]), axis=1), gradient, 0, 0))
     up_ref[...] = up[:wide]
@@ -286,10 +274,9 @@
 
 def curvature_kernel(
     top,
+    masks,
+    place_ref,
     small_ref,
-    small_other_ref,
-    same_ref,
-    mask_ref,
     own_ref,
     other_ref,
     weight_ref,
@@ -306,56 +293,66 @@
     far_ref,
     near_ref,
     left_ref,
+    wide_ref,
 ):
-    near_ref[:, 0:1] = gradient_near_ref[...]
-    _, _, curvature = token_columns(small_ref, small_other_ref, top)
+    near_ref[0:1] = gradient_near_ref[...]
+    _, _, curvature = token_columns(small_ref, top)
     tokens, wide = weight_ref.shape
     block = tokens // 2
     model_width = up_ref.shape[1]
     arrived = jnp.concatenate([arrived_ref[block:], arrived_ref[:block]], axis=0).astype(f32)
     resid = halves(curvature * (tangent_ref[...] + arrived))
     adapter_up = high_ref[0].reshape(wide, model_width), low_ref[0].reshape(wide, model_width)
-    put_left(left_ref, same_ref, mask_ref, weight_ref[...] * (dot_pairs(resid, adapter_up, 1, 1) + to_ref[...]))
+    terms = weight_ref[...] * (dot_pairs(resid, adapter_up, 1, 1) + to_ref[...])
+    put_left(left_ref, wide_ref, top, masks, place_ref, small_ref, terms)
     down = dot(left_ref[0], own_ref[...], 0, 0) + dot(left_ref[1], other_ref[...], 0, 0)
     weighted_u = halves(weighted_ref[:, wide:])
     up = add_halves(dot(jnp.concatenate(weighted_u, axis=1), resid[0], 0, 0)) + dot(weighted_u[0], resid[1], 0, 0)
     put_chunks(keep_ref, chunk_ref, far_ref, near_ref, 1, add_halves(down), up_ref[...] + up)
 
 
-def far_kernel(hidden_width, arrived_ref, chunk_ref, _, *out_refs):
-    for place, out_ref in enumerate(out_refs):
-        down, up = decode(arrived_ref[place], hidden_width)
-        own = chunk_ref[place]
-        out_ref[...] = encode(own[:, :hidden_width] + down, own[:, hidden_width:] + up)
-
-
-def near_kernel(hidden_width, gradient_ref, curvature_ref, *rest):
-    arrived_refs, (_, across_ref, total_ref) = rest[:-3], rest[-3:]
+def pair_kernel(hidden_width, arrived_ref, chunk_ref, _, across_ref, keep_ref):
+    for x in range(2):
+        down, up = decode(arrived_ref[x], hidden_width)
+        down, up = chunk_ref[x, :, :hidden_width] + down, chunk_ref[x, :, hidden_width:] + up
+        if x == 0:
+            keep_ref[...] = jnp.concatenate([down, up], axis=1)
+        else:
+            across_ref[...] = encode(down, up)
+
+
+def far_kernel(hidden_width, arrived_ref, keep_ref, _, out_ref):
+    down, up = decode(arrived_ref[...], hidden_width)
+    out_ref[...] = encode(keep_ref[:, :hidden_width] + down, keep_ref[:, hidden_width:] + up)
+
+
+def near_kernel(hidden_width, arrived_ref, gradient_ref, curvature_ref, _, across_ref, total_ref):
     for kind, keep_ref in enumerate((gradient_ref, curvature_ref)):
         for x in range(2):
-            down, up = keep_ref[x, :, :hidden_width], keep_ref[x, :, hidden_width:]
-            for ref in arrived_refs:
-                more = decode(ref[kind, x], hidden_width)
-                down, up = down + more[0], up + more[1]
+            down, up = decode(arrived_ref[kind, x], hidden_width)
+            down, up = keep_ref[x, :, :hidden_width] + down, keep_ref[x, :, hidden_width:] + up
             if x == 0:
                 total_ref[kind] = jnp.concatenate([down, up], axis=1)
             else:
                 across_ref[kind] = encode(down, up)
 
 
-def add_kernel(hidden_width, *refs):
-    coded_refs, total_ref = refs[:-2], refs[-1]
-    parts = [decode(ref[...], hidden_width) for ref in coded_refs]
-    total_ref[:, :hidden_width] = sum(part[0] for part in parts)
-    total_ref[:, hidden_width:] = sum(part[1] for part in parts)
-
-
-def total_kernel(hidden_width, own_ref, gradient_ref, curvature_ref, across_ref, *out_refs):
-    for kind, far_ref in enumerate((gradient_ref, curvature_ref)):
-        total = own_ref[kind] + far_ref[...]
+def add_kernel(hidden_width, total_ref, arrived_ref, _, out_ref):
+    down, up = decode(arrived_ref[...], hidden_width)
+    out_ref[:, :hidden_width] = total_ref[0, :, :hidden_width] + down
+    out_ref[:, hidden_width:] = total_ref[0, :, hidden_width:] + up
+
+
+def total_kernel(hidden_width, gradient_ref, total_ref, far_ref, across_ref, *out_refs):
+    far = decode(far_ref[...], hidden_width)
+    totals = [
+        (gradient_ref[:, :hidden_width], gradient_ref[:, hidden_width:]),
+        (total_ref[1, :, :hidden_width] + far[0], total_ref[1, :, hidden_width:] + far[1]),
+    ]
+    for kind in range(2):
         down, up = decode(across_ref[kind], hidden_width)
-        out_refs[2 * kind][...] = total[:, :hidden_width] + down
-        out_refs[2 * kind + 1][...] = total[:, hidden_width:] + up
+        out_refs[2 * kind][...] = totals[kind][0] + down
+        out_refs[2 * kind + 1][...] = totals[kind][1] + up
 
 
 class Ring:
@@ -412,7 +409,6 @@
     ring = Ring(lax.axis_size("expert"))
     slots = ring.length
     rows = slots // 2
-    far = rows // 2
     masks = [4 * z for z in range(rows)] + [4 * z + 2 for z in range(rows)]
     me = lax.axis_index("expert")
     tokens, top = expert_of_route.shape
@@ -468,32 +464,30 @@
     hidden = hidden_of_route.reshape(tokens * top, hidden_width)
     beside = []
 
+    hidden_other = exchange(hidden, 1)
+    gradient_other = exchange(output_gradient, 1)
+
     def passing(piece):
         *made, onward = call(
-            functools.partial(rows_kernel, top, masks),
+            functools.partial(tokens_kernel, top, masks),
             10**9,
             [
-                ((tokens * top, tokens), bf16),
-                ((2, tokens * top, wide), bf16),
+                ((both, small.shape[0]), f32),
                 ((2, tokens, wide), f32),
                 ((2, tokens, wide), f32),
-                ((tokens * top, hidden_width), bf16),
-                ((tokens, model_width), bf16),
                 (piece.shape, i16),
             ],
             place,
             small,
             small_other,
-            exchange(hidden, 1),
-            exchange(output_gradient, 1),
             piece,
-            scratch=[pltpu.SemaphoreType.DMA((3,))],
+            after=[hidden_other, gradient_other],
         )
         beside.extend(made)
         return onward
 
     pieces = ring.gather(piece, passing)
-    same, mask, local_rank, gate, hidden_other, gradient_other = beside
+    small_columns, local_rank, gate = beside
     capacity_row = jnp.pad(capacity.astype(f32), (counts_lane, lanes - counts_lane - experts))[None, :]
 
     by_offset = pieces[:rows] + [pieces[-2]] + pieces[rows:-2]
@@ -505,8 +499,7 @@
         2 * down_multiplies,
         [((2, both, wide), f32)],
         place,
-        small,
-        small_other,
+        small_columns,
         hidden,
         hidden_other,
         *pieces,
@@ -534,21 +527,21 @@
         *pieces,
     )
     arrived = exchange(coded, 1)
-    left = [pltpu.VMEM((2, top * tokens, 2 * wide), bf16)]
+    left = [pltpu.VMEM((2, top * tokens, 2 * wide), bf16), pltpu.VMEM((2, top * tokens, wide), f32)]
     def chunks(kinds):
         return [
             ((2, rank, hidden_width + model_width), f32),
-            ((far, rank, hidden_width + model_width), f32),
-            ((far, rank, coded_width), i16),
-            ((rows - far - 1, kinds, 2, rank, coded_width), i16),
+            ((2, rank, hidden_width + model_width), f32),
+            ((2, rank, coded_width), i16),
+            ((kinds, 2, rank, coded_width), i16),
         ]
 
     gradient_keep, gradient_chunk, gradient_far, near, up, to = call(
-        gradient_kernel,
+        functools.partial(gradient_kernel, top, masks),
         down_multiplies + 8 * up_multiplies,
         chunks(1) + [((wide, model_width), f32), ((both, wide), f32)],
-        same,
-        mask,
+        place,
+        small_columns,
         hidden,
         hidden_other,
         output_gradient,
@@ -559,15 +552,13 @@
         low,
         scratch=left,
     )
-    gradient_far = exchange(gradient_far, 2)
+    gradient_far = exchange(gradient_far, 4)
     curvature_keep, curvature_chunk, curvature_far, near = call(
-        functools.partial(curvature_kernel, top),
+        functools.partial(curvature_kernel, top, masks),
         down_multiplies + 6 * up_multiplies,
         chunks(2),
-        small,
-        small_other,
-        same,
-        mask,
+        place,
+        small_columns,
         hidden,
         hidden_other,
         weight,
@@ -584,49 +575,44 @@
 
     hop = 2 * 10**9
 
-    def along_z(arrived, own, after):
-        sums = call(
-            functools.partial(far_kernel, hidden_width),
-            hop,
-            [((rank, coded_width), i16)] * far,
-            arrived,
-            own,
-            after=[after],
-        )
-        return sums[0], [exchange(part, 4 * z) for z, part in zip(range(rows - far, rows), sums)]
-
-    def added(parts, after):
-        return call(
-            functools.partial(add_kernel, hidden_width),
-            hop,
-            [((rank, hidden_width + model_width), f32)],
-            *parts,
-            after=[after],
-        )[0]
-
-    curvature_far = exchange(curvature_far, 2)
-    near_parts = [exchange(near[z - 1], 4 * z) for z in range(1, rows - far)]
-    done, gradient_parts = along_z(gradient_far, gradient_chunk, near)
-    done, curvature_parts = along_z(curvature_far, curvature_chunk, done)
-    across, total = call(
-        functools.partial(near_kernel, hidden_width),
-        hop,
-        [((2, rank, coded_width), i16), ((2, rank, hidden_width + model_width), f32)],
+    one = (rank, hidden_width + model_width)
+    one_coded = (rank, coded_width)
+
+    def hop_call(kernel, outs, *operands, after=()):
+        return call(functools.partial(kernel, hidden_width), hop, outs, *operands, after=after)
+
+    curvature_far = exchange(curvature_far, 4)
+    near_arrived = exchange(near, 4)
+    gradient_across, gradient_pair = hop_call(
+        pair_kernel, [(one_coded, i16), (one, f32)], gradient_far, gradient_chunk, after=[near]
+    )
+    curvature_across, curvature_pair = hop_call(
+        pair_kernel, [(one_coded, i16), (one, f32)], curvature_far, curvature_chunk, after=[gradient_across]
+    )
+    (gradient_beyond,) = hop_call(
+        far_kernel, [(one_coded, i16)], exchange(gradient_across, 2), gradient_pair, after=[curvature_across]
+    )
+    (curvature_beyond,) = hop_call(
+        far_kernel, [(one_coded, i16)], exchange(curvature_across, 2), curvature_pair, after=[gradient_beyond]
+    )
+    near_across, total = hop_call(
+        near_kernel,
+        [((2,) + one_coded, i16), ((2,) + one, f32)],
+        near_arrived,
         gradient_keep,
         curvature_keep,
-        *near_parts,
-        after=[done],
-    )
-    gradient_total = added(gradient_parts, across)
-    curvature_total = added(curvature_parts, gradient_total)
-    down_gradient, up_gradient, curvature_down, curvature_up = call(
-        functools.partial(total_kernel, hidden_width),
-        hop,
+        after=[curvature_beyond],
+    )
+    (gradient_total,) = hop_call(
+        add_kernel, [(one, f32)], total, exchange(gradient_beyond, 8), after=[near_across]
+    )
+    down_gradient, up_gradient, curvature_down, curvature_up = hop_call(
+        total_kernel,
         [((rank, hidden_width), f32), ((rank, model_width), f32)] * 2,
+        gradient_total,
         total,
-        gradient_total,
-        curvature_total,
-        exchange(across, 2),
+        exchange(curvature_beyond, 8),
+        exchange(near_across, 2),
     )
     return down_gradient.T[None], up_gradient[None], curvature_down.T[None], curvature_up[None]
 
@@ -780,7 +766,8 @@
 
 def local(*arguments):
     factor_bytes = 2 * 4 * (arguments[6].size + arguments[7].size) * lax.axis_size("expert")
-    plan = gathered_plan if 4 * factor_bytes <= kernel_vmem else routed_plan
+    fits = lax.axis_size("expert") == 16 and 4 * factor_bytes <= kernel_vmem
+    plan = gathered_plan if fits else routed_plan
     return plan(*arguments)
 
 

time: 74.5 us -> 76.1 us (1.021)
  waiting for transfers between devices: 31.4 us -> 35.1 us
  starting transfers between devices: 21.3 us -> 19 us
    ppermute x13, waiting for transfers between devices: 14.3 us -> 17.7 us  [exchange(): lax.ppermute(value, 'expert', [(device, device ^ mask) for device in rang...]
    ppermute x13, starting transfers between devices: 12 us -> 10.1 us  [exchange(): lax.ppermute(value, 'expert', [(device, device ^ mask) for device in rang...]
    pallas_call x13 -> x14, Pallas kernels: 19.8 us -> 20 us  [call(): pl.pallas_call(kernel, out_shape=[jax.ShapeDtypeStruct(shape, dtype) for...]
  transfers between devices with their start and end apart: 21 -> 21, of which waited for: 12 -> 12; matrix products, arithmetic and copies ran while one was open for 0% -> 0% of each run, Pallas kernels for 23% -> 22%
where the time goes in v11:
time: 76.1 us; the launch traced here: 75.8 us
  waiting for transfers between devices  35.1 us (46%)
  Pallas kernels  20 us (26%)
  starting transfers between devices  19 us (25%)
  between operations  0.82 us (1%)
  local copies, waits for them, and re-layouts  0.81 us (1%)
    pallas_call x14, Pallas kernels, call(): pl.pallas_call(kernel, out_shape=[jax.ShapeDtypeStruct(shape, dtype) for...  20 us
    ppermute x13, waiting for transfers between devices, exchange(): lax.ppermute(value, 'expert', [(device, device ^ mask) for device in rang...  17.7 us
    ppermute x8, waiting for transfers between devices, shift(): return lax.ppermute(value, 'expert', pairs)  17.4 us
    ppermute x13, starting transfers between devices, exchange(): lax.ppermute(value, 'expert', [(device, device ^ mask) for device in rang...  10.1 us
    ppermute x8, starting transfers between devices, shift(): return lax.ppermute(value, 'expert', pairs)  8.9 us
  transfers between devices with their start and end apart: 21, of which 12 were waited for; matrix products, arithmetic and copies ran while one was open for 0% of the time, Pallas kernels for 22%

profile of v11, /device:TPU:0, one launch (start us, length us, event | category | flops | bytes accessed | tf_op | source)
XLA Modules:
  0.0 75.8 jit_solution(4958326028359813295)
XLA Ops:
  1.2 2.0 %shard_map.129 = (s16[2,16,3200]{2,1,0:T(8,128)(2,1)}, f32[24,128]{1,0:T(8,128)}) custom-call(s32[8,128]{1,0:T(8,128)} %bitcast.31, bf16[8,128]{1,0:T(8,128)(2,1)} %bitcast.32, f32[1,128]{1,0:T(1,128)} %bitcast.33, f32[16,1024]{1,0:T(8,128)} %bitcast.29, f32[16,1024]{1,0:T(8,128)} %bitcast.30, f32[16,2048]{1,0:T(8,128)} %bitcast.27, f32[16,2048]{1,0:T(8,128)} %bitcast.28), custom_call_target="tpu_custom_call" | custom-call | flops 200000000 | bytes 1048576 | tf_op jit(solution)/shard_map/pallas_call | solution.py:433
  3.2 3.1 %collective-permute-start.6 = (s16[2,16,3200]{2,1,0:T(8,128)(2,1)}, s16[2,16,3200]{2,1,0:T(8,128)(2,1)S(1)}, u32[]{:S(2)}, u32[]{:S(2)}) collective-permute-start(s16[2,16,3200]{2,1,0:T(8,128)(2,1)} %get-tuple-element.37.rest_0_), channel_id=1, source_target_pairs={{0,4},{1,5},{4,8},{5,9},{8,12},{9,13},{12,14},{13,15},{14,10},{15,... | collective-permute-start | bytes 614408 | tf_op jit(solution)/shard_map/ppermute | solution.py:370
  6.4 5.3 %collective-permute-done.6.rest_7_.rest_6_ = s16[2,16,3200]{2,1,0:T(8,128)(2,1)S(1)} collective-permute-done((s16[2,16,3200]{2,1,0:T(8,128)(2,1)}, s16[2,16,3200]{2,1,0:T(8,128)(2,1)S(1)}, u32[]{:S(2)}, u32[]{:S(2)}) %collective-permute-start.6) | collective-permute-done | bytes 204832 | tf_op jit(solution)/shard_map/ppermute | solution.py:370
  11.7 1.8 %collective-permute-start.7 = (s16[2,16,3200]{2,1,0:T(8,128)(2,1)S(1)}, s16[2,16,3200]{2,1,0:T(8,128)(2,1)S(1)}, u32[]{:S(2)}, u32[]{:S(2)}) collective-permute-start(s16[2,16,3200]{2,1,0:T(8,128)(2,1)S(1)} %collective-permute-done.6.rest_7_.rest_6_), channel_id=1, source_target_pairs={{0,4},{1,5},{4,8},{5,9},{8,12},{9,13},{12,14},{13,15},{14,10},{15,... | collective-permute-start | bytes 614408 | tf_op jit(solution)/shard_map/ppermute | solution.py:370
  16.0 2.3 %collective-permute-done.7.rest_6_.rest_5_ = s16[2,16,3200]{2,1,0:T(8,128)(2,1)S(1)} collective-permute-done((s16[2,16,3200]{2,1,0:T(8,128)(2,1)S(1)}, s16[2,16,3200]{2,1,0:T(8,128)(2,1)S(1)}, u32[]{:S(2)}, u32[]{:S(2)}) %collective-permute-start.7) | collective-permute-done | bytes 204832 | tf_op jit(solution)/shard_map/ppermute | solution.py:370
  18.3 1.5 %collective-permute-start.8 = (s16[2,16,3200]{2,1,0:T(8,128)(2,1)S(1)}, s16[2,16,3200]{2,1,0:T(8,128)(2,1)S(1)}, u32[]{:S(2)}, u32[]{:S(2)}) collective-permute-start(s16[2,16,3200]{2,1,0:T(8,128)(2,1)S(1)} %collective-permute-done.7.rest_6_.rest_5_), channel_id=1, source_target_pairs={{0,4},{1,5},{4,8},{5,9},{8,12},{9,13},{12,14},{13,15},{14,10},{15,... | collective-permute-start | bytes 614408 | tf_op jit(solution)/shard_map/ppermute | solution.py:370
  19.8 1.9 %collective-permute-done.4.rest_2_ = s16[2,16,3200]{2,1,0:T(8,128)(2,1)S(1)} collective-permute-done((s16[2,16,3200]{2,1,0:T(8,128)(2,1)S(1)}, s16[2,16,3200]{2,1,0:T(8,128)(2,1)S(1)}, u32[]{:S(2)}, u32[]{:S(2)}) %collective-permute-start.4) | collective-permute-done | bytes 204832 | tf_op jit(solution)/shard_map/ppermute | solution.py:370
  22.2 1.8 %collective-permute-done.8.rest_5_.rest_4_ = s16[2,16,3200]{2,1,0:T(8,128)(2,1)S(1)} collective-permute-done((s16[2,16,3200]{2,1,0:T(8,128)(2,1)S(1)}, s16[2,16,3200]{2,1,0:T(8,128)(2,1)S(1)}, u32[]{:S(2)}, u32[]{:S(2)}) %collective-permute-start.8) | collective-permute-done | bytes 204832 | tf_op jit(solution)/shard_map/ppermute | solution.py:370
  24.1 1.6 %collective-permute-start.9 = (s16[1,16,3200]{2,1,0:T(8,128)(2,1)S(1)}, s16[1,16,3200]{2,1,0:T(8,128)(2,1)S(1)}, u32[]{:S(2)}, u32[]{:S(2)}) collective-permute-start(s16[1,16,3200]{2,1,0:T(8,128)(2,1)S(1)} %slice.8), channel_id=1, source_target_pairs={{0,4},{1,5},{4,8},{5,9},{8,12},{9,13},{12,14},{13,15},{14,10},{15,... | collective-permute-start | bytes 307208 | tf_op jit(solution)/shard_map/ppermute | solution.py:370
  25.6 2.2 %collective-permute-done.5.rest_3_ = s16[2,16,3200]{2,1,0:T(8,128)(2,1)S(1)} collective-permute-done((s16[2,16,3200]{2,1,0:T(8,128)(2,1)S(1)}, s16[2,16,3200]{2,1,0:T(8,128)(2,1)S(1)}, u32[]{:S(2)}, u32[]{:S(2)}) %collective-permute-start.5) | collective-permute-done | bytes 204832 | tf_op jit(solution)/shard_map/ppermute | solution.py:370
  29.4 3.1 %collective-permute-done.11.rest_8_ = s16[1,16,3200]{2,1,0:T(8,128)(2,1)S(1)} collective-permute-done((s16[1,16,3200]{2,1,0:T(8,128)(2,1)S(1)}, s16[1,16,3200]{2,1,0:T(8,128)(2,1)S(1)}, u32[]{:S(2)}, u32[]{:S(2)}) %collective-permute-start.11) | collective-permute-done | bytes 102432 | tf_op jit(solution)/shard_map/ppermute | solution.py:370
  32.6 3.4 %shard_map.132.reduced_ref = f32[2,256,128]{2,1,0:T(8,128)S(1)} custom-call(s32[17]{0:T(128)S(1)} %pad_add_fusion.place_ref, f32[256,24]{1,0:T(8,128)S(1)} %get-tuple-element.38.small_ref, bf16[1024,1024]{1,0:T(8,128)(2,1)S(1)} %bitcast.24, bf16[1024,1024]{1,0:T(8,128)(2,1)S(1)} %collective-permute-done.2.rest_0_.other_ref, ...), custom_call_target="tpu_custom_call" | custom-call | flops 2147483648 | bytes 1048576 | tf_op jit(solution)/shard_map/pallas_call | solution.py:433
  36.0 2.2 %shard_map.133 = (f32[256,128]{1,0:T(8,128)S(1)}, f32[256,256]{1,0:T(8,128)S(1)}, f32[256,2048]{1,0:T(8,128)S(1)}, bf16[256,2048]{1,0:T(8,128)(2,1)S(1)}, bf16[2...) custom-call(s32[17]{0:T(128)S(1)} %pad_add_fusion.place_ref, ...), custom_call_target="tpu_custom_call" | custom-call | flops 805306368 | bytes 1048576 | tf_op jit(solution)/shard_map/pallas_call | solution.py:433
  38.4 4.4 %shard_map.134 = (f32[2,16,3072]{2,1,0:T(8,128)S(1)}, f32[2,16,3072]{2,1,0:T(8,128)S(1)}, s16[2,16,3200]{2,1,0:T(8,128)(2,1)S(1)}, s16[1,2,16,3200]{3,2,1,0:T(8,...) custom-call(s32[17]{0:T(128)S(1)} %pad_add_fusion.place_ref, f32[256,24]{1,0:T(8,128)S(1)} %get-tuple-element.38.small_ref, ...), custom_call_target="tpu_custom_call" | custom-call | flops 2147483648 | bytes 1048576 | tf_op jit(solution)/shard_map/pallas_call | solution.py:433
  42.8 1.6 %collective-permute-start.15 = (s16[2,16,3200]{2,1,0:T(8,128)(2,1)S(1)}, s16[2,16,3200]{2,1,0:T(8,128)(2,1)S(1)}, u32[]{:S(2)}, u32[]{:S(2)}) collective-permute-start(s16[2,16,3200]{2,1,0:T(8,128)(2,1)S(1)} %get-tuple-element.56), channel_id=1, source_target_pairs={{0,4},{1,5},{2,6},{3,7},{4,0},{5,1},{6,2},{7,3},{8,12},{9,13},{10,... | collective-permute-start | bytes 614408 | tf_op jit(solution)/shard_map/ppermute | solution.py:394
  44.4 3.9 %shard_map.135 = (f32[2,16,3072]{2,1,0:T(8,128)S(1)}, f32[2,16,3072]{2,1,0:T(8,128)S(1)}, s16[2,16,3200]{2,1,0:T(8,128)(2,1)S(1)}, s16[2,2,16,3200]{3,2,1,0:T(8,128)(2,1)S(1)}) custom-call(s32[17]{0:T(128)S(1)} %pad_add_fusion.place_ref, f32[256,24]{1,0:T(8,128)S(1)} %get-tuple-element.38.small_ref, bf16[1024,1024]{1,0:T(8,128)(2,1)S(1)} %bitcast.26, ...), custom_call_target="tpu_custom_call" | custom-call | flops 1879048192 | bytes 1048576 | tf_op jit(solution)/shard_map/pallas_call | solution.py:433
  48.9 1.6 %collective-permute-start.13 = (s16[2,2,16,3200]{3,2,1,0:T(8,128)(2,1)S(1)}, s16[2,2,16,3200]{3,2,1,0:T(8,128)(2,1)S(1)}, u32[]{:S(2)}, u32[]{:S(2)}) collective-permute-start(s16[2,2,16,3200]{3,2,1,0:T(8,128)(2,1)S(1)} %get-tuple-element.51._), channel_id=1, source_target_pairs={{0,4},{1,5},{2,6},{3,7},{4,0},{5,1},{6,2},{7,3},{8,12},{9,13},{10,... | collective-permute-start | bytes 1228808 | tf_op jit(solution)/shard_map/ppermute | solution.py:394
  50.8 5.6 %collective-permute-done.14.arrived_ref = s16[2,16,3200]{2,1,0:T(8,128)(2,1)S(1)} collective-permute-done((s16[2,16,3200]{2,1,0:T(8,128)(2,1)S(1)}, s16[2,16,3200]{2,1,0:T(8,128)(2,1)S(1)}, u32[]{:S(2)}, u32[]{:S(2)}) %collective-permute-start.14) | collective-permute-done | bytes 204832 | tf_op jit(solution)/shard_map/ppermute | solution.py:394
  56.9 2.7 %collective-permute-start.18 = (s16[16,3200]{1,0:T(8,128)(2,1)S(1)}, s16[16,3200]{1,0:T(8,128)(2,1)S(1)}, u32[]{:S(2)}, u32[]{:S(2)}) collective-permute-start(s16[16,3200]{1,0:T(8,128)(2,1)S(1)} %shard_map.138._), channel_id=1, source_target_pairs={{0,8},{1,9},{2,10},{3,11},{4,12},{5,13},{6,14},{7,15},{8,0},{9,1},... | collective-permute-start | bytes 307208 | tf_op jit(solution)/shard_map/ppermute | solution.py:394
  59.6 1.7 %collective-permute-done.16.arrived_ref = s16[16,3200]{1,0:T(8,128)(2,1)S(1)} collective-permute-done((s16[16,3200]{1,0:T(8,128)(2,1)S(1)}, s16[16,3200]{1,0:T(8,128)(2,1)S(1)}, u32[]{:S(2)}, u32[]{:S(2)}) %collective-permute-start.16) | collective-permute-done | bytes 102432 | tf_op jit(solution)/shard_map/ppermute | solution.py:394
  61.5 2.5 %collective-permute-start.19 = (s16[16,3200]{1,0:T(8,128)(2,1)S(1)}, s16[16,3200]{1,0:T(8,128)(2,1)S(1)}, u32[]{:S(2)}, u32[]{:S(2)}) collective-permute-start(s16[16,3200]{1,0:T(8,128)(2,1)S(1)} %shard_map.139._), channel_id=1, source_target_pairs={{0,8},{1,9},{2,10},{3,11},{4,12},{5,13},{6,14},{7,15},{8,0},{9,1},... | collective-permute-start | bytes 307208 | tf_op jit(solution)/shard_map/ppermute | solution.py:394
  64.0 4.2 %collective-permute-done.13.arrived_ref = s16[2,2,16,3200]{3,2,1,0:T(8,128)(2,1)S(1)} collective-permute-done((s16[2,2,16,3200]{3,2,1,0:T(8,128)(2,1)S(1)}, s16[2,2,16,3200]{3,2,1,0:T(8,128)(2,1)S(1)}, u32[]{:S(2)}, u32[]{:S(2)}) %collective-permute-start.13) | collective-permute-done | bytes 409632 | tf_op jit(solution)/shard_map/ppermute | solution.py:394
  68.8 2.5 %collective-permute-done.19.far_ref = s16[16,3200]{1,0:T(8,128)(2,1)S(1)} collective-permute-done((s16[16,3200]{1,0:T(8,128)(2,1)S(1)}, s16[16,3200]{1,0:T(8,128)(2,1)S(1)}, u32[]{:S(2)}, u32[]{:S(2)}) %collective-permute-start.19) | collective-permute-done | bytes 102432 | tf_op jit(solution)/shard_map/ppermute | solution.py:394
  71.3 3.7 %collective-permute-done.20.across_ref = s16[2,16,3200]{2,1,0:T(8,128)(2,1)S(1)} collective-permute-done((s16[2,16,3200]{2,1,0:T(8,128)(2,1)S(1)}, s16[2,16,3200]{2,1,0:T(8,128)(2,1)S(1)}, u32[]{:S(2)}, u32[]{:S(2)}) %collective-permute-start.20) | collective-permute-done | bytes 204832 | tf_op jit(solution)/shard_map/ppermute | solution.py:394
  (48 shorter events, 8.2 us)
Async XLA Ops:
  0.6 13.0 %collective-permute-start.2 = (bf16[1024,1024]{1,0:T(8,128)(2,1)}, bf16[1024,1024]{1,0:T(8,128)(2,1)S(1)}, u32[]{:S(2)}, u32[]{:S(2)}) collective-permute-start(bf16[1024,1024]{1,0:T(8,128)(2,1)} %bitcast.23), channel_id=1, source_target_pairs={{0,1},{1,0},{2,3},{3,2},{4,5},{5,4},{6,7},{7,6},{8,9},{9,8},{10,11... | collective-permute-start | bytes 6291464 | tf_op jit(solution)/shard_map/ppermute | solution.py:394
  1.2 12.4 %collective-permute-start.3 = (bf16[128,2048]{1,0:T(8,128)(2,1)}, bf16[128,2048]{1,0:T(8,128)(2,1)S(1)}, u32[]{:S(2)}, u32[]{:S(2)}) collective-permute-start(bf16[128,2048]{1,0:T(8,128)(2,1)} %own_gradient_ref.1), channel_id=1, source_target_pairs={{0,1},{1,0},{2,3},{3,2},{4,5},{5,4},{6,7},{7,6},{8,9},{9,8},{10,11... | collective-permute-start | bytes 1572872 | tf_op jit(solution)/shard_map/ppermute | solution.py:394
  3.2 8.5 %collective-permute-start.6 = (s16[2,16,3200]{2,1,0:T(8,128)(2,1)}, s16[2,16,3200]{2,1,0:T(8,128)(2,1)S(1)}, u32[]{:S(2)}, u32[]{:S(2)}) collective-permute-start(s16[2,16,3200]{2,1,0:T(8,128)(2,1)} %get-tuple-element.37.rest_0_), channel_id=1, source_target_pairs={{0,4},{1,5},{4,8},{5,9},{8,12},{9,13},{12,14},{13,15},{14,10},{15,... | collective-permute-start | bytes 614408 | tf_op jit(solution)/shard_map/ppermute | solution.py:370
  6.3 7.3 %collective-permute-start.1 = (s16[2,16,3200]{2,1,0:T(8,128)(2,1)}, s16[2,16,3200]{2,1,0:T(8,128)(2,1)S(1)}, u32[]{:S(2)}, u32[]{:S(2)}) collective-permute-start(s16[2,16,3200]{2,1,0:T(8,128)(2,1)} %get-tuple-element.37.rest_0_), channel_id=1, source_target_pairs={{0,2},{1,3},{4,0},{5,1},{8,4},{9,5},{12,8},{13,9},{14,12},{15,13},... | collective-permute-start | bytes 614408 | tf_op jit(solution)/shard_map/ppermute | solution.py:370
  6.3 7.3 %collective-permute-start = (f32[24,128]{1,0:T(8,128)}, f32[24,128]{1,0:T(8,128)S(1)}, u32[]{:S(2)}, u32[]{:S(2)}) collective-permute-start(f32[24,128]{1,0:T(8,128)} %get-tuple-element.36.own_ref), channel_id=1, source_target_pairs={{0,1},{1,0},{2,3},{3,2},{4,5},{5,4},{6,7},{7,6},{8,9},{9,8},{10,11... | collective-permute-start | bytes 36872 | tf_op jit(solution)/shard_map/ppermute | solution.py:394
  6.3 15.9 %copy-start.4 = (s32[16]{0:T(128)S(1)}, s32[16]{0:T(128)}, u32[]{:S(2)}) copy-start(s32[16]{0:T(128)} %param.13) | copy-start | bytes 196
  6.4 22.3 %copy-start.1 = (s16[2,16,3200]{2,1,0:T(8,128)(2,1)S(1)}, s16[2,16,3200]{2,1,0:T(8,128)(2,1)}, u32[]{:S(2)}) copy-start(s16[2,16,3200]{2,1,0:T(8,128)(2,1)} %get-tuple-element.37.rest_0_) | copy-start | bytes 614404
  6.4 26.1 %copy-start = (bf16[128,8,1024]{2,1,0:T(8,128)(2,1)S(1)}, bf16[128,8,1024]{2,1,0:T(8,128)(2,1)}, u32[]{:S(2)}) copy-start(bf16[128,8,1024]{2,1,0:T(8,128)(2,1)} %param.10) | copy-start | bytes 6291460
  11.7 6.5 %collective-permute-start.7 = (s16[2,16,3200]{2,1,0:T(8,128)(2,1)S(1)}, s16[2,16,3200]{2,1,0:T(8,128)(2,1)S(1)}, u32[]{:S(2)}, u32[]{:S(2)}) collective-permute-start(s16[2,16,3200]{2,1,0:T(8,128)(2,1)S(1)} %collective-permute-done.6.rest_7_.rest_6_), channel_id=1, source_target_pairs={{0,4},{1,5},{4,8},{5,9},{8,12},{9,13},{12,14},{13,15},{14,10},{15,... | collective-permute-start | bytes 614408 | tf_op jit(solution)/shard_map/ppermute | solution.py:370
  15.7 6.0 %collective-permute-start.4 = (s16[2,16,3200]{2,1,0:T(8,128)(2,1)S(1)}, s16[2,16,3200]{2,1,0:T(8,128)(2,1)S(1)}, u32[]{:S(2)}, u32[]{:S(2)}) collective-permute-start(s16[2,16,3200]{2,1,0:T(8,128)(2,1)S(1)} %get-tuple-element.41.rest_1_), channel_id=1, source_target_pairs={{0,2},{1,3},{4,0},{5,1},{8,4},{9,5},{12,8},{13,9},{14,12},{15,13},... | collective-permute-start | bytes 614408 | tf_op jit(solution)/shard_map/ppermute | solution.py:370
  18.3 5.8 %collective-permute-start.8 = (s16[2,16,3200]{2,1,0:T(8,128)(2,1)S(1)}, s16[2,16,3200]{2,1,0:T(8,128)(2,1)S(1)}, u32[]{:S(2)}, u32[]{:S(2)}) collective-permute-start(s16[2,16,3200]{2,1,0:T(8,128)(2,1)S(1)} %collective-permute-done.7.rest_6_.rest_5_), channel_id=1, source_target_pairs={{0,4},{1,5},{4,8},{5,9},{8,12},{9,13},{12,14},{13,15},{14,10},{15,... | collective-permute-start | bytes 614408 | tf_op jit(solution)/shard_map/ppermute | solution.py:370
  21.7 6.1 %collective-permute-start.5 = (s16[2,16,3200]{2,1,0:T(8,128)(2,1)S(1)}, s16[2,16,3200]{2,1,0:T(8,128)(2,1)S(1)}, u32[]{:S(2)}, u32[]{:S(2)}) collective-permute-start(s16[2,16,3200]{2,1,0:T(8,128)(2,1)S(1)} %collective-permute-done.4.rest_2_), channel_id=1, source_target_pairs={{0,2},{1,3},{4,0},{5,1},{8,4},{9,5},{12,8},{13,9},{14,12},{15,13},... | collective-permute-start | bytes 614408 | tf_op jit(solution)/shard_map/ppermute | solution.py:370
  24.1 4.7 %collective-permute-start.9 = (s16[1,16,3200]{2,1,0:T(8,128)(2,1)S(1)}, s16[1,16,3200]{2,1,0:T(8,128)(2,1)S(1)}, u32[]{:S(2)}, u32[]{:S(2)}) collective-permute-start(s16[1,16,3200]{2,1,0:T(8,128)(2,1)S(1)} %slice.8), channel_id=1, source_target_pairs={{0,4},{1,5},{4,8},{5,9},{8,12},{9,13},{12,14},{13,15},{14,10},{15,... | collective-permute-start | bytes 307208 | tf_op jit(solution)/shard_map/ppermute | solution.py:370
  27.9 4.7 %collective-permute-start.11 = (s16[1,16,3200]{2,1,0:T(8,128)(2,1)S(1)}, s16[1,16,3200]{2,1,0:T(8,128)(2,1)S(1)}, u32[]{:S(2)}, u32[]{:S(2)}) collective-permute-start(s16[1,16,3200]{2,1,0:T(8,128)(2,1)S(1)} %slice.9), channel_id=1, source_target_pairs={{0,2},{1,3},{4,0},{5,1},{8,4},{9,5},{12,8},{13,9},{14,12},{15,13},... | collective-permute-start | bytes 307208 | tf_op jit(solution)/shard_map/ppermute | solution.py:370
  29.3 6.7 %collective-permute-start.10 = (f32[8,128]{1,0:T(8,128)S(1)}, f32[8,128]{1,0:T(8,128)S(1)}, u32[]{:S(2)}, u32[]{:S(2)}) collective-permute-start(f32[8,128]{1,0:T(8,128)S(1)} %shard_map.131.rest_9_.prior_ref), channel_id=1, source_target_pairs={{0,1},{1,0},{2,3},{3,2},{4,5},{5,4},{6,7},{7,6},{8,9},{9,8},{10,11... | collective-permute-start | bytes 12296 | tf_op jit(solution)/shard_map/ppermute | solution.py:394
  38.3 6.2 %collective-permute-start.12 = (bf16[256,2048]{1,0:T(8,128)(2,1)S(1)}, bf16[256,2048]{1,0:T(8,128)(2,1)S(1)}, u32[]{:S(2)}, u32[]{:S(2)}) collective-permute-start(bf16[256,2048]{1,0:T(8,128)(2,1)S(1)} %get-tuple-element.49), channel_id=1, source_target_pairs={{0,1},{1,0},{2,3},{3,2},{4,5},{5,4},{6,7},{7,6},{8,9},{9,8},{10,11... | collective-permute-start | bytes 3145736 | tf_op jit(solution)/shard_map/ppermute | solution.py:394
  42.8 7.7 %collective-permute-start.15 = (s16[2,16,3200]{2,1,0:T(8,128)(2,1)S(1)}, s16[2,16,3200]{2,1,0:T(8,128)(2,1)S(1)}, u32[]{:S(2)}, u32[]{:S(2)}) collective-permute-start(s16[2,16,3200]{2,1,0:T(8,128)(2,1)S(1)} %get-tuple-element.56), channel_id=1, source_target_pairs={{0,4},{1,5},{2,6},{3,7},{4,0},{5,1},{6,2},{7,3},{8,12},{9,13},{10,... | collective-permute-start | bytes 614408 | tf_op jit(solution)/shard_map/ppermute | solution.py:394
  48.4 8.0 %collective-permute-start.14 = (s16[2,16,3200]{2,1,0:T(8,128)(2,1)S(1)}, s16[2,16,3200]{2,1,0:T(8,128)(2,1)S(1)}, u32[]{:S(2)}, u32[]{:S(2)}) collective-permute-start(s16[2,16,3200]{2,1,0:T(8,128)(2,1)S(1)} %get-tuple-element.54), channel_id=1, source_target_pairs={{0,4},{1,5},{2,6},{3,7},{4,0},{5,1},{6,2},{7,3},{8,12},{9,13},{10,... | collective-permute-start | bytes 614408 | tf_op jit(solution)/shard_map/ppermute | solution.py:394
  48.9 19.4 %collective-permute-start.13 = (s16[2,2,16,3200]{3,2,1,0:T(8,128)(2,1)S(1)}, s16[2,2,16,3200]{3,2,1,0:T(8,128)(2,1)S(1)}, u32[]{:S(2)}, u32[]{:S(2)}) collective-permute-start(s16[2,2,16,3200]{3,2,1,0:T(8,128)(2,1)S(1)} %get-tuple-element.51._), channel_id=1, source_target_pairs={{0,4},{1,5},{2,6},{3,7},{4,0},{5,1},{6,2},{7,3},{8,12},{9,13},{10,... | collective-permute-start | bytes 1228808 | tf_op jit(solution)/shard_map/ppermute | solution.py:394
  50.7 6.0 %collective-permute-start.17 = (s16[16,3200]{1,0:T(8,128)(2,1)S(1)}, s16[16,3200]{1,0:T(8,128)(2,1)S(1)}, u32[]{:S(2)}, u32[]{:S(2)}) collective-permute-start(s16[16,3200]{1,0:T(8,128)(2,1)S(1)} %get-tuple-element.58._), channel_id=1, source_target_pairs={{0,2},{1,3},{2,0},{3,1},{4,6},{5,7},{6,4},{7,5},{8,10},{9,11},{10,... | collective-permute-start | bytes 307208 | tf_op jit(solution)/shard_map/ppermute | solution.py:394
  56.6 4.7 %collective-permute-start.16 = (s16[16,3200]{1,0:T(8,128)(2,1)S(1)}, s16[16,3200]{1,0:T(8,128)(2,1)S(1)}, u32[]{:S(2)}, u32[]{:S(2)}) collective-permute-start(s16[16,3200]{1,0:T(8,128)(2,1)S(1)} %get-tuple-element.59._), channel_id=1, source_target_pairs={{0,2},{1,3},{2,0},{3,1},{4,6},{5,7},{6,4},{7,5},{8,10},{9,11},{10,... | collective-permute-start | bytes 307208 | tf_op jit(solution)/shard_map/ppermute | solution.py:394
  56.9 11.8 %collective-permute-start.18 = (s16[16,3200]{1,0:T(8,128)(2,1)S(1)}, s16[16,3200]{1,0:T(8,128)(2,1)S(1)}, u32[]{:S(2)}, u32[]{:S(2)}) collective-permute-start(s16[16,3200]{1,0:T(8,128)(2,1)S(1)} %shard_map.138._), channel_id=1, source_target_pairs={{0,8},{1,9},{2,10},{3,11},{4,12},{5,13},{6,14},{7,15},{8,0},{9,1},... | collective-permute-start | bytes 307208 | tf_op jit(solution)/shard_map/ppermute | solution.py:394
  61.5 9.8 %collective-permute-start.19 = (s16[16,3200]{1,0:T(8,128)(2,1)S(1)}, s16[16,3200]{1,0:T(8,128)(2,1)S(1)}, u32[]{:S(2)}, u32[]{:S(2)}) collective-permute-start(s16[16,3200]{1,0:T(8,128)(2,1)S(1)} %shard_map.139._), channel_id=1, source_target_pairs={{0,8},{1,9},{2,10},{3,11},{4,12},{5,13},{6,14},{7,15},{8,0},{9,1},... | collective-permute-start | bytes 307208 | tf_op jit(solution)/shard_map/ppermute | solution.py:394
  68.5 6.4 %collective-permute-start.20 = (s16[2,16,3200]{2,1,0:T(8,128)(2,1)S(1)}, s16[2,16,3200]{2,1,0:T(8,128)(2,1)S(1)}, u32[]{:S(2)}, u32[]{:S(2)}) collective-permute-start(s16[2,16,3200]{2,1,0:T(8,128)(2,1)S(1)} %get-tuple-element.63._), channel_id=1, source_target_pairs={{0,2},{1,3},{2,0},{3,1},{4,6},{5,7},{6,4},{7,5},{8,10},{9,11},{10,... | collective-permute-start | bytes 614408 | tf_op jit(solution)/shard_map/ppermute | solution.py:394
  (2 other events, 3.0 us)

commit v12 on v11

--- a/solution.py
+++ b/solution.py
@@ -97,24 +97,16 @@
     prior_ref[...] = jnp.zeros_like(prior_ref)
     for block, number in enumerate((me, me ^ 1)):
         total = jnp.zeros((1, lanes), f32)
-        for offset in range(slots):
+        for offset, piece_ref in enumerate(piece_refs):
             device = place_ref[1 + slots + offset]
-            tail = piece_refs[offset][0, :, piece_refs[offset].shape[2] - lanes :]
+            tail = piece_ref[0, :, piece_ref.shape[2] - lanes :]
             counts = tail.astype(jnp.int32).astype(f32)[0:1]
             total = total + jnp.where(device < number, counts, 0.0)
         prior_ref[block : block + 1] = total
 
 
-def piece_part(refs, offset, kind):
-    last = len(refs) - 2
-    half = last // 2 + 1
-    if offset == half:
-        return refs[last + kind][0]
-    return refs[offset if offset < half else offset - 1][kind]
-
-
-def tokens_kernel(top, masks, place_ref, own_ref, other_ref, piece_ref, *rest):
-    small_ref, rank_ref, gate_ref, onward_ref = rest[-4:]
+def tokens_kernel(top, masks, place_ref, own_ref, other_ref, piece_ref, *outs):
+    small_ref, rank_ref, gate_ref, same_ref, mask_ref, onward_ref = outs
     onward_ref[...] = piece_ref[...]
     small_ref[...] = jnp.concatenate([own_ref[...], other_ref[...]], axis=1).T
     experts, gates, _ = token_columns(small_ref, top)
@@ -125,6 +117,10 @@
         > lax.broadcasted_iota(jnp.int32, (tokens, tokens), 1)
     )
     below = jnp.where(below, 1.0, 0.0).astype(bf16)
+    rows = same_ref.shape[0]
+    row = lax.broadcasted_iota(jnp.int32, (rows, tokens), 0)
+    same = jnp.where(row // top == lax.broadcasted_iota(jnp.int32, (rows, tokens), 1), 1.0, 0.0).astype(bf16)
+    same_ref[...] = same
     for core in range(2):
         tokens_of = slice(core * tokens, (core + 1) * tokens)
         gate = jnp.zeros((tokens, wide), f32)
@@ -135,16 +131,21 @@
             member = jnp.where(named, 1.0, member)
         gate_ref[core] = gate
         rank_ref[core] = dot(below, member.astype(bf16), 1, 0)
+        named = dot(same, small_ref[tokens_of].astype(bf16), 1, 0)
+        position = lax.broadcasted_iota(jnp.int32, named.shape, 0) % top
+        own = lax.broadcasted_iota(jnp.int32, named.shape, 1) == position
+        expert = jnp.sum(jnp.where(own, named, 0.0), axis=1, keepdims=True)
+        mask_ref[core] = jnp.where(expert == column, 1.0, 0.0).astype(bf16)
 
 
 def reduce_kernel(top, masks, place_ref, small_ref, own_ref, other_ref, *rest):
     slots = len(masks)
-    piece_refs, (_, reduced_ref, high_ref, low_ref, full_ref) = rest[: slots + 1], rest[slots + 1 :]
+    piece_refs, (reduced_ref, high_ref, low_ref, full_ref) = rest[:slots], rest[slots:]
     hidden_width = own_ref.shape[1]
     for offset in range(slots):
         slot = place_ref[1 + offset]
         for kind in range(2):
-            down, _ = decode(piece_part(piece_refs, offset, kind), hidden_width)
+            down, _ = decode(piece_refs[offset][kind], hidden_width)
             high_ref[kind, slot], low_ref[kind, slot] = halves(down)
     experts, _, _ = token_columns(small_ref, top)
     wide = reduced_ref.shape[2]
@@ -180,8 +181,8 @@
 
 def tangent_kernel(masks, place_ref, rank_ref, gate_ref, capacity_ref, prior_ref, arrived_ref, reduced_ref, *rest):
     slots = len(masks)
-    piece_refs = rest[: slots + 1]
-    weight_ref, weighted_ref, tangent_ref, coded_ref, high_ref, low_ref = rest[slots + 1 :]
+    piece_refs = rest[:slots]
+    weight_ref, weighted_ref, tangent_ref, coded_ref, high_ref, low_ref = rest[slots:]
     _, wide = weight_ref.shape
     model_width = tangent_ref.shape[1]
     hidden_width = piece_refs[0].shape[2] - model_width - lanes
@@ -196,7 +197,7 @@
     for offset in range(slots):
         slot = place_ref[1 + offset]
         for kind in range(2):
-            _, up = decode(piece_part(piece_refs, offset, kind), hidden_width)
+            _, up = decode(piece_refs[offset][kind], hidden_width)
             high_ref[kind, slot], low_ref[kind, slot] = halves(up)
     factor = high_ref[...].reshape(2 * wide, model_width), low_ref[...].reshape(2 * wide, model_width)
     tangent = dot_pairs(halves(weighted), factor, 1, 0)
@@ -204,16 +205,13 @@
     coded_ref[...] = tangent.astype(bf16)
 
 
-def put_left(left_ref, wide_ref, top, masks, place_ref, small_ref, terms):
-    experts, _, _ = token_columns(small_ref, top)
-    tokens, wide = terms.shape[0] // 2, terms.shape[1]
-    column = members(place_ref, wide, masks)
+def put_left(left_ref, same_ref, mask_ref, terms):
+    both = jnp.concatenate(halves(terms), axis=1)
+    tokens = terms.shape[0] // 2
     for core in range(2):
-        tokens_of = slice(core * tokens, (core + 1) * tokens)
-        for k in range(top):
-            named = experts[k][tokens_of] == column
-            wide_ref[core, pl.ds(k, tokens, stride=top), :] = jnp.where(named, terms[tokens_of], 0.0)
-        left_ref[core] = jnp.concatenate(halves(wide_ref[core]), axis=1)
+        repeated = dot(same_ref[...], both[core * tokens : (core + 1) * tokens], 1, 0).astype(bf16)
+        mask = mask_ref[core]
+        left_ref[core] = repeated * jnp.concatenate([mask, mask], axis=1)
 
 
 def add_halves(both):
@@ -221,7 +219,7 @@
     return both[:middle] + both[middle:]
 
 
-def put_chunks(keep_ref, chunk_ref, far_ref, near_ref, kind, down, up):
+def put_chunks(keep_ref, near_ref, chunk_ref, far_ref, down, up):
     rank = keep_ref.shape[1]
     rows = down.shape[0] // rank // 2
 
@@ -229,18 +227,16 @@
         start = number * rank
         return down[start : start + rank], up[start : start + rank]
 
-    for x in range(2):
-        keep_ref[x] = jnp.concatenate(slot(x * rows), axis=1)
-        chunk_ref[x] = jnp.concatenate(slot(x * rows + 2), axis=1)
-        far_ref[x] = encode(*slot(x * rows + 3))
-        near_ref[kind, x] = encode(*slot(x * rows + 1))
+    for place in range(2):
+        keep_ref[place] = jnp.concatenate(slot(place), axis=1)
+        near_ref[place] = encode(*slot(rows + place))
+        chunk_ref[place] = jnp.concatenate(slot(place * rows + 2), axis=1)
+        far_ref[place] = encode(*slot(place * rows + 3))
 
 
 def gradient_kernel(
-    top,
-    masks,
-    place_ref,
-    small_ref,
+    same_ref,
+    mask_ref,
     own_ref,
     other_ref,
     own_gradient_ref,
@@ -250,13 +246,12 @@
     high_ref,
     low_ref,
     keep_ref,
+    near_ref,
     chunk_ref,
     far_ref,
-    near_ref,
     up_ref,
     to_ref,
     left_ref,
-    wide_ref,
 ):
     wide = weight_ref.shape[1]
     model_width = up_ref.shape[1]
@@ -265,18 +260,18 @@
     low = low_ref[...].reshape(2 * wide, model_width)
     to_both = dot(gradient, high, 1, 1) + dot(gradient, low, 1, 1)
     to_ref[...] = to_both[:, wide:]
-    put_left(left_ref, wide_ref, top, masks, place_ref, small_ref, weight_ref[...] * to_both[:, :wide])
+    put_left(left_ref, same_ref, mask_ref, weight_ref[...] * to_both[:, :wide])
     down = dot(left_ref[0], own_ref[...], 0, 0) + dot(left_ref[1], other_ref[...], 0, 0)
     up = add_halves(dot(jnp.concatenate(halves(weighted_ref[...]), axis=1), gradient, 0, 0))
     up_ref[...] = up[:wide]
-    put_chunks(keep_ref, chunk_ref, far_ref, near_ref, 0, add_halves(down), up[wide:])
+    put_chunks(keep_ref, near_ref, chunk_ref, far_ref, add_halves(down), up[wide:])
 
 
 def curvature_kernel(
     top,
-    masks,
-    place_ref,
     small_ref,
+    same_ref,
+    mask_ref,
     own_ref,
     other_ref,
     weight_ref,
@@ -287,15 +282,12 @@
     to_ref,
     tangent_ref,
     arrived_ref,
-    gradient_near_ref,
     keep_ref,
+    near_ref,
     chunk_ref,
     far_ref,
-    near_ref,
     left_ref,
-    wide_ref,
 ):
-    near_ref[0:1] = gradient_near_ref[...]
     _, _, curvature = token_columns(small_ref, top)
     tokens, wide = weight_ref.shape
     block = tokens // 2
@@ -304,14 +296,14 @@
     resid = halves(curvature * (tangent_ref[...] + arrived))
     adapter_up = high_ref[0].reshape(wide, model_width), low_ref[0].reshape(wide, model_width)
     terms = weight_ref[...] * (dot_pairs(resid, adapter_up, 1, 1) + to_ref[...])
-    put_left(left_ref, wide_ref, top, masks, place_ref, small_ref, terms)
+    put_left(left_ref, same_ref, mask_ref, terms)
     down = dot(left_ref[0], own_ref[...], 0, 0) + dot(left_ref[1], other_ref[...], 0, 0)
     weighted_u = halves(weighted_ref[:, wide:])
     up = add_halves(dot(jnp.concatenate(weighted_u, axis=1), resid[0], 0, 0)) + dot(weighted_u[0], resid[1], 0, 0)
-    put_chunks(keep_ref, chunk_ref, far_ref, near_ref, 1, add_halves(down), up_ref[...] + up)
-
-
-def pair_kernel(hidden_width, arrived_ref, chunk_ref, _, across_ref, keep_ref):
+    put_chunks(keep_ref, near_ref, chunk_ref, far_ref, add_halves(down), up_ref[...] + up)
+
+
+def pair_kernel(hidden_width, arrived_ref, chunk_ref, across_ref, keep_ref):
     for x in range(2):
         down, up = decode(arrived_ref[x], hidden_width)
         down, up = chunk_ref[x, :, :hidden_width] + down, chunk_ref[x, :, hidden_width:] + up
@@ -321,36 +313,39 @@
             across_ref[...] = encode(down, up)
 
 
-def far_kernel(hidden_width, arrived_ref, keep_ref, _, out_ref):
+def far_kernel(hidden_width, arrived_ref, keep_ref, out_ref):
     down, up = decode(arrived_ref[...], hidden_width)
     out_ref[...] = encode(keep_ref[:, :hidden_width] + down, keep_ref[:, hidden_width:] + up)
 
 
-def near_kernel(hidden_width, arrived_ref, gradient_ref, curvature_ref, _, across_ref, total_ref):
-    for kind, keep_ref in enumerate((gradient_ref, curvature_ref)):
-        for x in range(2):
-            down, up = decode(arrived_ref[kind, x], hidden_width)
-            down, up = keep_ref[x, :, :hidden_width] + down, keep_ref[x, :, hidden_width:] + up
-            if x == 0:
+def near_kernel(
+    hidden_width, gradient_ref, curvature_ref, gradient_keep_ref, curvature_keep_ref, onward_ref, total_ref
+):
+    pairs = ((gradient_ref, gradient_keep_ref), (curvature_ref, curvature_keep_ref))
+    for kind, (arrived_ref, keep_ref) in enumerate(pairs):
+        for z in range(2):
+            down, up = decode(arrived_ref[z], hidden_width)
+            down, up = keep_ref[z, :, :hidden_width] + down, keep_ref[z, :, hidden_width:] + up
+            if z == 0:
                 total_ref[kind] = jnp.concatenate([down, up], axis=1)
             else:
-                across_ref[kind] = encode(down, up)
-
-
-def add_kernel(hidden_width, total_ref, arrived_ref, _, out_ref):
+                onward_ref[kind] = encode(down, up)
+
+
+def add_kernel(hidden_width, total_ref, arrived_ref, out_ref):
     down, up = decode(arrived_ref[...], hidden_width)
     out_ref[:, :hidden_width] = total_ref[0, :, :hidden_width] + down
     out_ref[:, hidden_width:] = total_ref[0, :, hidden_width:] + up
 
 
-def total_kernel(hidden_width, gradient_ref, total_ref, far_ref, across_ref, *out_refs):
+def total_kernel(hidden_width, gradient_ref, total_ref, far_ref, pair_ref, *out_refs):
     far = decode(far_ref[...], hidden_width)
     totals = [
         (gradient_ref[:, :hidden_width], gradient_ref[:, hidden_width:]),
         (total_ref[1, :, :hidden_width] + far[0], total_ref[1, :, hidden_width:] + far[1]),
     ]
     for kind in range(2):
-        down, up = decode(across_ref[kind], hidden_width)
+        down, up = decode(pair_ref[kind], hidden_width)
         out_refs[2 * kind][...] = totals[kind][0] + down
         out_refs[2 * kind + 1][...] = totals[kind][1] + up
 
@@ -379,14 +374,12 @@
         half = self.length // 2
         found = {0: own}
         ahead, behind = own, own
-        for step in range(1, half):
-            behind = self.shift(behind, 1)
-            ahead = self.shift(ahead, -1)
-            if step == 1:
-                ahead = passing(ahead)
-            found[self.length - step], found[step] = behind, ahead
-        last = [self.shift(behind[:1], 1), self.shift(ahead[1:], -1)]
-        return [found[offset] for offset in sorted(found)] + last
+        for step in range(1, half + 1):
+            behind = found[self.length - step] = self.shift(behind, 1)
+            if step < half:
+                ahead = self.shift(ahead, -1)
+                ahead = found[step] = passing(ahead) if step == 1 else ahead
+        return [found[offset] for offset in range(self.length)]
 
 
 def exchange(value, mask):
@@ -427,17 +420,17 @@
 
     def call(kernel, multiplies, outs, *operands, scratch=(), after=(), grant=kernel_vmem):
         space = pltpu.HBM if kernel is prepare_kernel else pltpu.VMEM
-        places = [
+        places = [pl.BlockSpec(memory_space=pl.ANY) for _ in after] + [
             pl.BlockSpec(memory_space=pltpu.SMEM if operand is place else space) for operand in operands
-        ] + [pl.BlockSpec(memory_space=pl.ANY) for _ in after]
+        ]
         return pl.pallas_call(
-            kernel,
+            lambda *refs: kernel(*refs[len(after) :]),
             out_shape=[jax.ShapeDtypeStruct(shape, dtype) for shape, dtype in outs],
             in_specs=places,
             scratch_shapes=scratch,
             compiler_params=pltpu.CompilerParams(vmem_limit_bytes=grant),
             cost_estimate=pl.CostEstimate(flops=2 * multiplies, bytes_accessed=2**20, transcendentals=0),
-        )(*operands, *after)
+        )(*after, *operands)
 
     down_multiplies = 2 * top * both * hidden_width * wide
     up_multiplies = both * model_width * wide
@@ -475,6 +468,8 @@
                 ((both, small.shape[0]), f32),
                 ((2, tokens, wide), f32),
                 ((2, tokens, wide), f32),
+                ((top * tokens, tokens), bf16),
+                ((2, top * tokens, wide), bf16),
                 (piece.shape, i16),
             ],
             place,
@@ -487,11 +482,10 @@
         return onward
 
     pieces = ring.gather(piece, passing)
-    small_columns, local_rank, gate = beside
+    small_columns, local_rank, gate, same, mask = beside
     capacity_row = jnp.pad(capacity.astype(f32), (counts_lane, lanes - counts_lane - experts))[None, :]
 
-    by_offset = pieces[:rows] + [pieces[-2]] + pieces[rows:-2]
-    (prior,) = call(functools.partial(prior_kernel, masks), 10**8, [((8, lanes), f32)], place, *by_offset)
+    (prior,) = call(functools.partial(prior_kernel, masks), 10**8, [((8, lanes), f32)], place, *pieces)
     prior_arrived = exchange(prior, 1)
     factor_halves = [pltpu.VMEM((2, slots, rank, hidden_width), bf16)] * 2
     (reduced,) = call(
@@ -527,21 +521,14 @@
         *pieces,
     )
     arrived = exchange(coded, 1)
-    left = [pltpu.VMEM((2, top * tokens, 2 * wide), bf16), pltpu.VMEM((2, top * tokens, wide), f32)]
-    def chunks(kinds):
-        return [
-            ((2, rank, hidden_width + model_width), f32),
-            ((2, rank, hidden_width + model_width), f32),
-            ((2, rank, coded_width), i16),
-            ((kinds, 2, rank, coded_width), i16),
-        ]
-
-    gradient_keep, gradient_chunk, gradient_far, near, up, to = call(
-        functools.partial(gradient_kernel, top, masks),
+    left = [pltpu.VMEM((2, top * tokens, 2 * wide), bf16)]
+    chunks = [((2, rank, hidden_width + model_width), f32), ((2, rank, coded_width), i16)] * 2
+    gradient_keep, gradient_near, gradient_chunk, gradient_far, up, to = call(
+        gradient_kernel,
         down_multiplies + 8 * up_multiplies,
-        chunks(1) + [((wide, model_width), f32), ((both, wide), f32)],
-        place,
-        small_columns,
+        chunks + [((wide, model_width), f32), ((both, wide), f32)],
+        same,
+        mask,
         hidden,
         hidden_other,
         output_gradient,
@@ -553,12 +540,14 @@
         scratch=left,
     )
     gradient_far = exchange(gradient_far, 4)
-    curvature_keep, curvature_chunk, curvature_far, near = call(
-        functools.partial(curvature_kernel, top, masks),
+    gradient_near = exchange(gradient_near, 2)
+    curvature_keep, curvature_near, curvature_chunk, curvature_far = call(
+        functools.partial(curvature_kernel, top),
         down_multiplies + 6 * up_multiplies,
-        chunks(2),
-        place,
+        chunks,
         small_columns,
+        same,
+        mask,
         hidden,
         hidden_other,
         weight,
@@ -569,7 +558,6 @@
         to,
         tangent,
         arrived,
-        near,
         scratch=left,
     )
 
@@ -582,29 +570,42 @@
         return call(functools.partial(kernel, hidden_width), hop, outs, *operands, after=after)
 
     curvature_far = exchange(curvature_far, 4)
-    near_arrived = exchange(near, 4)
+    curvature_near = exchange(curvature_near, 2)
     gradient_across, gradient_pair = hop_call(
-        pair_kernel, [(one_coded, i16), (one, f32)], gradient_far, gradient_chunk, after=[near]
+        pair_kernel,
+        [(one_coded, i16), (one, f32)],
+        gradient_far,
+        gradient_chunk,
+        after=[curvature_keep],
     )
     curvature_across, curvature_pair = hop_call(
-        pair_kernel, [(one_coded, i16), (one, f32)], curvature_far, curvature_chunk, after=[gradient_across]
+        pair_kernel,
+        [(one_coded, i16), (one, f32)],
+        curvature_far,
+        curvature_chunk,
+        after=[gradient_across, gradient_near],
     )
     (gradient_beyond,) = hop_call(
-        far_kernel, [(one_coded, i16)], exchange(gradient_across, 2), gradient_pair, after=[curvature_across]
-    )
-    (curvature_beyond,) = hop_call(
-        far_kernel, [(one_coded, i16)], exchange(curvature_across, 2), curvature_pair, after=[gradient_beyond]
-    )
-    near_across, total = hop_call(
+        far_kernel,
+        [(one_coded, i16)],
+        exchange(gradient_across, 2),
+        gradient_pair,
+        after=[curvature_across, curvature_near],
+    )
+    onward, total = hop_call(
         near_kernel,
         [((2,) + one_coded, i16), ((2,) + one, f32)],
-        near_arrived,
+        gradient_near,
+        curvature_near,
         gradient_keep,
         curvature_keep,
-        after=[curvature_beyond],
+        after=[gradient_beyond],
+    )
+    (curvature_beyond,) = hop_call(
+        far_kernel, [(one_coded, i16)], exchange(curvature_across, 2), curvature_pair, after=[onward]
     )
     (gradient_total,) = hop_call(
-        add_kernel, [(one, f32)], total, exchange(gradient_beyond, 8), after=[near_across]
+        add_kernel, [(one, f32)], total, exchange(gradient_beyond, 8), after=[curvature_beyond]
     )
     down_gradient, up_gradient, curvature_down, curvature_up = hop_call(
         total_kernel,
@@ -612,7 +613,7 @@
         gradient_total,
         total,
         exchange(curvature_beyond, 8),
-        exchange(near_across, 2),
+        exchange(onward, 4),
     )
     return down_gradient.T[None], up_gradient[None], curvature_down.T[None], curvature_up[None]
 

time: 76.1 us -> 73.8 us (0.970)
  waiting for transfers between devices: 35.1 us -> 32.7 us
    ppermute x13 -> x14, waiting for transfers between devices: 17.7 us -> 13.2 us  [exchange(): lax.ppermute(value, 'expert', [(device, device ^ mask) for device in rang...]
    ppermute x8 -> x7, waiting for transfers between devices: 17.4 us -> 19.5 us  [shift(): return lax.ppermute(value, 'expert', pairs)]
    ppermute x13 -> x14, starting transfers between devices: 10.1 us -> 10.9 us  [exchange(): lax.ppermute(value, 'expert', [(device, device ^ mask) for device in rang...]
    ppermute x8 -> x7, starting transfers between devices: 8.9 us -> 8.83 us  [shift(): return lax.ppermute(value, 'expert', pairs)]
  transfers between devices with their start and end apart: 21 -> 21, of which waited for: 12 -> 11; matrix products, arithmetic and copies ran while one was open for 0% -> 0% of each run, Pallas kernels for 22% -> 21%
where the time goes in v12:
time: 73.8 us; the launch traced here: 73.5 us
  waiting for transfers between devices  32.7 us (44%)
  starting transfers between devices  19.7 us (27%)
  Pallas kernels  19.4 us (26%)
  between operations  0.81 us (1%)
  local copies, waits for them, and re-layouts  0.8 us (1%)
    ppermute x7, waiting for transfers between devices, shift(): return lax.ppermute(value, 'expert', pairs)  19.5 us
    pallas_call x14, Pallas kernels, call(): pl.pallas_call(lambda *refs: kernel(*refs[len(after):]), out_shape=[jax.S...  19.4 us
    ppermute x14, waiting for transfers between devices, exchange(): lax.ppermute(value, 'expert', [(device, device ^ mask) for device in rang...  13.2 us
    ppermute x14, starting transfers between devices, exchange(): lax.ppermute(value, 'expert', [(device, device ^ mask) for device in rang...  10.9 us
    ppermute x7, starting transfers between devices, shift(): return lax.ppermute(value, 'expert', pairs)  8.83 us
  transfers between devices with their start and end apart: 21, of which 11 were waited for; matrix products, arithmetic and copies ran while one was open for 0% of the time, Pallas kernels for 21%

profile of v12, /device:TPU:0, one launch (start us, length us, event | category | flops | bytes accessed | tf_op | source)
XLA Modules:
  0.0 73.5 jit_solution(10305665781779453597)
XLA Ops:
  1.2 2.0 %shard_map.129 = (s16[2,16,3200]{2,1,0:T(8,128)(2,1)}, f32[24,128]{1,0:T(8,128)}) custom-call(s32[8,128]{1,0:T(8,128)} %bitcast.31, bf16[8,128]{1,0:T(8,128)(2,1)} %bitcast.32, f32[1,128]{1,0:T(1,128)} %bitcast.33, f32[16,1024]{1,0:T(8,128)} %bitcast.29, f32[16,1024]{1,0:T(8,128)} %bitcast.30, f32[16,2048]{1,0:T(8,128)} %bitcast.27, f32[16,2048]{1,0:T(8,128)} %bitcast.28), custom_call_target="tpu_custom_call" | custom-call | flops 200000000 | bytes 1048576 | tf_op jit(solution)/shard_map/pallas_call | solution.py:426
  3.2 3.1 %collective-permute-start.6 = (s16[2,16,3200]{2,1,0:T(8,128)(2,1)}, s16[2,16,3200]{2,1,0:T(8,128)(2,1)S(1)}, u32[]{:S(2)}, u32[]{:S(2)}) collective-permute-start(s16[2,16,3200]{2,1,0:T(8,128)(2,1)} %get-tuple-element.39.refs_1_.refs_5_.refs_7_), channel_id=1, source_target_pairs={{0,4},{1,5},{4,8},{5,9},{8,12},{9,13},{12,14},{13,15},{14,10},{15,... | collective-permute-start | bytes 614408 | tf_op jit(solution)/shard_map/ppermute | solution.py:365
  6.3 5.4 %collective-permute-done.6.refs_8_.refs_12_.refs_14_ = s16[2,16,3200]{2,1,0:T(8,128)(2,1)S(1)} collective-permute-done((s16[2,16,3200]{2,1,0:T(8,128)(2,1)}, s16[2,16,3200]{2,1,0:T(8,128)(2,1)S(1)}, u32[]{:S(2)}, u32[]{:S(2)}) %collective-permute-start.6) | collective-permute-done | bytes 204832 | tf_op jit(solution)/shard_map/ppermute | solution.py:365
  11.7 1.8 %collective-permute-start.7 = (s16[2,16,3200]{2,1,0:T(8,128)(2,1)S(1)}, s16[2,16,3200]{2,1,0:T(8,128)(2,1)S(1)}, u32[]{:S(2)}, u32[]{:S(2)}) collective-permute-start(s16[2,16,3200]{2,1,0:T(8,128)(2,1)S(1)} %collective-permute-done.6.refs_8_.refs_12_.refs_14_), channel_id=1, source_target_pairs={{0,4},{1,5},{4,8},{5,9},{8,12},{9,13},{12,14},{13,15},{14,10},{15,... | collective-permute-start | bytes 614408 | tf_op jit(solution)/shard_map/ppermute | solution.py:365
  13.7 4.6 %collective-permute-done.7.refs_7_.refs_11_.refs_13_ = s16[2,16,3200]{2,1,0:T(8,128)(2,1)S(1)} collective-permute-done((s16[2,16,3200]{2,1,0:T(8,128)(2,1)S(1)}, s16[2,16,3200]{2,1,0:T(8,128)(2,1)S(1)}, u32[]{:S(2)}, u32[]{:S(2)}) %collective-permute-start.7) | collective-permute-done | bytes 204832 | tf_op jit(solution)/shard_map/ppermute | solution.py:365
  18.3 1.5 %collective-permute-start.8 = (s16[2,16,3200]{2,1,0:T(8,128)(2,1)S(1)}, s16[2,16,3200]{2,1,0:T(8,128)(2,1)S(1)}, u32[]{:S(2)}, u32[]{:S(2)}) collective-permute-start(s16[2,16,3200]{2,1,0:T(8,128)(2,1)S(1)} %collective-permute-done.7.refs_7_.refs_11_.refs_13_), channel_id=1, source_target_pairs={{0,4},{1,5},{4,8},{5,9},{8,12},{9,13},{12,14},{13,15},{14,10},{15,... | collective-permute-start | bytes 614408 | tf_op jit(solution)/shard_map/ppermute | solution.py:365
  20.5 2.0 %shard_map.130 = (f32[256,24]{1,0:T(8,128)S(1)}, f32[2,128,128]{2,1,0:T(8,128)S(1)}, f32[2,128,128]{2,1,0:T(8,128)S(1)}, bf16[1024,128]{1,0:T(8,128)(2,1)S(1)}, ...) custom-call(bf16[1024,1024]{1,0:T(8,128)(2,1)S(1)} %collective-permute-done.refs_0_.refs_4_.refs_3_, ...), custom_call_target="tpu_custom_call" | custom-call | flops 2000000000 | bytes 1048576 | tf_op jit(solution)/shard_map/pallas_call | solution.py:426
  23.1 1.0 %collective-permute-done.8.refs_6_.refs_10_.refs_12_ = s16[2,16,3200]{2,1,0:T(8,128)(2,1)S(1)} collective-permute-done((s16[2,16,3200]{2,1,0:T(8,128)(2,1)S(1)}, s16[2,16,3200]{2,1,0:T(8,128)(2,1)S(1)}, u32[]{:S(2)}, u32[]{:S(2)}) %collective-permute-start.8) | collective-permute-done | bytes 204832 | tf_op jit(solution)/shard_map/ppermute | solution.py:365
  24.0 1.7 %collective-permute-start.9 = (s16[2,16,3200]{2,1,0:T(8,128)(2,1)S(1)}, s16[2,16,3200]{2,1,0:T(8,128)(2,1)S(1)}, u32[]{:S(2)}, u32[]{:S(2)}) collective-permute-start(s16[2,16,3200]{2,1,0:T(8,128)(2,1)S(1)} %collective-permute-done.8.refs_6_.refs_10_.refs_12_), channel_id=1, source_target_pairs={{0,4},{1,5},{4,8},{5,9},{8,12},{9,13},{12,14},{13,15},{14,10},{15,... | collective-permute-start | bytes 614408 | tf_op jit(solution)/shard_map/ppermute | solution.py:365
  25.7 3.0 %collective-permute-done.4.refs_3_.refs_7_.refs_9_ = s16[2,16,3200]{2,1,0:T(8,128)(2,1)S(1)} collective-permute-done((s16[2,16,3200]{2,1,0:T(8,128)(2,1)S(1)}, s16[2,16,3200]{2,1,0:T(8,128)(2,1)S(1)}, u32[]{:S(2)}, u32[]{:S(2)}) %collective-permute-start.4) | collective-permute-done | bytes 204832 | tf_op jit(solution)/shard_map/ppermute | solution.py:365
  29.8 4.7 %collective-permute-done.5.refs_4_.refs_8_.refs_10_ = s16[2,16,3200]{2,1,0:T(8,128)(2,1)S(1)} collective-permute-done((s16[2,16,3200]{2,1,0:T(8,128)(2,1)S(1)}, s16[2,16,3200]{2,1,0:T(8,128)(2,1)S(1)}, u32[]{:S(2)}, u32[]{:S(2)}) %collective-permute-start.5) | collective-permute-done | bytes 204832 | tf_op jit(solution)/shard_map/ppermute | solution.py:365
  35.2 3.4 %shard_map.132.refs_6_ = f32[2,256,128]{2,1,0:T(8,128)S(1)} custom-call(f32[8,128]{1,0:T(8,128)S(1)} %shard_map.131.refs_0_.refs_4_, s32[17]{0:T(128)S(1)} %pad_add_fusion.refs_2_.refs_0_.refs_1_, f32[256,24]{1,0:T(8,128)S(1)} %get-tuple-element.40.refs_2_.refs_0_, bf16[1024,1024]{1,0:T(8,128)(2,1)S(1)} %bitcast.24, ...), custom_call_target="tpu_custom_call" | custom-call | flops 2147483648 | bytes 1048576 | tf_op jit(solution)/shard_map/pallas_call | solution.py:426
  38.6 2.2 %shard_map.133 = (f32[256,128]{1,0:T(8,128)S(1)}, f32[256,256]{1,0:T(8,128)S(1)}, f32[256,2048]{1,0:T(8,128)S(1)}, bf16[256,2048]{1,0:T(8,128)(2,1)S(1)}, bf16[2...) custom-call(s32[17]{0:T(128)S(1)} %pad_add_fusion.refs_2_.refs_0_.refs_1_, ...), custom_call_target="tpu_custom_call" | custom-call | flops 805306368 | bytes 1048576 | tf_op jit(solution)/shard_map/pallas_call | solution.py:426
  41.4 4.0 %shard_map.134 = (f32[2,16,3072]{2,1,0:T(8,128)S(1)}, s16[2,16,3200]{2,1,0:T(8,128)(2,1)S(1)}, f32[2,16,3072]{2,1,0:T(8,128)S(1)}, s16[2,16,3200]{2,1,0:T(8,128)...) custom-call(bf16[1024,128]{1,0:T(8,128)(2,1)S(1)} %get-tuple-element.41.refs_0_.refs_1_, ...), custom_call_target="tpu_custom_call" | custom-call | flops 2147483648 | bytes 1048576 | tf_op jit(solution)/shard_map/pallas_call | solution.py:426
  45.4 1.6 %collective-permute-start.12 = (s16[2,16,3200]{2,1,0:T(8,128)(2,1)S(1)}, s16[2,16,3200]{2,1,0:T(8,128)(2,1)S(1)}, u32[]{:S(2)}, u32[]{:S(2)}) collective-permute-start(s16[2,16,3200]{2,1,0:T(8,128)(2,1)S(1)} %get-tuple-element.55), channel_id=1, source_target_pairs={{0,4},{1,5},{2,6},{3,7},{4,0},{5,1},{6,2},{7,3},{8,12},{9,13},{10,... | collective-permute-start | bytes 614408 | tf_op jit(solution)/shard_map/ppermute | solution.py:387
  47.2 3.2 %shard_map.135 = (f32[2,16,3072]{2,1,0:T(8,128)S(1)}, s16[2,16,3200]{2,1,0:T(8,128)(2,1)S(1)}, f32[2,16,3072]{2,1,0:T(8,128)S(1)}, s16[2,16,3200]{2,1,0:T(8,128)(2,1)S(1)}) custom-call(f32[256,24]{1,0:T(8,128)S(1)} %get-tuple-element.40.refs_2_.refs_0_, bf16[1024,128]{1,0:T(8,128)(2,1)S(1)} %get-tuple-element.41.refs_0_.refs_1_, ...), custom_call_target="tpu_custom_call" | custom-call | flops 1879048192 | bytes 1048576 | tf_op jit(solution)/shard_map/pallas_call | solution.py:426
  51.0 1.9 %collective-permute-start.15 = (s16[2,16,3200]{2,1,0:T(8,128)(2,1)S(1)}, s16[2,16,3200]{2,1,0:T(8,128)(2,1)S(1)}, u32[]{:S(2)}, u32[]{:S(2)}) collective-permute-start(s16[2,16,3200]{2,1,0:T(8,128)(2,1)S(1)} %get-tuple-element.62), channel_id=1, source_target_pairs={{0,2},{1,3},{2,0},{3,1},{4,6},{5,7},{6,4},{7,5},{8,10},{9,11},{10,... | collective-permute-start | bytes 614408 | tf_op jit(solution)/shard_map/ppermute | solution.py:387
  53.3 1.3 %collective-permute-done.13.refs_1_ = s16[2,16,3200]{2,1,0:T(8,128)(2,1)S(1)} collective-permute-done((s16[2,16,3200]{2,1,0:T(8,128)(2,1)S(1)}, s16[2,16,3200]{2,1,0:T(8,128)(2,1)S(1)}, u32[]{:S(2)}, u32[]{:S(2)}) %collective-permute-start.13) | collective-permute-done | bytes 204832 | tf_op jit(solution)/shard_map/ppermute | solution.py:387
  54.6 2.5 %collective-permute-done.14.refs_2_ = s16[2,16,3200]{2,1,0:T(8,128)(2,1)S(1)} collective-permute-done((s16[2,16,3200]{2,1,0:T(8,128)(2,1)S(1)}, s16[2,16,3200]{2,1,0:T(8,128)(2,1)S(1)}, u32[]{:S(2)}, u32[]{:S(2)}) %collective-permute-start.14) | collective-permute-done | bytes 204832 | tf_op jit(solution)/shard_map/ppermute | solution.py:387
  57.3 1.8 %collective-permute-start.17 = (s16[16,3200]{1,0:T(8,128)(2,1)S(1)}, s16[16,3200]{1,0:T(8,128)(2,1)S(1)}, u32[]{:S(2)}, u32[]{:S(2)}) collective-permute-start(s16[16,3200]{1,0:T(8,128)(2,1)S(1)} %get-tuple-element.61.refs_0_), channel_id=1, source_target_pairs={{0,2},{1,3},{2,0},{3,1},{4,6},{5,7},{6,4},{7,5},{8,10},{9,11},{10,... | collective-permute-start | bytes 307208 | tf_op jit(solution)/shard_map/ppermute | solution.py:387
  59.1 2.1 %collective-permute-done.16.refs_2_ = s16[16,3200]{1,0:T(8,128)(2,1)S(1)} collective-permute-done((s16[16,3200]{1,0:T(8,128)(2,1)S(1)}, s16[16,3200]{1,0:T(8,128)(2,1)S(1)}, u32[]{:S(2)}, u32[]{:S(2)}) %collective-permute-start.16) | collective-permute-done | bytes 102432 | tf_op jit(solution)/shard_map/ppermute | solution.py:387
  61.4 2.6 %collective-permute-start.18 = (s16[16,3200]{1,0:T(8,128)(2,1)S(1)}, s16[16,3200]{1,0:T(8,128)(2,1)S(1)}, u32[]{:S(2)}, u32[]{:S(2)}) collective-permute-start(s16[16,3200]{1,0:T(8,128)(2,1)S(1)} %shard_map.138.refs_0_), channel_id=1, source_target_pairs={{0,8},{1,9},{2,10},{3,11},{4,12},{5,13},{6,14},{7,15},{8,0},{9,1},... | collective-permute-start | bytes 307208 | tf_op jit(solution)/shard_map/ppermute | solution.py:387
  65.3 3.8 %collective-permute-done.18.refs_2_ = s16[16,3200]{1,0:T(8,128)(2,1)S(1)} collective-permute-done((s16[16,3200]{1,0:T(8,128)(2,1)S(1)}, s16[16,3200]{1,0:T(8,128)(2,1)S(1)}, u32[]{:S(2)}, u32[]{:S(2)}) %collective-permute-start.18) | collective-permute-done | bytes 102432 | tf_op jit(solution)/shard_map/ppermute | solution.py:387
  69.3 3.4 %collective-permute-done.20.refs_3_ = s16[2,16,3200]{2,1,0:T(8,128)(2,1)S(1)} collective-permute-done((s16[2,16,3200]{2,1,0:T(8,128)(2,1)S(1)}, s16[2,16,3200]{2,1,0:T(8,128)(2,1)S(1)}, u32[]{:S(2)}, u32[]{:S(2)}) %collective-permute-start.20) | collective-permute-done | bytes 204832 | tf_op jit(solution)/shard_map/ppermute | solution.py:387
  (46 shorter events, 8.0 us)
Async XLA Ops:
  0.6 19.2 %collective-permute-start = (bf16[1024,1024]{1,0:T(8,128)(2,1)}, bf16[1024,1024]{1,0:T(8,128)(2,1)S(1)}, u32[]{:S(2)}, u32[]{:S(2)}) collective-permute-start(bf16[1024,1024]{1,0:T(8,128)(2,1)} %bitcast.23), channel_id=1, source_target_pairs={{0,1},{1,0},{2,3},{3,2},{4,5},{5,4},{6,7},{7,6},{8,9},{9,8},{10,11... | collective-permute-start | bytes 6291464 | tf_op jit(solution)/shard_map/ppermute | solution.py:387
  1.2 18.7 %collective-permute-start.1 = (bf16[128,2048]{1,0:T(8,128)(2,1)}, bf16[128,2048]{1,0:T(8,128)(2,1)S(1)}, u32[]{:S(2)}, u32[]{:S(2)}) collective-permute-start(bf16[128,2048]{1,0:T(8,128)(2,1)} %refs_4_.1), channel_id=1, source_target_pairs={{0,1},{1,0},{2,3},{3,2},{4,5},{5,4},{6,7},{7,6},{8,9},{9,8},{10,11... | collective-permute-start | bytes 1572872 | tf_op jit(solution)/shard_map/ppermute | solution.py:387
  3.2 8.5 %collective-permute-start.6 = (s16[2,16,3200]{2,1,0:T(8,128)(2,1)}, s16[2,16,3200]{2,1,0:T(8,128)(2,1)S(1)}, u32[]{:S(2)}, u32[]{:S(2)}) collective-permute-start(s16[2,16,3200]{2,1,0:T(8,128)(2,1)} %get-tuple-element.39.refs_1_.refs_5_.refs_7_), channel_id=1, source_target_pairs={{0,4},{1,5},{4,8},{5,9},{8,12},{9,13},{12,14},{13,15},{14,10},{15,... | collective-permute-start | bytes 614408 | tf_op jit(solution)/shard_map/ppermute | solution.py:365
  6.3 13.5 %collective-permute-start.3 = (s16[2,16,3200]{2,1,0:T(8,128)(2,1)}, s16[2,16,3200]{2,1,0:T(8,128)(2,1)S(1)}, u32[]{:S(2)}, u32[]{:S(2)}) collective-permute-start(s16[2,16,3200]{2,1,0:T(8,128)(2,1)} %get-tuple-element.39.refs_1_.refs_5_.refs_7_), channel_id=1, source_target_pairs={{0,2},{1,3},{4,0},{5,1},{8,4},{9,5},{12,8},{13,9},{14,12},{15,13},... | collective-permute-start | bytes 614408 | tf_op jit(solution)/shard_map/ppermute | solution.py:365
  6.3 13.5 %collective-permute-start.2 = (f32[24,128]{1,0:T(8,128)}, f32[24,128]{1,0:T(8,128)S(1)}, u32[]{:S(2)}, u32[]{:S(2)}) collective-permute-start(f32[24,128]{1,0:T(8,128)} %get-tuple-element.38.refs_3_), channel_id=1, source_target_pairs={{0,1},{1,0},{2,3},{3,2},{4,5},{5,4},{6,7},{7,6},{8,9},{9,8},{10,11... | collective-permute-start | bytes 36872 | tf_op jit(solution)/shard_map/ppermute | solution.py:387
  11.7 6.5 %collective-permute-start.7 = (s16[2,16,3200]{2,1,0:T(8,128)(2,1)S(1)}, s16[2,16,3200]{2,1,0:T(8,128)(2,1)S(1)}, u32[]{:S(2)}, u32[]{:S(2)}) collective-permute-start(s16[2,16,3200]{2,1,0:T(8,128)(2,1)S(1)} %collective-permute-done.6.refs_8_.refs_12_.refs_14_), channel_id=1, source_target_pairs={{0,4},{1,5},{4,8},{5,9},{8,12},{9,13},{12,14},{13,15},{14,10},{15,... | collective-permute-start | bytes 614408 | tf_op jit(solution)/shard_map/ppermute | solution.py:365
  13.6 15.3 %copy-start.4 = (s32[16]{0:T(128)S(1)}, s32[16]{0:T(128)}, u32[]{:S(2)}) copy-start(s32[16]{0:T(128)} %param.13) | copy-start | bytes 196
  13.7 20.8 %copy-start.2 = (s16[2,16,3200]{2,1,0:T(8,128)(2,1)S(1)}, s16[2,16,3200]{2,1,0:T(8,128)(2,1)}, u32[]{:S(2)}) copy-start(s16[2,16,3200]{2,1,0:T(8,128)(2,1)} %get-tuple-element.39.refs_1_.refs_5_.refs_7_) | copy-start | bytes 614404
  13.7 21.5 %copy-start = (bf16[128,8,1024]{2,1,0:T(8,128)(2,1)S(1)}, bf16[128,8,1024]{2,1,0:T(8,128)(2,1)}, u32[]{:S(2)}) copy-start(bf16[128,8,1024]{2,1,0:T(8,128)(2,1)} %param.10) | copy-start | bytes 6291460
  18.3 5.8 %collective-permute-start.8 = (s16[2,16,3200]{2,1,0:T(8,128)(2,1)S(1)}, s16[2,16,3200]{2,1,0:T(8,128)(2,1)S(1)}, u32[]{:S(2)}, u32[]{:S(2)}) collective-permute-start(s16[2,16,3200]{2,1,0:T(8,128)(2,1)S(1)} %collective-permute-done.7.refs_7_.refs_11_.refs_13_), channel_id=1, source_target_pairs={{0,4},{1,5},{4,8},{5,9},{8,12},{9,13},{12,14},{13,15},{14,10},{15,... | collective-permute-start | bytes 614408 | tf_op jit(solution)/shard_map/ppermute | solution.py:365
  22.5 6.3 %collective-permute-start.4 = (s16[2,16,3200]{2,1,0:T(8,128)(2,1)S(1)}, s16[2,16,3200]{2,1,0:T(8,128)(2,1)S(1)}, u32[]{:S(2)}, u32[]{:S(2)}) collective-permute-start(s16[2,16,3200]{2,1,0:T(8,128)(2,1)S(1)} %get-tuple-element.45.refs_2_.refs_6_.refs_8_), channel_id=1, source_target_pairs={{0,2},{1,3},{4,0},{5,1},{8,4},{9,5},{12,8},{13,9},{14,12},{15,13},... | collective-permute-start | bytes 614408 | tf_op jit(solution)/shard_map/ppermute | solution.py:365
  24.0 5.8 %collective-permute-start.9 = (s16[2,16,3200]{2,1,0:T(8,128)(2,1)S(1)}, s16[2,16,3200]{2,1,0:T(8,128)(2,1)S(1)}, u32[]{:S(2)}, u32[]{:S(2)}) collective-permute-start(s16[2,16,3200]{2,1,0:T(8,128)(2,1)S(1)} %collective-permute-done.8.refs_6_.refs_10_.refs_12_), channel_id=1, source_target_pairs={{0,4},{1,5},{4,8},{5,9},{8,12},{9,13},{12,14},{13,15},{14,10},{15,... | collective-permute-start | bytes 614408 | tf_op jit(solution)/shard_map/ppermute | solution.py:365
  28.8 5.8 %collective-permute-start.5 = (s16[2,16,3200]{2,1,0:T(8,128)(2,1)S(1)}, s16[2,16,3200]{2,1,0:T(8,128)(2,1)S(1)}, u32[]{:S(2)}, u32[]{:S(2)}) collective-permute-start(s16[2,16,3200]{2,1,0:T(8,128)(2,1)S(1)} %collective-permute-done.4.refs_3_.refs_7_.refs_9_), channel_id=1, source_target_pairs={{0,2},{1,3},{4,0},{5,1},{8,4},{9,5},{12,8},{13,9},{14,12},{15,13},... | collective-permute-start | bytes 614408 | tf_op jit(solution)/shard_map/ppermute | solution.py:365
  35.1 3.5 %collective-permute-start.10 = (f32[8,128]{1,0:T(8,128)S(1)}, f32[8,128]{1,0:T(8,128)S(1)}, u32[]{:S(2)}, u32[]{:S(2)}) collective-permute-start(f32[8,128]{1,0:T(8,128)S(1)} %shard_map.131.refs_0_.refs_4_), channel_id=1, source_target_pairs={{0,1},{1,0},{2,3},{3,2},{4,5},{5,4},{6,7},{7,6},{8,9},{9,8},{10,11... | collective-permute-start | bytes 12296 | tf_op jit(solution)/shard_map/ppermute | solution.py:387
  40.8 6.4 %collective-permute-start.11 = (bf16[256,2048]{1,0:T(8,128)(2,1)S(1)}, bf16[256,2048]{1,0:T(8,128)(2,1)S(1)}, u32[]{:S(2)}, u32[]{:S(2)}) collective-permute-start(bf16[256,2048]{1,0:T(8,128)(2,1)S(1)} %get-tuple-element.53), channel_id=1, source_target_pairs={{0,1},{1,0},{2,3},{3,2},{4,5},{5,4},{6,7},{7,6},{8,9},{9,8},{10,11... | collective-permute-start | bytes 3145736 | tf_op jit(solution)/shard_map/ppermute | solution.py:387
  45.4 7.4 %collective-permute-start.12 = (s16[2,16,3200]{2,1,0:T(8,128)(2,1)S(1)}, s16[2,16,3200]{2,1,0:T(8,128)(2,1)S(1)}, u32[]{:S(2)}, u32[]{:S(2)}) collective-permute-start(s16[2,16,3200]{2,1,0:T(8,128)(2,1)S(1)} %get-tuple-element.55), channel_id=1, source_target_pairs={{0,4},{1,5},{2,6},{3,7},{4,0},{5,1},{6,2},{7,3},{8,12},{9,13},{10,... | collective-permute-start | bytes 614408 | tf_op jit(solution)/shard_map/ppermute | solution.py:387
  47.0 7.6 %collective-permute-start.13 = (s16[2,16,3200]{2,1,0:T(8,128)(2,1)S(1)}, s16[2,16,3200]{2,1,0:T(8,128)(2,1)S(1)}, u32[]{:S(2)}, u32[]{:S(2)}) collective-permute-start(s16[2,16,3200]{2,1,0:T(8,128)(2,1)S(1)} %get-tuple-element.58), channel_id=1, source_target_pairs={{0,2},{1,3},{2,0},{3,1},{4,6},{5,7},{6,4},{7,5},{8,10},{9,11},{10,... | collective-permute-start | bytes 614408 | tf_op jit(solution)/shard_map/ppermute | solution.py:387
  50.5 6.6 %collective-permute-start.14 = (s16[2,16,3200]{2,1,0:T(8,128)(2,1)S(1)}, s16[2,16,3200]{2,1,0:T(8,128)(2,1)S(1)}, u32[]{:S(2)}, u32[]{:S(2)}) collective-permute-start(s16[2,16,3200]{2,1,0:T(8,128)(2,1)S(1)} %get-tuple-element.59), channel_id=1, source_target_pairs={{0,4},{1,5},{2,6},{3,7},{4,0},{5,1},{6,2},{7,3},{8,12},{9,13},{10,... | collective-permute-start | bytes 614408 | tf_op jit(solution)/shard_map/ppermute | solution.py:387
  51.0 10.2 %collective-permute-start.15 = (s16[2,16,3200]{2,1,0:T(8,128)(2,1)S(1)}, s16[2,16,3200]{2,1,0:T(8,128)(2,1)S(1)}, u32[]{:S(2)}, u32[]{:S(2)}) collective-permute-start(s16[2,16,3200]{2,1,0:T(8,128)(2,1)S(1)} %get-tuple-element.62), channel_id=1, source_target_pairs={{0,2},{1,3},{2,0},{3,1},{4,6},{5,7},{6,4},{7,5},{8,10},{9,11},{10,... | collective-permute-start | bytes 614408 | tf_op jit(solution)/shard_map/ppermute | solution.py:387
  53.1 8.1 %collective-permute-start.16 = (s16[16,3200]{1,0:T(8,128)(2,1)S(1)}, s16[16,3200]{1,0:T(8,128)(2,1)S(1)}, u32[]{:S(2)}, u32[]{:S(2)}) collective-permute-start(s16[16,3200]{1,0:T(8,128)(2,1)S(1)} %get-tuple-element.57.refs_0_), channel_id=1, source_target_pairs={{0,2},{1,3},{2,0},{3,1},{4,6},{5,7},{6,4},{7,5},{8,10},{9,11},{10,... | collective-permute-start | bytes 307208 | tf_op jit(solution)/shard_map/ppermute | solution.py:387
  57.3 7.2 %collective-permute-start.17 = (s16[16,3200]{1,0:T(8,128)(2,1)S(1)}, s16[16,3200]{1,0:T(8,128)(2,1)S(1)}, u32[]{:S(2)}, u32[]{:S(2)}) collective-permute-start(s16[16,3200]{1,0:T(8,128)(2,1)S(1)} %get-tuple-element.61.refs_0_), channel_id=1, source_target_pairs={{0,2},{1,3},{2,0},{3,1},{4,6},{5,7},{6,4},{7,5},{8,10},{9,11},{10,... | collective-permute-start | bytes 307208 | tf_op jit(solution)/shard_map/ppermute | solution.py:387
  61.4 7.8 %collective-permute-start.18 = (s16[16,3200]{1,0:T(8,128)(2,1)S(1)}, s16[16,3200]{1,0:T(8,128)(2,1)S(1)}, u32[]{:S(2)}, u32[]{:S(2)}) collective-permute-start(s16[16,3200]{1,0:T(8,128)(2,1)S(1)} %shard_map.138.refs_0_), channel_id=1, source_target_pairs={{0,8},{1,9},{2,10},{3,11},{4,12},{5,13},{6,14},{7,15},{8,0},{9,1},... | collective-permute-start | bytes 307208 | tf_op jit(solution)/shard_map/ppermute | solution.py:387
  64.3 8.4 %collective-permute-start.20 = (s16[2,16,3200]{2,1,0:T(8,128)(2,1)S(1)}, s16[2,16,3200]{2,1,0:T(8,128)(2,1)S(1)}, u32[]{:S(2)}, u32[]{:S(2)}) collective-permute-start(s16[2,16,3200]{2,1,0:T(8,128)(2,1)S(1)} %get-tuple-element.65.refs_0_), channel_id=1, source_target_pairs={{0,4},{1,5},{2,6},{3,7},{4,0},{5,1},{6,2},{7,3},{8,12},{9,13},{10,... | collective-permute-start | bytes 614408 | tf_op jit(solution)/shard_map/ppermute | solution.py:387
  64.7 8.0 %collective-permute-start.19 = (s16[16,3200]{1,0:T(8,128)(2,1)S(1)}, s16[16,3200]{1,0:T(8,128)(2,1)S(1)}, u32[]{:S(2)}, u32[]{:S(2)}) collective-permute-start(s16[16,3200]{1,0:T(8,128)(2,1)S(1)} %shard_map.140.refs_0_), channel_id=1, source_target_pairs={{0,8},{1,9},{2,10},{3,11},{4,12},{5,13},{6,14},{7,15},{8,0},{9,1},... | collective-permute-start | bytes 307208 | tf_op jit(solution)/shard_map/ppermute | solution.py:387
  (2 other events, 3.5 us)

commit v13 on v12

--- a/solution.py
+++ b/solution.py
@@ -97,7 +97,8 @@
     prior_ref[...] = jnp.zeros_like(prior_ref)
     for block, number in enumerate((me, me ^ 1)):
         total = jnp.zeros((1, lanes), f32)
-        for offset, piece_ref in enumerate(piece_refs):
+        for offset in range(slots):
+            piece_ref = piece_refs[offset]
             device = place_ref[1 + slots + offset]
             tail = piece_ref[0, :, piece_ref.shape[2] - lanes :]
             counts = tail.astype(jnp.int32).astype(f32)[0:1]
@@ -105,9 +106,22 @@
         prior_ref[block : block + 1] = total
 
 
-def tokens_kernel(top, masks, place_ref, own_ref, other_ref, piece_ref, *outs):
-    small_ref, rank_ref, gate_ref, same_ref, mask_ref, onward_ref = outs
-    onward_ref[...] = piece_ref[...]
+def piece_part(refs, offset, kind):
+    last = len(refs) - 2
+    half = last // 2 + 1
+    if offset == half:
+        return refs[last + kind][0]
+    return refs[offset if offset < half else offset - 1][kind]
+
+
+def tokens_kernel(top, masks, place_ref, own_ref, other_ref, hidden_other_ref, gradient_other_ref, *outs):
+    small_ref, rank_ref, gate_ref, same_ref, mask_ref, hidden_ref, gradient_ref, sem = outs
+    copies = [
+        pltpu.make_async_copy(hidden_other_ref, hidden_ref, sem.at[0]),
+        pltpu.make_async_copy(gradient_other_ref, gradient_ref, sem.at[1]),
+    ]
+    for copy in copies:
+        copy.start()
     small_ref[...] = jnp.concatenate([own_ref[...], other_ref[...]], axis=1).T
     experts, gates, _ = token_columns(small_ref, top)
     _, tokens, wide = rank_ref.shape
@@ -136,16 +150,18 @@
         own = lax.broadcasted_iota(jnp.int32, named.shape, 1) == position
         expert = jnp.sum(jnp.where(own, named, 0.0), axis=1, keepdims=True)
         mask_ref[core] = jnp.where(expert == column, 1.0, 0.0).astype(bf16)
+    for copy in copies:
+        copy.wait()
 
 
 def reduce_kernel(top, masks, place_ref, small_ref, own_ref, other_ref, *rest):
     slots = len(masks)
-    piece_refs, (reduced_ref, high_ref, low_ref, full_ref) = rest[:slots], rest[slots:]
+    piece_refs, (reduced_ref, high_ref, low_ref, full_ref) = rest[: slots + 1], rest[slots + 1 :]
     hidden_width = own_ref.shape[1]
     for offset in range(slots):
         slot = place_ref[1 + offset]
         for kind in range(2):
-            down, _ = decode(piece_refs[offset][kind], hidden_width)
+            down, _ = decode(piece_part(piece_refs, offset, kind), hidden_width)
             high_ref[kind, slot], low_ref[kind, slot] = halves(down)
     experts, _, _ = token_columns(small_ref, top)
     wide = reduced_ref.shape[2]
@@ -181,8 +197,8 @@
 
 def tangent_kernel(masks, place_ref, rank_ref, gate_ref, capacity_ref, prior_ref, arrived_ref, reduced_ref, *rest):
     slots = len(masks)
-    piece_refs = rest[:slots]
-    weight_ref, weighted_ref, tangent_ref, coded_ref, high_ref, low_ref = rest[slots:]
+    piece_refs = rest[: slots + 1]
+    weight_ref, weighted_ref, tangent_ref, coded_ref, high_ref, low_ref = rest[slots + 1 :]
     _, wide = weight_ref.shape
     model_width = tangent_ref.shape[1]
     hidden_width = piece_refs[0].shape[2] - model_width - lanes
@@ -197,7 +213,7 @@
     for offset in range(slots):
         slot = place_ref[1 + offset]
         for kind in range(2):
-            _, up = decode(piece_refs[offset][kind], hidden_width)
+            _, up = decode(piece_part(piece_refs, offset, kind), hidden_width)
             high_ref[kind, slot], low_ref[kind, slot] = halves(up)
     factor = high_ref[...].reshape(2 * wide, model_width), low_ref[...].reshape(2 * wide, model_width)
     tangent = dot_pairs(halves(weighted), factor, 1, 0)
@@ -303,7 +319,8 @@
     put_chunks(keep_ref, near_ref, chunk_ref, far_ref, add_halves(down), up_ref[...] + up)
 
 
-def pair_kernel(hidden_width, arrived_ref, chunk_ref, across_ref, keep_ref):
+def pair_kernel(hidden_width, arrived_ref, chunk_ref, near_ref, across_ref, keep_ref, onward_ref):
+    onward_ref[...] = near_ref[...]
     for x in range(2):
         down, up = decode(arrived_ref[x], hidden_width)
         down, up = chunk_ref[x, :, :hidden_width] + down, chunk_ref[x, :, hidden_width:] + up
@@ -370,16 +387,16 @@
         there = (place + jnp.arange(self.length, dtype=jnp.int32)) % self.length
         return jnp.where(there < rows, 4 * there, 4 * (self.length - 1 - there) + 2) + me % 2
 
-    def gather(self, own, passing):
+    def gather(self, own):
         half = self.length // 2
         found = {0: own}
         ahead, behind = own, own
-        for step in range(1, half + 1):
-            behind = found[self.length - step] = self.shift(behind, 1)
-            if step < half:
-                ahead = self.shift(ahead, -1)
-                ahead = found[step] = passing(ahead) if step == 1 else ahead
-        return [found[offset] for offset in range(self.length)]
+        for step in range(1, half):
+            behind = self.shift(behind, 1)
+            ahead = self.shift(ahead, -1)
+            found[self.length - step], found[step] = behind, ahead
+        last = [self.shift(behind[:1], 1), self.shift(ahead[1:], -1)]
+        return [found[offset] for offset in sorted(found)] + last
 
 
 def exchange(value, mask):
@@ -455,37 +472,32 @@
     )
     small_other = exchange(small, 1)
     hidden = hidden_of_route.reshape(tokens * top, hidden_width)
-    beside = []
-
-    hidden_other = exchange(hidden, 1)
-    gradient_other = exchange(output_gradient, 1)
-
-    def passing(piece):
-        *made, onward = call(
-            functools.partial(tokens_kernel, top, masks),
-            10**9,
-            [
-                ((both, small.shape[0]), f32),
-                ((2, tokens, wide), f32),
-                ((2, tokens, wide), f32),
-                ((top * tokens, tokens), bf16),
-                ((2, top * tokens, wide), bf16),
-                (piece.shape, i16),
-            ],
-            place,
-            small,
-            small_other,
-            piece,
-            after=[hidden_other, gradient_other],
-        )
-        beside.extend(made)
-        return onward
-
-    pieces = ring.gather(piece, passing)
-    small_columns, local_rank, gate, same, mask = beside
+    small_columns, local_rank, gate, same, mask, hidden_other, gradient_other = call(
+        functools.partial(tokens_kernel, top, masks),
+        10**9,
+        [
+            ((both, small.shape[0]), f32),
+            ((2, tokens, wide), f32),
+            ((2, tokens, wide), f32),
+            ((top * tokens, tokens), bf16),
+            ((2, top * tokens, wide), bf16),
+            (hidden.shape, bf16),
+            (output_gradient.shape, bf16),
+        ],
+        place,
+        small,
+        small_other,
+        exchange(hidden, 1),
+        exchange(output_gradient, 1),
+        scratch=[pltpu.SemaphoreType.DMA((2,))],
+    )
+    pieces = ring.gather(piece)
     capacity_row = jnp.pad(capacity.astype(f32), (counts_lane, lanes - counts_lane - experts))[None, :]
 
-    (prior,) = call(functools.partial(prior_kernel, masks), 10**8, [((8, lanes), f32)], place, *pieces)
+    by_offset = pieces[:rows] + [pieces[-2]] + pieces[rows:-2]
+    (prior,) = call(
+        functools.partial(prior_kernel, masks), 10**8, [((8, lanes), f32)], place, *by_offset, after=[same]
+    )
     prior_arrived = exchange(prior, 1)
     factor_halves = [pltpu.VMEM((2, slots, rank, hidden_width), bf16)] * 2
     (reduced,) = call(
@@ -570,27 +582,20 @@
         return call(functools.partial(kernel, hidden_width), hop, outs, *operands, after=after)
 
     curvature_far = exchange(curvature_far, 4)
+    pair = [(one_coded, i16), (one, f32), ((2,) + one_coded, i16)]
+    gradient_across, gradient_pair, curvature_near = hop_call(
+        pair_kernel, pair, gradient_far, gradient_chunk, curvature_near, after=[curvature_keep]
+    )
     curvature_near = exchange(curvature_near, 2)
-    gradient_across, gradient_pair = hop_call(
-        pair_kernel,
-        [(one_coded, i16), (one, f32)],
-        gradient_far,
-        gradient_chunk,
-        after=[curvature_keep],
-    )
-    curvature_across, curvature_pair = hop_call(
-        pair_kernel,
-        [(one_coded, i16), (one, f32)],
-        curvature_far,
-        curvature_chunk,
-        after=[gradient_across, gradient_near],
+    curvature_across, curvature_pair, gradient_near = hop_call(
+        pair_kernel, pair, curvature_far, curvature_chunk, gradient_near, after=[gradient_across]
     )
     (gradient_beyond,) = hop_call(
         far_kernel,
         [(one_coded, i16)],
         exchange(gradient_across, 2),
         gradient_pair,
-        after=[curvature_across, curvature_near],
+        after=[curvature_across],
     )
     onward, total = hop_call(
         near_kernel,

time: 73.8 us -> 68.2 us (0.924)
  waiting for transfers between devices: 32.7 us -> 22.6 us
  starting transfers between devices: 19.7 us -> 23.3 us
    ppermute x7 -> x8, waiting for transfers between devices: 19.5 us -> 14.1 us  [shift(): return lax.ppermute(value, 'expert', pairs)]
    ppermute x14, waiting for transfers between devices: 13.2 us -> 8.48 us  [exchange(): lax.ppermute(value, 'expert', [(device, device ^ mask) for device in rang...]
    ppermute x14, starting transfers between devices: 10.9 us -> 14.5 us  [exchange(): lax.ppermute(value, 'expert', [(device, device ^ mask) for device in rang...]
    ppermute x7 -> x8, starting transfers between devices: 8.83 us -> 8.83 us  [shift(): return lax.ppermute(value, 'expert', pairs)]
  transfers between devices with their start and end apart: 21 -> 22, of which waited for: 11 -> 8; matrix products, arithmetic and copies ran while one was open for 0% -> 1% of each run, Pallas kernels for 21% -> 24%
where the time goes in v13:
time: 68.2 us; the launch traced here: 67.9 us
  starting transfers between devices  23.3 us (34%)
  waiting for transfers between devices  22.6 us (33%)
  Pallas kernels  19.6 us (29%)
  local copies, waits for them, and re-layouts  0.84 us (1%)
  between operations  0.82 us (1%)
  other arithmetic  0.77 us (1%)
    pallas_call x14, Pallas kernels, call(): pl.pallas_call(lambda *refs: kernel(*refs[len(after):]), out_shape=[jax.S...  19.6 us
    ppermute x14, starting transfers between devices, exchange(): lax.ppermute(value, 'expert', [(device, device ^ mask) for device in rang...  14.5 us
    ppermute x8, waiting for transfers between devices, shift(): return lax.ppermute(value, 'expert', pairs)  14.1 us
    ppermute x8, starting transfers between devices, shift(): return lax.ppermute(value, 'expert', pairs)  8.83 us
    ppermute x14, waiting for transfers between devices, exchange(): lax.ppermute(value, 'expert', [(device, device ^ mask) for device in rang...  8.48 us
  transfers between devices with their start and end apart: 22, of which 8 were waited for; matrix products, arithmetic and copies ran while one was open for 1% of the time, Pallas kernels for 24%

profile of v13, /device:TPU:0, one launch (start us, length us, event | category | flops | bytes accessed | tf_op | source)
XLA Modules:
  0.0 67.9 jit_solution(15608037754304342274)
XLA Ops:
  1.2 2.0 %shard_map.129 = (s16[2,16,3200]{2,1,0:T(8,128)(2,1)}, f32[24,128]{1,0:T(8,128)}) custom-call(s32[8,128]{1,0:T(8,128)} %bitcast.31, bf16[8,128]{1,0:T(8,128)(2,1)} %bitcast.32, f32[1,128]{1,0:T(1,128)} %bitcast.33, f32[16,1024]{1,0:T(8,128)} %bitcast.29, f32[16,1024]{1,0:T(8,128)} %bitcast.30, f32[16,2048]{1,0:T(8,128)} %bitcast.27, f32[16,2048]{1,0:T(8,128)} %bitcast.28), custom_call_target="tpu_custom_call" | custom-call | flops 200000000 | bytes 1048576 | tf_op jit(solution)/shard_map/pallas_call | solution.py:443
  3.2 2.6 %collective-permute-start.6 = (s16[2,16,3200]{2,1,0:T(8,128)(2,1)}, s16[2,16,3200]{2,1,0:T(8,128)(2,1)S(1)}, u32[]{:S(2)}, u32[]{:S(2)}) collective-permute-start(s16[2,16,3200]{2,1,0:T(8,128)(2,1)} %get-tuple-element.48.refs_2_.refs_5_.refs_7_), channel_id=1, source_target_pairs={{0,4},{1,5},{4,8},{5,9},{8,12},{9,13},{12,14},{13,15},{14,10},{15,... | collective-permute-start | bytes 614408 | tf_op jit(solution)/shard_map/ppermute | solution.py:382
  6.0 5.6 %collective-permute-done.6.refs_9_.refs_11_.refs_13_ = s16[2,16,3200]{2,1,0:T(8,128)(2,1)S(1)} collective-permute-done((s16[2,16,3200]{2,1,0:T(8,128)(2,1)}, s16[2,16,3200]{2,1,0:T(8,128)(2,1)S(1)}, u32[]{:S(2)}, u32[]{:S(2)}) %collective-permute-start.6) | collective-permute-done | bytes 204832 | tf_op jit(solution)/shard_map/ppermute | solution.py:382
  11.7 1.8 %collective-permute-start.7 = (s16[2,16,3200]{2,1,0:T(8,128)(2,1)S(1)}, s16[2,16,3200]{2,1,0:T(8,128)(2,1)S(1)}, u32[]{:S(2)}, u32[]{:S(2)}) collective-permute-start(s16[2,16,3200]{2,1,0:T(8,128)(2,1)S(1)} %collective-permute-done.6.refs_9_.refs_11_.refs_13_), channel_id=1, source_target_pairs={{0,4},{1,5},{4,8},{5,9},{8,12},{9,13},{12,14},{13,15},{14,10},{15,... | collective-permute-start | bytes 614408 | tf_op jit(solution)/shard_map/ppermute | solution.py:382
  14.4 4.2 %collective-permute-done.7.refs_8_.refs_10_.refs_12_ = s16[2,16,3200]{2,1,0:T(8,128)(2,1)S(1)} collective-permute-done((s16[2,16,3200]{2,1,0:T(8,128)(2,1)S(1)}, s16[2,16,3200]{2,1,0:T(8,128)(2,1)S(1)}, u32[]{:S(2)}, u32[]{:S(2)}) %collective-permute-start.7) | collective-permute-done | bytes 204832 | tf_op jit(solution)/shard_map/ppermute | solution.py:382
  18.6 1.6 %collective-permute-start.8 = (s16[2,16,3200]{2,1,0:T(8,128)(2,1)S(1)}, s16[2,16,3200]{2,1,0:T(8,128)(2,1)S(1)}, u32[]{:S(2)}, u32[]{:S(2)}) collective-permute-start(s16[2,16,3200]{2,1,0:T(8,128)(2,1)S(1)} %collective-permute-done.7.refs_8_.refs_10_.refs_12_), channel_id=1, source_target_pairs={{0,4},{1,5},{4,8},{5,9},{8,12},{9,13},{12,14},{13,15},{14,10},{15,... | collective-permute-start | bytes 614408 | tf_op jit(solution)/shard_map/ppermute | solution.py:382
  20.7 3.9 %collective-permute-done.8.refs_7_.refs_9_.refs_11_ = s16[2,16,3200]{2,1,0:T(8,128)(2,1)S(1)} collective-permute-done((s16[2,16,3200]{2,1,0:T(8,128)(2,1)S(1)}, s16[2,16,3200]{2,1,0:T(8,128)(2,1)S(1)}, u32[]{:S(2)}, u32[]{:S(2)}) %collective-permute-start.8) | collective-permute-done | bytes 204832 | tf_op jit(solution)/shard_map/ppermute | solution.py:382
  24.6 1.4 %collective-permute-start.9 = (s16[1,16,3200]{2,1,0:T(8,128)(2,1)S(1)}, s16[1,16,3200]{2,1,0:T(8,128)(2,1)S(1)}, u32[]{:S(2)}, u32[]{:S(2)}) collective-permute-start(s16[1,16,3200]{2,1,0:T(8,128)(2,1)S(1)} %slice.8), channel_id=1, source_target_pairs={{0,4},{1,5},{4,8},{5,9},{8,12},{9,13},{12,14},{13,15},{14,10},{15,... | collective-permute-start | bytes 307208 | tf_op jit(solution)/shard_map/ppermute | solution.py:382
  27.5 2.2 %shard_map.130 = (f32[256,24]{1,0:T(8,128)S(1)}, f32[2,128,128]{2,1,0:T(8,128)S(1)}, f32[2,128,128]{2,1,0:T(8,128)S(1)}, bf16[1024,128]{1,0:T(8,128)(2,1)S(1)}, ...) custom-call(s32[17]{0:T(128)S(1)} %pad_add_fusion.refs_0_.refs_1_, ...), custom_call_target="tpu_custom_call" | custom-call | flops 2000000000 | bytes 1048576 | tf_op jit(solution)/shard_map/pallas_call | solution.py:443
  30.8 3.4 %shard_map.132.refs_6_ = f32[2,256,128]{2,1,0:T(8,128)S(1)} custom-call(f32[8,128]{1,0:T(8,128)S(1)} %shard_map.131.refs_0_.refs_4_, s32[17]{0:T(128)S(1)} %pad_add_fusion.refs_0_.refs_1_, f32[256,24]{1,0:T(8,128)S(1)} %get-tuple-element.42.refs_2_.refs_0_, bf16[1024,1024]{1,0:T(8,128)(2,1)S(1)} %bitcast.24, ...), custom_call_target="tpu_custom_call" | custom-call | flops 2147483648 | bytes 1048576 | tf_op jit(solution)/shard_map/pallas_call | solution.py:443
  34.3 2.2 %shard_map.133 = (f32[256,128]{1,0:T(8,128)S(1)}, f32[256,256]{1,0:T(8,128)S(1)}, f32[256,2048]{1,0:T(8,128)S(1)}, bf16[256,2048]{1,0:T(8,128)(2,1)S(1)}, bf16[2...) custom-call(s32[17]{0:T(128)S(1)} %pad_add_fusion.refs_0_.refs_1_, ...), custom_call_target="tpu_custom_call" | custom-call | flops 805306368 | bytes 1048576 | tf_op jit(solution)/shard_map/pallas_call | solution.py:443
  36.6 4.0 %shard_map.134 = (f32[2,16,3072]{2,1,0:T(8,128)S(1)}, s16[2,16,3200]{2,1,0:T(8,128)(2,1)S(1)}, f32[2,16,3072]{2,1,0:T(8,128)S(1)}, s16[2,16,3200]{2,1,0:T(8,128)...) custom-call(bf16[1024,128]{1,0:T(8,128)(2,1)S(1)} %get-tuple-element.43.refs_0_.refs_1_, ...), custom_call_target="tpu_custom_call" | custom-call | flops 2147483648 | bytes 1048576 | tf_op jit(solution)/shard_map/pallas_call | solution.py:443
  40.6 1.6 %collective-permute-start.13 = (s16[2,16,3200]{2,1,0:T(8,128)(2,1)S(1)}, s16[2,16,3200]{2,1,0:T(8,128)(2,1)S(1)}, u32[]{:S(2)}, u32[]{:S(2)}) collective-permute-start(s16[2,16,3200]{2,1,0:T(8,128)(2,1)S(1)} %get-tuple-element.59), channel_id=1, source_target_pairs={{0,4},{1,5},{2,6},{3,7},{4,0},{5,1},{6,2},{7,3},{8,12},{9,13},{10,... | collective-permute-start | bytes 614408 | tf_op jit(solution)/shard_map/ppermute | solution.py:404
  42.2 1.3 %collective-permute-start.15 = (s16[2,16,3200]{2,1,0:T(8,128)(2,1)S(1)}, s16[2,16,3200]{2,1,0:T(8,128)(2,1)S(1)}, u32[]{:S(2)}, u32[]{:S(2)}) collective-permute-start(s16[2,16,3200]{2,1,0:T(8,128)(2,1)S(1)} %get-tuple-element.65), channel_id=1, source_target_pairs={{0,2},{1,3},{2,0},{3,1},{4,6},{5,7},{6,4},{7,5},{8,10},{9,11},{10,... | collective-permute-start | bytes 614408 | tf_op jit(solution)/shard_map/ppermute | solution.py:404
  43.5 3.2 %shard_map.135 = (f32[2,16,3072]{2,1,0:T(8,128)S(1)}, s16[2,16,3200]{2,1,0:T(8,128)(2,1)S(1)}, f32[2,16,3072]{2,1,0:T(8,128)S(1)}, s16[2,16,3200]{2,1,0:T(8,128)(2,1)S(1)}) custom-call(f32[256,24]{1,0:T(8,128)S(1)} %get-tuple-element.42.refs_2_.refs_0_, bf16[1024,128]{1,0:T(8,128)(2,1)S(1)} %get-tuple-element.43.refs_0_.refs_1_, ...), custom_call_target="tpu_custom_call" | custom-call | flops 1879048192 | bytes 1048576 | tf_op jit(solution)/shard_map/pallas_call | solution.py:443
  47.3 0.8 %collective-permute-done.13.refs_1_ = s16[2,16,3200]{2,1,0:T(8,128)(2,1)S(1)} collective-permute-done((s16[2,16,3200]{2,1,0:T(8,128)(2,1)S(1)}, s16[2,16,3200]{2,1,0:T(8,128)(2,1)S(1)}, u32[]{:S(2)}, u32[]{:S(2)}) %collective-permute-start.13) | collective-permute-done | bytes 204832 | tf_op jit(solution)/shard_map/ppermute | solution.py:404
  48.3 0.9 %collective-permute-start.16 = (s16[16,3200]{1,0:T(8,128)(2,1)S(1)}, s16[16,3200]{1,0:T(8,128)(2,1)S(1)}, u32[]{:S(2)}, u32[]{:S(2)}) collective-permute-start(s16[16,3200]{1,0:T(8,128)(2,1)S(1)} %get-tuple-element.62.refs_0_), channel_id=1, source_target_pairs={{0,2},{1,3},{2,0},{3,1},{4,6},{5,7},{6,4},{7,5},{8,10},{9,11},{10,... | collective-permute-start | bytes 307208 | tf_op jit(solution)/shard_map/ppermute | solution.py:404
  49.3 1.2 %collective-permute-start.17 = (s16[2,16,3200]{2,1,0:T(8,128)(2,1)S(1)}, s16[2,16,3200]{2,1,0:T(8,128)(2,1)S(1)}, u32[]{:S(2)}, u32[]{:S(2)}) collective-permute-start(s16[2,16,3200]{2,1,0:T(8,128)(2,1)S(1)} %get-tuple-element.69), channel_id=1, source_target_pairs={{0,2},{1,3},{2,0},{3,1},{4,6},{5,7},{6,4},{7,5},{8,10},{9,11},{10,... | collective-permute-start | bytes 614408 | tf_op jit(solution)/shard_map/ppermute | solution.py:404
  50.4 2.8 %collective-permute-done.14.refs_1_ = s16[2,16,3200]{2,1,0:T(8,128)(2,1)S(1)} collective-permute-done((s16[2,16,3200]{2,1,0:T(8,128)(2,1)S(1)}, s16[2,16,3200]{2,1,0:T(8,128)(2,1)S(1)}, u32[]{:S(2)}, u32[]{:S(2)}) %collective-permute-start.14) | collective-permute-done | bytes 204832 | tf_op jit(solution)/shard_map/ppermute | solution.py:404
  53.5 1.2 %collective-permute-start.18 = (s16[16,3200]{1,0:T(8,128)(2,1)S(1)}, s16[16,3200]{1,0:T(8,128)(2,1)S(1)}, u32[]{:S(2)}, u32[]{:S(2)}) collective-permute-start(s16[16,3200]{1,0:T(8,128)(2,1)S(1)} %get-tuple-element.66.refs_0_), channel_id=1, source_target_pairs={{0,2},{1,3},{2,0},{3,1},{4,6},{5,7},{6,4},{7,5},{8,10},{9,11},{10,... | collective-permute-start | bytes 307208 | tf_op jit(solution)/shard_map/ppermute | solution.py:404
  54.9 2.6 %collective-permute-start.19 = (s16[16,3200]{1,0:T(8,128)(2,1)S(1)}, s16[16,3200]{1,0:T(8,128)(2,1)S(1)}, u32[]{:S(2)}, u32[]{:S(2)}) collective-permute-start(s16[16,3200]{1,0:T(8,128)(2,1)S(1)} %shard_map.138.refs_0_), channel_id=1, source_target_pairs={{0,8},{1,9},{2,10},{3,11},{4,12},{5,13},{6,14},{7,15},{8,0},{9,1},... | collective-permute-start | bytes 307208 | tf_op jit(solution)/shard_map/ppermute | solution.py:404
  58.6 1.6 %collective-permute-start.21 = (s16[2,16,3200]{2,1,0:T(8,128)(2,1)S(1)}, s16[2,16,3200]{2,1,0:T(8,128)(2,1)S(1)}, u32[]{:S(2)}, u32[]{:S(2)}) collective-permute-start(s16[2,16,3200]{2,1,0:T(8,128)(2,1)S(1)} %get-tuple-element.71.refs_0_), channel_id=1, source_target_pairs={{0,4},{1,5},{2,6},{3,7},{4,0},{5,1},{6,2},{7,3},{8,12},{9,13},{10,... | collective-permute-start | bytes 614408 | tf_op jit(solution)/shard_map/ppermute | solution.py:404
  60.4 2.6 %collective-permute-start.20 = (s16[16,3200]{1,0:T(8,128)(2,1)S(1)}, s16[16,3200]{1,0:T(8,128)(2,1)S(1)}, u32[]{:S(2)}, u32[]{:S(2)}) collective-permute-start(s16[16,3200]{1,0:T(8,128)(2,1)S(1)} %shard_map.140.refs_0_), channel_id=1, source_target_pairs={{0,8},{1,9},{2,10},{3,11},{4,12},{5,13},{6,14},{7,15},{8,0},{9,1},... | collective-permute-start | bytes 307208 | tf_op jit(solution)/shard_map/ppermute | solution.py:404
  63.1 3.9 %collective-permute-done.21.refs_3_ = s16[2,16,3200]{2,1,0:T(8,128)(2,1)S(1)} collective-permute-done((s16[2,16,3200]{2,1,0:T(8,128)(2,1)S(1)}, s16[2,16,3200]{2,1,0:T(8,128)(2,1)S(1)}, u32[]{:S(2)}, u32[]{:S(2)}) %collective-permute-start.21) | collective-permute-done | bytes 204832 | tf_op jit(solution)/shard_map/ppermute | solution.py:404
  (48 shorter events, 8.2 us)
Async XLA Ops:
  0.6 26.2 %collective-permute-start.1 = (bf16[1024,1024]{1,0:T(8,128)(2,1)}, bf16[1024,1024]{1,0:T(8,128)(2,1)S(1)}, u32[]{:S(2)}, u32[]{:S(2)}) collective-permute-start(bf16[1024,1024]{1,0:T(8,128)(2,1)} %bitcast.23), channel_id=1, source_target_pairs={{0,1},{1,0},{2,3},{3,2},{4,5},{5,4},{6,7},{7,6},{8,9},{9,8},{10,11... | collective-permute-start | bytes 6291464 | tf_op jit(solution)/shard_map/ppermute | solution.py:404
  3.2 8.5 %collective-permute-start.6 = (s16[2,16,3200]{2,1,0:T(8,128)(2,1)}, s16[2,16,3200]{2,1,0:T(8,128)(2,1)S(1)}, u32[]{:S(2)}, u32[]{:S(2)}) collective-permute-start(s16[2,16,3200]{2,1,0:T(8,128)(2,1)} %get-tuple-element.48.refs_2_.refs_5_.refs_7_), channel_id=1, source_target_pairs={{0,4},{1,5},{4,8},{5,9},{8,12},{9,13},{12,14},{13,15},{14,10},{15,... | collective-permute-start | bytes 614408 | tf_op jit(solution)/shard_map/ppermute | solution.py:382
  5.8 7.7 %collective-permute-start.3 = (s16[2,16,3200]{2,1,0:T(8,128)(2,1)}, s16[2,16,3200]{2,1,0:T(8,128)(2,1)S(1)}, u32[]{:S(2)}, u32[]{:S(2)}) collective-permute-start(s16[2,16,3200]{2,1,0:T(8,128)(2,1)} %get-tuple-element.48.refs_2_.refs_5_.refs_7_), channel_id=1, source_target_pairs={{0,2},{1,3},{4,0},{5,1},{8,4},{9,5},{12,8},{13,9},{14,12},{15,13},... | collective-permute-start | bytes 614408 | tf_op jit(solution)/shard_map/ppermute | solution.py:382
  5.8 21.0 %collective-permute-start.2 = (bf16[128,2048]{1,0:T(8,128)(2,1)}, bf16[128,2048]{1,0:T(8,128)(2,1)S(1)}, u32[]{:S(2)}, u32[]{:S(2)}) collective-permute-start(bf16[128,2048]{1,0:T(8,128)(2,1)} %refs_4_.1), channel_id=1, source_target_pairs={{0,1},{1,0},{2,3},{3,2},{4,5},{5,4},{6,7},{7,6},{8,9},{9,8},{10,11... | collective-permute-start | bytes 1572872 | tf_op jit(solution)/shard_map/ppermute | solution.py:404
  11.7 6.9 %collective-permute-start.7 = (s16[2,16,3200]{2,1,0:T(8,128)(2,1)S(1)}, s16[2,16,3200]{2,1,0:T(8,128)(2,1)S(1)}, u32[]{:S(2)}, u32[]{:S(2)}) collective-permute-start(s16[2,16,3200]{2,1,0:T(8,128)(2,1)S(1)} %collective-permute-done.6.refs_9_.refs_11_.refs_13_), channel_id=1, source_target_pairs={{0,4},{1,5},{4,8},{5,9},{8,12},{9,13},{12,14},{13,15},{14,10},{15,... | collective-permute-start | bytes 614408 | tf_op jit(solution)/shard_map/ppermute | solution.py:382
  13.5 6.7 %collective-permute-start.4 = (s16[2,16,3200]{2,1,0:T(8,128)(2,1)S(1)}, s16[2,16,3200]{2,1,0:T(8,128)(2,1)S(1)}, u32[]{:S(2)}, u32[]{:S(2)}) collective-permute-start(s16[2,16,3200]{2,1,0:T(8,128)(2,1)S(1)} %collective-permute-done.3.refs_3_.refs_6_.refs_8_), channel_id=1, source_target_pairs={{0,2},{1,3},{4,0},{5,1},{8,4},{9,5},{12,8},{13,9},{14,12},{15,13},... | collective-permute-start | bytes 614408 | tf_op jit(solution)/shard_map/ppermute | solution.py:382
  13.7 13.1 %collective-permute-start = (f32[24,128]{1,0:T(8,128)}, f32[24,128]{1,0:T(8,128)S(1)}, u32[]{:S(2)}, u32[]{:S(2)}) collective-permute-start(f32[24,128]{1,0:T(8,128)} %get-tuple-element.41.refs_1_), channel_id=1, source_target_pairs={{0,1},{1,0},{2,3},{3,2},{4,5},{5,4},{6,7},{7,6},{8,9},{9,8},{10,11... | collective-permute-start | bytes 36872 | tf_op jit(solution)/shard_map/ppermute | solution.py:404
  18.6 6.0 %collective-permute-start.8 = (s16[2,16,3200]{2,1,0:T(8,128)(2,1)S(1)}, s16[2,16,3200]{2,1,0:T(8,128)(2,1)S(1)}, u32[]{:S(2)}, u32[]{:S(2)}) collective-permute-start(s16[2,16,3200]{2,1,0:T(8,128)(2,1)S(1)} %collective-permute-done.7.refs_8_.refs_10_.refs_12_), channel_id=1, source_target_pairs={{0,4},{1,5},{4,8},{5,9},{8,12},{9,13},{12,14},{13,15},{14,10},{15,... | collective-permute-start | bytes 614408 | tf_op jit(solution)/shard_map/ppermute | solution.py:382
  20.2 5.9 %collective-permute-start.5 = (s16[2,16,3200]{2,1,0:T(8,128)(2,1)S(1)}, s16[2,16,3200]{2,1,0:T(8,128)(2,1)S(1)}, u32[]{:S(2)}, u32[]{:S(2)}) collective-permute-start(s16[2,16,3200]{2,1,0:T(8,128)(2,1)S(1)} %collective-permute-done.4.refs_4_.refs_7_.refs_9_), channel_id=1, source_target_pairs={{0,2},{1,3},{4,0},{5,1},{8,4},{9,5},{12,8},{13,9},{14,12},{15,13},... | collective-permute-start | bytes 614408 | tf_op jit(solution)/shard_map/ppermute | solution.py:382
  24.6 5.1 %collective-permute-start.9 = (s16[1,16,3200]{2,1,0:T(8,128)(2,1)S(1)}, s16[1,16,3200]{2,1,0:T(8,128)(2,1)S(1)}, u32[]{:S(2)}, u32[]{:S(2)}) collective-permute-start(s16[1,16,3200]{2,1,0:T(8,128)(2,1)S(1)} %slice.8), channel_id=1, source_target_pairs={{0,4},{1,5},{4,8},{5,9},{8,12},{9,13},{12,14},{13,15},{14,10},{15,... | collective-permute-start | bytes 307208 | tf_op jit(solution)/shard_map/ppermute | solution.py:382
  26.1 3.6 %copy-start.2 = (s16[2,16,3200]{2,1,0:T(8,128)(2,1)S(1)}, s16[2,16,3200]{2,1,0:T(8,128)(2,1)}, u32[]{:S(2)}) copy-start(s16[2,16,3200]{2,1,0:T(8,128)(2,1)} %get-tuple-element.48.refs_2_.refs_5_.refs_7_) | copy-start | bytes 614404
  26.1 4.7 %copy-start = (bf16[128,8,1024]{2,1,0:T(8,128)(2,1)S(1)}, bf16[128,8,1024]{2,1,0:T(8,128)(2,1)}, u32[]{:S(2)}) copy-start(bf16[128,8,1024]{2,1,0:T(8,128)(2,1)} %param.10) | copy-start | bytes 6291460
  26.1 4.7 %collective-permute-start.11 = (s16[1,16,3200]{2,1,0:T(8,128)(2,1)S(1)}, s16[1,16,3200]{2,1,0:T(8,128)(2,1)S(1)}, u32[]{:S(2)}, u32[]{:S(2)}) collective-permute-start(s16[1,16,3200]{2,1,0:T(8,128)(2,1)S(1)} %slice.9), channel_id=1, source_target_pairs={{0,2},{1,3},{4,0},{5,1},{8,4},{9,5},{12,8},{13,9},{14,12},{15,13},... | collective-permute-start | bytes 307208 | tf_op jit(solution)/shard_map/ppermute | solution.py:382
  30.3 4.0 %collective-permute-start.10 = (f32[8,128]{1,0:T(8,128)S(1)}, f32[8,128]{1,0:T(8,128)S(1)}, u32[]{:S(2)}, u32[]{:S(2)}) collective-permute-start(f32[8,128]{1,0:T(8,128)S(1)} %shard_map.131.refs_0_.refs_4_), channel_id=1, source_target_pairs={{0,1},{1,0},{2,3},{3,2},{4,5},{5,4},{6,7},{7,6},{8,9},{9,8},{10,11... | collective-permute-start | bytes 12296 | tf_op jit(solution)/shard_map/ppermute | solution.py:404
  36.5 7.1 %collective-permute-start.12 = (bf16[256,2048]{1,0:T(8,128)(2,1)S(1)}, bf16[256,2048]{1,0:T(8,128)(2,1)S(1)}, u32[]{:S(2)}, u32[]{:S(2)}) collective-permute-start(bf16[256,2048]{1,0:T(8,128)(2,1)S(1)} %get-tuple-element.57), channel_id=1, source_target_pairs={{0,1},{1,0},{2,3},{3,2},{4,5},{5,4},{6,7},{7,6},{8,9},{9,8},{10,11... | collective-permute-start | bytes 3145736 | tf_op jit(solution)/shard_map/ppermute | solution.py:404
  40.6 7.5 %collective-permute-start.13 = (s16[2,16,3200]{2,1,0:T(8,128)(2,1)S(1)}, s16[2,16,3200]{2,1,0:T(8,128)(2,1)S(1)}, u32[]{:S(2)}, u32[]{:S(2)}) collective-permute-start(s16[2,16,3200]{2,1,0:T(8,128)(2,1)S(1)} %get-tuple-element.59), channel_id=1, source_target_pairs={{0,4},{1,5},{2,6},{3,7},{4,0},{5,1},{6,2},{7,3},{8,12},{9,13},{10,... | collective-permute-start | bytes 614408 | tf_op jit(solution)/shard_map/ppermute | solution.py:404
  42.2 8.2 %collective-permute-start.15 = (s16[2,16,3200]{2,1,0:T(8,128)(2,1)S(1)}, s16[2,16,3200]{2,1,0:T(8,128)(2,1)S(1)}, u32[]{:S(2)}, u32[]{:S(2)}) collective-permute-start(s16[2,16,3200]{2,1,0:T(8,128)(2,1)S(1)} %get-tuple-element.65), channel_id=1, source_target_pairs={{0,2},{1,3},{2,0},{3,1},{4,6},{5,7},{6,4},{7,5},{8,10},{9,11},{10,... | collective-permute-start | bytes 614408 | tf_op jit(solution)/shard_map/ppermute | solution.py:404
  46.8 6.5 %collective-permute-start.14 = (s16[2,16,3200]{2,1,0:T(8,128)(2,1)S(1)}, s16[2,16,3200]{2,1,0:T(8,128)(2,1)S(1)}, u32[]{:S(2)}, u32[]{:S(2)}) collective-permute-start(s16[2,16,3200]{2,1,0:T(8,128)(2,1)S(1)} %get-tuple-element.63), channel_id=1, source_target_pairs={{0,4},{1,5},{2,6},{3,7},{4,0},{5,1},{6,2},{7,3},{8,12},{9,13},{10,... | collective-permute-start | bytes 614408 | tf_op jit(solution)/shard_map/ppermute | solution.py:404
  48.3 6.4 %collective-permute-start.16 = (s16[16,3200]{1,0:T(8,128)(2,1)S(1)}, s16[16,3200]{1,0:T(8,128)(2,1)S(1)}, u32[]{:S(2)}, u32[]{:S(2)}) collective-permute-start(s16[16,3200]{1,0:T(8,128)(2,1)S(1)} %get-tuple-element.62.refs_0_), channel_id=1, source_target_pairs={{0,2},{1,3},{2,0},{3,1},{4,6},{5,7},{6,4},{7,5},{8,10},{9,11},{10,... | collective-permute-start | bytes 307208 | tf_op jit(solution)/shard_map/ppermute | solution.py:404
  49.3 9.1 %collective-permute-start.17 = (s16[2,16,3200]{2,1,0:T(8,128)(2,1)S(1)}, s16[2,16,3200]{2,1,0:T(8,128)(2,1)S(1)}, u32[]{:S(2)}, u32[]{:S(2)}) collective-permute-start(s16[2,16,3200]{2,1,0:T(8,128)(2,1)S(1)} %get-tuple-element.69), channel_id=1, source_target_pairs={{0,2},{1,3},{2,0},{3,1},{4,6},{5,7},{6,4},{7,5},{8,10},{9,11},{10,... | collective-permute-start | bytes 614408 | tf_op jit(solution)/shard_map/ppermute | solution.py:404
  53.5 6.7 %collective-permute-start.18 = (s16[16,3200]{1,0:T(8,128)(2,1)S(1)}, s16[16,3200]{1,0:T(8,128)(2,1)S(1)}, u32[]{:S(2)}, u32[]{:S(2)}) collective-permute-start(s16[16,3200]{1,0:T(8,128)(2,1)S(1)} %get-tuple-element.66.refs_0_), channel_id=1, source_target_pairs={{0,2},{1,3},{2,0},{3,1},{4,6},{5,7},{6,4},{7,5},{8,10},{9,11},{10,... | collective-permute-start | bytes 307208 | tf_op jit(solution)/shard_map/ppermute | solution.py:404
  54.9 8.1 %collective-permute-start.19 = (s16[16,3200]{1,0:T(8,128)(2,1)S(1)}, s16[16,3200]{1,0:T(8,128)(2,1)S(1)}, u32[]{:S(2)}, u32[]{:S(2)}) collective-permute-start(s16[16,3200]{1,0:T(8,128)(2,1)S(1)} %shard_map.138.refs_0_), channel_id=1, source_target_pairs={{0,8},{1,9},{2,10},{3,11},{4,12},{5,13},{6,14},{7,15},{8,0},{9,1},... | collective-permute-start | bytes 307208 | tf_op jit(solution)/shard_map/ppermute | solution.py:404
  58.6 8.5 %collective-permute-start.21 = (s16[2,16,3200]{2,1,0:T(8,128)(2,1)S(1)}, s16[2,16,3200]{2,1,0:T(8,128)(2,1)S(1)}, u32[]{:S(2)}, u32[]{:S(2)}) collective-permute-start(s16[2,16,3200]{2,1,0:T(8,128)(2,1)S(1)} %get-tuple-element.71.refs_0_), channel_id=1, source_target_pairs={{0,4},{1,5},{2,6},{3,7},{4,0},{5,1},{6,2},{7,3},{8,12},{9,13},{10,... | collective-permute-start | bytes 614408 | tf_op jit(solution)/shard_map/ppermute | solution.py:404
  60.4 6.6 %collective-permute-start.20 = (s16[16,3200]{1,0:T(8,128)(2,1)S(1)}, s16[16,3200]{1,0:T(8,128)(2,1)S(1)}, u32[]{:S(2)}, u32[]{:S(2)}) collective-permute-start(s16[16,3200]{1,0:T(8,128)(2,1)S(1)} %shard_map.140.refs_0_), channel_id=1, source_target_pairs={{0,8},{1,9},{2,10},{3,11},{4,12},{5,13},{6,14},{7,15},{8,0},{9,1},... | collective-permute-start | bytes 307208 | tf_op jit(solution)/shard_map/ppermute | solution.py:404
  (2 other events, 3.1 us)

commit v14 on v13

--- a/solution.py
+++ b/solution.py
@@ -53,7 +53,7 @@
     return value[..., :hidden_width] * down_scale, value[..., hidden_width:width] * up_scale
 
 
-def prepare_kernel(*refs):
+def prepare_kernel(experts, *refs):
     (piece_ref, small_ref), sem, refs = refs[7:9], refs[-1], refs[:7] + refs[9:-1]
     copies = [pltpu.make_async_copy(refs[i], refs[7 + i], sem.at[i]) for i in range(7)]
     for copy in copies:
@@ -68,7 +68,7 @@
     small_ref[2 * top : 2 * top + 1] = curvature
     lane = lax.broadcasted_iota(jnp.int32, (1, lanes), 1)
     counts = jnp.zeros((1, lanes), f32)
-    for number in range(lanes - counts_lane):
+    for number in range(experts):
         named = jnp.where(expert == number, 1.0, 0.0)
         total = jnp.sum(jnp.sum(named, axis=0, keepdims=True), axis=1, keepdims=True)
         counts = jnp.where(lane == counts_lane + number, total, counts)
@@ -82,39 +82,34 @@
     return experts, gates, small_ref[:, 2 * top : 2 * top + 1]
 
 
-def members(place_ref, wide, masks):
-    slot_of = lax.broadcasted_iota(jnp.int32, (1, wide), 1) // (wide // len(masks))
+def members(place_ref, wide, first=0, count=None):
+    piece_of = lax.broadcasted_iota(jnp.int32, (1, wide), 1) // (wide // count)
     found = jnp.zeros((1, wide), jnp.int32)
-    for slot, mask in enumerate(masks):
-        found = jnp.where(slot_of == slot, place_ref[0] ^ mask, found)
+    for number in range(count):
+        found = jnp.where(piece_of == number, place_ref[1 + first + number], found)
     return found.astype(f32)
 
 
-def prior_kernel(masks, place_ref, *rest):
+def prior_kernel(place_ref, *rest):
     piece_refs, prior_ref = rest[:-1], rest[-1]
     me = place_ref[0]
-    slots = len(masks)
     prior_ref[...] = jnp.zeros_like(prior_ref)
     for block, number in enumerate((me, me ^ 1)):
         total = jnp.zeros((1, lanes), f32)
-        for offset in range(slots):
-            piece_ref = piece_refs[offset]
-            device = place_ref[1 + slots + offset]
+        for arrival, piece_ref in enumerate(piece_refs):
             tail = piece_ref[0, :, piece_ref.shape[2] - lanes :]
             counts = tail.astype(jnp.int32).astype(f32)[0:1]
-            total = total + jnp.where(device < number, counts, 0.0)
+            total = total + jnp.where(place_ref[1 + arrival] < number, counts, 0.0)
         prior_ref[block : block + 1] = total
 
 
-def piece_part(refs, offset, kind):
-    last = len(refs) - 2
-    half = last // 2 + 1
-    if offset == half:
-        return refs[last + kind][0]
-    return refs[offset if offset < half else offset - 1][kind]
-
-
-def tokens_kernel(top, masks, place_ref, own_ref, other_ref, hidden_other_ref, gradient_other_ref, *outs):
+def piece_part(refs, arrival, kind, halved):
+    if halved and arrival == len(refs) - 2:
+        return refs[arrival + kind][0]
+    return refs[arrival][kind]
+
+
+def tokens_kernel(top, slots, place_ref, own_ref, other_ref, hidden_other_ref, gradient_other_ref, *outs):
     small_ref, rank_ref, gate_ref, same_ref, mask_ref, hidden_ref, gradient_ref, sem = outs
     copies = [
         pltpu.make_async_copy(hidden_other_ref, hidden_ref, sem.at[0]),
@@ -125,7 +120,7 @@
     small_ref[...] = jnp.concatenate([own_ref[...], other_ref[...]], axis=1).T
     experts, gates, _ = token_columns(small_ref, top)
     _, tokens, wide = rank_ref.shape
-    column = members(place_ref, wide, masks)
+    column = members(place_ref, wide, 0, slots)
     below = (
         lax.broadcasted_iota(jnp.int32, (tokens, tokens), 0)
         > lax.broadcasted_iota(jnp.int32, (tokens, tokens), 1)
@@ -154,67 +149,75 @@
         copy.wait()
 
 
-def reduce_kernel(top, masks, place_ref, small_ref, own_ref, other_ref, *rest):
-    slots = len(masks)
-    piece_refs, (reduced_ref, high_ref, low_ref, full_ref) = rest[: slots + 1], rest[slots + 1 :]
+def pass_kernel(behind_ref, ahead_ref, behind_out_ref, ahead_out_ref):
+    behind_out_ref[...] = behind_ref[...]
+    ahead_out_ref[...] = ahead_ref[...]
+
+
+def reduce_kernel(top, first, count, halved, place_ref, small_ref, own_ref, other_ref, *rest):
+    piece_refs, (reduced_ref, full_ref) = rest[:-2], rest[-2:]
     hidden_width = own_ref.shape[1]
-    for offset in range(slots):
-        slot = place_ref[1 + offset]
-        for kind in range(2):
-            down, _ = decode(piece_part(piece_refs, offset, kind), hidden_width)
-            high_ref[kind, slot], low_ref[kind, slot] = halves(down)
+    downs = [
+        decode(piece_part(piece_refs, arrival, kind, halved), hidden_width)[0]
+        for kind in range(2)
+        for arrival in range(count)
+    ]
+    factor = jnp.concatenate(halves(jnp.concatenate(downs, axis=0)), axis=0)
     experts, _, _ = token_columns(small_ref, top)
-    wide = reduced_ref.shape[2]
-    column = members(place_ref, wide, masks)
-    high = high_ref[...].reshape(2 * wide, hidden_width)
-    low = low_ref[...].reshape(2 * wide, hidden_width)
+    wide = reduced_ref.shape[1]
+    column = members(place_ref, wide // 2, first, count)
+    column = jnp.concatenate([column, column], axis=1)
     tokens = own_ref.shape[0] // top
     for core, hidden_ref in enumerate((own_ref, other_ref)):
-        full = dot(hidden_ref[...], high, 1, 1) + dot(hidden_ref[...], low, 1, 1)
-        full_ref[0], full_ref[1] = full[:, :wide], full[:, wide:]
+        full = dot(hidden_ref[...], factor, 1, 1)
+        full_ref[...] = full[:, :wide] + full[:, wide:]
         tokens_of = slice(core * tokens, (core + 1) * tokens)
-        for kind in range(2):
-            total = jnp.zeros((tokens, wide), f32)
-            for k in range(top):
-                here = full_ref[kind, pl.ds(k, tokens, stride=top), :]
-                total = jnp.where(experts[k][tokens_of] == column, here, total)
-            reduced_ref[kind, tokens_of] = total
-
-
-def rank_limits(place_ref, masks, wide, capacity_ref, prior_ref, arrived_ref):
+        total = jnp.zeros((tokens, wide), f32)
+        for k in range(top):
+            here = full_ref[pl.ds(k, tokens, stride=top), :]
+            total = jnp.where(experts[k][tokens_of] == column, here, total)
+        reduced_ref[tokens_of] = total
+
+
+def rank_limits(place_ref, wide, slots, capacity_ref, prior_ref, arrived_ref):
     lane = lax.broadcasted_iota(jnp.int32, (1, lanes), 1)
-    slot_of = lax.broadcasted_iota(jnp.int32, (1, wide), 1) // (wide // len(masks))
+    piece_of = lax.broadcasted_iota(jnp.int32, (1, wide), 1) // (wide // slots)
     limits = []
     for block in range(2):
         total = capacity_ref[...] - prior_ref[block : block + 1] - arrived_ref[1 - block : 2 - block]
         limit = jnp.zeros((1, wide), f32)
-        for slot, mask in enumerate(masks):
-            picked = jnp.where(lane == counts_lane + (place_ref[0] ^ mask), total, 0.0)
-            limit = jnp.where(slot_of == slot, jnp.sum(picked, axis=1, keepdims=True), limit)
+        for arrival in range(slots):
+            picked = jnp.where(lane == counts_lane + place_ref[1 + arrival], total, 0.0)
+            limit = jnp.where(piece_of == arrival, jnp.sum(picked, axis=1, keepdims=True), limit)
         limits.append(limit)
     return limits
 
 
-def tangent_kernel(masks, place_ref, rank_ref, gate_ref, capacity_ref, prior_ref, arrived_ref, reduced_ref, *rest):
-    slots = len(masks)
+def tangent_kernel(
+    slots, place_ref, rank_ref, gate_ref, capacity_ref, prior_ref, arrived_ref, early_ref, late_ref, *rest
+):
     piece_refs = rest[: slots + 1]
     weight_ref, weighted_ref, tangent_ref, coded_ref, high_ref, low_ref = rest[slots + 1 :]
     _, wide = weight_ref.shape
     model_width = tangent_ref.shape[1]
     hidden_width = piece_refs[0].shape[2] - model_width - lanes
-    limits = rank_limits(place_ref, masks, wide, capacity_ref, prior_ref, arrived_ref)
+    limits = rank_limits(place_ref, wide, slots, capacity_ref, prior_ref, arrived_ref)
     weights = [
         jnp.where(rank_ref[core] < limits[core], adapter_scale * gate_ref[core], 0.0) for core in range(2)
     ]
     weight = jnp.concatenate(weights, axis=0)
     weight_ref[...] = weight
-    weighted = jnp.concatenate([weight * reduced_ref[0], weight * reduced_ref[1]], axis=1)
+    half = wide // 2
+    reduced = [
+        jnp.concatenate([ref[:, kind * half : (kind + 1) * half] for ref in (early_ref, late_ref)], axis=1)
+        for kind in range(2)
+    ]
+    weighted = jnp.concatenate([weight * part for part in reduced], axis=1)
     weighted_ref[...] = weighted
-    for offset in range(slots):
-        slot = place_ref[1 + offset]
+    for arrival in range(slots):
         for kind in range(2):
-            _, up = decode(piece_part(piece_refs, offset, kind), hidden_width)
-            high_ref[kind, slot], low_ref[kind, slot] = halves(up)
+            _, up = decode(piece_part(piece_refs, arrival, kind, True), hidden_width)
+            high_ref[kind, arrival], low_ref[kind, arrival] = halves(up)
     factor = high_ref[...].reshape(2 * wide, model_width), low_ref[...].reshape(2 * wide, model_width)
     tangent = dot_pairs(halves(weighted), factor, 1, 0)
     tangent_ref[...] = tangent
@@ -235,22 +238,25 @@
     return both[:middle] + both[middle:]
 
 
-def put_chunks(keep_ref, near_ref, chunk_ref, far_ref, down, up):
+def put_chunks(place_ref, down_ref, up_ref, keep_ref, near_ref, chunk_ref, far_ref, down, up):
     rank = keep_ref.shape[1]
-    rows = down.shape[0] // rank // 2
+    slots = down.shape[0] // rank
+    down_ref[...] = down
+    up_ref[...] = up
 
     def slot(number):
-        start = number * rank
-        return down[start : start + rank], up[start : start + rank]
+        start = pl.multiple_of(place_ref[1 + slots + number] * rank, rank)
+        return down_ref[pl.ds(start, rank), :], up_ref[pl.ds(start, rank), :]
 
     for place in range(2):
         keep_ref[place] = jnp.concatenate(slot(place), axis=1)
-        near_ref[place] = encode(*slot(rows + place))
-        chunk_ref[place] = jnp.concatenate(slot(place * rows + 2), axis=1)
-        far_ref[place] = encode(*slot(place * rows + 3))
+        near_ref[place] = encode(*slot(slots // 2 + place))
+        chunk_ref[place] = jnp.concatenate(slot(place * slots // 2 + 2), axis=1)
+        far_ref[place] = encode(*slot(place * slots // 2 + 3))
 
 
 def gradient_kernel(
+    place_ref,
     same_ref,
     mask_ref,
     own_ref,
@@ -268,6 +274,8 @@
     up_ref,
     to_ref,
     left_ref,
+    down_sum_ref,
+    up_sum_ref,
 ):
     wide = weight_ref.shape[1]
     model_width = up_ref.shape[1]
@@ -280,11 +288,13 @@
     down = dot(left_ref[0], own_ref[...], 0, 0) + dot(left_ref[1], other_ref[...], 0, 0)
     up = add_halves(dot(jnp.concatenate(halves(weighted_ref[...]), axis=1), gradient, 0, 0))
     up_ref[...] = up[:wide]
-    put_chunks(keep_ref, near_ref, chunk_ref, far_ref, add_halves(down), up[wide:])
+    out_refs = keep_ref, near_ref, chunk_ref, far_ref
+    put_chunks(place_ref, down_sum_ref, up_sum_ref, *out_refs, add_halves(down), up[wide:])
 
 
 def curvature_kernel(
     top,
+    place_ref,
     small_ref,
     same_ref,
     mask_ref,
@@ -303,6 +313,8 @@
     chunk_ref,
     far_ref,
     left_ref,
+    down_sum_ref,
+    up_sum_ref,
 ):
     _, _, curvature = token_columns(small_ref, top)
     tokens, wide = weight_ref.shape
@@ -316,7 +328,8 @@
     down = dot(left_ref[0], own_ref[...], 0, 0) + dot(left_ref[1], other_ref[...], 0, 0)
     weighted_u = halves(weighted_ref[:, wide:])
     up = add_halves(dot(jnp.concatenate(weighted_u, axis=1), resid[0], 0, 0)) + dot(weighted_u[0], resid[1], 0, 0)
-    put_chunks(keep_ref, near_ref, chunk_ref, far_ref, add_halves(down), up_ref[...] + up)
+    out_refs = keep_ref, near_ref, chunk_ref, far_ref
+    put_chunks(place_ref, down_sum_ref, up_sum_ref, *out_refs, add_halves(down), up_ref[...] + up)
 
 
 def pair_kernel(hidden_width, arrived_ref, chunk_ref, near_ref, across_ref, keep_ref, onward_ref):
@@ -384,19 +397,23 @@
     def members(self, me):
         rows = self.length // 2
         place = jnp.where(me // 2 % 2 == 0, me // 4, self.length - 1 - me // 4)
-        there = (place + jnp.arange(self.length, dtype=jnp.int32)) % self.length
+        half = self.length // 2
+        offsets = [0] + [offset for step in range(1, half) for offset in (self.length - step, step)] + [half]
+        there = (place + jnp.array(offsets, jnp.int32)) % self.length
         return jnp.where(there < rows, 4 * there, 4 * (self.length - 1 - there) + 2) + me % 2
 
-    def gather(self, own):
+    def gather(self, own, passing):
         half = self.length // 2
-        found = {0: own}
+        pieces = [own]
         ahead, behind = own, own
         for step in range(1, half):
             behind = self.shift(behind, 1)
             ahead = self.shift(ahead, -1)
-            found[self.length - step], found[step] = behind, ahead
-        last = [self.shift(behind[:1], 1), self.shift(ahead[1:], -1)]
-        return [found[offset] for offset in sorted(found)] + last
+            if step == 2:
+                behind, ahead = passing(behind, ahead)
+            pieces += [behind, ahead]
+        pieces += [self.shift(behind[:1], 1), self.shift(ahead[1:], -1)]
+        return pieces
 
 
 def exchange(value, mask):
@@ -430,15 +447,13 @@
     wide = slots * rank
     coded_width = hidden_width + model_width + lanes
 
-    ring_members = ring.members(me)
-    differs = ring_members ^ me
-    slot_of_offset = differs // 4 + rows * (differs // 2 % 2)
-    place = jnp.concatenate([me[None], slot_of_offset, ring_members]).astype(jnp.int32)
+
+    place = []
 
     def call(kernel, multiplies, outs, *operands, scratch=(), after=(), grant=kernel_vmem):
-        space = pltpu.HBM if kernel is prepare_kernel else pltpu.VMEM
+        space = pltpu.VMEM if grant == kernel_vmem else pltpu.HBM
         places = [pl.BlockSpec(memory_space=pl.ANY) for _ in after] + [
-            pl.BlockSpec(memory_space=pltpu.SMEM if operand is place else space) for operand in operands
+            pl.BlockSpec(memory_space=pltpu.SMEM if any(operand is it for it in place) else space) for operand in operands
         ]
         return pl.pallas_call(
             lambda *refs: kernel(*refs[len(after) :]),
@@ -462,7 +477,7 @@
         up_direction[0],
     )
     piece, small = call(
-        prepare_kernel,
+        functools.partial(prepare_kernel, experts),
         10**8,
         [((2, rank, coded_width), i16), (((2 * top + 8) // 8 * 8, tokens), f32)],
         *first,
@@ -470,10 +485,15 @@
         + [pltpu.SemaphoreType.DMA((len(first),))],
         grant=whole_vmem,
     )
+    arrivals = ring.members(me)
+    number = jnp.arange(slots, dtype=jnp.int32)
+    slot_of_arrival = (arrivals ^ me) // 4 + rows * ((arrivals ^ me) // 2 % 2)
+    arrival_of_slot = jnp.sum(jnp.where(slot_of_arrival == number[:, None], number, 0), axis=1)
+    place.append(jnp.concatenate([me[None], arrivals, arrival_of_slot]).astype(jnp.int32))
     small_other = exchange(small, 1)
     hidden = hidden_of_route.reshape(tokens * top, hidden_width)
     small_columns, local_rank, gate, same, mask, hidden_other, gradient_other = call(
-        functools.partial(tokens_kernel, top, masks),
+        functools.partial(tokens_kernel, top, slots),
         10**9,
         [
             ((both, small.shape[0]), f32),
@@ -484,36 +504,40 @@
             (hidden.shape, bf16),
             (output_gradient.shape, bf16),
         ],
-        place,
+        *place,
         small,
         small_other,
         exchange(hidden, 1),
         exchange(output_gradient, 1),
         scratch=[pltpu.SemaphoreType.DMA((2,))],
     )
-    pieces = ring.gather(piece)
+    def passing(behind, ahead):
+        return call(pass_kernel, 10**8, [(piece.shape, i16)] * 2, behind, ahead, after=[same])
+
+    pieces = ring.gather(piece, passing)
     capacity_row = jnp.pad(capacity.astype(f32), (counts_lane, lanes - counts_lane - experts))[None, :]
 
-    by_offset = pieces[:rows] + [pieces[-2]] + pieces[rows:-2]
-    (prior,) = call(
-        functools.partial(prior_kernel, masks), 10**8, [((8, lanes), f32)], place, *by_offset, after=[same]
-    )
+    def reduced(first, count, halved, *parts, after=()):
+        return call(
+            functools.partial(reduce_kernel, top, first, count, halved),
+            2 * down_multiplies * count // slots,
+            [((both, 2 * count * rank), f32)],
+            *place,
+            small_columns,
+            hidden,
+            hidden_other,
+            *parts,
+            scratch=[pltpu.VMEM((tokens * top, 2 * count * rank), f32)],
+            after=after,
+        )[0]
+
+    early = slots // 2
+    reduced_early = reduced(0, early, False, *pieces[:early])
+    (prior,) = call(prior_kernel, 10**8, [((8, lanes), f32)], *place, *pieces[:-1], after=[reduced_early])
     prior_arrived = exchange(prior, 1)
-    factor_halves = [pltpu.VMEM((2, slots, rank, hidden_width), bf16)] * 2
-    (reduced,) = call(
-        functools.partial(reduce_kernel, top, masks),
-        2 * down_multiplies,
-        [((2, both, wide), f32)],
-        place,
-        small_columns,
-        hidden,
-        hidden_other,
-        *pieces,
-        scratch=factor_halves + [pltpu.VMEM((2, tokens * top, wide), f32)],
-        after=[prior],
-    )
+    reduced_late = reduced(early, slots - early, True, *pieces[early:], after=[prior])
     weight, weighted, tangent, coded, high, low = call(
-        functools.partial(tangent_kernel, masks),
+        functools.partial(tangent_kernel, slots),
         6 * up_multiplies,
         [
             ((both, wide), f32),
@@ -523,22 +547,28 @@
             ((2, slots, rank, model_width), bf16),
             ((2, slots, rank, model_width), bf16),
         ],
-        place,
+        *place,
         local_rank,
         gate,
         capacity_row,
         prior,
         prior_arrived,
-        reduced,
+        reduced_early,
+        reduced_late,
         *pieces,
     )
     arrived = exchange(coded, 1)
-    left = [pltpu.VMEM((2, top * tokens, 2 * wide), bf16)]
+    left = [
+        pltpu.VMEM((2, top * tokens, 2 * wide), bf16),
+        pltpu.VMEM((wide, hidden_width), f32),
+        pltpu.VMEM((wide, model_width), f32),
+    ]
     chunks = [((2, rank, hidden_width + model_width), f32), ((2, rank, coded_width), i16)] * 2
     gradient_keep, gradient_near, gradient_chunk, gradient_far, up, to = call(
         gradient_kernel,
         down_multiplies + 8 * up_multiplies,
         chunks + [((wide, model_width), f32), ((both, wide), f32)],
+        *place,
         same,
         mask,
         hidden,
@@ -557,6 +587,7 @@
         functools.partial(curvature_kernel, top),
         down_multiplies + 6 * up_multiplies,
         chunks,
+        *place,
         small_columns,
         same,
         mask,

time: 68.2 us -> 68.2 us (level)
  waiting for transfers between devices: 22.6 us -> 19.9 us
  Pallas kernels: 19.6 us -> 21.2 us
  starting transfers between devices: 23.3 us -> 24.3 us
    ppermute x8, waiting for transfers between devices: 14.1 us -> 11.7 us  [shift(): return lax.ppermute(value, 'expert', pairs)]
    pallas_call x14 -> x16, Pallas kernels: 19.6 us -> 21.2 us  [call(): pl.pallas_call(lambda *refs: kernel(*refs[len(after):]), out_shape=[jax.S...]
    ppermute x8, starting transfers between devices: 8.83 us -> 9.53 us  [shift(): return lax.ppermute(value, 'expert', pairs)]
  transfers between devices with their start and end apart: 22 -> 22, of which waited for: 8 -> 8; matrix products, arithmetic and copies ran while one was open for 1% -> 1% of each run, Pallas kernels for 24% -> 27%
where the time goes in v14:
time: 68.2 us; the launch traced here: 67.9 us
  starting transfers between devices  24.3 us (36%)
  Pallas kernels  21.2 us (31%)
  waiting for transfers between devices  19.9 us (29%)
  other arithmetic  0.88 us (1%)
  local copies, waits for them, and re-layouts  0.85 us (1%)
  between operations  0.82 us (1%)
    pallas_call x16, Pallas kernels, call(): pl.pallas_call(lambda *refs: kernel(*refs[len(after):]), out_shape=[jax.S...  21.2 us
    ppermute x14, starting transfers between devices, exchange(): lax.ppermute(value, 'expert', [(device, device ^ mask) for device in rang...  14.7 us
    ppermute x8, waiting for transfers between devices, shift(): return lax.ppermute(value, 'expert', pairs)  11.7 us
    ppermute x8, starting transfers between devices, shift(): return lax.ppermute(value, 'expert', pairs)  9.53 us
    ppermute x14, waiting for transfers between devices, exchange(): lax.ppermute(value, 'expert', [(device, device ^ mask) for device in rang...  8.24 us
  transfers between devices with their start and end apart: 22, of which 8 were waited for; matrix products, arithmetic and copies ran while one was open for 1% of the time, Pallas kernels for 27%

profile of v14, /device:TPU:0, one launch (start us, length us, event | category | flops | bytes accessed | tf_op | source)
XLA Modules:
  0.0 67.9 jit_solution(17866746971369208660)
XLA Ops:
  1.2 2.0 %shard_map.138 = (s16[2,16,3200]{2,1,0:T(8,128)(2,1)}, f32[24,128]{1,0:T(8,128)}) custom-call(s32[8,128]{1,0:T(8,128)} %bitcast.32, bf16[8,128]{1,0:T(8,128)(2,1)} %bitcast.33, f32[1,128]{1,0:T(1,128)} %bitcast.34, f32[16,1024]{1,0:T(8,128)} %bitcast.30, f32[16,1024]{1,0:T(8,128)} %bitcast.31, f32[16,2048]{1,0:T(8,128)} %bitcast.28, f32[16,2048]{1,0:T(8,128)} %bitcast.29), custom_call_target="tpu_custom_call" | custom-call | flops 200000000 | bytes 1048576 | tf_op jit(solution)/shard_map/pallas_call | solution.py:458
  3.2 3.0 %collective-permute-start.4 = (s16[2,16,3200]{2,1,0:T(8,128)(2,1)}, s16[2,16,3200]{2,1,0:T(8,128)(2,1)S(1)}, u32[]{:S(2)}, u32[]{:S(2)}) collective-permute-start(s16[2,16,3200]{2,1,0:T(8,128)(2,1)} %get-tuple-element.50.refs_4_.refs_2_.refs_8_), channel_id=1, source_target_pairs={{0,2},{1,3},{4,0},{5,1},{8,4},{9,5},{12,8},{13,9},{14,12},{15,13},... | collective-permute-start | bytes 614408 | tf_op jit(solution)/shard_map/ppermute | solution.py:395
  7.1 4.7 %collective-permute-done.4.refs_6_.refs_4_.refs_10_ = s16[2,16,3200]{2,1,0:T(8,128)(2,1)S(1)} collective-permute-done((s16[2,16,3200]{2,1,0:T(8,128)(2,1)}, s16[2,16,3200]{2,1,0:T(8,128)(2,1)S(1)}, u32[]{:S(2)}, u32[]{:S(2)}) %collective-permute-start.4) | collective-permute-done | bytes 204832 | tf_op jit(solution)/shard_map/ppermute | solution.py:395
  11.8 1.7 %collective-permute-start.6 = (s16[2,16,3200]{2,1,0:T(8,128)(2,1)S(1)}, s16[2,16,3200]{2,1,0:T(8,128)(2,1)S(1)}, u32[]{:S(2)}, u32[]{:S(2)}) collective-permute-start(s16[2,16,3200]{2,1,0:T(8,128)(2,1)S(1)} %collective-permute-done.4.refs_6_.refs_4_.refs_10_), channel_id=1, source_target_pairs={{0,2},{1,3},{4,0},{5,1},{8,4},{9,5},{12,8},{13,9},{14,12},{15,13},... | collective-permute-start | bytes 614408 | tf_op jit(solution)/shard_map/ppermute | solution.py:395
  14.7 2.2 %shard_map.139 = (f32[256,24]{1,0:T(8,128)S(1)}, f32[2,128,128]{2,1,0:T(8,128)S(1)}, f32[2,128,128]{2,1,0:T(8,128)S(1)}, bf16[1024,128]{1,0:T(8,128)(2,1)S(1)}, ...) custom-call(s32[17]{0:T(128)S(1)} %pad_add_fusion.refs_0_.refs_1_, ...), custom_call_target="tpu_custom_call" | custom-call | flops 2000000000 | bytes 1048576 | tf_op jit(solution)/shard_map/pallas_call | solution.py:458
  16.8 1.5 %collective-permute-done.6.refs_2_ = s16[2,16,3200]{2,1,0:T(8,128)(2,1)S(1)} collective-permute-done((s16[2,16,3200]{2,1,0:T(8,128)(2,1)S(1)}, s16[2,16,3200]{2,1,0:T(8,128)(2,1)S(1)}, u32[]{:S(2)}, u32[]{:S(2)}) %collective-permute-start.6) | collective-permute-done | bytes 204832 | tf_op jit(solution)/shard_map/ppermute | solution.py:395
  18.3 1.1 %collective-permute-done.5.refs_1_ = s16[2,16,3200]{2,1,0:T(8,128)(2,1)S(1)} collective-permute-done((s16[2,16,3200]{2,1,0:T(8,128)(2,1)S(1)}, s16[2,16,3200]{2,1,0:T(8,128)(2,1)S(1)}, u32[]{:S(2)}, u32[]{:S(2)}) %collective-permute-start.5) | collective-permute-done | bytes 204832 | tf_op jit(solution)/shard_map/ppermute | solution.py:395
  20.2 1.3 %collective-permute-start.8 = (s16[2,16,3200]{2,1,0:T(8,128)(2,1)S(1)}, s16[2,16,3200]{2,1,0:T(8,128)(2,1)S(1)}, u32[]{:S(2)}, u32[]{:S(2)}) collective-permute-start(s16[2,16,3200]{2,1,0:T(8,128)(2,1)S(1)} %get-tuple-element.52.refs_6_.refs_5_.refs_12_), channel_id=1, source_target_pairs={{0,2},{1,3},{4,0},{5,1},{8,4},{9,5},{12,8},{13,9},{14,12},{15,13},... | collective-permute-start | bytes 614408 | tf_op jit(solution)/shard_map/ppermute | solution.py:395
  21.5 4.1 %collective-permute-done.7.refs_7_.refs_6_.refs_13_ = s16[2,16,3200]{2,1,0:T(8,128)(2,1)S(1)} collective-permute-done((s16[2,16,3200]{2,1,0:T(8,128)(2,1)S(1)}, s16[2,16,3200]{2,1,0:T(8,128)(2,1)S(1)}, u32[]{:S(2)}, u32[]{:S(2)}) %collective-permute-start.7) | collective-permute-done | bytes 204832 | tf_op jit(solution)/shard_map/ppermute | solution.py:395
  26.1 1.9 %collective-permute-start.11 = (s16[1,16,3200]{2,1,0:T(8,128)(2,1)S(1)}, s16[1,16,3200]{2,1,0:T(8,128)(2,1)S(1)}, u32[]{:S(2)}, u32[]{:S(2)}) collective-permute-start(s16[1,16,3200]{2,1,0:T(8,128)(2,1)S(1)} %slice.9), channel_id=1, source_target_pairs={{0,2},{1,3},{4,0},{5,1},{8,4},{9,5},{12,8},{13,9},{14,12},{15,13},... | collective-permute-start | bytes 307208 | tf_op jit(solution)/shard_map/ppermute | solution.py:395
  28.0 2.0 %shard_map.141.refs_0_.refs_6_ = f32[256,128]{1,0:T(8,128)S(1)} custom-call(s32[17]{0:T(128)S(1)} %pad_add_fusion.refs_0_.refs_1_, f32[256,24]{1,0:T(8,128)S(1)} %get-tuple-element.44.refs_1_.refs_2_, bf16[1024,1024]{1,0:T(8,128)(2,1)S(1)} %bitcast.24, bf16[1024,1024]{1,0:T(8,128)(2,1)S(1)} %get-tuple-element.47.refs_3_.refs_4_.refs_5_, ...), custom_call_target="tpu_custom_call" | custom-call | flops 1073741824 | bytes 1048576 | tf_op jit(solution)/shard_map/pallas_call | solution.py:458
  31.0 2.0 %shard_map.143.refs_7_ = f32[256,128]{1,0:T(8,128)S(1)} custom-call(f32[8,128]{1,0:T(8,128)S(1)} %shard_map.142.refs_0_.refs_4_, s32[17]{0:T(128)S(1)} %pad_add_fusion.refs_0_.refs_1_, f32[256,24]{1,0:T(8,128)S(1)} %get-tuple-element.44.refs_1_.refs_2_, bf16[1024,1024]{1,0:T(8,128)(2,1)S(1)} %bitcast.25, ...), custom_call_target="tpu_custom_call" | custom-call | flops 1073741824 | bytes 1048576 | tf_op jit(solution)/shard_map/pallas_call | solution.py:458
  33.1 2.0 %shard_map.144 = (f32[256,128]{1,0:T(8,128)S(1)}, f32[256,256]{1,0:T(8,128)S(1)}, f32[256,2048]{1,0:T(8,128)S(1)}, bf16[256,2048]{1,0:T(8,128)(2,1)S(1)}, bf16[2...) custom-call(s32[17]{0:T(128)S(1)} %pad_add_fusion.refs_0_.refs_1_, ...), custom_call_target="tpu_custom_call" | custom-call | flops 805306368 | bytes 1048576 | tf_op jit(solution)/shard_map/pallas_call | solution.py:458
  35.6 4.6 %shard_map.145 = (f32[2,16,3072]{2,1,0:T(8,128)S(1)}, s16[2,16,3200]{2,1,0:T(8,128)(2,1)S(1)}, f32[2,16,3072]{2,1,0:T(8,128)S(1)}, s16[2,16,3200]{2,1,0:T(8,128)...) custom-call(s32[17]{0:T(128)S(1)} %pad_add_fusion.refs_0_.refs_1_, ...), custom_call_target="tpu_custom_call" | custom-call | flops 2147483648 | bytes 1048576 | tf_op jit(solution)/shard_map/pallas_call | solution.py:458
  40.2 1.3 %collective-permute-start.13 = (s16[2,16,3200]{2,1,0:T(8,128)(2,1)S(1)}, s16[2,16,3200]{2,1,0:T(8,128)(2,1)S(1)}, u32[]{:S(2)}, u32[]{:S(2)}) collective-permute-start(s16[2,16,3200]{2,1,0:T(8,128)(2,1)S(1)} %get-tuple-element.63), channel_id=1, source_target_pairs={{0,4},{1,5},{2,6},{3,7},{4,0},{5,1},{6,2},{7,3},{8,12},{9,13},{10,... | collective-permute-start | bytes 614408 | tf_op jit(solution)/shard_map/ppermute | solution.py:421
  41.5 2.0 %collective-permute-start.15 = (s16[2,16,3200]{2,1,0:T(8,128)(2,1)S(1)}, s16[2,16,3200]{2,1,0:T(8,128)(2,1)S(1)}, u32[]{:S(2)}, u32[]{:S(2)}) collective-permute-start(s16[2,16,3200]{2,1,0:T(8,128)(2,1)S(1)} %get-tuple-element.69), channel_id=1, source_target_pairs={{0,2},{1,3},{2,0},{3,1},{4,6},{5,7},{6,4},{7,5},{8,10},{9,11},{10,... | collective-permute-start | bytes 614408 | tf_op jit(solution)/shard_map/ppermute | solution.py:421
  43.4 3.9 %shard_map.146 = (f32[2,16,3072]{2,1,0:T(8,128)S(1)}, s16[2,16,3200]{2,1,0:T(8,128)(2,1)S(1)}, f32[2,16,3072]{2,1,0:T(8,128)S(1)}, s16[2,16,3200]{2,1,0:T(8,128)(2,1)S(1)}) custom-call(s32[17]{0:T(128)S(1)} %pad_add_fusion.refs_0_.refs_1_, f32[256,24]{1,0:T(8,128)S(1)} %get-tuple-element.44.refs_1_.refs_2_, ...), custom_call_target="tpu_custom_call" | custom-call | flops 1879048192 | bytes 1048576 | tf_op jit(solution)/shard_map/pallas_call | solution.py:458
  48.0 1.2 %collective-permute-start.16 = (s16[16,3200]{1,0:T(8,128)(2,1)S(1)}, s16[16,3200]{1,0:T(8,128)(2,1)S(1)}, u32[]{:S(2)}, u32[]{:S(2)}) collective-permute-start(s16[16,3200]{1,0:T(8,128)(2,1)S(1)} %get-tuple-element.66.refs_0_), channel_id=1, source_target_pairs={{0,2},{1,3},{2,0},{3,1},{4,6},{5,7},{6,4},{7,5},{8,10},{9,11},{10,... | collective-permute-start | bytes 307208 | tf_op jit(solution)/shard_map/ppermute | solution.py:421
  49.2 0.9 %collective-permute-start.17 = (s16[2,16,3200]{2,1,0:T(8,128)(2,1)S(1)}, s16[2,16,3200]{2,1,0:T(8,128)(2,1)S(1)}, u32[]{:S(2)}, u32[]{:S(2)}) collective-permute-start(s16[2,16,3200]{2,1,0:T(8,128)(2,1)S(1)} %get-tuple-element.73), channel_id=1, source_target_pairs={{0,2},{1,3},{2,0},{3,1},{4,6},{5,7},{6,4},{7,5},{8,10},{9,11},{10,... | collective-permute-start | bytes 614408 | tf_op jit(solution)/shard_map/ppermute | solution.py:421
  50.1 3.8 %collective-permute-done.14.refs_1_ = s16[2,16,3200]{2,1,0:T(8,128)(2,1)S(1)} collective-permute-done((s16[2,16,3200]{2,1,0:T(8,128)(2,1)S(1)}, s16[2,16,3200]{2,1,0:T(8,128)(2,1)S(1)}, u32[]{:S(2)}, u32[]{:S(2)}) %collective-permute-start.14) | collective-permute-done | bytes 204832 | tf_op jit(solution)/shard_map/ppermute | solution.py:421
  54.8 2.8 %collective-permute-start.19 = (s16[16,3200]{1,0:T(8,128)(2,1)S(1)}, s16[16,3200]{1,0:T(8,128)(2,1)S(1)}, u32[]{:S(2)}, u32[]{:S(2)}) collective-permute-start(s16[16,3200]{1,0:T(8,128)(2,1)S(1)} %shard_map.149.refs_0_), channel_id=1, source_target_pairs={{0,8},{1,9},{2,10},{3,11},{4,12},{5,13},{6,14},{7,15},{8,0},{9,1},... | collective-permute-start | bytes 307208 | tf_op jit(solution)/shard_map/ppermute | solution.py:421
  57.9 1.7 %collective-permute-start.21 = (s16[2,16,3200]{2,1,0:T(8,128)(2,1)S(1)}, s16[2,16,3200]{2,1,0:T(8,128)(2,1)S(1)}, u32[]{:S(2)}, u32[]{:S(2)}) collective-permute-start(s16[2,16,3200]{2,1,0:T(8,128)(2,1)S(1)} %get-tuple-element.75.refs_0_), channel_id=1, source_target_pairs={{0,4},{1,5},{2,6},{3,7},{4,0},{5,1},{6,2},{7,3},{8,12},{9,13},{10,... | collective-permute-start | bytes 614408 | tf_op jit(solution)/shard_map/ppermute | solution.py:421
  59.8 2.8 %collective-permute-start.20 = (s16[16,3200]{1,0:T(8,128)(2,1)S(1)}, s16[16,3200]{1,0:T(8,128)(2,1)S(1)}, u32[]{:S(2)}, u32[]{:S(2)}) collective-permute-start(s16[16,3200]{1,0:T(8,128)(2,1)S(1)} %shard_map.151.refs_0_), channel_id=1, source_target_pairs={{0,8},{1,9},{2,10},{3,11},{4,12},{5,13},{6,14},{7,15},{8,0},{9,1},... | collective-permute-start | bytes 307208 | tf_op jit(solution)/shard_map/ppermute | solution.py:421
  62.7 4.4 %collective-permute-done.21.refs_3_ = s16[2,16,3200]{2,1,0:T(8,128)(2,1)S(1)} collective-permute-done((s16[2,16,3200]{2,1,0:T(8,128)(2,1)S(1)}, s16[2,16,3200]{2,1,0:T(8,128)(2,1)S(1)}, u32[]{:S(2)}, u32[]{:S(2)}) %collective-permute-start.21) | collective-permute-done | bytes 204832 | tf_op jit(solution)/shard_map/ppermute | solution.py:421
  (53 shorter events, 8.7 us)
Async XLA Ops:
  0.6 13.3 %collective-permute-start.1 = (bf16[1024,1024]{1,0:T(8,128)(2,1)}, bf16[1024,1024]{1,0:T(8,128)(2,1)S(1)}, u32[]{:S(2)}, u32[]{:S(2)}) collective-permute-start(bf16[1024,1024]{1,0:T(8,128)(2,1)} %bitcast.23), channel_id=1, source_target_pairs={{0,1},{1,0},{2,3},{3,2},{4,5},{5,4},{6,7},{7,6},{8,9},{9,8},{10,11... | collective-permute-start | bytes 6291464 | tf_op jit(solution)/shard_map/ppermute | solution.py:421
  1.2 12.8 %collective-permute-start.2 = (bf16[128,2048]{1,0:T(8,128)(2,1)}, bf16[128,2048]{1,0:T(8,128)(2,1)S(1)}, u32[]{:S(2)}, u32[]{:S(2)}) collective-permute-start(bf16[128,2048]{1,0:T(8,128)(2,1)} %refs_5_.1), channel_id=1, source_target_pairs={{0,1},{1,0},{2,3},{3,2},{4,5},{5,4},{6,7},{7,6},{8,9},{9,8},{10,11... | collective-permute-start | bytes 1572872 | tf_op jit(solution)/shard_map/ppermute | solution.py:421
  3.2 8.6 %collective-permute-start.4 = (s16[2,16,3200]{2,1,0:T(8,128)(2,1)}, s16[2,16,3200]{2,1,0:T(8,128)(2,1)S(1)}, u32[]{:S(2)}, u32[]{:S(2)}) collective-permute-start(s16[2,16,3200]{2,1,0:T(8,128)(2,1)} %get-tuple-element.50.refs_4_.refs_2_.refs_8_), channel_id=1, source_target_pairs={{0,2},{1,3},{4,0},{5,1},{8,4},{9,5},{12,8},{13,9},{14,12},{15,13},... | collective-permute-start | bytes 614408 | tf_op jit(solution)/shard_map/ppermute | solution.py:395
  6.2 7.3 %collective-permute-start.3 = (s16[2,16,3200]{2,1,0:T(8,128)(2,1)}, s16[2,16,3200]{2,1,0:T(8,128)(2,1)S(1)}, u32[]{:S(2)}, u32[]{:S(2)}) collective-permute-start(s16[2,16,3200]{2,1,0:T(8,128)(2,1)} %get-tuple-element.50.refs_4_.refs_2_.refs_8_), channel_id=1, source_target_pairs={{0,4},{1,5},{4,8},{5,9},{8,12},{9,13},{12,14},{13,15},{14,10},{15,... | collective-permute-start | bytes 614408 | tf_op jit(solution)/shard_map/ppermute | solution.py:395
  6.3 7.6 %collective-permute-start = (f32[24,128]{1,0:T(8,128)}, f32[24,128]{1,0:T(8,128)S(1)}, u32[]{:S(2)}, u32[]{:S(2)}) collective-permute-start(f32[24,128]{1,0:T(8,128)} %get-tuple-element.43.refs_1_), channel_id=1, source_target_pairs={{0,1},{1,0},{2,3},{3,2},{4,5},{5,4},{6,7},{7,6},{8,9},{9,8},{10,11... | collective-permute-start | bytes 36872 | tf_op jit(solution)/shard_map/ppermute | solution.py:421
  11.8 6.5 %collective-permute-start.6 = (s16[2,16,3200]{2,1,0:T(8,128)(2,1)S(1)}, s16[2,16,3200]{2,1,0:T(8,128)(2,1)S(1)}, u32[]{:S(2)}, u32[]{:S(2)}) collective-permute-start(s16[2,16,3200]{2,1,0:T(8,128)(2,1)S(1)} %collective-permute-done.4.refs_6_.refs_4_.refs_10_), channel_id=1, source_target_pairs={{0,2},{1,3},{4,0},{5,1},{8,4},{9,5},{12,8},{13,9},{14,12},{15,13},... | collective-permute-start | bytes 614408 | tf_op jit(solution)/shard_map/ppermute | solution.py:395
  13.4 5.9 %collective-permute-start.5 = (s16[2,16,3200]{2,1,0:T(8,128)(2,1)S(1)}, s16[2,16,3200]{2,1,0:T(8,128)(2,1)S(1)}, u32[]{:S(2)}, u32[]{:S(2)}) collective-permute-start(s16[2,16,3200]{2,1,0:T(8,128)(2,1)S(1)} %collective-permute-done.3.refs_5_.refs_3_.refs_9_), channel_id=1, source_target_pairs={{0,4},{1,5},{4,8},{5,9},{8,12},{9,13},{12,14},{13,15},{14,10},{15,... | collective-permute-start | bytes 614408 | tf_op jit(solution)/shard_map/ppermute | solution.py:395
  13.9 14.1 %copy-start.1 = (s16[2,16,3200]{2,1,0:T(8,128)(2,1)S(1)}, s16[2,16,3200]{2,1,0:T(8,128)(2,1)}, u32[]{:S(2)}) copy-start(s16[2,16,3200]{2,1,0:T(8,128)(2,1)} %get-tuple-element.50.refs_4_.refs_2_.refs_8_) | copy-start | bytes 614404
  14.7 13.4 %copy-start = (bf16[128,8,1024]{2,1,0:T(8,128)(2,1)S(1)}, bf16[128,8,1024]{2,1,0:T(8,128)(2,1)}, u32[]{:S(2)}) copy-start(bf16[128,8,1024]{2,1,0:T(8,128)(2,1)} %param.11) | copy-start | bytes 6291460
  19.4 6.2 %collective-permute-start.7 = (s16[2,16,3200]{2,1,0:T(8,128)(2,1)S(1)}, s16[2,16,3200]{2,1,0:T(8,128)(2,1)S(1)}, u32[]{:S(2)}, u32[]{:S(2)}) collective-permute-start(s16[2,16,3200]{2,1,0:T(8,128)(2,1)S(1)} %get-tuple-element.51.refs_7_.refs_5_.refs_11_), channel_id=1, source_target_pairs={{0,4},{1,5},{4,8},{5,9},{8,12},{9,13},{12,14},{13,15},{14,10},{15,... | collective-permute-start | bytes 614408 | tf_op jit(solution)/shard_map/ppermute | solution.py:395
  20.2 6.0 %collective-permute-start.8 = (s16[2,16,3200]{2,1,0:T(8,128)(2,1)S(1)}, s16[2,16,3200]{2,1,0:T(8,128)(2,1)S(1)}, u32[]{:S(2)}, u32[]{:S(2)}) collective-permute-start(s16[2,16,3200]{2,1,0:T(8,128)(2,1)S(1)} %get-tuple-element.52.refs_6_.refs_5_.refs_12_), channel_id=1, source_target_pairs={{0,2},{1,3},{4,0},{5,1},{8,4},{9,5},{12,8},{13,9},{14,12},{15,13},... | collective-permute-start | bytes 614408 | tf_op jit(solution)/shard_map/ppermute | solution.py:395
  25.6 4.7 %collective-permute-start.9 = (s16[1,16,3200]{2,1,0:T(8,128)(2,1)S(1)}, s16[1,16,3200]{2,1,0:T(8,128)(2,1)S(1)}, u32[]{:S(2)}, u32[]{:S(2)}) collective-permute-start(s16[1,16,3200]{2,1,0:T(8,128)(2,1)S(1)} %slice.8), channel_id=1, source_target_pairs={{0,4},{1,5},{4,8},{5,9},{8,12},{9,13},{12,14},{13,15},{14,10},{15,... | collective-permute-start | bytes 307208 | tf_op jit(solution)/shard_map/ppermute | solution.py:395
  26.1 4.9 %collective-permute-start.11 = (s16[1,16,3200]{2,1,0:T(8,128)(2,1)S(1)}, s16[1,16,3200]{2,1,0:T(8,128)(2,1)S(1)}, u32[]{:S(2)}, u32[]{:S(2)}) collective-permute-start(s16[1,16,3200]{2,1,0:T(8,128)(2,1)S(1)} %slice.9), channel_id=1, source_target_pairs={{0,2},{1,3},{4,0},{5,1},{8,4},{9,5},{12,8},{13,9},{14,12},{15,13},... | collective-permute-start | bytes 307208 | tf_op jit(solution)/shard_map/ppermute | solution.py:395
  30.9 2.1 %collective-permute-start.10 = (f32[8,128]{1,0:T(8,128)S(1)}, f32[8,128]{1,0:T(8,128)S(1)}, u32[]{:S(2)}, u32[]{:S(2)}) collective-permute-start(f32[8,128]{1,0:T(8,128)S(1)} %shard_map.142.refs_0_.refs_4_), channel_id=1, source_target_pairs={{0,1},{1,0},{2,3},{3,2},{4,5},{5,4},{6,7},{7,6},{8,9},{9,8},{10,11... | collective-permute-start | bytes 12296 | tf_op jit(solution)/shard_map/ppermute | solution.py:421
  35.1 8.4 %collective-permute-start.12 = (bf16[256,2048]{1,0:T(8,128)(2,1)S(1)}, bf16[256,2048]{1,0:T(8,128)(2,1)S(1)}, u32[]{:S(2)}, u32[]{:S(2)}) collective-permute-start(bf16[256,2048]{1,0:T(8,128)(2,1)S(1)} %get-tuple-element.61), channel_id=1, source_target_pairs={{0,1},{1,0},{2,3},{3,2},{4,5},{5,4},{6,7},{7,6},{8,9},{9,8},{10,11... | collective-permute-start | bytes 3145736 | tf_op jit(solution)/shard_map/ppermute | solution.py:421
  40.2 7.6 %collective-permute-start.13 = (s16[2,16,3200]{2,1,0:T(8,128)(2,1)S(1)}, s16[2,16,3200]{2,1,0:T(8,128)(2,1)S(1)}, u32[]{:S(2)}, u32[]{:S(2)}) collective-permute-start(s16[2,16,3200]{2,1,0:T(8,128)(2,1)S(1)} %get-tuple-element.63), channel_id=1, source_target_pairs={{0,4},{1,5},{2,6},{3,7},{4,0},{5,1},{6,2},{7,3},{8,12},{9,13},{10,... | collective-permute-start | bytes 614408 | tf_op jit(solution)/shard_map/ppermute | solution.py:421
  41.5 8.7 %collective-permute-start.15 = (s16[2,16,3200]{2,1,0:T(8,128)(2,1)S(1)}, s16[2,16,3200]{2,1,0:T(8,128)(2,1)S(1)}, u32[]{:S(2)}, u32[]{:S(2)}) collective-permute-start(s16[2,16,3200]{2,1,0:T(8,128)(2,1)S(1)} %get-tuple-element.69), channel_id=1, source_target_pairs={{0,2},{1,3},{2,0},{3,1},{4,6},{5,7},{6,4},{7,5},{8,10},{9,11},{10,... | collective-permute-start | bytes 614408 | tf_op jit(solution)/shard_map/ppermute | solution.py:421
  47.3 6.6 %collective-permute-start.14 = (s16[2,16,3200]{2,1,0:T(8,128)(2,1)S(1)}, s16[2,16,3200]{2,1,0:T(8,128)(2,1)S(1)}, u32[]{:S(2)}, u32[]{:S(2)}) collective-permute-start(s16[2,16,3200]{2,1,0:T(8,128)(2,1)S(1)} %get-tuple-element.67), channel_id=1, source_target_pairs={{0,4},{1,5},{2,6},{3,7},{4,0},{5,1},{6,2},{7,3},{8,12},{9,13},{10,... | collective-permute-start | bytes 614408 | tf_op jit(solution)/shard_map/ppermute | solution.py:421
  48.0 6.6 %collective-permute-start.16 = (s16[16,3200]{1,0:T(8,128)(2,1)S(1)}, s16[16,3200]{1,0:T(8,128)(2,1)S(1)}, u32[]{:S(2)}, u32[]{:S(2)}) collective-permute-start(s16[16,3200]{1,0:T(8,128)(2,1)S(1)} %get-tuple-element.66.refs_0_), channel_id=1, source_target_pairs={{0,2},{1,3},{2,0},{3,1},{4,6},{5,7},{6,4},{7,5},{8,10},{9,11},{10,... | collective-permute-start | bytes 307208 | tf_op jit(solution)/shard_map/ppermute | solution.py:421
  49.2 8.4 %collective-permute-start.17 = (s16[2,16,3200]{2,1,0:T(8,128)(2,1)S(1)}, s16[2,16,3200]{2,1,0:T(8,128)(2,1)S(1)}, u32[]{:S(2)}, u32[]{:S(2)}) collective-permute-start(s16[2,16,3200]{2,1,0:T(8,128)(2,1)S(1)} %get-tuple-element.73), channel_id=1, source_target_pairs={{0,2},{1,3},{2,0},{3,1},{4,6},{5,7},{6,4},{7,5},{8,10},{9,11},{10,... | collective-permute-start | bytes 614408 | tf_op jit(solution)/shard_map/ppermute | solution.py:421
  54.1 5.4 %collective-permute-start.18 = (s16[16,3200]{1,0:T(8,128)(2,1)S(1)}, s16[16,3200]{1,0:T(8,128)(2,1)S(1)}, u32[]{:S(2)}, u32[]{:S(2)}) collective-permute-start(s16[16,3200]{1,0:T(8,128)(2,1)S(1)} %get-tuple-element.70.refs_0_), channel_id=1, source_target_pairs={{0,2},{1,3},{2,0},{3,1},{4,6},{5,7},{6,4},{7,5},{8,10},{9,11},{10,... | collective-permute-start | bytes 307208 | tf_op jit(solution)/shard_map/ppermute | solution.py:421
  54.8 7.8 %collective-permute-start.19 = (s16[16,3200]{1,0:T(8,128)(2,1)S(1)}, s16[16,3200]{1,0:T(8,128)(2,1)S(1)}, u32[]{:S(2)}, u32[]{:S(2)}) collective-permute-start(s16[16,3200]{1,0:T(8,128)(2,1)S(1)} %shard_map.149.refs_0_), channel_id=1, source_target_pairs={{0,8},{1,9},{2,10},{3,11},{4,12},{5,13},{6,14},{7,15},{8,0},{9,1},... | collective-permute-start | bytes 307208 | tf_op jit(solution)/shard_map/ppermute | solution.py:421
  57.9 9.2 %collective-permute-start.21 = (s16[2,16,3200]{2,1,0:T(8,128)(2,1)S(1)}, s16[2,16,3200]{2,1,0:T(8,128)(2,1)S(1)}, u32[]{:S(2)}, u32[]{:S(2)}) collective-permute-start(s16[2,16,3200]{2,1,0:T(8,128)(2,1)S(1)} %get-tuple-element.75.refs_0_), channel_id=1, source_target_pairs={{0,4},{1,5},{2,6},{3,7},{4,0},{5,1},{6,2},{7,3},{8,12},{9,13},{10,... | collective-permute-start | bytes 614408 | tf_op jit(solution)/shard_map/ppermute | solution.py:421
  59.8 7.3 %collective-permute-start.20 = (s16[16,3200]{1,0:T(8,128)(2,1)S(1)}, s16[16,3200]{1,0:T(8,128)(2,1)S(1)}, u32[]{:S(2)}, u32[]{:S(2)}) collective-permute-start(s16[16,3200]{1,0:T(8,128)(2,1)S(1)} %shard_map.151.refs_0_), channel_id=1, source_target_pairs={{0,8},{1,9},{2,10},{3,11},{4,12},{5,13},{6,14},{7,15},{8,0},{9,1},... | collective-permute-start | bytes 307208 | tf_op jit(solution)/shard_map/ppermute | solution.py:421
  (3 other events, 11.0 us)

commit v15 on v14

--- a/solution.py
+++ b/solution.py
@@ -82,9 +82,10 @@
     return experts, gates, small_ref[:, 2 * top : 2 * top + 1]
 
 
-def members(place_ref, wide, first=0, count=None):
-    piece_of = lax.broadcasted_iota(jnp.int32, (1, wide), 1) // (wide // count)
-    found = jnp.zeros((1, wide), jnp.int32)
+def members(place_ref, wide, first, count, dim=1):
+    shape = (1, wide) if dim == 1 else (wide, 1)
+    piece_of = lax.broadcasted_iota(jnp.int32, shape, dim) // (wide // count)
+    found = jnp.zeros(shape, jnp.int32)
     for number in range(count):
         found = jnp.where(piece_of == number, place_ref[1 + first + number], found)
     return found.astype(f32)
@@ -120,7 +121,7 @@
     small_ref[...] = jnp.concatenate([own_ref[...], other_ref[...]], axis=1).T
     experts, gates, _ = token_columns(small_ref, top)
     _, tokens, wide = rank_ref.shape
-    column = members(place_ref, wide, 0, slots)
+    column = members(place_ref, wide, slots, slots)
     below = (
         lax.broadcasted_iota(jnp.int32, (tokens, tokens), 0)
         > lax.broadcasted_iota(jnp.int32, (tokens, tokens), 1)
@@ -186,9 +187,9 @@
     for block in range(2):
         total = capacity_ref[...] - prior_ref[block : block + 1] - arrived_ref[1 - block : 2 - block]
         limit = jnp.zeros((1, wide), f32)
-        for arrival in range(slots):
-            picked = jnp.where(lane == counts_lane + place_ref[1 + arrival], total, 0.0)
-            limit = jnp.where(piece_of == arrival, jnp.sum(picked, axis=1, keepdims=True), limit)
+        for slot in range(slots):
+            picked = jnp.where(lane == counts_lane + place_ref[1 + slots + slot], total, 0.0)
+            limit = jnp.where(piece_of == slot, jnp.sum(picked, axis=1, keepdims=True), limit)
         limits.append(limit)
     return limits
 
@@ -212,12 +213,19 @@
         jnp.concatenate([ref[:, kind * half : (kind + 1) * half] for ref in (early_ref, late_ref)], axis=1)
         for kind in range(2)
     ]
+    rank = wide // slots
+    by_arrival = members(place_ref, wide, 0, slots, 0) == members(place_ref, wide, slots, slots)
+    row = lax.broadcasted_iota(jnp.int32, (wide, wide), 0)
+    same_index = row % rank == lax.broadcasted_iota(jnp.int32, (wide, wide), 1) % rank
+    order = jnp.where(by_arrival & same_index, 1.0, 0.0).astype(bf16)
+    reduced = [sum(dot(part, order, 1, 0) for part in halves(both)) for both in reduced]
     weighted = jnp.concatenate([weight * part for part in reduced], axis=1)
     weighted_ref[...] = weighted
     for arrival in range(slots):
         for kind in range(2):
             _, up = decode(piece_part(piece_refs, arrival, kind, True), hidden_width)
-            high_ref[kind, arrival], low_ref[kind, arrival] = halves(up)
+            slot = place_ref[1 + 2 * slots + arrival]
+            high_ref[kind, slot], low_ref[kind, slot] = halves(up)
     factor = high_ref[...].reshape(2 * wide, model_width), low_ref[...].reshape(2 * wide, model_width)
     tangent = dot_pairs(halves(weighted), factor, 1, 0)
     tangent_ref[...] = tangent
@@ -238,25 +246,22 @@
     return both[:middle] + both[middle:]
 
 
-def put_chunks(place_ref, down_ref, up_ref, keep_ref, near_ref, chunk_ref, far_ref, down, up):
+def put_chunks(keep_ref, near_ref, chunk_ref, far_ref, down, up):
     rank = keep_ref.shape[1]
-    slots = down.shape[0] // rank
-    down_ref[...] = down
-    up_ref[...] = up
+    rows = down.shape[0] // rank // 2
 
     def slot(number):
-        start = pl.multiple_of(place_ref[1 + slots + number] * rank, rank)
-        return down_ref[pl.ds(start, rank), :], up_ref[pl.ds(start, rank), :]
+        start = number * rank
+        return down[start : start + rank], up[start : start + rank]
 
     for place in range(2):
         keep_ref[place] = jnp.concatenate(slot(place), axis=1)
-        near_ref[place] = encode(*slot(slots // 2 + place))
-        chunk_ref[place] = jnp.concatenate(slot(place * slots // 2 + 2), axis=1)
-        far_ref[place] = encode(*slot(place * slots // 2 + 3))
+        near_ref[place] = encode(*slot(rows + place))
+        chunk_ref[place] = jnp.concatenate(slot(place * rows + 2), axis=1)
+        far_ref[place] = encode(*slot(place * rows + 3))
 
 
 def gradient_kernel(
-    place_ref,
     same_ref,
     mask_ref,
     own_ref,
@@ -274,8 +279,6 @@
     up_ref,
     to_ref,
     left_ref,
-    down_sum_ref,
-    up_sum_ref,
 ):
     wide = weight_ref.shape[1]
     model_width = up_ref.shape[1]
@@ -288,13 +291,11 @@
     down = dot(left_ref[0], own_ref[...], 0, 0) + dot(left_ref[1], other_ref[...], 0, 0)
     up = add_halves(dot(jnp.concatenate(halves(weighted_ref[...]), axis=1), gradient, 0, 0))
     up_ref[...] = up[:wide]
-    out_refs = keep_ref, near_ref, chunk_ref, far_ref
-    put_chunks(place_ref, down_sum_ref, up_sum_ref, *out_refs, add_halves(down), up[wide:])
+    put_chunks(keep_ref, near_ref, chunk_ref, far_ref, add_halves(down), up[wide:])
 
 
 def curvature_kernel(
     top,
-    place_ref,
     small_ref,
     same_ref,
     mask_ref,
@@ -308,14 +309,15 @@
     to_ref,
     tangent_ref,
     arrived_ref,
+    gradient_near_ref,
     keep_ref,
     near_ref,
     chunk_ref,
     far_ref,
+    onward_ref,
     left_ref,
-    down_sum_ref,
-    up_sum_ref,
 ):
+    onward_ref[...] = gradient_near_ref[...]
     _, _, curvature = token_columns(small_ref, top)
     tokens, wide = weight_ref.shape
     block = tokens // 2
@@ -328,12 +330,13 @@
     down = dot(left_ref[0], own_ref[...], 0, 0) + dot(left_ref[1], other_ref[...], 0, 0)
     weighted_u = halves(weighted_ref[:, wide:])
     up = add_halves(dot(jnp.concatenate(weighted_u, axis=1), resid[0], 0, 0)) + dot(weighted_u[0], resid[1], 0, 0)
-    out_refs = keep_ref, near_ref, chunk_ref, far_ref
-    put_chunks(place_ref, down_sum_ref, up_sum_ref, *out_refs, add_halves(down), up_ref[...] + up)
-
-
-def pair_kernel(hidden_width, arrived_ref, chunk_ref, near_ref, across_ref, keep_ref, onward_ref):
-    onward_ref[...] = near_ref[...]
+    put_chunks(keep_ref, near_ref, chunk_ref, far_ref, add_halves(down), up_ref[...] + up)
+
+
+def pair_kernel(hidden_width, arrived_ref, chunk_ref, *refs):
+    passing, (across_ref, keep_ref) = (refs[:1], refs[1:3]) if len(refs) == 4 else ((), refs)
+    for near_ref in passing:
+        refs[3][...] = near_ref[...]
     for x in range(2):
         down, up = decode(arrived_ref[x], hidden_width)
         down, up = chunk_ref[x, :, :hidden_width] + down, chunk_ref[x, :, hidden_width:] + up
@@ -348,36 +351,28 @@
     out_ref[...] = encode(keep_ref[:, :hidden_width] + down, keep_ref[:, hidden_width:] + up)
 
 
-def near_kernel(
-    hidden_width, gradient_ref, curvature_ref, gradient_keep_ref, curvature_keep_ref, onward_ref, total_ref
-):
-    pairs = ((gradient_ref, gradient_keep_ref), (curvature_ref, curvature_keep_ref))
-    for kind, (arrived_ref, keep_ref) in enumerate(pairs):
-        for z in range(2):
-            down, up = decode(arrived_ref[z], hidden_width)
-            down, up = keep_ref[z, :, :hidden_width] + down, keep_ref[z, :, hidden_width:] + up
-            if z == 0:
-                total_ref[kind] = jnp.concatenate([down, up], axis=1)
-            else:
-                onward_ref[kind] = encode(down, up)
-
-
-def add_kernel(hidden_width, total_ref, arrived_ref, out_ref):
-    down, up = decode(arrived_ref[...], hidden_width)
-    out_ref[:, :hidden_width] = total_ref[0, :, :hidden_width] + down
-    out_ref[:, hidden_width:] = total_ref[0, :, hidden_width:] + up
-
-
-def total_kernel(hidden_width, gradient_ref, total_ref, far_ref, pair_ref, *out_refs):
-    far = decode(far_ref[...], hidden_width)
-    totals = [
-        (gradient_ref[:, :hidden_width], gradient_ref[:, hidden_width:]),
-        (total_ref[1, :, :hidden_width] + far[0], total_ref[1, :, hidden_width:] + far[1]),
-    ]
-    for kind in range(2):
-        down, up = decode(pair_ref[kind], hidden_width)
-        out_refs[2 * kind][...] = totals[kind][0] + down
-        out_refs[2 * kind + 1][...] = totals[kind][1] + up
+def near_kernel(hidden_width, arrived_ref, keep_ref, onward_ref, total_ref):
+    for z in range(2):
+        down, up = decode(arrived_ref[z], hidden_width)
+        down, up = keep_ref[z, :, :hidden_width] + down, keep_ref[z, :, hidden_width:] + up
+        if z == 0:
+            total_ref[...] = jnp.concatenate([down, up], axis=1)
+        else:
+            onward_ref[...] = encode(down, up)
+
+
+def add_kernel(hidden_width, total_ref, near_ref, far_ref, out_ref):
+    near, far = decode(near_ref[...], hidden_width), decode(far_ref[...], hidden_width)
+    out_ref[:, :hidden_width] = total_ref[:, :hidden_width] + near[0] + far[0]
+    out_ref[:, hidden_width:] = total_ref[:, hidden_width:] + near[1] + far[1]
+
+
+def total_kernel(hidden_width, gradient_ref, total_ref, near_ref, far_ref, *out_refs):
+    near, far = decode(near_ref[...], hidden_width), decode(far_ref[...], hidden_width)
+    out_refs[0][...] = gradient_ref[:, :hidden_width]
+    out_refs[1][...] = gradient_ref[:, hidden_width:]
+    out_refs[2][...] = total_ref[:, :hidden_width] + near[0] + far[0]
+    out_refs[3][...] = total_ref[:, hidden_width:] + near[1] + far[1]
 
 
 class Ring:
@@ -486,10 +481,8 @@
         grant=whole_vmem,
     )
     arrivals = ring.members(me)
-    number = jnp.arange(slots, dtype=jnp.int32)
     slot_of_arrival = (arrivals ^ me) // 4 + rows * ((arrivals ^ me) // 2 % 2)
-    arrival_of_slot = jnp.sum(jnp.where(slot_of_arrival == number[:, None], number, 0), axis=1)
-    place.append(jnp.concatenate([me[None], arrivals, arrival_of_slot]).astype(jnp.int32))
+    place.append(jnp.concatenate([me[None], arrivals, me ^ jnp.array(masks, jnp.int32), slot_of_arrival]).astype(jnp.int32))
     small_other = exchange(small, 1)
     hidden = hidden_of_route.reshape(tokens * top, hidden_width)
     small_columns, local_rank, gate, same, mask, hidden_other, gradient_other = call(
@@ -558,17 +551,12 @@
         *pieces,
     )
     arrived = exchange(coded, 1)
-    left = [
-        pltpu.VMEM((2, top * tokens, 2 * wide), bf16),
-        pltpu.VMEM((wide, hidden_width), f32),
-        pltpu.VMEM((wide, model_width), f32),
-    ]
+    left = [pltpu.VMEM((2, top * tokens, 2 * wide), bf16)]
     chunks = [((2, rank, hidden_width + model_width), f32), ((2, rank, coded_width), i16)] * 2
     gradient_keep, gradient_near, gradient_chunk, gradient_far, up, to = call(
         gradient_kernel,
         down_multiplies + 8 * up_multiplies,
         chunks + [((wide, model_width), f32), ((both, wide), f32)],
-        *place,
         same,
         mask,
         hidden,
@@ -582,12 +570,10 @@
         scratch=left,
     )
     gradient_far = exchange(gradient_far, 4)
-    gradient_near = exchange(gradient_near, 2)
-    curvature_keep, curvature_near, curvature_chunk, curvature_far = call(
+    curvature_keep, curvature_near, curvature_chunk, curvature_far, gradient_near = call(
         functools.partial(curvature_kernel, top),
         down_multiplies + 6 * up_multiplies,
-        chunks,
-        *place,
+        chunks + [(gradient_near.shape, i16)],
         small_columns,
         same,
         mask,
@@ -601,6 +587,7 @@
         to,
         tangent,
         arrived,
+        gradient_near,
         scratch=left,
     )
 
@@ -613,43 +600,49 @@
         return call(functools.partial(kernel, hidden_width), hop, outs, *operands, after=after)
 
     curvature_far = exchange(curvature_far, 4)
-    pair = [(one_coded, i16), (one, f32), ((2,) + one_coded, i16)]
+    gradient_near = exchange(gradient_near, 2)
+    pair = [(one_coded, i16), (one, f32)]
     gradient_across, gradient_pair, curvature_near = hop_call(
-        pair_kernel, pair, gradient_far, gradient_chunk, curvature_near, after=[curvature_keep]
+        pair_kernel,
+        pair + [(curvature_near.shape, i16)],
+        gradient_far,
+        gradient_chunk,
+        curvature_near,
+        after=[curvature_keep],
     )
     curvature_near = exchange(curvature_near, 2)
-    curvature_across, curvature_pair, gradient_near = hop_call(
-        pair_kernel, pair, curvature_far, curvature_chunk, gradient_near, after=[gradient_across]
-    )
+    curvature_across, curvature_pair = hop_call(
+        pair_kernel, pair, curvature_far, curvature_chunk, after=[gradient_across]
+    )
+    near = [(one_coded, i16), (one, f32)]
+    gradient_onward, gradient_total = hop_call(
+        near_kernel, near, gradient_near, gradient_keep, after=[curvature_across]
+    )
+    gradient_onward = exchange(gradient_onward, 4)
     (gradient_beyond,) = hop_call(
-        far_kernel,
-        [(one_coded, i16)],
-        exchange(gradient_across, 2),
-        gradient_pair,
-        after=[curvature_across],
-    )
-    onward, total = hop_call(
-        near_kernel,
-        [((2,) + one_coded, i16), ((2,) + one, f32)],
-        gradient_near,
-        curvature_near,
-        gradient_keep,
-        curvature_keep,
-        after=[gradient_beyond],
+        far_kernel, [(one_coded, i16)], exchange(gradient_across, 2), gradient_pair, after=[gradient_total]
     )
     (curvature_beyond,) = hop_call(
-        far_kernel, [(one_coded, i16)], exchange(curvature_across, 2), curvature_pair, after=[onward]
+        far_kernel, [(one_coded, i16)], exchange(curvature_across, 2), curvature_pair, after=[gradient_beyond]
+    )
+    curvature_onward, curvature_total = hop_call(
+        near_kernel, near, curvature_near, curvature_keep, after=[curvature_beyond, gradient_onward]
     )
     (gradient_total,) = hop_call(
-        add_kernel, [(one, f32)], total, exchange(gradient_beyond, 8), after=[curvature_beyond]
+        add_kernel,
+        [(one, f32)],
+        gradient_total,
+        gradient_onward,
+        exchange(gradient_beyond, 8),
+        after=[curvature_total],
     )
     down_gradient, up_gradient, curvature_down, curvature_up = hop_call(
         total_kernel,
         [((rank, hidden_width), f32), ((rank, model_width), f32)] * 2,
         gradient_total,
-        total,
+        curvature_total,
+        exchange(curvature_onward, 4),
         exchange(curvature_beyond, 8),
-        exchange(onward, 4),
     )
     return down_gradient.T[None], up_gradient[None], curvature_down.T[None], curvature_up[None]
 

time: 68.2 us -> 69.6 us (1.021)
  starting transfers between devices: 24.3 us -> 26 us
  Pallas kernels: 21.2 us -> 20.3 us
    ppermute x14 -> x15, starting transfers between devices: 14.7 us -> 16.9 us  [exchange(): lax.ppermute(value, 'expert', [(device, device ^ mask) for device in rang...]
    pallas_call x16 -> x17, Pallas kernels: 21.2 us -> 20.3 us  [call(): pl.pallas_call(lambda *refs: kernel(*refs[len(after):]), out_shape=[jax.S...]
    ppermute x14 -> x15, waiting for transfers between devices: 8.24 us -> 8.54 us  [exchange(): lax.ppermute(value, 'expert', [(device, device ^ mask) for device in rang...]
  transfers between devices with their start and end apart: 22 -> 23, of which waited for: 8 -> 12; matrix products, arithmetic and copies ran while one was open for 1% -> 2% of each run, Pallas kernels for 27% -> 25%
where the time goes in v15:
time: 69.6 us; the launch traced here: 69.3 us
  starting transfers between devices  26 us (37%)
  Pallas kernels  20.3 us (29%)
  waiting for transfers between devices  19.9 us (29%)
  other arithmetic  1.43 us (2%)
  local copies, waits for them, and re-layouts  0.85 us (1%)
  between operations  0.82 us (1%)
    pallas_call x17, Pallas kernels, call(): pl.pallas_call(lambda *refs: kernel(*refs[len(after):]), out_shape=[jax.S...  20.3 us
    ppermute x15, starting transfers between devices, exchange(): lax.ppermute(value, 'expert', [(device, device ^ mask) for device in rang...  16.9 us
    ppermute x8, waiting for transfers between devices, shift(): return lax.ppermute(value, 'expert', pairs)  11.3 us
    ppermute x8, starting transfers between devices, shift(): return lax.ppermute(value, 'expert', pairs)  9.12 us
    ppermute x15, waiting for transfers between devices, exchange(): lax.ppermute(value, 'expert', [(device, device ^ mask) for device in rang...  8.54 us
  transfers between devices with their start and end apart: 23, of which 12 were waited for; matrix products, arithmetic and copies ran while one was open for 2% of the time, Pallas kernels for 25%

profile of v15, /device:TPU:0, one launch (start us, length us, event | category | flops | bytes accessed | tf_op | source)
XLA Modules:
  0.0 69.3 jit_solution(15816361306076645377)
XLA Ops:
  1.2 2.0 %shard_map.147 = (s16[2,16,3200]{2,1,0:T(8,128)(2,1)}, f32[24,128]{1,0:T(8,128)}) custom-call(s32[8,128]{1,0:T(8,128)} %bitcast.32, bf16[8,128]{1,0:T(8,128)(2,1)} %bitcast.33, f32[1,128]{1,0:T(1,128)} %bitcast.34, f32[16,1024]{1,0:T(8,128)} %bitcast.30, f32[16,1024]{1,0:T(8,128)} %bitcast.31, f32[16,2048]{1,0:T(8,128)} %bitcast.28, f32[16,2048]{1,0:T(8,128)} %bitcast.29), custom_call_target="tpu_custom_call" | custom-call | flops 200000000 | bytes 1048576 | tf_op jit(solution)/shard_map/pallas_call | solution.py:453
  3.1 2.6 %collective-permute-start.4 = (s16[2,16,3200]{2,1,0:T(8,128)(2,1)}, s16[2,16,3200]{2,1,0:T(8,128)(2,1)S(1)}, u32[]{:S(2)}, u32[]{:S(2)}) collective-permute-start(s16[2,16,3200]{2,1,0:T(8,128)(2,1)} %get-tuple-element.52.refs_4_.refs_2_.refs_8_), channel_id=1, source_target_pairs={{0,2},{1,3},{4,0},{5,1},{8,4},{9,5},{12,8},{13,9},{14,12},{15,13},... | collective-permute-start | bytes 614408 | tf_op jit(solution)/shard_map/ppermute | solution.py:390
  7.7 4.0 %collective-permute-done.4.refs_6_.refs_4_.refs_10_ = s16[2,16,3200]{2,1,0:T(8,128)(2,1)S(1)} collective-permute-done((s16[2,16,3200]{2,1,0:T(8,128)(2,1)}, s16[2,16,3200]{2,1,0:T(8,128)(2,1)S(1)}, u32[]{:S(2)}, u32[]{:S(2)}) %collective-permute-start.4) | collective-permute-done | bytes 204832 | tf_op jit(solution)/shard_map/ppermute | solution.py:390
  11.7 1.7 %collective-permute-start.6 = (s16[2,16,3200]{2,1,0:T(8,128)(2,1)S(1)}, s16[2,16,3200]{2,1,0:T(8,128)(2,1)S(1)}, u32[]{:S(2)}, u32[]{:S(2)}) collective-permute-start(s16[2,16,3200]{2,1,0:T(8,128)(2,1)S(1)} %collective-permute-done.4.refs_6_.refs_4_.refs_10_), channel_id=1, source_target_pairs={{0,2},{1,3},{4,0},{5,1},{8,4},{9,5},{12,8},{13,9},{14,12},{15,13},... | collective-permute-start | bytes 614408 | tf_op jit(solution)/shard_map/ppermute | solution.py:390
  14.6 2.2 %shard_map.148 = (f32[256,24]{1,0:T(8,128)S(1)}, f32[2,128,128]{2,1,0:T(8,128)S(1)}, f32[2,128,128]{2,1,0:T(8,128)S(1)}, bf16[1024,128]{1,0:T(8,128)(2,1)S(1)}, ...) custom-call(s32[25]{0:T(128)S(1)} %pad_add_fusion.refs_0_.refs_1_, ...), custom_call_target="tpu_custom_call" | custom-call | flops 2000000000 | bytes 1048576 | tf_op jit(solution)/shard_map/pallas_call | solution.py:453
  16.8 1.9 %collective-permute-done.6.refs_2_ = s16[2,16,3200]{2,1,0:T(8,128)(2,1)S(1)} collective-permute-done((s16[2,16,3200]{2,1,0:T(8,128)(2,1)S(1)}, s16[2,16,3200]{2,1,0:T(8,128)(2,1)S(1)}, u32[]{:S(2)}, u32[]{:S(2)}) %collective-permute-start.6) | collective-permute-done | bytes 204832 | tf_op jit(solution)/shard_map/ppermute | solution.py:390
  20.4 1.5 %collective-permute-start.8 = (s16[2,16,3200]{2,1,0:T(8,128)(2,1)S(1)}, s16[2,16,3200]{2,1,0:T(8,128)(2,1)S(1)}, u32[]{:S(2)}, u32[]{:S(2)}) collective-permute-start(s16[2,16,3200]{2,1,0:T(8,128)(2,1)S(1)} %get-tuple-element.54.refs_6_.refs_5_.refs_12_), channel_id=1, source_target_pairs={{0,2},{1,3},{4,0},{5,1},{8,4},{9,5},{12,8},{13,9},{14,12},{15,13},... | collective-permute-start | bytes 614408 | tf_op jit(solution)/shard_map/ppermute | solution.py:390
  21.9 3.7 %collective-permute-done.7.refs_7_.refs_6_.refs_13_ = s16[2,16,3200]{2,1,0:T(8,128)(2,1)S(1)} collective-permute-done((s16[2,16,3200]{2,1,0:T(8,128)(2,1)S(1)}, s16[2,16,3200]{2,1,0:T(8,128)(2,1)S(1)}, u32[]{:S(2)}, u32[]{:S(2)}) %collective-permute-start.7) | collective-permute-done | bytes 204832 | tf_op jit(solution)/shard_map/ppermute | solution.py:390
  26.4 1.7 %collective-permute-start.11 = (s16[1,16,3200]{2,1,0:T(8,128)(2,1)S(1)}, s16[1,16,3200]{2,1,0:T(8,128)(2,1)S(1)}, u32[]{:S(2)}, u32[]{:S(2)}) collective-permute-start(s16[1,16,3200]{2,1,0:T(8,128)(2,1)S(1)} %slice.9), channel_id=1, source_target_pairs={{0,2},{1,3},{4,0},{5,1},{8,4},{9,5},{12,8},{13,9},{14,12},{15,13},... | collective-permute-start | bytes 307208 | tf_op jit(solution)/shard_map/ppermute | solution.py:390
  28.0 2.0 %shard_map.150.refs_0_.refs_6_ = f32[256,128]{1,0:T(8,128)S(1)} custom-call(s32[25]{0:T(128)S(1)} %pad_add_fusion.refs_0_.refs_1_, f32[256,24]{1,0:T(8,128)S(1)} %get-tuple-element.46.refs_1_.refs_2_.refs_0_, bf16[1024,1024]{1,0:T(8,128)(2,1)S(1)} %bitcast.24, bf16[1024,1024]{1,0:T(8,128)(2,1)S(1)} %get-tuple-element.49.refs_3_.refs_4_, ...), custom_call_target="tpu_custom_call" | custom-call | flops 1073741824 | bytes 1048576 | tf_op jit(solution)/shard_map/pallas_call | solution.py:453
  31.3 2.0 %shard_map.152.refs_7_ = f32[256,128]{1,0:T(8,128)S(1)} custom-call(f32[8,128]{1,0:T(8,128)S(1)} %shard_map.151.refs_0_.refs_4_, s32[25]{0:T(128)S(1)} %pad_add_fusion.refs_0_.refs_1_, f32[256,24]{1,0:T(8,128)S(1)} %get-tuple-element.46.refs_1_.refs_2_.refs_0_, bf16[1024,1024]{1,0:T(8,128)(2,1)S(1)} %bitcast.25, ...), custom_call_target="tpu_custom_call" | custom-call | flops 1073741824 | bytes 1048576 | tf_op jit(solution)/shard_map/pallas_call | solution.py:453
  33.3 2.3 %shard_map.153 = (f32[256,128]{1,0:T(8,128)S(1)}, f32[256,256]{1,0:T(8,128)S(1)}, f32[256,2048]{1,0:T(8,128)S(1)}, bf16[256,2048]{1,0:T(8,128)(2,1)S(1)}, bf16[2...) custom-call(s32[25]{0:T(128)S(1)} %pad_add_fusion.refs_0_.refs_1_, ...), custom_call_target="tpu_custom_call" | custom-call | flops 805306368 | bytes 1048576 | tf_op jit(solution)/shard_map/pallas_call | solution.py:453
  35.9 4.0 %shard_map.154 = (f32[2,16,3072]{2,1,0:T(8,128)S(1)}, s16[2,16,3200]{2,1,0:T(8,128)(2,1)S(1)}, f32[2,16,3072]{2,1,0:T(8,128)S(1)}, s16[2,16,3200]{2,1,0:T(8,128)...) custom-call(bf16[1024,128]{1,0:T(8,128)(2,1)S(1)} %get-tuple-element.47.refs_0_.refs_1_, ...), custom_call_target="tpu_custom_call" | custom-call | flops 2147483648 | bytes 1048576 | tf_op jit(solution)/shard_map/pallas_call | solution.py:453
  41.2 3.2 %shard_map.155 = (f32[2,16,3072]{2,1,0:T(8,128)S(1)}, s16[2,16,3200]{2,1,0:T(8,128)(2,1)S(1)}, f32[2,16,3072]{2,1,0:T(8,128)S(1)}, s16[2,16,3200]{2,1,0:T(8,128)(2,1)S(1)}, s16[2,16,3200]{2,1,0:T(8,128)(2,1)S(1)}) custom-call(f32[256,24]{1,0:T(8,128)S(1)} %get-tuple-element.46.refs_1_.refs_2_.refs_0_, ...), custom_call_target="tpu_custom_call" | custom-call | flops 1879048192 | bytes 1048576 | tf_op jit(solution)/shard_map/pallas_call | solution.py:453
  45.3 1.6 %collective-permute-start.15 = (s16[2,16,3200]{2,1,0:T(8,128)(2,1)S(1)}, s16[2,16,3200]{2,1,0:T(8,128)(2,1)S(1)}, u32[]{:S(2)}, u32[]{:S(2)}) collective-permute-start(s16[2,16,3200]{2,1,0:T(8,128)(2,1)S(1)} %get-tuple-element.73), channel_id=1, source_target_pairs={{0,2},{1,3},{2,0},{3,1},{4,6},{5,7},{6,4},{7,5},{8,10},{9,11},{10,... | collective-permute-start | bytes 614408 | tf_op jit(solution)/shard_map/ppermute | solution.py:416
  47.4 1.5 %collective-permute-start.16 = (s16[16,3200]{1,0:T(8,128)(2,1)S(1)}, s16[16,3200]{1,0:T(8,128)(2,1)S(1)}, u32[]{:S(2)}, u32[]{:S(2)}) collective-permute-start(s16[16,3200]{1,0:T(8,128)(2,1)S(1)} %get-tuple-element.69.refs_0_), channel_id=1, source_target_pairs={{0,2},{1,3},{2,0},{3,1},{4,6},{5,7},{6,4},{7,5},{8,10},{9,11},{10,... | collective-permute-start | bytes 307208 | tf_op jit(solution)/shard_map/ppermute | solution.py:416
  49.5 2.2 %collective-permute-done.14.refs_1_ = s16[2,16,3200]{2,1,0:T(8,128)(2,1)S(1)} collective-permute-done((s16[2,16,3200]{2,1,0:T(8,128)(2,1)S(1)}, s16[2,16,3200]{2,1,0:T(8,128)(2,1)S(1)}, u32[]{:S(2)}, u32[]{:S(2)}) %collective-permute-start.14) | collective-permute-done | bytes 204832 | tf_op jit(solution)/shard_map/ppermute | solution.py:416
  51.9 1.6 %collective-permute-start.17 = (s16[16,3200]{1,0:T(8,128)(2,1)S(1)}, s16[16,3200]{1,0:T(8,128)(2,1)S(1)}, u32[]{:S(2)}, u32[]{:S(2)}) collective-permute-start(s16[16,3200]{1,0:T(8,128)(2,1)S(1)} %get-tuple-element.72.refs_0_), channel_id=1, source_target_pairs={{0,2},{1,3},{2,0},{3,1},{4,6},{5,7},{6,4},{7,5},{8,10},{9,11},{10,... | collective-permute-start | bytes 307208 | tf_op jit(solution)/shard_map/ppermute | solution.py:416
  55.6 2.4 %collective-permute-start.20 = (s16[16,3200]{1,0:T(8,128)(2,1)S(1)}, s16[16,3200]{1,0:T(8,128)(2,1)S(1)}, u32[]{:S(2)}, u32[]{:S(2)}) collective-permute-start(s16[16,3200]{1,0:T(8,128)(2,1)S(1)} %shard_map.159.refs_0_), channel_id=1, source_target_pairs={{0,8},{1,9},{2,10},{3,11},{4,12},{5,13},{6,14},{7,15},{8,0},{9,1},... | collective-permute-start | bytes 307208 | tf_op jit(solution)/shard_map/ppermute | solution.py:416
  58.0 2.7 %collective-permute-done.17.refs_1_ = s16[16,3200]{1,0:T(8,128)(2,1)S(1)} collective-permute-done((s16[16,3200]{1,0:T(8,128)(2,1)S(1)}, s16[16,3200]{1,0:T(8,128)(2,1)S(1)}, u32[]{:S(2)}, u32[]{:S(2)}) %collective-permute-start.17) | collective-permute-done | bytes 102432 | tf_op jit(solution)/shard_map/ppermute | solution.py:416
  60.9 2.6 %collective-permute-start.22 = (s16[16,3200]{1,0:T(8,128)(2,1)S(1)}, s16[16,3200]{1,0:T(8,128)(2,1)S(1)}, u32[]{:S(2)}, u32[]{:S(2)}) collective-permute-start(s16[16,3200]{1,0:T(8,128)(2,1)S(1)} %shard_map.160.refs_0_), channel_id=1, source_target_pairs={{0,8},{1,9},{2,10},{3,11},{4,12},{5,13},{6,14},{7,15},{8,0},{9,1},... | collective-permute-start | bytes 307208 | tf_op jit(solution)/shard_map/ppermute | solution.py:416
  63.8 1.6 %collective-permute-start.21 = (s16[16,3200]{1,0:T(8,128)(2,1)S(1)}, s16[16,3200]{1,0:T(8,128)(2,1)S(1)}, u32[]{:S(2)}, u32[]{:S(2)}) collective-permute-start(s16[16,3200]{1,0:T(8,128)(2,1)S(1)} %get-tuple-element.81), channel_id=1, source_target_pairs={{0,4},{1,5},{2,6},{3,7},{4,0},{5,1},{6,2},{7,3},{8,12},{9,13},{10,... | collective-permute-start | bytes 307208 | tf_op jit(solution)/shard_map/ppermute | solution.py:416
  65.5 1.4 %collective-permute-done.22.refs_3_ = s16[16,3200]{1,0:T(8,128)(2,1)S(1)} collective-permute-done((s16[16,3200]{1,0:T(8,128)(2,1)S(1)}, s16[16,3200]{1,0:T(8,128)(2,1)S(1)}, u32[]{:S(2)}, u32[]{:S(2)}) %collective-permute-start.22) | collective-permute-done | bytes 102432 | tf_op jit(solution)/shard_map/ppermute | solution.py:416
  67.0 1.5 %collective-permute-done.21.refs_2_ = s16[16,3200]{1,0:T(8,128)(2,1)S(1)} collective-permute-done((s16[16,3200]{1,0:T(8,128)(2,1)S(1)}, s16[16,3200]{1,0:T(8,128)(2,1)S(1)}, u32[]{:S(2)}, u32[]{:S(2)}) %collective-permute-start.21) | collective-permute-done | bytes 102432 | tf_op jit(solution)/shard_map/ppermute | solution.py:416
  (56 shorter events, 14.7 us)
Async XLA Ops:
  0.6 13.2 %collective-permute-start.1 = (bf16[1024,1024]{1,0:T(8,128)(2,1)}, bf16[1024,1024]{1,0:T(8,128)(2,1)S(1)}, u32[]{:S(2)}, u32[]{:S(2)}) collective-permute-start(bf16[1024,1024]{1,0:T(8,128)(2,1)} %bitcast.23), channel_id=1, source_target_pairs={{0,1},{1,0},{2,3},{3,2},{4,5},{5,4},{6,7},{7,6},{8,9},{9,8},{10,11... | collective-permute-start | bytes 6291464 | tf_op jit(solution)/shard_map/ppermute | solution.py:416
  3.1 8.6 %collective-permute-start.4 = (s16[2,16,3200]{2,1,0:T(8,128)(2,1)}, s16[2,16,3200]{2,1,0:T(8,128)(2,1)S(1)}, u32[]{:S(2)}, u32[]{:S(2)}) collective-permute-start(s16[2,16,3200]{2,1,0:T(8,128)(2,1)} %get-tuple-element.52.refs_4_.refs_2_.refs_8_), channel_id=1, source_target_pairs={{0,2},{1,3},{4,0},{5,1},{8,4},{9,5},{12,8},{13,9},{14,12},{15,13},... | collective-permute-start | bytes 614408 | tf_op jit(solution)/shard_map/ppermute | solution.py:390
  5.7 7.7 %collective-permute-start.3 = (s16[2,16,3200]{2,1,0:T(8,128)(2,1)}, s16[2,16,3200]{2,1,0:T(8,128)(2,1)S(1)}, u32[]{:S(2)}, u32[]{:S(2)}) collective-permute-start(s16[2,16,3200]{2,1,0:T(8,128)(2,1)} %get-tuple-element.52.refs_4_.refs_2_.refs_8_), channel_id=1, source_target_pairs={{0,4},{1,5},{4,8},{5,9},{8,12},{9,13},{12,14},{13,15},{14,10},{15,... | collective-permute-start | bytes 614408 | tf_op jit(solution)/shard_map/ppermute | solution.py:390
  5.8 8.0 %collective-permute-start = (f32[24,128]{1,0:T(8,128)}, f32[24,128]{1,0:T(8,128)S(1)}, u32[]{:S(2)}, u32[]{:S(2)}) collective-permute-start(f32[24,128]{1,0:T(8,128)} %get-tuple-element.45.refs_1_), channel_id=1, source_target_pairs={{0,1},{1,0},{2,3},{3,2},{4,5},{5,4},{6,7},{7,6},{8,9},{9,8},{10,11... | collective-permute-start | bytes 36872 | tf_op jit(solution)/shard_map/ppermute | solution.py:416
  6.0 7.8 %collective-permute-start.2 = (bf16[128,2048]{1,0:T(8,128)(2,1)}, bf16[128,2048]{1,0:T(8,128)(2,1)S(1)}, u32[]{:S(2)}, u32[]{:S(2)}) collective-permute-start(bf16[128,2048]{1,0:T(8,128)(2,1)} %refs_4_.1), channel_id=1, source_target_pairs={{0,1},{1,0},{2,3},{3,2},{4,5},{5,4},{6,7},{7,6},{8,9},{9,8},{10,11... | collective-permute-start | bytes 1572872 | tf_op jit(solution)/shard_map/ppermute | solution.py:416
  11.7 6.9 %collective-permute-start.6 = (s16[2,16,3200]{2,1,0:T(8,128)(2,1)S(1)}, s16[2,16,3200]{2,1,0:T(8,128)(2,1)S(1)}, u32[]{:S(2)}, u32[]{:S(2)}) collective-permute-start(s16[2,16,3200]{2,1,0:T(8,128)(2,1)S(1)} %collective-permute-done.4.refs_6_.refs_4_.refs_10_), channel_id=1, source_target_pairs={{0,2},{1,3},{4,0},{5,1},{8,4},{9,5},{12,8},{13,9},{14,12},{15,13},... | collective-permute-start | bytes 614408 | tf_op jit(solution)/shard_map/ppermute | solution.py:390
  13.4 6.4 %collective-permute-start.5 = (s16[2,16,3200]{2,1,0:T(8,128)(2,1)S(1)}, s16[2,16,3200]{2,1,0:T(8,128)(2,1)S(1)}, u32[]{:S(2)}, u32[]{:S(2)}) collective-permute-start(s16[2,16,3200]{2,1,0:T(8,128)(2,1)S(1)} %collective-permute-done.3.refs_5_.refs_3_.refs_9_), channel_id=1, source_target_pairs={{0,4},{1,5},{4,8},{5,9},{8,12},{9,13},{12,14},{13,15},{14,10},{15,... | collective-permute-start | bytes 614408 | tf_op jit(solution)/shard_map/ppermute | solution.py:390
  13.8 14.2 %copy-start.1 = (s16[2,16,3200]{2,1,0:T(8,128)(2,1)S(1)}, s16[2,16,3200]{2,1,0:T(8,128)(2,1)}, u32[]{:S(2)}) copy-start(s16[2,16,3200]{2,1,0:T(8,128)(2,1)} %get-tuple-element.52.refs_4_.refs_2_.refs_8_) | copy-start | bytes 614404
  19.8 5.8 %collective-permute-start.7 = (s16[2,16,3200]{2,1,0:T(8,128)(2,1)S(1)}, s16[2,16,3200]{2,1,0:T(8,128)(2,1)S(1)}, u32[]{:S(2)}, u32[]{:S(2)}) collective-permute-start(s16[2,16,3200]{2,1,0:T(8,128)(2,1)S(1)} %get-tuple-element.53.refs_7_.refs_5_.refs_11_), channel_id=1, source_target_pairs={{0,4},{1,5},{4,8},{5,9},{8,12},{9,13},{12,14},{13,15},{14,10},{15,... | collective-permute-start | bytes 614408 | tf_op jit(solution)/shard_map/ppermute | solution.py:390
  20.4 5.9 %collective-permute-start.8 = (s16[2,16,3200]{2,1,0:T(8,128)(2,1)S(1)}, s16[2,16,3200]{2,1,0:T(8,128)(2,1)S(1)}, u32[]{:S(2)}, u32[]{:S(2)}) collective-permute-start(s16[2,16,3200]{2,1,0:T(8,128)(2,1)S(1)} %get-tuple-element.54.refs_6_.refs_5_.refs_12_), channel_id=1, source_target_pairs={{0,2},{1,3},{4,0},{5,1},{8,4},{9,5},{12,8},{13,9},{14,12},{15,13},... | collective-permute-start | bytes 614408 | tf_op jit(solution)/shard_map/ppermute | solution.py:390
  25.6 4.7 %collective-permute-start.9 = (s16[1,16,3200]{2,1,0:T(8,128)(2,1)S(1)}, s16[1,16,3200]{2,1,0:T(8,128)(2,1)S(1)}, u32[]{:S(2)}, u32[]{:S(2)}) collective-permute-start(s16[1,16,3200]{2,1,0:T(8,128)(2,1)S(1)} %slice.8), channel_id=1, source_target_pairs={{0,4},{1,5},{4,8},{5,9},{8,12},{9,13},{12,14},{13,15},{14,10},{15,... | collective-permute-start | bytes 307208 | tf_op jit(solution)/shard_map/ppermute | solution.py:390
  26.4 4.9 %collective-permute-start.11 = (s16[1,16,3200]{2,1,0:T(8,128)(2,1)S(1)}, s16[1,16,3200]{2,1,0:T(8,128)(2,1)S(1)}, u32[]{:S(2)}, u32[]{:S(2)}) collective-permute-start(s16[1,16,3200]{2,1,0:T(8,128)(2,1)S(1)} %slice.9), channel_id=1, source_target_pairs={{0,2},{1,3},{4,0},{5,1},{8,4},{9,5},{12,8},{13,9},{14,12},{15,13},... | collective-permute-start | bytes 307208 | tf_op jit(solution)/shard_map/ppermute | solution.py:390
  30.9 2.3 %collective-permute-start.10 = (f32[8,128]{1,0:T(8,128)S(1)}, f32[8,128]{1,0:T(8,128)S(1)}, u32[]{:S(2)}, u32[]{:S(2)}) collective-permute-start(f32[8,128]{1,0:T(8,128)S(1)} %shard_map.151.refs_0_.refs_4_), channel_id=1, source_target_pairs={{0,1},{1,0},{2,3},{3,2},{4,5},{5,4},{6,7},{7,6},{8,9},{9,8},{10,11... | collective-permute-start | bytes 12296 | tf_op jit(solution)/shard_map/ppermute | solution.py:416
  35.6 5.7 %collective-permute-start.12 = (bf16[256,2048]{1,0:T(8,128)(2,1)S(1)}, bf16[256,2048]{1,0:T(8,128)(2,1)S(1)}, u32[]{:S(2)}, u32[]{:S(2)}) collective-permute-start(bf16[256,2048]{1,0:T(8,128)(2,1)S(1)} %get-tuple-element.63), channel_id=1, source_target_pairs={{0,1},{1,0},{2,3},{3,2},{4,5},{5,4},{6,7},{7,6},{8,9},{9,8},{10,11... | collective-permute-start | bytes 3145736 | tf_op jit(solution)/shard_map/ppermute | solution.py:416
  39.9 7.3 %collective-permute-start.13 = (s16[2,16,3200]{2,1,0:T(8,128)(2,1)S(1)}, s16[2,16,3200]{2,1,0:T(8,128)(2,1)S(1)}, u32[]{:S(2)}, u32[]{:S(2)}) collective-permute-start(s16[2,16,3200]{2,1,0:T(8,128)(2,1)S(1)} %get-tuple-element.66), channel_id=1, source_target_pairs={{0,4},{1,5},{2,6},{3,7},{4,0},{5,1},{6,2},{7,3},{8,12},{9,13},{10,... | collective-permute-start | bytes 614408 | tf_op jit(solution)/shard_map/ppermute | solution.py:416
  44.5 7.2 %collective-permute-start.14 = (s16[2,16,3200]{2,1,0:T(8,128)(2,1)S(1)}, s16[2,16,3200]{2,1,0:T(8,128)(2,1)S(1)}, u32[]{:S(2)}, u32[]{:S(2)}) collective-permute-start(s16[2,16,3200]{2,1,0:T(8,128)(2,1)S(1)} %get-tuple-element.70), channel_id=1, source_target_pairs={{0,4},{1,5},{2,6},{3,7},{4,0},{5,1},{6,2},{7,3},{8,12},{9,13},{10,... | collective-permute-start | bytes 614408 | tf_op jit(solution)/shard_map/ppermute | solution.py:416
  45.3 8.2 %collective-permute-start.15 = (s16[2,16,3200]{2,1,0:T(8,128)(2,1)S(1)}, s16[2,16,3200]{2,1,0:T(8,128)(2,1)S(1)}, u32[]{:S(2)}, u32[]{:S(2)}) collective-permute-start(s16[2,16,3200]{2,1,0:T(8,128)(2,1)S(1)} %get-tuple-element.73), channel_id=1, source_target_pairs={{0,2},{1,3},{2,0},{3,1},{4,6},{5,7},{6,4},{7,5},{8,10},{9,11},{10,... | collective-permute-start | bytes 614408 | tf_op jit(solution)/shard_map/ppermute | solution.py:416
  47.4 8.0 %collective-permute-start.16 = (s16[16,3200]{1,0:T(8,128)(2,1)S(1)}, s16[16,3200]{1,0:T(8,128)(2,1)S(1)}, u32[]{:S(2)}, u32[]{:S(2)}) collective-permute-start(s16[16,3200]{1,0:T(8,128)(2,1)S(1)} %get-tuple-element.69.refs_0_), channel_id=1, source_target_pairs={{0,2},{1,3},{2,0},{3,1},{4,6},{5,7},{6,4},{7,5},{8,10},{9,11},{10,... | collective-permute-start | bytes 307208 | tf_op jit(solution)/shard_map/ppermute | solution.py:416
  48.9 14.6 %collective-permute-start.19 = (s16[2,16,3200]{2,1,0:T(8,128)(2,1)S(1)}, s16[2,16,3200]{2,1,0:T(8,128)(2,1)S(1)}, u32[]{:S(2)}, u32[]{:S(2)}) collective-permute-start(s16[2,16,3200]{2,1,0:T(8,128)(2,1)S(1)} %get-tuple-element.79), channel_id=1, source_target_pairs={{0,2},{1,3},{2,0},{3,1},{4,6},{5,7},{6,4},{7,5},{8,10},{9,11},{10,... | collective-permute-start | bytes 614408 | tf_op jit(solution)/shard_map/ppermute | solution.py:416
  51.9 8.8 %collective-permute-start.17 = (s16[16,3200]{1,0:T(8,128)(2,1)S(1)}, s16[16,3200]{1,0:T(8,128)(2,1)S(1)}, u32[]{:S(2)}, u32[]{:S(2)}) collective-permute-start(s16[16,3200]{1,0:T(8,128)(2,1)S(1)} %get-tuple-element.72.refs_0_), channel_id=1, source_target_pairs={{0,2},{1,3},{2,0},{3,1},{4,6},{5,7},{6,4},{7,5},{8,10},{9,11},{10,... | collective-permute-start | bytes 307208 | tf_op jit(solution)/shard_map/ppermute | solution.py:416
  53.7 9.8 %collective-permute-start.18 = (s16[16,3200]{1,0:T(8,128)(2,1)S(1)}, s16[16,3200]{1,0:T(8,128)(2,1)S(1)}, u32[]{:S(2)}, u32[]{:S(2)}) collective-permute-start(s16[16,3200]{1,0:T(8,128)(2,1)S(1)} %get-tuple-element.78), channel_id=1, source_target_pairs={{0,4},{1,5},{2,6},{3,7},{4,0},{5,1},{6,2},{7,3},{8,12},{9,13},{10,... | collective-permute-start | bytes 307208 | tf_op jit(solution)/shard_map/ppermute | solution.py:416
  55.6 9.8 %collective-permute-start.20 = (s16[16,3200]{1,0:T(8,128)(2,1)S(1)}, s16[16,3200]{1,0:T(8,128)(2,1)S(1)}, u32[]{:S(2)}, u32[]{:S(2)}) collective-permute-start(s16[16,3200]{1,0:T(8,128)(2,1)S(1)} %shard_map.159.refs_0_), channel_id=1, source_target_pairs={{0,8},{1,9},{2,10},{3,11},{4,12},{5,13},{6,14},{7,15},{8,0},{9,1},... | collective-permute-start | bytes 307208 | tf_op jit(solution)/shard_map/ppermute | solution.py:416
  60.9 6.1 %collective-permute-start.22 = (s16[16,3200]{1,0:T(8,128)(2,1)S(1)}, s16[16,3200]{1,0:T(8,128)(2,1)S(1)}, u32[]{:S(2)}, u32[]{:S(2)}) collective-permute-start(s16[16,3200]{1,0:T(8,128)(2,1)S(1)} %shard_map.160.refs_0_), channel_id=1, source_target_pairs={{0,8},{1,9},{2,10},{3,11},{4,12},{5,13},{6,14},{7,15},{8,0},{9,1},... | collective-permute-start | bytes 307208 | tf_op jit(solution)/shard_map/ppermute | solution.py:416
  63.8 4.7 %collective-permute-start.21 = (s16[16,3200]{1,0:T(8,128)(2,1)S(1)}, s16[16,3200]{1,0:T(8,128)(2,1)S(1)}, u32[]{:S(2)}, u32[]{:S(2)}) collective-permute-start(s16[16,3200]{1,0:T(8,128)(2,1)S(1)} %get-tuple-element.81), channel_id=1, source_target_pairs={{0,4},{1,5},{2,6},{3,7},{4,0},{5,1},{6,2},{7,3},{8,12},{9,13},{10,... | collective-permute-start | bytes 307208 | tf_op jit(solution)/shard_map/ppermute | solution.py:416
  (4 other events, 25.0 us)

commit v16 on v15

--- a/solution.py
+++ b/solution.py
@@ -246,7 +246,7 @@
     return both[:middle] + both[middle:]
 
 
-def put_chunks(keep_ref, near_ref, chunk_ref, far_ref, down, up):
+def put_chunks(keep_ref, near_ref, chunk_ref, far_ref, step, down, up):
     rank = keep_ref.shape[1]
     rows = down.shape[0] // rank // 2
 
@@ -255,8 +255,8 @@
         return down[start : start + rank], up[start : start + rank]
 
     for place in range(2):
-        keep_ref[place] = jnp.concatenate(slot(place), axis=1)
-        near_ref[place] = encode(*slot(rows + place))
+        keep_ref[place] = jnp.concatenate(slot(place * step), axis=1)
+        near_ref[place] = encode(*slot(rows + 1 - step + place * step))
         chunk_ref[place] = jnp.concatenate(slot(place * rows + 2), axis=1)
         far_ref[place] = encode(*slot(place * rows + 3))
 
@@ -291,11 +291,12 @@
     down = dot(left_ref[0], own_ref[...], 0, 0) + dot(left_ref[1], other_ref[...], 0, 0)
     up = add_halves(dot(jnp.concatenate(halves(weighted_ref[...]), axis=1), gradient, 0, 0))
     up_ref[...] = up[:wide]
-    put_chunks(keep_ref, near_ref, chunk_ref, far_ref, add_halves(down), up[wide:])
+    put_chunks(keep_ref, near_ref, chunk_ref, far_ref, 1, add_halves(down), up[wide:])
 
 
 def curvature_kernel(
     top,
+    slots,
     small_ref,
     same_ref,
     mask_ref,
@@ -330,13 +331,10 @@
     down = dot(left_ref[0], own_ref[...], 0, 0) + dot(left_ref[1], other_ref[...], 0, 0)
     weighted_u = halves(weighted_ref[:, wide:])
     up = add_halves(dot(jnp.concatenate(weighted_u, axis=1), resid[0], 0, 0)) + dot(weighted_u[0], resid[1], 0, 0)
-    put_chunks(keep_ref, near_ref, chunk_ref, far_ref, add_halves(down), up_ref[...] + up)
-
-
-def pair_kernel(hidden_width, arrived_ref, chunk_ref, *refs):
-    passing, (across_ref, keep_ref) = (refs[:1], refs[1:3]) if len(refs) == 4 else ((), refs)
-    for near_ref in passing:
-        refs[3][...] = near_ref[...]
+    put_chunks(keep_ref, near_ref, chunk_ref, far_ref, slots // 2, add_halves(down), up_ref[...] + up)
+
+
+def pair_kernel(hidden_width, arrived_ref, chunk_ref, across_ref, keep_ref):
     for x in range(2):
         down, up = decode(arrived_ref[x], hidden_width)
         down, up = chunk_ref[x, :, :hidden_width] + down, chunk_ref[x, :, hidden_width:] + up
@@ -352,10 +350,10 @@
 
 
 def near_kernel(hidden_width, arrived_ref, keep_ref, onward_ref, total_ref):
-    for z in range(2):
-        down, up = decode(arrived_ref[z], hidden_width)
-        down, up = keep_ref[z, :, :hidden_width] + down, keep_ref[z, :, hidden_width:] + up
-        if z == 0:
+    for place in range(2):
+        down, up = decode(arrived_ref[place], hidden_width)
+        down, up = keep_ref[place, :, :hidden_width] + down, keep_ref[place, :, hidden_width:] + up
+        if place == 0:
             total_ref[...] = jnp.concatenate([down, up], axis=1)
         else:
             onward_ref[...] = encode(down, up)
@@ -571,7 +569,7 @@
     )
     gradient_far = exchange(gradient_far, 4)
     curvature_keep, curvature_near, curvature_chunk, curvature_far, gradient_near = call(
-        functools.partial(curvature_kernel, top),
+        functools.partial(curvature_kernel, top, slots),
         down_multiplies + 6 * up_multiplies,
         chunks + [(gradient_near.shape, i16)],
         small_columns,
@@ -602,25 +600,20 @@
     curvature_far = exchange(curvature_far, 4)
     gradient_near = exchange(gradient_near, 2)
     pair = [(one_coded, i16), (one, f32)]
-    gradient_across, gradient_pair, curvature_near = hop_call(
-        pair_kernel,
-        pair + [(curvature_near.shape, i16)],
-        gradient_far,
-        gradient_chunk,
-        curvature_near,
-        after=[curvature_keep],
-    )
-    curvature_near = exchange(curvature_near, 2)
+    gradient_across, gradient_pair = hop_call(
+        pair_kernel, pair, gradient_far, gradient_chunk, after=[curvature_keep]
+    )
     curvature_across, curvature_pair = hop_call(
         pair_kernel, pair, curvature_far, curvature_chunk, after=[gradient_across]
     )
+    curvature_near = exchange(curvature_near, 4)
     near = [(one_coded, i16), (one, f32)]
     gradient_onward, gradient_total = hop_call(
         near_kernel, near, gradient_near, gradient_keep, after=[curvature_across]
     )
     gradient_onward = exchange(gradient_onward, 4)
     (gradient_beyond,) = hop_call(
-        far_kernel, [(one_coded, i16)], exchange(gradient_across, 2), gradient_pair, after=[gradient_total]
+        far_kernel, [(one_coded, i16)], exchange(gradient_across, 2), gradient_pair, after=[gradient_total, curvature_near]
     )
     (curvature_beyond,) = hop_call(
         far_kernel, [(one_coded, i16)], exchange(curvature_across, 2), curvature_pair, after=[gradient_beyond]
@@ -641,7 +634,7 @@
         [((rank, hidden_width), f32), ((rank, model_width), f32)] * 2,
         gradient_total,
         curvature_total,
-        exchange(curvature_onward, 4),
+        exchange(curvature_onward, 2),
         exchange(curvature_beyond, 8),
     )
     return down_gradient.T[None], up_gradient[None], curvature_down.T[None], curvature_up[None]

time: 69.6 us -> 69.7 us (level)
  waiting for transfers between devices: 19.9 us -> 22.2 us
  starting transfers between devices: 26 us -> 23.9 us
    ppermute x15, waiting for transfers between devices: 8.54 us -> 10.8 us  [exchange(): lax.ppermute(value, 'expert', [(device, device ^ mask) for device in rang...]
    ppermute x15, starting transfers between devices: 16.9 us -> 14.7 us  [exchange(): lax.ppermute(value, 'expert', [(device, device ^ mask) for device in rang...]
  transfers between devices with their start and end apart: 23 -> 23, of which waited for: 12 -> 11; matrix products, arithmetic and copies ran while one was open for 2% -> 2% of each run, Pallas kernels for 25% -> 25%
where the time goes in v16:
time: 69.7 us; the launch traced here: 69.4 us
  starting transfers between devices  23.9 us (34%)
  waiting for transfers between devices  22.2 us (32%)
  Pallas kernels  20.3 us (29%)
  other arithmetic  1.43 us (2%)
  local copies, waits for them, and re-layouts  0.85 us (1%)
  between operations  0.83 us (1%)
    pallas_call x17, Pallas kernels, call(): pl.pallas_call(lambda *refs: kernel(*refs[len(after):]), out_shape=[jax.S...  20.3 us
    ppermute x15, starting transfers between devices, exchange(): lax.ppermute(value, 'expert', [(device, device ^ mask) for device in rang...  14.7 us
    ppermute x8, waiting for transfers between devices, shift(): return lax.ppermute(value, 'expert', pairs)  11.3 us
    ppermute x15, waiting for transfers between devices, exchange(): lax.ppermute(value, 'expert', [(device, device ^ mask) for device in rang...  10.8 us
    ppermute x8, starting transfers between devices, shift(): return lax.ppermute(value, 'expert', pairs)  9.12 us
  transfers between devices with their start and end apart: 23, of which 11 were waited for; matrix products, arithmetic and copies ran while one was open for 2% of the time, Pallas kernels for 25%

profile of v16, /device:TPU:0, one launch (start us, length us, event | category | flops | bytes accessed | tf_op | source)
XLA Modules:
  0.0 69.4 jit_solution(9349619964249893109)
XLA Ops:
  1.2 2.0 %shard_map.147 = (s16[2,16,3200]{2,1,0:T(8,128)(2,1)}, f32[24,128]{1,0:T(8,128)}) custom-call(s32[8,128]{1,0:T(8,128)} %bitcast.32, bf16[8,128]{1,0:T(8,128)(2,1)} %bitcast.33, f32[1,128]{1,0:T(1,128)} %bitcast.34, f32[16,1024]{1,0:T(8,128)} %bitcast.30, f32[16,1024]{1,0:T(8,128)} %bitcast.31, f32[16,2048]{1,0:T(8,128)} %bitcast.28, f32[16,2048]{1,0:T(8,128)} %bitcast.29), custom_call_target="tpu_custom_call" | custom-call | flops 200000000 | bytes 1048576 | tf_op jit(solution)/shard_map/pallas_call | solution.py:451
  3.1 2.6 %collective-permute-start.4 = (s16[2,16,3200]{2,1,0:T(8,128)(2,1)}, s16[2,16,3200]{2,1,0:T(8,128)(2,1)S(1)}, u32[]{:S(2)}, u32[]{:S(2)}) collective-permute-start(s16[2,16,3200]{2,1,0:T(8,128)(2,1)} %get-tuple-element.51.refs_4_.refs_2_.refs_8_), channel_id=1, source_target_pairs={{0,2},{1,3},{4,0},{5,1},{8,4},{9,5},{12,8},{13,9},{14,12},{15,13},... | collective-permute-start | bytes 614408 | tf_op jit(solution)/shard_map/ppermute | solution.py:388
  7.7 4.0 %collective-permute-done.4.refs_6_.refs_4_.refs_10_ = s16[2,16,3200]{2,1,0:T(8,128)(2,1)S(1)} collective-permute-done((s16[2,16,3200]{2,1,0:T(8,128)(2,1)}, s16[2,16,3200]{2,1,0:T(8,128)(2,1)S(1)}, u32[]{:S(2)}, u32[]{:S(2)}) %collective-permute-start.4) | collective-permute-done | bytes 204832 | tf_op jit(solution)/shard_map/ppermute | solution.py:388
  11.7 1.7 %collective-permute-start.6 = (s16[2,16,3200]{2,1,0:T(8,128)(2,1)S(1)}, s16[2,16,3200]{2,1,0:T(8,128)(2,1)S(1)}, u32[]{:S(2)}, u32[]{:S(2)}) collective-permute-start(s16[2,16,3200]{2,1,0:T(8,128)(2,1)S(1)} %collective-permute-done.4.refs_6_.refs_4_.refs_10_), channel_id=1, source_target_pairs={{0,2},{1,3},{4,0},{5,1},{8,4},{9,5},{12,8},{13,9},{14,12},{15,13},... | collective-permute-start | bytes 614408 | tf_op jit(solution)/shard_map/ppermute | solution.py:388
  14.6 2.2 %shard_map.148 = (f32[256,24]{1,0:T(8,128)S(1)}, f32[2,128,128]{2,1,0:T(8,128)S(1)}, f32[2,128,128]{2,1,0:T(8,128)S(1)}, bf16[1024,128]{1,0:T(8,128)(2,1)S(1)}, ...) custom-call(s32[25]{0:T(128)S(1)} %pad_add_fusion.refs_0_.refs_1_, ...), custom_call_target="tpu_custom_call" | custom-call | flops 2000000000 | bytes 1048576 | tf_op jit(solution)/shard_map/pallas_call | solution.py:451
  16.8 1.9 %collective-permute-done.6.refs_2_ = s16[2,16,3200]{2,1,0:T(8,128)(2,1)S(1)} collective-permute-done((s16[2,16,3200]{2,1,0:T(8,128)(2,1)S(1)}, s16[2,16,3200]{2,1,0:T(8,128)(2,1)S(1)}, u32[]{:S(2)}, u32[]{:S(2)}) %collective-permute-start.6) | collective-permute-done | bytes 204832 | tf_op jit(solution)/shard_map/ppermute | solution.py:388
  18.6 1.2 %collective-permute-done.5.refs_1_ = s16[2,16,3200]{2,1,0:T(8,128)(2,1)S(1)} collective-permute-done((s16[2,16,3200]{2,1,0:T(8,128)(2,1)S(1)}, s16[2,16,3200]{2,1,0:T(8,128)(2,1)S(1)}, u32[]{:S(2)}, u32[]{:S(2)}) %collective-permute-start.5) | collective-permute-done | bytes 204832 | tf_op jit(solution)/shard_map/ppermute | solution.py:388
  20.4 1.5 %collective-permute-start.8 = (s16[2,16,3200]{2,1,0:T(8,128)(2,1)S(1)}, s16[2,16,3200]{2,1,0:T(8,128)(2,1)S(1)}, u32[]{:S(2)}, u32[]{:S(2)}) collective-permute-start(s16[2,16,3200]{2,1,0:T(8,128)(2,1)S(1)} %get-tuple-element.53.refs_6_.refs_5_.refs_12_), channel_id=1, source_target_pairs={{0,2},{1,3},{4,0},{5,1},{8,4},{9,5},{12,8},{13,9},{14,12},{15,13},... | collective-permute-start | bytes 614408 | tf_op jit(solution)/shard_map/ppermute | solution.py:388
  21.9 3.7 %collective-permute-done.7.refs_7_.refs_6_.refs_13_ = s16[2,16,3200]{2,1,0:T(8,128)(2,1)S(1)} collective-permute-done((s16[2,16,3200]{2,1,0:T(8,128)(2,1)S(1)}, s16[2,16,3200]{2,1,0:T(8,128)(2,1)S(1)}, u32[]{:S(2)}, u32[]{:S(2)}) %collective-permute-start.7) | collective-permute-done | bytes 204832 | tf_op jit(solution)/shard_map/ppermute | solution.py:388
  26.4 1.7 %collective-permute-start.11 = (s16[1,16,3200]{2,1,0:T(8,128)(2,1)S(1)}, s16[1,16,3200]{2,1,0:T(8,128)(2,1)S(1)}, u32[]{:S(2)}, u32[]{:S(2)}) collective-permute-start(s16[1,16,3200]{2,1,0:T(8,128)(2,1)S(1)} %slice.9), channel_id=1, source_target_pairs={{0,2},{1,3},{4,0},{5,1},{8,4},{9,5},{12,8},{13,9},{14,12},{15,13},... | collective-permute-start | bytes 307208 | tf_op jit(solution)/shard_map/ppermute | solution.py:388
  28.0 2.0 %shard_map.150.refs_0_.refs_6_ = f32[256,128]{1,0:T(8,128)S(1)} custom-call(s32[25]{0:T(128)S(1)} %pad_add_fusion.refs_0_.refs_1_, f32[256,24]{1,0:T(8,128)S(1)} %get-tuple-element.45.refs_1_.refs_2_.refs_0_, bf16[1024,1024]{1,0:T(8,128)(2,1)S(1)} %bitcast.24, bf16[1024,1024]{1,0:T(8,128)(2,1)S(1)} %get-tuple-element.48.refs_3_.refs_4_, ...), custom_call_target="tpu_custom_call" | custom-call | flops 1073741824 | bytes 1048576 | tf_op jit(solution)/shard_map/pallas_call | solution.py:451
  31.3 2.0 %shard_map.152.refs_7_ = f32[256,128]{1,0:T(8,128)S(1)} custom-call(f32[8,128]{1,0:T(8,128)S(1)} %shard_map.151.refs_0_.refs_4_, s32[25]{0:T(128)S(1)} %pad_add_fusion.refs_0_.refs_1_, f32[256,24]{1,0:T(8,128)S(1)} %get-tuple-element.45.refs_1_.refs_2_.refs_0_, bf16[1024,1024]{1,0:T(8,128)(2,1)S(1)} %bitcast.25, ...), custom_call_target="tpu_custom_call" | custom-call | flops 1073741824 | bytes 1048576 | tf_op jit(solution)/shard_map/pallas_call | solution.py:451
  33.3 2.3 %shard_map.153 = (f32[256,128]{1,0:T(8,128)S(1)}, f32[256,256]{1,0:T(8,128)S(1)}, f32[256,2048]{1,0:T(8,128)S(1)}, bf16[256,2048]{1,0:T(8,128)(2,1)S(1)}, bf16[2...) custom-call(s32[25]{0:T(128)S(1)} %pad_add_fusion.refs_0_.refs_1_, ...), custom_call_target="tpu_custom_call" | custom-call | flops 805306368 | bytes 1048576 | tf_op jit(solution)/shard_map/pallas_call | solution.py:451
  35.9 4.0 %shard_map.154 = (f32[2,16,3072]{2,1,0:T(8,128)S(1)}, s16[2,16,3200]{2,1,0:T(8,128)(2,1)S(1)}, f32[2,16,3072]{2,1,0:T(8,128)S(1)}, s16[2,16,3200]{2,1,0:T(8,128)...) custom-call(bf16[1024,128]{1,0:T(8,128)(2,1)S(1)} %get-tuple-element.46.refs_0_.refs_1_, ...), custom_call_target="tpu_custom_call" | custom-call | flops 2147483648 | bytes 1048576 | tf_op jit(solution)/shard_map/pallas_call | solution.py:451
  39.9 1.4 %collective-permute-start.13 = (s16[2,16,3200]{2,1,0:T(8,128)(2,1)S(1)}, s16[2,16,3200]{2,1,0:T(8,128)(2,1)S(1)}, u32[]{:S(2)}, u32[]{:S(2)}) collective-permute-start(s16[2,16,3200]{2,1,0:T(8,128)(2,1)S(1)} %get-tuple-element.65), channel_id=1, source_target_pairs={{0,4},{1,5},{2,6},{3,7},{4,0},{5,1},{6,2},{7,3},{8,12},{9,13},{10,... | collective-permute-start | bytes 614408 | tf_op jit(solution)/shard_map/ppermute | solution.py:414
  41.2 3.2 %shard_map.155 = (f32[2,16,3072]{2,1,0:T(8,128)S(1)}, s16[2,16,3200]{2,1,0:T(8,128)(2,1)S(1)}, f32[2,16,3072]{2,1,0:T(8,128)S(1)}, s16[2,16,3200]{2,1,0:T(8,128)(2,1)S(1)}, s16[2,16,3200]{2,1,0:T(8,128)(2,1)S(1)}) custom-call(f32[256,24]{1,0:T(8,128)S(1)} %get-tuple-element.45.refs_1_.refs_2_.refs_0_, ...), custom_call_target="tpu_custom_call" | custom-call | flops 1879048192 | bytes 1048576 | tf_op jit(solution)/shard_map/pallas_call | solution.py:451
  45.2 1.6 %collective-permute-start.15 = (s16[2,16,3200]{2,1,0:T(8,128)(2,1)S(1)}, s16[2,16,3200]{2,1,0:T(8,128)(2,1)S(1)}, u32[]{:S(2)}, u32[]{:S(2)}) collective-permute-start(s16[2,16,3200]{2,1,0:T(8,128)(2,1)S(1)} %get-tuple-element.71), channel_id=1, source_target_pairs={{0,2},{1,3},{2,0},{3,1},{4,6},{5,7},{6,4},{7,5},{8,10},{9,11},{10,... | collective-permute-start | bytes 614408 | tf_op jit(solution)/shard_map/ppermute | solution.py:414
  46.8 1.6 %collective-permute-start.16 = (s16[2,16,3200]{2,1,0:T(8,128)(2,1)S(1)}, s16[2,16,3200]{2,1,0:T(8,128)(2,1)S(1)}, u32[]{:S(2)}, u32[]{:S(2)}) collective-permute-start(s16[2,16,3200]{2,1,0:T(8,128)(2,1)S(1)} %get-tuple-element.74), channel_id=1, source_target_pairs={{0,4},{1,5},{2,6},{3,7},{4,0},{5,1},{6,2},{7,3},{8,12},{9,13},{10,... | collective-permute-start | bytes 614408 | tf_op jit(solution)/shard_map/ppermute | solution.py:414
  48.9 3.5 %collective-permute-done.14.refs_1_ = s16[2,16,3200]{2,1,0:T(8,128)(2,1)S(1)} collective-permute-done((s16[2,16,3200]{2,1,0:T(8,128)(2,1)S(1)}, s16[2,16,3200]{2,1,0:T(8,128)(2,1)S(1)}, u32[]{:S(2)}, u32[]{:S(2)}) %collective-permute-start.14) | collective-permute-done | bytes 204832 | tf_op jit(solution)/shard_map/ppermute | solution.py:414
  52.7 2.0 %collective-permute-start.18 = (s16[16,3200]{1,0:T(8,128)(2,1)S(1)}, s16[16,3200]{1,0:T(8,128)(2,1)S(1)}, u32[]{:S(2)}, u32[]{:S(2)}) collective-permute-start(s16[16,3200]{1,0:T(8,128)(2,1)S(1)} %get-tuple-element.70.refs_0_), channel_id=1, source_target_pairs={{0,2},{1,3},{2,0},{3,1},{4,6},{5,7},{6,4},{7,5},{8,10},{9,11},{10,... | collective-permute-start | bytes 307208 | tf_op jit(solution)/shard_map/ppermute | solution.py:414
  54.8 1.1 %collective-permute-start.19 = (s16[16,3200]{1,0:T(8,128)(2,1)S(1)}, s16[16,3200]{1,0:T(8,128)(2,1)S(1)}, u32[]{:S(2)}, u32[]{:S(2)}) collective-permute-start(s16[16,3200]{1,0:T(8,128)(2,1)S(1)} %get-tuple-element.77), channel_id=1, source_target_pairs={{0,4},{1,5},{2,6},{3,7},{4,0},{5,1},{6,2},{7,3},{8,12},{9,13},{10,... | collective-permute-start | bytes 307208 | tf_op jit(solution)/shard_map/ppermute | solution.py:414
  57.0 2.5 %collective-permute-start.20 = (s16[16,3200]{1,0:T(8,128)(2,1)S(1)}, s16[16,3200]{1,0:T(8,128)(2,1)S(1)}, u32[]{:S(2)}, u32[]{:S(2)}) collective-permute-start(s16[16,3200]{1,0:T(8,128)(2,1)S(1)} %shard_map.159.refs_0_), channel_id=1, source_target_pairs={{0,8},{1,9},{2,10},{3,11},{4,12},{5,13},{6,14},{7,15},{8,0},{9,1},... | collective-permute-start | bytes 307208 | tf_op jit(solution)/shard_map/ppermute | solution.py:414
  60.9 1.6 %collective-permute-start.21 = (s16[16,3200]{1,0:T(8,128)(2,1)S(1)}, s16[16,3200]{1,0:T(8,128)(2,1)S(1)}, u32[]{:S(2)}, u32[]{:S(2)}) collective-permute-start(s16[16,3200]{1,0:T(8,128)(2,1)S(1)} %get-tuple-element.79), channel_id=1, source_target_pairs={{0,2},{1,3},{2,0},{3,1},{4,6},{5,7},{6,4},{7,5},{8,10},{9,11},{10,... | collective-permute-start | bytes 307208 | tf_op jit(solution)/shard_map/ppermute | solution.py:414
  62.5 5.0 %collective-permute-done.20.refs_3_ = s16[16,3200]{1,0:T(8,128)(2,1)S(1)} collective-permute-done((s16[16,3200]{1,0:T(8,128)(2,1)S(1)}, s16[16,3200]{1,0:T(8,128)(2,1)S(1)}, u32[]{:S(2)}, u32[]{:S(2)}) %collective-permute-start.20) | collective-permute-done | bytes 102432 | tf_op jit(solution)/shard_map/ppermute | solution.py:414
  (56 shorter events, 12.7 us)
Async XLA Ops:
  0.6 13.2 %collective-permute-start.1 = (bf16[1024,1024]{1,0:T(8,128)(2,1)}, bf16[1024,1024]{1,0:T(8,128)(2,1)S(1)}, u32[]{:S(2)}, u32[]{:S(2)}) collective-permute-start(bf16[1024,1024]{1,0:T(8,128)(2,1)} %bitcast.23), channel_id=1, source_target_pairs={{0,1},{1,0},{2,3},{3,2},{4,5},{5,4},{6,7},{7,6},{8,9},{9,8},{10,11... | collective-permute-start | bytes 6291464 | tf_op jit(solution)/shard_map/ppermute | solution.py:414
  3.1 8.6 %collective-permute-start.4 = (s16[2,16,3200]{2,1,0:T(8,128)(2,1)}, s16[2,16,3200]{2,1,0:T(8,128)(2,1)S(1)}, u32[]{:S(2)}, u32[]{:S(2)}) collective-permute-start(s16[2,16,3200]{2,1,0:T(8,128)(2,1)} %get-tuple-element.51.refs_4_.refs_2_.refs_8_), channel_id=1, source_target_pairs={{0,2},{1,3},{4,0},{5,1},{8,4},{9,5},{12,8},{13,9},{14,12},{15,13},... | collective-permute-start | bytes 614408 | tf_op jit(solution)/shard_map/ppermute | solution.py:388
  5.7 7.7 %collective-permute-start.3 = (s16[2,16,3200]{2,1,0:T(8,128)(2,1)}, s16[2,16,3200]{2,1,0:T(8,128)(2,1)S(1)}, u32[]{:S(2)}, u32[]{:S(2)}) collective-permute-start(s16[2,16,3200]{2,1,0:T(8,128)(2,1)} %get-tuple-element.51.refs_4_.refs_2_.refs_8_), channel_id=1, source_target_pairs={{0,4},{1,5},{4,8},{5,9},{8,12},{9,13},{12,14},{13,15},{14,10},{15,... | collective-permute-start | bytes 614408 | tf_op jit(solution)/shard_map/ppermute | solution.py:388
  5.8 8.0 %collective-permute-start = (f32[24,128]{1,0:T(8,128)}, f32[24,128]{1,0:T(8,128)S(1)}, u32[]{:S(2)}, u32[]{:S(2)}) collective-permute-start(f32[24,128]{1,0:T(8,128)} %get-tuple-element.44.refs_1_), channel_id=1, source_target_pairs={{0,1},{1,0},{2,3},{3,2},{4,5},{5,4},{6,7},{7,6},{8,9},{9,8},{10,11... | collective-permute-start | bytes 36872 | tf_op jit(solution)/shard_map/ppermute | solution.py:414
  6.0 7.8 %collective-permute-start.2 = (bf16[128,2048]{1,0:T(8,128)(2,1)}, bf16[128,2048]{1,0:T(8,128)(2,1)S(1)}, u32[]{:S(2)}, u32[]{:S(2)}) collective-permute-start(bf16[128,2048]{1,0:T(8,128)(2,1)} %refs_4_.1), channel_id=1, source_target_pairs={{0,1},{1,0},{2,3},{3,2},{4,5},{5,4},{6,7},{7,6},{8,9},{9,8},{10,11... | collective-permute-start | bytes 1572872 | tf_op jit(solution)/shard_map/ppermute | solution.py:414
  11.7 6.9 %collective-permute-start.6 = (s16[2,16,3200]{2,1,0:T(8,128)(2,1)S(1)}, s16[2,16,3200]{2,1,0:T(8,128)(2,1)S(1)}, u32[]{:S(2)}, u32[]{:S(2)}) collective-permute-start(s16[2,16,3200]{2,1,0:T(8,128)(2,1)S(1)} %collective-permute-done.4.refs_6_.refs_4_.refs_10_), channel_id=1, source_target_pairs={{0,2},{1,3},{4,0},{5,1},{8,4},{9,5},{12,8},{13,9},{14,12},{15,13},... | collective-permute-start | bytes 614408 | tf_op jit(solution)/shard_map/ppermute | solution.py:388
  13.4 6.4 %collective-permute-start.5 = (s16[2,16,3200]{2,1,0:T(8,128)(2,1)S(1)}, s16[2,16,3200]{2,1,0:T(8,128)(2,1)S(1)}, u32[]{:S(2)}, u32[]{:S(2)}) collective-permute-start(s16[2,16,3200]{2,1,0:T(8,128)(2,1)S(1)} %collective-permute-done.3.refs_5_.refs_3_.refs_9_), channel_id=1, source_target_pairs={{0,4},{1,5},{4,8},{5,9},{8,12},{9,13},{12,14},{13,15},{14,10},{15,... | collective-permute-start | bytes 614408 | tf_op jit(solution)/shard_map/ppermute | solution.py:388
  13.8 14.2 %copy-start.1 = (s16[2,16,3200]{2,1,0:T(8,128)(2,1)S(1)}, s16[2,16,3200]{2,1,0:T(8,128)(2,1)}, u32[]{:S(2)}) copy-start(s16[2,16,3200]{2,1,0:T(8,128)(2,1)} %get-tuple-element.51.refs_4_.refs_2_.refs_8_) | copy-start | bytes 614404
  19.8 5.8 %collective-permute-start.7 = (s16[2,16,3200]{2,1,0:T(8,128)(2,1)S(1)}, s16[2,16,3200]{2,1,0:T(8,128)(2,1)S(1)}, u32[]{:S(2)}, u32[]{:S(2)}) collective-permute-start(s16[2,16,3200]{2,1,0:T(8,128)(2,1)S(1)} %get-tuple-element.52.refs_7_.refs_5_.refs_11_), channel_id=1, source_target_pairs={{0,4},{1,5},{4,8},{5,9},{8,12},{9,13},{12,14},{13,15},{14,10},{15,... | collective-permute-start | bytes 614408 | tf_op jit(solution)/shard_map/ppermute | solution.py:388
  20.4 5.9 %collective-permute-start.8 = (s16[2,16,3200]{2,1,0:T(8,128)(2,1)S(1)}, s16[2,16,3200]{2,1,0:T(8,128)(2,1)S(1)}, u32[]{:S(2)}, u32[]{:S(2)}) collective-permute-start(s16[2,16,3200]{2,1,0:T(8,128)(2,1)S(1)} %get-tuple-element.53.refs_6_.refs_5_.refs_12_), channel_id=1, source_target_pairs={{0,2},{1,3},{4,0},{5,1},{8,4},{9,5},{12,8},{13,9},{14,12},{15,13},... | collective-permute-start | bytes 614408 | tf_op jit(solution)/shard_map/ppermute | solution.py:388
  25.6 4.7 %collective-permute-start.9 = (s16[1,16,3200]{2,1,0:T(8,128)(2,1)S(1)}, s16[1,16,3200]{2,1,0:T(8,128)(2,1)S(1)}, u32[]{:S(2)}, u32[]{:S(2)}) collective-permute-start(s16[1,16,3200]{2,1,0:T(8,128)(2,1)S(1)} %slice.8), channel_id=1, source_target_pairs={{0,4},{1,5},{4,8},{5,9},{8,12},{9,13},{12,14},{13,15},{14,10},{15,... | collective-permute-start | bytes 307208 | tf_op jit(solution)/shard_map/ppermute | solution.py:388
  26.4 4.9 %collective-permute-start.11 = (s16[1,16,3200]{2,1,0:T(8,128)(2,1)S(1)}, s16[1,16,3200]{2,1,0:T(8,128)(2,1)S(1)}, u32[]{:S(2)}, u32[]{:S(2)}) collective-permute-start(s16[1,16,3200]{2,1,0:T(8,128)(2,1)S(1)} %slice.9), channel_id=1, source_target_pairs={{0,2},{1,3},{4,0},{5,1},{8,4},{9,5},{12,8},{13,9},{14,12},{15,13},... | collective-permute-start | bytes 307208 | tf_op jit(solution)/shard_map/ppermute | solution.py:388
  30.9 2.3 %collective-permute-start.10 = (f32[8,128]{1,0:T(8,128)S(1)}, f32[8,128]{1,0:T(8,128)S(1)}, u32[]{:S(2)}, u32[]{:S(2)}) collective-permute-start(f32[8,128]{1,0:T(8,128)S(1)} %shard_map.151.refs_0_.refs_4_), channel_id=1, source_target_pairs={{0,1},{1,0},{2,3},{3,2},{4,5},{5,4},{6,7},{7,6},{8,9},{9,8},{10,11... | collective-permute-start | bytes 12296 | tf_op jit(solution)/shard_map/ppermute | solution.py:414
  35.6 5.7 %collective-permute-start.12 = (bf16[256,2048]{1,0:T(8,128)(2,1)S(1)}, bf16[256,2048]{1,0:T(8,128)(2,1)S(1)}, u32[]{:S(2)}, u32[]{:S(2)}) collective-permute-start(bf16[256,2048]{1,0:T(8,128)(2,1)S(1)} %get-tuple-element.62), channel_id=1, source_target_pairs={{0,1},{1,0},{2,3},{3,2},{4,5},{5,4},{6,7},{7,6},{8,9},{9,8},{10,11... | collective-permute-start | bytes 3145736 | tf_op jit(solution)/shard_map/ppermute | solution.py:414
  39.9 8.5 %collective-permute-start.13 = (s16[2,16,3200]{2,1,0:T(8,128)(2,1)S(1)}, s16[2,16,3200]{2,1,0:T(8,128)(2,1)S(1)}, u32[]{:S(2)}, u32[]{:S(2)}) collective-permute-start(s16[2,16,3200]{2,1,0:T(8,128)(2,1)S(1)} %get-tuple-element.65), channel_id=1, source_target_pairs={{0,4},{1,5},{2,6},{3,7},{4,0},{5,1},{6,2},{7,3},{8,12},{9,13},{10,... | collective-permute-start | bytes 614408 | tf_op jit(solution)/shard_map/ppermute | solution.py:414
  44.5 8.0 %collective-permute-start.14 = (s16[2,16,3200]{2,1,0:T(8,128)(2,1)S(1)}, s16[2,16,3200]{2,1,0:T(8,128)(2,1)S(1)}, u32[]{:S(2)}, u32[]{:S(2)}) collective-permute-start(s16[2,16,3200]{2,1,0:T(8,128)(2,1)S(1)} %get-tuple-element.68), channel_id=1, source_target_pairs={{0,4},{1,5},{2,6},{3,7},{4,0},{5,1},{6,2},{7,3},{8,12},{9,13},{10,... | collective-permute-start | bytes 614408 | tf_op jit(solution)/shard_map/ppermute | solution.py:414
  45.2 9.4 %collective-permute-start.15 = (s16[2,16,3200]{2,1,0:T(8,128)(2,1)S(1)}, s16[2,16,3200]{2,1,0:T(8,128)(2,1)S(1)}, u32[]{:S(2)}, u32[]{:S(2)}) collective-permute-start(s16[2,16,3200]{2,1,0:T(8,128)(2,1)S(1)} %get-tuple-element.71), channel_id=1, source_target_pairs={{0,2},{1,3},{2,0},{3,1},{4,6},{5,7},{6,4},{7,5},{8,10},{9,11},{10,... | collective-permute-start | bytes 614408 | tf_op jit(solution)/shard_map/ppermute | solution.py:414
  46.8 10.0 %collective-permute-start.16 = (s16[2,16,3200]{2,1,0:T(8,128)(2,1)S(1)}, s16[2,16,3200]{2,1,0:T(8,128)(2,1)S(1)}, u32[]{:S(2)}, u32[]{:S(2)}) collective-permute-start(s16[2,16,3200]{2,1,0:T(8,128)(2,1)S(1)} %get-tuple-element.74), channel_id=1, source_target_pairs={{0,4},{1,5},{2,6},{3,7},{4,0},{5,1},{6,2},{7,3},{8,12},{9,13},{10,... | collective-permute-start | bytes 614408 | tf_op jit(solution)/shard_map/ppermute | solution.py:414
  48.6 7.4 %collective-permute-start.17 = (s16[16,3200]{1,0:T(8,128)(2,1)S(1)}, s16[16,3200]{1,0:T(8,128)(2,1)S(1)}, u32[]{:S(2)}, u32[]{:S(2)}) collective-permute-start(s16[16,3200]{1,0:T(8,128)(2,1)S(1)} %get-tuple-element.67.refs_0_), channel_id=1, source_target_pairs={{0,2},{1,3},{2,0},{3,1},{4,6},{5,7},{6,4},{7,5},{8,10},{9,11},{10,... | collective-permute-start | bytes 307208 | tf_op jit(solution)/shard_map/ppermute | solution.py:414
  52.7 6.9 %collective-permute-start.18 = (s16[16,3200]{1,0:T(8,128)(2,1)S(1)}, s16[16,3200]{1,0:T(8,128)(2,1)S(1)}, u32[]{:S(2)}, u32[]{:S(2)}) collective-permute-start(s16[16,3200]{1,0:T(8,128)(2,1)S(1)} %get-tuple-element.70.refs_0_), channel_id=1, source_target_pairs={{0,2},{1,3},{2,0},{3,1},{4,6},{5,7},{6,4},{7,5},{8,10},{9,11},{10,... | collective-permute-start | bytes 307208 | tf_op jit(solution)/shard_map/ppermute | solution.py:414
  54.8 5.8 %collective-permute-start.19 = (s16[16,3200]{1,0:T(8,128)(2,1)S(1)}, s16[16,3200]{1,0:T(8,128)(2,1)S(1)}, u32[]{:S(2)}, u32[]{:S(2)}) collective-permute-start(s16[16,3200]{1,0:T(8,128)(2,1)S(1)} %get-tuple-element.77), channel_id=1, source_target_pairs={{0,4},{1,5},{2,6},{3,7},{4,0},{5,1},{6,2},{7,3},{8,12},{9,13},{10,... | collective-permute-start | bytes 307208 | tf_op jit(solution)/shard_map/ppermute | solution.py:414
  57.0 10.4 %collective-permute-start.20 = (s16[16,3200]{1,0:T(8,128)(2,1)S(1)}, s16[16,3200]{1,0:T(8,128)(2,1)S(1)}, u32[]{:S(2)}, u32[]{:S(2)}) collective-permute-start(s16[16,3200]{1,0:T(8,128)(2,1)S(1)} %shard_map.159.refs_0_), channel_id=1, source_target_pairs={{0,8},{1,9},{2,10},{3,11},{4,12},{5,13},{6,14},{7,15},{8,0},{9,1},... | collective-permute-start | bytes 307208 | tf_op jit(solution)/shard_map/ppermute | solution.py:414
  59.8 8.9 %collective-permute-start.22 = (s16[16,3200]{1,0:T(8,128)(2,1)S(1)}, s16[16,3200]{1,0:T(8,128)(2,1)S(1)}, u32[]{:S(2)}, u32[]{:S(2)}) collective-permute-start(s16[16,3200]{1,0:T(8,128)(2,1)S(1)} %shard_map.160.refs_0_), channel_id=1, source_target_pairs={{0,8},{1,9},{2,10},{3,11},{4,12},{5,13},{6,14},{7,15},{8,0},{9,1},... | collective-permute-start | bytes 307208 | tf_op jit(solution)/shard_map/ppermute | solution.py:414
  60.9 6.7 %collective-permute-start.21 = (s16[16,3200]{1,0:T(8,128)(2,1)S(1)}, s16[16,3200]{1,0:T(8,128)(2,1)S(1)}, u32[]{:S(2)}, u32[]{:S(2)}) collective-permute-start(s16[16,3200]{1,0:T(8,128)(2,1)S(1)} %get-tuple-element.79), channel_id=1, source_target_pairs={{0,2},{1,3},{2,0},{3,1},{4,6},{5,7},{6,4},{7,5},{8,10},{9,11},{10,... | collective-permute-start | bytes 307208 | tf_op jit(solution)/shard_map/ppermute | solution.py:414
  (4 other events, 25.0 us)

commit v17 on v15

--- a/solution.py
+++ b/solution.py
@@ -309,15 +309,12 @@
     to_ref,
     tangent_ref,
     arrived_ref,
-    gradient_near_ref,
     keep_ref,
     near_ref,
     chunk_ref,
     far_ref,
-    onward_ref,
     left_ref,
 ):
-    onward_ref[...] = gradient_near_ref[...]
     _, _, curvature = token_columns(small_ref, top)
     tokens, wide = weight_ref.shape
     block = tokens // 2
@@ -352,10 +349,10 @@
 
 
 def near_kernel(hidden_width, arrived_ref, keep_ref, onward_ref, total_ref):
-    for z in range(2):
-        down, up = decode(arrived_ref[z], hidden_width)
-        down, up = keep_ref[z, :, :hidden_width] + down, keep_ref[z, :, hidden_width:] + up
-        if z == 0:
+    for place in range(2):
+        down, up = decode(arrived_ref[place], hidden_width)
+        down, up = keep_ref[place, :, :hidden_width] + down, keep_ref[place, :, hidden_width:] + up
+        if place == 0:
             total_ref[...] = jnp.concatenate([down, up], axis=1)
         else:
             onward_ref[...] = encode(down, up)
@@ -570,10 +567,11 @@
         scratch=left,
     )
     gradient_far = exchange(gradient_far, 4)
-    curvature_keep, curvature_near, curvature_chunk, curvature_far, gradient_near = call(
+    gradient_near = exchange(gradient_near, 2)
+    curvature_keep, curvature_near, curvature_chunk, curvature_far = call(
         functools.partial(curvature_kernel, top),
         down_multiplies + 6 * up_multiplies,
-        chunks + [(gradient_near.shape, i16)],
+        chunks,
         small_columns,
         same,
         mask,
@@ -587,7 +585,6 @@
         to,
         tangent,
         arrived,
-        gradient_near,
         scratch=left,
     )
 
@@ -600,7 +597,6 @@
         return call(functools.partial(kernel, hidden_width), hop, outs, *operands, after=after)
 
     curvature_far = exchange(curvature_far, 4)
-    gradient_near = exchange(gradient_near, 2)
     pair = [(one_coded, i16), (one, f32)]
     gradient_across, gradient_pair, curvature_near = hop_call(
         pair_kernel,
@@ -611,22 +607,22 @@
         after=[curvature_keep],
     )
     curvature_near = exchange(curvature_near, 2)
-    curvature_across, curvature_pair = hop_call(
-        pair_kernel, pair, curvature_far, curvature_chunk, after=[gradient_across]
-    )
     near = [(one_coded, i16), (one, f32)]
     gradient_onward, gradient_total = hop_call(
-        near_kernel, near, gradient_near, gradient_keep, after=[curvature_across]
+        near_kernel, near, gradient_near, gradient_keep, after=[gradient_across]
     )
     gradient_onward = exchange(gradient_onward, 4)
+    curvature_across, curvature_pair = hop_call(
+        pair_kernel, pair, curvature_far, curvature_chunk, after=[gradient_total]
+    )
     (gradient_beyond,) = hop_call(
-        far_kernel, [(one_coded, i16)], exchange(gradient_across, 2), gradient_pair, after=[gradient_total]
+        far_kernel, [(one_coded, i16)], exchange(gradient_across, 2), gradient_pair, after=[curvature_across, gradient_onward]
     )
     (curvature_beyond,) = hop_call(
         far_kernel, [(one_coded, i16)], exchange(curvature_across, 2), curvature_pair, after=[gradient_beyond]
     )
     curvature_onward, curvature_total = hop_call(
-        near_kernel, near, curvature_near, curvature_keep, after=[curvature_beyond, gradient_onward]
+        near_kernel, near, curvature_near, curvature_keep, after=[curvature_beyond]
     )
     (gradient_total,) = hop_call(
         add_kernel,

time: 69.6 us -> 68.6 us (0.986)
  starting transfers between devices: 26 us -> 25 us
    ppermute x15, starting transfers between devices: 16.9 us -> 15.9 us  [exchange(): lax.ppermute(value, 'expert', [(device, device ^ mask) for device in rang...]
where the time goes in v17:
time: 68.6 us; the launch traced here: 68.3 us
  starting transfers between devices  25 us (36%)
  Pallas kernels  20.3 us (30%)
  waiting for transfers between devices  20 us (29%)
  other arithmetic  1.43 us (2%)
  local copies, waits for them, and re-layouts  0.85 us (1%)
  between operations  0.82 us (1%)
    pallas_call x17, Pallas kernels, call(): pl.pallas_call(lambda *refs: kernel(*refs[len(after):]), out_shape=[jax.S...  20.3 us
    ppermute x15, starting transfers between devices, exchange(): lax.ppermute(value, 'expert', [(device, device ^ mask) for device in rang...  15.9 us
    ppermute x8, waiting for transfers between devices, shift(): return lax.ppermute(value, 'expert', pairs)  11.3 us
    ppermute x8, starting transfers between devices, shift(): return lax.ppermute(value, 'expert', pairs)  9.12 us
    ppermute x15, waiting for transfers between devices, exchange(): lax.ppermute(value, 'expert', [(device, device ^ mask) for device in rang...  8.62 us
  transfers between devices with their start and end apart: 23, of which 12 were waited for; matrix products, arithmetic and copies ran while one was open for 2% of the time, Pallas kernels for 25%

profile of v17, /device:TPU:0, one launch (start us, length us, event | category | flops | bytes accessed | tf_op | source)
XLA Modules:
  0.0 68.3 jit_solution(9203586437901708977)
XLA Ops:
  1.2 2.0 %shard_map.147 = (s16[2,16,3200]{2,1,0:T(8,128)(2,1)}, f32[24,128]{1,0:T(8,128)}) custom-call(s32[8,128]{1,0:T(8,128)} %bitcast.32, bf16[8,128]{1,0:T(8,128)(2,1)} %bitcast.33, f32[1,128]{1,0:T(1,128)} %bitcast.34, f32[16,1024]{1,0:T(8,128)} %bitcast.30, f32[16,1024]{1,0:T(8,128)} %bitcast.31, f32[16,2048]{1,0:T(8,128)} %bitcast.28, f32[16,2048]{1,0:T(8,128)} %bitcast.29), custom_call_target="tpu_custom_call" | custom-call | flops 200000000 | bytes 1048576 | tf_op jit(solution)/shard_map/pallas_call | solution.py:450
  3.1 2.6 %collective-permute-start.4 = (s16[2,16,3200]{2,1,0:T(8,128)(2,1)}, s16[2,16,3200]{2,1,0:T(8,128)(2,1)S(1)}, u32[]{:S(2)}, u32[]{:S(2)}) collective-permute-start(s16[2,16,3200]{2,1,0:T(8,128)(2,1)} %get-tuple-element.51.refs_4_.refs_2_.refs_8_), channel_id=1, source_target_pairs={{0,2},{1,3},{4,0},{5,1},{8,4},{9,5},{12,8},{13,9},{14,12},{15,13},... | collective-permute-start | bytes 614408 | tf_op jit(solution)/shard_map/ppermute | solution.py:387
  7.7 4.0 %collective-permute-done.4.refs_6_.refs_4_.refs_10_ = s16[2,16,3200]{2,1,0:T(8,128)(2,1)S(1)} collective-permute-done((s16[2,16,3200]{2,1,0:T(8,128)(2,1)}, s16[2,16,3200]{2,1,0:T(8,128)(2,1)S(1)}, u32[]{:S(2)}, u32[]{:S(2)}) %collective-permute-start.4) | collective-permute-done | bytes 204832 | tf_op jit(solution)/shard_map/ppermute | solution.py:387
  11.7 1.7 %collective-permute-start.6 = (s16[2,16,3200]{2,1,0:T(8,128)(2,1)S(1)}, s16[2,16,3200]{2,1,0:T(8,128)(2,1)S(1)}, u32[]{:S(2)}, u32[]{:S(2)}) collective-permute-start(s16[2,16,3200]{2,1,0:T(8,128)(2,1)S(1)} %collective-permute-done.4.refs_6_.refs_4_.refs_10_), channel_id=1, source_target_pairs={{0,2},{1,3},{4,0},{5,1},{8,4},{9,5},{12,8},{13,9},{14,12},{15,13},... | collective-permute-start | bytes 614408 | tf_op jit(solution)/shard_map/ppermute | solution.py:387
  14.6 2.2 %shard_map.148 = (f32[256,24]{1,0:T(8,128)S(1)}, f32[2,128,128]{2,1,0:T(8,128)S(1)}, f32[2,128,128]{2,1,0:T(8,128)S(1)}, bf16[1024,128]{1,0:T(8,128)(2,1)S(1)}, ...) custom-call(s32[25]{0:T(128)S(1)} %pad_add_fusion.refs_0_.refs_1_, ...), custom_call_target="tpu_custom_call" | custom-call | flops 2000000000 | bytes 1048576 | tf_op jit(solution)/shard_map/pallas_call | solution.py:450
  16.8 1.9 %collective-permute-done.6.refs_2_ = s16[2,16,3200]{2,1,0:T(8,128)(2,1)S(1)} collective-permute-done((s16[2,16,3200]{2,1,0:T(8,128)(2,1)S(1)}, s16[2,16,3200]{2,1,0:T(8,128)(2,1)S(1)}, u32[]{:S(2)}, u32[]{:S(2)}) %collective-permute-start.6) | collective-permute-done | bytes 204832 | tf_op jit(solution)/shard_map/ppermute | solution.py:387
  18.6 1.2 %collective-permute-done.5.refs_1_ = s16[2,16,3200]{2,1,0:T(8,128)(2,1)S(1)} collective-permute-done((s16[2,16,3200]{2,1,0:T(8,128)(2,1)S(1)}, s16[2,16,3200]{2,1,0:T(8,128)(2,1)S(1)}, u32[]{:S(2)}, u32[]{:S(2)}) %collective-permute-start.5) | collective-permute-done | bytes 204832 | tf_op jit(solution)/shard_map/ppermute | solution.py:387
  20.4 1.5 %collective-permute-start.8 = (s16[2,16,3200]{2,1,0:T(8,128)(2,1)S(1)}, s16[2,16,3200]{2,1,0:T(8,128)(2,1)S(1)}, u32[]{:S(2)}, u32[]{:S(2)}) collective-permute-start(s16[2,16,3200]{2,1,0:T(8,128)(2,1)S(1)} %get-tuple-element.53.refs_6_.refs_5_.refs_12_), channel_id=1, source_target_pairs={{0,2},{1,3},{4,0},{5,1},{8,4},{9,5},{12,8},{13,9},{14,12},{15,13},... | collective-permute-start | bytes 614408 | tf_op jit(solution)/shard_map/ppermute | solution.py:387
  21.9 3.7 %collective-permute-done.7.refs_7_.refs_6_.refs_13_ = s16[2,16,3200]{2,1,0:T(8,128)(2,1)S(1)} collective-permute-done((s16[2,16,3200]{2,1,0:T(8,128)(2,1)S(1)}, s16[2,16,3200]{2,1,0:T(8,128)(2,1)S(1)}, u32[]{:S(2)}, u32[]{:S(2)}) %collective-permute-start.7) | collective-permute-done | bytes 204832 | tf_op jit(solution)/shard_map/ppermute | solution.py:387
  26.4 1.7 %collective-permute-start.11 = (s16[1,16,3200]{2,1,0:T(8,128)(2,1)S(1)}, s16[1,16,3200]{2,1,0:T(8,128)(2,1)S(1)}, u32[]{:S(2)}, u32[]{:S(2)}) collective-permute-start(s16[1,16,3200]{2,1,0:T(8,128)(2,1)S(1)} %slice.9), channel_id=1, source_target_pairs={{0,2},{1,3},{4,0},{5,1},{8,4},{9,5},{12,8},{13,9},{14,12},{15,13},... | collective-permute-start | bytes 307208 | tf_op jit(solution)/shard_map/ppermute | solution.py:387
  28.0 2.0 %shard_map.150.refs_0_.refs_6_ = f32[256,128]{1,0:T(8,128)S(1)} custom-call(s32[25]{0:T(128)S(1)} %pad_add_fusion.refs_0_.refs_1_, f32[256,24]{1,0:T(8,128)S(1)} %get-tuple-element.45.refs_1_.refs_2_.refs_0_, bf16[1024,1024]{1,0:T(8,128)(2,1)S(1)} %bitcast.24, bf16[1024,1024]{1,0:T(8,128)(2,1)S(1)} %get-tuple-element.48.refs_3_.refs_4_, ...), custom_call_target="tpu_custom_call" | custom-call | flops 1073741824 | bytes 1048576 | tf_op jit(solution)/shard_map/pallas_call | solution.py:450
  31.3 2.0 %shard_map.152.refs_7_ = f32[256,128]{1,0:T(8,128)S(1)} custom-call(f32[8,128]{1,0:T(8,128)S(1)} %shard_map.151.refs_0_.refs_4_, s32[25]{0:T(128)S(1)} %pad_add_fusion.refs_0_.refs_1_, f32[256,24]{1,0:T(8,128)S(1)} %get-tuple-element.45.refs_1_.refs_2_.refs_0_, bf16[1024,1024]{1,0:T(8,128)(2,1)S(1)} %bitcast.25, ...), custom_call_target="tpu_custom_call" | custom-call | flops 1073741824 | bytes 1048576 | tf_op jit(solution)/shard_map/pallas_call | solution.py:450
  33.3 2.3 %shard_map.153 = (f32[256,128]{1,0:T(8,128)S(1)}, f32[256,256]{1,0:T(8,128)S(1)}, f32[256,2048]{1,0:T(8,128)S(1)}, bf16[256,2048]{1,0:T(8,128)(2,1)S(1)}, bf16[2...) custom-call(s32[25]{0:T(128)S(1)} %pad_add_fusion.refs_0_.refs_1_, ...), custom_call_target="tpu_custom_call" | custom-call | flops 805306368 | bytes 1048576 | tf_op jit(solution)/shard_map/pallas_call | solution.py:450
  35.9 4.0 %shard_map.154 = (f32[2,16,3072]{2,1,0:T(8,128)S(1)}, s16[2,16,3200]{2,1,0:T(8,128)(2,1)S(1)}, f32[2,16,3072]{2,1,0:T(8,128)S(1)}, s16[2,16,3200]{2,1,0:T(8,128)...) custom-call(bf16[1024,128]{1,0:T(8,128)(2,1)S(1)} %get-tuple-element.46.refs_0_.refs_1_, ...), custom_call_target="tpu_custom_call" | custom-call | flops 2147483648 | bytes 1048576 | tf_op jit(solution)/shard_map/pallas_call | solution.py:450
  39.9 1.4 %collective-permute-start.13 = (s16[2,16,3200]{2,1,0:T(8,128)(2,1)S(1)}, s16[2,16,3200]{2,1,0:T(8,128)(2,1)S(1)}, u32[]{:S(2)}, u32[]{:S(2)}) collective-permute-start(s16[2,16,3200]{2,1,0:T(8,128)(2,1)S(1)} %get-tuple-element.64), channel_id=1, source_target_pairs={{0,4},{1,5},{2,6},{3,7},{4,0},{5,1},{6,2},{7,3},{8,12},{9,13},{10,... | collective-permute-start | bytes 614408 | tf_op jit(solution)/shard_map/ppermute | solution.py:413
  41.2 1.8 %collective-permute-start.14 = (s16[2,16,3200]{2,1,0:T(8,128)(2,1)S(1)}, s16[2,16,3200]{2,1,0:T(8,128)(2,1)S(1)}, u32[]{:S(2)}, u32[]{:S(2)}) collective-permute-start(s16[2,16,3200]{2,1,0:T(8,128)(2,1)S(1)} %get-tuple-element.68), channel_id=1, source_target_pairs={{0,2},{1,3},{2,0},{3,1},{4,6},{5,7},{6,4},{7,5},{8,10},{9,11},{10,... | collective-permute-start | bytes 614408 | tf_op jit(solution)/shard_map/ppermute | solution.py:413
  43.1 3.2 %shard_map.155 = (f32[2,16,3072]{2,1,0:T(8,128)S(1)}, s16[2,16,3200]{2,1,0:T(8,128)(2,1)S(1)}, f32[2,16,3072]{2,1,0:T(8,128)S(1)}, s16[2,16,3200]{2,1,0:T(8,128)(2,1)S(1)}) custom-call(f32[256,24]{1,0:T(8,128)S(1)} %get-tuple-element.45.refs_1_.refs_2_.refs_0_, bf16[1024,128]{1,0:T(8,128)(2,1)S(1)} %get-tuple-element.46.refs_0_.refs_1_, ...), custom_call_target="tpu_custom_call" | custom-call | flops 1879048192 | bytes 1048576 | tf_op jit(solution)/shard_map/pallas_call | solution.py:450
  47.4 1.5 %collective-permute-start.17 = (s16[16,3200]{1,0:T(8,128)(2,1)S(1)}, s16[16,3200]{1,0:T(8,128)(2,1)S(1)}, u32[]{:S(2)}, u32[]{:S(2)}) collective-permute-start(s16[16,3200]{1,0:T(8,128)(2,1)S(1)} %get-tuple-element.67.refs_0_), channel_id=1, source_target_pairs={{0,2},{1,3},{2,0},{3,1},{4,6},{5,7},{6,4},{7,5},{8,10},{9,11},{10,... | collective-permute-start | bytes 307208 | tf_op jit(solution)/shard_map/ppermute | solution.py:413
  49.7 1.7 %collective-permute-start.16 = (s16[16,3200]{1,0:T(8,128)(2,1)S(1)}, s16[16,3200]{1,0:T(8,128)(2,1)S(1)}, u32[]{:S(2)}, u32[]{:S(2)}) collective-permute-start(s16[16,3200]{1,0:T(8,128)(2,1)S(1)} %get-tuple-element.74), channel_id=1, source_target_pairs={{0,4},{1,5},{2,6},{3,7},{4,0},{5,1},{6,2},{7,3},{8,12},{9,13},{10,... | collective-permute-start | bytes 307208 | tf_op jit(solution)/shard_map/ppermute | solution.py:413
  51.4 2.6 %collective-permute-done.15.refs_1_ = s16[2,16,3200]{2,1,0:T(8,128)(2,1)S(1)} collective-permute-done((s16[2,16,3200]{2,1,0:T(8,128)(2,1)S(1)}, s16[2,16,3200]{2,1,0:T(8,128)(2,1)S(1)}, u32[]{:S(2)}, u32[]{:S(2)}) %collective-permute-start.15) | collective-permute-done | bytes 204832 | tf_op jit(solution)/shard_map/ppermute | solution.py:413
  55.3 2.7 %collective-permute-start.20 = (s16[16,3200]{1,0:T(8,128)(2,1)S(1)}, s16[16,3200]{1,0:T(8,128)(2,1)S(1)}, u32[]{:S(2)}, u32[]{:S(2)}) collective-permute-start(s16[16,3200]{1,0:T(8,128)(2,1)S(1)} %shard_map.159.refs_0_), channel_id=1, source_target_pairs={{0,8},{1,9},{2,10},{3,11},{4,12},{5,13},{6,14},{7,15},{8,0},{9,1},... | collective-permute-start | bytes 307208 | tf_op jit(solution)/shard_map/ppermute | solution.py:413
  59.2 2.6 %collective-permute-start.22 = (s16[16,3200]{1,0:T(8,128)(2,1)S(1)}, s16[16,3200]{1,0:T(8,128)(2,1)S(1)}, u32[]{:S(2)}, u32[]{:S(2)}) collective-permute-start(s16[16,3200]{1,0:T(8,128)(2,1)S(1)} %shard_map.160.refs_0_), channel_id=1, source_target_pairs={{0,8},{1,9},{2,10},{3,11},{4,12},{5,13},{6,14},{7,15},{8,0},{9,1},... | collective-permute-start | bytes 307208 | tf_op jit(solution)/shard_map/ppermute | solution.py:413
  62.0 1.3 %collective-permute-start.21 = (s16[16,3200]{1,0:T(8,128)(2,1)S(1)}, s16[16,3200]{1,0:T(8,128)(2,1)S(1)}, u32[]{:S(2)}, u32[]{:S(2)}) collective-permute-start(s16[16,3200]{1,0:T(8,128)(2,1)S(1)} %get-tuple-element.79), channel_id=1, source_target_pairs={{0,4},{1,5},{2,6},{3,7},{4,0},{5,1},{6,2},{7,3},{8,12},{9,13},{10,... | collective-permute-start | bytes 307208 | tf_op jit(solution)/shard_map/ppermute | solution.py:413
  64.2 3.4 %collective-permute-done.21.refs_2_ = s16[16,3200]{1,0:T(8,128)(2,1)S(1)} collective-permute-done((s16[16,3200]{1,0:T(8,128)(2,1)S(1)}, s16[16,3200]{1,0:T(8,128)(2,1)S(1)}, u32[]{:S(2)}, u32[]{:S(2)}) %collective-permute-start.21) | collective-permute-done | bytes 102432 | tf_op jit(solution)/shard_map/ppermute | solution.py:413
  (56 shorter events, 12.8 us)
Async XLA Ops:
  0.6 13.2 %collective-permute-start.1 = (bf16[1024,1024]{1,0:T(8,128)(2,1)}, bf16[1024,1024]{1,0:T(8,128)(2,1)S(1)}, u32[]{:S(2)}, u32[]{:S(2)}) collective-permute-start(bf16[1024,1024]{1,0:T(8,128)(2,1)} %bitcast.23), channel_id=1, source_target_pairs={{0,1},{1,0},{2,3},{3,2},{4,5},{5,4},{6,7},{7,6},{8,9},{9,8},{10,11... | collective-permute-start | bytes 6291464 | tf_op jit(solution)/shard_map/ppermute | solution.py:413
  3.1 8.6 %collective-permute-start.4 = (s16[2,16,3200]{2,1,0:T(8,128)(2,1)}, s16[2,16,3200]{2,1,0:T(8,128)(2,1)S(1)}, u32[]{:S(2)}, u32[]{:S(2)}) collective-permute-start(s16[2,16,3200]{2,1,0:T(8,128)(2,1)} %get-tuple-element.51.refs_4_.refs_2_.refs_8_), channel_id=1, source_target_pairs={{0,2},{1,3},{4,0},{5,1},{8,4},{9,5},{12,8},{13,9},{14,12},{15,13},... | collective-permute-start | bytes 614408 | tf_op jit(solution)/shard_map/ppermute | solution.py:387
  5.7 7.7 %collective-permute-start.3 = (s16[2,16,3200]{2,1,0:T(8,128)(2,1)}, s16[2,16,3200]{2,1,0:T(8,128)(2,1)S(1)}, u32[]{:S(2)}, u32[]{:S(2)}) collective-permute-start(s16[2,16,3200]{2,1,0:T(8,128)(2,1)} %get-tuple-element.51.refs_4_.refs_2_.refs_8_), channel_id=1, source_target_pairs={{0,4},{1,5},{4,8},{5,9},{8,12},{9,13},{12,14},{13,15},{14,10},{15,... | collective-permute-start | bytes 614408 | tf_op jit(solution)/shard_map/ppermute | solution.py:387
  5.8 8.0 %collective-permute-start = (f32[24,128]{1,0:T(8,128)}, f32[24,128]{1,0:T(8,128)S(1)}, u32[]{:S(2)}, u32[]{:S(2)}) collective-permute-start(f32[24,128]{1,0:T(8,128)} %get-tuple-element.44.refs_1_), channel_id=1, source_target_pairs={{0,1},{1,0},{2,3},{3,2},{4,5},{5,4},{6,7},{7,6},{8,9},{9,8},{10,11... | collective-permute-start | bytes 36872 | tf_op jit(solution)/shard_map/ppermute | solution.py:413
  6.0 7.8 %collective-permute-start.2 = (bf16[128,2048]{1,0:T(8,128)(2,1)}, bf16[128,2048]{1,0:T(8,128)(2,1)S(1)}, u32[]{:S(2)}, u32[]{:S(2)}) collective-permute-start(bf16[128,2048]{1,0:T(8,128)(2,1)} %refs_4_.1), channel_id=1, source_target_pairs={{0,1},{1,0},{2,3},{3,2},{4,5},{5,4},{6,7},{7,6},{8,9},{9,8},{10,11... | collective-permute-start | bytes 1572872 | tf_op jit(solution)/shard_map/ppermute | solution.py:413
  11.7 6.9 %collective-permute-start.6 = (s16[2,16,3200]{2,1,0:T(8,128)(2,1)S(1)}, s16[2,16,3200]{2,1,0:T(8,128)(2,1)S(1)}, u32[]{:S(2)}, u32[]{:S(2)}) collective-permute-start(s16[2,16,3200]{2,1,0:T(8,128)(2,1)S(1)} %collective-permute-done.4.refs_6_.refs_4_.refs_10_), channel_id=1, source_target_pairs={{0,2},{1,3},{4,0},{5,1},{8,4},{9,5},{12,8},{13,9},{14,12},{15,13},... | collective-permute-start | bytes 614408 | tf_op jit(solution)/shard_map/ppermute | solution.py:387
  13.4 6.4 %collective-permute-start.5 = (s16[2,16,3200]{2,1,0:T(8,128)(2,1)S(1)}, s16[2,16,3200]{2,1,0:T(8,128)(2,1)S(1)}, u32[]{:S(2)}, u32[]{:S(2)}) collective-permute-start(s16[2,16,3200]{2,1,0:T(8,128)(2,1)S(1)} %collective-permute-done.3.refs_5_.refs_3_.refs_9_), channel_id=1, source_target_pairs={{0,4},{1,5},{4,8},{5,9},{8,12},{9,13},{12,14},{13,15},{14,10},{15,... | collective-permute-start | bytes 614408 | tf_op jit(solution)/shard_map/ppermute | solution.py:387
  13.8 14.2 %copy-start.1 = (s16[2,16,3200]{2,1,0:T(8,128)(2,1)S(1)}, s16[2,16,3200]{2,1,0:T(8,128)(2,1)}, u32[]{:S(2)}) copy-start(s16[2,16,3200]{2,1,0:T(8,128)(2,1)} %get-tuple-element.51.refs_4_.refs_2_.refs_8_) | copy-start | bytes 614404
  19.8 5.8 %collective-permute-start.7 = (s16[2,16,3200]{2,1,0:T(8,128)(2,1)S(1)}, s16[2,16,3200]{2,1,0:T(8,128)(2,1)S(1)}, u32[]{:S(2)}, u32[]{:S(2)}) collective-permute-start(s16[2,16,3200]{2,1,0:T(8,128)(2,1)S(1)} %get-tuple-element.52.refs_7_.refs_5_.refs_11_), channel_id=1, source_target_pairs={{0,4},{1,5},{4,8},{5,9},{8,12},{9,13},{12,14},{13,15},{14,10},{15,... | collective-permute-start | bytes 614408 | tf_op jit(solution)/shard_map/ppermute | solution.py:387
  20.4 5.9 %collective-permute-start.8 = (s16[2,16,3200]{2,1,0:T(8,128)(2,1)S(1)}, s16[2,16,3200]{2,1,0:T(8,128)(2,1)S(1)}, u32[]{:S(2)}, u32[]{:S(2)}) collective-permute-start(s16[2,16,3200]{2,1,0:T(8,128)(2,1)S(1)} %get-tuple-element.53.refs_6_.refs_5_.refs_12_), channel_id=1, source_target_pairs={{0,2},{1,3},{4,0},{5,1},{8,4},{9,5},{12,8},{13,9},{14,12},{15,13},... | collective-permute-start | bytes 614408 | tf_op jit(solution)/shard_map/ppermute | solution.py:387
  25.6 4.7 %collective-permute-start.9 = (s16[1,16,3200]{2,1,0:T(8,128)(2,1)S(1)}, s16[1,16,3200]{2,1,0:T(8,128)(2,1)S(1)}, u32[]{:S(2)}, u32[]{:S(2)}) collective-permute-start(s16[1,16,3200]{2,1,0:T(8,128)(2,1)S(1)} %slice.8), channel_id=1, source_target_pairs={{0,4},{1,5},{4,8},{5,9},{8,12},{9,13},{12,14},{13,15},{14,10},{15,... | collective-permute-start | bytes 307208 | tf_op jit(solution)/shard_map/ppermute | solution.py:387
  26.4 4.9 %collective-permute-start.11 = (s16[1,16,3200]{2,1,0:T(8,128)(2,1)S(1)}, s16[1,16,3200]{2,1,0:T(8,128)(2,1)S(1)}, u32[]{:S(2)}, u32[]{:S(2)}) collective-permute-start(s16[1,16,3200]{2,1,0:T(8,128)(2,1)S(1)} %slice.9), channel_id=1, source_target_pairs={{0,2},{1,3},{4,0},{5,1},{8,4},{9,5},{12,8},{13,9},{14,12},{15,13},... | collective-permute-start | bytes 307208 | tf_op jit(solution)/shard_map/ppermute | solution.py:387
  30.9 2.3 %collective-permute-start.10 = (f32[8,128]{1,0:T(8,128)S(1)}, f32[8,128]{1,0:T(8,128)S(1)}, u32[]{:S(2)}, u32[]{:S(2)}) collective-permute-start(f32[8,128]{1,0:T(8,128)S(1)} %shard_map.151.refs_0_.refs_4_), channel_id=1, source_target_pairs={{0,1},{1,0},{2,3},{3,2},{4,5},{5,4},{6,7},{7,6},{8,9},{9,8},{10,11... | collective-permute-start | bytes 12296 | tf_op jit(solution)/shard_map/ppermute | solution.py:413
  35.5 7.5 %collective-permute-start.12 = (bf16[256,2048]{1,0:T(8,128)(2,1)S(1)}, bf16[256,2048]{1,0:T(8,128)(2,1)S(1)}, u32[]{:S(2)}, u32[]{:S(2)}) collective-permute-start(bf16[256,2048]{1,0:T(8,128)(2,1)S(1)} %get-tuple-element.62), channel_id=1, source_target_pairs={{0,1},{1,0},{2,3},{3,2},{4,5},{5,4},{6,7},{7,6},{8,9},{9,8},{10,11... | collective-permute-start | bytes 3145736 | tf_op jit(solution)/shard_map/ppermute | solution.py:413
  39.9 7.3 %collective-permute-start.13 = (s16[2,16,3200]{2,1,0:T(8,128)(2,1)S(1)}, s16[2,16,3200]{2,1,0:T(8,128)(2,1)S(1)}, u32[]{:S(2)}, u32[]{:S(2)}) collective-permute-start(s16[2,16,3200]{2,1,0:T(8,128)(2,1)S(1)} %get-tuple-element.64), channel_id=1, source_target_pairs={{0,4},{1,5},{2,6},{3,7},{4,0},{5,1},{6,2},{7,3},{8,12},{9,13},{10,... | collective-permute-start | bytes 614408 | tf_op jit(solution)/shard_map/ppermute | solution.py:413
  41.2 8.2 %collective-permute-start.14 = (s16[2,16,3200]{2,1,0:T(8,128)(2,1)S(1)}, s16[2,16,3200]{2,1,0:T(8,128)(2,1)S(1)}, u32[]{:S(2)}, u32[]{:S(2)}) collective-permute-start(s16[2,16,3200]{2,1,0:T(8,128)(2,1)S(1)} %get-tuple-element.68), channel_id=1, source_target_pairs={{0,2},{1,3},{2,0},{3,1},{4,6},{5,7},{6,4},{7,5},{8,10},{9,11},{10,... | collective-permute-start | bytes 614408 | tf_op jit(solution)/shard_map/ppermute | solution.py:413
  46.3 7.7 %collective-permute-start.15 = (s16[2,16,3200]{2,1,0:T(8,128)(2,1)S(1)}, s16[2,16,3200]{2,1,0:T(8,128)(2,1)S(1)}, u32[]{:S(2)}, u32[]{:S(2)}) collective-permute-start(s16[2,16,3200]{2,1,0:T(8,128)(2,1)S(1)} %get-tuple-element.71), channel_id=1, source_target_pairs={{0,4},{1,5},{2,6},{3,7},{4,0},{5,1},{6,2},{7,3},{8,12},{9,13},{10,... | collective-permute-start | bytes 614408 | tf_op jit(solution)/shard_map/ppermute | solution.py:413
  47.4 7.2 %collective-permute-start.17 = (s16[16,3200]{1,0:T(8,128)(2,1)S(1)}, s16[16,3200]{1,0:T(8,128)(2,1)S(1)}, u32[]{:S(2)}, u32[]{:S(2)}) collective-permute-start(s16[16,3200]{1,0:T(8,128)(2,1)S(1)} %get-tuple-element.67.refs_0_), channel_id=1, source_target_pairs={{0,2},{1,3},{2,0},{3,1},{4,6},{5,7},{6,4},{7,5},{8,10},{9,11},{10,... | collective-permute-start | bytes 307208 | tf_op jit(solution)/shard_map/ppermute | solution.py:413
  48.9 12.9 %collective-permute-start.19 = (s16[2,16,3200]{2,1,0:T(8,128)(2,1)S(1)}, s16[2,16,3200]{2,1,0:T(8,128)(2,1)S(1)}, u32[]{:S(2)}, u32[]{:S(2)}) collective-permute-start(s16[2,16,3200]{2,1,0:T(8,128)(2,1)S(1)} %get-tuple-element.77), channel_id=1, source_target_pairs={{0,2},{1,3},{2,0},{3,1},{4,6},{5,7},{6,4},{7,5},{8,10},{9,11},{10,... | collective-permute-start | bytes 614408 | tf_op jit(solution)/shard_map/ppermute | solution.py:413
  49.7 5.4 %collective-permute-start.16 = (s16[16,3200]{1,0:T(8,128)(2,1)S(1)}, s16[16,3200]{1,0:T(8,128)(2,1)S(1)}, u32[]{:S(2)}, u32[]{:S(2)}) collective-permute-start(s16[16,3200]{1,0:T(8,128)(2,1)S(1)} %get-tuple-element.74), channel_id=1, source_target_pairs={{0,4},{1,5},{2,6},{3,7},{4,0},{5,1},{6,2},{7,3},{8,12},{9,13},{10,... | collective-permute-start | bytes 307208 | tf_op jit(solution)/shard_map/ppermute | solution.py:413
  54.2 4.7 %collective-permute-start.18 = (s16[16,3200]{1,0:T(8,128)(2,1)S(1)}, s16[16,3200]{1,0:T(8,128)(2,1)S(1)}, u32[]{:S(2)}, u32[]{:S(2)}) collective-permute-start(s16[16,3200]{1,0:T(8,128)(2,1)S(1)} %get-tuple-element.73.refs_0_), channel_id=1, source_target_pairs={{0,2},{1,3},{2,0},{3,1},{4,6},{5,7},{6,4},{7,5},{8,10},{9,11},{10,... | collective-permute-start | bytes 307208 | tf_op jit(solution)/shard_map/ppermute | solution.py:413
  55.3 8.8 %collective-permute-start.20 = (s16[16,3200]{1,0:T(8,128)(2,1)S(1)}, s16[16,3200]{1,0:T(8,128)(2,1)S(1)}, u32[]{:S(2)}, u32[]{:S(2)}) collective-permute-start(s16[16,3200]{1,0:T(8,128)(2,1)S(1)} %shard_map.159.refs_0_), channel_id=1, source_target_pairs={{0,8},{1,9},{2,10},{3,11},{4,12},{5,13},{6,14},{7,15},{8,0},{9,1},... | collective-permute-start | bytes 307208 | tf_op jit(solution)/shard_map/ppermute | solution.py:413
  59.2 8.4 %collective-permute-start.22 = (s16[16,3200]{1,0:T(8,128)(2,1)S(1)}, s16[16,3200]{1,0:T(8,128)(2,1)S(1)}, u32[]{:S(2)}, u32[]{:S(2)}) collective-permute-start(s16[16,3200]{1,0:T(8,128)(2,1)S(1)} %shard_map.160.refs_0_), channel_id=1, source_target_pairs={{0,8},{1,9},{2,10},{3,11},{4,12},{5,13},{6,14},{7,15},{8,0},{9,1},... | collective-permute-start | bytes 307208 | tf_op jit(solution)/shard_map/ppermute | solution.py:413
  62.0 5.6 %collective-permute-start.21 = (s16[16,3200]{1,0:T(8,128)(2,1)S(1)}, s16[16,3200]{1,0:T(8,128)(2,1)S(1)}, u32[]{:S(2)}, u32[]{:S(2)}) collective-permute-start(s16[16,3200]{1,0:T(8,128)(2,1)S(1)} %get-tuple-element.79), channel_id=1, source_target_pairs={{0,4},{1,5},{2,6},{3,7},{4,0},{5,1},{6,2},{7,3},{8,12},{9,13},{10,... | collective-permute-start | bytes 307208 | tf_op jit(solution)/shard_map/ppermute | solution.py:413
  (4 other events, 25.0 us)

commit v18 on v14

--- a/solution.py
+++ b/solution.py
@@ -82,9 +82,10 @@
     return experts, gates, small_ref[:, 2 * top : 2 * top + 1]
 
 
-def members(place_ref, wide, first=0, count=None):
-    piece_of = lax.broadcasted_iota(jnp.int32, (1, wide), 1) // (wide // count)
-    found = jnp.zeros((1, wide), jnp.int32)
+def members(place_ref, wide, first, count, dim=1):
+    shape = (1, wide) if dim == 1 else (wide, 1)
+    piece_of = lax.broadcasted_iota(jnp.int32, shape, dim) // (wide // count)
+    found = jnp.zeros(shape, jnp.int32)
     for number in range(count):
         found = jnp.where(piece_of == number, place_ref[1 + first + number], found)
     return found.astype(f32)
@@ -120,7 +121,7 @@
     small_ref[...] = jnp.concatenate([own_ref[...], other_ref[...]], axis=1).T
     experts, gates, _ = token_columns(small_ref, top)
     _, tokens, wide = rank_ref.shape
-    column = members(place_ref, wide, 0, slots)
+    column = members(place_ref, wide, slots, slots)
     below = (
         lax.broadcasted_iota(jnp.int32, (tokens, tokens), 0)
         > lax.broadcasted_iota(jnp.int32, (tokens, tokens), 1)
@@ -186,9 +187,9 @@
     for block in range(2):
         total = capacity_ref[...] - prior_ref[block : block + 1] - arrived_ref[1 - block : 2 - block]
         limit = jnp.zeros((1, wide), f32)
-        for arrival in range(slots):
-            picked = jnp.where(lane == counts_lane + place_ref[1 + arrival], total, 0.0)
-            limit = jnp.where(piece_of == arrival, jnp.sum(picked, axis=1, keepdims=True), limit)
+        for slot in range(slots):
+            picked = jnp.where(lane == counts_lane + place_ref[1 + slots + slot], total, 0.0)
+            limit = jnp.where(piece_of == slot, jnp.sum(picked, axis=1, keepdims=True), limit)
         limits.append(limit)
     return limits
 
@@ -212,12 +213,19 @@
         jnp.concatenate([ref[:, kind * half : (kind + 1) * half] for ref in (early_ref, late_ref)], axis=1)
         for kind in range(2)
     ]
+    rank = wide // slots
+    by_arrival = members(place_ref, wide, 0, slots, 0) == members(place_ref, wide, slots, slots)
+    row = lax.broadcasted_iota(jnp.int32, (wide, wide), 0)
+    same_index = row % rank == lax.broadcasted_iota(jnp.int32, (wide, wide), 1) % rank
+    order = jnp.where(by_arrival & same_index, 1.0, 0.0).astype(bf16)
+    reduced = [sum(dot(part, order, 1, 0) for part in halves(both)) for both in reduced]
     weighted = jnp.concatenate([weight * part for part in reduced], axis=1)
     weighted_ref[...] = weighted
     for arrival in range(slots):
         for kind in range(2):
             _, up = decode(piece_part(piece_refs, arrival, kind, True), hidden_width)
-            high_ref[kind, arrival], low_ref[kind, arrival] = halves(up)
+            slot = place_ref[1 + 2 * slots + arrival]
+            high_ref[kind, slot], low_ref[kind, slot] = halves(up)
     factor = high_ref[...].reshape(2 * wide, model_width), low_ref[...].reshape(2 * wide, model_width)
     tangent = dot_pairs(halves(weighted), factor, 1, 0)
     tangent_ref[...] = tangent
@@ -238,25 +246,22 @@
     return both[:middle] + both[middle:]
 
 
-def put_chunks(place_ref, down_ref, up_ref, keep_ref, near_ref, chunk_ref, far_ref, down, up):
+def put_chunks(keep_ref, near_ref, chunk_ref, far_ref, down, up):
     rank = keep_ref.shape[1]
-    slots = down.shape[0] // rank
-    down_ref[...] = down
-    up_ref[...] = up
+    rows = down.shape[0] // rank // 2
 
     def slot(number):
-        start = pl.multiple_of(place_ref[1 + slots + number] * rank, rank)
-        return down_ref[pl.ds(start, rank), :], up_ref[pl.ds(start, rank), :]
+        start = number * rank
+        return down[start : start + rank], up[start : start + rank]
 
     for place in range(2):
         keep_ref[place] = jnp.concatenate(slot(place), axis=1)
-        near_ref[place] = encode(*slot(slots // 2 + place))
-        chunk_ref[place] = jnp.concatenate(slot(place * slots // 2 + 2), axis=1)
-        far_ref[place] = encode(*slot(place * slots // 2 + 3))
+        near_ref[place] = encode(*slot(rows + place))
+        chunk_ref[place] = jnp.concatenate(slot(place * rows + 2), axis=1)
+        far_ref[place] = encode(*slot(place * rows + 3))
 
 
 def gradient_kernel(
-    place_ref,
     same_ref,
     mask_ref,
     own_ref,
@@ -274,8 +279,6 @@
     up_ref,
     to_ref,
     left_ref,
-    down_sum_ref,
-    up_sum_ref,
 ):
     wide = weight_ref.shape[1]
     model_width = up_ref.shape[1]
@@ -288,13 +291,11 @@
     down = dot(left_ref[0], own_ref[...], 0, 0) + dot(left_ref[1], other_ref[...], 0, 0)
     up = add_halves(dot(jnp.concatenate(halves(weighted_ref[...]), axis=1), gradient, 0, 0))
     up_ref[...] = up[:wide]
-    out_refs = keep_ref, near_ref, chunk_ref, far_ref
-    put_chunks(place_ref, down_sum_ref, up_sum_ref, *out_refs, add_halves(down), up[wide:])
+    put_chunks(keep_ref, near_ref, chunk_ref, far_ref, add_halves(down), up[wide:])
 
 
 def curvature_kernel(
     top,
-    place_ref,
     small_ref,
     same_ref,
     mask_ref,
@@ -313,8 +314,6 @@
     chunk_ref,
     far_ref,
     left_ref,
-    down_sum_ref,
-    up_sum_ref,
 ):
     _, _, curvature = token_columns(small_ref, top)
     tokens, wide = weight_ref.shape
@@ -328,8 +327,7 @@
     down = dot(left_ref[0], own_ref[...], 0, 0) + dot(left_ref[1], other_ref[...], 0, 0)
     weighted_u = halves(weighted_ref[:, wide:])
     up = add_halves(dot(jnp.concatenate(weighted_u, axis=1), resid[0], 0, 0)) + dot(weighted_u[0], resid[1], 0, 0)
-    out_refs = keep_ref, near_ref, chunk_ref, far_ref
-    put_chunks(place_ref, down_sum_ref, up_sum_ref, *out_refs, add_halves(down), up_ref[...] + up)
+    put_chunks(keep_ref, near_ref, chunk_ref, far_ref, add_halves(down), up_ref[...] + up)
 
 
 def pair_kernel(hidden_width, arrived_ref, chunk_ref, near_ref, across_ref, keep_ref, onward_ref):
@@ -486,10 +484,8 @@
         grant=whole_vmem,
     )
     arrivals = ring.members(me)
-    number = jnp.arange(slots, dtype=jnp.int32)
     slot_of_arrival = (arrivals ^ me) // 4 + rows * ((arrivals ^ me) // 2 % 2)
-    arrival_of_slot = jnp.sum(jnp.where(slot_of_arrival == number[:, None], number, 0), axis=1)
-    place.append(jnp.concatenate([me[None], arrivals, arrival_of_slot]).astype(jnp.int32))
+    place.append(jnp.concatenate([me[None], arrivals, me ^ jnp.array(masks, jnp.int32), slot_of_arrival]).astype(jnp.int32))
     small_other = exchange(small, 1)
     hidden = hidden_of_route.reshape(tokens * top, hidden_width)
     small_columns, local_rank, gate, same, mask, hidden_other, gradient_other = call(
@@ -558,17 +554,12 @@
         *pieces,
     )
     arrived = exchange(coded, 1)
-    left = [
-        pltpu.VMEM((2, top * tokens, 2 * wide), bf16),
-        pltpu.VMEM((wide, hidden_width), f32),
-        pltpu.VMEM((wide, model_width), f32),
-    ]
+    left = [pltpu.VMEM((2, top * tokens, 2 * wide), bf16)]
     chunks = [((2, rank, hidden_width + model_width), f32), ((2, rank, coded_width), i16)] * 2
     gradient_keep, gradient_near, gradient_chunk, gradient_far, up, to = call(
         gradient_kernel,
         down_multiplies + 8 * up_multiplies,
         chunks + [((wide, model_width), f32), ((both, wide), f32)],
-        *place,
         same,
         mask,
         hidden,
@@ -587,7 +578,6 @@
         functools.partial(curvature_kernel, top),
         down_multiplies + 6 * up_multiplies,
         chunks,
-        *place,
         small_columns,
         same,
         mask,

time: 68.2 us -> 66.9 us (0.981)
  Pallas kernels: 21.2 us -> 20.2 us
  waiting for transfers between devices: 19.9 us -> 19.1 us
    pallas_call x16, Pallas kernels: 21.2 us -> 20.2 us  [call(): pl.pallas_call(lambda *refs: kernel(*refs[len(after):]), out_shape=[jax.S...]
  transfers between devices with their start and end apart: 22 -> 22, of which waited for: 8 -> 10; matrix products, arithmetic and copies ran while one was open for 1% -> 2% of each run, Pallas kernels for 27% -> 26%
where the time goes in v18:
time: 66.9 us; the launch traced here: 66.6 us
  starting transfers between devices  24.2 us (36%)
  Pallas kernels  20.2 us (30%)
  waiting for transfers between devices  19.1 us (29%)
  other arithmetic  1.43 us (2%)
  local copies, waits for them, and re-layouts  0.85 us (1%)
  between operations  0.81 us (1%)
    pallas_call x16, Pallas kernels, call(): pl.pallas_call(lambda *refs: kernel(*refs[len(after):]), out_shape=[jax.S...  20.2 us
    ppermute x14, starting transfers between devices, exchange(): lax.ppermute(value, 'expert', [(device, device ^ mask) for device in rang...  15.1 us
    ppermute x8, waiting for transfers between devices, shift(): return lax.ppermute(value, 'expert', pairs)  11.3 us
    ppermute x8, starting transfers between devices, shift(): return lax.ppermute(value, 'expert', pairs)  9.12 us
    ppermute x14, waiting for transfers between devices, exchange(): lax.ppermute(value, 'expert', [(device, device ^ mask) for device in rang...  7.74 us
  transfers between devices with their start and end apart: 22, of which 10 were waited for; matrix products, arithmetic and copies ran while one was open for 2% of the time, Pallas kernels for 26%

profile of v18, /device:TPU:0, one launch (start us, length us, event | category | flops | bytes accessed | tf_op | source)
XLA Modules:
  0.0 66.6 jit_solution(16611373022929748453)
XLA Ops:
  1.2 2.0 %shard_map.147 = (s16[2,16,3200]{2,1,0:T(8,128)(2,1)}, f32[24,128]{1,0:T(8,128)}) custom-call(s32[8,128]{1,0:T(8,128)} %bitcast.32, bf16[8,128]{1,0:T(8,128)(2,1)} %bitcast.33, f32[1,128]{1,0:T(1,128)} %bitcast.34, f32[16,1024]{1,0:T(8,128)} %bitcast.30, f32[16,1024]{1,0:T(8,128)} %bitcast.31, f32[16,2048]{1,0:T(8,128)} %bitcast.28, f32[16,2048]{1,0:T(8,128)} %bitcast.29), custom_call_target="tpu_custom_call" | custom-call | flops 200000000 | bytes 1048576 | tf_op jit(solution)/shard_map/pallas_call | solution.py:456
  3.1 2.6 %collective-permute-start.4 = (s16[2,16,3200]{2,1,0:T(8,128)(2,1)}, s16[2,16,3200]{2,1,0:T(8,128)(2,1)S(1)}, u32[]{:S(2)}, u32[]{:S(2)}) collective-permute-start(s16[2,16,3200]{2,1,0:T(8,128)(2,1)} %get-tuple-element.50.refs_4_.refs_2_.refs_8_), channel_id=1, source_target_pairs={{0,2},{1,3},{4,0},{5,1},{8,4},{9,5},{12,8},{13,9},{14,12},{15,13},... | collective-permute-start | bytes 614408 | tf_op jit(solution)/shard_map/ppermute | solution.py:393
  7.7 4.0 %collective-permute-done.4.refs_6_.refs_4_.refs_10_ = s16[2,16,3200]{2,1,0:T(8,128)(2,1)S(1)} collective-permute-done((s16[2,16,3200]{2,1,0:T(8,128)(2,1)}, s16[2,16,3200]{2,1,0:T(8,128)(2,1)S(1)}, u32[]{:S(2)}, u32[]{:S(2)}) %collective-permute-start.4) | collective-permute-done | bytes 204832 | tf_op jit(solution)/shard_map/ppermute | solution.py:393
  11.7 1.7 %collective-permute-start.6 = (s16[2,16,3200]{2,1,0:T(8,128)(2,1)S(1)}, s16[2,16,3200]{2,1,0:T(8,128)(2,1)S(1)}, u32[]{:S(2)}, u32[]{:S(2)}) collective-permute-start(s16[2,16,3200]{2,1,0:T(8,128)(2,1)S(1)} %collective-permute-done.4.refs_6_.refs_4_.refs_10_), channel_id=1, source_target_pairs={{0,2},{1,3},{4,0},{5,1},{8,4},{9,5},{12,8},{13,9},{14,12},{15,13},... | collective-permute-start | bytes 614408 | tf_op jit(solution)/shard_map/ppermute | solution.py:393
  14.6 2.2 %shard_map.148 = (f32[256,24]{1,0:T(8,128)S(1)}, f32[2,128,128]{2,1,0:T(8,128)S(1)}, f32[2,128,128]{2,1,0:T(8,128)S(1)}, bf16[1024,128]{1,0:T(8,128)(2,1)S(1)}, ...) custom-call(s32[25]{0:T(128)S(1)} %pad_add_fusion.refs_0_.refs_1_, ...), custom_call_target="tpu_custom_call" | custom-call | flops 2000000000 | bytes 1048576 | tf_op jit(solution)/shard_map/pallas_call | solution.py:456
  16.8 1.9 %collective-permute-done.6.refs_2_ = s16[2,16,3200]{2,1,0:T(8,128)(2,1)S(1)} collective-permute-done((s16[2,16,3200]{2,1,0:T(8,128)(2,1)S(1)}, s16[2,16,3200]{2,1,0:T(8,128)(2,1)S(1)}, u32[]{:S(2)}, u32[]{:S(2)}) %collective-permute-start.6) | collective-permute-done | bytes 204832 | tf_op jit(solution)/shard_map/ppermute | solution.py:393
  18.6 1.2 %collective-permute-done.5.refs_1_ = s16[2,16,3200]{2,1,0:T(8,128)(2,1)S(1)} collective-permute-done((s16[2,16,3200]{2,1,0:T(8,128)(2,1)S(1)}, s16[2,16,3200]{2,1,0:T(8,128)(2,1)S(1)}, u32[]{:S(2)}, u32[]{:S(2)}) %collective-permute-start.5) | collective-permute-done | bytes 204832 | tf_op jit(solution)/shard_map/ppermute | solution.py:393
  20.4 1.5 %collective-permute-start.8 = (s16[2,16,3200]{2,1,0:T(8,128)(2,1)S(1)}, s16[2,16,3200]{2,1,0:T(8,128)(2,1)S(1)}, u32[]{:S(2)}, u32[]{:S(2)}) collective-permute-start(s16[2,16,3200]{2,1,0:T(8,128)(2,1)S(1)} %get-tuple-element.52.refs_6_.refs_5_.refs_12_), channel_id=1, source_target_pairs={{0,2},{1,3},{4,0},{5,1},{8,4},{9,5},{12,8},{13,9},{14,12},{15,13},... | collective-permute-start | bytes 614408 | tf_op jit(solution)/shard_map/ppermute | solution.py:393
  21.9 3.7 %collective-permute-done.7.refs_7_.refs_6_.refs_13_ = s16[2,16,3200]{2,1,0:T(8,128)(2,1)S(1)} collective-permute-done((s16[2,16,3200]{2,1,0:T(8,128)(2,1)S(1)}, s16[2,16,3200]{2,1,0:T(8,128)(2,1)S(1)}, u32[]{:S(2)}, u32[]{:S(2)}) %collective-permute-start.7) | collective-permute-done | bytes 204832 | tf_op jit(solution)/shard_map/ppermute | solution.py:393
  26.3 1.7 %collective-permute-start.11 = (s16[1,16,3200]{2,1,0:T(8,128)(2,1)S(1)}, s16[1,16,3200]{2,1,0:T(8,128)(2,1)S(1)}, u32[]{:S(2)}, u32[]{:S(2)}) collective-permute-start(s16[1,16,3200]{2,1,0:T(8,128)(2,1)S(1)} %slice.9), channel_id=1, source_target_pairs={{0,2},{1,3},{4,0},{5,1},{8,4},{9,5},{12,8},{13,9},{14,12},{15,13},... | collective-permute-start | bytes 307208 | tf_op jit(solution)/shard_map/ppermute | solution.py:393
  28.0 2.0 %shard_map.150.refs_0_.refs_6_ = f32[256,128]{1,0:T(8,128)S(1)} custom-call(s32[25]{0:T(128)S(1)} %pad_add_fusion.refs_0_.refs_1_, f32[256,24]{1,0:T(8,128)S(1)} %get-tuple-element.44.refs_1_.refs_2_.refs_0_, bf16[1024,1024]{1,0:T(8,128)(2,1)S(1)} %bitcast.24, bf16[1024,1024]{1,0:T(8,128)(2,1)S(1)} %get-tuple-element.47.refs_3_.refs_4_, ...), custom_call_target="tpu_custom_call" | custom-call | flops 1073741824 | bytes 1048576 | tf_op jit(solution)/shard_map/pallas_call | solution.py:456
  31.2 2.0 %shard_map.152.refs_7_ = f32[256,128]{1,0:T(8,128)S(1)} custom-call(f32[8,128]{1,0:T(8,128)S(1)} %shard_map.151.refs_0_.refs_4_, s32[25]{0:T(128)S(1)} %pad_add_fusion.refs_0_.refs_1_, f32[256,24]{1,0:T(8,128)S(1)} %get-tuple-element.44.refs_1_.refs_2_.refs_0_, bf16[1024,1024]{1,0:T(8,128)(2,1)S(1)} %bitcast.25, ...), custom_call_target="tpu_custom_call" | custom-call | flops 1073741824 | bytes 1048576 | tf_op jit(solution)/shard_map/pallas_call | solution.py:456
  33.3 2.3 %shard_map.153 = (f32[256,128]{1,0:T(8,128)S(1)}, f32[256,256]{1,0:T(8,128)S(1)}, f32[256,2048]{1,0:T(8,128)S(1)}, bf16[256,2048]{1,0:T(8,128)(2,1)S(1)}, bf16[2...) custom-call(s32[25]{0:T(128)S(1)} %pad_add_fusion.refs_0_.refs_1_, ...), custom_call_target="tpu_custom_call" | custom-call | flops 805306368 | bytes 1048576 | tf_op jit(solution)/shard_map/pallas_call | solution.py:456
  35.9 4.0 %shard_map.154 = (f32[2,16,3072]{2,1,0:T(8,128)S(1)}, s16[2,16,3200]{2,1,0:T(8,128)(2,1)S(1)}, f32[2,16,3072]{2,1,0:T(8,128)S(1)}, s16[2,16,3200]{2,1,0:T(8,128)...) custom-call(bf16[1024,128]{1,0:T(8,128)(2,1)S(1)} %get-tuple-element.45.refs_0_.refs_1_, ...), custom_call_target="tpu_custom_call" | custom-call | flops 2147483648 | bytes 1048576 | tf_op jit(solution)/shard_map/pallas_call | solution.py:456
  39.9 1.4 %collective-permute-start.13 = (s16[2,16,3200]{2,1,0:T(8,128)(2,1)S(1)}, s16[2,16,3200]{2,1,0:T(8,128)(2,1)S(1)}, u32[]{:S(2)}, u32[]{:S(2)}) collective-permute-start(s16[2,16,3200]{2,1,0:T(8,128)(2,1)S(1)} %get-tuple-element.63), channel_id=1, source_target_pairs={{0,4},{1,5},{2,6},{3,7},{4,0},{5,1},{6,2},{7,3},{8,12},{9,13},{10,... | collective-permute-start | bytes 614408 | tf_op jit(solution)/shard_map/ppermute | solution.py:419
  41.2 1.8 %collective-permute-start.15 = (s16[2,16,3200]{2,1,0:T(8,128)(2,1)S(1)}, s16[2,16,3200]{2,1,0:T(8,128)(2,1)S(1)}, u32[]{:S(2)}, u32[]{:S(2)}) collective-permute-start(s16[2,16,3200]{2,1,0:T(8,128)(2,1)S(1)} %get-tuple-element.69), channel_id=1, source_target_pairs={{0,2},{1,3},{2,0},{3,1},{4,6},{5,7},{6,4},{7,5},{8,10},{9,11},{10,... | collective-permute-start | bytes 614408 | tf_op jit(solution)/shard_map/ppermute | solution.py:419
  43.1 3.2 %shard_map.155 = (f32[2,16,3072]{2,1,0:T(8,128)S(1)}, s16[2,16,3200]{2,1,0:T(8,128)(2,1)S(1)}, f32[2,16,3072]{2,1,0:T(8,128)S(1)}, s16[2,16,3200]{2,1,0:T(8,128)(2,1)S(1)}) custom-call(f32[256,24]{1,0:T(8,128)S(1)} %get-tuple-element.44.refs_1_.refs_2_.refs_0_, bf16[1024,128]{1,0:T(8,128)(2,1)S(1)} %get-tuple-element.45.refs_0_.refs_1_, ...), custom_call_target="tpu_custom_call" | custom-call | flops 1879048192 | bytes 1048576 | tf_op jit(solution)/shard_map/pallas_call | solution.py:456
  47.4 1.5 %collective-permute-start.16 = (s16[16,3200]{1,0:T(8,128)(2,1)S(1)}, s16[16,3200]{1,0:T(8,128)(2,1)S(1)}, u32[]{:S(2)}, u32[]{:S(2)}) collective-permute-start(s16[16,3200]{1,0:T(8,128)(2,1)S(1)} %get-tuple-element.66.refs_0_), channel_id=1, source_target_pairs={{0,2},{1,3},{2,0},{3,1},{4,6},{5,7},{6,4},{7,5},{8,10},{9,11},{10,... | collective-permute-start | bytes 307208 | tf_op jit(solution)/shard_map/ppermute | solution.py:419
  49.5 3.4 %collective-permute-done.14.refs_1_ = s16[2,16,3200]{2,1,0:T(8,128)(2,1)S(1)} collective-permute-done((s16[2,16,3200]{2,1,0:T(8,128)(2,1)S(1)}, s16[2,16,3200]{2,1,0:T(8,128)(2,1)S(1)}, u32[]{:S(2)}, u32[]{:S(2)}) %collective-permute-start.14) | collective-permute-done | bytes 204832 | tf_op jit(solution)/shard_map/ppermute | solution.py:419
  53.9 2.7 %collective-permute-start.19 = (s16[16,3200]{1,0:T(8,128)(2,1)S(1)}, s16[16,3200]{1,0:T(8,128)(2,1)S(1)}, u32[]{:S(2)}, u32[]{:S(2)}) collective-permute-start(s16[16,3200]{1,0:T(8,128)(2,1)S(1)} %shard_map.158.refs_0_), channel_id=1, source_target_pairs={{0,8},{1,9},{2,10},{3,11},{4,12},{5,13},{6,14},{7,15},{8,0},{9,1},... | collective-permute-start | bytes 307208 | tf_op jit(solution)/shard_map/ppermute | solution.py:419
  57.4 1.9 %collective-permute-start.21 = (s16[2,16,3200]{2,1,0:T(8,128)(2,1)S(1)}, s16[2,16,3200]{2,1,0:T(8,128)(2,1)S(1)}, u32[]{:S(2)}, u32[]{:S(2)}) collective-permute-start(s16[2,16,3200]{2,1,0:T(8,128)(2,1)S(1)} %get-tuple-element.75.refs_0_), channel_id=1, source_target_pairs={{0,4},{1,5},{2,6},{3,7},{4,0},{5,1},{6,2},{7,3},{8,12},{9,13},{10,... | collective-permute-start | bytes 614408 | tf_op jit(solution)/shard_map/ppermute | solution.py:419
  59.5 2.8 %collective-permute-start.20 = (s16[16,3200]{1,0:T(8,128)(2,1)S(1)}, s16[16,3200]{1,0:T(8,128)(2,1)S(1)}, u32[]{:S(2)}, u32[]{:S(2)}) collective-permute-start(s16[16,3200]{1,0:T(8,128)(2,1)S(1)} %shard_map.160.refs_0_), channel_id=1, source_target_pairs={{0,8},{1,9},{2,10},{3,11},{4,12},{5,13},{6,14},{7,15},{8,0},{9,1},... | collective-permute-start | bytes 307208 | tf_op jit(solution)/shard_map/ppermute | solution.py:419
  62.4 3.4 %collective-permute-done.21.refs_3_ = s16[2,16,3200]{2,1,0:T(8,128)(2,1)S(1)} collective-permute-done((s16[2,16,3200]{2,1,0:T(8,128)(2,1)S(1)}, s16[2,16,3200]{2,1,0:T(8,128)(2,1)S(1)}, u32[]{:S(2)}, u32[]{:S(2)}) %collective-permute-start.21) | collective-permute-done | bytes 204832 | tf_op jit(solution)/shard_map/ppermute | solution.py:419
  65.7 0.8 %shard_map.162 = (f32[16,1024]{1,0:T(8,128)}, f32[16,2048]{1,0:T(8,128)}, f32[16,1024]{1,0:T(8,128)}, f32[16,2048]{1,0:T(8,128)}) custom-call(f32[16,3072]{1,0:T(8,128)S(1)} %shard_map.161.refs_0_, f32[2,16,3072]{2,1,0:T(8,128)S(1)} %get-tuple-element.77.refs_1_, s16[16,3200]{1,0:T(8,128)(2,1)S(1)} %collective-permute-done.20.refs_2_, ...), custom_call_target="tpu_custom_call" | custom-call | flops 4000000000 | bytes 1048576 | tf_op jit(solution)/shard_map/pallas_call | solution.py:456
  (53 shorter events, 10.4 us)
Async XLA Ops:
  0.6 13.2 %collective-permute-start.1 = (bf16[1024,1024]{1,0:T(8,128)(2,1)}, bf16[1024,1024]{1,0:T(8,128)(2,1)S(1)}, u32[]{:S(2)}, u32[]{:S(2)}) collective-permute-start(bf16[1024,1024]{1,0:T(8,128)(2,1)} %bitcast.23), channel_id=1, source_target_pairs={{0,1},{1,0},{2,3},{3,2},{4,5},{5,4},{6,7},{7,6},{8,9},{9,8},{10,11... | collective-permute-start | bytes 6291464 | tf_op jit(solution)/shard_map/ppermute | solution.py:419
  3.1 8.6 %collective-permute-start.4 = (s16[2,16,3200]{2,1,0:T(8,128)(2,1)}, s16[2,16,3200]{2,1,0:T(8,128)(2,1)S(1)}, u32[]{:S(2)}, u32[]{:S(2)}) collective-permute-start(s16[2,16,3200]{2,1,0:T(8,128)(2,1)} %get-tuple-element.50.refs_4_.refs_2_.refs_8_), channel_id=1, source_target_pairs={{0,2},{1,3},{4,0},{5,1},{8,4},{9,5},{12,8},{13,9},{14,12},{15,13},... | collective-permute-start | bytes 614408 | tf_op jit(solution)/shard_map/ppermute | solution.py:393
  5.7 7.7 %collective-permute-start.3 = (s16[2,16,3200]{2,1,0:T(8,128)(2,1)}, s16[2,16,3200]{2,1,0:T(8,128)(2,1)S(1)}, u32[]{:S(2)}, u32[]{:S(2)}) collective-permute-start(s16[2,16,3200]{2,1,0:T(8,128)(2,1)} %get-tuple-element.50.refs_4_.refs_2_.refs_8_), channel_id=1, source_target_pairs={{0,4},{1,5},{4,8},{5,9},{8,12},{9,13},{12,14},{13,15},{14,10},{15,... | collective-permute-start | bytes 614408 | tf_op jit(solution)/shard_map/ppermute | solution.py:393
  5.8 8.0 %collective-permute-start = (f32[24,128]{1,0:T(8,128)}, f32[24,128]{1,0:T(8,128)S(1)}, u32[]{:S(2)}, u32[]{:S(2)}) collective-permute-start(f32[24,128]{1,0:T(8,128)} %get-tuple-element.43.refs_1_), channel_id=1, source_target_pairs={{0,1},{1,0},{2,3},{3,2},{4,5},{5,4},{6,7},{7,6},{8,9},{9,8},{10,11... | collective-permute-start | bytes 36872 | tf_op jit(solution)/shard_map/ppermute | solution.py:419
  6.0 7.8 %collective-permute-start.2 = (bf16[128,2048]{1,0:T(8,128)(2,1)}, bf16[128,2048]{1,0:T(8,128)(2,1)S(1)}, u32[]{:S(2)}, u32[]{:S(2)}) collective-permute-start(bf16[128,2048]{1,0:T(8,128)(2,1)} %refs_4_.1), channel_id=1, source_target_pairs={{0,1},{1,0},{2,3},{3,2},{4,5},{5,4},{6,7},{7,6},{8,9},{9,8},{10,11... | collective-permute-start | bytes 1572872 | tf_op jit(solution)/shard_map/ppermute | solution.py:419
  11.7 6.9 %collective-permute-start.6 = (s16[2,16,3200]{2,1,0:T(8,128)(2,1)S(1)}, s16[2,16,3200]{2,1,0:T(8,128)(2,1)S(1)}, u32[]{:S(2)}, u32[]{:S(2)}) collective-permute-start(s16[2,16,3200]{2,1,0:T(8,128)(2,1)S(1)} %collective-permute-done.4.refs_6_.refs_4_.refs_10_), channel_id=1, source_target_pairs={{0,2},{1,3},{4,0},{5,1},{8,4},{9,5},{12,8},{13,9},{14,12},{15,13},... | collective-permute-start | bytes 614408 | tf_op jit(solution)/shard_map/ppermute | solution.py:393
  13.4 6.4 %collective-permute-start.5 = (s16[2,16,3200]{2,1,0:T(8,128)(2,1)S(1)}, s16[2,16,3200]{2,1,0:T(8,128)(2,1)S(1)}, u32[]{:S(2)}, u32[]{:S(2)}) collective-permute-start(s16[2,16,3200]{2,1,0:T(8,128)(2,1)S(1)} %collective-permute-done.3.refs_5_.refs_3_.refs_9_), channel_id=1, source_target_pairs={{0,4},{1,5},{4,8},{5,9},{8,12},{9,13},{12,14},{13,15},{14,10},{15,... | collective-permute-start | bytes 614408 | tf_op jit(solution)/shard_map/ppermute | solution.py:393
  13.8 14.2 %copy-start.1 = (s16[2,16,3200]{2,1,0:T(8,128)(2,1)S(1)}, s16[2,16,3200]{2,1,0:T(8,128)(2,1)}, u32[]{:S(2)}) copy-start(s16[2,16,3200]{2,1,0:T(8,128)(2,1)} %get-tuple-element.50.refs_4_.refs_2_.refs_8_) | copy-start | bytes 614404
  14.6 13.5 %copy-start = (bf16[128,8,1024]{2,1,0:T(8,128)(2,1)S(1)}, bf16[128,8,1024]{2,1,0:T(8,128)(2,1)}, u32[]{:S(2)}) copy-start(bf16[128,8,1024]{2,1,0:T(8,128)(2,1)} %param.12) | copy-start | bytes 6291460
  19.8 5.8 %collective-permute-start.7 = (s16[2,16,3200]{2,1,0:T(8,128)(2,1)S(1)}, s16[2,16,3200]{2,1,0:T(8,128)(2,1)S(1)}, u32[]{:S(2)}, u32[]{:S(2)}) collective-permute-start(s16[2,16,3200]{2,1,0:T(8,128)(2,1)S(1)} %get-tuple-element.51.refs_7_.refs_5_.refs_11_), channel_id=1, source_target_pairs={{0,4},{1,5},{4,8},{5,9},{8,12},{9,13},{12,14},{13,15},{14,10},{15,... | collective-permute-start | bytes 614408 | tf_op jit(solution)/shard_map/ppermute | solution.py:393
  20.4 5.9 %collective-permute-start.8 = (s16[2,16,3200]{2,1,0:T(8,128)(2,1)S(1)}, s16[2,16,3200]{2,1,0:T(8,128)(2,1)S(1)}, u32[]{:S(2)}, u32[]{:S(2)}) collective-permute-start(s16[2,16,3200]{2,1,0:T(8,128)(2,1)S(1)} %get-tuple-element.52.refs_6_.refs_5_.refs_12_), channel_id=1, source_target_pairs={{0,2},{1,3},{4,0},{5,1},{8,4},{9,5},{12,8},{13,9},{14,12},{15,13},... | collective-permute-start | bytes 614408 | tf_op jit(solution)/shard_map/ppermute | solution.py:393
  25.6 4.7 %collective-permute-start.9 = (s16[1,16,3200]{2,1,0:T(8,128)(2,1)S(1)}, s16[1,16,3200]{2,1,0:T(8,128)(2,1)S(1)}, u32[]{:S(2)}, u32[]{:S(2)}) collective-permute-start(s16[1,16,3200]{2,1,0:T(8,128)(2,1)S(1)} %slice.8), channel_id=1, source_target_pairs={{0,4},{1,5},{4,8},{5,9},{8,12},{9,13},{12,14},{13,15},{14,10},{15,... | collective-permute-start | bytes 307208 | tf_op jit(solution)/shard_map/ppermute | solution.py:393
  26.3 4.9 %collective-permute-start.11 = (s16[1,16,3200]{2,1,0:T(8,128)(2,1)S(1)}, s16[1,16,3200]{2,1,0:T(8,128)(2,1)S(1)}, u32[]{:S(2)}, u32[]{:S(2)}) collective-permute-start(s16[1,16,3200]{2,1,0:T(8,128)(2,1)S(1)} %slice.9), channel_id=1, source_target_pairs={{0,2},{1,3},{4,0},{5,1},{8,4},{9,5},{12,8},{13,9},{14,12},{15,13},... | collective-permute-start | bytes 307208 | tf_op jit(solution)/shard_map/ppermute | solution.py:393
  30.9 2.3 %collective-permute-start.10 = (f32[8,128]{1,0:T(8,128)S(1)}, f32[8,128]{1,0:T(8,128)S(1)}, u32[]{:S(2)}, u32[]{:S(2)}) collective-permute-start(f32[8,128]{1,0:T(8,128)S(1)} %shard_map.151.refs_0_.refs_4_), channel_id=1, source_target_pairs={{0,1},{1,0},{2,3},{3,2},{4,5},{5,4},{6,7},{7,6},{8,9},{9,8},{10,11... | collective-permute-start | bytes 12296 | tf_op jit(solution)/shard_map/ppermute | solution.py:419
  35.5 7.5 %collective-permute-start.12 = (bf16[256,2048]{1,0:T(8,128)(2,1)S(1)}, bf16[256,2048]{1,0:T(8,128)(2,1)S(1)}, u32[]{:S(2)}, u32[]{:S(2)}) collective-permute-start(bf16[256,2048]{1,0:T(8,128)(2,1)S(1)} %get-tuple-element.61), channel_id=1, source_target_pairs={{0,1},{1,0},{2,3},{3,2},{4,5},{5,4},{6,7},{7,6},{8,9},{9,8},{10,11... | collective-permute-start | bytes 3145736 | tf_op jit(solution)/shard_map/ppermute | solution.py:419
  39.9 7.3 %collective-permute-start.13 = (s16[2,16,3200]{2,1,0:T(8,128)(2,1)S(1)}, s16[2,16,3200]{2,1,0:T(8,128)(2,1)S(1)}, u32[]{:S(2)}, u32[]{:S(2)}) collective-permute-start(s16[2,16,3200]{2,1,0:T(8,128)(2,1)S(1)} %get-tuple-element.63), channel_id=1, source_target_pairs={{0,4},{1,5},{2,6},{3,7},{4,0},{5,1},{6,2},{7,3},{8,12},{9,13},{10,... | collective-permute-start | bytes 614408 | tf_op jit(solution)/shard_map/ppermute | solution.py:419
  41.2 8.2 %collective-permute-start.15 = (s16[2,16,3200]{2,1,0:T(8,128)(2,1)S(1)}, s16[2,16,3200]{2,1,0:T(8,128)(2,1)S(1)}, u32[]{:S(2)}, u32[]{:S(2)}) collective-permute-start(s16[2,16,3200]{2,1,0:T(8,128)(2,1)S(1)} %get-tuple-element.69), channel_id=1, source_target_pairs={{0,2},{1,3},{2,0},{3,1},{4,6},{5,7},{6,4},{7,5},{8,10},{9,11},{10,... | collective-permute-start | bytes 614408 | tf_op jit(solution)/shard_map/ppermute | solution.py:419
  46.3 6.6 %collective-permute-start.14 = (s16[2,16,3200]{2,1,0:T(8,128)(2,1)S(1)}, s16[2,16,3200]{2,1,0:T(8,128)(2,1)S(1)}, u32[]{:S(2)}, u32[]{:S(2)}) collective-permute-start(s16[2,16,3200]{2,1,0:T(8,128)(2,1)S(1)} %get-tuple-element.67), channel_id=1, source_target_pairs={{0,4},{1,5},{2,6},{3,7},{4,0},{5,1},{6,2},{7,3},{8,12},{9,13},{10,... | collective-permute-start | bytes 614408 | tf_op jit(solution)/shard_map/ppermute | solution.py:419
  47.4 6.4 %collective-permute-start.16 = (s16[16,3200]{1,0:T(8,128)(2,1)S(1)}, s16[16,3200]{1,0:T(8,128)(2,1)S(1)}, u32[]{:S(2)}, u32[]{:S(2)}) collective-permute-start(s16[16,3200]{1,0:T(8,128)(2,1)S(1)} %get-tuple-element.66.refs_0_), channel_id=1, source_target_pairs={{0,2},{1,3},{2,0},{3,1},{4,6},{5,7},{6,4},{7,5},{8,10},{9,11},{10,... | collective-permute-start | bytes 307208 | tf_op jit(solution)/shard_map/ppermute | solution.py:419
  48.9 8.3 %collective-permute-start.17 = (s16[2,16,3200]{2,1,0:T(8,128)(2,1)S(1)}, s16[2,16,3200]{2,1,0:T(8,128)(2,1)S(1)}, u32[]{:S(2)}, u32[]{:S(2)}) collective-permute-start(s16[2,16,3200]{2,1,0:T(8,128)(2,1)S(1)} %get-tuple-element.73), channel_id=1, source_target_pairs={{0,2},{1,3},{2,0},{3,1},{4,6},{5,7},{6,4},{7,5},{8,10},{9,11},{10,... | collective-permute-start | bytes 614408 | tf_op jit(solution)/shard_map/ppermute | solution.py:419
  53.1 6.2 %collective-permute-start.18 = (s16[16,3200]{1,0:T(8,128)(2,1)S(1)}, s16[16,3200]{1,0:T(8,128)(2,1)S(1)}, u32[]{:S(2)}, u32[]{:S(2)}) collective-permute-start(s16[16,3200]{1,0:T(8,128)(2,1)S(1)} %get-tuple-element.70.refs_0_), channel_id=1, source_target_pairs={{0,2},{1,3},{2,0},{3,1},{4,6},{5,7},{6,4},{7,5},{8,10},{9,11},{10,... | collective-permute-start | bytes 307208 | tf_op jit(solution)/shard_map/ppermute | solution.py:419
  53.9 8.3 %collective-permute-start.19 = (s16[16,3200]{1,0:T(8,128)(2,1)S(1)}, s16[16,3200]{1,0:T(8,128)(2,1)S(1)}, u32[]{:S(2)}, u32[]{:S(2)}) collective-permute-start(s16[16,3200]{1,0:T(8,128)(2,1)S(1)} %shard_map.158.refs_0_), channel_id=1, source_target_pairs={{0,8},{1,9},{2,10},{3,11},{4,12},{5,13},{6,14},{7,15},{8,0},{9,1},... | collective-permute-start | bytes 307208 | tf_op jit(solution)/shard_map/ppermute | solution.py:419
  57.4 8.3 %collective-permute-start.21 = (s16[2,16,3200]{2,1,0:T(8,128)(2,1)S(1)}, s16[2,16,3200]{2,1,0:T(8,128)(2,1)S(1)}, u32[]{:S(2)}, u32[]{:S(2)}) collective-permute-start(s16[2,16,3200]{2,1,0:T(8,128)(2,1)S(1)} %get-tuple-element.75.refs_0_), channel_id=1, source_target_pairs={{0,4},{1,5},{2,6},{3,7},{4,0},{5,1},{6,2},{7,3},{8,12},{9,13},{10,... | collective-permute-start | bytes 614408 | tf_op jit(solution)/shard_map/ppermute | solution.py:419
  59.5 6.2 %collective-permute-start.20 = (s16[16,3200]{1,0:T(8,128)(2,1)S(1)}, s16[16,3200]{1,0:T(8,128)(2,1)S(1)}, u32[]{:S(2)}, u32[]{:S(2)}) collective-permute-start(s16[16,3200]{1,0:T(8,128)(2,1)S(1)} %shard_map.160.refs_0_), channel_id=1, source_target_pairs={{0,8},{1,9},{2,10},{3,11},{4,12},{5,13},{6,14},{7,15},{8,0},{9,1},... | collective-permute-start | bytes 307208 | tf_op jit(solution)/shard_map/ppermute | solution.py:419
  (3 other events, 11.5 us)

commit v19 on v18

--- a/solution.py
+++ b/solution.py
@@ -194,11 +194,34 @@
     return limits
 
 
+def unpack_kernel(slots, hidden_width, place_ref, *refs):
+    piece_refs, (high_ref, low_ref) = refs[:-2], refs[-2:]
+    for arrival in range(slots):
+        slot = place_ref[1 + 2 * slots + arrival]
+        for kind in range(2):
+            if arrival < len(piece_refs):
+                _, up = decode(piece_refs[arrival][kind], hidden_width)
+                high_ref[kind, slot], low_ref[kind, slot] = halves(up)
+            else:
+                high_ref[kind, slot] = low_ref[kind, slot] = jnp.zeros(high_ref.shape[2:], bf16)
+
+
 def tangent_kernel(
-    slots, place_ref, rank_ref, gate_ref, capacity_ref, prior_ref, arrived_ref, early_ref, late_ref, *rest
+    slots,
+    place_ref,
+    rank_ref,
+    gate_ref,
+    capacity_ref,
+    prior_ref,
+    arrived_ref,
+    early_ref,
+    late_ref,
+    most_high_ref,
+    most_low_ref,
+    *rest,
 ):
-    piece_refs = rest[: slots + 1]
-    weight_ref, weighted_ref, tangent_ref, coded_ref, high_ref, low_ref = rest[slots + 1 :]
+    piece_refs = rest[:2]
+    weight_ref, weighted_ref, tangent_ref, coded_ref, high_ref, low_ref = rest[2:]
     _, wide = weight_ref.shape
     model_width = tangent_ref.shape[1]
     hidden_width = piece_refs[0].shape[2] - model_width - lanes
@@ -221,11 +244,11 @@
     reduced = [sum(dot(part, order, 1, 0) for part in halves(both)) for both in reduced]
     weighted = jnp.concatenate([weight * part for part in reduced], axis=1)
     weighted_ref[...] = weighted
-    for arrival in range(slots):
-        for kind in range(2):
-            _, up = decode(piece_part(piece_refs, arrival, kind, True), hidden_width)
-            slot = place_ref[1 + 2 * slots + arrival]
-            high_ref[kind, slot], low_ref[kind, slot] = halves(up)
+    high_ref[...], low_ref[...] = most_high_ref[...], most_low_ref[...]
+    slot = place_ref[3 * slots]
+    for kind, piece_ref in enumerate(piece_refs):
+        _, up = decode(piece_ref[0], hidden_width)
+        high_ref[kind, slot], low_ref[kind, slot] = halves(up)
     factor = high_ref[...].reshape(2 * wide, model_width), low_ref[...].reshape(2 * wide, model_width)
     tangent = dot_pairs(halves(weighted), factor, 1, 0)
     tangent_ref[...] = tangent
@@ -407,8 +430,8 @@
         for step in range(1, half):
             behind = self.shift(behind, 1)
             ahead = self.shift(ahead, -1)
-            if step == 2:
-                behind, ahead = passing(behind, ahead)
+            if step > 1:
+                behind, ahead = passing(behind, ahead, pieces)
             pieces += [behind, ahead]
         pieces += [self.shift(behind[:1], 1), self.shift(ahead[1:], -1)]
         return pieces
@@ -507,12 +530,6 @@
         exchange(output_gradient, 1),
         scratch=[pltpu.SemaphoreType.DMA((2,))],
     )
-    def passing(behind, ahead):
-        return call(pass_kernel, 10**8, [(piece.shape, i16)] * 2, behind, ahead, after=[same])
-
-    pieces = ring.gather(piece, passing)
-    capacity_row = jnp.pad(capacity.astype(f32), (counts_lane, lanes - counts_lane - experts))[None, :]
-
     def reduced(first, count, halved, *parts, after=()):
         return call(
             functools.partial(reduce_kernel, top, first, count, halved),
@@ -528,8 +545,24 @@
         )[0]
 
     early = slots // 2
-    reduced_early = reduced(0, early, False, *pieces[:early])
-    (prior,) = call(prior_kernel, 10**8, [((8, lanes), f32)], *place, *pieces[:-1], after=[reduced_early])
+    first_half = []
+
+    def passing(behind, ahead, pieces):
+        beside = same
+        if len(pieces) > early:
+            beside = reduced(0, early, False, *pieces[:early])
+            first_half.append(beside)
+        return call(pass_kernel, 10**8, [(piece.shape, i16)] * 2, behind, ahead, after=[beside])
+
+    pieces = ring.gather(piece, passing)
+    capacity_row = jnp.pad(capacity.astype(f32), (counts_lane, lanes - counts_lane - experts))[None, :]
+
+    (reduced_early,) = first_half
+    up_halves = [((2, slots, rank, model_width), bf16)] * 2
+    high, low = call(
+        functools.partial(unpack_kernel, slots, hidden_width), 10**8, up_halves, *place, *pieces[:-2]
+    )
+    (prior,) = call(prior_kernel, 10**8, [((8, lanes), f32)], *place, *pieces[:-1], after=[high])
     prior_arrived = exchange(prior, 1)
     reduced_late = reduced(early, slots - early, True, *pieces[early:], after=[prior])
     weight, weighted, tangent, coded, high, low = call(
@@ -540,9 +573,8 @@
             ((both, 2 * wide), f32),
             ((both, model_width), f32),
             ((both, model_width), bf16),
-            ((2, slots, rank, model_width), bf16),
-            ((2, slots, rank, model_width), bf16),
-        ],
+        ]
+        + up_halves,
         *place,
         local_rank,
         gate,
@@ -551,7 +583,9 @@
         prior_arrived,
         reduced_early,
         reduced_late,
-        *pieces,
+        high,
+        low,
+        *pieces[-2:],
     )
     arrived = exchange(coded, 1)
     left = [pltpu.VMEM((2, top * tokens, 2 * wide), bf16)]

time: 66.9 us -> 68.1 us (1.018)
  waiting for transfers between devices: 19.1 us -> 21.4 us
  starting transfers between devices: 24.2 us -> 22.4 us
  Pallas kernels: 20.2 us -> 20.9 us
    ppermute x14, starting transfers between devices: 15.1 us -> 13.5 us  [exchange(): lax.ppermute(value, 'expert', [(device, device ^ mask) for device in rang...]
    ppermute x14, waiting for transfers between devices: 7.74 us -> 9.02 us  [exchange(): lax.ppermute(value, 'expert', [(device, device ^ mask) for device in rang...]
    ppermute x8, waiting for transfers between devices: 11.3 us -> 12.3 us  [shift(): return lax.ppermute(value, 'expert', pairs)]
    pallas_call x16 -> x18, Pallas kernels: 20.2 us -> 20.9 us  [call(): pl.pallas_call(lambda *refs: kernel(*refs[len(after):]), out_shape=[jax.S...]
  transfers between devices with their start and end apart: 22 -> 22, of which waited for: 10 -> 10; matrix products, arithmetic and copies ran while one was open for 2% -> 2% of each run, Pallas kernels for 26% -> 27%
where the time goes in v19:
time: 68.1 us; the launch traced here: 67.8 us
  starting transfers between devices  22.4 us (33%)
  waiting for transfers between devices  21.4 us (31%)
  Pallas kernels  20.9 us (31%)
  other arithmetic  1.43 us (2%)
  local copies, waits for them, and re-layouts  0.96 us (1%)
  between operations  0.85 us (1%)
    pallas_call x18, Pallas kernels, call(): pl.pallas_call(lambda *refs: kernel(*refs[len(after):]), out_shape=[jax.S...  20.9 us
    ppermute x14, starting transfers between devices, exchange(): lax.ppermute(value, 'expert', [(device, device ^ mask) for device in rang...  13.5 us
    ppermute x8, waiting for transfers between devices, shift(): return lax.ppermute(value, 'expert', pairs)  12.3 us
    ppermute x14, waiting for transfers between devices, exchange(): lax.ppermute(value, 'expert', [(device, device ^ mask) for device in rang...  9.02 us
    ppermute x8, starting transfers between devices, shift(): return lax.ppermute(value, 'expert', pairs)  8.89 us
  transfers between devices with their start and end apart: 22, of which 10 were waited for; matrix products, arithmetic and copies ran while one was open for 2% of the time, Pallas kernels for 27%

profile of v19, /device:TPU:0, one launch (start us, length us, event | category | flops | bytes accessed | tf_op | source)
XLA Modules:
  0.0 67.8 jit_solution(17477648164026777450)
XLA Ops:
  1.2 2.0 %shard_map.147 = (s16[2,16,3200]{2,1,0:T(8,128)(2,1)}, f32[24,128]{1,0:T(8,128)}) custom-call(s32[8,128]{1,0:T(8,128)} %bitcast.32, bf16[8,128]{1,0:T(8,128)(2,1)} %bitcast.33, f32[1,128]{1,0:T(1,128)} %bitcast.34, f32[16,1024]{1,0:T(8,128)} %bitcast.30, f32[16,1024]{1,0:T(8,128)} %bitcast.31, f32[16,2048]{1,0:T(8,128)} %bitcast.28, f32[16,2048]{1,0:T(8,128)} %bitcast.29), custom_call_target="tpu_custom_call" | custom-call | flops 200000000 | bytes 1048576 | tf_op jit(solution)/shard_map/pallas_call | solution.py:479
  3.1 2.6 %collective-permute-start.4 = (s16[2,16,3200]{2,1,0:T(8,128)(2,1)}, s16[2,16,3200]{2,1,0:T(8,128)(2,1)S(1)}, u32[]{:S(2)}, u32[]{:S(2)}) collective-permute-start(s16[2,16,3200]{2,1,0:T(8,128)(2,1)} %get-tuple-element.54.refs_4_.refs_1_.refs_2_), channel_id=1, source_target_pairs={{0,2},{1,3},{4,0},{5,1},{8,4},{9,5},{12,8},{13,9},{14,12},{15,13},... | collective-permute-start | bytes 614408 | tf_op jit(solution)/shard_map/ppermute | solution.py:416
  7.7 4.0 %collective-permute-done.4.refs_6_.refs_3_.refs_4_ = s16[2,16,3200]{2,1,0:T(8,128)(2,1)S(1)} collective-permute-done((s16[2,16,3200]{2,1,0:T(8,128)(2,1)}, s16[2,16,3200]{2,1,0:T(8,128)(2,1)S(1)}, u32[]{:S(2)}, u32[]{:S(2)}) %collective-permute-start.4) | collective-permute-done | bytes 204832 | tf_op jit(solution)/shard_map/ppermute | solution.py:416
  11.7 1.7 %collective-permute-start.6 = (s16[2,16,3200]{2,1,0:T(8,128)(2,1)S(1)}, s16[2,16,3200]{2,1,0:T(8,128)(2,1)S(1)}, u32[]{:S(2)}, u32[]{:S(2)}) collective-permute-start(s16[2,16,3200]{2,1,0:T(8,128)(2,1)S(1)} %collective-permute-done.4.refs_6_.refs_3_.refs_4_), channel_id=1, source_target_pairs={{0,2},{1,3},{4,0},{5,1},{8,4},{9,5},{12,8},{13,9},{14,12},{15,13},... | collective-permute-start | bytes 614408 | tf_op jit(solution)/shard_map/ppermute | solution.py:416
  14.7 2.2 %shard_map.148 = (f32[256,24]{1,0:T(8,128)S(1)}, f32[2,128,128]{2,1,0:T(8,128)S(1)}, f32[2,128,128]{2,1,0:T(8,128)S(1)}, bf16[1024,128]{1,0:T(8,128)(2,1)S(1)}, ...) custom-call(s32[25]{0:T(128)S(1)} %pad_add_fusion.refs_0_.refs_1_, ...), custom_call_target="tpu_custom_call" | custom-call | flops 2000000000 | bytes 1048576 | tf_op jit(solution)/shard_map/pallas_call | solution.py:479
  16.9 1.7 %collective-permute-done.6.refs_2_ = s16[2,16,3200]{2,1,0:T(8,128)(2,1)S(1)} collective-permute-done((s16[2,16,3200]{2,1,0:T(8,128)(2,1)S(1)}, s16[2,16,3200]{2,1,0:T(8,128)(2,1)S(1)}, u32[]{:S(2)}, u32[]{:S(2)}) %collective-permute-start.6) | collective-permute-done | bytes 204832 | tf_op jit(solution)/shard_map/ppermute | solution.py:416
  18.6 1.2 %collective-permute-done.5.refs_1_ = s16[2,16,3200]{2,1,0:T(8,128)(2,1)S(1)} collective-permute-done((s16[2,16,3200]{2,1,0:T(8,128)(2,1)S(1)}, s16[2,16,3200]{2,1,0:T(8,128)(2,1)S(1)}, u32[]{:S(2)}, u32[]{:S(2)}) %collective-permute-start.5) | collective-permute-done | bytes 204832 | tf_op jit(solution)/shard_map/ppermute | solution.py:416
  20.4 1.5 %collective-permute-start.8 = (s16[2,16,3200]{2,1,0:T(8,128)(2,1)S(1)}, s16[2,16,3200]{2,1,0:T(8,128)(2,1)S(1)}, u32[]{:S(2)}, u32[]{:S(2)}) collective-permute-start(s16[2,16,3200]{2,1,0:T(8,128)(2,1)S(1)} %get-tuple-element.56.refs_5_.refs_6_), channel_id=1, source_target_pairs={{0,2},{1,3},{4,0},{5,1},{8,4},{9,5},{12,8},{13,9},{14,12},{15,13},... | collective-permute-start | bytes 614408 | tf_op jit(solution)/shard_map/ppermute | solution.py:416
  21.9 2.0 %shard_map.150.refs_0_.refs_6_ = f32[256,128]{1,0:T(8,128)S(1)} custom-call(s32[25]{0:T(128)S(1)} %pad_add_fusion.refs_0_.refs_1_, f32[256,24]{1,0:T(8,128)S(1)} %get-tuple-element.48.refs_1_.refs_2_.refs_0_, bf16[1024,1024]{1,0:T(8,128)(2,1)S(1)} %bitcast.24, bf16[1024,1024]{1,0:T(8,128)(2,1)S(1)} %get-tuple-element.51.refs_3_.refs_4_, ...), custom_call_target="tpu_custom_call" | custom-call | flops 1073741824 | bytes 1048576 | tf_op jit(solution)/shard_map/pallas_call | solution.py:479
  23.9 1.7 %collective-permute-done.7.refs_1_ = s16[2,16,3200]{2,1,0:T(8,128)(2,1)S(1)} collective-permute-done((s16[2,16,3200]{2,1,0:T(8,128)(2,1)S(1)}, s16[2,16,3200]{2,1,0:T(8,128)(2,1)S(1)}, u32[]{:S(2)}, u32[]{:S(2)}) %collective-permute-start.7) | collective-permute-done | bytes 204832 | tf_op jit(solution)/shard_map/ppermute | solution.py:416
  26.3 1.6 %collective-permute-start.11 = (s16[1,16,3200]{2,1,0:T(8,128)(2,1)S(1)}, s16[1,16,3200]{2,1,0:T(8,128)(2,1)S(1)}, u32[]{:S(2)}, u32[]{:S(2)}) collective-permute-start(s16[1,16,3200]{2,1,0:T(8,128)(2,1)S(1)} %slice.7), channel_id=1, source_target_pairs={{0,2},{1,3},{4,0},{5,1},{8,4},{9,5},{12,8},{13,9},{14,12},{15,13},... | collective-permute-start | bytes 307208 | tf_op jit(solution)/shard_map/ppermute | solution.py:416
  28.4 1.0 %shard_map.152 = (bf16[2,8,16,2048]{3,2,1,0:T(8,128)(2,1)S(1)}, bf16[2,8,16,2048]{3,2,1,0:T(8,128)(2,1)S(1)}) custom-call(s32[25]{0:T(128)S(1)} %pad_add_fusion.refs_0_.refs_1_, s16[2,16,3200]{2,1,0:T(8,128)(2,1)S(1)} %copy-done.1, s16[2,16,3200]{2,1,0:T(8,128)(2,1)S(1)} %collective-permute-done.3.refs_5_.refs_2_.refs_3_, ...), custom_call_target="tpu_custom_call" | custom-call | flops 200000000 | bytes 1048576 | tf_op jit(solution)/shard_map/pallas_call | solution.py:479
  29.5 3.1 %collective-permute-done.9.refs_9_.refs_8_.refs_10_ = s16[1,16,3200]{2,1,0:T(8,128)(2,1)S(1)} collective-permute-done((s16[1,16,3200]{2,1,0:T(8,128)(2,1)S(1)}, s16[1,16,3200]{2,1,0:T(8,128)(2,1)S(1)}, u32[]{:S(2)}, u32[]{:S(2)}) %collective-permute-start.9) | collective-permute-done | bytes 102432 | tf_op jit(solution)/shard_map/ppermute | solution.py:416
  33.2 2.0 %shard_map.154.refs_7_ = f32[256,128]{1,0:T(8,128)S(1)} custom-call(f32[8,128]{1,0:T(8,128)S(1)} %shard_map.153.refs_0_.refs_4_, s32[25]{0:T(128)S(1)} %pad_add_fusion.refs_0_.refs_1_, f32[256,24]{1,0:T(8,128)S(1)} %get-tuple-element.48.refs_1_.refs_2_.refs_0_, bf16[1024,1024]{1,0:T(8,128)(2,1)S(1)} %bitcast.25, ...), custom_call_target="tpu_custom_call" | custom-call | flops 1073741824 | bytes 1048576 | tf_op jit(solution)/shard_map/pallas_call | solution.py:479
  35.3 1.9 %shard_map.155 = (f32[256,128]{1,0:T(8,128)S(1)}, f32[256,256]{1,0:T(8,128)S(1)}, f32[256,2048]{1,0:T(8,128)S(1)}, bf16[256,2048]{1,0:T(8,128)(2,1)S(1)}, bf16[2...) custom-call(s32[25]{0:T(128)S(1)} %pad_add_fusion.refs_0_.refs_1_, ...), custom_call_target="tpu_custom_call" | custom-call | flops 805306368 | bytes 1048576 | tf_op jit(solution)/shard_map/pallas_call | solution.py:479
  37.7 4.0 %shard_map.156 = (f32[2,16,3072]{2,1,0:T(8,128)S(1)}, s16[2,16,3200]{2,1,0:T(8,128)(2,1)S(1)}, f32[2,16,3072]{2,1,0:T(8,128)S(1)}, s16[2,16,3200]{2,1,0:T(8,128)...) custom-call(bf16[1024,128]{1,0:T(8,128)(2,1)S(1)} %get-tuple-element.49.refs_0_.refs_1_, ...), custom_call_target="tpu_custom_call" | custom-call | flops 2147483648 | bytes 1048576 | tf_op jit(solution)/shard_map/pallas_call | solution.py:479
  42.2 2.7 %collective-permute-start.15 = (s16[2,16,3200]{2,1,0:T(8,128)(2,1)S(1)}, s16[2,16,3200]{2,1,0:T(8,128)(2,1)S(1)}, u32[]{:S(2)}, u32[]{:S(2)}) collective-permute-start(s16[2,16,3200]{2,1,0:T(8,128)(2,1)S(1)} %get-tuple-element.77), channel_id=1, source_target_pairs={{0,2},{1,3},{2,0},{3,1},{4,6},{5,7},{6,4},{7,5},{8,10},{9,11},{10,... | collective-permute-start | bytes 614408 | tf_op jit(solution)/shard_map/ppermute | solution.py:442
  44.9 3.2 %shard_map.157 = (f32[2,16,3072]{2,1,0:T(8,128)S(1)}, s16[2,16,3200]{2,1,0:T(8,128)(2,1)S(1)}, f32[2,16,3072]{2,1,0:T(8,128)S(1)}, s16[2,16,3200]{2,1,0:T(8,128)(2,1)S(1)}) custom-call(f32[256,24]{1,0:T(8,128)S(1)} %get-tuple-element.48.refs_1_.refs_2_.refs_0_, bf16[1024,128]{1,0:T(8,128)(2,1)S(1)} %get-tuple-element.49.refs_0_.refs_1_, ...), custom_call_target="tpu_custom_call" | custom-call | flops 1879048192 | bytes 1048576 | tf_op jit(solution)/shard_map/pallas_call | solution.py:479
  49.0 1.6 %collective-permute-start.16 = (s16[16,3200]{1,0:T(8,128)(2,1)S(1)}, s16[16,3200]{1,0:T(8,128)(2,1)S(1)}, u32[]{:S(2)}, u32[]{:S(2)}) collective-permute-start(s16[16,3200]{1,0:T(8,128)(2,1)S(1)} %get-tuple-element.74.refs_0_), channel_id=1, source_target_pairs={{0,2},{1,3},{2,0},{3,1},{4,6},{5,7},{6,4},{7,5},{8,10},{9,11},{10,... | collective-permute-start | bytes 307208 | tf_op jit(solution)/shard_map/ppermute | solution.py:442
  51.1 3.6 %collective-permute-done.14.refs_1_ = s16[2,16,3200]{2,1,0:T(8,128)(2,1)S(1)} collective-permute-done((s16[2,16,3200]{2,1,0:T(8,128)(2,1)S(1)}, s16[2,16,3200]{2,1,0:T(8,128)(2,1)S(1)}, u32[]{:S(2)}, u32[]{:S(2)}) %collective-permute-start.14) | collective-permute-done | bytes 204832 | tf_op jit(solution)/shard_map/ppermute | solution.py:442
  55.5 2.3 %collective-permute-start.19 = (s16[16,3200]{1,0:T(8,128)(2,1)S(1)}, s16[16,3200]{1,0:T(8,128)(2,1)S(1)}, u32[]{:S(2)}, u32[]{:S(2)}) collective-permute-start(s16[16,3200]{1,0:T(8,128)(2,1)S(1)} %shard_map.160.refs_0_), channel_id=1, source_target_pairs={{0,8},{1,9},{2,10},{3,11},{4,12},{5,13},{6,14},{7,15},{8,0},{9,1},... | collective-permute-start | bytes 307208 | tf_op jit(solution)/shard_map/ppermute | solution.py:442
  59.0 1.6 %collective-permute-start.21 = (s16[2,16,3200]{2,1,0:T(8,128)(2,1)S(1)}, s16[2,16,3200]{2,1,0:T(8,128)(2,1)S(1)}, u32[]{:S(2)}, u32[]{:S(2)}) collective-permute-start(s16[2,16,3200]{2,1,0:T(8,128)(2,1)S(1)} %get-tuple-element.83.refs_0_), channel_id=1, source_target_pairs={{0,4},{1,5},{2,6},{3,7},{4,0},{5,1},{6,2},{7,3},{8,12},{9,13},{10,... | collective-permute-start | bytes 614408 | tf_op jit(solution)/shard_map/ppermute | solution.py:442
  60.8 1.7 %collective-permute-start.20 = (s16[16,3200]{1,0:T(8,128)(2,1)S(1)}, s16[16,3200]{1,0:T(8,128)(2,1)S(1)}, u32[]{:S(2)}, u32[]{:S(2)}) collective-permute-start(s16[16,3200]{1,0:T(8,128)(2,1)S(1)} %shard_map.162.refs_0_), channel_id=1, source_target_pairs={{0,8},{1,9},{2,10},{3,11},{4,12},{5,13},{6,14},{7,15},{8,0},{9,1},... | collective-permute-start | bytes 307208 | tf_op jit(solution)/shard_map/ppermute | solution.py:442
  62.6 4.4 %collective-permute-done.21.refs_3_ = s16[2,16,3200]{2,1,0:T(8,128)(2,1)S(1)} collective-permute-done((s16[2,16,3200]{2,1,0:T(8,128)(2,1)S(1)}, s16[2,16,3200]{2,1,0:T(8,128)(2,1)S(1)}, u32[]{:S(2)}, u32[]{:S(2)}) %collective-permute-start.21) | collective-permute-done | bytes 204832 | tf_op jit(solution)/shard_map/ppermute | solution.py:442
  (55 shorter events, 11.7 us)
Async XLA Ops:
  0.6 13.2 %collective-permute-start.1 = (bf16[1024,1024]{1,0:T(8,128)(2,1)}, bf16[1024,1024]{1,0:T(8,128)(2,1)S(1)}, u32[]{:S(2)}, u32[]{:S(2)}) collective-permute-start(bf16[1024,1024]{1,0:T(8,128)(2,1)} %bitcast.23), channel_id=1, source_target_pairs={{0,1},{1,0},{2,3},{3,2},{4,5},{5,4},{6,7},{7,6},{8,9},{9,8},{10,11... | collective-permute-start | bytes 6291464 | tf_op jit(solution)/shard_map/ppermute | solution.py:442
  3.1 8.6 %collective-permute-start.4 = (s16[2,16,3200]{2,1,0:T(8,128)(2,1)}, s16[2,16,3200]{2,1,0:T(8,128)(2,1)S(1)}, u32[]{:S(2)}, u32[]{:S(2)}) collective-permute-start(s16[2,16,3200]{2,1,0:T(8,128)(2,1)} %get-tuple-element.54.refs_4_.refs_1_.refs_2_), channel_id=1, source_target_pairs={{0,2},{1,3},{4,0},{5,1},{8,4},{9,5},{12,8},{13,9},{14,12},{15,13},... | collective-permute-start | bytes 614408 | tf_op jit(solution)/shard_map/ppermute | solution.py:416
  5.7 7.7 %collective-permute-start.3 = (s16[2,16,3200]{2,1,0:T(8,128)(2,1)}, s16[2,16,3200]{2,1,0:T(8,128)(2,1)S(1)}, u32[]{:S(2)}, u32[]{:S(2)}) collective-permute-start(s16[2,16,3200]{2,1,0:T(8,128)(2,1)} %get-tuple-element.54.refs_4_.refs_1_.refs_2_), channel_id=1, source_target_pairs={{0,4},{1,5},{4,8},{5,9},{8,12},{9,13},{12,14},{13,15},{14,10},{15,... | collective-permute-start | bytes 614408 | tf_op jit(solution)/shard_map/ppermute | solution.py:416
  5.8 8.0 %collective-permute-start = (f32[24,128]{1,0:T(8,128)}, f32[24,128]{1,0:T(8,128)S(1)}, u32[]{:S(2)}, u32[]{:S(2)}) collective-permute-start(f32[24,128]{1,0:T(8,128)} %get-tuple-element.47.refs_1_), channel_id=1, source_target_pairs={{0,1},{1,0},{2,3},{3,2},{4,5},{5,4},{6,7},{7,6},{8,9},{9,8},{10,11... | collective-permute-start | bytes 36872 | tf_op jit(solution)/shard_map/ppermute | solution.py:442
  6.0 7.8 %collective-permute-start.2 = (bf16[128,2048]{1,0:T(8,128)(2,1)}, bf16[128,2048]{1,0:T(8,128)(2,1)S(1)}, u32[]{:S(2)}, u32[]{:S(2)}) collective-permute-start(bf16[128,2048]{1,0:T(8,128)(2,1)} %refs_4_.1), channel_id=1, source_target_pairs={{0,1},{1,0},{2,3},{3,2},{4,5},{5,4},{6,7},{7,6},{8,9},{9,8},{10,11... | collective-permute-start | bytes 1572872 | tf_op jit(solution)/shard_map/ppermute | solution.py:442
  11.7 6.9 %collective-permute-start.6 = (s16[2,16,3200]{2,1,0:T(8,128)(2,1)S(1)}, s16[2,16,3200]{2,1,0:T(8,128)(2,1)S(1)}, u32[]{:S(2)}, u32[]{:S(2)}) collective-permute-start(s16[2,16,3200]{2,1,0:T(8,128)(2,1)S(1)} %collective-permute-done.4.refs_6_.refs_3_.refs_4_), channel_id=1, source_target_pairs={{0,2},{1,3},{4,0},{5,1},{8,4},{9,5},{12,8},{13,9},{14,12},{15,13},... | collective-permute-start | bytes 614408 | tf_op jit(solution)/shard_map/ppermute | solution.py:416
  13.4 6.4 %collective-permute-start.5 = (s16[2,16,3200]{2,1,0:T(8,128)(2,1)S(1)}, s16[2,16,3200]{2,1,0:T(8,128)(2,1)S(1)}, u32[]{:S(2)}, u32[]{:S(2)}) collective-permute-start(s16[2,16,3200]{2,1,0:T(8,128)(2,1)S(1)} %collective-permute-done.3.refs_5_.refs_2_.refs_3_), channel_id=1, source_target_pairs={{0,4},{1,5},{4,8},{5,9},{8,12},{9,13},{12,14},{13,15},{14,10},{15,... | collective-permute-start | bytes 614408 | tf_op jit(solution)/shard_map/ppermute | solution.py:416
  13.7 8.2 %copy-start.4 = (s32[16]{0:T(128)S(1)}, s32[16]{0:T(128)}, u32[]{:S(2)}) copy-start(s32[16]{0:T(128)} %param.15) | copy-start | bytes 196
  13.8 8.1 %copy-start.1 = (s16[2,16,3200]{2,1,0:T(8,128)(2,1)S(1)}, s16[2,16,3200]{2,1,0:T(8,128)(2,1)}, u32[]{:S(2)}) copy-start(s16[2,16,3200]{2,1,0:T(8,128)(2,1)} %get-tuple-element.54.refs_4_.refs_1_.refs_2_) | copy-start | bytes 614404
  19.8 5.8 %collective-permute-start.7 = (s16[2,16,3200]{2,1,0:T(8,128)(2,1)S(1)}, s16[2,16,3200]{2,1,0:T(8,128)(2,1)S(1)}, u32[]{:S(2)}, u32[]{:S(2)}) collective-permute-start(s16[2,16,3200]{2,1,0:T(8,128)(2,1)S(1)} %get-tuple-element.55.refs_7_.refs_4_.refs_5_), channel_id=1, source_target_pairs={{0,4},{1,5},{4,8},{5,9},{8,12},{9,13},{12,14},{13,15},{14,10},{15,... | collective-permute-start | bytes 614408 | tf_op jit(solution)/shard_map/ppermute | solution.py:416
  20.4 5.8 %collective-permute-start.8 = (s16[2,16,3200]{2,1,0:T(8,128)(2,1)S(1)}, s16[2,16,3200]{2,1,0:T(8,128)(2,1)S(1)}, u32[]{:S(2)}, u32[]{:S(2)}) collective-permute-start(s16[2,16,3200]{2,1,0:T(8,128)(2,1)S(1)} %get-tuple-element.56.refs_5_.refs_6_), channel_id=1, source_target_pairs={{0,2},{1,3},{4,0},{5,1},{8,4},{9,5},{12,8},{13,9},{14,12},{15,13},... | collective-permute-start | bytes 614408 | tf_op jit(solution)/shard_map/ppermute | solution.py:416
  26.3 7.0 %collective-permute-start.11 = (s16[1,16,3200]{2,1,0:T(8,128)(2,1)S(1)}, s16[1,16,3200]{2,1,0:T(8,128)(2,1)S(1)}, u32[]{:S(2)}, u32[]{:S(2)}) collective-permute-start(s16[1,16,3200]{2,1,0:T(8,128)(2,1)S(1)} %slice.7), channel_id=1, source_target_pairs={{0,2},{1,3},{4,0},{5,1},{8,4},{9,5},{12,8},{13,9},{14,12},{15,13},... | collective-permute-start | bytes 307208 | tf_op jit(solution)/shard_map/ppermute | solution.py:416
  27.9 4.7 %collective-permute-start.9 = (s16[1,16,3200]{2,1,0:T(8,128)(2,1)S(1)}, s16[1,16,3200]{2,1,0:T(8,128)(2,1)S(1)}, u32[]{:S(2)}, u32[]{:S(2)}) collective-permute-start(s16[1,16,3200]{2,1,0:T(8,128)(2,1)S(1)} %slice.6), channel_id=1, source_target_pairs={{0,4},{1,5},{4,8},{5,9},{8,12},{9,13},{12,14},{13,15},{14,10},{15,... | collective-permute-start | bytes 307208 | tf_op jit(solution)/shard_map/ppermute | solution.py:416
  33.1 2.1 %collective-permute-start.10 = (f32[8,128]{1,0:T(8,128)S(1)}, f32[8,128]{1,0:T(8,128)S(1)}, u32[]{:S(2)}, u32[]{:S(2)}) collective-permute-start(f32[8,128]{1,0:T(8,128)S(1)} %shard_map.153.refs_0_.refs_4_), channel_id=1, source_target_pairs={{0,1},{1,0},{2,3},{3,2},{4,5},{5,4},{6,7},{7,6},{8,9},{9,8},{10,11... | collective-permute-start | bytes 12296 | tf_op jit(solution)/shard_map/ppermute | solution.py:442
  37.1 7.8 %collective-permute-start.12 = (bf16[256,2048]{1,0:T(8,128)(2,1)S(1)}, bf16[256,2048]{1,0:T(8,128)(2,1)S(1)}, u32[]{:S(2)}, u32[]{:S(2)}) collective-permute-start(bf16[256,2048]{1,0:T(8,128)(2,1)S(1)} %get-tuple-element.69), channel_id=1, source_target_pairs={{0,1},{1,0},{2,3},{3,2},{4,5},{5,4},{6,7},{7,6},{8,9},{9,8},{10,11... | collective-permute-start | bytes 3145736 | tf_op jit(solution)/shard_map/ppermute | solution.py:442
  41.7 7.1 %collective-permute-start.13 = (s16[2,16,3200]{2,1,0:T(8,128)(2,1)S(1)}, s16[2,16,3200]{2,1,0:T(8,128)(2,1)S(1)}, u32[]{:S(2)}, u32[]{:S(2)}) collective-permute-start(s16[2,16,3200]{2,1,0:T(8,128)(2,1)S(1)} %get-tuple-element.71), channel_id=1, source_target_pairs={{0,4},{1,5},{2,6},{3,7},{4,0},{5,1},{6,2},{7,3},{8,12},{9,13},{10,... | collective-permute-start | bytes 614408 | tf_op jit(solution)/shard_map/ppermute | solution.py:442
  42.2 8.9 %collective-permute-start.15 = (s16[2,16,3200]{2,1,0:T(8,128)(2,1)S(1)}, s16[2,16,3200]{2,1,0:T(8,128)(2,1)S(1)}, u32[]{:S(2)}, u32[]{:S(2)}) collective-permute-start(s16[2,16,3200]{2,1,0:T(8,128)(2,1)S(1)} %get-tuple-element.77), channel_id=1, source_target_pairs={{0,2},{1,3},{2,0},{3,1},{4,6},{5,7},{6,4},{7,5},{8,10},{9,11},{10,... | collective-permute-start | bytes 614408 | tf_op jit(solution)/shard_map/ppermute | solution.py:442
  48.2 6.5 %collective-permute-start.14 = (s16[2,16,3200]{2,1,0:T(8,128)(2,1)S(1)}, s16[2,16,3200]{2,1,0:T(8,128)(2,1)S(1)}, u32[]{:S(2)}, u32[]{:S(2)}) collective-permute-start(s16[2,16,3200]{2,1,0:T(8,128)(2,1)S(1)} %get-tuple-element.75), channel_id=1, source_target_pairs={{0,4},{1,5},{2,6},{3,7},{4,0},{5,1},{6,2},{7,3},{8,12},{9,13},{10,... | collective-permute-start | bytes 614408 | tf_op jit(solution)/shard_map/ppermute | solution.py:442
  49.0 6.3 %collective-permute-start.16 = (s16[16,3200]{1,0:T(8,128)(2,1)S(1)}, s16[16,3200]{1,0:T(8,128)(2,1)S(1)}, u32[]{:S(2)}, u32[]{:S(2)}) collective-permute-start(s16[16,3200]{1,0:T(8,128)(2,1)S(1)} %get-tuple-element.74.refs_0_), channel_id=1, source_target_pairs={{0,2},{1,3},{2,0},{3,1},{4,6},{5,7},{6,4},{7,5},{8,10},{9,11},{10,... | collective-permute-start | bytes 307208 | tf_op jit(solution)/shard_map/ppermute | solution.py:442
  50.6 8.1 %collective-permute-start.17 = (s16[2,16,3200]{2,1,0:T(8,128)(2,1)S(1)}, s16[2,16,3200]{2,1,0:T(8,128)(2,1)S(1)}, u32[]{:S(2)}, u32[]{:S(2)}) collective-permute-start(s16[2,16,3200]{2,1,0:T(8,128)(2,1)S(1)} %get-tuple-element.81), channel_id=1, source_target_pairs={{0,2},{1,3},{2,0},{3,1},{4,6},{5,7},{6,4},{7,5},{8,10},{9,11},{10,... | collective-permute-start | bytes 614408 | tf_op jit(solution)/shard_map/ppermute | solution.py:442
  54.9 5.7 %collective-permute-start.18 = (s16[16,3200]{1,0:T(8,128)(2,1)S(1)}, s16[16,3200]{1,0:T(8,128)(2,1)S(1)}, u32[]{:S(2)}, u32[]{:S(2)}) collective-permute-start(s16[16,3200]{1,0:T(8,128)(2,1)S(1)} %get-tuple-element.78.refs_0_), channel_id=1, source_target_pairs={{0,2},{1,3},{2,0},{3,1},{4,6},{5,7},{6,4},{7,5},{8,10},{9,11},{10,... | collective-permute-start | bytes 307208 | tf_op jit(solution)/shard_map/ppermute | solution.py:442
  55.5 7.1 %collective-permute-start.19 = (s16[16,3200]{1,0:T(8,128)(2,1)S(1)}, s16[16,3200]{1,0:T(8,128)(2,1)S(1)}, u32[]{:S(2)}, u32[]{:S(2)}) collective-permute-start(s16[16,3200]{1,0:T(8,128)(2,1)S(1)} %shard_map.160.refs_0_), channel_id=1, source_target_pairs={{0,8},{1,9},{2,10},{3,11},{4,12},{5,13},{6,14},{7,15},{8,0},{9,1},... | collective-permute-start | bytes 307208 | tf_op jit(solution)/shard_map/ppermute | solution.py:442
  59.0 8.0 %collective-permute-start.21 = (s16[2,16,3200]{2,1,0:T(8,128)(2,1)S(1)}, s16[2,16,3200]{2,1,0:T(8,128)(2,1)S(1)}, u32[]{:S(2)}, u32[]{:S(2)}) collective-permute-start(s16[2,16,3200]{2,1,0:T(8,128)(2,1)S(1)} %get-tuple-element.83.refs_0_), channel_id=1, source_target_pairs={{0,4},{1,5},{2,6},{3,7},{4,0},{5,1},{6,2},{7,3},{8,12},{9,13},{10,... | collective-permute-start | bytes 614408 | tf_op jit(solution)/shard_map/ppermute | solution.py:442
  60.8 6.2 %collective-permute-start.20 = (s16[16,3200]{1,0:T(8,128)(2,1)S(1)}, s16[16,3200]{1,0:T(8,128)(2,1)S(1)}, u32[]{:S(2)}, u32[]{:S(2)}) collective-permute-start(s16[16,3200]{1,0:T(8,128)(2,1)S(1)} %shard_map.162.refs_0_), channel_id=1, source_target_pairs={{0,8},{1,9},{2,10},{3,11},{4,12},{5,13},{6,14},{7,15},{8,0},{9,1},... | collective-permute-start | bytes 307208 | tf_op jit(solution)/shard_map/ppermute | solution.py:442
  (3 other events, 11.4 us)

commit v20 on v16

--- a/solution.py
+++ b/solution.py
@@ -334,7 +334,10 @@
     put_chunks(keep_ref, near_ref, chunk_ref, far_ref, slots // 2, add_halves(down), up_ref[...] + up)
 
 
-def pair_kernel(hidden_width, arrived_ref, chunk_ref, across_ref, keep_ref):
+def pair_kernel(hidden_width, arrived_ref, chunk_ref, *refs):
+    passing, (across_ref, keep_ref) = (refs[:1], refs[1:3]) if len(refs) == 4 else ((), refs)
+    for near_ref in passing:
+        refs[3][...] = near_ref[...]
     for x in range(2):
         down, up = decode(arrived_ref[x], hidden_width)
         down, up = chunk_ref[x, :, :hidden_width] + down, chunk_ref[x, :, hidden_width:] + up
@@ -600,26 +603,35 @@
     curvature_far = exchange(curvature_far, 4)
     gradient_near = exchange(gradient_near, 2)
     pair = [(one_coded, i16), (one, f32)]
-    gradient_across, gradient_pair = hop_call(
-        pair_kernel, pair, gradient_far, gradient_chunk, after=[curvature_keep]
-    )
+    gradient_across, gradient_pair, curvature_near = hop_call(
+        pair_kernel,
+        pair + [(curvature_near.shape, i16)],
+        gradient_far,
+        gradient_chunk,
+        curvature_near,
+        after=[curvature_keep],
+    )
+    curvature_near = exchange(curvature_near, 4)
     curvature_across, curvature_pair = hop_call(
         pair_kernel, pair, curvature_far, curvature_chunk, after=[gradient_across]
     )
-    curvature_near = exchange(curvature_near, 4)
     near = [(one_coded, i16), (one, f32)]
     gradient_onward, gradient_total = hop_call(
         near_kernel, near, gradient_near, gradient_keep, after=[curvature_across]
     )
     gradient_onward = exchange(gradient_onward, 4)
     (gradient_beyond,) = hop_call(
-        far_kernel, [(one_coded, i16)], exchange(gradient_across, 2), gradient_pair, after=[gradient_total, curvature_near]
+        far_kernel, [(one_coded, i16)], exchange(gradient_across, 2), gradient_pair, after=[gradient_total]
+    )
+    curvature_onward, curvature_total = hop_call(
+        near_kernel, near, curvature_near, curvature_keep, after=[gradient_beyond]
     )
     (curvature_beyond,) = hop_call(
-        far_kernel, [(one_coded, i16)], exchange(curvature_across, 2), curvature_pair, after=[gradient_beyond]
-    )
-    curvature_onward, curvature_total = hop_call(
-        near_kernel, near, curvature_near, curvature_keep, after=[curvature_beyond, gradient_onward]
+        far_kernel,
+        [(one_coded, i16)],
+        exchange(curvature_across, 2),
+        curvature_pair,
+        after=[curvature_total, gradient_onward],
     )
     (gradient_total,) = hop_call(
         add_kernel,
@@ -627,7 +639,7 @@
         gradient_total,
         gradient_onward,
         exchange(gradient_beyond, 8),
-        after=[curvature_total],
+        after=[curvature_beyond],
     )
     down_gradient, up_gradient, curvature_down, curvature_up = hop_call(
         total_kernel,

time: 69.7 us -> 68.4 us (0.981)
  waiting for transfers between devices: 22.2 us -> 18.5 us
  starting transfers between devices: 23.9 us -> 26.1 us
    ppermute x15, waiting for transfers between devices: 10.8 us -> 7.2 us  [exchange(): lax.ppermute(value, 'expert', [(device, device ^ mask) for device in rang...]
    ppermute x15, starting transfers between devices: 14.7 us -> 17 us  [exchange(): lax.ppermute(value, 'expert', [(device, device ^ mask) for device in rang...]
where the time goes in v20:
time: 68.4 us; the launch traced here: 68.1 us
  starting transfers between devices  26.1 us (38%)
  Pallas kernels  20.3 us (30%)
  waiting for transfers between devices  18.5 us (27%)
  other arithmetic  1.43 us (2%)
  local copies, waits for them, and re-layouts  0.85 us (1%)
  between operations  0.83 us (1%)
    pallas_call x17, Pallas kernels, call(): pl.pallas_call(lambda *refs: kernel(*refs[len(after):]), out_shape=[jax.S...  20.3 us
    ppermute x15, starting transfers between devices, exchange(): lax.ppermute(value, 'expert', [(device, device ^ mask) for device in rang...  17 us
    ppermute x8, waiting for transfers between devices, shift(): return lax.ppermute(value, 'expert', pairs)  11.3 us
    ppermute x8, starting transfers between devices, shift(): return lax.ppermute(value, 'expert', pairs)  9.12 us
    ppermute x15, waiting for transfers between devices, exchange(): lax.ppermute(value, 'expert', [(device, device ^ mask) for device in rang...  7.2 us
  transfers between devices with their start and end apart: 23, of which 11 were waited for; matrix products, arithmetic and copies ran while one was open for 2% of the time, Pallas kernels for 25%

profile of v20, /device:TPU:0, one launch (start us, length us, event | category | flops | bytes accessed | tf_op | source)
XLA Modules:
  0.0 68.1 jit_solution(6414622852854716991)
XLA Ops:
  1.2 2.0 %shard_map.147 = (s16[2,16,3200]{2,1,0:T(8,128)(2,1)}, f32[24,128]{1,0:T(8,128)}) custom-call(s32[8,128]{1,0:T(8,128)} %bitcast.32, bf16[8,128]{1,0:T(8,128)(2,1)} %bitcast.33, f32[1,128]{1,0:T(1,128)} %bitcast.34, f32[16,1024]{1,0:T(8,128)} %bitcast.30, f32[16,1024]{1,0:T(8,128)} %bitcast.31, f32[16,2048]{1,0:T(8,128)} %bitcast.28, f32[16,2048]{1,0:T(8,128)} %bitcast.29), custom_call_target="tpu_custom_call" | custom-call | flops 200000000 | bytes 1048576 | tf_op jit(solution)/shard_map/pallas_call | solution.py:454
  3.1 2.6 %collective-permute-start.4 = (s16[2,16,3200]{2,1,0:T(8,128)(2,1)}, s16[2,16,3200]{2,1,0:T(8,128)(2,1)S(1)}, u32[]{:S(2)}, u32[]{:S(2)}) collective-permute-start(s16[2,16,3200]{2,1,0:T(8,128)(2,1)} %get-tuple-element.52.refs_4_.refs_2_.refs_8_), channel_id=1, source_target_pairs={{0,2},{1,3},{4,0},{5,1},{8,4},{9,5},{12,8},{13,9},{14,12},{15,13},... | collective-permute-start | bytes 614408 | tf_op jit(solution)/shard_map/ppermute | solution.py:391
  7.7 4.0 %collective-permute-done.4.refs_6_.refs_4_.refs_10_ = s16[2,16,3200]{2,1,0:T(8,128)(2,1)S(1)} collective-permute-done((s16[2,16,3200]{2,1,0:T(8,128)(2,1)}, s16[2,16,3200]{2,1,0:T(8,128)(2,1)S(1)}, u32[]{:S(2)}, u32[]{:S(2)}) %collective-permute-start.4) | collective-permute-done | bytes 204832 | tf_op jit(solution)/shard_map/ppermute | solution.py:391
  11.7 1.7 %collective-permute-start.6 = (s16[2,16,3200]{2,1,0:T(8,128)(2,1)S(1)}, s16[2,16,3200]{2,1,0:T(8,128)(2,1)S(1)}, u32[]{:S(2)}, u32[]{:S(2)}) collective-permute-start(s16[2,16,3200]{2,1,0:T(8,128)(2,1)S(1)} %collective-permute-done.4.refs_6_.refs_4_.refs_10_), channel_id=1, source_target_pairs={{0,2},{1,3},{4,0},{5,1},{8,4},{9,5},{12,8},{13,9},{14,12},{15,13},... | collective-permute-start | bytes 614408 | tf_op jit(solution)/shard_map/ppermute | solution.py:391
  14.6 2.2 %shard_map.148 = (f32[256,24]{1,0:T(8,128)S(1)}, f32[2,128,128]{2,1,0:T(8,128)S(1)}, f32[2,128,128]{2,1,0:T(8,128)S(1)}, bf16[1024,128]{1,0:T(8,128)(2,1)S(1)}, ...) custom-call(s32[25]{0:T(128)S(1)} %pad_add_fusion.refs_0_.refs_1_, ...), custom_call_target="tpu_custom_call" | custom-call | flops 2000000000 | bytes 1048576 | tf_op jit(solution)/shard_map/pallas_call | solution.py:454
  16.8 1.9 %collective-permute-done.6.refs_2_ = s16[2,16,3200]{2,1,0:T(8,128)(2,1)S(1)} collective-permute-done((s16[2,16,3200]{2,1,0:T(8,128)(2,1)S(1)}, s16[2,16,3200]{2,1,0:T(8,128)(2,1)S(1)}, u32[]{:S(2)}, u32[]{:S(2)}) %collective-permute-start.6) | collective-permute-done | bytes 204832 | tf_op jit(solution)/shard_map/ppermute | solution.py:391
  18.6 1.2 %collective-permute-done.5.refs_1_ = s16[2,16,3200]{2,1,0:T(8,128)(2,1)S(1)} collective-permute-done((s16[2,16,3200]{2,1,0:T(8,128)(2,1)S(1)}, s16[2,16,3200]{2,1,0:T(8,128)(2,1)S(1)}, u32[]{:S(2)}, u32[]{:S(2)}) %collective-permute-start.5) | collective-permute-done | bytes 204832 | tf_op jit(solution)/shard_map/ppermute | solution.py:391
  20.4 1.5 %collective-permute-start.8 = (s16[2,16,3200]{2,1,0:T(8,128)(2,1)S(1)}, s16[2,16,3200]{2,1,0:T(8,128)(2,1)S(1)}, u32[]{:S(2)}, u32[]{:S(2)}) collective-permute-start(s16[2,16,3200]{2,1,0:T(8,128)(2,1)S(1)} %get-tuple-element.54.refs_6_.refs_5_.refs_12_), channel_id=1, source_target_pairs={{0,2},{1,3},{4,0},{5,1},{8,4},{9,5},{12,8},{13,9},{14,12},{15,13},... | collective-permute-start | bytes 614408 | tf_op jit(solution)/shard_map/ppermute | solution.py:391
  21.9 3.7 %collective-permute-done.7.refs_7_.refs_6_.refs_13_ = s16[2,16,3200]{2,1,0:T(8,128)(2,1)S(1)} collective-permute-done((s16[2,16,3200]{2,1,0:T(8,128)(2,1)S(1)}, s16[2,16,3200]{2,1,0:T(8,128)(2,1)S(1)}, u32[]{:S(2)}, u32[]{:S(2)}) %collective-permute-start.7) | collective-permute-done | bytes 204832 | tf_op jit(solution)/shard_map/ppermute | solution.py:391
  26.4 1.7 %collective-permute-start.11 = (s16[1,16,3200]{2,1,0:T(8,128)(2,1)S(1)}, s16[1,16,3200]{2,1,0:T(8,128)(2,1)S(1)}, u32[]{:S(2)}, u32[]{:S(2)}) collective-permute-start(s16[1,16,3200]{2,1,0:T(8,128)(2,1)S(1)} %slice.9), channel_id=1, source_target_pairs={{0,2},{1,3},{4,0},{5,1},{8,4},{9,5},{12,8},{13,9},{14,12},{15,13},... | collective-permute-start | bytes 307208 | tf_op jit(solution)/shard_map/ppermute | solution.py:391
  28.0 2.0 %shard_map.150.refs_0_.refs_6_ = f32[256,128]{1,0:T(8,128)S(1)} custom-call(s32[25]{0:T(128)S(1)} %pad_add_fusion.refs_0_.refs_1_, f32[256,24]{1,0:T(8,128)S(1)} %get-tuple-element.46.refs_1_.refs_2_.refs_0_, bf16[1024,1024]{1,0:T(8,128)(2,1)S(1)} %bitcast.24, bf16[1024,1024]{1,0:T(8,128)(2,1)S(1)} %get-tuple-element.49.refs_3_.refs_4_, ...), custom_call_target="tpu_custom_call" | custom-call | flops 1073741824 | bytes 1048576 | tf_op jit(solution)/shard_map/pallas_call | solution.py:454
  31.3 2.0 %shard_map.152.refs_7_ = f32[256,128]{1,0:T(8,128)S(1)} custom-call(f32[8,128]{1,0:T(8,128)S(1)} %shard_map.151.refs_0_.refs_4_, s32[25]{0:T(128)S(1)} %pad_add_fusion.refs_0_.refs_1_, f32[256,24]{1,0:T(8,128)S(1)} %get-tuple-element.46.refs_1_.refs_2_.refs_0_, bf16[1024,1024]{1,0:T(8,128)(2,1)S(1)} %bitcast.25, ...), custom_call_target="tpu_custom_call" | custom-call | flops 1073741824 | bytes 1048576 | tf_op jit(solution)/shard_map/pallas_call | solution.py:454
  33.3 2.3 %shard_map.153 = (f32[256,128]{1,0:T(8,128)S(1)}, f32[256,256]{1,0:T(8,128)S(1)}, f32[256,2048]{1,0:T(8,128)S(1)}, bf16[256,2048]{1,0:T(8,128)(2,1)S(1)}, bf16[2...) custom-call(s32[25]{0:T(128)S(1)} %pad_add_fusion.refs_0_.refs_1_, ...), custom_call_target="tpu_custom_call" | custom-call | flops 805306368 | bytes 1048576 | tf_op jit(solution)/shard_map/pallas_call | solution.py:454
  35.9 4.0 %shard_map.154 = (f32[2,16,3072]{2,1,0:T(8,128)S(1)}, s16[2,16,3200]{2,1,0:T(8,128)(2,1)S(1)}, f32[2,16,3072]{2,1,0:T(8,128)S(1)}, s16[2,16,3200]{2,1,0:T(8,128)...) custom-call(bf16[1024,128]{1,0:T(8,128)(2,1)S(1)} %get-tuple-element.47.refs_0_.refs_1_, ...), custom_call_target="tpu_custom_call" | custom-call | flops 2147483648 | bytes 1048576 | tf_op jit(solution)/shard_map/pallas_call | solution.py:454
  39.9 1.4 %collective-permute-start.13 = (s16[2,16,3200]{2,1,0:T(8,128)(2,1)S(1)}, s16[2,16,3200]{2,1,0:T(8,128)(2,1)S(1)}, u32[]{:S(2)}, u32[]{:S(2)}) collective-permute-start(s16[2,16,3200]{2,1,0:T(8,128)(2,1)S(1)} %get-tuple-element.66), channel_id=1, source_target_pairs={{0,4},{1,5},{2,6},{3,7},{4,0},{5,1},{6,2},{7,3},{8,12},{9,13},{10,... | collective-permute-start | bytes 614408 | tf_op jit(solution)/shard_map/ppermute | solution.py:417
  41.2 3.2 %shard_map.155 = (f32[2,16,3072]{2,1,0:T(8,128)S(1)}, s16[2,16,3200]{2,1,0:T(8,128)(2,1)S(1)}, f32[2,16,3072]{2,1,0:T(8,128)S(1)}, s16[2,16,3200]{2,1,0:T(8,128)(2,1)S(1)}, s16[2,16,3200]{2,1,0:T(8,128)(2,1)S(1)}) custom-call(f32[256,24]{1,0:T(8,128)S(1)} %get-tuple-element.46.refs_1_.refs_2_.refs_0_, ...), custom_call_target="tpu_custom_call" | custom-call | flops 1879048192 | bytes 1048576 | tf_op jit(solution)/shard_map/pallas_call | solution.py:454
  45.2 1.6 %collective-permute-start.15 = (s16[2,16,3200]{2,1,0:T(8,128)(2,1)S(1)}, s16[2,16,3200]{2,1,0:T(8,128)(2,1)S(1)}, u32[]{:S(2)}, u32[]{:S(2)}) collective-permute-start(s16[2,16,3200]{2,1,0:T(8,128)(2,1)S(1)} %get-tuple-element.73), channel_id=1, source_target_pairs={{0,2},{1,3},{2,0},{3,1},{4,6},{5,7},{6,4},{7,5},{8,10},{9,11},{10,... | collective-permute-start | bytes 614408 | tf_op jit(solution)/shard_map/ppermute | solution.py:417
  47.4 1.5 %collective-permute-start.16 = (s16[16,3200]{1,0:T(8,128)(2,1)S(1)}, s16[16,3200]{1,0:T(8,128)(2,1)S(1)}, u32[]{:S(2)}, u32[]{:S(2)}) collective-permute-start(s16[16,3200]{1,0:T(8,128)(2,1)S(1)} %get-tuple-element.69.refs_0_), channel_id=1, source_target_pairs={{0,2},{1,3},{2,0},{3,1},{4,6},{5,7},{6,4},{7,5},{8,10},{9,11},{10,... | collective-permute-start | bytes 307208 | tf_op jit(solution)/shard_map/ppermute | solution.py:417
  48.9 2.4 %collective-permute-start.17 = (s16[2,16,3200]{2,1,0:T(8,128)(2,1)S(1)}, s16[2,16,3200]{2,1,0:T(8,128)(2,1)S(1)}, u32[]{:S(2)}, u32[]{:S(2)}) collective-permute-start(s16[2,16,3200]{2,1,0:T(8,128)(2,1)S(1)} %get-tuple-element.77), channel_id=1, source_target_pairs={{0,4},{1,5},{2,6},{3,7},{4,0},{5,1},{6,2},{7,3},{8,12},{9,13},{10,... | collective-permute-start | bytes 614408 | tf_op jit(solution)/shard_map/ppermute | solution.py:417
  52.7 2.0 %collective-permute-start.19 = (s16[16,3200]{1,0:T(8,128)(2,1)S(1)}, s16[16,3200]{1,0:T(8,128)(2,1)S(1)}, u32[]{:S(2)}, u32[]{:S(2)}) collective-permute-start(s16[16,3200]{1,0:T(8,128)(2,1)S(1)} %get-tuple-element.72.refs_0_), channel_id=1, source_target_pairs={{0,2},{1,3},{2,0},{3,1},{4,6},{5,7},{6,4},{7,5},{8,10},{9,11},{10,... | collective-permute-start | bytes 307208 | tf_op jit(solution)/shard_map/ppermute | solution.py:417
  56.2 2.2 %collective-permute-start.20 = (s16[16,3200]{1,0:T(8,128)(2,1)S(1)}, s16[16,3200]{1,0:T(8,128)(2,1)S(1)}, u32[]{:S(2)}, u32[]{:S(2)}) collective-permute-start(s16[16,3200]{1,0:T(8,128)(2,1)S(1)} %shard_map.159.refs_0_), channel_id=1, source_target_pairs={{0,8},{1,9},{2,10},{3,11},{4,12},{5,13},{6,14},{7,15},{8,0},{9,1},... | collective-permute-start | bytes 307208 | tf_op jit(solution)/shard_map/ppermute | solution.py:417
  60.4 1.8 %collective-permute-start.22 = (s16[16,3200]{1,0:T(8,128)(2,1)S(1)}, s16[16,3200]{1,0:T(8,128)(2,1)S(1)}, u32[]{:S(2)}, u32[]{:S(2)}) collective-permute-start(s16[16,3200]{1,0:T(8,128)(2,1)S(1)} %shard_map.161.refs_0_), channel_id=1, source_target_pairs={{0,8},{1,9},{2,10},{3,11},{4,12},{5,13},{6,14},{7,15},{8,0},{9,1},... | collective-permute-start | bytes 307208 | tf_op jit(solution)/shard_map/ppermute | solution.py:417
  62.3 2.4 %collective-permute-done.20.refs_3_ = s16[16,3200]{1,0:T(8,128)(2,1)S(1)} collective-permute-done((s16[16,3200]{1,0:T(8,128)(2,1)S(1)}, s16[16,3200]{1,0:T(8,128)(2,1)S(1)}, u32[]{:S(2)}, u32[]{:S(2)}) %collective-permute-start.20) | collective-permute-done | bytes 102432 | tf_op jit(solution)/shard_map/ppermute | solution.py:417
  64.8 2.5 %collective-permute-done.22.refs_3_ = s16[16,3200]{1,0:T(8,128)(2,1)S(1)} collective-permute-done((s16[16,3200]{1,0:T(8,128)(2,1)S(1)}, s16[16,3200]{1,0:T(8,128)(2,1)S(1)}, u32[]{:S(2)}, u32[]{:S(2)}) %collective-permute-start.22) | collective-permute-done | bytes 102432 | tf_op jit(solution)/shard_map/ppermute | solution.py:417
  (56 shorter events, 13.7 us)
Async XLA Ops:
  0.6 13.2 %collective-permute-start.1 = (bf16[1024,1024]{1,0:T(8,128)(2,1)}, bf16[1024,1024]{1,0:T(8,128)(2,1)S(1)}, u32[]{:S(2)}, u32[]{:S(2)}) collective-permute-start(bf16[1024,1024]{1,0:T(8,128)(2,1)} %bitcast.23), channel_id=1, source_target_pairs={{0,1},{1,0},{2,3},{3,2},{4,5},{5,4},{6,7},{7,6},{8,9},{9,8},{10,11... | collective-permute-start | bytes 6291464 | tf_op jit(solution)/shard_map/ppermute | solution.py:417
  3.1 8.6 %collective-permute-start.4 = (s16[2,16,3200]{2,1,0:T(8,128)(2,1)}, s16[2,16,3200]{2,1,0:T(8,128)(2,1)S(1)}, u32[]{:S(2)}, u32[]{:S(2)}) collective-permute-start(s16[2,16,3200]{2,1,0:T(8,128)(2,1)} %get-tuple-element.52.refs_4_.refs_2_.refs_8_), channel_id=1, source_target_pairs={{0,2},{1,3},{4,0},{5,1},{8,4},{9,5},{12,8},{13,9},{14,12},{15,13},... | collective-permute-start | bytes 614408 | tf_op jit(solution)/shard_map/ppermute | solution.py:391
  5.7 7.7 %collective-permute-start.3 = (s16[2,16,3200]{2,1,0:T(8,128)(2,1)}, s16[2,16,3200]{2,1,0:T(8,128)(2,1)S(1)}, u32[]{:S(2)}, u32[]{:S(2)}) collective-permute-start(s16[2,16,3200]{2,1,0:T(8,128)(2,1)} %get-tuple-element.52.refs_4_.refs_2_.refs_8_), channel_id=1, source_target_pairs={{0,4},{1,5},{4,8},{5,9},{8,12},{9,13},{12,14},{13,15},{14,10},{15,... | collective-permute-start | bytes 614408 | tf_op jit(solution)/shard_map/ppermute | solution.py:391
  5.8 8.0 %collective-permute-start = (f32[24,128]{1,0:T(8,128)}, f32[24,128]{1,0:T(8,128)S(1)}, u32[]{:S(2)}, u32[]{:S(2)}) collective-permute-start(f32[24,128]{1,0:T(8,128)} %get-tuple-element.45.refs_1_), channel_id=1, source_target_pairs={{0,1},{1,0},{2,3},{3,2},{4,5},{5,4},{6,7},{7,6},{8,9},{9,8},{10,11... | collective-permute-start | bytes 36872 | tf_op jit(solution)/shard_map/ppermute | solution.py:417
  6.0 7.8 %collective-permute-start.2 = (bf16[128,2048]{1,0:T(8,128)(2,1)}, bf16[128,2048]{1,0:T(8,128)(2,1)S(1)}, u32[]{:S(2)}, u32[]{:S(2)}) collective-permute-start(bf16[128,2048]{1,0:T(8,128)(2,1)} %refs_4_.1), channel_id=1, source_target_pairs={{0,1},{1,0},{2,3},{3,2},{4,5},{5,4},{6,7},{7,6},{8,9},{9,8},{10,11... | collective-permute-start | bytes 1572872 | tf_op jit(solution)/shard_map/ppermute | solution.py:417
  11.7 6.9 %collective-permute-start.6 = (s16[2,16,3200]{2,1,0:T(8,128)(2,1)S(1)}, s16[2,16,3200]{2,1,0:T(8,128)(2,1)S(1)}, u32[]{:S(2)}, u32[]{:S(2)}) collective-permute-start(s16[2,16,3200]{2,1,0:T(8,128)(2,1)S(1)} %collective-permute-done.4.refs_6_.refs_4_.refs_10_), channel_id=1, source_target_pairs={{0,2},{1,3},{4,0},{5,1},{8,4},{9,5},{12,8},{13,9},{14,12},{15,13},... | collective-permute-start | bytes 614408 | tf_op jit(solution)/shard_map/ppermute | solution.py:391
  13.4 6.4 %collective-permute-start.5 = (s16[2,16,3200]{2,1,0:T(8,128)(2,1)S(1)}, s16[2,16,3200]{2,1,0:T(8,128)(2,1)S(1)}, u32[]{:S(2)}, u32[]{:S(2)}) collective-permute-start(s16[2,16,3200]{2,1,0:T(8,128)(2,1)S(1)} %collective-permute-done.3.refs_5_.refs_3_.refs_9_), channel_id=1, source_target_pairs={{0,4},{1,5},{4,8},{5,9},{8,12},{9,13},{12,14},{13,15},{14,10},{15,... | collective-permute-start | bytes 614408 | tf_op jit(solution)/shard_map/ppermute | solution.py:391
  13.8 14.2 %copy-start.1 = (s16[2,16,3200]{2,1,0:T(8,128)(2,1)S(1)}, s16[2,16,3200]{2,1,0:T(8,128)(2,1)}, u32[]{:S(2)}) copy-start(s16[2,16,3200]{2,1,0:T(8,128)(2,1)} %get-tuple-element.52.refs_4_.refs_2_.refs_8_) | copy-start | bytes 614404
  19.8 5.8 %collective-permute-start.7 = (s16[2,16,3200]{2,1,0:T(8,128)(2,1)S(1)}, s16[2,16,3200]{2,1,0:T(8,128)(2,1)S(1)}, u32[]{:S(2)}, u32[]{:S(2)}) collective-permute-start(s16[2,16,3200]{2,1,0:T(8,128)(2,1)S(1)} %get-tuple-element.53.refs_7_.refs_5_.refs_11_), channel_id=1, source_target_pairs={{0,4},{1,5},{4,8},{5,9},{8,12},{9,13},{12,14},{13,15},{14,10},{15,... | collective-permute-start | bytes 614408 | tf_op jit(solution)/shard_map/ppermute | solution.py:391
  20.4 5.9 %collective-permute-start.8 = (s16[2,16,3200]{2,1,0:T(8,128)(2,1)S(1)}, s16[2,16,3200]{2,1,0:T(8,128)(2,1)S(1)}, u32[]{:S(2)}, u32[]{:S(2)}) collective-permute-start(s16[2,16,3200]{2,1,0:T(8,128)(2,1)S(1)} %get-tuple-element.54.refs_6_.refs_5_.refs_12_), channel_id=1, source_target_pairs={{0,2},{1,3},{4,0},{5,1},{8,4},{9,5},{12,8},{13,9},{14,12},{15,13},... | collective-permute-start | bytes 614408 | tf_op jit(solution)/shard_map/ppermute | solution.py:391
  25.6 4.7 %collective-permute-start.9 = (s16[1,16,3200]{2,1,0:T(8,128)(2,1)S(1)}, s16[1,16,3200]{2,1,0:T(8,128)(2,1)S(1)}, u32[]{:S(2)}, u32[]{:S(2)}) collective-permute-start(s16[1,16,3200]{2,1,0:T(8,128)(2,1)S(1)} %slice.8), channel_id=1, source_target_pairs={{0,4},{1,5},{4,8},{5,9},{8,12},{9,13},{12,14},{13,15},{14,10},{15,... | collective-permute-start | bytes 307208 | tf_op jit(solution)/shard_map/ppermute | solution.py:391
  26.4 4.9 %collective-permute-start.11 = (s16[1,16,3200]{2,1,0:T(8,128)(2,1)S(1)}, s16[1,16,3200]{2,1,0:T(8,128)(2,1)S(1)}, u32[]{:S(2)}, u32[]{:S(2)}) collective-permute-start(s16[1,16,3200]{2,1,0:T(8,128)(2,1)S(1)} %slice.9), channel_id=1, source_target_pairs={{0,2},{1,3},{4,0},{5,1},{8,4},{9,5},{12,8},{13,9},{14,12},{15,13},... | collective-permute-start | bytes 307208 | tf_op jit(solution)/shard_map/ppermute | solution.py:391
  30.9 2.3 %collective-permute-start.10 = (f32[8,128]{1,0:T(8,128)S(1)}, f32[8,128]{1,0:T(8,128)S(1)}, u32[]{:S(2)}, u32[]{:S(2)}) collective-permute-start(f32[8,128]{1,0:T(8,128)S(1)} %shard_map.151.refs_0_.refs_4_), channel_id=1, source_target_pairs={{0,1},{1,0},{2,3},{3,2},{4,5},{5,4},{6,7},{7,6},{8,9},{9,8},{10,11... | collective-permute-start | bytes 12296 | tf_op jit(solution)/shard_map/ppermute | solution.py:417
  35.6 5.7 %collective-permute-start.12 = (bf16[256,2048]{1,0:T(8,128)(2,1)S(1)}, bf16[256,2048]{1,0:T(8,128)(2,1)S(1)}, u32[]{:S(2)}, u32[]{:S(2)}) collective-permute-start(bf16[256,2048]{1,0:T(8,128)(2,1)S(1)} %get-tuple-element.63), channel_id=1, source_target_pairs={{0,1},{1,0},{2,3},{3,2},{4,5},{5,4},{6,7},{7,6},{8,9},{9,8},{10,11... | collective-permute-start | bytes 3145736 | tf_op jit(solution)/shard_map/ppermute | solution.py:417
  39.9 7.3 %collective-permute-start.13 = (s16[2,16,3200]{2,1,0:T(8,128)(2,1)S(1)}, s16[2,16,3200]{2,1,0:T(8,128)(2,1)S(1)}, u32[]{:S(2)}, u32[]{:S(2)}) collective-permute-start(s16[2,16,3200]{2,1,0:T(8,128)(2,1)S(1)} %get-tuple-element.66), channel_id=1, source_target_pairs={{0,4},{1,5},{2,6},{3,7},{4,0},{5,1},{6,2},{7,3},{8,12},{9,13},{10,... | collective-permute-start | bytes 614408 | tf_op jit(solution)/shard_map/ppermute | solution.py:417
  44.5 8.0 %collective-permute-start.14 = (s16[2,16,3200]{2,1,0:T(8,128)(2,1)S(1)}, s16[2,16,3200]{2,1,0:T(8,128)(2,1)S(1)}, u32[]{:S(2)}, u32[]{:S(2)}) collective-permute-start(s16[2,16,3200]{2,1,0:T(8,128)(2,1)S(1)} %get-tuple-element.70), channel_id=1, source_target_pairs={{0,4},{1,5},{2,6},{3,7},{4,0},{5,1},{6,2},{7,3},{8,12},{9,13},{10,... | collective-permute-start | bytes 614408 | tf_op jit(solution)/shard_map/ppermute | solution.py:417
  45.2 9.4 %collective-permute-start.15 = (s16[2,16,3200]{2,1,0:T(8,128)(2,1)S(1)}, s16[2,16,3200]{2,1,0:T(8,128)(2,1)S(1)}, u32[]{:S(2)}, u32[]{:S(2)}) collective-permute-start(s16[2,16,3200]{2,1,0:T(8,128)(2,1)S(1)} %get-tuple-element.73), channel_id=1, source_target_pairs={{0,2},{1,3},{2,0},{3,1},{4,6},{5,7},{6,4},{7,5},{8,10},{9,11},{10,... | collective-permute-start | bytes 614408 | tf_op jit(solution)/shard_map/ppermute | solution.py:417
  47.4 8.6 %collective-permute-start.16 = (s16[16,3200]{1,0:T(8,128)(2,1)S(1)}, s16[16,3200]{1,0:T(8,128)(2,1)S(1)}, u32[]{:S(2)}, u32[]{:S(2)}) collective-permute-start(s16[16,3200]{1,0:T(8,128)(2,1)S(1)} %get-tuple-element.69.refs_0_), channel_id=1, source_target_pairs={{0,2},{1,3},{2,0},{3,1},{4,6},{5,7},{6,4},{7,5},{8,10},{9,11},{10,... | collective-permute-start | bytes 307208 | tf_op jit(solution)/shard_map/ppermute | solution.py:417
  48.9 9.5 %collective-permute-start.17 = (s16[2,16,3200]{2,1,0:T(8,128)(2,1)S(1)}, s16[2,16,3200]{2,1,0:T(8,128)(2,1)S(1)}, u32[]{:S(2)}, u32[]{:S(2)}) collective-permute-start(s16[2,16,3200]{2,1,0:T(8,128)(2,1)S(1)} %get-tuple-element.77), channel_id=1, source_target_pairs={{0,4},{1,5},{2,6},{3,7},{4,0},{5,1},{6,2},{7,3},{8,12},{9,13},{10,... | collective-permute-start | bytes 614408 | tf_op jit(solution)/shard_map/ppermute | solution.py:417
  52.7 7.6 %collective-permute-start.19 = (s16[16,3200]{1,0:T(8,128)(2,1)S(1)}, s16[16,3200]{1,0:T(8,128)(2,1)S(1)}, u32[]{:S(2)}, u32[]{:S(2)}) collective-permute-start(s16[16,3200]{1,0:T(8,128)(2,1)S(1)} %get-tuple-element.72.refs_0_), channel_id=1, source_target_pairs={{0,2},{1,3},{2,0},{3,1},{4,6},{5,7},{6,4},{7,5},{8,10},{9,11},{10,... | collective-permute-start | bytes 307208 | tf_op jit(solution)/shard_map/ppermute | solution.py:417
  54.8 5.4 %collective-permute-start.18 = (s16[16,3200]{1,0:T(8,128)(2,1)S(1)}, s16[16,3200]{1,0:T(8,128)(2,1)S(1)}, u32[]{:S(2)}, u32[]{:S(2)}) collective-permute-start(s16[16,3200]{1,0:T(8,128)(2,1)S(1)} %get-tuple-element.79), channel_id=1, source_target_pairs={{0,4},{1,5},{2,6},{3,7},{4,0},{5,1},{6,2},{7,3},{8,12},{9,13},{10,... | collective-permute-start | bytes 307208 | tf_op jit(solution)/shard_map/ppermute | solution.py:417
  56.2 8.5 %collective-permute-start.20 = (s16[16,3200]{1,0:T(8,128)(2,1)S(1)}, s16[16,3200]{1,0:T(8,128)(2,1)S(1)}, u32[]{:S(2)}, u32[]{:S(2)}) collective-permute-start(s16[16,3200]{1,0:T(8,128)(2,1)S(1)} %shard_map.159.refs_0_), channel_id=1, source_target_pairs={{0,8},{1,9},{2,10},{3,11},{4,12},{5,13},{6,14},{7,15},{8,0},{9,1},... | collective-permute-start | bytes 307208 | tf_op jit(solution)/shard_map/ppermute | solution.py:417
  58.7 6.1 %collective-permute-start.21 = (s16[16,3200]{1,0:T(8,128)(2,1)S(1)}, s16[16,3200]{1,0:T(8,128)(2,1)S(1)}, u32[]{:S(2)}, u32[]{:S(2)}) collective-permute-start(s16[16,3200]{1,0:T(8,128)(2,1)S(1)} %get-tuple-element.81), channel_id=1, source_target_pairs={{0,2},{1,3},{2,0},{3,1},{4,6},{5,7},{6,4},{7,5},{8,10},{9,11},{10,... | collective-permute-start | bytes 307208 | tf_op jit(solution)/shard_map/ppermute | solution.py:417
  60.4 6.9 %collective-permute-start.22 = (s16[16,3200]{1,0:T(8,128)(2,1)S(1)}, s16[16,3200]{1,0:T(8,128)(2,1)S(1)}, u32[]{:S(2)}, u32[]{:S(2)}) collective-permute-start(s16[16,3200]{1,0:T(8,128)(2,1)S(1)} %shard_map.161.refs_0_), channel_id=1, source_target_pairs={{0,8},{1,9},{2,10},{3,11},{4,12},{5,13},{6,14},{7,15},{8,0},{9,1},... | collective-permute-start | bytes 307208 | tf_op jit(solution)/shard_map/ppermute | solution.py:417
  (4 other events, 25.0 us)

commit v21 on v18

--- a/solution.py
+++ b/solution.py
@@ -58,9 +58,9 @@
     copies = [pltpu.make_async_copy(refs[i], refs[7 + i], sem.at[i]) for i in range(7)]
     for copy in copies:
         copy.start()
-    for copy in copies:
+    for copy in copies[:3]:
         copy.wait()
-    expert, gate, curvature, down_direction, adapter_down, adapter_up, up_direction = [ref[...] for ref in refs[7:]]
+    expert, gate, curvature = [ref[...] for ref in refs[7:10]]
     top = expert.shape[0]
     small_ref[...] = jnp.zeros_like(small_ref)
     small_ref[:top] = expert.astype(f32)
@@ -72,6 +72,9 @@
         named = jnp.where(expert == number, 1.0, 0.0)
         total = jnp.sum(jnp.sum(named, axis=0, keepdims=True), axis=1, keepdims=True)
         counts = jnp.where(lane == counts_lane + number, total, counts)
+    for copy in copies[3:]:
+        copy.wait()
+    down_direction, adapter_down, adapter_up, up_direction = [ref[...] for ref in refs[10:]]
     piece_ref[0] = encode(down_direction, adapter_up, counts)
     piece_ref[1] = encode(adapter_down, up_direction, counts)
 
@@ -171,7 +174,7 @@
     tokens = own_ref.shape[0] // top
     for core, hidden_ref in enumerate((own_ref, other_ref)):
         full = dot(hidden_ref[...], factor, 1, 1)
-        full_ref[...] = full[:, :wide] + full[:, wide:]
+        full_ref[: tokens * top] = full[:, :wide] + full[:, wide:]
         tokens_of = slice(core * tokens, (core + 1) * tokens)
         total = jnp.zeros((tokens, wide), f32)
         for k in range(top):
@@ -523,7 +526,7 @@
             hidden,
             hidden_other,
             *parts,
-            scratch=[pltpu.VMEM((tokens * top, 2 * count * rank), f32)],
+            scratch=[pltpu.VMEM((tokens * top + top, 2 * count * rank), f32)],
             after=after,
         )[0]
 

time: 66.9 us -> 66.9 us (level)
  no operation moved by 1% of the time
where the time goes in v21:
time: 66.9 us; the launch traced here: 66.6 us
  starting transfers between devices  24.2 us (36%)
  Pallas kernels  20.2 us (30%)
  waiting for transfers between devices  19.1 us (29%)
  other arithmetic  1.43 us (2%)
  local copies, waits for them, and re-layouts  0.85 us (1%)
  between operations  0.81 us (1%)
    pallas_call x16, Pallas kernels, call(): pl.pallas_call(lambda *refs: kernel(*refs[len(after):]), out_shape=[jax.S...  20.2 us
    ppermute x14, starting transfers between devices, exchange(): lax.ppermute(value, 'expert', [(device, device ^ mask) for device in rang...  15.1 us
    ppermute x8, waiting for transfers between devices, shift(): return lax.ppermute(value, 'expert', pairs)  11.3 us
    ppermute x8, starting transfers between devices, shift(): return lax.ppermute(value, 'expert', pairs)  9.12 us
    ppermute x14, waiting for transfers between devices, exchange(): lax.ppermute(value, 'expert', [(device, device ^ mask) for device in rang...  7.74 us
  transfers between devices with their start and end apart: 22, of which 10 were waited for; matrix products, arithmetic and copies ran while one was open for 2% of the time, Pallas kernels for 26%

profile of v21, /device:TPU:0, one launch (start us, length us, event | category | flops | bytes accessed | tf_op | source)
XLA Modules:
  0.0 66.6 jit_solution(3600235344644533682)
XLA Ops:
  1.2 2.0 %shard_map.147 = (s16[2,16,3200]{2,1,0:T(8,128)(2,1)}, f32[24,128]{1,0:T(8,128)}) custom-call(s32[8,128]{1,0:T(8,128)} %bitcast.32, bf16[8,128]{1,0:T(8,128)(2,1)} %bitcast.33, f32[1,128]{1,0:T(1,128)} %bitcast.34, f32[16,1024]{1,0:T(8,128)} %bitcast.30, f32[16,1024]{1,0:T(8,128)} %bitcast.31, f32[16,2048]{1,0:T(8,128)} %bitcast.28, f32[16,2048]{1,0:T(8,128)} %bitcast.29), custom_call_target="tpu_custom_call" | custom-call | flops 200000000 | bytes 1048576 | tf_op jit(solution)/shard_map/pallas_call | solution.py:459
  3.1 2.6 %collective-permute-start.4 = (s16[2,16,3200]{2,1,0:T(8,128)(2,1)}, s16[2,16,3200]{2,1,0:T(8,128)(2,1)S(1)}, u32[]{:S(2)}, u32[]{:S(2)}) collective-permute-start(s16[2,16,3200]{2,1,0:T(8,128)(2,1)} %get-tuple-element.50.refs_4_.refs_2_.refs_8_), channel_id=1, source_target_pairs={{0,2},{1,3},{4,0},{5,1},{8,4},{9,5},{12,8},{13,9},{14,12},{15,13},... | collective-permute-start | bytes 614408 | tf_op jit(solution)/shard_map/ppermute | solution.py:396
  7.7 4.0 %collective-permute-done.4.refs_6_.refs_4_.refs_10_ = s16[2,16,3200]{2,1,0:T(8,128)(2,1)S(1)} collective-permute-done((s16[2,16,3200]{2,1,0:T(8,128)(2,1)}, s16[2,16,3200]{2,1,0:T(8,128)(2,1)S(1)}, u32[]{:S(2)}, u32[]{:S(2)}) %collective-permute-start.4) | collective-permute-done | bytes 204832 | tf_op jit(solution)/shard_map/ppermute | solution.py:396
  11.7 1.7 %collective-permute-start.6 = (s16[2,16,3200]{2,1,0:T(8,128)(2,1)S(1)}, s16[2,16,3200]{2,1,0:T(8,128)(2,1)S(1)}, u32[]{:S(2)}, u32[]{:S(2)}) collective-permute-start(s16[2,16,3200]{2,1,0:T(8,128)(2,1)S(1)} %collective-permute-done.4.refs_6_.refs_4_.refs_10_), channel_id=1, source_target_pairs={{0,2},{1,3},{4,0},{5,1},{8,4},{9,5},{12,8},{13,9},{14,12},{15,13},... | collective-permute-start | bytes 614408 | tf_op jit(solution)/shard_map/ppermute | solution.py:396
  14.6 2.2 %shard_map.148 = (f32[256,24]{1,0:T(8,128)S(1)}, f32[2,128,128]{2,1,0:T(8,128)S(1)}, f32[2,128,128]{2,1,0:T(8,128)S(1)}, bf16[1024,128]{1,0:T(8,128)(2,1)S(1)}, ...) custom-call(s32[25]{0:T(128)S(1)} %pad_add_fusion.refs_0_.refs_1_, ...), custom_call_target="tpu_custom_call" | custom-call | flops 2000000000 | bytes 1048576 | tf_op jit(solution)/shard_map/pallas_call | solution.py:459
  16.8 1.9 %collective-permute-done.6.refs_2_ = s16[2,16,3200]{2,1,0:T(8,128)(2,1)S(1)} collective-permute-done((s16[2,16,3200]{2,1,0:T(8,128)(2,1)S(1)}, s16[2,16,3200]{2,1,0:T(8,128)(2,1)S(1)}, u32[]{:S(2)}, u32[]{:S(2)}) %collective-permute-start.6) | collective-permute-done | bytes 204832 | tf_op jit(solution)/shard_map/ppermute | solution.py:396
  18.6 1.2 %collective-permute-done.5.refs_1_ = s16[2,16,3200]{2,1,0:T(8,128)(2,1)S(1)} collective-permute-done((s16[2,16,3200]{2,1,0:T(8,128)(2,1)S(1)}, s16[2,16,3200]{2,1,0:T(8,128)(2,1)S(1)}, u32[]{:S(2)}, u32[]{:S(2)}) %collective-permute-start.5) | collective-permute-done | bytes 204832 | tf_op jit(solution)/shard_map/ppermute | solution.py:396
  20.4 1.5 %collective-permute-start.8 = (s16[2,16,3200]{2,1,0:T(8,128)(2,1)S(1)}, s16[2,16,3200]{2,1,0:T(8,128)(2,1)S(1)}, u32[]{:S(2)}, u32[]{:S(2)}) collective-permute-start(s16[2,16,3200]{2,1,0:T(8,128)(2,1)S(1)} %get-tuple-element.52.refs_6_.refs_5_.refs_12_), channel_id=1, source_target_pairs={{0,2},{1,3},{4,0},{5,1},{8,4},{9,5},{12,8},{13,9},{14,12},{15,13},... | collective-permute-start | bytes 614408 | tf_op jit(solution)/shard_map/ppermute | solution.py:396
  21.9 3.7 %collective-permute-done.7.refs_7_.refs_6_.refs_13_ = s16[2,16,3200]{2,1,0:T(8,128)(2,1)S(1)} collective-permute-done((s16[2,16,3200]{2,1,0:T(8,128)(2,1)S(1)}, s16[2,16,3200]{2,1,0:T(8,128)(2,1)S(1)}, u32[]{:S(2)}, u32[]{:S(2)}) %collective-permute-start.7) | collective-permute-done | bytes 204832 | tf_op jit(solution)/shard_map/ppermute | solution.py:396
  26.4 1.7 %collective-permute-start.11 = (s16[1,16,3200]{2,1,0:T(8,128)(2,1)S(1)}, s16[1,16,3200]{2,1,0:T(8,128)(2,1)S(1)}, u32[]{:S(2)}, u32[]{:S(2)}) collective-permute-start(s16[1,16,3200]{2,1,0:T(8,128)(2,1)S(1)} %slice.9), channel_id=1, source_target_pairs={{0,2},{1,3},{4,0},{5,1},{8,4},{9,5},{12,8},{13,9},{14,12},{15,13},... | collective-permute-start | bytes 307208 | tf_op jit(solution)/shard_map/ppermute | solution.py:396
  28.0 2.0 %shard_map.150.refs_0_.refs_6_ = f32[256,128]{1,0:T(8,128)S(1)} custom-call(s32[25]{0:T(128)S(1)} %pad_add_fusion.refs_0_.refs_1_, f32[256,24]{1,0:T(8,128)S(1)} %get-tuple-element.44.refs_1_.refs_2_.refs_0_, bf16[1024,1024]{1,0:T(8,128)(2,1)S(1)} %bitcast.24, bf16[1024,1024]{1,0:T(8,128)(2,1)S(1)} %get-tuple-element.47.refs_3_.refs_4_, ...), custom_call_target="tpu_custom_call" | custom-call | flops 1073741824 | bytes 1048576 | tf_op jit(solution)/shard_map/pallas_call | solution.py:459
  31.2 2.0 %shard_map.152.refs_7_ = f32[256,128]{1,0:T(8,128)S(1)} custom-call(f32[8,128]{1,0:T(8,128)S(1)} %shard_map.151.refs_0_.refs_4_, s32[25]{0:T(128)S(1)} %pad_add_fusion.refs_0_.refs_1_, f32[256,24]{1,0:T(8,128)S(1)} %get-tuple-element.44.refs_1_.refs_2_.refs_0_, bf16[1024,1024]{1,0:T(8,128)(2,1)S(1)} %bitcast.25, ...), custom_call_target="tpu_custom_call" | custom-call | flops 1073741824 | bytes 1048576 | tf_op jit(solution)/shard_map/pallas_call | solution.py:459
  33.3 2.3 %shard_map.153 = (f32[256,128]{1,0:T(8,128)S(1)}, f32[256,256]{1,0:T(8,128)S(1)}, f32[256,2048]{1,0:T(8,128)S(1)}, bf16[256,2048]{1,0:T(8,128)(2,1)S(1)}, bf16[2...) custom-call(s32[25]{0:T(128)S(1)} %pad_add_fusion.refs_0_.refs_1_, ...), custom_call_target="tpu_custom_call" | custom-call | flops 805306368 | bytes 1048576 | tf_op jit(solution)/shard_map/pallas_call | solution.py:459
  35.9 4.0 %shard_map.154 = (f32[2,16,3072]{2,1,0:T(8,128)S(1)}, s16[2,16,3200]{2,1,0:T(8,128)(2,1)S(1)}, f32[2,16,3072]{2,1,0:T(8,128)S(1)}, s16[2,16,3200]{2,1,0:T(8,128)...) custom-call(bf16[1024,128]{1,0:T(8,128)(2,1)S(1)} %get-tuple-element.45.refs_0_.refs_1_, ...), custom_call_target="tpu_custom_call" | custom-call | flops 2147483648 | bytes 1048576 | tf_op jit(solution)/shard_map/pallas_call | solution.py:459
  39.9 1.4 %collective-permute-start.13 = (s16[2,16,3200]{2,1,0:T(8,128)(2,1)S(1)}, s16[2,16,3200]{2,1,0:T(8,128)(2,1)S(1)}, u32[]{:S(2)}, u32[]{:S(2)}) collective-permute-start(s16[2,16,3200]{2,1,0:T(8,128)(2,1)S(1)} %get-tuple-element.63), channel_id=1, source_target_pairs={{0,4},{1,5},{2,6},{3,7},{4,0},{5,1},{6,2},{7,3},{8,12},{9,13},{10,... | collective-permute-start | bytes 614408 | tf_op jit(solution)/shard_map/ppermute | solution.py:422
  41.2 1.8 %collective-permute-start.15 = (s16[2,16,3200]{2,1,0:T(8,128)(2,1)S(1)}, s16[2,16,3200]{2,1,0:T(8,128)(2,1)S(1)}, u32[]{:S(2)}, u32[]{:S(2)}) collective-permute-start(s16[2,16,3200]{2,1,0:T(8,128)(2,1)S(1)} %get-tuple-element.69), channel_id=1, source_target_pairs={{0,2},{1,3},{2,0},{3,1},{4,6},{5,7},{6,4},{7,5},{8,10},{9,11},{10,... | collective-permute-start | bytes 614408 | tf_op jit(solution)/shard_map/ppermute | solution.py:422
  43.1 3.2 %shard_map.155 = (f32[2,16,3072]{2,1,0:T(8,128)S(1)}, s16[2,16,3200]{2,1,0:T(8,128)(2,1)S(1)}, f32[2,16,3072]{2,1,0:T(8,128)S(1)}, s16[2,16,3200]{2,1,0:T(8,128)(2,1)S(1)}) custom-call(f32[256,24]{1,0:T(8,128)S(1)} %get-tuple-element.44.refs_1_.refs_2_.refs_0_, bf16[1024,128]{1,0:T(8,128)(2,1)S(1)} %get-tuple-element.45.refs_0_.refs_1_, ...), custom_call_target="tpu_custom_call" | custom-call | flops 1879048192 | bytes 1048576 | tf_op jit(solution)/shard_map/pallas_call | solution.py:459
  47.4 1.5 %collective-permute-start.16 = (s16[16,3200]{1,0:T(8,128)(2,1)S(1)}, s16[16,3200]{1,0:T(8,128)(2,1)S(1)}, u32[]{:S(2)}, u32[]{:S(2)}) collective-permute-start(s16[16,3200]{1,0:T(8,128)(2,1)S(1)} %get-tuple-element.66.refs_0_), channel_id=1, source_target_pairs={{0,2},{1,3},{2,0},{3,1},{4,6},{5,7},{6,4},{7,5},{8,10},{9,11},{10,... | collective-permute-start | bytes 307208 | tf_op jit(solution)/shard_map/ppermute | solution.py:422
  49.5 3.4 %collective-permute-done.14.refs_1_ = s16[2,16,3200]{2,1,0:T(8,128)(2,1)S(1)} collective-permute-done((s16[2,16,3200]{2,1,0:T(8,128)(2,1)S(1)}, s16[2,16,3200]{2,1,0:T(8,128)(2,1)S(1)}, u32[]{:S(2)}, u32[]{:S(2)}) %collective-permute-start.14) | collective-permute-done | bytes 204832 | tf_op jit(solution)/shard_map/ppermute | solution.py:422
  53.9 2.7 %collective-permute-start.19 = (s16[16,3200]{1,0:T(8,128)(2,1)S(1)}, s16[16,3200]{1,0:T(8,128)(2,1)S(1)}, u32[]{:S(2)}, u32[]{:S(2)}) collective-permute-start(s16[16,3200]{1,0:T(8,128)(2,1)S(1)} %shard_map.158.refs_0_), channel_id=1, source_target_pairs={{0,8},{1,9},{2,10},{3,11},{4,12},{5,13},{6,14},{7,15},{8,0},{9,1},... | collective-permute-start | bytes 307208 | tf_op jit(solution)/shard_map/ppermute | solution.py:422
  57.4 1.9 %collective-permute-start.21 = (s16[2,16,3200]{2,1,0:T(8,128)(2,1)S(1)}, s16[2,16,3200]{2,1,0:T(8,128)(2,1)S(1)}, u32[]{:S(2)}, u32[]{:S(2)}) collective-permute-start(s16[2,16,3200]{2,1,0:T(8,128)(2,1)S(1)} %get-tuple-element.75.refs_0_), channel_id=1, source_target_pairs={{0,4},{1,5},{2,6},{3,7},{4,0},{5,1},{6,2},{7,3},{8,12},{9,13},{10,... | collective-permute-start | bytes 614408 | tf_op jit(solution)/shard_map/ppermute | solution.py:422
  59.5 2.8 %collective-permute-start.20 = (s16[16,3200]{1,0:T(8,128)(2,1)S(1)}, s16[16,3200]{1,0:T(8,128)(2,1)S(1)}, u32[]{:S(2)}, u32[]{:S(2)}) collective-permute-start(s16[16,3200]{1,0:T(8,128)(2,1)S(1)} %shard_map.160.refs_0_), channel_id=1, source_target_pairs={{0,8},{1,9},{2,10},{3,11},{4,12},{5,13},{6,14},{7,15},{8,0},{9,1},... | collective-permute-start | bytes 307208 | tf_op jit(solution)/shard_map/ppermute | solution.py:422
  62.4 3.4 %collective-permute-done.21.refs_3_ = s16[2,16,3200]{2,1,0:T(8,128)(2,1)S(1)} collective-permute-done((s16[2,16,3200]{2,1,0:T(8,128)(2,1)S(1)}, s16[2,16,3200]{2,1,0:T(8,128)(2,1)S(1)}, u32[]{:S(2)}, u32[]{:S(2)}) %collective-permute-start.21) | collective-permute-done | bytes 204832 | tf_op jit(solution)/shard_map/ppermute | solution.py:422
  65.7 0.8 %shard_map.162 = (f32[16,1024]{1,0:T(8,128)}, f32[16,2048]{1,0:T(8,128)}, f32[16,1024]{1,0:T(8,128)}, f32[16,2048]{1,0:T(8,128)}) custom-call(f32[16,3072]{1,0:T(8,128)S(1)} %shard_map.161.refs_0_, f32[2,16,3072]{2,1,0:T(8,128)S(1)} %get-tuple-element.77.refs_1_, s16[16,3200]{1,0:T(8,128)(2,1)S(1)} %collective-permute-done.20.refs_2_, ...), custom_call_target="tpu_custom_call" | custom-call | flops 4000000000 | bytes 1048576 | tf_op jit(solution)/shard_map/pallas_call | solution.py:459
  (53 shorter events, 10.4 us)
Async XLA Ops:
  0.6 13.2 %collective-permute-start.1 = (bf16[1024,1024]{1,0:T(8,128)(2,1)}, bf16[1024,1024]{1,0:T(8,128)(2,1)S(1)}, u32[]{:S(2)}, u32[]{:S(2)}) collective-permute-start(bf16[1024,1024]{1,0:T(8,128)(2,1)} %bitcast.23), channel_id=1, source_target_pairs={{0,1},{1,0},{2,3},{3,2},{4,5},{5,4},{6,7},{7,6},{8,9},{9,8},{10,11... | collective-permute-start | bytes 6291464 | tf_op jit(solution)/shard_map/ppermute | solution.py:422
  3.1 8.6 %collective-permute-start.4 = (s16[2,16,3200]{2,1,0:T(8,128)(2,1)}, s16[2,16,3200]{2,1,0:T(8,128)(2,1)S(1)}, u32[]{:S(2)}, u32[]{:S(2)}) collective-permute-start(s16[2,16,3200]{2,1,0:T(8,128)(2,1)} %get-tuple-element.50.refs_4_.refs_2_.refs_8_), channel_id=1, source_target_pairs={{0,2},{1,3},{4,0},{5,1},{8,4},{9,5},{12,8},{13,9},{14,12},{15,13},... | collective-permute-start | bytes 614408 | tf_op jit(solution)/shard_map/ppermute | solution.py:396
  5.7 7.7 %collective-permute-start.3 = (s16[2,16,3200]{2,1,0:T(8,128)(2,1)}, s16[2,16,3200]{2,1,0:T(8,128)(2,1)S(1)}, u32[]{:S(2)}, u32[]{:S(2)}) collective-permute-start(s16[2,16,3200]{2,1,0:T(8,128)(2,1)} %get-tuple-element.50.refs_4_.refs_2_.refs_8_), channel_id=1, source_target_pairs={{0,4},{1,5},{4,8},{5,9},{8,12},{9,13},{12,14},{13,15},{14,10},{15,... | collective-permute-start | bytes 614408 | tf_op jit(solution)/shard_map/ppermute | solution.py:396
  5.8 8.0 %collective-permute-start = (f32[24,128]{1,0:T(8,128)}, f32[24,128]{1,0:T(8,128)S(1)}, u32[]{:S(2)}, u32[]{:S(2)}) collective-permute-start(f32[24,128]{1,0:T(8,128)} %get-tuple-element.43.refs_1_), channel_id=1, source_target_pairs={{0,1},{1,0},{2,3},{3,2},{4,5},{5,4},{6,7},{7,6},{8,9},{9,8},{10,11... | collective-permute-start | bytes 36872 | tf_op jit(solution)/shard_map/ppermute | solution.py:422
  6.0 7.8 %collective-permute-start.2 = (bf16[128,2048]{1,0:T(8,128)(2,1)}, bf16[128,2048]{1,0:T(8,128)(2,1)S(1)}, u32[]{:S(2)}, u32[]{:S(2)}) collective-permute-start(bf16[128,2048]{1,0:T(8,128)(2,1)} %refs_4_.1), channel_id=1, source_target_pairs={{0,1},{1,0},{2,3},{3,2},{4,5},{5,4},{6,7},{7,6},{8,9},{9,8},{10,11... | collective-permute-start | bytes 1572872 | tf_op jit(solution)/shard_map/ppermute | solution.py:422
  11.7 6.9 %collective-permute-start.6 = (s16[2,16,3200]{2,1,0:T(8,128)(2,1)S(1)}, s16[2,16,3200]{2,1,0:T(8,128)(2,1)S(1)}, u32[]{:S(2)}, u32[]{:S(2)}) collective-permute-start(s16[2,16,3200]{2,1,0:T(8,128)(2,1)S(1)} %collective-permute-done.4.refs_6_.refs_4_.refs_10_), channel_id=1, source_target_pairs={{0,2},{1,3},{4,0},{5,1},{8,4},{9,5},{12,8},{13,9},{14,12},{15,13},... | collective-permute-start | bytes 614408 | tf_op jit(solution)/shard_map/ppermute | solution.py:396
  13.4 6.4 %collective-permute-start.5 = (s16[2,16,3200]{2,1,0:T(8,128)(2,1)S(1)}, s16[2,16,3200]{2,1,0:T(8,128)(2,1)S(1)}, u32[]{:S(2)}, u32[]{:S(2)}) collective-permute-start(s16[2,16,3200]{2,1,0:T(8,128)(2,1)S(1)} %collective-permute-done.3.refs_5_.refs_3_.refs_9_), channel_id=1, source_target_pairs={{0,4},{1,5},{4,8},{5,9},{8,12},{9,13},{12,14},{13,15},{14,10},{15,... | collective-permute-start | bytes 614408 | tf_op jit(solution)/shard_map/ppermute | solution.py:396
  13.8 14.2 %copy-start.1 = (s16[2,16,3200]{2,1,0:T(8,128)(2,1)S(1)}, s16[2,16,3200]{2,1,0:T(8,128)(2,1)}, u32[]{:S(2)}) copy-start(s16[2,16,3200]{2,1,0:T(8,128)(2,1)} %get-tuple-element.50.refs_4_.refs_2_.refs_8_) | copy-start | bytes 614404
  14.6 13.5 %copy-start = (bf16[128,8,1024]{2,1,0:T(8,128)(2,1)S(1)}, bf16[128,8,1024]{2,1,0:T(8,128)(2,1)}, u32[]{:S(2)}) copy-start(bf16[128,8,1024]{2,1,0:T(8,128)(2,1)} %param.12) | copy-start | bytes 6291460
  19.8 5.8 %collective-permute-start.7 = (s16[2,16,3200]{2,1,0:T(8,128)(2,1)S(1)}, s16[2,16,3200]{2,1,0:T(8,128)(2,1)S(1)}, u32[]{:S(2)}, u32[]{:S(2)}) collective-permute-start(s16[2,16,3200]{2,1,0:T(8,128)(2,1)S(1)} %get-tuple-element.51.refs_7_.refs_5_.refs_11_), channel_id=1, source_target_pairs={{0,4},{1,5},{4,8},{5,9},{8,12},{9,13},{12,14},{13,15},{14,10},{15,... | collective-permute-start | bytes 614408 | tf_op jit(solution)/shard_map/ppermute | solution.py:396
  20.4 5.9 %collective-permute-start.8 = (s16[2,16,3200]{2,1,0:T(8,128)(2,1)S(1)}, s16[2,16,3200]{2,1,0:T(8,128)(2,1)S(1)}, u32[]{:S(2)}, u32[]{:S(2)}) collective-permute-start(s16[2,16,3200]{2,1,0:T(8,128)(2,1)S(1)} %get-tuple-element.52.refs_6_.refs_5_.refs_12_), channel_id=1, source_target_pairs={{0,2},{1,3},{4,0},{5,1},{8,4},{9,5},{12,8},{13,9},{14,12},{15,13},... | collective-permute-start | bytes 614408 | tf_op jit(solution)/shard_map/ppermute | solution.py:396
  25.6 4.7 %collective-permute-start.9 = (s16[1,16,3200]{2,1,0:T(8,128)(2,1)S(1)}, s16[1,16,3200]{2,1,0:T(8,128)(2,1)S(1)}, u32[]{:S(2)}, u32[]{:S(2)}) collective-permute-start(s16[1,16,3200]{2,1,0:T(8,128)(2,1)S(1)} %slice.8), channel_id=1, source_target_pairs={{0,4},{1,5},{4,8},{5,9},{8,12},{9,13},{12,14},{13,15},{14,10},{15,... | collective-permute-start | bytes 307208 | tf_op jit(solution)/shard_map/ppermute | solution.py:396
  26.4 4.9 %collective-permute-start.11 = (s16[1,16,3200]{2,1,0:T(8,128)(2,1)S(1)}, s16[1,16,3200]{2,1,0:T(8,128)(2,1)S(1)}, u32[]{:S(2)}, u32[]{:S(2)}) collective-permute-start(s16[1,16,3200]{2,1,0:T(8,128)(2,1)S(1)} %slice.9), channel_id=1, source_target_pairs={{0,2},{1,3},{4,0},{5,1},{8,4},{9,5},{12,8},{13,9},{14,12},{15,13},... | collective-permute-start | bytes 307208 | tf_op jit(solution)/shard_map/ppermute | solution.py:396
  30.9 2.3 %collective-permute-start.10 = (f32[8,128]{1,0:T(8,128)S(1)}, f32[8,128]{1,0:T(8,128)S(1)}, u32[]{:S(2)}, u32[]{:S(2)}) collective-permute-start(f32[8,128]{1,0:T(8,128)S(1)} %shard_map.151.refs_0_.refs_4_), channel_id=1, source_target_pairs={{0,1},{1,0},{2,3},{3,2},{4,5},{5,4},{6,7},{7,6},{8,9},{9,8},{10,11... | collective-permute-start | bytes 12296 | tf_op jit(solution)/shard_map/ppermute | solution.py:422
  35.5 7.5 %collective-permute-start.12 = (bf16[256,2048]{1,0:T(8,128)(2,1)S(1)}, bf16[256,2048]{1,0:T(8,128)(2,1)S(1)}, u32[]{:S(2)}, u32[]{:S(2)}) collective-permute-start(bf16[256,2048]{1,0:T(8,128)(2,1)S(1)} %get-tuple-element.61), channel_id=1, source_target_pairs={{0,1},{1,0},{2,3},{3,2},{4,5},{5,4},{6,7},{7,6},{8,9},{9,8},{10,11... | collective-permute-start | bytes 3145736 | tf_op jit(solution)/shard_map/ppermute | solution.py:422
  39.9 7.3 %collective-permute-start.13 = (s16[2,16,3200]{2,1,0:T(8,128)(2,1)S(1)}, s16[2,16,3200]{2,1,0:T(8,128)(2,1)S(1)}, u32[]{:S(2)}, u32[]{:S(2)}) collective-permute-start(s16[2,16,3200]{2,1,0:T(8,128)(2,1)S(1)} %get-tuple-element.63), channel_id=1, source_target_pairs={{0,4},{1,5},{2,6},{3,7},{4,0},{5,1},{6,2},{7,3},{8,12},{9,13},{10,... | collective-permute-start | bytes 614408 | tf_op jit(solution)/shard_map/ppermute | solution.py:422
  41.2 8.2 %collective-permute-start.15 = (s16[2,16,3200]{2,1,0:T(8,128)(2,1)S(1)}, s16[2,16,3200]{2,1,0:T(8,128)(2,1)S(1)}, u32[]{:S(2)}, u32[]{:S(2)}) collective-permute-start(s16[2,16,3200]{2,1,0:T(8,128)(2,1)S(1)} %get-tuple-element.69), channel_id=1, source_target_pairs={{0,2},{1,3},{2,0},{3,1},{4,6},{5,7},{6,4},{7,5},{8,10},{9,11},{10,... | collective-permute-start | bytes 614408 | tf_op jit(solution)/shard_map/ppermute | solution.py:422
  46.3 6.6 %collective-permute-start.14 = (s16[2,16,3200]{2,1,0:T(8,128)(2,1)S(1)}, s16[2,16,3200]{2,1,0:T(8,128)(2,1)S(1)}, u32[]{:S(2)}, u32[]{:S(2)}) collective-permute-start(s16[2,16,3200]{2,1,0:T(8,128)(2,1)S(1)} %get-tuple-element.67), channel_id=1, source_target_pairs={{0,4},{1,5},{2,6},{3,7},{4,0},{5,1},{6,2},{7,3},{8,12},{9,13},{10,... | collective-permute-start | bytes 614408 | tf_op jit(solution)/shard_map/ppermute | solution.py:422
  47.4 6.4 %collective-permute-start.16 = (s16[16,3200]{1,0:T(8,128)(2,1)S(1)}, s16[16,3200]{1,0:T(8,128)(2,1)S(1)}, u32[]{:S(2)}, u32[]{:S(2)}) collective-permute-start(s16[16,3200]{1,0:T(8,128)(2,1)S(1)} %get-tuple-element.66.refs_0_), channel_id=1, source_target_pairs={{0,2},{1,3},{2,0},{3,1},{4,6},{5,7},{6,4},{7,5},{8,10},{9,11},{10,... | collective-permute-start | bytes 307208 | tf_op jit(solution)/shard_map/ppermute | solution.py:422
  48.9 8.3 %collective-permute-start.17 = (s16[2,16,3200]{2,1,0:T(8,128)(2,1)S(1)}, s16[2,16,3200]{2,1,0:T(8,128)(2,1)S(1)}, u32[]{:S(2)}, u32[]{:S(2)}) collective-permute-start(s16[2,16,3200]{2,1,0:T(8,128)(2,1)S(1)} %get-tuple-element.73), channel_id=1, source_target_pairs={{0,2},{1,3},{2,0},{3,1},{4,6},{5,7},{6,4},{7,5},{8,10},{9,11},{10,... | collective-permute-start | bytes 614408 | tf_op jit(solution)/shard_map/ppermute | solution.py:422
  53.1 6.2 %collective-permute-start.18 = (s16[16,3200]{1,0:T(8,128)(2,1)S(1)}, s16[16,3200]{1,0:T(8,128)(2,1)S(1)}, u32[]{:S(2)}, u32[]{:S(2)}) collective-permute-start(s16[16,3200]{1,0:T(8,128)(2,1)S(1)} %get-tuple-element.70.refs_0_), channel_id=1, source_target_pairs={{0,2},{1,3},{2,0},{3,1},{4,6},{5,7},{6,4},{7,5},{8,10},{9,11},{10,... | collective-permute-start | bytes 307208 | tf_op jit(solution)/shard_map/ppermute | solution.py:422
  53.9 8.3 %collective-permute-start.19 = (s16[16,3200]{1,0:T(8,128)(2,1)S(1)}, s16[16,3200]{1,0:T(8,128)(2,1)S(1)}, u32[]{:S(2)}, u32[]{:S(2)}) collective-permute-start(s16[16,3200]{1,0:T(8,128)(2,1)S(1)} %shard_map.158.refs_0_), channel_id=1, source_target_pairs={{0,8},{1,9},{2,10},{3,11},{4,12},{5,13},{6,14},{7,15},{8,0},{9,1},... | collective-permute-start | bytes 307208 | tf_op jit(solution)/shard_map/ppermute | solution.py:422
  57.4 8.3 %collective-permute-start.21 = (s16[2,16,3200]{2,1,0:T(8,128)(2,1)S(1)}, s16[2,16,3200]{2,1,0:T(8,128)(2,1)S(1)}, u32[]{:S(2)}, u32[]{:S(2)}) collective-permute-start(s16[2,16,3200]{2,1,0:T(8,128)(2,1)S(1)} %get-tuple-element.75.refs_0_), channel_id=1, source_target_pairs={{0,4},{1,5},{2,6},{3,7},{4,0},{5,1},{6,2},{7,3},{8,12},{9,13},{10,... | collective-permute-start | bytes 614408 | tf_op jit(solution)/shard_map/ppermute | solution.py:422
  59.5 6.2 %collective-permute-start.20 = (s16[16,3200]{1,0:T(8,128)(2,1)S(1)}, s16[16,3200]{1,0:T(8,128)(2,1)S(1)}, u32[]{:S(2)}, u32[]{:S(2)}) collective-permute-start(s16[16,3200]{1,0:T(8,128)(2,1)S(1)} %shard_map.160.refs_0_), channel_id=1, source_target_pairs={{0,8},{1,9},{2,10},{3,11},{4,12},{5,13},{6,14},{7,15},{8,0},{9,1},... | collective-permute-start | bytes 307208 | tf_op jit(solution)/shard_map/ppermute | solution.py:422
  (3 other events, 11.5 us)

commit v22 on v18

--- a/solution.py
+++ b/solution.py
@@ -407,7 +407,7 @@
         for step in range(1, half):
             behind = self.shift(behind, 1)
             ahead = self.shift(ahead, -1)
-            if step == 2:
+            if step == 1:
                 behind, ahead = passing(behind, ahead)
             pieces += [behind, ahead]
         pieces += [self.shift(behind[:1], 1), self.shift(ahead[1:], -1)]

time: 66.9 us -> 67.3 us (level)
  waiting for transfers between devices: 19.1 us -> 20.4 us
  starting transfers between devices: 24.2 us -> 23.4 us
    ppermute x14, waiting for transfers between devices: 7.74 us -> 9.26 us  [exchange(): lax.ppermute(value, 'expert', [(device, device ^ mask) for device in rang...]
    ppermute x14, starting transfers between devices: 15.1 us -> 14.3 us  [exchange(): lax.ppermute(value, 'expert', [(device, device ^ mask) for device in rang...]
  transfers between devices with their start and end apart: 22 -> 22, of which waited for: 10 -> 12; matrix products, arithmetic and copies ran while one was open for 2% -> 2% of each run, Pallas kernels for 26% -> 25%
where the time goes in v22:
time: 67.3 us; the launch traced here: 67 us
  starting transfers between devices  23.4 us (35%)
  waiting for transfers between devices  20.4 us (30%)
  Pallas kernels  20.2 us (30%)
  other arithmetic  1.42 us (2%)
  local copies, waits for them, and re-layouts  0.82 us (1%)
  between operations  0.82 us (1%)
    pallas_call x16, Pallas kernels, call(): pl.pallas_call(lambda *refs: kernel(*refs[len(after):]), out_shape=[jax.S...  20.2 us
    ppermute x14, starting transfers between devices, exchange(): lax.ppermute(value, 'expert', [(device, device ^ mask) for device in rang...  14.3 us
    ppermute x8, waiting for transfers between devices, shift(): return lax.ppermute(value, 'expert', pairs)  11.1 us
    ppermute x14, waiting for transfers between devices, exchange(): lax.ppermute(value, 'expert', [(device, device ^ mask) for device in rang...  9.26 us
    ppermute x8, starting transfers between devices, shift(): return lax.ppermute(value, 'expert', pairs)  9.12 us
  transfers between devices with their start and end apart: 22, of which 12 were waited for; matrix products, arithmetic and copies ran while one was open for 2% of the time, Pallas kernels for 25%

profile of v22, /device:TPU:0, one launch (start us, length us, event | category | flops | bytes accessed | tf_op | source)
XLA Modules:
  0.0 67.0 jit_solution(12996038590200830797)
XLA Ops:
  1.2 2.0 %shard_map.147 = (s16[2,16,3200]{2,1,0:T(8,128)(2,1)}, f32[24,128]{1,0:T(8,128)}) custom-call(s32[8,128]{1,0:T(8,128)} %bitcast.32, bf16[8,128]{1,0:T(8,128)(2,1)} %bitcast.33, f32[1,128]{1,0:T(1,128)} %bitcast.34, f32[16,1024]{1,0:T(8,128)} %bitcast.30, f32[16,1024]{1,0:T(8,128)} %bitcast.31, f32[16,2048]{1,0:T(8,128)} %bitcast.28, f32[16,2048]{1,0:T(8,128)} %bitcast.29), custom_call_target="tpu_custom_call" | custom-call | flops 200000000 | bytes 1048576 | tf_op jit(solution)/shard_map/pallas_call | solution.py:456
  3.1 2.6 %collective-permute-start.4 = (s16[2,16,3200]{2,1,0:T(8,128)(2,1)}, s16[2,16,3200]{2,1,0:T(8,128)(2,1)S(1)}, u32[]{:S(2)}, u32[]{:S(2)}) collective-permute-start(s16[2,16,3200]{2,1,0:T(8,128)(2,1)} %get-tuple-element.50.refs_4_.refs_2_.refs_8_), channel_id=1, source_target_pairs={{0,2},{1,3},{4,0},{5,1},{8,4},{9,5},{12,8},{13,9},{14,12},{15,13},... | collective-permute-start | bytes 614408 | tf_op jit(solution)/shard_map/ppermute | solution.py:393
  8.9 2.2 %shard_map.148 = (f32[256,24]{1,0:T(8,128)S(1)}, f32[2,128,128]{2,1,0:T(8,128)S(1)}, f32[2,128,128]{2,1,0:T(8,128)S(1)}, bf16[1024,128]{1,0:T(8,128)(2,1)S(1)}, ...) custom-call(s32[25]{0:T(128)S(1)} %pad_add_fusion.refs_0_.refs_1_, ...), custom_call_target="tpu_custom_call" | custom-call | flops 2000000000 | bytes 1048576 | tf_op jit(solution)/shard_map/pallas_call | solution.py:456
  11.7 1.4 %collective-permute-done.3.refs_1_ = s16[2,16,3200]{2,1,0:T(8,128)(2,1)S(1)} collective-permute-done((s16[2,16,3200]{2,1,0:T(8,128)(2,1)}, s16[2,16,3200]{2,1,0:T(8,128)(2,1)S(1)}, u32[]{:S(2)}, u32[]{:S(2)}) %collective-permute-start.3) | collective-permute-done | bytes 204832 | tf_op jit(solution)/shard_map/ppermute | solution.py:393
  13.6 1.6 %collective-permute-start.6 = (s16[2,16,3200]{2,1,0:T(8,128)(2,1)S(1)}, s16[2,16,3200]{2,1,0:T(8,128)(2,1)S(1)}, u32[]{:S(2)}, u32[]{:S(2)}) collective-permute-start(s16[2,16,3200]{2,1,0:T(8,128)(2,1)S(1)} %get-tuple-element.52.refs_6_.refs_4_.refs_10_), channel_id=1, source_target_pairs={{0,2},{1,3},{4,0},{5,1},{8,4},{9,5},{12,8},{13,9},{14,12},{15,13},... | collective-permute-start | bytes 614408 | tf_op jit(solution)/shard_map/ppermute | solution.py:393
  15.2 4.4 %collective-permute-done.5.refs_7_.refs_5_.refs_11_ = s16[2,16,3200]{2,1,0:T(8,128)(2,1)S(1)} collective-permute-done((s16[2,16,3200]{2,1,0:T(8,128)(2,1)S(1)}, s16[2,16,3200]{2,1,0:T(8,128)(2,1)S(1)}, u32[]{:S(2)}, u32[]{:S(2)}) %collective-permute-start.5) | collective-permute-done | bytes 204832 | tf_op jit(solution)/shard_map/ppermute | solution.py:393
  20.4 1.2 %collective-permute-start.8 = (s16[2,16,3200]{2,1,0:T(8,128)(2,1)S(1)}, s16[2,16,3200]{2,1,0:T(8,128)(2,1)S(1)}, u32[]{:S(2)}, u32[]{:S(2)}) collective-permute-start(s16[2,16,3200]{2,1,0:T(8,128)(2,1)S(1)} %collective-permute-done.6.refs_6_.refs_5_.refs_12_), channel_id=1, source_target_pairs={{0,2},{1,3},{4,0},{5,1},{8,4},{9,5},{12,8},{13,9},{14,12},{15,13},... | collective-permute-start | bytes 614408 | tf_op jit(solution)/shard_map/ppermute | solution.py:393
  21.6 3.7 %collective-permute-done.7.refs_7_.refs_6_.refs_13_ = s16[2,16,3200]{2,1,0:T(8,128)(2,1)S(1)} collective-permute-done((s16[2,16,3200]{2,1,0:T(8,128)(2,1)S(1)}, s16[2,16,3200]{2,1,0:T(8,128)(2,1)S(1)}, u32[]{:S(2)}, u32[]{:S(2)}) %collective-permute-start.7) | collective-permute-done | bytes 204832 | tf_op jit(solution)/shard_map/ppermute | solution.py:393
  25.3 1.1 %collective-permute-start.9 = (s16[1,16,3200]{2,1,0:T(8,128)(2,1)S(1)}, s16[1,16,3200]{2,1,0:T(8,128)(2,1)S(1)}, u32[]{:S(2)}, u32[]{:S(2)}) collective-permute-start(s16[1,16,3200]{2,1,0:T(8,128)(2,1)S(1)} %slice.8), channel_id=1, source_target_pairs={{0,4},{1,5},{4,8},{5,9},{8,12},{9,13},{12,14},{13,15},{14,10},{15,... | collective-permute-start | bytes 307208 | tf_op jit(solution)/shard_map/ppermute | solution.py:393
  26.5 1.2 %collective-permute-start.11 = (s16[1,16,3200]{2,1,0:T(8,128)(2,1)S(1)}, s16[1,16,3200]{2,1,0:T(8,128)(2,1)S(1)}, u32[]{:S(2)}, u32[]{:S(2)}) collective-permute-start(s16[1,16,3200]{2,1,0:T(8,128)(2,1)S(1)} %slice.9), channel_id=1, source_target_pairs={{0,2},{1,3},{4,0},{5,1},{8,4},{9,5},{12,8},{13,9},{14,12},{15,13},... | collective-permute-start | bytes 307208 | tf_op jit(solution)/shard_map/ppermute | solution.py:393
  27.7 2.0 %shard_map.150.refs_0_.refs_6_ = f32[256,128]{1,0:T(8,128)S(1)} custom-call(s32[25]{0:T(128)S(1)} %pad_add_fusion.refs_0_.refs_1_, f32[256,24]{1,0:T(8,128)S(1)} %get-tuple-element.44.refs_1_.refs_2_.refs_0_, bf16[1024,1024]{1,0:T(8,128)(2,1)S(1)} %bitcast.24, bf16[1024,1024]{1,0:T(8,128)(2,1)S(1)} %get-tuple-element.47.refs_3_.refs_4_, ...), custom_call_target="tpu_custom_call" | custom-call | flops 1073741824 | bytes 1048576 | tf_op jit(solution)/shard_map/pallas_call | solution.py:456
  31.4 2.0 %shard_map.152.refs_7_ = f32[256,128]{1,0:T(8,128)S(1)} custom-call(f32[8,128]{1,0:T(8,128)S(1)} %shard_map.151.refs_0_.refs_4_, s32[25]{0:T(128)S(1)} %pad_add_fusion.refs_0_.refs_1_, f32[256,24]{1,0:T(8,128)S(1)} %get-tuple-element.44.refs_1_.refs_2_.refs_0_, bf16[1024,1024]{1,0:T(8,128)(2,1)S(1)} %bitcast.25, ...), custom_call_target="tpu_custom_call" | custom-call | flops 1073741824 | bytes 1048576 | tf_op jit(solution)/shard_map/pallas_call | solution.py:456
  33.4 2.3 %shard_map.153 = (f32[256,128]{1,0:T(8,128)S(1)}, f32[256,256]{1,0:T(8,128)S(1)}, f32[256,2048]{1,0:T(8,128)S(1)}, bf16[256,2048]{1,0:T(8,128)(2,1)S(1)}, bf16[2...) custom-call(s32[25]{0:T(128)S(1)} %pad_add_fusion.refs_0_.refs_1_, ...), custom_call_target="tpu_custom_call" | custom-call | flops 805306368 | bytes 1048576 | tf_op jit(solution)/shard_map/pallas_call | solution.py:456
  35.7 4.0 %shard_map.154 = (f32[2,16,3072]{2,1,0:T(8,128)S(1)}, s16[2,16,3200]{2,1,0:T(8,128)(2,1)S(1)}, f32[2,16,3072]{2,1,0:T(8,128)S(1)}, s16[2,16,3200]{2,1,0:T(8,128)...) custom-call(bf16[1024,128]{1,0:T(8,128)(2,1)S(1)} %get-tuple-element.45.refs_0_.refs_1_, ...), custom_call_target="tpu_custom_call" | custom-call | flops 2147483648 | bytes 1048576 | tf_op jit(solution)/shard_map/pallas_call | solution.py:456
  39.7 1.5 %collective-permute-start.13 = (s16[2,16,3200]{2,1,0:T(8,128)(2,1)S(1)}, s16[2,16,3200]{2,1,0:T(8,128)(2,1)S(1)}, u32[]{:S(2)}, u32[]{:S(2)}) collective-permute-start(s16[2,16,3200]{2,1,0:T(8,128)(2,1)S(1)} %get-tuple-element.63), channel_id=1, source_target_pairs={{0,4},{1,5},{2,6},{3,7},{4,0},{5,1},{6,2},{7,3},{8,12},{9,13},{10,... | collective-permute-start | bytes 614408 | tf_op jit(solution)/shard_map/ppermute | solution.py:419
  41.3 1.5 %collective-permute-start.15 = (s16[2,16,3200]{2,1,0:T(8,128)(2,1)S(1)}, s16[2,16,3200]{2,1,0:T(8,128)(2,1)S(1)}, u32[]{:S(2)}, u32[]{:S(2)}) collective-permute-start(s16[2,16,3200]{2,1,0:T(8,128)(2,1)S(1)} %get-tuple-element.69), channel_id=1, source_target_pairs={{0,2},{1,3},{2,0},{3,1},{4,6},{5,7},{6,4},{7,5},{8,10},{9,11},{10,... | collective-permute-start | bytes 614408 | tf_op jit(solution)/shard_map/ppermute | solution.py:419
  42.8 3.2 %shard_map.155 = (f32[2,16,3072]{2,1,0:T(8,128)S(1)}, s16[2,16,3200]{2,1,0:T(8,128)(2,1)S(1)}, f32[2,16,3072]{2,1,0:T(8,128)S(1)}, s16[2,16,3200]{2,1,0:T(8,128)(2,1)S(1)}) custom-call(f32[256,24]{1,0:T(8,128)S(1)} %get-tuple-element.44.refs_1_.refs_2_.refs_0_, bf16[1024,128]{1,0:T(8,128)(2,1)S(1)} %get-tuple-element.45.refs_0_.refs_1_, ...), custom_call_target="tpu_custom_call" | custom-call | flops 1879048192 | bytes 1048576 | tf_op jit(solution)/shard_map/pallas_call | solution.py:456
  47.5 1.1 %collective-permute-start.16 = (s16[16,3200]{1,0:T(8,128)(2,1)S(1)}, s16[16,3200]{1,0:T(8,128)(2,1)S(1)}, u32[]{:S(2)}, u32[]{:S(2)}) collective-permute-start(s16[16,3200]{1,0:T(8,128)(2,1)S(1)} %get-tuple-element.66.refs_0_), channel_id=1, source_target_pairs={{0,2},{1,3},{2,0},{3,1},{4,6},{5,7},{6,4},{7,5},{8,10},{9,11},{10,... | collective-permute-start | bytes 307208 | tf_op jit(solution)/shard_map/ppermute | solution.py:419
  49.6 3.0 %collective-permute-done.14.refs_1_ = s16[2,16,3200]{2,1,0:T(8,128)(2,1)S(1)} collective-permute-done((s16[2,16,3200]{2,1,0:T(8,128)(2,1)S(1)}, s16[2,16,3200]{2,1,0:T(8,128)(2,1)S(1)}, u32[]{:S(2)}, u32[]{:S(2)}) %collective-permute-start.14) | collective-permute-done | bytes 204832 | tf_op jit(solution)/shard_map/ppermute | solution.py:419
  54.0 2.5 %collective-permute-start.19 = (s16[16,3200]{1,0:T(8,128)(2,1)S(1)}, s16[16,3200]{1,0:T(8,128)(2,1)S(1)}, u32[]{:S(2)}, u32[]{:S(2)}) collective-permute-start(s16[16,3200]{1,0:T(8,128)(2,1)S(1)} %shard_map.158.refs_0_), channel_id=1, source_target_pairs={{0,8},{1,9},{2,10},{3,11},{4,12},{5,13},{6,14},{7,15},{8,0},{9,1},... | collective-permute-start | bytes 307208 | tf_op jit(solution)/shard_map/ppermute | solution.py:419
  56.5 1.0 %collective-permute-done.17.refs_2_ = s16[2,16,3200]{2,1,0:T(8,128)(2,1)S(1)} collective-permute-done((s16[2,16,3200]{2,1,0:T(8,128)(2,1)S(1)}, s16[2,16,3200]{2,1,0:T(8,128)(2,1)S(1)}, u32[]{:S(2)}, u32[]{:S(2)}) %collective-permute-start.17) | collective-permute-done | bytes 204832 | tf_op jit(solution)/shard_map/ppermute | solution.py:419
  57.8 1.5 %collective-permute-start.21 = (s16[2,16,3200]{2,1,0:T(8,128)(2,1)S(1)}, s16[2,16,3200]{2,1,0:T(8,128)(2,1)S(1)}, u32[]{:S(2)}, u32[]{:S(2)}) collective-permute-start(s16[2,16,3200]{2,1,0:T(8,128)(2,1)S(1)} %get-tuple-element.75.refs_0_), channel_id=1, source_target_pairs={{0,4},{1,5},{2,6},{3,7},{4,0},{5,1},{6,2},{7,3},{8,12},{9,13},{10,... | collective-permute-start | bytes 614408 | tf_op jit(solution)/shard_map/ppermute | solution.py:419
  59.5 2.5 %collective-permute-start.20 = (s16[16,3200]{1,0:T(8,128)(2,1)S(1)}, s16[16,3200]{1,0:T(8,128)(2,1)S(1)}, u32[]{:S(2)}, u32[]{:S(2)}) collective-permute-start(s16[16,3200]{1,0:T(8,128)(2,1)S(1)} %shard_map.160.refs_0_), channel_id=1, source_target_pairs={{0,8},{1,9},{2,10},{3,11},{4,12},{5,13},{6,14},{7,15},{8,0},{9,1},... | collective-permute-start | bytes 307208 | tf_op jit(solution)/shard_map/ppermute | solution.py:419
  62.2 3.1 %collective-permute-done.20.refs_2_ = s16[16,3200]{1,0:T(8,128)(2,1)S(1)} collective-permute-done((s16[16,3200]{1,0:T(8,128)(2,1)S(1)}, s16[16,3200]{1,0:T(8,128)(2,1)S(1)}, u32[]{:S(2)}, u32[]{:S(2)}) %collective-permute-start.20) | collective-permute-done | bytes 102432 | tf_op jit(solution)/shard_map/ppermute | solution.py:419
  (53 shorter events, 13.7 us)
Async XLA Ops:
  0.6 7.5 %collective-permute-start.1 = (bf16[1024,1024]{1,0:T(8,128)(2,1)}, bf16[1024,1024]{1,0:T(8,128)(2,1)S(1)}, u32[]{:S(2)}, u32[]{:S(2)}) collective-permute-start(bf16[1024,1024]{1,0:T(8,128)(2,1)} %bitcast.23), channel_id=1, source_target_pairs={{0,1},{1,0},{2,3},{3,2},{4,5},{5,4},{6,7},{7,6},{8,9},{9,8},{10,11... | collective-permute-start | bytes 6291464 | tf_op jit(solution)/shard_map/ppermute | solution.py:419
  3.1 8.6 %collective-permute-start.4 = (s16[2,16,3200]{2,1,0:T(8,128)(2,1)}, s16[2,16,3200]{2,1,0:T(8,128)(2,1)S(1)}, u32[]{:S(2)}, u32[]{:S(2)}) collective-permute-start(s16[2,16,3200]{2,1,0:T(8,128)(2,1)} %get-tuple-element.50.refs_4_.refs_2_.refs_8_), channel_id=1, source_target_pairs={{0,2},{1,3},{4,0},{5,1},{8,4},{9,5},{12,8},{13,9},{14,12},{15,13},... | collective-permute-start | bytes 614408 | tf_op jit(solution)/shard_map/ppermute | solution.py:393
  5.7 7.4 %collective-permute-start.3 = (s16[2,16,3200]{2,1,0:T(8,128)(2,1)}, s16[2,16,3200]{2,1,0:T(8,128)(2,1)S(1)}, u32[]{:S(2)}, u32[]{:S(2)}) collective-permute-start(s16[2,16,3200]{2,1,0:T(8,128)(2,1)} %get-tuple-element.50.refs_4_.refs_2_.refs_8_), channel_id=1, source_target_pairs={{0,4},{1,5},{4,8},{5,9},{8,12},{9,13},{12,14},{13,15},{14,10},{15,... | collective-permute-start | bytes 614408 | tf_op jit(solution)/shard_map/ppermute | solution.py:393
  5.8 1.9 %collective-permute-start = (f32[24,128]{1,0:T(8,128)}, f32[24,128]{1,0:T(8,128)S(1)}, u32[]{:S(2)}, u32[]{:S(2)}) collective-permute-start(f32[24,128]{1,0:T(8,128)} %get-tuple-element.43.refs_1_), channel_id=1, source_target_pairs={{0,1},{1,0},{2,3},{3,2},{4,5},{5,4},{6,7},{7,6},{8,9},{9,8},{10,11... | collective-permute-start | bytes 36872 | tf_op jit(solution)/shard_map/ppermute | solution.py:419
  6.0 2.1 %collective-permute-start.2 = (bf16[128,2048]{1,0:T(8,128)(2,1)}, bf16[128,2048]{1,0:T(8,128)(2,1)S(1)}, u32[]{:S(2)}, u32[]{:S(2)}) collective-permute-start(bf16[128,2048]{1,0:T(8,128)(2,1)} %refs_4_.1), channel_id=1, source_target_pairs={{0,1},{1,0},{2,3},{3,2},{4,5},{5,4},{6,7},{7,6},{8,9},{9,8},{10,11... | collective-permute-start | bytes 1572872 | tf_op jit(solution)/shard_map/ppermute | solution.py:419
  7.8 19.9 %copy-start.1 = (s16[2,16,3200]{2,1,0:T(8,128)(2,1)S(1)}, s16[2,16,3200]{2,1,0:T(8,128)(2,1)}, u32[]{:S(2)}) copy-start(s16[2,16,3200]{2,1,0:T(8,128)(2,1)} %get-tuple-element.50.refs_4_.refs_2_.refs_8_) | copy-start | bytes 614404
  8.9 18.8 %copy-start = (bf16[128,8,1024]{2,1,0:T(8,128)(2,1)S(1)}, bf16[128,8,1024]{2,1,0:T(8,128)(2,1)}, u32[]{:S(2)}) copy-start(bf16[128,8,1024]{2,1,0:T(8,128)(2,1)} %param.12) | copy-start | bytes 6291460
  13.1 6.4 %collective-permute-start.5 = (s16[2,16,3200]{2,1,0:T(8,128)(2,1)S(1)}, s16[2,16,3200]{2,1,0:T(8,128)(2,1)S(1)}, u32[]{:S(2)}, u32[]{:S(2)}) collective-permute-start(s16[2,16,3200]{2,1,0:T(8,128)(2,1)S(1)} %get-tuple-element.51.refs_5_.refs_3_.refs_9_), channel_id=1, source_target_pairs={{0,4},{1,5},{4,8},{5,9},{8,12},{9,13},{12,14},{13,15},{14,10},{15,... | collective-permute-start | bytes 614408 | tf_op jit(solution)/shard_map/ppermute | solution.py:393
  13.6 6.8 %collective-permute-start.6 = (s16[2,16,3200]{2,1,0:T(8,128)(2,1)S(1)}, s16[2,16,3200]{2,1,0:T(8,128)(2,1)S(1)}, u32[]{:S(2)}, u32[]{:S(2)}) collective-permute-start(s16[2,16,3200]{2,1,0:T(8,128)(2,1)S(1)} %get-tuple-element.52.refs_6_.refs_4_.refs_10_), channel_id=1, source_target_pairs={{0,2},{1,3},{4,0},{5,1},{8,4},{9,5},{12,8},{13,9},{14,12},{15,13},... | collective-permute-start | bytes 614408 | tf_op jit(solution)/shard_map/ppermute | solution.py:393
  19.5 5.8 %collective-permute-start.7 = (s16[2,16,3200]{2,1,0:T(8,128)(2,1)S(1)}, s16[2,16,3200]{2,1,0:T(8,128)(2,1)S(1)}, u32[]{:S(2)}, u32[]{:S(2)}) collective-permute-start(s16[2,16,3200]{2,1,0:T(8,128)(2,1)S(1)} %collective-permute-done.5.refs_7_.refs_5_.refs_11_), channel_id=1, source_target_pairs={{0,4},{1,5},{4,8},{5,9},{8,12},{9,13},{12,14},{13,15},{14,10},{15,... | collective-permute-start | bytes 614408 | tf_op jit(solution)/shard_map/ppermute | solution.py:393
  20.4 6.1 %collective-permute-start.8 = (s16[2,16,3200]{2,1,0:T(8,128)(2,1)S(1)}, s16[2,16,3200]{2,1,0:T(8,128)(2,1)S(1)}, u32[]{:S(2)}, u32[]{:S(2)}) collective-permute-start(s16[2,16,3200]{2,1,0:T(8,128)(2,1)S(1)} %collective-permute-done.6.refs_6_.refs_5_.refs_12_), channel_id=1, source_target_pairs={{0,2},{1,3},{4,0},{5,1},{8,4},{9,5},{12,8},{13,9},{14,12},{15,13},... | collective-permute-start | bytes 614408 | tf_op jit(solution)/shard_map/ppermute | solution.py:393
  25.3 4.7 %collective-permute-start.9 = (s16[1,16,3200]{2,1,0:T(8,128)(2,1)S(1)}, s16[1,16,3200]{2,1,0:T(8,128)(2,1)S(1)}, u32[]{:S(2)}, u32[]{:S(2)}) collective-permute-start(s16[1,16,3200]{2,1,0:T(8,128)(2,1)S(1)} %slice.8), channel_id=1, source_target_pairs={{0,4},{1,5},{4,8},{5,9},{8,12},{9,13},{12,14},{13,15},{14,10},{15,... | collective-permute-start | bytes 307208 | tf_op jit(solution)/shard_map/ppermute | solution.py:393
  26.5 4.9 %collective-permute-start.11 = (s16[1,16,3200]{2,1,0:T(8,128)(2,1)S(1)}, s16[1,16,3200]{2,1,0:T(8,128)(2,1)S(1)}, u32[]{:S(2)}, u32[]{:S(2)}) collective-permute-start(s16[1,16,3200]{2,1,0:T(8,128)(2,1)S(1)} %slice.9), channel_id=1, source_target_pairs={{0,2},{1,3},{4,0},{5,1},{8,4},{9,5},{12,8},{13,9},{14,12},{15,13},... | collective-permute-start | bytes 307208 | tf_op jit(solution)/shard_map/ppermute | solution.py:393
  30.6 2.8 %collective-permute-start.10 = (f32[8,128]{1,0:T(8,128)S(1)}, f32[8,128]{1,0:T(8,128)S(1)}, u32[]{:S(2)}, u32[]{:S(2)}) collective-permute-start(f32[8,128]{1,0:T(8,128)S(1)} %shard_map.151.refs_0_.refs_4_), channel_id=1, source_target_pairs={{0,1},{1,0},{2,3},{3,2},{4,5},{5,4},{6,7},{7,6},{8,9},{9,8},{10,11... | collective-permute-start | bytes 12296 | tf_op jit(solution)/shard_map/ppermute | solution.py:419
  35.7 7.1 %collective-permute-start.12 = (bf16[256,2048]{1,0:T(8,128)(2,1)S(1)}, bf16[256,2048]{1,0:T(8,128)(2,1)S(1)}, u32[]{:S(2)}, u32[]{:S(2)}) collective-permute-start(bf16[256,2048]{1,0:T(8,128)(2,1)S(1)} %get-tuple-element.61), channel_id=1, source_target_pairs={{0,1},{1,0},{2,3},{3,2},{4,5},{5,4},{6,7},{7,6},{8,9},{9,8},{10,11... | collective-permute-start | bytes 3145736 | tf_op jit(solution)/shard_map/ppermute | solution.py:419
  39.7 7.5 %collective-permute-start.13 = (s16[2,16,3200]{2,1,0:T(8,128)(2,1)S(1)}, s16[2,16,3200]{2,1,0:T(8,128)(2,1)S(1)}, u32[]{:S(2)}, u32[]{:S(2)}) collective-permute-start(s16[2,16,3200]{2,1,0:T(8,128)(2,1)S(1)} %get-tuple-element.63), channel_id=1, source_target_pairs={{0,4},{1,5},{2,6},{3,7},{4,0},{5,1},{6,2},{7,3},{8,12},{9,13},{10,... | collective-permute-start | bytes 614408 | tf_op jit(solution)/shard_map/ppermute | solution.py:419
  41.3 8.3 %collective-permute-start.15 = (s16[2,16,3200]{2,1,0:T(8,128)(2,1)S(1)}, s16[2,16,3200]{2,1,0:T(8,128)(2,1)S(1)}, u32[]{:S(2)}, u32[]{:S(2)}) collective-permute-start(s16[2,16,3200]{2,1,0:T(8,128)(2,1)S(1)} %get-tuple-element.69), channel_id=1, source_target_pairs={{0,2},{1,3},{2,0},{3,1},{4,6},{5,7},{6,4},{7,5},{8,10},{9,11},{10,... | collective-permute-start | bytes 614408 | tf_op jit(solution)/shard_map/ppermute | solution.py:419
  46.0 6.6 %collective-permute-start.14 = (s16[2,16,3200]{2,1,0:T(8,128)(2,1)S(1)}, s16[2,16,3200]{2,1,0:T(8,128)(2,1)S(1)}, u32[]{:S(2)}, u32[]{:S(2)}) collective-permute-start(s16[2,16,3200]{2,1,0:T(8,128)(2,1)S(1)} %get-tuple-element.67), channel_id=1, source_target_pairs={{0,4},{1,5},{2,6},{3,7},{4,0},{5,1},{6,2},{7,3},{8,12},{9,13},{10,... | collective-permute-start | bytes 614408 | tf_op jit(solution)/shard_map/ppermute | solution.py:419
  47.5 6.3 %collective-permute-start.16 = (s16[16,3200]{1,0:T(8,128)(2,1)S(1)}, s16[16,3200]{1,0:T(8,128)(2,1)S(1)}, u32[]{:S(2)}, u32[]{:S(2)}) collective-permute-start(s16[16,3200]{1,0:T(8,128)(2,1)S(1)} %get-tuple-element.66.refs_0_), channel_id=1, source_target_pairs={{0,2},{1,3},{2,0},{3,1},{4,6},{5,7},{6,4},{7,5},{8,10},{9,11},{10,... | collective-permute-start | bytes 307208 | tf_op jit(solution)/shard_map/ppermute | solution.py:419
  48.6 9.0 %collective-permute-start.17 = (s16[2,16,3200]{2,1,0:T(8,128)(2,1)S(1)}, s16[2,16,3200]{2,1,0:T(8,128)(2,1)S(1)}, u32[]{:S(2)}, u32[]{:S(2)}) collective-permute-start(s16[2,16,3200]{2,1,0:T(8,128)(2,1)S(1)} %get-tuple-element.73), channel_id=1, source_target_pairs={{0,2},{1,3},{2,0},{3,1},{4,6},{5,7},{6,4},{7,5},{8,10},{9,11},{10,... | collective-permute-start | bytes 614408 | tf_op jit(solution)/shard_map/ppermute | solution.py:419
  52.8 6.5 %collective-permute-start.18 = (s16[16,3200]{1,0:T(8,128)(2,1)S(1)}, s16[16,3200]{1,0:T(8,128)(2,1)S(1)}, u32[]{:S(2)}, u32[]{:S(2)}) collective-permute-start(s16[16,3200]{1,0:T(8,128)(2,1)S(1)} %get-tuple-element.70.refs_0_), channel_id=1, source_target_pairs={{0,2},{1,3},{2,0},{3,1},{4,6},{5,7},{6,4},{7,5},{8,10},{9,11},{10,... | collective-permute-start | bytes 307208 | tf_op jit(solution)/shard_map/ppermute | solution.py:419
  54.0 8.1 %collective-permute-start.19 = (s16[16,3200]{1,0:T(8,128)(2,1)S(1)}, s16[16,3200]{1,0:T(8,128)(2,1)S(1)}, u32[]{:S(2)}, u32[]{:S(2)}) collective-permute-start(s16[16,3200]{1,0:T(8,128)(2,1)S(1)} %shard_map.158.refs_0_), channel_id=1, source_target_pairs={{0,8},{1,9},{2,10},{3,11},{4,12},{5,13},{6,14},{7,15},{8,0},{9,1},... | collective-permute-start | bytes 307208 | tf_op jit(solution)/shard_map/ppermute | solution.py:419
  57.8 8.4 %collective-permute-start.21 = (s16[2,16,3200]{2,1,0:T(8,128)(2,1)S(1)}, s16[2,16,3200]{2,1,0:T(8,128)(2,1)S(1)}, u32[]{:S(2)}, u32[]{:S(2)}) collective-permute-start(s16[2,16,3200]{2,1,0:T(8,128)(2,1)S(1)} %get-tuple-element.75.refs_0_), channel_id=1, source_target_pairs={{0,4},{1,5},{2,6},{3,7},{4,0},{5,1},{6,2},{7,3},{8,12},{9,13},{10,... | collective-permute-start | bytes 614408 | tf_op jit(solution)/shard_map/ppermute | solution.py:419
  59.5 5.7 %collective-permute-start.20 = (s16[16,3200]{1,0:T(8,128)(2,1)S(1)}, s16[16,3200]{1,0:T(8,128)(2,1)S(1)}, u32[]{:S(2)}, u32[]{:S(2)}) collective-permute-start(s16[16,3200]{1,0:T(8,128)(2,1)S(1)} %shard_map.160.refs_0_), channel_id=1, source_target_pairs={{0,8},{1,9},{2,10},{3,11},{4,12},{5,13},{6,14},{7,15},{8,0},{9,1},... | collective-permute-start | bytes 307208 | tf_op jit(solution)/shard_map/ppermute | solution.py:419
  (3 other events, 17.0 us)

commit v23 on v18

--- a/solution.py
+++ b/solution.py
@@ -320,13 +320,13 @@
     block = tokens // 2
     model_width = up_ref.shape[1]
     arrived = jnp.concatenate([arrived_ref[block:], arrived_ref[:block]], axis=0).astype(f32)
-    resid = halves(curvature * (tangent_ref[...] + arrived))
+    resid = (curvature * (tangent_ref[...] + arrived)).astype(bf16)
     adapter_up = high_ref[0].reshape(wide, model_width), low_ref[0].reshape(wide, model_width)
-    terms = weight_ref[...] * (dot_pairs(resid, adapter_up, 1, 1) + to_ref[...])
+    terms = weight_ref[...] * (dot(resid, adapter_up[0], 1, 1) + dot(resid, adapter_up[1], 1, 1) + to_ref[...])
     put_left(left_ref, same_ref, mask_ref, terms)
     down = dot(left_ref[0], own_ref[...], 0, 0) + dot(left_ref[1], other_ref[...], 0, 0)
     weighted_u = halves(weighted_ref[:, wide:])
-    up = add_halves(dot(jnp.concatenate(weighted_u, axis=1), resid[0], 0, 0)) + dot(weighted_u[0], resid[1], 0, 0)
+    up = add_halves(dot(jnp.concatenate(weighted_u, axis=1), resid, 0, 0))
     put_chunks(keep_ref, near_ref, chunk_ref, far_ref, add_halves(down), up_ref[...] + up)
 
 

time: 66.9 us -> 66.9 us (level)
  transfers between devices with their start and end apart: 22 -> 22, of which waited for: 10 -> 10; matrix products, arithmetic and copies ran while one was open for 2% -> 2% of each run, Pallas kernels for 26% -> 25%
where the time goes in v23:
time: 66.9 us; the launch traced here: 66.6 us
  starting transfers between devices  24.3 us (36%)
  Pallas kernels  19.7 us (29%)
  waiting for transfers between devices  19.5 us (29%)
  other arithmetic  1.43 us (2%)
  local copies, waits for them, and re-layouts  0.85 us (1%)
  between operations  0.81 us (1%)
    pallas_call x16, Pallas kernels, call(): pl.pallas_call(lambda *refs: kernel(*refs[len(after):]), out_shape=[jax.S...  19.7 us
    ppermute x14, starting transfers between devices, exchange(): lax.ppermute(value, 'expert', [(device, device ^ mask) for device in rang...  15.2 us
    ppermute x8, waiting for transfers between devices, shift(): return lax.ppermute(value, 'expert', pairs)  11.3 us
    ppermute x8, starting transfers between devices, shift(): return lax.ppermute(value, 'expert', pairs)  9.12 us
    ppermute x14, waiting for transfers between devices, exchange(): lax.ppermute(value, 'expert', [(device, device ^ mask) for device in rang...  8.2 us
  transfers between devices with their start and end apart: 22, of which 10 were waited for; matrix products, arithmetic and copies ran while one was open for 2% of the time, Pallas kernels for 25%

profile of v23, /device:TPU:0, one launch (start us, length us, event | category | flops | bytes accessed | tf_op | source)
XLA Modules:
  0.0 66.6 jit_solution(11150837910338088235)
XLA Ops:
  1.2 2.0 %shard_map.147 = (s16[2,16,3200]{2,1,0:T(8,128)(2,1)}, f32[24,128]{1,0:T(8,128)}) custom-call(s32[8,128]{1,0:T(8,128)} %bitcast.32, bf16[8,128]{1,0:T(8,128)(2,1)} %bitcast.33, f32[1,128]{1,0:T(1,128)} %bitcast.34, f32[16,1024]{1,0:T(8,128)} %bitcast.30, f32[16,1024]{1,0:T(8,128)} %bitcast.31, f32[16,2048]{1,0:T(8,128)} %bitcast.28, f32[16,2048]{1,0:T(8,128)} %bitcast.29), custom_call_target="tpu_custom_call" | custom-call | flops 200000000 | bytes 1048576 | tf_op jit(solution)/shard_map/pallas_call | solution.py:456
  3.1 2.6 %collective-permute-start.4 = (s16[2,16,3200]{2,1,0:T(8,128)(2,1)}, s16[2,16,3200]{2,1,0:T(8,128)(2,1)S(1)}, u32[]{:S(2)}, u32[]{:S(2)}) collective-permute-start(s16[2,16,3200]{2,1,0:T(8,128)(2,1)} %get-tuple-element.50.refs_4_.refs_2_.refs_8_), channel_id=1, source_target_pairs={{0,2},{1,3},{4,0},{5,1},{8,4},{9,5},{12,8},{13,9},{14,12},{15,13},... | collective-permute-start | bytes 614408 | tf_op jit(solution)/shard_map/ppermute | solution.py:393
  7.7 4.0 %collective-permute-done.4.refs_6_.refs_4_.refs_10_ = s16[2,16,3200]{2,1,0:T(8,128)(2,1)S(1)} collective-permute-done((s16[2,16,3200]{2,1,0:T(8,128)(2,1)}, s16[2,16,3200]{2,1,0:T(8,128)(2,1)S(1)}, u32[]{:S(2)}, u32[]{:S(2)}) %collective-permute-start.4) | collective-permute-done | bytes 204832 | tf_op jit(solution)/shard_map/ppermute | solution.py:393
  11.7 1.7 %collective-permute-start.6 = (s16[2,16,3200]{2,1,0:T(8,128)(2,1)S(1)}, s16[2,16,3200]{2,1,0:T(8,128)(2,1)S(1)}, u32[]{:S(2)}, u32[]{:S(2)}) collective-permute-start(s16[2,16,3200]{2,1,0:T(8,128)(2,1)S(1)} %collective-permute-done.4.refs_6_.refs_4_.refs_10_), channel_id=1, source_target_pairs={{0,2},{1,3},{4,0},{5,1},{8,4},{9,5},{12,8},{13,9},{14,12},{15,13},... | collective-permute-start | bytes 614408 | tf_op jit(solution)/shard_map/ppermute | solution.py:393
  14.6 2.2 %shard_map.148 = (f32[256,24]{1,0:T(8,128)S(1)}, f32[2,128,128]{2,1,0:T(8,128)S(1)}, f32[2,128,128]{2,1,0:T(8,128)S(1)}, bf16[1024,128]{1,0:T(8,128)(2,1)S(1)}, ...) custom-call(s32[25]{0:T(128)S(1)} %pad_add_fusion.refs_0_.refs_1_, ...), custom_call_target="tpu_custom_call" | custom-call | flops 2000000000 | bytes 1048576 | tf_op jit(solution)/shard_map/pallas_call | solution.py:456
  16.8 1.9 %collective-permute-done.6.refs_2_ = s16[2,16,3200]{2,1,0:T(8,128)(2,1)S(1)} collective-permute-done((s16[2,16,3200]{2,1,0:T(8,128)(2,1)S(1)}, s16[2,16,3200]{2,1,0:T(8,128)(2,1)S(1)}, u32[]{:S(2)}, u32[]{:S(2)}) %collective-permute-start.6) | collective-permute-done | bytes 204832 | tf_op jit(solution)/shard_map/ppermute | solution.py:393
  18.6 1.2 %collective-permute-done.5.refs_1_ = s16[2,16,3200]{2,1,0:T(8,128)(2,1)S(1)} collective-permute-done((s16[2,16,3200]{2,1,0:T(8,128)(2,1)S(1)}, s16[2,16,3200]{2,1,0:T(8,128)(2,1)S(1)}, u32[]{:S(2)}, u32[]{:S(2)}) %collective-permute-start.5) | collective-permute-done | bytes 204832 | tf_op jit(solution)/shard_map/ppermute | solution.py:393
  20.4 1.5 %collective-permute-start.8 = (s16[2,16,3200]{2,1,0:T(8,128)(2,1)S(1)}, s16[2,16,3200]{2,1,0:T(8,128)(2,1)S(1)}, u32[]{:S(2)}, u32[]{:S(2)}) collective-permute-start(s16[2,16,3200]{2,1,0:T(8,128)(2,1)S(1)} %get-tuple-element.52.refs_6_.refs_5_.refs_12_), channel_id=1, source_target_pairs={{0,2},{1,3},{4,0},{5,1},{8,4},{9,5},{12,8},{13,9},{14,12},{15,13},... | collective-permute-start | bytes 614408 | tf_op jit(solution)/shard_map/ppermute | solution.py:393
  21.9 3.7 %collective-permute-done.7.refs_7_.refs_6_.refs_13_ = s16[2,16,3200]{2,1,0:T(8,128)(2,1)S(1)} collective-permute-done((s16[2,16,3200]{2,1,0:T(8,128)(2,1)S(1)}, s16[2,16,3200]{2,1,0:T(8,128)(2,1)S(1)}, u32[]{:S(2)}, u32[]{:S(2)}) %collective-permute-start.7) | collective-permute-done | bytes 204832 | tf_op jit(solution)/shard_map/ppermute | solution.py:393
  26.3 1.7 %collective-permute-start.11 = (s16[1,16,3200]{2,1,0:T(8,128)(2,1)S(1)}, s16[1,16,3200]{2,1,0:T(8,128)(2,1)S(1)}, u32[]{:S(2)}, u32[]{:S(2)}) collective-permute-start(s16[1,16,3200]{2,1,0:T(8,128)(2,1)S(1)} %slice.9), channel_id=1, source_target_pairs={{0,2},{1,3},{4,0},{5,1},{8,4},{9,5},{12,8},{13,9},{14,12},{15,13},... | collective-permute-start | bytes 307208 | tf_op jit(solution)/shard_map/ppermute | solution.py:393
  28.0 2.0 %shard_map.150.refs_0_.refs_6_ = f32[256,128]{1,0:T(8,128)S(1)} custom-call(s32[25]{0:T(128)S(1)} %pad_add_fusion.refs_0_.refs_1_, f32[256,24]{1,0:T(8,128)S(1)} %get-tuple-element.44.refs_1_.refs_2_.refs_0_, bf16[1024,1024]{1,0:T(8,128)(2,1)S(1)} %bitcast.24, bf16[1024,1024]{1,0:T(8,128)(2,1)S(1)} %get-tuple-element.47.refs_3_.refs_4_, ...), custom_call_target="tpu_custom_call" | custom-call | flops 1073741824 | bytes 1048576 | tf_op jit(solution)/shard_map/pallas_call | solution.py:456
  31.2 2.0 %shard_map.152.refs_7_ = f32[256,128]{1,0:T(8,128)S(1)} custom-call(f32[8,128]{1,0:T(8,128)S(1)} %shard_map.151.refs_0_.refs_4_, s32[25]{0:T(128)S(1)} %pad_add_fusion.refs_0_.refs_1_, f32[256,24]{1,0:T(8,128)S(1)} %get-tuple-element.44.refs_1_.refs_2_.refs_0_, bf16[1024,1024]{1,0:T(8,128)(2,1)S(1)} %bitcast.25, ...), custom_call_target="tpu_custom_call" | custom-call | flops 1073741824 | bytes 1048576 | tf_op jit(solution)/shard_map/pallas_call | solution.py:456
  33.3 2.3 %shard_map.153 = (f32[256,128]{1,0:T(8,128)S(1)}, f32[256,256]{1,0:T(8,128)S(1)}, f32[256,2048]{1,0:T(8,128)S(1)}, bf16[256,2048]{1,0:T(8,128)(2,1)S(1)}, bf16[2...) custom-call(s32[25]{0:T(128)S(1)} %pad_add_fusion.refs_0_.refs_1_, ...), custom_call_target="tpu_custom_call" | custom-call | flops 805306368 | bytes 1048576 | tf_op jit(solution)/shard_map/pallas_call | solution.py:456
  35.9 4.0 %shard_map.154 = (f32[2,16,3072]{2,1,0:T(8,128)S(1)}, s16[2,16,3200]{2,1,0:T(8,128)(2,1)S(1)}, f32[2,16,3072]{2,1,0:T(8,128)S(1)}, s16[2,16,3200]{2,1,0:T(8,128)...) custom-call(bf16[1024,128]{1,0:T(8,128)(2,1)S(1)} %get-tuple-element.45.refs_0_.refs_1_, ...), custom_call_target="tpu_custom_call" | custom-call | flops 2147483648 | bytes 1048576 | tf_op jit(solution)/shard_map/pallas_call | solution.py:456
  39.9 1.4 %collective-permute-start.13 = (s16[2,16,3200]{2,1,0:T(8,128)(2,1)S(1)}, s16[2,16,3200]{2,1,0:T(8,128)(2,1)S(1)}, u32[]{:S(2)}, u32[]{:S(2)}) collective-permute-start(s16[2,16,3200]{2,1,0:T(8,128)(2,1)S(1)} %get-tuple-element.63), channel_id=1, source_target_pairs={{0,4},{1,5},{2,6},{3,7},{4,0},{5,1},{6,2},{7,3},{8,12},{9,13},{10,... | collective-permute-start | bytes 614408 | tf_op jit(solution)/shard_map/ppermute | solution.py:419
  41.2 1.8 %collective-permute-start.15 = (s16[2,16,3200]{2,1,0:T(8,128)(2,1)S(1)}, s16[2,16,3200]{2,1,0:T(8,128)(2,1)S(1)}, u32[]{:S(2)}, u32[]{:S(2)}) collective-permute-start(s16[2,16,3200]{2,1,0:T(8,128)(2,1)S(1)} %get-tuple-element.69), channel_id=1, source_target_pairs={{0,2},{1,3},{2,0},{3,1},{4,6},{5,7},{6,4},{7,5},{8,10},{9,11},{10,... | collective-permute-start | bytes 614408 | tf_op jit(solution)/shard_map/ppermute | solution.py:419
  43.1 2.7 %shard_map.155 = (f32[2,16,3072]{2,1,0:T(8,128)S(1)}, s16[2,16,3200]{2,1,0:T(8,128)(2,1)S(1)}, f32[2,16,3072]{2,1,0:T(8,128)S(1)}, s16[2,16,3200]{2,1,0:T(8,128)(2,1)S(1)}) custom-call(f32[256,24]{1,0:T(8,128)S(1)} %get-tuple-element.44.refs_1_.refs_2_.refs_0_, bf16[1024,128]{1,0:T(8,128)(2,1)S(1)} %get-tuple-element.45.refs_0_.refs_1_, ...), custom_call_target="tpu_custom_call" | custom-call | flops 1879048192 | bytes 1048576 | tf_op jit(solution)/shard_map/pallas_call | solution.py:456
  47.4 1.5 %collective-permute-start.16 = (s16[16,3200]{1,0:T(8,128)(2,1)S(1)}, s16[16,3200]{1,0:T(8,128)(2,1)S(1)}, u32[]{:S(2)}, u32[]{:S(2)}) collective-permute-start(s16[16,3200]{1,0:T(8,128)(2,1)S(1)} %get-tuple-element.66.refs_0_), channel_id=1, source_target_pairs={{0,2},{1,3},{2,0},{3,1},{4,6},{5,7},{6,4},{7,5},{8,10},{9,11},{10,... | collective-permute-start | bytes 307208 | tf_op jit(solution)/shard_map/ppermute | solution.py:419
  49.5 2.9 %collective-permute-done.14.refs_1_ = s16[2,16,3200]{2,1,0:T(8,128)(2,1)S(1)} collective-permute-done((s16[2,16,3200]{2,1,0:T(8,128)(2,1)S(1)}, s16[2,16,3200]{2,1,0:T(8,128)(2,1)S(1)}, u32[]{:S(2)}, u32[]{:S(2)}) %collective-permute-start.14) | collective-permute-done | bytes 204832 | tf_op jit(solution)/shard_map/ppermute | solution.py:419
  53.5 2.7 %collective-permute-start.19 = (s16[16,3200]{1,0:T(8,128)(2,1)S(1)}, s16[16,3200]{1,0:T(8,128)(2,1)S(1)}, u32[]{:S(2)}, u32[]{:S(2)}) collective-permute-start(s16[16,3200]{1,0:T(8,128)(2,1)S(1)} %shard_map.158.refs_0_), channel_id=1, source_target_pairs={{0,8},{1,9},{2,10},{3,11},{4,12},{5,13},{6,14},{7,15},{8,0},{9,1},... | collective-permute-start | bytes 307208 | tf_op jit(solution)/shard_map/ppermute | solution.py:419
  56.1 1.0 %collective-permute-done.17.refs_2_ = s16[2,16,3200]{2,1,0:T(8,128)(2,1)S(1)} collective-permute-done((s16[2,16,3200]{2,1,0:T(8,128)(2,1)S(1)}, s16[2,16,3200]{2,1,0:T(8,128)(2,1)S(1)}, u32[]{:S(2)}, u32[]{:S(2)}) %collective-permute-start.17) | collective-permute-done | bytes 204832 | tf_op jit(solution)/shard_map/ppermute | solution.py:419
  57.4 1.9 %collective-permute-start.21 = (s16[2,16,3200]{2,1,0:T(8,128)(2,1)S(1)}, s16[2,16,3200]{2,1,0:T(8,128)(2,1)S(1)}, u32[]{:S(2)}, u32[]{:S(2)}) collective-permute-start(s16[2,16,3200]{2,1,0:T(8,128)(2,1)S(1)} %get-tuple-element.75.refs_0_), channel_id=1, source_target_pairs={{0,4},{1,5},{2,6},{3,7},{4,0},{5,1},{6,2},{7,3},{8,12},{9,13},{10,... | collective-permute-start | bytes 614408 | tf_op jit(solution)/shard_map/ppermute | solution.py:419
  59.5 2.8 %collective-permute-start.20 = (s16[16,3200]{1,0:T(8,128)(2,1)S(1)}, s16[16,3200]{1,0:T(8,128)(2,1)S(1)}, u32[]{:S(2)}, u32[]{:S(2)}) collective-permute-start(s16[16,3200]{1,0:T(8,128)(2,1)S(1)} %shard_map.160.refs_0_), channel_id=1, source_target_pairs={{0,8},{1,9},{2,10},{3,11},{4,12},{5,13},{6,14},{7,15},{8,0},{9,1},... | collective-permute-start | bytes 307208 | tf_op jit(solution)/shard_map/ppermute | solution.py:419
  62.4 3.4 %collective-permute-done.21.refs_3_ = s16[2,16,3200]{2,1,0:T(8,128)(2,1)S(1)} collective-permute-done((s16[2,16,3200]{2,1,0:T(8,128)(2,1)S(1)}, s16[2,16,3200]{2,1,0:T(8,128)(2,1)S(1)}, u32[]{:S(2)}, u32[]{:S(2)}) %collective-permute-start.21) | collective-permute-done | bytes 204832 | tf_op jit(solution)/shard_map/ppermute | solution.py:419
  (53 shorter events, 11.2 us)
Async XLA Ops:
  0.6 13.2 %collective-permute-start.1 = (bf16[1024,1024]{1,0:T(8,128)(2,1)}, bf16[1024,1024]{1,0:T(8,128)(2,1)S(1)}, u32[]{:S(2)}, u32[]{:S(2)}) collective-permute-start(bf16[1024,1024]{1,0:T(8,128)(2,1)} %bitcast.23), channel_id=1, source_target_pairs={{0,1},{1,0},{2,3},{3,2},{4,5},{5,4},{6,7},{7,6},{8,9},{9,8},{10,11... | collective-permute-start | bytes 6291464 | tf_op jit(solution)/shard_map/ppermute | solution.py:419
  3.1 8.6 %collective-permute-start.4 = (s16[2,16,3200]{2,1,0:T(8,128)(2,1)}, s16[2,16,3200]{2,1,0:T(8,128)(2,1)S(1)}, u32[]{:S(2)}, u32[]{:S(2)}) collective-permute-start(s16[2,16,3200]{2,1,0:T(8,128)(2,1)} %get-tuple-element.50.refs_4_.refs_2_.refs_8_), channel_id=1, source_target_pairs={{0,2},{1,3},{4,0},{5,1},{8,4},{9,5},{12,8},{13,9},{14,12},{15,13},... | collective-permute-start | bytes 614408 | tf_op jit(solution)/shard_map/ppermute | solution.py:393
  5.7 7.7 %collective-permute-start.3 = (s16[2,16,3200]{2,1,0:T(8,128)(2,1)}, s16[2,16,3200]{2,1,0:T(8,128)(2,1)S(1)}, u32[]{:S(2)}, u32[]{:S(2)}) collective-permute-start(s16[2,16,3200]{2,1,0:T(8,128)(2,1)} %get-tuple-element.50.refs_4_.refs_2_.refs_8_), channel_id=1, source_target_pairs={{0,4},{1,5},{4,8},{5,9},{8,12},{9,13},{12,14},{13,15},{14,10},{15,... | collective-permute-start | bytes 614408 | tf_op jit(solution)/shard_map/ppermute | solution.py:393
  5.8 8.0 %collective-permute-start = (f32[24,128]{1,0:T(8,128)}, f32[24,128]{1,0:T(8,128)S(1)}, u32[]{:S(2)}, u32[]{:S(2)}) collective-permute-start(f32[24,128]{1,0:T(8,128)} %get-tuple-element.43.refs_1_), channel_id=1, source_target_pairs={{0,1},{1,0},{2,3},{3,2},{4,5},{5,4},{6,7},{7,6},{8,9},{9,8},{10,11... | collective-permute-start | bytes 36872 | tf_op jit(solution)/shard_map/ppermute | solution.py:419
  6.0 7.8 %collective-permute-start.2 = (bf16[128,2048]{1,0:T(8,128)(2,1)}, bf16[128,2048]{1,0:T(8,128)(2,1)S(1)}, u32[]{:S(2)}, u32[]{:S(2)}) collective-permute-start(bf16[128,2048]{1,0:T(8,128)(2,1)} %refs_4_.1), channel_id=1, source_target_pairs={{0,1},{1,0},{2,3},{3,2},{4,5},{5,4},{6,7},{7,6},{8,9},{9,8},{10,11... | collective-permute-start | bytes 1572872 | tf_op jit(solution)/shard_map/ppermute | solution.py:419
  11.7 6.9 %collective-permute-start.6 = (s16[2,16,3200]{2,1,0:T(8,128)(2,1)S(1)}, s16[2,16,3200]{2,1,0:T(8,128)(2,1)S(1)}, u32[]{:S(2)}, u32[]{:S(2)}) collective-permute-start(s16[2,16,3200]{2,1,0:T(8,128)(2,1)S(1)} %collective-permute-done.4.refs_6_.refs_4_.refs_10_), channel_id=1, source_target_pairs={{0,2},{1,3},{4,0},{5,1},{8,4},{9,5},{12,8},{13,9},{14,12},{15,13},... | collective-permute-start | bytes 614408 | tf_op jit(solution)/shard_map/ppermute | solution.py:393
  13.4 6.4 %collective-permute-start.5 = (s16[2,16,3200]{2,1,0:T(8,128)(2,1)S(1)}, s16[2,16,3200]{2,1,0:T(8,128)(2,1)S(1)}, u32[]{:S(2)}, u32[]{:S(2)}) collective-permute-start(s16[2,16,3200]{2,1,0:T(8,128)(2,1)S(1)} %collective-permute-done.3.refs_5_.refs_3_.refs_9_), channel_id=1, source_target_pairs={{0,4},{1,5},{4,8},{5,9},{8,12},{9,13},{12,14},{13,15},{14,10},{15,... | collective-permute-start | bytes 614408 | tf_op jit(solution)/shard_map/ppermute | solution.py:393
  13.8 14.2 %copy-start.1 = (s16[2,16,3200]{2,1,0:T(8,128)(2,1)S(1)}, s16[2,16,3200]{2,1,0:T(8,128)(2,1)}, u32[]{:S(2)}) copy-start(s16[2,16,3200]{2,1,0:T(8,128)(2,1)} %get-tuple-element.50.refs_4_.refs_2_.refs_8_) | copy-start | bytes 614404
  14.6 13.5 %copy-start = (bf16[128,8,1024]{2,1,0:T(8,128)(2,1)S(1)}, bf16[128,8,1024]{2,1,0:T(8,128)(2,1)}, u32[]{:S(2)}) copy-start(bf16[128,8,1024]{2,1,0:T(8,128)(2,1)} %param.12) | copy-start | bytes 6291460
  19.8 5.8 %collective-permute-start.7 = (s16[2,16,3200]{2,1,0:T(8,128)(2,1)S(1)}, s16[2,16,3200]{2,1,0:T(8,128)(2,1)S(1)}, u32[]{:S(2)}, u32[]{:S(2)}) collective-permute-start(s16[2,16,3200]{2,1,0:T(8,128)(2,1)S(1)} %get-tuple-element.51.refs_7_.refs_5_.refs_11_), channel_id=1, source_target_pairs={{0,4},{1,5},{4,8},{5,9},{8,12},{9,13},{12,14},{13,15},{14,10},{15,... | collective-permute-start | bytes 614408 | tf_op jit(solution)/shard_map/ppermute | solution.py:393
  20.4 5.9 %collective-permute-start.8 = (s16[2,16,3200]{2,1,0:T(8,128)(2,1)S(1)}, s16[2,16,3200]{2,1,0:T(8,128)(2,1)S(1)}, u32[]{:S(2)}, u32[]{:S(2)}) collective-permute-start(s16[2,16,3200]{2,1,0:T(8,128)(2,1)S(1)} %get-tuple-element.52.refs_6_.refs_5_.refs_12_), channel_id=1, source_target_pairs={{0,2},{1,3},{4,0},{5,1},{8,4},{9,5},{12,8},{13,9},{14,12},{15,13},... | collective-permute-start | bytes 614408 | tf_op jit(solution)/shard_map/ppermute | solution.py:393
  25.6 4.7 %collective-permute-start.9 = (s16[1,16,3200]{2,1,0:T(8,128)(2,1)S(1)}, s16[1,16,3200]{2,1,0:T(8,128)(2,1)S(1)}, u32[]{:S(2)}, u32[]{:S(2)}) collective-permute-start(s16[1,16,3200]{2,1,0:T(8,128)(2,1)S(1)} %slice.8), channel_id=1, source_target_pairs={{0,4},{1,5},{4,8},{5,9},{8,12},{9,13},{12,14},{13,15},{14,10},{15,... | collective-permute-start | bytes 307208 | tf_op jit(solution)/shard_map/ppermute | solution.py:393
  26.3 4.9 %collective-permute-start.11 = (s16[1,16,3200]{2,1,0:T(8,128)(2,1)S(1)}, s16[1,16,3200]{2,1,0:T(8,128)(2,1)S(1)}, u32[]{:S(2)}, u32[]{:S(2)}) collective-permute-start(s16[1,16,3200]{2,1,0:T(8,128)(2,1)S(1)} %slice.9), channel_id=1, source_target_pairs={{0,2},{1,3},{4,0},{5,1},{8,4},{9,5},{12,8},{13,9},{14,12},{15,13},... | collective-permute-start | bytes 307208 | tf_op jit(solution)/shard_map/ppermute | solution.py:393
  30.9 2.3 %collective-permute-start.10 = (f32[8,128]{1,0:T(8,128)S(1)}, f32[8,128]{1,0:T(8,128)S(1)}, u32[]{:S(2)}, u32[]{:S(2)}) collective-permute-start(f32[8,128]{1,0:T(8,128)S(1)} %shard_map.151.refs_0_.refs_4_), channel_id=1, source_target_pairs={{0,1},{1,0},{2,3},{3,2},{4,5},{5,4},{6,7},{7,6},{8,9},{9,8},{10,11... | collective-permute-start | bytes 12296 | tf_op jit(solution)/shard_map/ppermute | solution.py:419
  35.5 7.5 %collective-permute-start.12 = (bf16[256,2048]{1,0:T(8,128)(2,1)S(1)}, bf16[256,2048]{1,0:T(8,128)(2,1)S(1)}, u32[]{:S(2)}, u32[]{:S(2)}) collective-permute-start(bf16[256,2048]{1,0:T(8,128)(2,1)S(1)} %get-tuple-element.61), channel_id=1, source_target_pairs={{0,1},{1,0},{2,3},{3,2},{4,5},{5,4},{6,7},{7,6},{8,9},{9,8},{10,11... | collective-permute-start | bytes 3145736 | tf_op jit(solution)/shard_map/ppermute | solution.py:419
  39.9 7.3 %collective-permute-start.13 = (s16[2,16,3200]{2,1,0:T(8,128)(2,1)S(1)}, s16[2,16,3200]{2,1,0:T(8,128)(2,1)S(1)}, u32[]{:S(2)}, u32[]{:S(2)}) collective-permute-start(s16[2,16,3200]{2,1,0:T(8,128)(2,1)S(1)} %get-tuple-element.63), channel_id=1, source_target_pairs={{0,4},{1,5},{2,6},{3,7},{4,0},{5,1},{6,2},{7,3},{8,12},{9,13},{10,... | collective-permute-start | bytes 614408 | tf_op jit(solution)/shard_map/ppermute | solution.py:419
  41.2 8.2 %collective-permute-start.15 = (s16[2,16,3200]{2,1,0:T(8,128)(2,1)S(1)}, s16[2,16,3200]{2,1,0:T(8,128)(2,1)S(1)}, u32[]{:S(2)}, u32[]{:S(2)}) collective-permute-start(s16[2,16,3200]{2,1,0:T(8,128)(2,1)S(1)} %get-tuple-element.69), channel_id=1, source_target_pairs={{0,2},{1,3},{2,0},{3,1},{4,6},{5,7},{6,4},{7,5},{8,10},{9,11},{10,... | collective-permute-start | bytes 614408 | tf_op jit(solution)/shard_map/ppermute | solution.py:419
  45.8 6.6 %collective-permute-start.14 = (s16[2,16,3200]{2,1,0:T(8,128)(2,1)S(1)}, s16[2,16,3200]{2,1,0:T(8,128)(2,1)S(1)}, u32[]{:S(2)}, u32[]{:S(2)}) collective-permute-start(s16[2,16,3200]{2,1,0:T(8,128)(2,1)S(1)} %get-tuple-element.67), channel_id=1, source_target_pairs={{0,4},{1,5},{2,6},{3,7},{4,0},{5,1},{6,2},{7,3},{8,12},{9,13},{10,... | collective-permute-start | bytes 614408 | tf_op jit(solution)/shard_map/ppermute | solution.py:419
  47.4 5.9 %collective-permute-start.16 = (s16[16,3200]{1,0:T(8,128)(2,1)S(1)}, s16[16,3200]{1,0:T(8,128)(2,1)S(1)}, u32[]{:S(2)}, u32[]{:S(2)}) collective-permute-start(s16[16,3200]{1,0:T(8,128)(2,1)S(1)} %get-tuple-element.66.refs_0_), channel_id=1, source_target_pairs={{0,2},{1,3},{2,0},{3,1},{4,6},{5,7},{6,4},{7,5},{8,10},{9,11},{10,... | collective-permute-start | bytes 307208 | tf_op jit(solution)/shard_map/ppermute | solution.py:419
  48.9 8.3 %collective-permute-start.17 = (s16[2,16,3200]{2,1,0:T(8,128)(2,1)S(1)}, s16[2,16,3200]{2,1,0:T(8,128)(2,1)S(1)}, u32[]{:S(2)}, u32[]{:S(2)}) collective-permute-start(s16[2,16,3200]{2,1,0:T(8,128)(2,1)S(1)} %get-tuple-element.73), channel_id=1, source_target_pairs={{0,2},{1,3},{2,0},{3,1},{4,6},{5,7},{6,4},{7,5},{8,10},{9,11},{10,... | collective-permute-start | bytes 614408 | tf_op jit(solution)/shard_map/ppermute | solution.py:419
  52.6 6.6 %collective-permute-start.18 = (s16[16,3200]{1,0:T(8,128)(2,1)S(1)}, s16[16,3200]{1,0:T(8,128)(2,1)S(1)}, u32[]{:S(2)}, u32[]{:S(2)}) collective-permute-start(s16[16,3200]{1,0:T(8,128)(2,1)S(1)} %get-tuple-element.70.refs_0_), channel_id=1, source_target_pairs={{0,2},{1,3},{2,0},{3,1},{4,6},{5,7},{6,4},{7,5},{8,10},{9,11},{10,... | collective-permute-start | bytes 307208 | tf_op jit(solution)/shard_map/ppermute | solution.py:419
  53.5 8.8 %collective-permute-start.19 = (s16[16,3200]{1,0:T(8,128)(2,1)S(1)}, s16[16,3200]{1,0:T(8,128)(2,1)S(1)}, u32[]{:S(2)}, u32[]{:S(2)}) collective-permute-start(s16[16,3200]{1,0:T(8,128)(2,1)S(1)} %shard_map.158.refs_0_), channel_id=1, source_target_pairs={{0,8},{1,9},{2,10},{3,11},{4,12},{5,13},{6,14},{7,15},{8,0},{9,1},... | collective-permute-start | bytes 307208 | tf_op jit(solution)/shard_map/ppermute | solution.py:419
  57.4 8.3 %collective-permute-start.21 = (s16[2,16,3200]{2,1,0:T(8,128)(2,1)S(1)}, s16[2,16,3200]{2,1,0:T(8,128)(2,1)S(1)}, u32[]{:S(2)}, u32[]{:S(2)}) collective-permute-start(s16[2,16,3200]{2,1,0:T(8,128)(2,1)S(1)} %get-tuple-element.75.refs_0_), channel_id=1, source_target_pairs={{0,4},{1,5},{2,6},{3,7},{4,0},{5,1},{6,2},{7,3},{8,12},{9,13},{10,... | collective-permute-start | bytes 614408 | tf_op jit(solution)/shard_map/ppermute | solution.py:419
  59.5 6.2 %collective-permute-start.20 = (s16[16,3200]{1,0:T(8,128)(2,1)S(1)}, s16[16,3200]{1,0:T(8,128)(2,1)S(1)}, u32[]{:S(2)}, u32[]{:S(2)}) collective-permute-start(s16[16,3200]{1,0:T(8,128)(2,1)S(1)} %shard_map.160.refs_0_), channel_id=1, source_target_pairs={{0,8},{1,9},{2,10},{3,11},{4,12},{5,13},{6,14},{7,15},{8,0},{9,1},... | collective-permute-start | bytes 307208 | tf_op jit(solution)/shard_map/ppermute | solution.py:419
  (3 other events, 11.5 us)
